TPU v7x, 32 devices: a whole 2x2x4 slice. The times are simulated.
32 devices in a mesh: dp: 2 (over y), expert: 16 (over z, x, core).
Axes of the slice: x: 2, y: 2, z: 4, core: 2. Of those that a mesh axis runs over, the one named last changes fastest.
Arguments:
- attn: bfloat16 [16, 64, 4096], P('expert', None, 'dp'), may hold values from -6 to 6
- resid: bfloat16 [16, 64, 2048], P('expert', 'dp'), may hold values from -6 to 6
- w_out: bfloat16 [4096, 2048], P('dp', 'expert'), may hold values from -0.09375 to 0.09375
- gain_post: float32 [2048], replicated, may hold values from 0.1 to 1.9
- route_ids: int32 [16, 64, 8], P('expert', 'dp'), may hold values from 0 to 15, all different within a row; in each aligned block of 32 rows (0 to 31, 32 to 63, ..., all dimensions but the last counted through in order) at most 32 rows name the same one
- route_logits: float32 [16, 64, 8], P('expert', 'dp'), may hold values from -2 to 260
- live_count: int32 [16, 2], P('expert', 'dp'), may hold values from 1 to 32, as said below
- w_gate_up: bfloat16 [16, 2048, 1536], P('expert', 'dp'), may hold values from -0.125 to 0.125
- w_down: bfloat16 [16, 768, 2048], P('expert', None, 'dp'), may hold values from -0.21875 to 0.21875
- gain_final: float32 [2048], replicated, may hold values from 0.1 to 1.9
Outputs:
- stream_out: bfloat16 [16, 64, 2048], P('expert', 'dp')
- normed_out: bfloat16 [16, 64, 2048], P('expert', 'dp')
Inputs may be any that keep to these rules, and one draw needn't show every extreme that they name: `route_ids`: each row names 8 different experts; among the rows of one device no expert is named more than 32 times. `live_count`: the devices whose dp index is a multiple of 3 hold prefill rows, all live; the others hold decode rows with a varying count.
All inputs are finite; a program needn't handle non-finite values.
Results may differ from a plain program's by a relative error of at most 0.018.
Values may be sent and summed in bfloat16 or wider, within the bound.
No kernel may reach another device: no remote copies, remote signals or barrier semaphores. Data moves between devices by JAX's collectives and lax.ppermute only.
A program may use at most 64 MiB of HBM per device.

v0:
```python
import math

import jax
import jax.numpy as jnp
from jax import lax
from jax.sharding import PartitionSpec as P


def rms_scale(values, gain):
    return values * lax.rsqrt(jnp.mean(values * values, axis=-1, keepdims=True) + 1e-06) * gain


def swiglu_rows(rows_in, gate_up, down, hidden_units):
    both = jnp.dot(rows_in, gate_up, preferred_element_type=jnp.float32)
    inner = (jax.nn.silu(both[:, :hidden_units]) * both[:, hidden_units:]).astype(jnp.bfloat16)
    return jnp.dot(inner, down, preferred_element_type=jnp.float32).astype(jnp.bfloat16)


def body(
    attn,
    resid,
    w_out,
    gain_post,
    route_ids,
    route_logits,
    live_count,
    w_gate_up,
    w_down,
    gain_final,
):
    rows_here = resid.shape[1]
    model_width = resid.shape[2]
    top_count = route_ids.shape[2]
    dp_count = lax.axis_size("dp")
    expert_count = lax.axis_size("expert")
    hidden_units = w_down.shape[1]
    capacity = dp_count * max(1, 2 * rows_here * top_count // (expert_count * dp_count))
    slot_count = expert_count * capacity
    flat_attn = attn[0]
    partial_out = jnp.dot(
        flat_attn,
        lax.all_gather(w_out, "expert", axis=1, tiled=True),
        preferred_element_type=jnp.float32,
    )
    projected = lax.psum_scatter(
        partial_out.astype(jnp.bfloat16), "dp", scatter_dimension=0, tiled=True
    ).astype(jnp.float32)
    stream_in = (resid[0].astype(jnp.float32) + projected).astype(jnp.bfloat16)
    stream_float = stream_in.astype(jnp.float32)
    normed_in = rms_scale(stream_float, gain_post).astype(jnp.bfloat16)
    probs = jax.nn.softmax(route_logits[0], axis=-1).astype(jnp.bfloat16)
    alive = jnp.arange(rows_here, dtype=jnp.int32) < live_count[0, 0]
    expert_of = route_ids[0].reshape(-1)
    route_alive = jnp.repeat(alive, top_count)
    onehot = (
        (expert_of[:, None] == jnp.arange(expert_count, dtype=jnp.int32)[None, :])
        & route_alive[:, None]
    ).astype(jnp.int32)
    earlier = jnp.sum((jnp.cumsum(onehot, axis=0) - onehot) * onehot, axis=1)
    target = expert_of * capacity + earlier
    match = (target[:, None] == jnp.arange(slot_count, dtype=jnp.int32)[None, :]) & route_alive[
        :, None
    ]
    placed = match.reshape(rows_here, top_count, slot_count)
    gather_matrix = jnp.any(placed, axis=1).astype(jnp.bfloat16)
    send_rows = lax.dot_general(
        gather_matrix, normed_in, (((0,), (0,)), ((), ())), preferred_element_type=jnp.float32
    ).astype(jnp.bfloat16)
    send_flags = jnp.sum(gather_matrix.astype(jnp.float32), axis=0).astype(jnp.bfloat16)
    combine_matrix = jnp.sum(
        jnp.where(placed, probs.astype(jnp.float32)[:, :, None], jnp.float32(0.0)), axis=1
    ).astype(jnp.bfloat16)
    arrived_rows, arrived_flags = (
        lax.all_to_all(
            send_rows.reshape(expert_count, capacity, model_width),
            "expert",
            split_axis=0,
            concat_axis=0,
            tiled=True,
        ),
        lax.all_to_all(
            send_flags.reshape(expert_count, capacity),
            "expert",
            split_axis=0,
            concat_axis=0,
            tiled=True,
        ),
    )
    arrived = arrived_rows.reshape(slot_count, model_width)
    flags = arrived_flags.reshape(slot_count)
    gate_up_full, down_full = (
        lax.all_gather(w_gate_up, "dp", axis=1, tiled=True),
        lax.all_gather(w_down, "dp", axis=2, tiled=True),
    )
    live_slot = (flags > 0.5).astype(jnp.int32)
    order = jnp.argsort(1 - live_slot, stable=True)
    live_total = jnp.sum(live_slot)
    packed = arrived[order]
    block_len = math.gcd(slot_count, 128)
    block_total = (live_total + block_len - 1) // block_len

    def run_block(index, outputs):
        begin = index * block_len
        rows_in = lax.dynamic_slice_in_dim(packed, begin, block_len, 0)
        block_out = swiglu_rows(rows_in, gate_up_full[0], down_full[0], hidden_units)
        return lax.dynamic_update_slice_in_dim(outputs, block_out, begin, 0)

    packed_out = lax.fori_loop(
        0, block_total, run_block, jnp.zeros((slot_count, model_width), jnp.bfloat16)
    )
    position = (
        jnp.zeros((slot_count,), jnp.int32).at[order].set(jnp.arange(slot_count, dtype=jnp.int32))
    )
    results = packed_out[position]
    returned = lax.all_to_all(
        results.reshape(expert_count, capacity, model_width),
        "expert",
        split_axis=0,
        concat_axis=0,
        tiled=True,
    )
    returned = returned.reshape(slot_count, model_width)
    mixture = jnp.dot(combine_matrix, returned, preferred_element_type=jnp.float32)
    stream_out = (stream_float + mixture).astype(jnp.bfloat16)
    normed_out = rms_scale(stream_out.astype(jnp.float32), gain_final).astype(jnp.bfloat16)
    return (stream_out[None], normed_out[None])


def solution(mesh):
    placed = (
        P("expert", None, "dp"),
        P("expert", "dp", None),
        P("dp", "expert"),
        P(),
        P("expert", "dp", None),
        P("expert", "dp", None),
        P("expert", "dp"),
        P("expert", "dp", None),
        P("expert", None, "dp"),
        P(),
    )
    return jax.shard_map(
        body,
        mesh=mesh,
        in_specs=placed,
        out_specs=(P("expert", "dp", None), P("expert", "dp", None)),
        check_vma=False,
    )
```

profile of v0, /device:TPU:0, one launch (start us, length us, event | category | flops | bytes accessed | tf_op | source)
XLA Modules:
  0.0 311.1 jit_solution(14957122388057156022)
XLA Ops:
  7.2 0.0 copy-start
  7.2 0.0 all-gather.4.cloned.1.call-start
  7.2 0.7 all-gather.4.cloned.1.call-update
  7.9 0.0 reduce-scatter.2.cloned.1.call-start
  8.0 83.0 %all-gather.4.cloned.1.call-done = bf16[2048,2048]{1,0:T(8,128)(2,1)} async-done(((bf16[2048,128]{1,0:T(8,128)(2,1)}), bf16[2048,2048]{1,0:T(8,128)(2,1)}) %all-gather.4.cloned.1.call-update) | async-done | bytes 8388624 | tf_op jit(solution)/shard_map/all_gather | solution.py:42
  91.0 0.0 copy-done
  91.0 5.7 %convolution_convert_fusion.1 = bf16[64,2048]{1,0:T(8,128)(2,1)} fusion(bf16[2048,2048]{1,0:T(8,128)(2,1)} %all-gather.4.cloned.1.call-done, bf16[1,64,2048]{2,1,0:T(8,128)(2,1)S(1)} %copy-done), kind=kOutput, calls=%fused_computation.16 | convolution fusion | flops 537001984 | bytes 8912896 | tf_op jit(solution)/shard_map/dot_general | solution.py:40
  96.7 0.0 reduce-scatter.2.cloned.1.call-update
  96.7 0.0 copy-start.7
  96.7 0.0 all-gather.8.cloned.1.call-start
  96.7 0.7 all-gather.8.cloned.1.call-update
  97.4 0.0 copy-start.1
  97.4 0.0 copy-start.5
  97.5 0.0 all-gather.6.cloned.1.call-start
  97.5 0.5 all-gather.6.cloned.1.call-update
  98.0 0.0 copy-done.7
  98.0 0.1 copy.25
  98.1 0.1 eq.43
  98.2 0.1 eq.39
  99.0 0.1 broadcast_in_dim.46
  99.0 0.1 broadcast_in_dim.47
  99.2 0.6 reduce-window.6
  99.7 0.2 slice_reduce_fusion
  100.0 0.1 broadcast_in_dim.45
  100.1 0.1 and.30
  100.2 0.1 fusion.34
  100.3 0.1 reduce_sum.69
  100.4 0.3 fusion.18
  100.6 0.7 all_to_all.16
  101.3 3.5 %all-to-all-start = ((bf16[16,1,32]{2,1,0:T(2,128)(2,1)}), bf16[16,1,32]{2,1,0:T(2,128)(2,1)S(1)}, u32[]{:S(2)}, u32[]{:S(2)}) async-start(bf16[16,1,32]{2,1,0:T(2,128)(2,1)} %all_to_all.16), calls=%async_computation.1 | async-start | bytes 16384 | tf_op jit(solution)/shard_map/all_to_all | solution.py:81
  104.8 1.9 reduce-scatter.2.cloned.1.call-done
  106.7 0.0 copy-done.1
  106.7 1.1 fusion.22
  107.8 0.0 copy-done.5
  107.8 3.0 convolution_convert_fusion
  110.8 0.3 all-to-all-done
  111.1 5.3 %all-to-all-start.1 = ((bf16[16,32,2048]{2,1,0:T(8,128)(2,1)}), bf16[16,32,2048]{2,1,0:T(8,128)(2,1)S(1)}, u32[]{:S(2)}, u32[]{:S(2)}) async-start(bf16[16,32,2048]{2,1,0:T(8,128)(2,1)} %bitcast.74), calls=%async_computation.2 | async-start | bytes 4194304 | tf_op jit(solution)/shard_map/all_to_all | solution.py:74
  116.4 0.6 subtract_reduce_fusion
  117.7 0.1 sub.38
  117.8 3.8 %sort.17 = (s32[512]{0:T(512)}, s32[512]{0:T(512)S(1)}) sort(s32[512]{0:T(512)S(1)} %sub.38, s32[512]{0:T(512)S(1)} %iota.44), dimensions={0}, to_apply=%region_11.12 | sort | flops 4608 | bytes 8192 | tf_op jit(solution)/shard_map/jit(argsort)/sort | solution.py:96
  121.6 2.4 scatter_custom_fusion
  124.0 33.4 %all-to-all-done.1 = bf16[16,32,2048]{2,1,0:T(8,128)(2,1)S(1)} async-done(((bf16[16,32,2048]{2,1,0:T(8,128)(2,1)}), bf16[16,32,2048]{2,1,0:T(8,128)(2,1)S(1)}, u32[]{:S(2)}, u32[]{:S(2)}) %all-to-all-start.1) | async-done | bytes 2097184 | tf_op jit(solution)/shard_map/all_to_all | solution.py:74
  157.5 3.3 %gather_fusion = bf16[512,2048]{1,0:T(8,128)(2,1)} fusion(bf16[512,2048]{1,0:T(8,128)(2,1)S(1)} %bitcast.72, s32[1024]{0:T(1024)S(1)} %pad_clamp_fusion.1), kind=kCustom, calls=%fused_computation | custom fusion | bytes 4196352 | tf_op jit(solution)/shard_map/gather | solution.py:98
  160.8 74.4 %all-gather.6.cloned.1.call-done = bf16[1,2048,1536]{2,1,0:T(8,128)(2,1)} async-done(((bf16[1,1024,1536]{2,1,0:T(8,128)(2,1)}), bf16[1,2048,1536]{2,1,0:T(8,128)(2,1)}) %all-gather.6.cloned.1.call-update) | async-done | bytes 6291472 | tf_op jit(solution)/shard_map/all_gather | solution.py:92
  235.2 0.2 broadcast_in_dim.50
  235.4 9.5 %while.10 = (s32[]{:T(128)}, bf16[512,2048]{1,0:T(8,128)(2,1)S(1)}, s32[]{:T(128)}, bf16[512,2048]{1,0:T(8,128)(2,1)}, bf16[1,2048,1536]{2,1,0:T(8,128)(2,1)}, /...) while((s32[]{:T(128)}, bf16[512,2048]{1,0:T(8,128)(2,1)S(1)}, ...), condition=%wide.region_13.14_spmd, body=%wide.region_12.13_spmd.sunk | while | flops 1208811520 | bytes 24641720 | solution.py:108
  235.4 0.0 copy-start.8
  235.4 4.1 %fusion.59 = f32[128,1536]{1,0:T(8,128)S(1)} fusion(bf16[1,2048,1536]{2,1,0:T(8,128)(2,1)} %get-tuple-element.116, bf16[512,2048]{1,0:T(8,128)(2,1)} %get-tuple-element.115, s32[]{:T(128)S(6)} %select_n.28), kind=kOutput, calls=%fused_computation.3.clone.1 | convolution fusion | flops 805306368 | bytes 7602180 | tf_op jit(solution)/shard_map/while/body/dot_general | solution.py:14
  239.5 0.0 copy-done.8
  239.6 0.6 fusion.60
  240.2 0.0 copy-start.8
  240.2 4.1 %fusion.59 = f32[128,1536]{1,0:T(8,128)S(1)} fusion(bf16[1,2048,1536]{2,1,0:T(8,128)(2,1)} %get-tuple-element.116, bf16[512,2048]{1,0:T(8,128)(2,1)} %get-tuple-element.115, s32[]{:T(128)S(6)} %select_n.28), kind=kOutput, calls=%fused_computation.3.clone.1 | convolution fusion | flops 805306368 | bytes 7602180 | tf_op jit(solution)/shard_map/while/body/dot_general | solution.py:14
  244.3 0.0 copy-done.8
  244.3 0.6 fusion.60
  244.9 3.3 %gather_fusion.1 = bf16[512,2048]{1,0:T(8,128)(2,1)} fusion(bf16[512,2048]{1,0:T(8,128)(2,1)S(1)} %get-tuple-element.37, s32[1024]{0:T(1024)S(1)} %pad_clamp_fusion), kind=kCustom, calls=%fused_computation.1 | custom fusion | bytes 4196352 | tf_op jit(solution)/shard_map/gather | solution.py:114
  248.3 13.8 %all-to-all-start.2 = ((bf16[16,32,2048]{2,1,0:T(8,128)(2,1)}), bf16[16,32,2048]{2,1,0:T(8,128)(2,1)S(1)}, u32[]{:S(2)}, u32[]{:S(2)}) async-start(bf16[16,32,2048]{2,1,0:T(8,128)(2,1)} %bitcast.73), calls=%async_computation.3 | async-start | bytes 4194304 | tf_op jit(solution)/shard_map/all_to_all | solution.py:115
  262.1 0.0 copy-done.4
  262.1 0.0 copy-start.6
  262.2 0.1 copy.29
  262.2 0.3 select_reduce_fusion
  262.5 40.7 %all-to-all-done.2 = bf16[16,32,2048]{2,1,0:T(8,128)(2,1)S(1)} async-done(((bf16[16,32,2048]{2,1,0:T(8,128)(2,1)}), bf16[16,32,2048]{2,1,0:T(8,128)(2,1)S(1)}, u32[]{:S(2)}, u32[]{:S(2)}) %all-to-all-start.2) | async-done | bytes 2097184 | tf_op jit(solution)/shard_map/all_to_all | solution.py:115
  303.2 0.6 fusion.19
  303.8 0.0 copy-start.3
  303.8 0.8 fusion.28
  (24 shorter events, 0.2 us)
Async XLA Ops:
  7.2 83.8 %copy-start = (bf16[1,64,2048]{2,1,0:T(8,128)(2,1)S(1)}, bf16[1,64,2048]{2,1,0:T(8,128)(2,1)}, u32[]{:S(2)}) copy-start(bf16[1,64,2048]{2,1,0:T(8,128)(2,1)} %param.12) | copy-start | bytes 786436
  7.2 83.8 %all-gather.4.cloned.1.call-start = ((), (), s32[]{:S(2)}) async-start(), calls=%async_computation.4 | async-start | bytes 8912896 | tf_op jit(solution)/shard_map/all_gather | solution.py:42
  7.9 98.8 %reduce-scatter.2.cloned.1.call-start = ((), (), s32[]{:S(2)}) async-start(), calls=%async_computation.5 | async-start | bytes 393216 | tf_op jit(solution)/shard_map/reduce_scatter | solution.py:45
  96.7 1.4 copy-start.7
  96.7 64.1 %all-gather.8.cloned.1.call-start = ((), (), s32[]{:S(2)}) async-start(), calls=%async_computation.7 | async-start | bytes 4718592 | tf_op jit(solution)/shard_map/all_gather | solution.py:93
  97.4 9.3 %copy-start.1 = (bf16[1,32,2048]{2,1,0:T(8,128)(2,1)S(1)}, bf16[1,32,2048]{2,1,0:T(8,128)(2,1)}, u32[]{:S(2)}) copy-start(bf16[1,32,2048]{2,1,0:T(8,128)(2,1)} %param.13) | copy-start | bytes 393220
  97.4 10.4 %copy-start.5 = (f32[2048]{0:T(1024)S(1)}, f32[2048]{0:T(1024)}, u32[]{:S(2)}) copy-start(f32[2048]{0:T(1024)} %param.15) | copy-start | bytes 24580
  97.5 137.7 %all-gather.6.cloned.1.call-start = ((), (), s32[]{:S(2)}) async-start(), calls=%async_computation.6 | async-start | bytes 9437184 | tf_op jit(solution)/shard_map/all_gather | solution.py:92
  101.3 9.8 %all-to-all-start = ((bf16[16,1,32]{2,1,0:T(2,128)(2,1)}), bf16[16,1,32]{2,1,0:T(2,128)(2,1)S(1)}, u32[]{:S(2)}, u32[]{:S(2)}) async-start(bf16[16,1,32]{2,1,0:T(2,128)(2,1)} %all_to_all.16), calls=%async_computation.1 | async-start | bytes 16384 | tf_op jit(solution)/shard_map/all_to_all | solution.py:81
  111.1 46.4 %all-to-all-start.1 = ((bf16[16,32,2048]{2,1,0:T(8,128)(2,1)}), bf16[16,32,2048]{2,1,0:T(8,128)(2,1)S(1)}, u32[]{:S(2)}, u32[]{:S(2)}) async-start(bf16[16,32,2048]{2,1,0:T(8,128)(2,1)} %bitcast.74), calls=%async_computation.2 | async-start | bytes 4194304 | tf_op jit(solution)/shard_map/all_to_all | solution.py:74
  235.4 4.1 %copy-start.8 = (bf16[1,768,2048]{2,1,0:T(8,128)(2,1)S(1)}, bf16[1,768,2048]{2,1,0:T(8,128)(2,1)}, u32[]{:S(2)}) copy-start(bf16[1,768,2048]{2,1,0:T(8,128)(2,1)} %get-tuple-element.117) | copy-start | bytes 9437188 | tf_op jit(solution)/shard_map/while
  240.2 4.1 %copy-start.8 = (bf16[1,768,2048]{2,1,0:T(8,128)(2,1)S(1)}, bf16[1,768,2048]{2,1,0:T(8,128)(2,1)}, u32[]{:S(2)}) copy-start(bf16[1,768,2048]{2,1,0:T(8,128)(2,1)} %get-tuple-element.117) | copy-start | bytes 9437188 | tf_op jit(solution)/shard_map/while
  248.3 13.8 %copy-start.4 = (f32[1,32,8]{1,2,0:T(8,128)S(1)}, f32[1,32,8]{1,2,0:T(8,128)}, u32[]{:S(2)}) copy-start(f32[1,32,8]{1,2,0:T(8,128)} %param.17) | copy-start | bytes 3076
  248.3 54.9 %copy-start.2 = (bf16[32,2048]{1,0:T(8,128)(2,1)S(1)}, bf16[32,2048]{1,0:T(8,128)(2,1)}, u32[]{:S(2)}) copy-start(bf16[32,2048]{1,0:T(8,128)(2,1)} %reduce-scatter.2.cloned.1.call-done) | copy-start | bytes 393220
  248.3 54.9 %all-to-all-start.2 = ((bf16[16,32,2048]{2,1,0:T(8,128)(2,1)}), bf16[16,32,2048]{2,1,0:T(8,128)(2,1)S(1)}, u32[]{:S(2)}, u32[]{:S(2)}) async-start(bf16[16,32,2048]{2,1,0:T(8,128)(2,1)} %bitcast.73), calls=%async_computation.3 | async-start | bytes 4194304 | tf_op jit(solution)/shard_map/all_to_all | solution.py:115
  262.1 41.7 %copy-start.6 = (f32[2048]{0:T(1024)S(1)}, f32[2048]{0:T(1024)}, u32[]{:S(2)}) copy-start(f32[2048]{0:T(1024)} %param.21) | copy-start | bytes 24580
  303.8 0.8 copy-start.3
Sparse Core Ops, SparseCore 0:
  10.2 80.7 all-gather.3
  96.8 9.8 reduce-scatter.1
  108.3 44.8 all-gather.7
  154.7 80.3 all-gather.5
where the time goes:
time: 317 us; the launch traced here: 311 us
  waiting for transfers between devices  236 us (74%)
  starting transfers between devices  22.7 us (7%)
  matrix products  18.6 us (6%)
  between operations  15.3 us (5%)
  local copies, waits for them, and re-layouts  11.1 us (4%)
  other arithmetic  7.64 us (2%)
    all_gather x1, waiting for transfers between devices, body(): lax.all_gather(w_out, 'expert', axis=1, tiled=True)  83 us
    all_gather x1, waiting for transfers between devices, body(): lax.all_gather(w_gate_up, 'dp', axis=1, tiled=True)  74.4 us
    all_to_all x1, waiting for transfers between devices, body(): lax.all_to_all(results.reshape(expert_count, capacity, model_width), 'exp...  40.7 us
    all_to_all x1, waiting for transfers between devices, body(): lax.all_to_all(send_rows.reshape(expert_count, capacity, model_width), 'e...  33.4 us
    all_to_all x1, starting transfers between devices, body(): lax.all_to_all(results.reshape(expert_count, capacity, model_width), 'exp...  13.8 us
    dot_general x2, matrix products, swiglu_rows(): both = jnp.dot(rows_in, gate_up, preferred_element_type=jnp.float32)  8.17 us
  transfers between devices with their start and end apart: 7, of which 6 were waited for; matrix products, arithmetic and copies ran while one was open for 5% of the time, Pallas kernels for 0%

commit v1 on v0

--- a/solution.py
+++ b/solution.py
@@ -3,6 +3,8 @@
 import jax
 import jax.numpy as jnp
 from jax import lax
+from jax.experimental import pallas as pl
+from jax.experimental.pallas import tpu as pltpu
 from jax.sharding import PartitionSpec as P
 
 
@@ -16,7 +18,7 @@
     return jnp.dot(inner, down, preferred_element_type=jnp.float32).astype(jnp.bfloat16)
 
 
-def body(
+def body_general(
     attn,
     resid,
     w_out,
@@ -126,6 +128,247 @@
     return (stream_out[None], normed_out[None])
 
 
+VMEM_BYTES = 56 * 1024 * 1024
+
+
+def whole_vmem():
+    return pl.BlockSpec(memory_space=pltpu.VMEM)
+
+
+def whole_smem():
+    return pl.BlockSpec(memory_space=pltpu.SMEM)
+
+
+def proj_kernel(place, a0, a1, a2, a3, w0, w1, w2, w3, r0, r1, r2, r3, base_ref, send_ref, rows, part):
+    outer, inner, dp = place[0], place[1], place[2]
+    full, width = a0.shape
+    half = full // 2
+    block = w0.shape[1]
+    for s, a in enumerate((a0, a1, a2, a3)):
+        spot = lax.rem(outer + 4 - s, 4)
+        rows[pl.ds(pl.multiple_of(spot * full, full), full), :] = a[...]
+    for j, w in enumerate((w0, w1, w2, w3)):
+        spot = pl.multiple_of((inner ^ j) * block, block)
+        part[:, pl.ds(spot, block)] = jnp.dot(
+            rows[...], w[...], preferred_element_type=jnp.float32
+        ).astype(jnp.bfloat16)
+    for s, r in enumerate((r0, r1, r2, r3)):
+        spot = lax.rem(outer + 4 - s, 4)
+        mine = pl.multiple_of(spot * full + dp * half, half)
+        other = pl.multiple_of(spot * full + (1 - dp) * half, half)
+        out = pl.ds(pl.multiple_of(spot * half, half), half)
+        base_ref[out, :] = r[...].astype(jnp.float32) + part[pl.ds(mine, half), :].astype(jnp.float32)
+        send_ref[out, :] = part[pl.ds(other, half), :]
+
+
+def gate_kernel(place, blocks, blocks_x, blocks_c, gain, ga, ua, gb, ub, inner_ref, own_ref, normed):
+    outer, dp = place[0], place[2]
+    step = pl.program_id(0)
+    count, width = blocks.shape[1], blocks.shape[2]
+    half = normed.shape[1] // 2
+    small = own_ref.shape[0]
+
+    @pl.when(step == 0)
+    def _():
+        for j in range(4):
+            square = jnp.zeros((count, 1), jnp.float32)
+            for s in range(4):
+                block = (blocks, blocks_c.at[0], blocks_x, blocks_c.at[1])[j][s]
+                spot = lax.rem(outer + 4 - s, 4)
+                cols = pl.ds(pl.multiple_of(spot * width, width), width)
+                normed[j * count : (j + 1) * count, cols] = block
+                value = block.astype(jnp.float32)
+                square = square + jnp.sum(value * value, axis=1, keepdims=True)
+            if j == 0:
+                own_ref[...] = normed[pl.ds(pl.multiple_of(outer * small, small), small), :]
+            scale = lax.rsqrt(square / (4 * width) + 1e-06)
+            for s in range(4):
+                cols = slice(s * width, (s + 1) * width)
+                value = normed[j * count : (j + 1) * count, cols].astype(jnp.float32)
+                normed[j * count : (j + 1) * count, cols] = (value * scale * gain[:, cols]).astype(jnp.bfloat16)
+
+    mine = normed[:, pl.ds(pl.multiple_of(dp * half, half), half)]
+    other = normed[:, pl.ds(pl.multiple_of((1 - dp) * half, half), half)]
+    dot = lambda a, b: jnp.dot(a, b, preferred_element_type=jnp.float32)
+    gate = dot(mine, ga[...]) + dot(other, gb[...])
+    up = dot(mine, ua[...]) + dot(other, ub[...])
+    inner_ref[...] = (gate / (1.0 + jnp.exp(-gate)) * up).astype(jnp.bfloat16)
+
+
+def down_kernel(inner, weight, wd, out_ref):
+    value = jnp.dot(inner[...], wd[...], preferred_element_type=jnp.float32).astype(jnp.bfloat16)
+    out_ref[...] = (value.astype(jnp.float32) * weight[...]).astype(jnp.bfloat16)
+
+
+def body_paired(
+    attn,
+    resid,
+    w_out,
+    gain_post,
+    route_ids,
+    route_logits,
+    live_count,
+    w_gate_up,
+    w_down,
+    gain_final,
+):
+    rows_here = resid.shape[1]
+    model_width = resid.shape[2]
+    expert_count = lax.axis_size("expert")
+    hidden = w_down.shape[1]
+    half_width = w_down.shape[2]
+    quarter = model_width // 4
+    dp = lax.axis_index("dp")
+    expert = lax.axis_index("expert")
+    outer, inner_at = expert // 4, expert % 4
+    place = jnp.stack([outer, inner_at, dp]).astype(jnp.int32)
+    bf16, f32 = jnp.bfloat16, jnp.float32
+    vmem, smem = whole_vmem(), whole_smem()
+    params = pltpu.CompilerParams(vmem_limit_bytes=VMEM_BYTES)
+
+    def swap_dp(x):
+        return lax.ppermute(x, "dp", [(0, 1), (1, 0)])
+
+    def shift_outer(x, s):
+        return lax.ppermute(
+            x, "expert", [(i, (i + 4 * s) % expert_count) for i in range(expert_count)]
+        )
+
+    def swap_inner(x, j):
+        return lax.ppermute(x, "expert", [(i, i ^ j) for i in range(expert_count)])
+
+    a = [attn[0]] + [shift_outer(attn[0], s) for s in (1, 2, 3)]
+    w_x = swap_inner(w_out, 2)
+    w_c = swap_inner(w_out, 1)
+    w_cx = swap_inner(w_x, 1)
+
+    def resid_piece(s):
+        return lax.dynamic_slice_in_dim(resid[0], ((outer + s) % 4) * quarter, quarter, 1)
+
+    r = [resid_piece(0)] + [shift_outer(resid_piece(s), s) for s in (1, 2, 3)]
+    gate_up_other = swap_dp(w_gate_up)
+    down_other = swap_dp(w_down)
+
+    probs = jax.nn.softmax(route_logits[0], axis=-1).astype(bf16)
+    alive = jnp.arange(rows_here, dtype=jnp.int32) < live_count[0, 0]
+    chosen = (
+        route_ids[0][:, :, None] == jnp.arange(expert_count, dtype=jnp.int32)[None, None, :]
+    ) & alive[:, None, None]
+    share = jnp.sum(jnp.where(chosen, probs.astype(f32)[:, :, None], 0.0), axis=1).astype(bf16)
+    shares = lax.all_gather(share, "expert", axis=0, tiled=False)
+    shares = shares.reshape(4, 4, rows_here, expert_count)
+    seat = jnp.arange(4, dtype=jnp.int32)
+    seated = seat[None, :] == (inner_at ^ seat[:, None])
+    pick = seated[:, None, :, None, None] & (
+        jnp.arange(expert_count, dtype=jnp.int32) == expert
+    )[None, None, None, None, :]
+    weight = jnp.sum(jnp.where(pick, shares.astype(f32)[None], 0.0), axis=(2, 4))
+    weight = weight.reshape(16 * rows_here, 1)
+
+    base, send = pl.pallas_call(
+        proj_kernel,
+        out_shape=(
+            jax.ShapeDtypeStruct((4 * rows_here, quarter), f32),
+            jax.ShapeDtypeStruct((4 * rows_here, quarter), bf16),
+        ),
+        in_specs=[smem] + [vmem] * 12,
+        out_specs=(vmem, vmem),
+        scratch_shapes=[
+            pltpu.VMEM((8 * rows_here, attn.shape[2]), bf16),
+            pltpu.VMEM((8 * rows_here, quarter), bf16),
+        ],
+        compiler_params=params,
+        name="projection",
+    )(place, *a, w_out, w_c, w_x, w_cx, *r)
+    stream_block = (base + swap_dp(send).astype(f32)).astype(bf16)
+
+    blocks = jnp.stack([stream_block] + [shift_outer(stream_block, s) for s in (1, 2, 3)])
+    blocks_x = swap_inner(blocks, 2)
+    blocks_c = swap_inner(jnp.stack([blocks, blocks_x]), 1)
+
+    unit = 256
+    hidden_steps = hidden // unit
+    row_total = 16 * rows_here
+    fixed = lambda *shape: pl.BlockSpec(shape, lambda i: (0,) * len(shape))
+    gate_spec = pl.BlockSpec((half_width, unit), lambda i: (0, i))
+    up_spec = pl.BlockSpec((half_width, unit), lambda i: (0, i + hidden_steps))
+    inner, stream_own = pl.pallas_call(
+        gate_kernel,
+        grid=(hidden_steps,),
+        out_shape=(
+            jax.ShapeDtypeStruct((row_total, hidden), bf16),
+            jax.ShapeDtypeStruct((rows_here, model_width), bf16),
+        ),
+        in_specs=[
+            smem,
+            fixed(*blocks.shape),
+            fixed(*blocks_x.shape),
+            fixed(*blocks_c.shape),
+            fixed(1, model_width),
+            gate_spec,
+            up_spec,
+            gate_spec,
+            up_spec,
+        ],
+        out_specs=(
+            pl.BlockSpec((row_total, unit), lambda i: (0, i)),
+            fixed(rows_here, model_width),
+        ),
+        scratch_shapes=[pltpu.VMEM((row_total, model_width), bf16)],
+        compiler_params=params,
+        name="gate_up",
+    )(
+        place,
+        blocks,
+        blocks_x,
+        blocks_c,
+        gain_post[None],
+        w_gate_up[0],
+        w_gate_up[0],
+        gate_up_other[0],
+        gate_up_other[0],
+    )
+
+    def down_half(wd):
+        return pl.pallas_call(
+            down_kernel,
+            grid=(half_width // 256,),
+            out_shape=jax.ShapeDtypeStruct((row_total, half_width), bf16),
+            in_specs=[
+                fixed(row_total, hidden),
+                fixed(row_total, 1),
+                pl.BlockSpec((hidden, 256), lambda i: (0, i)),
+            ],
+            out_specs=pl.BlockSpec((row_total, 256), lambda i: (0, i)),
+            compiler_params=params,
+            name="down",
+        )(inner, weight, wd)
+
+    mine, other = down_half(w_down[0]), down_half(down_other[0])
+    swapped = dp > 0
+    partial = jnp.concatenate(
+        [jnp.where(swapped, other, mine), jnp.where(swapped, mine, other)], axis=1
+    ).reshape(4, 4 * rows_here, model_width)
+
+    def add(x, y):
+        return (x.astype(f32) + y.astype(f32)).astype(bf16)
+
+    arrived = swap_inner(jnp.stack([partial[1], partial[3]]), 1)
+    far = add(partial[2], arrived[1])
+    near = add(partial[0], arrived[0])
+    near = add(near, swap_inner(far, 2)).reshape(4, rows_here, model_width)
+
+    def outer_piece(s):
+        return lax.dynamic_index_in_dim(near, (outer + s) % 4, 0, keepdims=False)
+
+    mixture = outer_piece(0).astype(f32)
+    for s in (1, 2, 3):
+        mixture = mixture + shift_outer(outer_piece(s), s).astype(f32)
+    stream_out = (stream_own.astype(f32) + mixture).astype(bf16)
+    normed_out = rms_scale(stream_out.astype(f32), gain_final).astype(bf16)
+    return (stream_out[None], normed_out[None])
+
+
 def solution(mesh):
     placed = (
         P("expert", None, "dp"),
@@ -139,8 +382,9 @@
         P("expert", None, "dp"),
         P(),
     )
+    paired = mesh.shape["dp"] == 2 and mesh.shape["expert"] == 16
     return jax.shard_map(
-        body,
+        body_paired if paired else body_general,
         mesh=mesh,
         in_specs=placed,
         out_specs=(P("expert", "dp", None), P("expert", "dp", None)),

time: 317 us -> 182 us (0.57); the launches traced: 311 us -> 182 us
  waiting for transfers between devices: 236 us -> 94.2 us
  blocking collectives: 0 us -> 22.3 us
  Pallas kernels: 0 us -> 21.7 us
  matrix products: 18.6 us -> 0 us
  between operations: 15.3 us -> 1.47 us
  local copies, waits for them, and re-layouts: 11.1 us -> 4.23 us
  starting transfers between devices: 22.7 us -> 27.6 us
    all_gather x3 -> x0, waiting for transfers between devices: 157 us -> none  [the longest x1 83 us: body(): lax.all_gather(w_out, 'expert', axis=1, tiled=True)]
    ppermute x0 -> x22, waiting for transfers between devices: none -> 94.2 us  [the longest x12 34.8 us: shift_outer(): lax.ppermute(x, 'expert', [(i, (i + 4 * s) % expert_count) for i in range...]
    all_to_all x3 -> x0, waiting for transfers between devices: 74.4 us -> none  [the longest x1 40.7 us: body(): lax.all_to_all(results.reshape(expert_count, capacity, model_width), 'exp...]
    ppermute x0 -> x22, starting transfers between devices: none -> 27.6 us  [the longest x12 19.1 us: shift_outer(): lax.ppermute(x, 'expert', [(i, (i + 4 * s) % expert_count) for i in range...]
    all_to_all x3 -> x0, starting transfers between devices: 22.5 us -> none  [the longest x1 13.8 us: body(): lax.all_to_all(results.reshape(expert_count, capacity, model_width), 'exp...]
    all_gather x0 -> x1, blocking collectives: none -> 22.3 us  [body_paired(): shares = lax.all_gather(share, 'expert', axis=0, tiled=False)]
    pallas_call x0 -> x4, Pallas kernels: none -> 21.7 us  [the longest x2 9.24 us: down_half(): pl.pallas_call(down_kernel, grid=(half_width // 256,), out_shape=jax.Shap...]
    dot_general x7 -> x0, matrix products: 18.6 us -> none  [the longest x2 8.17 us: swiglu_rows(): both = jnp.dot(rows_in, gate_up, preferred_element_type=jnp.float32)]
  transfers between devices with their start and end apart: 7 -> 22, of which waited for: 6 -> 13; matrix products, arithmetic and copies ran while one was open for 5% -> 4% of each run, Pallas kernels for 0% -> 7%
where the time goes in v1:
time: 182 us
  waiting for transfers between devices  94.2 us (52%)
  starting transfers between devices  27.6 us (15%)
  blocking collectives  22.3 us (12%)
  Pallas kernels  21.7 us (12%)
  other arithmetic  10.3 us (6%)
  local copies, waits for them, and re-layouts  4.23 us (2%)
    ppermute x12, waiting for transfers between devices, shift_outer(): lax.ppermute(x, 'expert', [(i, (i + 4 * s) % expert_count) for i in range...  34.8 us
    ppermute x7, waiting for transfers between devices, swap_inner(): return lax.ppermute(x, 'expert', [(i, i ^ j) for i in range(expert_count)])  34.6 us
    ppermute x3, waiting for transfers between devices, swap_dp(): return lax.ppermute(x, 'dp', [(0, 1), (1, 0)])  24.9 us
    all_gather x1, blocking collectives, body_paired(): shares = lax.all_gather(share, 'expert', axis=0, tiled=False)  22.3 us
    ppermute x12, starting transfers between devices, shift_outer(): lax.ppermute(x, 'expert', [(i, (i + 4 * s) % expert_count) for i in range...  19.1 us
    pallas_call x2, Pallas kernels, down_half(): pl.pallas_call(down_kernel, grid=(half_width // 256,), out_shape=jax.Shap...  9.24 us
    pallas_call x1, Pallas kernels, body_paired(): pl.pallas_call(gate_kernel, grid=(hidden_steps,), out_shape=(jax.ShapeDty...  8.47 us
    ppermute x3, starting transfers between devices, swap_dp(): return lax.ppermute(x, 'dp', [(0, 1), (1, 0)])  4.51 us
  transfers between devices with their start and end apart: 22, of which 13 were waited for; matrix products, arithmetic and copies ran while one was open for 4% of the time, Pallas kernels for 7%

profile of v1, /device:TPU:0, one launch (start us, length us, event | category | flops | bytes accessed | tf_op | source)
XLA Modules:
  0.0 181.8 jit_solution(4899785321092371226)
XLA Ops:
  0.6 3.0 %collective-permute-start.4 = (bf16[2048,128]{1,0:T(8,128)(2,1)}, bf16[2048,128]{1,0:T(8,128)(2,1)}, u32[]{:S(2)}, u32[]{:S(2)}) collective-permute-start(bf16[2048,128]{1,0:T(8,128)(2,1)} %w0.1), channel_id=1, source_target_pairs={{0,2},{1,3},{2,0},{3,1},{4,6},{5,7},{6,4},{7,5},{8,10},{9,11},{10,... | collective-permute-start | bytes 1572872 | tf_op jit(solution)/shard_map/ppermute | solution.py:238
  3.6 1.5 collective-permute-start.15
  5.2 1.6 collective-permute-start
  6.7 0.0 collective-permute-start.3
  6.7 9.1 %collective-permute-done.4.w2 = bf16[2048,128]{1,0:T(8,128)(2,1)} collective-permute-done((bf16[2048,128]{1,0:T(8,128)(2,1)}, bf16[2048,128]{1,0:T(8,128)(2,1)}, u32[]{:S(2)}, u32[]{:S(2)}) %collective-permute-start.4) | collective-permute-done | bytes 524320 | tf_op jit(solution)/shard_map/ppermute | solution.py:238
  15.9 0.0 collective-permute-start.5
  15.9 1.4 dynamic-slice_bitcast_fusion.3
  17.3 1.8 %collective-permute-start.6 = (bf16[32,512]{1,0:T(8,128)(2,1)S(1)}, bf16[32,512]{1,0:T(8,128)(2,1)S(1)}, u32[]{:S(2)}, u32[]{:S(2)}) collective-permute-start(bf16[32,512]{1,0:T(8,128)(2,1)S(1)} %get-tuple-element.22), channel_id=1, source_target_pairs={{0,4},{1,5},{2,6},{3,7},{4,8},{5,9},{6,10},{7,11},{8,12},{9,13},{1... | collective-permute-start | bytes 98312 | tf_op jit(solution)/shard_map/ppermute | solution.py:233
  19.1 4.1 %collective-permute-done.6.r1 = bf16[32,512]{1,0:T(8,128)(2,1)S(1)} collective-permute-done((bf16[32,512]{1,0:T(8,128)(2,1)S(1)}, bf16[32,512]{1,0:T(8,128)(2,1)S(1)}, u32[]{:S(2)}, u32[]{:S(2)}) %collective-permute-start.6) | collective-permute-done | bytes 32800 | tf_op jit(solution)/shard_map/ppermute | solution.py:233
  23.2 0.8 collective-permute-start.7
  24.1 4.0 %collective-permute-done.7.r2 = bf16[32,512]{1,0:T(8,128)(2,1)S(1)} collective-permute-done((bf16[32,512]{1,0:T(8,128)(2,1)S(1)}, bf16[32,512]{1,0:T(8,128)(2,1)S(1)}, u32[]{:S(2)}, u32[]{:S(2)}) %collective-permute-start.7) | collective-permute-done | bytes 32800 | tf_op jit(solution)/shard_map/ppermute | solution.py:233
  28.0 2.1 %collective-permute-start.8 = (bf16[32,512]{1,0:T(8,128)(2,1)S(1)}, bf16[32,512]{1,0:T(8,128)(2,1)S(1)}, u32[]{:S(2)}, u32[]{:S(2)}) collective-permute-start(bf16[32,512]{1,0:T(8,128)(2,1)S(1)} %get-tuple-element.21), channel_id=1, source_target_pairs={{0,12},{1,13},{2,14},{3,15},{4,0},{5,1},{6,2},{7,3},{8,4},{9,5},{1... | collective-permute-start | bytes 98312 | tf_op jit(solution)/shard_map/ppermute | solution.py:233
  30.1 1.8 %collective-permute-done.8.r3 = bf16[32,512]{1,0:T(8,128)(2,1)S(1)} collective-permute-done((bf16[32,512]{1,0:T(8,128)(2,1)S(1)}, bf16[32,512]{1,0:T(8,128)(2,1)S(1)}, u32[]{:S(2)}, u32[]{:S(2)}) %collective-permute-start.8) | collective-permute-done | bytes 32800 | tf_op jit(solution)/shard_map/ppermute | solution.py:233
  32.0 0.9 collective-permute-start.1
  32.8 0.0 collective-permute-done.a1
  32.8 3.4 %collective-permute-start.2 = (bf16[64,2048]{1,0:T(8,128)(2,1)}, bf16[64,2048]{1,0:T(8,128)(2,1)}, u32[]{:S(2)}, u32[]{:S(2)}) collective-permute-start(bf16[64,2048]{1,0:T(8,128)(2,1)} %bitcast.81), channel_id=1, source_target_pairs={{0,12},{1,13},{2,14},{3,15},{4,0},{5,1},{6,2},{7,3},{8,4},{9,5},{1... | collective-permute-start | bytes 786440 | tf_op jit(solution)/shard_map/ppermute | solution.py:233
  36.2 0.6 pad_add_fusion.place
  36.8 9.0 %collective-permute-done.1.a2 = bf16[64,2048]{1,0:T(8,128)(2,1)} collective-permute-done((bf16[64,2048]{1,0:T(8,128)(2,1)}, bf16[64,2048]{1,0:T(8,128)(2,1)}, u32[]{:S(2)}, u32[]{:S(2)}) %collective-permute-start.1) | collective-permute-done | bytes 262176 | tf_op jit(solution)/shard_map/ppermute | solution.py:233
  45.8 0.0 collective-permute-done.2.a3
  45.8 0.0 collective-permute-done.3.w1
  45.8 0.0 collective-permute-done.5.w3
  45.9 0.0 copy-start.6
  45.9 4.0 %projection.1 = (f32[128,512]{1,0:T(8,128)}, bf16[128,512]{1,0:T(8,128)(2,1)}) custom-call(s32[3]{0:T(128)} %pad_add_fusion.place, bf16[64,2048]{1,0:T(8,128)(2,1)} %bitcast.82, bf16[64,2048]{1,0:T(8,128)(2,1)} %copy-done.4, bf16[64,2048]{1,0:T(8,128)(2,1)} %collective-permute-done.1.a2, bf16[64,2048]{1,0:T(8,128)(2,1)} %collective-permute-done.2.a3, ...), custom_call_target="tpu_custom_call" | custom-call | tf_op jit(solution)/shard_map/projection/pallas_call | solution.py:268
  49.8 1.5 collective-permute-start.9
  51.3 24.9 %collective-permute-done.9 = bf16[128,512]{1,0:T(8,128)(2,1)S(1)} collective-permute-done((bf16[128,512]{1,0:T(8,128)(2,1)}, bf16[128,512]{1,0:T(8,128)(2,1)S(1)}, u32[]{:S(2)}, u32[]{:S(2)}) %collective-permute-start.9) | collective-permute-done | bytes 131104 | tf_op jit(solution)/shard_map/ppermute | solution.py:230
  76.2 1.0 add_convert_fusion.1
  77.2 2.7 %collective-permute-start.11 = (bf16[128,512]{1,0:T(8,128)(2,1)S(1)}, bf16[128,512]{1,0:T(8,128)(2,1)S(1)}, u32[]{:S(2)}, u32[]{:S(2)}) collective-permute-start(bf16[128,512]{1,0:T(8,128)(2,1)S(1)} %add_convert_fusion.1), channel_id=1, source_target_pairs={{0,8},{1,9},{2,10},{3,11},{4,12},{5,13},{6,14},{7,15},{8,0},{9,1},... | collective-permute-start | bytes 393224 | tf_op jit(solution)/shard_map/ppermute | solution.py:233
  79.9 1.3 collective-permute-start.12
  81.2 0.7 collective-permute-start.10
  81.9 5.7 %collective-permute-done.11 = bf16[128,512]{1,0:T(8,128)(2,1)S(1)} collective-permute-done((bf16[128,512]{1,0:T(8,128)(2,1)S(1)}, bf16[128,512]{1,0:T(8,128)(2,1)S(1)}, u32[]{:S(2)}, u32[]{:S(2)}) %collective-permute-start.11) | collective-permute-done | bytes 131104 | tf_op jit(solution)/shard_map/ppermute | solution.py:233
  87.6 0.0 collective-permute-done.12
  87.6 1.4 collective-permute-done.10
  89.1 1.1 fusion.19
  90.1 0.5 collective-permute-start.13
  90.7 1.5 collective-permute-start.16
  92.9 8.7 %collective-permute-done.13.blocks_x = bf16[4,128,512]{2,1,0:T(8,128)(2,1)} collective-permute-done((bf16[4,128,512]{2,1,0:T(8,128)(2,1)}, bf16[4,128,512]{2,1,0:T(8,128)(2,1)}, u32[]{:S(2)}, u32[]{:S(2)}) %collective-permute-start.13) | collective-permute-done | bytes 524320 | tf_op jit(solution)/shard_map/ppermute | solution.py:238
  101.6 2.3 %pad_maximum_fusion = bf16[2,4,128,512]{3,2,1,0:T(8,128)(2,1)} fusion(bf16[1,4,128,512]{3,2,1,0:T(8,128)(2,1)} %bitcast.13, bf16[1,4,128,512]{3,2,1,0:T(8,128)(2,1)} %get-tuple-element.19), kind=kLoop, calls=%fused_computation.6 | loop fusion | flops 524288 | bytes 2097152 | tf_op jit(solution)/shard_map/stack | solution.py:287
  104.0 0.0 collective-permute-start.14
  104.0 22.3 %all-gather.1 = bf16[16,32,16]{1,2,0:T(8,128)(2,1)S(1)} all-gather(bf16[1,32,16]{1,2,0:T(8,128)(2,1)S(1)} %bitcast.86), channel_id=2, replica_groups=mesh['dp'=2,'expert'=16] {'expert'}, dimensions={0}, use_global_device_ids=true | all-gather | bytes 17408 | tf_op jit(solution)/shard_map/all_gather | solution.py:258
  126.3 0.1 iota_compare_fusion.1
  126.4 0.1 broadcast_and_fusion
  126.5 0.1 select_reduce_fusion
  126.6 1.0 reshape.144.weight
  127.6 1.6 copy-done
  129.2 8.5 %gate_up.1 = (bf16[512,768]{1,0:T(8,128)(2,1)}, bf16[32,2048]{1,0:T(8,128)(2,1)}) custom-call(s32[3]{0:T(128)} %pad_add_fusion.place, bf16[4,128,512]{2,1,0:T(8,128)(2,1)} %get-tuple-element.20.blocks, bf16[4,128,512]{2,1,0:T(8,128)(2,1)} %collective-permute-done.13.blocks_x, bf16[2,4,128,512]{3,2,1,0:T(8,128)(2,1)} %collective-permute-done.14.blocks_c, ...), custom_call_target="tpu_custom_call" | custom-call | tf_op jit(solution)/shard_map/gate_up/pallas_call | solution.py:295
  137.7 0.0 collective-permute-done.16
  137.7 4.6 %down.2 = bf16[512,1024]{1,0:T(8,128)(2,1)} custom-call(bf16[512,768]{1,0:T(8,128)(2,1)} %get-tuple-element.9.inner, f32[512,1]{1,0:T(8,128)} %reshape.144.weight, bf16[768,1024]{1,0:T(8,128)(2,1)} %bitcast.22.wd), custom_call_target="tpu_custom_call" | custom-call | tf_op jit(solution)/shard_map/down/pallas_call | solution.py:333
  142.3 4.7 %down.3 = bf16[512,1024]{1,0:T(8,128)(2,1)} custom-call(bf16[512,768]{1,0:T(8,128)(2,1)} %get-tuple-element.9.inner, f32[512,1]{1,0:T(8,128)} %reshape.144.weight, bf16[768,1024]{1,0:T(8,128)(2,1)} %bitcast.23.wd), custom_call_target="tpu_custom_call" | custom-call | tf_op jit(solution)/shard_map/down/pallas_call | solution.py:333
  146.9 1.4 broadcast_select_fusion
  148.3 0.1 fusion.6
  148.4 0.1 pad_maximum_fusion.1
  148.5 0.4 collective-permute-start.17
  148.9 2.3 %collective-permute-done.17 = bf16[2,128,2048]{2,1,0:T(8,128)(2,1)S(1)} collective-permute-done((bf16[2,128,2048]{2,1,0:T(8,128)(2,1)S(1)}, bf16[2,128,2048]{2,1,0:T(8,128)(2,1)S(1)}, u32[]{:S(2)}, u32[]{:S(2)}) %collective-permute-start.17) | collective-permute-done | bytes 1048608 | tf_op jit(solution)/shard_map/ppermute | solution.py:238
  151.2 1.0 fusion
  152.3 0.1 copy-done.2
  152.4 14.4 %collective-permute-done.18 = bf16[128,2048]{1,0:T(8,128)(2,1)} collective-permute-done((bf16[128,2048]{1,0:T(8,128)(2,1)}, bf16[128,2048]{1,0:T(8,128)(2,1)}, u32[]{:S(2)}, u32[]{:S(2)}) %collective-permute-start.18) | collective-permute-done | bytes 524320 | tf_op jit(solution)/shard_map/ppermute | solution.py:238
  166.8 1.4 add_convert_fusion
  168.2 0.1 collective-permute-start.19
  168.3 0.2 collective-permute-start.20
  168.5 3.6 %collective-permute-start.21 = (bf16[32,2048]{1,0:T(8,128)(2,1)S(1)}, bf16[32,2048]{1,0:T(8,128)(2,1)S(1)}, u32[]{:S(2)}, u32[]{:S(2)}) collective-permute-start(bf16[32,2048]{1,0:T(8,128)(2,1)S(1)} %get-tuple-element.17), channel_id=1, source_target_pairs={{0,12},{1,13},{2,14},{3,15},{4,0},{5,1},{6,2},{7,3},{8,4},{9,5},{1... | collective-permute-start | bytes 393224 | tf_op jit(solution)/shard_map/ppermute | solution.py:233
  172.1 4.4 %collective-permute-done.19 = bf16[32,2048]{1,0:T(8,128)(2,1)S(1)} collective-permute-done((bf16[32,2048]{1,0:T(8,128)(2,1)S(1)}, bf16[32,2048]{1,0:T(8,128)(2,1)S(1)}, u32[]{:S(2)}, u32[]{:S(2)}) %collective-permute-start.19) | collective-permute-done | bytes 131104 | tf_op jit(solution)/shard_map/ppermute | solution.py:233
  176.6 4.3 %collective-permute-done.20 = bf16[32,2048]{1,0:T(8,128)(2,1)S(1)} collective-permute-done((bf16[32,2048]{1,0:T(8,128)(2,1)S(1)}, bf16[32,2048]{1,0:T(8,128)(2,1)S(1)}, u32[]{:S(2)}, u32[]{:S(2)}) %collective-permute-start.20) | collective-permute-done | bytes 131104 | tf_op jit(solution)/shard_map/ppermute | solution.py:233
  180.8 0.2 fusion.7
  181.1 0.8 fusion.14
  (35 shorter events, 0.2 us)
Async XLA Ops:
  0.6 15.2 %collective-permute-start.4 = (bf16[2048,128]{1,0:T(8,128)(2,1)}, bf16[2048,128]{1,0:T(8,128)(2,1)}, u32[]{:S(2)}, u32[]{:S(2)}) collective-permute-start(bf16[2048,128]{1,0:T(8,128)(2,1)} %w0.1), channel_id=1, source_target_pairs={{0,2},{1,3},{2,0},{3,1},{4,6},{5,7},{6,4},{7,5},{8,10},{9,11},{10,... | collective-permute-start | bytes 1572872 | tf_op jit(solution)/shard_map/ppermute | solution.py:238
  3.6 123.9 %collective-permute-start.15 = (bf16[1,1024,1536]{2,1,0:T(8,128)(2,1)}, bf16[1,1024,1536]{2,1,0:T(8,128)(2,1)S(1)}, u32[]{:S(2)}, u32[]{:S(2)}) collective-permute-start(bf16[1,1024,1536]{2,1,0:T(8,128)(2,1)} %param.17), channel_id=1, source_target_pairs={{0,16},{16,0},{1,17},{17,1},{2,18},{18,2},{3,19},{19,3},{4,20},{20... | collective-permute-start | bytes 9437192 | tf_op jit(solution)/shard_map/ppermute | solution.py:230
  5.2 27.7 %collective-permute-start = (bf16[64,2048]{1,0:T(8,128)(2,1)}, bf16[64,2048]{1,0:T(8,128)(2,1)S(1)}, u32[]{:S(2)}, u32[]{:S(2)}) collective-permute-start(bf16[64,2048]{1,0:T(8,128)(2,1)} %bitcast.79), channel_id=1, source_target_pairs={{0,4},{1,5},{2,6},{3,7},{4,8},{5,9},{6,10},{7,11},{8,12},{9,13},{1... | collective-permute-start | bytes 786440 | tf_op jit(solution)/shard_map/ppermute | solution.py:233
  6.7 39.1 %collective-permute-start.3 = (bf16[2048,128]{1,0:T(8,128)(2,1)}, bf16[2048,128]{1,0:T(8,128)(2,1)}, u32[]{:S(2)}, u32[]{:S(2)}) collective-permute-start(bf16[2048,128]{1,0:T(8,128)(2,1)} %w0.1), channel_id=1, source_target_pairs={{0,1},{1,0},{2,3},{3,2},{4,5},{5,4},{6,7},{7,6},{8,9},{9,8},{10,11... | collective-permute-start | bytes 1572872 | tf_op jit(solution)/shard_map/ppermute | solution.py:238
  15.9 29.9 %collective-permute-start.5 = (bf16[2048,128]{1,0:T(8,128)(2,1)}, bf16[2048,128]{1,0:T(8,128)(2,1)}, u32[]{:S(2)}, u32[]{:S(2)}) collective-permute-start(bf16[2048,128]{1,0:T(8,128)(2,1)} %collective-permute-done.4.w2), channel_id=1, source_target_pairs={{0,1},{1,0},{2,3},{3,2},{4,5},{5,4},{6,7},{7,6},{8,9},{9,8},{10,11... | collective-permute-start | bytes 1572872 | tf_op jit(solution)/shard_map/ppermute | solution.py:238
  17.3 5.9 %collective-permute-start.6 = (bf16[32,512]{1,0:T(8,128)(2,1)S(1)}, bf16[32,512]{1,0:T(8,128)(2,1)S(1)}, u32[]{:S(2)}, u32[]{:S(2)}) collective-permute-start(bf16[32,512]{1,0:T(8,128)(2,1)S(1)} %get-tuple-element.22), channel_id=1, source_target_pairs={{0,4},{1,5},{2,6},{3,7},{4,8},{5,9},{6,10},{7,11},{8,12},{9,13},{1... | collective-permute-start | bytes 98312 | tf_op jit(solution)/shard_map/ppermute | solution.py:233
  23.2 22.6 %copy-start.7 = (bf16[32,512]{1,0:T(8,128)(2,1)}, bf16[32,512]{1,0:T(8,128)(2,1)S(1)}, u32[]{:S(2)}) copy-start(bf16[32,512]{1,0:T(8,128)(2,1)S(1)} %collective-permute-done.6.r1) | copy-start | bytes 98308
  23.2 4.8 %collective-permute-start.7 = (bf16[32,512]{1,0:T(8,128)(2,1)S(1)}, bf16[32,512]{1,0:T(8,128)(2,1)S(1)}, u32[]{:S(2)}, u32[]{:S(2)}) collective-permute-start(bf16[32,512]{1,0:T(8,128)(2,1)S(1)} %get-tuple-element.24), channel_id=1, source_target_pairs={{0,8},{1,9},{2,10},{3,11},{4,12},{5,13},{6,14},{7,15},{8,0},{9,1},... | collective-permute-start | bytes 98312 | tf_op jit(solution)/shard_map/ppermute | solution.py:233
  28.0 17.8 %copy-start.8 = (bf16[32,512]{1,0:T(8,128)(2,1)}, bf16[32,512]{1,0:T(8,128)(2,1)S(1)}, u32[]{:S(2)}) copy-start(bf16[32,512]{1,0:T(8,128)(2,1)S(1)} %collective-permute-done.7.r2) | copy-start | bytes 98308
  28.0 3.9 %collective-permute-start.8 = (bf16[32,512]{1,0:T(8,128)(2,1)S(1)}, bf16[32,512]{1,0:T(8,128)(2,1)S(1)}, u32[]{:S(2)}, u32[]{:S(2)}) collective-permute-start(bf16[32,512]{1,0:T(8,128)(2,1)S(1)} %get-tuple-element.21), channel_id=1, source_target_pairs={{0,12},{1,13},{2,14},{3,15},{4,0},{5,1},{6,2},{7,3},{8,4},{9,5},{1... | collective-permute-start | bytes 98312 | tf_op jit(solution)/shard_map/ppermute | solution.py:233
  32.0 13.9 %copy-start.9 = (bf16[32,512]{1,0:T(8,128)(2,1)}, bf16[32,512]{1,0:T(8,128)(2,1)S(1)}, u32[]{:S(2)}) copy-start(bf16[32,512]{1,0:T(8,128)(2,1)S(1)} %collective-permute-done.8.r3) | copy-start | bytes 98308
  32.0 13.9 %collective-permute-start.1 = (bf16[64,2048]{1,0:T(8,128)(2,1)}, bf16[64,2048]{1,0:T(8,128)(2,1)}, u32[]{:S(2)}, u32[]{:S(2)}) collective-permute-start(bf16[64,2048]{1,0:T(8,128)(2,1)} %bitcast.80), channel_id=1, source_target_pairs={{0,8},{1,9},{2,10},{3,11},{4,12},{5,13},{6,14},{7,15},{8,0},{9,1},... | collective-permute-start | bytes 786440 | tf_op jit(solution)/shard_map/ppermute | solution.py:233
  32.8 13.0 %copy-start.4 = (bf16[64,2048]{1,0:T(8,128)(2,1)}, bf16[64,2048]{1,0:T(8,128)(2,1)S(1)}, u32[]{:S(2)}) copy-start(bf16[64,2048]{1,0:T(8,128)(2,1)S(1)} %collective-permute-done.a1) | copy-start | bytes 786436
  32.8 13.0 %collective-permute-start.2 = (bf16[64,2048]{1,0:T(8,128)(2,1)}, bf16[64,2048]{1,0:T(8,128)(2,1)}, u32[]{:S(2)}, u32[]{:S(2)}) collective-permute-start(bf16[64,2048]{1,0:T(8,128)(2,1)} %bitcast.81), channel_id=1, source_target_pairs={{0,12},{1,13},{2,14},{3,15},{4,0},{5,1},{6,2},{7,3},{8,4},{9,5},{1... | collective-permute-start | bytes 786440 | tf_op jit(solution)/shard_map/ppermute | solution.py:233
  45.9 47.0 %copy-start.6 = (f32[1,32,8]{1,2,0:T(8,128)S(1)}, f32[1,32,8]{1,2,0:T(8,128)}, u32[]{:S(2)}) copy-start(f32[1,32,8]{1,2,0:T(8,128)} %param.15) | copy-start | bytes 3076
  49.8 26.4 %collective-permute-start.9 = (bf16[128,512]{1,0:T(8,128)(2,1)}, bf16[128,512]{1,0:T(8,128)(2,1)S(1)}, u32[]{:S(2)}, u32[]{:S(2)}) collective-permute-start(bf16[128,512]{1,0:T(8,128)(2,1)} %get-tuple-element.7), channel_id=1, source_target_pairs={{0,16},{16,0},{1,17},{17,1},{2,18},{18,2},{3,19},{19,3},{4,20},{20... | collective-permute-start | bytes 393224 | tf_op jit(solution)/shard_map/ppermute | solution.py:230
  76.2 27.7 %copy-start.11 = (s32[1,32,8]{1,2,0:T(8,128)S(1)}, s32[1,32,8]{1,2,0:T(8,128)}, u32[]{:S(2)}) copy-start(s32[1,32,8]{1,2,0:T(8,128)} %param.14) | copy-start | bytes 3076
  77.2 10.4 %collective-permute-start.11 = (bf16[128,512]{1,0:T(8,128)(2,1)S(1)}, bf16[128,512]{1,0:T(8,128)(2,1)S(1)}, u32[]{:S(2)}, u32[]{:S(2)}) collective-permute-start(bf16[128,512]{1,0:T(8,128)(2,1)S(1)} %add_convert_fusion.1), channel_id=1, source_target_pairs={{0,8},{1,9},{2,10},{3,11},{4,12},{5,13},{6,14},{7,15},{8,0},{9,1},... | collective-permute-start | bytes 393224 | tf_op jit(solution)/shard_map/ppermute | solution.py:233
  79.9 7.8 %collective-permute-start.12 = (bf16[128,512]{1,0:T(8,128)(2,1)S(1)}, bf16[128,512]{1,0:T(8,128)(2,1)S(1)}, u32[]{:S(2)}, u32[]{:S(2)}) collective-permute-start(bf16[128,512]{1,0:T(8,128)(2,1)S(1)} %add_convert_fusion.1), channel_id=1, source_target_pairs={{0,12},{1,13},{2,14},{3,15},{4,0},{5,1},{6,2},{7,3},{8,4},{9,5},{1... | collective-permute-start | bytes 393224 | tf_op jit(solution)/shard_map/ppermute | solution.py:233
  81.2 7.8 %collective-permute-start.10 = (bf16[128,512]{1,0:T(8,128)(2,1)S(1)}, bf16[128,512]{1,0:T(8,128)(2,1)S(1)}, u32[]{:S(2)}, u32[]{:S(2)}) collective-permute-start(bf16[128,512]{1,0:T(8,128)(2,1)S(1)} %add_convert_fusion.1), channel_id=1, source_target_pairs={{0,4},{1,5},{2,6},{3,7},{4,8},{5,9},{6,10},{7,11},{8,12},{9,13},{1... | collective-permute-start | bytes 393224 | tf_op jit(solution)/shard_map/ppermute | solution.py:233
  90.1 11.5 %collective-permute-start.13 = (bf16[4,128,512]{2,1,0:T(8,128)(2,1)}, bf16[4,128,512]{2,1,0:T(8,128)(2,1)}, u32[]{:S(2)}, u32[]{:S(2)}) collective-permute-start(bf16[4,128,512]{2,1,0:T(8,128)(2,1)} %get-tuple-element.20.blocks), channel_id=1, source_target_pairs={{0,2},{1,3},{2,0},{3,1},{4,6},{5,7},{6,4},{7,5},{8,10},{9,11},{10,... | collective-permute-start | bytes 1572872 | tf_op jit(solution)/shard_map/ppermute | solution.py:238
  90.7 47.0 %collective-permute-start.16 = (bf16[1,768,1024]{2,1,0:T(8,128)(2,1)}, bf16[1,768,1024]{2,1,0:T(8,128)(2,1)}, u32[]{:S(2)}, u32[]{:S(2)}) collective-permute-start(bf16[1,768,1024]{2,1,0:T(8,128)(2,1)} %param.18), channel_id=1, source_target_pairs={{0,16},{16,0},{1,17},{17,1},{2,18},{18,2},{3,19},{19,3},{4,20},{20... | collective-permute-start | bytes 4718600 | tf_op jit(solution)/shard_map/ppermute | solution.py:230
  104.0 23.6 %collective-permute-start.14 = (bf16[2,4,128,512]{3,2,1,0:T(8,128)(2,1)}, bf16[2,4,128,512]{3,2,1,0:T(8,128)(2,1)}, u32[]{:S(2)}, u32[]{:S(2)}) collective-permute-start(bf16[2,4,128,512]{3,2,1,0:T(8,128)(2,1)} %pad_maximum_fusion), channel_id=1, source_target_pairs={{0,1},{1,0},{2,3},{3,2},{4,5},{5,4},{6,7},{7,6},{8,9},{9,8},{10,11... | collective-permute-start | bytes 3145736 | tf_op jit(solution)/shard_map/ppermute | solution.py:238
  127.6 1.6 copy-start
  142.3 4.7 %copy-start.1 = (bf16[512,1024]{1,0:T(8,128)(2,1)S(1)}, bf16[512,1024]{1,0:T(8,128)(2,1)}, u32[]{:S(2)}) copy-start(bf16[512,1024]{1,0:T(8,128)(2,1)} %down.2) | copy-start | bytes 3145732
  148.5 2.7 %collective-permute-start.17 = (bf16[2,128,2048]{2,1,0:T(8,128)(2,1)S(1)}, bf16[2,128,2048]{2,1,0:T(8,128)(2,1)S(1)}, u32[]{:S(2)}, u32[]{:S(2)}) collective-permute-start(bf16[2,128,2048]{2,1,0:T(8,128)(2,1)S(1)} %pad_maximum_fusion.1), channel_id=1, source_target_pairs={{0,1},{1,0},{2,3},{3,2},{4,5},{5,4},{6,7},{7,6},{8,9},{9,8},{10,11... | collective-permute-start | bytes 3145736 | tf_op jit(solution)/shard_map/ppermute | solution.py:238
  151.2 1.2 copy-start.2
  152.3 14.5 %collective-permute-start.18 = (bf16[128,2048]{1,0:T(8,128)(2,1)}, bf16[128,2048]{1,0:T(8,128)(2,1)}, u32[]{:S(2)}, u32[]{:S(2)}) collective-permute-start(bf16[128,2048]{1,0:T(8,128)(2,1)} %fusion), channel_id=1, source_target_pairs={{0,2},{1,3},{2,0},{3,1},{4,6},{5,7},{6,4},{7,5},{8,10},{9,11},{10,... | collective-permute-start | bytes 1572872 | tf_op jit(solution)/shard_map/ppermute | solution.py:238
  152.4 28.4 %copy-start.5 = (bf16[32,2048]{1,0:T(8,128)(2,1)S(1)}, bf16[32,2048]{1,0:T(8,128)(2,1)}, u32[]{:S(2)}) copy-start(bf16[32,2048]{1,0:T(8,128)(2,1)} %get-tuple-element.8) | copy-start | bytes 393220
  152.4 28.7 %copy-start.10 = (f32[2048]{0:T(1024)S(1)}, f32[2048]{0:T(1024)}, u32[]{:S(2)}) copy-start(f32[2048]{0:T(1024)} %param.19) | copy-start | bytes 24580
  168.2 8.3 %collective-permute-start.19 = (bf16[32,2048]{1,0:T(8,128)(2,1)S(1)}, bf16[32,2048]{1,0:T(8,128)(2,1)S(1)}, u32[]{:S(2)}, u32[]{:S(2)}) collective-permute-start(bf16[32,2048]{1,0:T(8,128)(2,1)S(1)} %get-tuple-element.16), channel_id=1, source_target_pairs={{0,4},{1,5},{2,6},{3,7},{4,8},{5,9},{6,10},{7,11},{8,12},{9,13},{1... | collective-permute-start | bytes 393224 | tf_op jit(solution)/shard_map/ppermute | solution.py:233
  168.3 12.5 %collective-permute-start.20 = (bf16[32,2048]{1,0:T(8,128)(2,1)S(1)}, bf16[32,2048]{1,0:T(8,128)(2,1)S(1)}, u32[]{:S(2)}, u32[]{:S(2)}) collective-permute-start(bf16[32,2048]{1,0:T(8,128)(2,1)S(1)} %get-tuple-element.18), channel_id=1, source_target_pairs={{0,8},{1,9},{2,10},{3,11},{4,12},{5,13},{6,14},{7,15},{8,0},{9,1},... | collective-permute-start | bytes 393224 | tf_op jit(solution)/shard_map/ppermute | solution.py:233
  168.5 12.3 %collective-permute-start.21 = (bf16[32,2048]{1,0:T(8,128)(2,1)S(1)}, bf16[32,2048]{1,0:T(8,128)(2,1)S(1)}, u32[]{:S(2)}, u32[]{:S(2)}) collective-permute-start(bf16[32,2048]{1,0:T(8,128)(2,1)S(1)} %get-tuple-element.17), channel_id=1, source_target_pairs={{0,12},{1,13},{2,14},{3,15},{4,0},{5,1},{6,2},{7,3},{8,4},{9,5},{1... | collective-permute-start | bytes 393224 | tf_op jit(solution)/shard_map/ppermute | solution.py:233
  181.0 0.8 copy-start.3

commit v2 on v1

--- a/solution.py
+++ b/solution.py
@@ -129,6 +129,7 @@
 
 
 VMEM_BYTES = 56 * 1024 * 1024
+BF16, F32 = jnp.bfloat16, jnp.float32
 
 
 def whole_vmem():
@@ -139,9 +140,21 @@
     return pl.BlockSpec(memory_space=pltpu.SMEM)
 
 
+def fixed(*shape):
+    return pl.BlockSpec(shape, lambda i: (0,) * len(shape))
+
+
+def dot(a, b):
+    return jnp.dot(a, b, preferred_element_type=F32)
+
+
+def kernel_params():
+    return pltpu.CompilerParams(vmem_limit_bytes=VMEM_BYTES)
+
+
 def proj_kernel(place, a0, a1, a2, a3, w0, w1, w2, w3, r0, r1, r2, r3, base_ref, send_ref, rows, part):
     outer, inner, dp = place[0], place[1], place[2]
-    full, width = a0.shape
+    full = a0.shape[0]
     half = full // 2
     block = w0.shape[1]
     for s, a in enumerate((a0, a1, a2, a3)):
@@ -149,55 +162,91 @@
         rows[pl.ds(pl.multiple_of(spot * full, full), full), :] = a[...]
     for j, w in enumerate((w0, w1, w2, w3)):
         spot = pl.multiple_of((inner ^ j) * block, block)
-        part[:, pl.ds(spot, block)] = jnp.dot(
-            rows[...], w[...], preferred_element_type=jnp.float32
-        ).astype(jnp.bfloat16)
+        part[:, pl.ds(spot, block)] = dot(rows[...], w[...]).astype(BF16)
     for s, r in enumerate((r0, r1, r2, r3)):
         spot = lax.rem(outer + 4 - s, 4)
         mine = pl.multiple_of(spot * full + dp * half, half)
         other = pl.multiple_of(spot * full + (1 - dp) * half, half)
         out = pl.ds(pl.multiple_of(spot * half, half), half)
-        base_ref[out, :] = r[...].astype(jnp.float32) + part[pl.ds(mine, half), :].astype(jnp.float32)
+        base_ref[out, :] = r[...].astype(F32) + part[pl.ds(mine, half), :].astype(F32)
         send_ref[out, :] = part[pl.ds(other, half), :]
 
 
-def gate_kernel(place, blocks, blocks_x, blocks_c, gain, ga, ua, gb, ub, inner_ref, own_ref, normed):
-    outer, dp = place[0], place[2]
+def first_gate_kernel(
+    place, blocks, blocks_x, blocks_c, blocks_cx, gain, ga, ua, gb, ub,
+    gate_ref, up_ref, last_ref, share_ref, own_ref, normed,
+):
+    outer, inner, dp = place[0], place[1], place[2]
     step = pl.program_id(0)
-    count, width = blocks.shape[1], blocks.shape[2]
+    width = blocks.shape[2]
+    count = share_ref.shape[0] // 4
+    experts = blocks.shape[1] - count
     half = normed.shape[1] // 2
     small = own_ref.shape[0]
+    depth = gb.shape[0]
+    rest = half - depth
 
     @pl.when(step == 0)
     def _():
-        for j in range(4):
-            square = jnp.zeros((count, 1), jnp.float32)
+        expert = outer * 4 + inner
+        picked = lax.broadcasted_iota(jnp.int32, (experts, count), 0) == expert
+        diagonal = lax.broadcasted_iota(jnp.int32, (count, count), 0) == lax.broadcasted_iota(
+            jnp.int32, (count, count), 1
+        )
+        for j, group in enumerate((blocks, blocks_c, blocks_x, blocks_cx)):
+            rows = slice(j * count, (j + 1) * count)
+            square = jnp.zeros((count, 1), F32)
+            share = jnp.zeros((experts, count), F32)
             for s in range(4):
-                block = (blocks, blocks_c.at[0], blocks_x, blocks_c.at[1])[j][s]
                 spot = lax.rem(outer + 4 - s, 4)
-                cols = pl.ds(pl.multiple_of(spot * width, width), width)
-                normed[j * count : (j + 1) * count, cols] = block
-                value = block.astype(jnp.float32)
+                value = group[s, 0:count, :]
+                normed[rows, pl.ds(pl.multiple_of(spot * width, width), width)] = value
+                value = value.astype(F32)
                 square = square + jnp.sum(value * value, axis=1, keepdims=True)
+                share = share + group[s, count : count + experts, 0:count].astype(F32)
+            line = jnp.sum(jnp.where(picked, share, 0.0), axis=0, keepdims=True)
+            column = jnp.sum(jnp.where(diagonal, line, 0.0), axis=1, keepdims=True)
+            share_ref[rows, :] = jnp.broadcast_to(column, (count, share_ref.shape[1]))
             if j == 0:
                 own_ref[...] = normed[pl.ds(pl.multiple_of(outer * small, small), small), :]
             scale = lax.rsqrt(square / (4 * width) + 1e-06)
             for s in range(4):
                 cols = slice(s * width, (s + 1) * width)
-                value = normed[j * count : (j + 1) * count, cols].astype(jnp.float32)
-                normed[j * count : (j + 1) * count, cols] = (value * scale * gain[:, cols]).astype(jnp.bfloat16)
+                value = normed[rows, cols].astype(F32)
+                normed[rows, cols] = (value * scale * gain[:, cols]).astype(BF16)
+        last_ref[...] = normed[:, pl.ds(pl.multiple_of((1 - dp) * half + depth, 128), rest)]
 
     mine = normed[:, pl.ds(pl.multiple_of(dp * half, half), half)]
-    other = normed[:, pl.ds(pl.multiple_of((1 - dp) * half, half), half)]
-    dot = lambda a, b: jnp.dot(a, b, preferred_element_type=jnp.float32)
-    gate = dot(mine, ga[...]) + dot(other, gb[...])
-    up = dot(mine, ua[...]) + dot(other, ub[...])
-    inner_ref[...] = (gate / (1.0 + jnp.exp(-gate)) * up).astype(jnp.bfloat16)
-
-
-def down_kernel(inner, weight, wd, out_ref):
-    value = jnp.dot(inner[...], wd[...], preferred_element_type=jnp.float32).astype(jnp.bfloat16)
-    out_ref[...] = (value.astype(jnp.float32) * weight[...]).astype(jnp.bfloat16)
+    early = normed[:, pl.ds(pl.multiple_of((1 - dp) * half, half), depth)]
+    gate_ref[...] = dot(mine, ga[...]) + dot(early, gb[...])
+    up_ref[...] = dot(mine, ua[...]) + dot(early, ub[...])
+
+
+def last_gate_kernel(gate, up, rows, share, gw, uw, inner_ref):
+    g = gate[...] + dot(rows[...], gw[...])
+    u = up[...] + dot(rows[...], uw[...])
+    inner_ref[...] = (g / (1.0 + jnp.exp(-g)) * u * share[:, 0:1]).astype(BF16)
+
+
+def down_kernel(inner, wd, keep_ref, send_ref):
+    count = inner.shape[0] // 4
+    value = dot(inner[...], wd[...]).astype(BF16)
+    for i in range(2):
+        keep_ref[i * count : (i + 1) * count, :] = value[2 * i * count : (2 * i + 1) * count]
+        send_ref[i * count : (i + 1) * count, :] = value[(2 * i + 1) * count : (2 * i + 2) * count]
+
+
+def tail_kernel(place, own, m0, m1, m2, m3, o0, o1, o2, o3, gain, stream_ref, normed_ref):
+    dp = place[2]
+    half = m0.shape[1]
+    for at, pieces in ((dp, (m0, m1, m2, m3)), (1 - dp, (o0, o1, o2, o3))):
+        cols = pl.ds(pl.multiple_of(at * half, half), half)
+        total = own[:, cols].astype(F32)
+        mixture = pieces[0][...].astype(F32)
+        for piece in pieces[1:]:
+            mixture = mixture + piece[...].astype(F32)
+        stream_ref[:, cols] = (total + mixture).astype(BF16)
+    normed_ref[...] = rms_scale(stream_ref[...].astype(F32), gain[...]).astype(BF16)
 
 
 def body_paired(
@@ -222,9 +271,7 @@
     expert = lax.axis_index("expert")
     outer, inner_at = expert // 4, expert % 4
     place = jnp.stack([outer, inner_at, dp]).astype(jnp.int32)
-    bf16, f32 = jnp.bfloat16, jnp.float32
     vmem, smem = whole_vmem(), whole_smem()
-    params = pltpu.CompilerParams(vmem_limit_bytes=VMEM_BYTES)
 
     def swap_dp(x):
         return lax.ppermute(x, "dp", [(0, 1), (1, 0)])
@@ -234,138 +281,179 @@
             x, "expert", [(i, (i + 4 * s) % expert_count) for i in range(expert_count)]
         )
 
+    def cross_outer(x, s):
+        return lax.ppermute(
+            x,
+            ("dp", "expert"),
+            [
+                (d * expert_count + i, (1 - d) * expert_count + (i + 4 * s) % expert_count)
+                for d in range(2)
+                for i in range(expert_count)
+            ],
+        )
+
     def swap_inner(x, j):
         return lax.ppermute(x, "expert", [(i, i ^ j) for i in range(expert_count)])
 
+    def after(x, *results):
+        return lax.optimization_barrier((x, *results))[0]
+
+    depth = half_width * 3 // 8
     a = [attn[0]] + [shift_outer(attn[0], s) for s in (1, 2, 3)]
     w_x = swap_inner(w_out, 2)
-    w_c = swap_inner(w_out, 1)
+    gate_up_early = swap_dp(w_gate_up[0, :depth])
+    w_c = swap_inner(after(w_out, w_x), 1)
     w_cx = swap_inner(w_x, 1)
 
     def resid_piece(s):
         return lax.dynamic_slice_in_dim(resid[0], ((outer + s) % 4) * quarter, quarter, 1)
 
-    r = [resid_piece(0)] + [shift_outer(resid_piece(s), s) for s in (1, 2, 3)]
-    gate_up_other = swap_dp(w_gate_up)
-    down_other = swap_dp(w_down)
-
-    probs = jax.nn.softmax(route_logits[0], axis=-1).astype(bf16)
+    r = [resid_piece(0)] + [shift_outer(after(resid_piece(s), w_cx), s) for s in (1, 2, 3)]
+
+    probs = jax.nn.softmax(route_logits[0], axis=-1).astype(BF16)
     alive = jnp.arange(rows_here, dtype=jnp.int32) < live_count[0, 0]
     chosen = (
-        route_ids[0][:, :, None] == jnp.arange(expert_count, dtype=jnp.int32)[None, None, :]
-    ) & alive[:, None, None]
-    share = jnp.sum(jnp.where(chosen, probs.astype(f32)[:, :, None], 0.0), axis=1).astype(bf16)
-    shares = lax.all_gather(share, "expert", axis=0, tiled=False)
-    shares = shares.reshape(4, 4, rows_here, expert_count)
-    seat = jnp.arange(4, dtype=jnp.int32)
-    seated = seat[None, :] == (inner_at ^ seat[:, None])
-    pick = seated[:, None, :, None, None] & (
-        jnp.arange(expert_count, dtype=jnp.int32) == expert
-    )[None, None, None, None, :]
-    weight = jnp.sum(jnp.where(pick, shares.astype(f32)[None], 0.0), axis=(2, 4))
-    weight = weight.reshape(16 * rows_here, 1)
+        route_ids[0][None] == jnp.arange(expert_count, dtype=jnp.int32)[:, None, None]
+    ) & alive[None, :, None]
+    share = jnp.sum(jnp.where(chosen, probs.astype(F32)[None], 0.0), axis=2)
+    spots = jnp.arange(quarter // rows_here, dtype=jnp.int32) == outer
+    share = jnp.where(spots[None, :, None], share[:, None, :], 0.0)
+    share = share.reshape(expert_count, quarter).astype(BF16)
 
     base, send = pl.pallas_call(
         proj_kernel,
         out_shape=(
-            jax.ShapeDtypeStruct((4 * rows_here, quarter), f32),
-            jax.ShapeDtypeStruct((4 * rows_here, quarter), bf16),
+            jax.ShapeDtypeStruct((4 * rows_here, quarter), F32),
+            jax.ShapeDtypeStruct((4 * rows_here, quarter), BF16),
         ),
         in_specs=[smem] + [vmem] * 12,
         out_specs=(vmem, vmem),
         scratch_shapes=[
-            pltpu.VMEM((8 * rows_here, attn.shape[2]), bf16),
-            pltpu.VMEM((8 * rows_here, quarter), bf16),
+            pltpu.VMEM((8 * rows_here, attn.shape[2]), BF16),
+            pltpu.VMEM((8 * rows_here, quarter), BF16),
         ],
-        compiler_params=params,
+        compiler_params=kernel_params(),
         name="projection",
     )(place, *a, w_out, w_c, w_x, w_cx, *r)
-    stream_block = (base + swap_dp(send).astype(f32)).astype(bf16)
-
-    blocks = jnp.stack([stream_block] + [shift_outer(stream_block, s) for s in (1, 2, 3)])
+    arrived = swap_dp(send)
+    gate_up_late = swap_dp(after(w_gate_up[0, depth:], arrived))
+    block = (base + arrived.astype(F32)).astype(BF16)
+    block = jnp.concatenate([block, share], axis=0)
+
+    blocks = jnp.stack([block] + [shift_outer(block, s) for s in (1, 2, 3)])
     blocks_x = swap_inner(blocks, 2)
-    blocks_c = swap_inner(jnp.stack([blocks, blocks_x]), 1)
+    blocks_c = swap_inner(blocks, 1)
+    blocks_cx = swap_inner(blocks_x, 1)
 
     unit = 256
-    hidden_steps = hidden // unit
+    steps = hidden // unit
     row_total = 16 * rows_here
-    fixed = lambda *shape: pl.BlockSpec(shape, lambda i: (0,) * len(shape))
-    gate_spec = pl.BlockSpec((half_width, unit), lambda i: (0, i))
-    up_spec = pl.BlockSpec((half_width, unit), lambda i: (0, i + hidden_steps))
-    inner, stream_own = pl.pallas_call(
-        gate_kernel,
-        grid=(hidden_steps,),
+    block_spec = fixed(*blocks.shape)
+    gate_cols = lambda k: pl.BlockSpec((k, unit), lambda i: (0, i))
+    up_cols = lambda k: pl.BlockSpec((k, unit), lambda i: (0, i + steps))
+    out_cols = pl.BlockSpec((row_total, unit), lambda i: (0, i))
+    gate, up, last_rows, share_rows, stream_own = pl.pallas_call(
+        first_gate_kernel,
+        grid=(steps,),
         out_shape=(
-            jax.ShapeDtypeStruct((row_total, hidden), bf16),
-            jax.ShapeDtypeStruct((rows_here, model_width), bf16),
+            jax.ShapeDtypeStruct((row_total, hidden), F32),
+            jax.ShapeDtypeStruct((row_total, hidden), F32),
+            jax.ShapeDtypeStruct((row_total, half_width - depth), BF16),
+            jax.ShapeDtypeStruct((row_total, 128), F32),
+            jax.ShapeDtypeStruct((rows_here, model_width), BF16),
         ),
-        in_specs=[
-            smem,
-            fixed(*blocks.shape),
-            fixed(*blocks_x.shape),
-            fixed(*blocks_c.shape),
+        in_specs=[smem]
+        + [block_spec] * 4
+        + [
             fixed(1, model_width),
-            gate_spec,
-            up_spec,
-            gate_spec,
-            up_spec,
+            gate_cols(half_width),
+            up_cols(half_width),
+            gate_cols(depth),
+            up_cols(depth),
         ],
         out_specs=(
-            pl.BlockSpec((row_total, unit), lambda i: (0, i)),
+            out_cols,
+            out_cols,
+            fixed(row_total, half_width - depth),
+            fixed(row_total, 128),
             fixed(rows_here, model_width),
         ),
-        scratch_shapes=[pltpu.VMEM((row_total, model_width), bf16)],
-        compiler_params=params,
-        name="gate_up",
+        scratch_shapes=[pltpu.VMEM((row_total, model_width), BF16)],
+        compiler_params=kernel_params(),
+        name="first_gate_up",
     )(
         place,
         blocks,
         blocks_x,
         blocks_c,
+        blocks_cx,
         gain_post[None],
         w_gate_up[0],
         w_gate_up[0],
-        gate_up_other[0],
-        gate_up_other[0],
-    )
-
-    def down_half(wd):
+        gate_up_early,
+        gate_up_early,
+    )
+    inner = pl.pallas_call(
+        last_gate_kernel,
+        grid=(steps,),
+        out_shape=jax.ShapeDtypeStruct((row_total, hidden), BF16),
+        in_specs=[
+            out_cols,
+            out_cols,
+            fixed(row_total, half_width - depth),
+            fixed(row_total, 128),
+            gate_cols(half_width - depth),
+            up_cols(half_width - depth),
+        ],
+        out_specs=out_cols,
+        compiler_params=kernel_params(),
+        name="last_gate_up",
+    )(gate, up, last_rows, share_rows, gate_up_late, gate_up_late)
+    inner_other = swap_dp(inner)
+
+    def down(rows):
+        out = jax.ShapeDtypeStruct((row_total // 2, half_width), BF16)
+        spec = pl.BlockSpec((row_total // 2, 256), lambda i: (0, i))
         return pl.pallas_call(
             down_kernel,
             grid=(half_width // 256,),
-            out_shape=jax.ShapeDtypeStruct((row_total, half_width), bf16),
+            out_shape=(out, out),
             in_specs=[
                 fixed(row_total, hidden),
-                fixed(row_total, 1),
                 pl.BlockSpec((hidden, 256), lambda i: (0, i)),
             ],
-            out_specs=pl.BlockSpec((row_total, 256), lambda i: (0, i)),
-            compiler_params=params,
+            out_specs=(spec, spec),
+            compiler_params=kernel_params(),
             name="down",
-        )(inner, weight, wd)
-
-    mine, other = down_half(w_down[0]), down_half(down_other[0])
-    swapped = dp > 0
-    partial = jnp.concatenate(
-        [jnp.where(swapped, other, mine), jnp.where(swapped, mine, other)], axis=1
-    ).reshape(4, 4 * rows_here, model_width)
+        )(rows, w_down[0])
 
     def add(x, y):
-        return (x.astype(f32) + y.astype(f32)).astype(bf16)
-
-    arrived = swap_inner(jnp.stack([partial[1], partial[3]]), 1)
-    far = add(partial[2], arrived[1])
-    near = add(partial[0], arrived[0])
-    near = add(near, swap_inner(far, 2)).reshape(4, rows_here, model_width)
-
-    def outer_piece(s):
+        return (x.astype(F32) + y.astype(F32)).astype(BF16)
+
+    def sum_inner(rows):
+        keep, send = down(rows)
+        near = add(keep, swap_inner(send, 1))
+        count = near.shape[0] // 2
+        near = add(near[:count], swap_inner(near[count:], 2))
+        return near.reshape(4, rows_here, half_width)
+
+    def outer_piece(near, s):
         return lax.dynamic_index_in_dim(near, (outer + s) % 4, 0, keepdims=False)
 
-    mixture = outer_piece(0).astype(f32)
-    for s in (1, 2, 3):
-        mixture = mixture + shift_outer(outer_piece(s), s).astype(f32)
-    stream_out = (stream_own.astype(f32) + mixture).astype(bf16)
-    normed_out = rms_scale(stream_out.astype(f32), gain_final).astype(bf16)
+    near = sum_inner(inner)
+    mine = [outer_piece(near, 0)] + [shift_outer(outer_piece(near, s), s) for s in (1, 2, 3)]
+    near = sum_inner(inner_other)
+    others = [cross_outer(outer_piece(near, s), s) for s in range(4)]
+
+    out = jax.ShapeDtypeStruct((rows_here, model_width), BF16)
+    stream_out, normed_out = pl.pallas_call(
+        tail_kernel,
+        out_shape=(out, out),
+        in_specs=[smem] + [vmem] * 10,
+        out_specs=(vmem, vmem),
+        compiler_params=kernel_params(),
+        name="closing",
+    )(place, stream_own, *mine, *others, gain_final[None])
     return (stream_out[None], normed_out[None])
 
 

time: 182 us -> 176 us (0.967)
  blocking collectives: 22.3 us -> 0 us
  starting transfers between devices: 27.6 us -> 35.6 us
  local copies, waits for them, and re-layouts: 4.23 us -> 11.8 us
  Pallas kernels: 21.7 us -> 28.3 us
  other arithmetic: 10.3 us -> 3.7 us
    ppermute x3 -> x4, waiting for transfers between devices: 24.9 us -> 57.3 us  [swap_dp(): return lax.ppermute(x, 'dp', [(0, 1), (1, 0)])]
    ppermute x12, waiting for transfers between devices: 34.8 us -> 8.51 us  [shift_outer(): lax.ppermute(x, 'expert', [(i, (i + 4 * s) % expert_count) for i in range...]
    all_gather x1 -> x0, blocking collectives: 22.3 us -> none  [body_paired(): shares = lax.all_gather(share, 'expert', axis=0, tiled=False)]
    ppermute x7 -> x10, waiting for transfers between devices: 34.6 us -> 23.5 us  [swap_inner(): return lax.ppermute(x, 'expert', [(i, i ^ j) for i in range(expert_count)])]
    pallas_call x3 -> x5, Pallas kernels: 17.7 us -> 24.4 us  [the longest x2 8.84 us: down(): pl.pallas_call(down_kernel, grid=(half_width // 256,), out_shape=(out, ou...]
    ppermute x0 -> x4, starting transfers between devices: none -> 6.45 us  [cross_outer(): lax.ppermute(x, ('dp', 'expert'), [(d * expert_count + i, (1 - d) * exper...]
    ppermute x0 -> x4, waiting for transfers between devices: none -> 5.04 us  [cross_outer(): lax.ppermute(x, ('dp', 'expert'), [(d * expert_count + i, (1 - d) * exper...]
    another operation x3 -> x2, other arithmetic: 3.48 us -> 0.1 us  [body_paired(): blocks = jnp.stack([block] + [shift_outer(block, s) for s in (1, 2, 3)])]
  transfers between devices with their start and end apart: 22 -> 30, of which waited for: 13 -> 15; matrix products, arithmetic and copies ran while one was open for 4% -> 6% of each run, Pallas kernels for 7% -> 10%
where the time goes in v2:
time: 176 us
  waiting for transfers between devices  94.3 us (54%)
  starting transfers between devices  35.6 us (20%)
  Pallas kernels  28.3 us (16%)
  local copies, waits for them, and re-layouts  11.8 us (7%)
  other arithmetic  3.7 us (2%)
  between operations  1.79 us (1%)
    ppermute x4, waiting for transfers between devices, swap_dp(): return lax.ppermute(x, 'dp', [(0, 1), (1, 0)])  57.3 us
    ppermute x10, waiting for transfers between devices, swap_inner(): return lax.ppermute(x, 'expert', [(i, i ^ j) for i in range(expert_count)])  23.5 us
    ppermute x12, starting transfers between devices, shift_outer(): lax.ppermute(x, 'expert', [(i, (i + 4 * s) % expert_count) for i in range...  17.4 us
    pallas_call x2, Pallas kernels, down(): pl.pallas_call(down_kernel, grid=(half_width // 256,), out_shape=(out, ou...  8.84 us
    ppermute x12, waiting for transfers between devices, shift_outer(): lax.ppermute(x, 'expert', [(i, (i + 4 * s) % expert_count) for i in range...  8.51 us
    pallas_call x1, Pallas kernels, body_paired(): pl.pallas_call(first_gate_kernel, grid=(steps,), out_shape=(jax.ShapeDtyp...  8.14 us
    ppermute x10, starting transfers between devices, swap_inner(): return lax.ppermute(x, 'expert', [(i, i ^ j) for i in range(expert_count)])  6.7 us
    ppermute x4, starting transfers between devices, cross_outer(): lax.ppermute(x, ('dp', 'expert'), [(d * expert_count + i, (1 - d) * exper...  6.45 us
  transfers between devices with their start and end apart: 30, of which 15 were waited for; matrix products, arithmetic and copies ran while one was open for 6% of the time, Pallas kernels for 10%

profile of v2, /device:TPU:0, one launch (start us, length us, event | category | flops | bytes accessed | tf_op | source)
XLA Modules:
  0.0 175.5 jit_solution(6261266553121011821)
XLA Ops:
  0.6 5.1 %collective-permute-start.2 = (bf16[64,2048]{1,0:T(8,128)(2,1)}, bf16[64,2048]{1,0:T(8,128)(2,1)}, u32[]{:S(2)}, u32[]{:S(2)}) collective-permute-start(bf16[64,2048]{1,0:T(8,128)(2,1)} %bitcast.63), channel_id=1, source_target_pairs={{0,12},{1,13},{2,14},{3,15},{4,0},{5,1},{6,2},{7,3},{8,4},{9,5},{1... | collective-permute-start | bytes 786440 | tf_op jit(solution)/shard_map/ppermute | solution.py:280
  5.7 1.0 collective-permute-start
  6.7 1.5 collective-permute-start.3
  8.2 0.7 reduce_max.9
  8.9 0.7 fusion.2
  9.7 1.7 slice_bitcast_fusion
  11.4 8.4 %collective-permute-done.3.w2 = bf16[2048,128]{1,0:T(8,128)(2,1)S(1)} collective-permute-done((bf16[2048,128]{1,0:T(8,128)(2,1)}, bf16[2048,128]{1,0:T(8,128)(2,1)S(1)}, u32[]{:S(2)}, u32[]{:S(2)}) %collective-permute-start.3) | collective-permute-done | bytes 524320 | tf_op jit(solution)/shard_map/ppermute | solution.py:296
  20.5 0.5 collective-permute-start.4
  21.2 1.5 dynamic-slice_bitcast_fusion.8
  22.7 2.5 %collective-permute-start.6 = (bf16[32,512]{1,0:T(8,128)(2,1)}, bf16[32,512]{1,0:T(8,128)(2,1)}, u32[]{:S(2)}, u32[]{:S(2)}) collective-permute-start(bf16[32,512]{1,0:T(8,128)(2,1)} %get-tuple-element.21), channel_id=1, source_target_pairs={{0,4},{1,5},{2,6},{3,7},{4,8},{5,9},{6,10},{7,11},{8,12},{9,13},{1... | collective-permute-start | bytes 98312 | tf_op jit(solution)/shard_map/ppermute | solution.py:280
  25.2 1.2 collective-permute-start.7
  26.4 3.1 %collective-permute-done.1.a2 = bf16[64,2048]{1,0:T(8,128)(2,1)} collective-permute-done((bf16[64,2048]{1,0:T(8,128)(2,1)}, bf16[64,2048]{1,0:T(8,128)(2,1)}, u32[]{:S(2)}, u32[]{:S(2)}) %collective-permute-start.1) | collective-permute-done | bytes 262176 | tf_op jit(solution)/shard_map/ppermute | solution.py:280
  29.5 0.6 pad_add_fusion.place
  30.2 0.1 broadcast_in_dim.62
  30.3 0.6 broadcast_in_dim.63
  30.9 0.6 broadcast_in_dim.69
  31.5 1.0 broadcast_in_dim.70
  32.5 1.3 collective-permute-done.8.r3
  33.8 3.9 %projection.1 = (f32[128,512]{1,0:T(8,128)}, bf16[128,512]{1,0:T(8,128)(2,1)}) custom-call(s32[3]{0:T(128)} %pad_add_fusion.place, bf16[64,2048]{1,0:T(8,128)(2,1)} %bitcast.66, bf16[64,2048]{1,0:T(8,128)(2,1)} %collective-permute-done.a1, bf16[64,2048]{1,0:T(8,128)(2,1)} %collective-permute-done.1.a2, bf16[64,2048]{1,0:T(8,128)(2,1)} %collective-permute-done.2.a3, ...), custom_call_target="tpu_custom_call" | custom-call | tf_op jit(solution)/shard_map/projection/pallas_call | solution.py:323
  37.7 1.5 collective-permute-start.9
  39.3 5.0 %collective-permute-done.9 = bf16[128,512]{1,0:T(8,128)(2,1)S(1)} collective-permute-done((bf16[128,512]{1,0:T(8,128)(2,1)}, bf16[128,512]{1,0:T(8,128)(2,1)S(1)}, u32[]{:S(2)}, u32[]{:S(2)}) %collective-permute-start.9) | collective-permute-done | bytes 131104 | tf_op jit(solution)/shard_map/ppermute | solution.py:277
  44.3 1.5 collective-permute-start.17
  45.8 1.0 add_convert_fusion.4
  46.8 0.1 collective-permute-start.11
  46.9 1.7 collective-permute-start.10
  48.6 2.2 %collective-permute-start.12 = (bf16[144,512]{1,0:T(8,128)(2,1)S(1)}, bf16[144,512]{1,0:T(8,128)(2,1)S(1)}, u32[]{:S(2)}, u32[]{:S(2)}) collective-permute-start(bf16[144,512]{1,0:T(8,128)(2,1)S(1)} %get-tuple-element.47), channel_id=1, source_target_pairs={{0,12},{1,13},{2,14},{3,15},{4,0},{5,1},{6,2},{7,3},{8,4},{9,5},{1... | collective-permute-start | bytes 442376 | tf_op jit(solution)/shard_map/ppermute | solution.py:280
  50.8 1.3 slice_bitcast_fusion.1
  52.1 0.6 collective-permute-start.16
  52.7 3.4 %collective-permute-done.11 = bf16[144,512]{1,0:T(8,128)(2,1)S(1)} collective-permute-done((bf16[144,512]{1,0:T(8,128)(2,1)S(1)}, bf16[144,512]{1,0:T(8,128)(2,1)S(1)}, u32[]{:S(2)}, u32[]{:S(2)}) %collective-permute-start.11) | collective-permute-done | bytes 147488 | tf_op jit(solution)/shard_map/ppermute | solution.py:280
  56.1 0.7 collective-permute-done.12
  56.8 0.1 pad_maximum_fusion.blocks
  56.9 1.6 collective-permute-start.13
  58.5 8.4 %collective-permute-done.13.blocks_x = bf16[4,144,512]{2,1,0:T(8,128)(2,1)S(1)} collective-permute-done((bf16[4,144,512]{2,1,0:T(8,128)(2,1)S(1)}, bf16[4,144,512]{2,1,0:T(8,128)(2,1)S(1)}, u32[]{:S(2)}, u32[]{:S(2)}) %collective-permute-start.13) | collective-permute-done | bytes 589856 | tf_op jit(solution)/shard_map/ppermute | solution.py:296
  66.8 43.5 %collective-permute-done.16.gb.ub = bf16[384,1536]{1,0:T(8,128)(2,1)S(1)} collective-permute-done((bf16[384,1536]{1,0:T(8,128)(2,1)S(1)}, bf16[384,1536]{1,0:T(8,128)(2,1)S(1)}, u32[]{:S(2)}, u32[]{:S(2)}) %collective-permute-start.16) | collective-permute-done | bytes 1179680 | tf_op jit(solution)/shard_map/ppermute | solution.py:277
  110.4 1.0 copy-done.1
  111.4 0.2 copy-done.5
  111.5 0.2 copy-done.6
  111.8 8.1 %first_gate_up.1 = (f32[512,768]{1,0:T(8,128)}, f32[512,768]{1,0:T(8,128)}, bf16[512,640]{1,0:T(8,128)(2,1)}, f32[512,128]{1,0:T(8,128)}, bf16[32,2048]{1,0:T(8,128)(2,1)}) custom-call(s32[3]{0:T(128)} %pad_add_fusion.place, bf16[4,144,512]{2,1,0:T(8,128)(2,1)} %copy-done.2, bf16[4,144,512]{2,1,0:T(8,128)(2,1)} %copy-done.4, bf16[4,144,512]{2,1,0:T(8,128)(2,1)} %copy-done.5, ...), custom_call_target="tpu_custom_call" | custom-call | tf_op jit(solution)/shard_map/first_gate_up/pallas_call | solution.py:355
  119.9 1.3 copy-done
  121.2 5.4 %last_gate_up.1.inner = bf16[512,768]{1,0:T(8,128)(2,1)} custom-call(f32[512,768]{1,0:T(8,128)} %get-tuple-element.27.gate, f32[512,768]{1,0:T(8,128)} %get-tuple-element.28.up, bf16[512,640]{1,0:T(8,128)(2,1)} %get-tuple-element.29.rows, f32[512,128]{1,0:T(8,128)} %get-tuple-element.30.share, bf16[640,1536]{1,0:T(8,128)(2,1)} %copy-done, ...), custom_call_target="tpu_custom_call" | custom-call | tf_op jit(solution)/shard_map/last_gate_up/pallas_call | solution.py:396
  126.6 1.5 collective-permute-start.23
  128.1 4.4 %down.2 = (bf16[256,1024]{1,0:T(8,128)(2,1)}, bf16[256,1024]{1,0:T(8,128)(2,1)}) custom-call(bf16[512,768]{1,0:T(8,128)(2,1)} %last_gate_up.1.inner, bf16[768,1024]{1,0:T(8,128)(2,1)} %bitcast.59), custom_call_target="tpu_custom_call" | custom-call | tf_op jit(solution)/shard_map/down/pallas_call | solution.py:417
  132.5 8.8 %collective-permute-done.23.inner = bf16[512,768]{1,0:T(8,128)(2,1)S(1)} collective-permute-done((bf16[512,768]{1,0:T(8,128)(2,1)}, bf16[512,768]{1,0:T(8,128)(2,1)S(1)}, u32[]{:S(2)}, u32[]{:S(2)}) %collective-permute-start.23) | collective-permute-done | bytes 786464 | tf_op jit(solution)/shard_map/ppermute | solution.py:277
  141.3 0.9 copy-done.3
  142.2 4.4 %down.3 = (bf16[256,1024]{1,0:T(8,128)(2,1)}, bf16[256,1024]{1,0:T(8,128)(2,1)}) custom-call(bf16[512,768]{1,0:T(8,128)(2,1)} %copy-done.3, bf16[768,1024]{1,0:T(8,128)(2,1)} %bitcast.60), custom_call_target="tpu_custom_call" | custom-call | tf_op jit(solution)/shard_map/down/pallas_call | solution.py:417
  146.7 0.2 add_convert_fusion.1
  146.9 1.6 collective-permute-start.19
  148.4 0.3 collective-permute-done.24
  148.7 0.2 add_convert_fusion
  149.0 1.6 collective-permute-start.25
  150.5 5.6 %collective-permute-done.19 = bf16[128,1024]{1,0:T(8,128)(2,1)S(1)} collective-permute-done((bf16[128,1024]{1,0:T(8,128)(2,1)S(1)}, bf16[128,1024]{1,0:T(8,128)(2,1)S(1)}, u32[]{:S(2)}, u32[]{:S(2)}) %collective-permute-start.19) | collective-permute-done | bytes 262176 | tf_op jit(solution)/shard_map/ppermute | solution.py:296
  156.1 0.6 dynamic-slice_bitcast_fusion.4
  156.8 2.5 %collective-permute-start.22 = (bf16[32,1024]{1,0:T(8,128)(2,1)S(1)}, bf16[32,1024]{1,0:T(8,128)(2,1)S(1)}, u32[]{:S(2)}, u32[]{:S(2)}) collective-permute-start(bf16[32,1024]{1,0:T(8,128)(2,1)S(1)} %get-tuple-element.42), channel_id=1, source_target_pairs={{0,12},{1,13},{2,14},{3,15},{4,0},{5,1},{6,2},{7,3},{8,4},{9,5},{1... | collective-permute-start | bytes 196616 | tf_op jit(solution)/shard_map/ppermute | solution.py:280
  159.3 1.1 collective-permute-start.20
  160.4 0.9 collective-permute-done.25
  161.4 3.5 %collective-permute-start.29 = (bf16[32,1024]{1,0:T(8,128)(2,1)S(1)}, bf16[32,1024]{1,0:T(8,128)(2,1)S(1)}, u32[]{:S(2)}, u32[]{:S(2)}) collective-permute-start(bf16[32,1024]{1,0:T(8,128)(2,1)S(1)} %get-tuple-element.38), channel_id=1, source_target_pairs={{0,28},{1,29},{2,30},{3,31},{4,16},{5,17},{6,18},{7,19},{8,20},{9,... | collective-permute-start | bytes 196616 | tf_op jit(solution)/shard_map/ppermute | solution.py:285
  164.9 0.4 collective-permute-start.28
  165.3 1.6 collective-permute-start.27
  166.9 0.9 collective-permute-start.26
  167.8 3.7 %collective-permute-done.28.o2 = bf16[32,1024]{1,0:T(8,128)(2,1)S(1)} collective-permute-done((bf16[32,1024]{1,0:T(8,128)(2,1)S(1)}, bf16[32,1024]{1,0:T(8,128)(2,1)S(1)}, u32[]{:S(2)}, u32[]{:S(2)}) %collective-permute-start.28) | collective-permute-done | bytes 65568 | tf_op jit(solution)/shard_map/ppermute | solution.py:285
  171.5 0.8 collective-permute-done.27.o1
  172.3 0.6 collective-permute-done.26.o0
  172.9 0.6 copy-done.18
  173.5 2.0 %closing.1 = (bf16[32,2048]{1,0:T(8,128)(2,1)}, bf16[32,2048]{1,0:T(8,128)(2,1)}) custom-call(s32[3]{0:T(128)} %pad_add_fusion.place, bf16[32,2048]{1,0:T(8,128)(2,1)} %get-tuple-element.26.own, bf16[32,1024]{1,0:T(8,128)(2,1)} %get-tuple-element.45.m0, bf16[32,1024]{1,0:T(8,128)(2,1)} %copy-done.14, bf16[32,1024]{1,0:T(8,128)(2,1)} %copy-done.13, ...), custom_call_target="tpu_custom_call" | custom-call | tf_op jit(solution)/shard_map/closing/pallas_call | solution.py:449
  (72 shorter events, 0.5 us)
Async XLA Ops:
  0.6 24.6 %collective-permute-start.2 = (bf16[64,2048]{1,0:T(8,128)(2,1)}, bf16[64,2048]{1,0:T(8,128)(2,1)}, u32[]{:S(2)}, u32[]{:S(2)}) collective-permute-start(bf16[64,2048]{1,0:T(8,128)(2,1)} %bitcast.63), channel_id=1, source_target_pairs={{0,12},{1,13},{2,14},{3,15},{4,0},{5,1},{6,2},{7,3},{8,4},{9,5},{1... | collective-permute-start | bytes 786440 | tf_op jit(solution)/shard_map/ppermute | solution.py:280
  5.7 23.8 %collective-permute-start.1 = (bf16[64,2048]{1,0:T(8,128)(2,1)}, bf16[64,2048]{1,0:T(8,128)(2,1)}, u32[]{:S(2)}, u32[]{:S(2)}) collective-permute-start(bf16[64,2048]{1,0:T(8,128)(2,1)} %bitcast.64), channel_id=1, source_target_pairs={{0,8},{1,9},{2,10},{3,11},{4,12},{5,13},{6,14},{7,15},{8,0},{9,1},... | collective-permute-start | bytes 786440 | tf_op jit(solution)/shard_map/ppermute | solution.py:280
  5.7 26.7 %collective-permute-start = (bf16[64,2048]{1,0:T(8,128)(2,1)}, bf16[64,2048]{1,0:T(8,128)(2,1)}, u32[]{:S(2)}, u32[]{:S(2)}) collective-permute-start(bf16[64,2048]{1,0:T(8,128)(2,1)} %bitcast.65), channel_id=1, source_target_pairs={{0,4},{1,5},{2,6},{3,7},{4,8},{5,9},{6,10},{7,11},{8,12},{9,13},{1... | collective-permute-start | bytes 786440 | tf_op jit(solution)/shard_map/ppermute | solution.py:280
  6.7 13.0 %collective-permute-start.3 = (bf16[2048,128]{1,0:T(8,128)(2,1)}, bf16[2048,128]{1,0:T(8,128)(2,1)S(1)}, u32[]{:S(2)}, u32[]{:S(2)}) collective-permute-start(bf16[2048,128]{1,0:T(8,128)(2,1)} %w0.1), channel_id=1, source_target_pairs={{0,2},{1,3},{2,0},{3,1},{4,6},{5,7},{6,4},{7,5},{8,10},{9,11},{10,... | collective-permute-start | bytes 1572872 | tf_op jit(solution)/shard_map/ppermute | solution.py:296
  9.6 10.1 %copy-start.19 = (f32[1,32,8]{1,2,0:T(8,128)S(1)}, f32[1,32,8]{1,2,0:T(8,128)}, u32[]{:S(2)}) copy-start(f32[1,32,8]{1,2,0:T(8,128)} %param.15) | copy-start | bytes 3076
  9.7 10.8 %copy-start.9 = (bf16[2048,128]{1,0:T(8,128)(2,1)S(1)}, bf16[2048,128]{1,0:T(8,128)(2,1)}, u32[]{:S(2)}) copy-start(bf16[2048,128]{1,0:T(8,128)(2,1)} %w0.1) | copy-start | bytes 1572868
  9.7 11.4 %copy-start.20 = (s32[1,32,8]{1,2,0:T(8,128)S(1)}, s32[1,32,8]{1,2,0:T(8,128)}, u32[]{:S(2)}) copy-start(s32[1,32,8]{1,2,0:T(8,128)} %param.14) | copy-start | bytes 3076
  19.8 14.0 %copy-start.10 = (bf16[2048,128]{1,0:T(8,128)(2,1)}, bf16[2048,128]{1,0:T(8,128)(2,1)S(1)}, u32[]{:S(2)}) copy-start(bf16[2048,128]{1,0:T(8,128)(2,1)S(1)} %collective-permute-done.3.w2) | copy-start | bytes 1572868
  19.8 2.9 %collective-permute-start.5 = (bf16[2048,128]{1,0:T(8,128)(2,1)S(1)}, bf16[2048,128]{1,0:T(8,128)(2,1)S(1)}, u32[]{:S(2)}, u32[]{:S(2)}) collective-permute-start(bf16[2048,128]{1,0:T(8,128)(2,1)S(1)} %collective-permute-done.3.w2), channel_id=1, source_target_pairs={{0,1},{1,0},{2,3},{3,2},{4,5},{5,4},{6,7},{7,6},{8,9},{9,8},{10,11... | collective-permute-start | bytes 1572872 | tf_op jit(solution)/shard_map/ppermute | solution.py:296
  20.5 12.0 %collective-permute-start.4 = (bf16[2048,128]{1,0:T(8,128)(2,1)S(1)}, bf16[2048,128]{1,0:T(8,128)(2,1)}, u32[]{:S(2)}, u32[]{:S(2)}) collective-permute-start(bf16[2048,128]{1,0:T(8,128)(2,1)S(1)} %copy-done.9), channel_id=1, source_target_pairs={{0,1},{1,0},{2,3},{3,2},{4,5},{5,4},{6,7},{7,6},{8,9},{9,8},{10,11... | collective-permute-start | bytes 1572872 | tf_op jit(solution)/shard_map/ppermute | solution.py:296
  22.7 11.1 %copy-start.11 = (bf16[2048,128]{1,0:T(8,128)(2,1)}, bf16[2048,128]{1,0:T(8,128)(2,1)S(1)}, u32[]{:S(2)}) copy-start(bf16[2048,128]{1,0:T(8,128)(2,1)S(1)} %collective-permute-done.5.w3) | copy-start | bytes 1572868
  22.7 9.8 %collective-permute-start.6 = (bf16[32,512]{1,0:T(8,128)(2,1)}, bf16[32,512]{1,0:T(8,128)(2,1)}, u32[]{:S(2)}, u32[]{:S(2)}) collective-permute-start(bf16[32,512]{1,0:T(8,128)(2,1)} %get-tuple-element.21), channel_id=1, source_target_pairs={{0,4},{1,5},{2,6},{3,7},{4,8},{5,9},{6,10},{7,11},{8,12},{9,13},{1... | collective-permute-start | bytes 98312 | tf_op jit(solution)/shard_map/ppermute | solution.py:280
  25.2 7.3 %collective-permute-start.7 = (bf16[32,512]{1,0:T(8,128)(2,1)}, bf16[32,512]{1,0:T(8,128)(2,1)}, u32[]{:S(2)}, u32[]{:S(2)}) collective-permute-start(bf16[32,512]{1,0:T(8,128)(2,1)} %get-tuple-element.22), channel_id=1, source_target_pairs={{0,8},{1,9},{2,10},{3,11},{4,12},{5,13},{6,14},{7,15},{8,0},{9,1},... | collective-permute-start | bytes 98312 | tf_op jit(solution)/shard_map/ppermute | solution.py:280
  29.5 4.2 %collective-permute-start.8 = (bf16[32,512]{1,0:T(8,128)(2,1)}, bf16[32,512]{1,0:T(8,128)(2,1)}, u32[]{:S(2)}, u32[]{:S(2)}) collective-permute-start(bf16[32,512]{1,0:T(8,128)(2,1)} %get-tuple-element.23), channel_id=1, source_target_pairs={{0,12},{1,13},{2,14},{3,15},{4,0},{5,1},{6,2},{7,3},{8,4},{9,5},{1... | collective-permute-start | bytes 98312 | tf_op jit(solution)/shard_map/ppermute | solution.py:280
  32.5 6.8 %copy-start.21 = (pred[512]{0:T(512)(128)(4,1)S(1)}, pred[512]{0:T(512)(128)(4,1)}, u32[]{:S(2)}) copy-start(pred[512]{0:T(512)(128)(4,1)} %broadcast_in_dim.63) | copy-start | bytes 1540
  37.7 6.6 %collective-permute-start.9 = (bf16[128,512]{1,0:T(8,128)(2,1)}, bf16[128,512]{1,0:T(8,128)(2,1)S(1)}, u32[]{:S(2)}, u32[]{:S(2)}) collective-permute-start(bf16[128,512]{1,0:T(8,128)(2,1)} %get-tuple-element.25), channel_id=1, source_target_pairs={{0,16},{16,0},{1,17},{17,1},{2,18},{18,2},{3,19},{19,3},{4,20},{20... | collective-permute-start | bytes 393224 | tf_op jit(solution)/shard_map/ppermute | solution.py:277
  44.3 75.6 %collective-permute-start.17 = (bf16[640,1536]{1,0:T(8,128)(2,1)S(1)}, bf16[640,1536]{1,0:T(8,128)(2,1)S(1)}, u32[]{:S(2)}, u32[]{:S(2)}) collective-permute-start(bf16[640,1536]{1,0:T(8,128)(2,1)S(1)} %slice_bitcast_fusion), channel_id=1, source_target_pairs={{0,16},{16,0},{1,17},{17,1},{2,18},{18,2},{3,19},{19,3},{4,20},{20... | collective-permute-start | bytes 5898248 | tf_op jit(solution)/shard_map/ppermute | solution.py:277
  46.8 9.3 %collective-permute-start.11 = (bf16[144,512]{1,0:T(8,128)(2,1)S(1)}, bf16[144,512]{1,0:T(8,128)(2,1)S(1)}, u32[]{:S(2)}, u32[]{:S(2)}) collective-permute-start(bf16[144,512]{1,0:T(8,128)(2,1)S(1)} %get-tuple-element.47), channel_id=1, source_target_pairs={{0,8},{1,9},{2,10},{3,11},{4,12},{5,13},{6,14},{7,15},{8,0},{9,1},... | collective-permute-start | bytes 442376 | tf_op jit(solution)/shard_map/ppermute | solution.py:280
  46.9 9.2 %collective-permute-start.10 = (bf16[144,512]{1,0:T(8,128)(2,1)S(1)}, bf16[144,512]{1,0:T(8,128)(2,1)S(1)}, u32[]{:S(2)}, u32[]{:S(2)}) collective-permute-start(bf16[144,512]{1,0:T(8,128)(2,1)S(1)} %get-tuple-element.47), channel_id=1, source_target_pairs={{0,4},{1,5},{2,6},{3,7},{4,8},{5,9},{6,10},{7,11},{8,12},{9,13},{1... | collective-permute-start | bytes 442376 | tf_op jit(solution)/shard_map/ppermute | solution.py:280
  48.6 8.2 %collective-permute-start.12 = (bf16[144,512]{1,0:T(8,128)(2,1)S(1)}, bf16[144,512]{1,0:T(8,128)(2,1)S(1)}, u32[]{:S(2)}, u32[]{:S(2)}) collective-permute-start(bf16[144,512]{1,0:T(8,128)(2,1)S(1)} %get-tuple-element.47), channel_id=1, source_target_pairs={{0,12},{1,13},{2,14},{3,15},{4,0},{5,1},{6,2},{7,3},{8,4},{9,5},{1... | collective-permute-start | bytes 442376 | tf_op jit(solution)/shard_map/ppermute | solution.py:280
  52.1 58.2 %collective-permute-start.16 = (bf16[384,1536]{1,0:T(8,128)(2,1)S(1)}, bf16[384,1536]{1,0:T(8,128)(2,1)S(1)}, u32[]{:S(2)}, u32[]{:S(2)}) collective-permute-start(bf16[384,1536]{1,0:T(8,128)(2,1)S(1)} %slice_bitcast_fusion.1), channel_id=1, source_target_pairs={{0,16},{16,0},{1,17},{17,1},{2,18},{18,2},{3,19},{19,3},{4,20},{20... | collective-permute-start | bytes 3538952 | tf_op jit(solution)/shard_map/ppermute | solution.py:277
  56.9 53.5 %copy-start.2 = (bf16[4,144,512]{2,1,0:T(8,128)(2,1)}, bf16[4,144,512]{2,1,0:T(8,128)(2,1)S(1)}, u32[]{:S(2)}) copy-start(bf16[4,144,512]{2,1,0:T(8,128)(2,1)S(1)} %pad_maximum_fusion.blocks) | copy-start | bytes 1769476
  56.9 9.9 %collective-permute-start.13 = (bf16[4,144,512]{2,1,0:T(8,128)(2,1)S(1)}, bf16[4,144,512]{2,1,0:T(8,128)(2,1)S(1)}, u32[]{:S(2)}, u32[]{:S(2)}) collective-permute-start(bf16[4,144,512]{2,1,0:T(8,128)(2,1)S(1)} %pad_maximum_fusion.blocks), channel_id=1, source_target_pairs={{0,2},{1,3},{2,0},{3,1},{4,6},{5,7},{6,4},{7,5},{8,10},{9,11},{10,... | collective-permute-start | bytes 1769480 | tf_op jit(solution)/shard_map/ppermute | solution.py:296
  58.5 51.9 %collective-permute-start.14 = (bf16[4,144,512]{2,1,0:T(8,128)(2,1)S(1)}, bf16[4,144,512]{2,1,0:T(8,128)(2,1)S(1)}, u32[]{:S(2)}, u32[]{:S(2)}) collective-permute-start(bf16[4,144,512]{2,1,0:T(8,128)(2,1)S(1)} %pad_maximum_fusion.blocks), channel_id=1, source_target_pairs={{0,1},{1,0},{2,3},{3,2},{4,5},{5,4},{6,7},{7,6},{8,9},{9,8},{10,11... | collective-permute-start | bytes 1769480 | tf_op jit(solution)/shard_map/ppermute | solution.py:296
  66.8 43.5 %copy-start.4 = (bf16[4,144,512]{2,1,0:T(8,128)(2,1)}, bf16[4,144,512]{2,1,0:T(8,128)(2,1)S(1)}, u32[]{:S(2)}) copy-start(bf16[4,144,512]{2,1,0:T(8,128)(2,1)S(1)} %collective-permute-done.13.blocks_x) | copy-start | bytes 1769476
  66.8 43.5 %collective-permute-start.15 = (bf16[4,144,512]{2,1,0:T(8,128)(2,1)S(1)}, bf16[4,144,512]{2,1,0:T(8,128)(2,1)S(1)}, u32[]{:S(2)}, u32[]{:S(2)}) collective-permute-start(bf16[4,144,512]{2,1,0:T(8,128)(2,1)S(1)} %collective-permute-done.13.blocks_x), channel_id=1, source_target_pairs={{0,1},{1,0},{2,3},{3,2},{4,5},{5,4},{6,7},{7,6},{8,9},{9,8},{10,11... | collective-permute-start | bytes 1769480 | tf_op jit(solution)/shard_map/ppermute | solution.py:296
  110.3 1.0 copy-start.1
  110.3 1.2 copy-start.5
  110.3 1.4 copy-start.6
  119.9 1.3 copy-start
  126.6 14.7 %collective-permute-start.23 = (bf16[512,768]{1,0:T(8,128)(2,1)}, bf16[512,768]{1,0:T(8,128)(2,1)S(1)}, u32[]{:S(2)}, u32[]{:S(2)}) collective-permute-start(bf16[512,768]{1,0:T(8,128)(2,1)} %last_gate_up.1.inner), channel_id=1, source_target_pairs={{0,16},{16,0},{1,17},{17,1},{2,18},{18,2},{3,19},{19,3},{4,20},{20... | collective-permute-start | bytes 2359304 | tf_op jit(solution)/shard_map/ppermute | solution.py:277
  132.5 14.1 %copy-start.8 = (bf16[256,1024]{1,0:T(8,128)(2,1)S(1)}, bf16[256,1024]{1,0:T(8,128)(2,1)}, u32[]{:S(2)}) copy-start(bf16[256,1024]{1,0:T(8,128)(2,1)} %get-tuple-element.32) | copy-start | bytes 1572868
  132.5 14.1 %collective-permute-start.18 = (bf16[256,1024]{1,0:T(8,128)(2,1)}, bf16[256,1024]{1,0:T(8,128)(2,1)S(1)}, u32[]{:S(2)}, u32[]{:S(2)}) collective-permute-start(bf16[256,1024]{1,0:T(8,128)(2,1)} %get-tuple-element.33), channel_id=1, source_target_pairs={{0,1},{1,0},{2,3},{3,2},{4,5},{5,4},{6,7},{7,6},{8,9},{9,8},{10,11... | collective-permute-start | bytes 1572872 | tf_op jit(solution)/shard_map/ppermute | solution.py:296
  141.3 0.9 copy-start.3
  146.6 2.1 %copy-start.7 = (bf16[256,1024]{1,0:T(8,128)(2,1)S(1)}, bf16[256,1024]{1,0:T(8,128)(2,1)}, u32[]{:S(2)}) copy-start(bf16[256,1024]{1,0:T(8,128)(2,1)} %get-tuple-element.34) | copy-start | bytes 1572868
  146.6 2.1 %collective-permute-start.24 = (bf16[256,1024]{1,0:T(8,128)(2,1)}, bf16[256,1024]{1,0:T(8,128)(2,1)S(1)}, u32[]{:S(2)}, u32[]{:S(2)}) collective-permute-start(bf16[256,1024]{1,0:T(8,128)(2,1)} %get-tuple-element.35), channel_id=1, source_target_pairs={{0,1},{1,0},{2,3},{3,2},{4,5},{5,4},{6,7},{7,6},{8,9},{9,8},{10,11... | collective-permute-start | bytes 1572872 | tf_op jit(solution)/shard_map/ppermute | solution.py:296
  146.9 9.2 %collective-permute-start.19 = (bf16[128,1024]{1,0:T(8,128)(2,1)S(1)}, bf16[128,1024]{1,0:T(8,128)(2,1)S(1)}, u32[]{:S(2)}, u32[]{:S(2)}) collective-permute-start(bf16[128,1024]{1,0:T(8,128)(2,1)S(1)} %slice.25), channel_id=1, source_target_pairs={{0,2},{1,3},{2,0},{3,1},{4,6},{5,7},{6,4},{7,5},{8,10},{9,11},{10,... | collective-permute-start | bytes 786440 | tf_op jit(solution)/shard_map/ppermute | solution.py:296
  149.0 12.3 %collective-permute-start.25 = (bf16[128,1024]{1,0:T(8,128)(2,1)S(1)}, bf16[128,1024]{1,0:T(8,128)(2,1)S(1)}, u32[]{:S(2)}, u32[]{:S(2)}) collective-permute-start(bf16[128,1024]{1,0:T(8,128)(2,1)S(1)} %slice.27), channel_id=1, source_target_pairs={{0,2},{1,3},{2,0},{3,1},{4,6},{5,7},{6,4},{7,5},{8,10},{9,11},{10,... | collective-permute-start | bytes 786440 | tf_op jit(solution)/shard_map/ppermute | solution.py:296
  156.8 8.5 %collective-permute-start.22 = (bf16[32,1024]{1,0:T(8,128)(2,1)S(1)}, bf16[32,1024]{1,0:T(8,128)(2,1)S(1)}, u32[]{:S(2)}, u32[]{:S(2)}) collective-permute-start(bf16[32,1024]{1,0:T(8,128)(2,1)S(1)} %get-tuple-element.42), channel_id=1, source_target_pairs={{0,12},{1,13},{2,14},{3,15},{4,0},{5,1},{6,2},{7,3},{8,4},{9,5},{1... | collective-permute-start | bytes 196616 | tf_op jit(solution)/shard_map/ppermute | solution.py:280
  159.3 7.6 %collective-permute-start.21 = (bf16[32,1024]{1,0:T(8,128)(2,1)S(1)}, bf16[32,1024]{1,0:T(8,128)(2,1)S(1)}, u32[]{:S(2)}, u32[]{:S(2)}) collective-permute-start(bf16[32,1024]{1,0:T(8,128)(2,1)S(1)} %get-tuple-element.43), channel_id=1, source_target_pairs={{0,8},{1,9},{2,10},{3,11},{4,12},{5,13},{6,14},{7,15},{8,0},{9,1},... | collective-permute-start | bytes 196616 | tf_op jit(solution)/shard_map/ppermute | solution.py:280
  159.3 8.5 %collective-permute-start.20 = (bf16[32,1024]{1,0:T(8,128)(2,1)S(1)}, bf16[32,1024]{1,0:T(8,128)(2,1)S(1)}, u32[]{:S(2)}, u32[]{:S(2)}) collective-permute-start(bf16[32,1024]{1,0:T(8,128)(2,1)S(1)} %get-tuple-element.44), channel_id=1, source_target_pairs={{0,4},{1,5},{2,6},{3,7},{4,8},{5,9},{6,10},{7,11},{8,12},{9,13},{1... | collective-permute-start | bytes 196616 | tf_op jit(solution)/shard_map/ppermute | solution.py:280
  161.4 6.5 %collective-permute-start.29 = (bf16[32,1024]{1,0:T(8,128)(2,1)S(1)}, bf16[32,1024]{1,0:T(8,128)(2,1)S(1)}, u32[]{:S(2)}, u32[]{:S(2)}) collective-permute-start(bf16[32,1024]{1,0:T(8,128)(2,1)S(1)} %get-tuple-element.38), channel_id=1, source_target_pairs={{0,28},{1,29},{2,30},{3,31},{4,16},{5,17},{6,18},{7,19},{8,20},{9,... | collective-permute-start | bytes 196616 | tf_op jit(solution)/shard_map/ppermute | solution.py:285
  164.9 6.7 %collective-permute-start.28 = (bf16[32,1024]{1,0:T(8,128)(2,1)S(1)}, bf16[32,1024]{1,0:T(8,128)(2,1)S(1)}, u32[]{:S(2)}, u32[]{:S(2)}) collective-permute-start(bf16[32,1024]{1,0:T(8,128)(2,1)S(1)} %get-tuple-element.39), channel_id=1, source_target_pairs={{0,24},{1,25},{2,26},{3,27},{4,28},{5,29},{6,30},{7,31},{8,16},{9,... | collective-permute-start | bytes 196616 | tf_op jit(solution)/shard_map/ppermute | solution.py:285
  165.3 7.6 %copy-start.12 = (bf16[32,1024]{1,0:T(8,128)(2,1)}, bf16[32,1024]{1,0:T(8,128)(2,1)S(1)}, u32[]{:S(2)}) copy-start(bf16[32,1024]{1,0:T(8,128)(2,1)S(1)} %collective-permute-done.22.m3) | copy-start | bytes 196612
  165.3 7.0 %collective-permute-start.27 = (bf16[32,1024]{1,0:T(8,128)(2,1)S(1)}, bf16[32,1024]{1,0:T(8,128)(2,1)S(1)}, u32[]{:S(2)}, u32[]{:S(2)}) collective-permute-start(bf16[32,1024]{1,0:T(8,128)(2,1)S(1)} %get-tuple-element.40), channel_id=1, source_target_pairs={{0,20},{1,21},{2,22},{3,23},{4,24},{5,25},{6,26},{7,27},{8,28},{9,... | collective-permute-start | bytes 196616 | tf_op jit(solution)/shard_map/ppermute | solution.py:285
  166.9 6.0 %copy-start.13 = (bf16[32,1024]{1,0:T(8,128)(2,1)}, bf16[32,1024]{1,0:T(8,128)(2,1)S(1)}, u32[]{:S(2)}) copy-start(bf16[32,1024]{1,0:T(8,128)(2,1)S(1)} %collective-permute-done.21.m2) | copy-start | bytes 196612
  166.9 6.0 %collective-permute-start.26 = (bf16[32,1024]{1,0:T(8,128)(2,1)S(1)}, bf16[32,1024]{1,0:T(8,128)(2,1)S(1)}, u32[]{:S(2)}, u32[]{:S(2)}) collective-permute-start(bf16[32,1024]{1,0:T(8,128)(2,1)S(1)} %get-tuple-element.41), channel_id=1, source_target_pairs={{0,16},{1,17},{2,18},{3,19},{4,20},{5,21},{6,22},{7,23},{8,24},{9,... | collective-permute-start | bytes 196616 | tf_op jit(solution)/shard_map/ppermute | solution.py:285
  167.8 5.1 %copy-start.14 = (bf16[32,1024]{1,0:T(8,128)(2,1)}, bf16[32,1024]{1,0:T(8,128)(2,1)S(1)}, u32[]{:S(2)}) copy-start(bf16[32,1024]{1,0:T(8,128)(2,1)S(1)} %collective-permute-done.20.m1) | copy-start | bytes 196612
  167.8 5.1 %copy-start.15 = (bf16[32,1024]{1,0:T(8,128)(2,1)}, bf16[32,1024]{1,0:T(8,128)(2,1)S(1)}, u32[]{:S(2)}) copy-start(bf16[32,1024]{1,0:T(8,128)(2,1)S(1)} %collective-permute-done.29.o3) | copy-start | bytes 196612
  171.5 1.4 copy-start.16
  172.3 0.6 copy-start.17
  172.9 0.6 copy-start.18

commit v3 on v2

--- a/solution.py
+++ b/solution.py
@@ -128,7 +128,7 @@
     return (stream_out[None], normed_out[None])
 
 
-VMEM_BYTES = 56 * 1024 * 1024
+MIB = 1024 * 1024
 BF16, F32 = jnp.bfloat16, jnp.float32
 
 
@@ -148,11 +148,11 @@
     return jnp.dot(a, b, preferred_element_type=F32)
 
 
-def kernel_params():
-    return pltpu.CompilerParams(vmem_limit_bytes=VMEM_BYTES)
-
-
-def proj_kernel(place, a0, a1, a2, a3, w0, w1, w2, w3, r0, r1, r2, r3, base_ref, send_ref, rows, part):
+def kernel_params(mib):
+    return pltpu.CompilerParams(vmem_limit_bytes=mib * MIB)
+
+
+def proj_kernel(place, a0, a1, a2, a3, w0, w1, w2, w3, keep_ref, send_ref, rows, part):
     outer, inner, dp = place[0], place[1], place[2]
     full = a0.shape[0]
     half = full // 2
@@ -163,13 +163,22 @@
     for j, w in enumerate((w0, w1, w2, w3)):
         spot = pl.multiple_of((inner ^ j) * block, block)
         part[:, pl.ds(spot, block)] = dot(rows[...], w[...]).astype(BF16)
-    for s, r in enumerate((r0, r1, r2, r3)):
-        spot = lax.rem(outer + 4 - s, 4)
+    for spot in range(4):
         mine = pl.multiple_of(spot * full + dp * half, half)
         other = pl.multiple_of(spot * full + (1 - dp) * half, half)
-        out = pl.ds(pl.multiple_of(spot * half, half), half)
-        base_ref[out, :] = r[...].astype(F32) + part[pl.ds(mine, half), :].astype(F32)
-        send_ref[out, :] = part[pl.ds(other, half), :]
+        keep_ref[spot * half : (spot + 1) * half, :] = part[pl.ds(mine, half), :]
+        send_ref[spot * half : (spot + 1) * half, :] = part[pl.ds(other, half), :]
+
+
+def stream_kernel(place, keep, arrived, r0, r1, r2, r3, share, block_ref):
+    outer = place[0]
+    count = keep.shape[0]
+    small = r0.shape[0]
+    for s, r in enumerate((r0, r1, r2, r3)):
+        rows = pl.ds(pl.multiple_of(lax.rem(outer + 4 - s, 4) * small, small), small)
+        product = keep[rows, :].astype(F32) + arrived[rows, :].astype(F32)
+        block_ref[rows, :] = (r[...].astype(F32) + product).astype(BF16)
+    block_ref[count:, :] = share[...]
 
 
 def first_gate_kernel(
@@ -299,9 +308,11 @@
         return lax.optimization_barrier((x, *results))[0]
 
     depth = half_width * 3 // 8
-    a = [attn[0]] + [shift_outer(attn[0], s) for s in (1, 2, 3)]
+    early_piece = w_gate_up[0, :depth]
+    sent = after(attn[0], early_piece)
+    a = [attn[0]] + [shift_outer(sent, s) for s in (1, 2, 3)]
     w_x = swap_inner(w_out, 2)
-    gate_up_early = swap_dp(w_gate_up[0, :depth])
+    gate_up_early = swap_dp(early_piece)
     w_c = swap_inner(after(w_out, w_x), 1)
     w_cx = swap_inner(w_x, 1)
 
@@ -320,25 +331,29 @@
     share = jnp.where(spots[None, :, None], share[:, None, :], 0.0)
     share = share.reshape(expert_count, quarter).astype(BF16)
 
-    base, send = pl.pallas_call(
+    product = jax.ShapeDtypeStruct((4 * rows_here, quarter), BF16)
+    keep, send = pl.pallas_call(
         proj_kernel,
-        out_shape=(
-            jax.ShapeDtypeStruct((4 * rows_here, quarter), F32),
-            jax.ShapeDtypeStruct((4 * rows_here, quarter), BF16),
-        ),
-        in_specs=[smem] + [vmem] * 12,
+        out_shape=(product, product),
+        in_specs=[smem] + [vmem] * 8,
         out_specs=(vmem, vmem),
         scratch_shapes=[
             pltpu.VMEM((8 * rows_here, attn.shape[2]), BF16),
             pltpu.VMEM((8 * rows_here, quarter), BF16),
         ],
-        compiler_params=kernel_params(),
+        compiler_params=kernel_params(16),
         name="projection",
-    )(place, *a, w_out, w_c, w_x, w_cx, *r)
-    arrived = swap_dp(send)
+    )(place, *a, w_out, w_c, w_x, w_cx)
+    arrived = swap_dp(after(send, gate_up_early, *r[1:]))
     gate_up_late = swap_dp(after(w_gate_up[0, depth:], arrived))
-    block = (base + arrived.astype(F32)).astype(BF16)
-    block = jnp.concatenate([block, share], axis=0)
+    block = pl.pallas_call(
+        stream_kernel,
+        out_shape=jax.ShapeDtypeStruct((4 * rows_here + expert_count, quarter), BF16),
+        in_specs=[smem] + [vmem] * 7,
+        out_specs=vmem,
+        compiler_params=kernel_params(8),
+        name="stream",
+    )(place, keep, arrived, *r, share)
 
     blocks = jnp.stack([block] + [shift_outer(block, s) for s in (1, 2, 3)])
     blocks_x = swap_inner(blocks, 2)
@@ -379,7 +394,7 @@
             fixed(rows_here, model_width),
         ),
         scratch_shapes=[pltpu.VMEM((row_total, model_width), BF16)],
-        compiler_params=kernel_params(),
+        compiler_params=kernel_params(24),
         name="first_gate_up",
     )(
         place,
@@ -406,7 +421,7 @@
             up_cols(half_width - depth),
         ],
         out_specs=out_cols,
-        compiler_params=kernel_params(),
+        compiler_params=kernel_params(16),
         name="last_gate_up",
     )(gate, up, last_rows, share_rows, gate_up_late, gate_up_late)
     inner_other = swap_dp(inner)
@@ -423,18 +438,19 @@
                 pl.BlockSpec((hidden, 256), lambda i: (0, i)),
             ],
             out_specs=(spec, spec),
-            compiler_params=kernel_params(),
+            compiler_params=kernel_params(12),
             name="down",
         )(rows, w_down[0])
 
     def add(x, y):
         return (x.astype(F32) + y.astype(F32)).astype(BF16)
 
-    def sum_inner(rows):
+    def sum_inner(rows, *earlier):
         keep, send = down(rows)
         near = add(keep, swap_inner(send, 1))
         count = near.shape[0] // 2
-        near = add(near[:count], swap_inner(near[count:], 2))
+        far = near[count:] if not earlier else after(near[count:], *earlier)
+        near = add(near[:count], swap_inner(far, 2))
         return near.reshape(4, rows_here, half_width)
 
     def outer_piece(near, s):
@@ -442,7 +458,7 @@
 
     near = sum_inner(inner)
     mine = [outer_piece(near, 0)] + [shift_outer(outer_piece(near, s), s) for s in (1, 2, 3)]
-    near = sum_inner(inner_other)
+    near = sum_inner(after(inner_other, near), *mine[1:])
     others = [cross_outer(outer_piece(near, s), s) for s in range(4)]
 
     out = jax.ShapeDtypeStruct((rows_here, model_width), BF16)
@@ -451,7 +467,7 @@
         out_shape=(out, out),
         in_specs=[smem] + [vmem] * 10,
         out_specs=(vmem, vmem),
-        compiler_params=kernel_params(),
+        compiler_params=kernel_params(8),
         name="closing",
     )(place, stream_own, *mine, *others, gain_final[None])
     return (stream_out[None], normed_out[None])

time: 176 us -> 167 us (0.949)
  Pallas kernels: 28.3 us -> 18.2 us
  local copies, waits for them, and re-layouts: 11.8 us -> 20 us
  starting transfers between devices: 35.6 us -> 32.8 us
  other arithmetic: 3.7 us -> 1.46 us
    ppermute x4, waiting for transfers between devices: 57.3 us -> 15.5 us  [swap_dp(): return lax.ppermute(x, 'dp', [(0, 1), (1, 0)])]
    ppermute x12, waiting for transfers between devices: 8.51 us -> 32.5 us  [shift_outer(): lax.ppermute(x, 'expert', [(i, (i + 4 * s) % expert_count) for i in range...]
    ppermute x10, waiting for transfers between devices: 23.5 us -> 40.8 us  [swap_inner(): return lax.ppermute(x, 'expert', [(i, i ^ j) for i in range(expert_count)])]
    unnamed x44 -> x48, local copies, waits for them, and re-layouts: 4.24 us -> 13.7 us
    pallas_call x2, Pallas kernels: 8.84 us -> 3.7 us  [down(): pl.pallas_call(down_kernel, grid=(half_width // 256,), out_shape=(out, ou...]
    pallas_call x1, Pallas kernels: 8.14 us -> 5.55 us  [body_paired(): pl.pallas_call(first_gate_kernel, grid=(steps,), out_shape=(jax.ShapeDtyp...]
    broadcast_in_dim x4, local copies, waits for them, and re-layouts: 2.28 us -> 0.29 us  [body_paired(): share = jnp.where(spots[None, :, None], share[:, None, :], 0.0)]
    ppermute x4, starting transfers between devices: 5.12 us -> 3.35 us  [swap_dp(): return lax.ppermute(x, 'dp', [(0, 1), (1, 0)])]
  transfers between devices with their start and end apart: 30 -> 30, of which waited for: 15 -> 18; matrix products, arithmetic and copies ran while one was open for 6% -> 5% of each run, Pallas kernels for 10% -> 6%
where the time goes in v3:
time: 167 us
  waiting for transfers between devices  92.6 us (55%)
  starting transfers between devices  32.8 us (20%)
  local copies, waits for them, and re-layouts  20 us (12%)
  Pallas kernels  18.2 us (11%)
    ppermute x10, waiting for transfers between devices, swap_inner(): return lax.ppermute(x, 'expert', [(i, i ^ j) for i in range(expert_count)])  40.8 us
    ppermute x12, waiting for transfers between devices, shift_outer(): lax.ppermute(x, 'expert', [(i, (i + 4 * s) % expert_count) for i in range...  32.5 us
    ppermute x12, starting transfers between devices, shift_outer(): lax.ppermute(x, 'expert', [(i, (i + 4 * s) % expert_count) for i in range...  15.6 us
    ppermute x4, waiting for transfers between devices, swap_dp(): return lax.ppermute(x, 'dp', [(0, 1), (1, 0)])  15.5 us
    unnamed x48, local copies, waits for them, and re-layouts  13.7 us
    ppermute x10, starting transfers between devices, swap_inner(): return lax.ppermute(x, 'expert', [(i, i ^ j) for i in range(expert_count)])  7.77 us
    ppermute x4, starting transfers between devices, cross_outer(): lax.ppermute(x, ('dp', 'expert'), [(d * expert_count + i, (1 - d) * exper...  6.1 us
    pallas_call x1, Pallas kernels, body_paired(): pl.pallas_call(first_gate_kernel, grid=(steps,), out_shape=(jax.ShapeDtyp...  5.55 us
  transfers between devices with their start and end apart: 30, of which 18 were waited for; matrix products, arithmetic and copies ran while one was open for 5% of the time, Pallas kernels for 6%

profile of v3, /device:TPU:0, one launch (start us, length us, event | category | flops | bytes accessed | tf_op | source)
XLA Modules:
  0.0 166.7 jit_solution(1794997721685946289)
XLA Ops:
  0.6 3.0 %collective-permute-start.3 = (bf16[2048,128]{1,0:T(8,128)(2,1)}, bf16[2048,128]{1,0:T(8,128)(2,1)S(1)}, u32[]{:S(2)}, u32[]{:S(2)}) collective-permute-start(bf16[2048,128]{1,0:T(8,128)(2,1)} %w0.1), channel_id=1, source_target_pairs={{0,2},{1,3},{2,0},{3,1},{4,6},{5,7},{6,4},{7,5},{8,10},{9,11},{10,... | collective-permute-start | bytes 1572872 | tf_op jit(solution)/shard_map/ppermute | solution.py:305
  3.6 12.1 %collective-permute-done.3.w2 = bf16[2048,128]{1,0:T(8,128)(2,1)S(1)} collective-permute-done((bf16[2048,128]{1,0:T(8,128)(2,1)}, bf16[2048,128]{1,0:T(8,128)(2,1)S(1)}, u32[]{:S(2)}, u32[]{:S(2)}) %collective-permute-start.3) | collective-permute-done | bytes 524320 | tf_op jit(solution)/shard_map/ppermute | solution.py:305
  15.8 0.8 copy-done.2
  16.6 2.4 %slice_bitcast_fusion.1 = bf16[384,1536]{1,0:T(8,128)(2,1)} fusion(bf16[1,1024,1536]{2,1,0:T(8,128)(2,1)} %param.17), kind=kLoop, calls=%fused_computation.1 | loop fusion | bytes 2359296 | tf_op jit(solution)/shard_map/squeeze | solution.py:311
  18.9 1.8 %collective-permute-start.6 = (bf16[384,1536]{1,0:T(8,128)(2,1)}, bf16[384,1536]{1,0:T(8,128)(2,1)}, u32[]{:S(2)}, u32[]{:S(2)}) collective-permute-start(bf16[384,1536]{1,0:T(8,128)(2,1)} %slice_bitcast_fusion.1), channel_id=1, source_target_pairs={{0,16},{16,0},{1,17},{17,1},{2,18},{18,2},{3,19},{19,3},{4,20},{20... | collective-permute-start | bytes 3538952 | tf_op jit(solution)/shard_map/ppermute | solution.py:286
  20.7 3.6 %collective-permute-start.2 = (bf16[64,2048]{1,0:T(8,128)(2,1)S(1)}, bf16[64,2048]{1,0:T(8,128)(2,1)S(1)}, u32[]{:S(2)}, u32[]{:S(2)}) collective-permute-start(bf16[64,2048]{1,0:T(8,128)(2,1)S(1)} %bitcast.61), channel_id=1, source_target_pairs={{0,12},{1,13},{2,14},{3,15},{4,0},{5,1},{6,2},{7,3},{8,4},{9,5},{1... | collective-permute-start | bytes 786440 | tf_op jit(solution)/shard_map/ppermute | solution.py:289
  24.3 1.0 collective-permute-start
  25.3 0.8 copy-done.4
  26.1 3.0 %slice_bitcast_fusion = bf16[640,1536]{1,0:T(8,128)(2,1)} fusion(bf16[1,1024,1536]{2,1,0:T(8,128)(2,1)} %param.17), kind=kLoop, calls=%fused_computation | loop fusion | bytes 3932160 | tf_op jit(solution)/shard_map/squeeze | solution.py:348
  29.1 0.6 dynamic-slice_bitcast_fusion.8
  29.8 1.3 collective-permute-done.2.a3
  31.1 0.7 copy-done.7
  31.8 1.2 collective-permute-start.7
  32.9 15.1 %collective-permute-done.1.a2 = bf16[64,2048]{1,0:T(8,128)(2,1)S(1)} collective-permute-done((bf16[64,2048]{1,0:T(8,128)(2,1)S(1)}, bf16[64,2048]{1,0:T(8,128)(2,1)S(1)}, u32[]{:S(2)}, u32[]{:S(2)}) %collective-permute-start.1) | collective-permute-done | bytes 262176 | tf_op jit(solution)/shard_map/ppermute | solution.py:289
  48.1 0.7 copy-done.9
  48.8 0.7 copy-done.11
  50.3 1.2 copy-done.3
  51.4 1.0 copy-done.5
  52.5 0.9 copy-done.8
  53.4 0.9 copy-done.10
  54.4 0.9 copy-done.12
  55.3 3.2 %projection.1 = (bf16[128,512]{1,0:T(8,128)(2,1)S(1)}, bf16[128,512]{1,0:T(8,128)(2,1)}) custom-call(s32[3]{0:T(128)S(1)} %pad_add_fusion.place, bf16[64,2048]{1,0:T(8,128)(2,1)S(1)} %bitcast.64, bf16[64,2048]{1,0:T(8,128)(2,1)S(1)} %copy-done.12, bf16[64,2048]{1,0:T(8,128)(2,1)S(1)} %copy-done.10, bf16[64,2048]{1,0:T(8,128)(2,1)S(1)} %copy-done.8, ...), custom_call_target="tpu_custom_call" | custom-call | tf_op jit(solution)/shard_map/projection/pallas_call | solution.py:335
  58.6 0.6 copy-done.14
  59.2 0.6 copy-done.16
  59.8 0.6 copy-done.18
  60.4 0.5 collective-permute-start.10
  61.1 4.5 %collective-permute-done.10.arrived = bf16[128,512]{1,0:T(8,128)(2,1)S(1)} collective-permute-done((bf16[128,512]{1,0:T(8,128)(2,1)}, bf16[128,512]{1,0:T(8,128)(2,1)S(1)}, u32[]{:S(2)}, u32[]{:S(2)}) %collective-permute-start.10) | collective-permute-done | bytes 131104 | tf_op jit(solution)/shard_map/ppermute | solution.py:286
  65.6 0.5 collective-permute-start.17
  66.1 0.7 select_reduce_fusion
  67.0 0.7 copy-done.13
  67.7 0.8 copy-done.15
  68.5 0.8 copy-done.17
  69.2 0.8 copy-done.19
  70.0 0.6 stream.1
  70.6 4.4 %collective-permute-start.13 = (bf16[144,512]{1,0:T(8,128)(2,1)S(1)}, bf16[144,512]{1,0:T(8,128)(2,1)S(1)}, u32[]{:S(2)}, u32[]{:S(2)}) collective-permute-start(bf16[144,512]{1,0:T(8,128)(2,1)S(1)} %stream.1), channel_id=1, source_target_pairs={{0,12},{1,13},{2,14},{3,15},{4,0},{5,1},{6,2},{7,3},{8,4},{9,5},{1... | collective-permute-start | bytes 442376 | tf_op jit(solution)/shard_map/ppermute | solution.py:289
  75.0 0.6 collective-permute-start.11
  75.7 3.2 %collective-permute-done.13 = bf16[144,512]{1,0:T(8,128)(2,1)S(1)} collective-permute-done((bf16[144,512]{1,0:T(8,128)(2,1)S(1)}, bf16[144,512]{1,0:T(8,128)(2,1)S(1)}, u32[]{:S(2)}, u32[]{:S(2)}) %collective-permute-start.13) | collective-permute-done | bytes 147488 | tf_op jit(solution)/shard_map/ppermute | solution.py:289
  78.9 7.0 %collective-permute-done.12 = bf16[144,512]{1,0:T(8,128)(2,1)S(1)} collective-permute-done((bf16[144,512]{1,0:T(8,128)(2,1)S(1)}, bf16[144,512]{1,0:T(8,128)(2,1)S(1)}, u32[]{:S(2)}, u32[]{:S(2)}) %collective-permute-start.12) | collective-permute-done | bytes 147488 | tf_op jit(solution)/shard_map/ppermute | solution.py:289
  86.0 1.6 collective-permute-start.14
  87.6 12.0 %collective-permute-done.14.blocks_x = bf16[4,144,512]{2,1,0:T(8,128)(2,1)S(1)} collective-permute-done((bf16[4,144,512]{2,1,0:T(8,128)(2,1)S(1)}, bf16[4,144,512]{2,1,0:T(8,128)(2,1)S(1)}, u32[]{:S(2)}, u32[]{:S(2)}) %collective-permute-start.14) | collective-permute-done | bytes 589856 | tf_op jit(solution)/shard_map/ppermute | solution.py:305
  99.6 2.0 %collective-permute-done.16.blocks_cx = bf16[4,144,512]{2,1,0:T(8,128)(2,1)S(1)} collective-permute-done((bf16[4,144,512]{2,1,0:T(8,128)(2,1)S(1)}, bf16[4,144,512]{2,1,0:T(8,128)(2,1)S(1)}, u32[]{:S(2)}, u32[]{:S(2)}) %collective-permute-start.16) | collective-permute-done | bytes 589856 | tf_op jit(solution)/shard_map/ppermute | solution.py:305
  101.6 5.6 %first_gate_up.1 = (f32[512,768]{1,0:T(8,128)S(1)}, f32[512,768]{1,0:T(8,128)S(1)}, bf16[512,640]{1,0:T(8,128)(2,1)S(1)}, f32[512,128]{1,0:T(8,128)S(1)}, bf16[32,2048]{1,0:T(8,128)(2,1)S(1)}) custom-call(s32[3]{0:T(128)S(1)} %pad_add_fusion.place, bf16[4,144,512]{2,1,0:T(8,128)(2,1)S(1)} %pad_maximum_fusion.blocks, ...), custom_call_target="tpu_custom_call" | custom-call | tf_op jit(solution)/shard_map/first_gate_up/pallas_call | solution.py:370
  107.1 1.7 %collective-permute-done.17.gw.uw = bf16[640,1536]{1,0:T(8,128)(2,1)} collective-permute-done((bf16[640,1536]{1,0:T(8,128)(2,1)}, bf16[640,1536]{1,0:T(8,128)(2,1)}, u32[]{:S(2)}, u32[]{:S(2)}) %collective-permute-start.17) | collective-permute-done | bytes 1966112 | tf_op jit(solution)/shard_map/ppermute | solution.py:286
  108.9 3.7 %last_gate_up.1.inner = bf16[512,768]{1,0:T(8,128)(2,1)S(1)} custom-call(f32[512,768]{1,0:T(8,128)S(1)} %get-tuple-element.33.gate, f32[512,768]{1,0:T(8,128)S(1)} %get-tuple-element.34.up, bf16[512,640]{1,0:T(8,128)(2,1)S(1)} %get-tuple-element.35.rows, f32[512,128]{1,0:T(8,128)S(1)} %get-tuple-element.36.share, ...), custom_call_target="tpu_custom_call" | custom-call | tf_op jit(solution)/shard_map/last_gate_up/pallas_call | solution.py:411
  112.6 1.9 %down.2 = (bf16[256,1024]{1,0:T(8,128)(2,1)S(1)}, bf16[256,1024]{1,0:T(8,128)(2,1)S(1)}) custom-call(bf16[512,768]{1,0:T(8,128)(2,1)S(1)} %last_gate_up.1.inner, bf16[768,1024]{1,0:T(8,128)(2,1)S(1)} %bitcast.58), custom_call_target="tpu_custom_call" | custom-call | tf_op jit(solution)/shard_map/down/pallas_call | solution.py:432
  114.6 0.6 collective-permute-start.23
  115.1 1.3 collective-permute-done.18
  116.7 1.6 collective-permute-start.19
  118.2 6.9 %collective-permute-done.19 = bf16[128,1024]{1,0:T(8,128)(2,1)S(1)} collective-permute-done((bf16[128,1024]{1,0:T(8,128)(2,1)S(1)}, bf16[128,1024]{1,0:T(8,128)(2,1)S(1)}, u32[]{:S(2)}, u32[]{:S(2)}) %collective-permute-start.19) | collective-permute-done | bytes 262176 | tf_op jit(solution)/shard_map/ppermute | solution.py:305
  125.2 9.3 %collective-permute-done.23.inner = bf16[512,768]{1,0:T(8,128)(2,1)S(1)} collective-permute-done((bf16[512,768]{1,0:T(8,128)(2,1)S(1)}, bf16[512,768]{1,0:T(8,128)(2,1)S(1)}, u32[]{:S(2)}, u32[]{:S(2)}) %collective-permute-start.23) | collective-permute-done | bytes 786464 | tf_op jit(solution)/shard_map/ppermute | solution.py:286
  134.5 1.8 %down.3 = (bf16[256,1024]{1,0:T(8,128)(2,1)S(1)}, bf16[256,1024]{1,0:T(8,128)(2,1)S(1)}) custom-call(bf16[512,768]{1,0:T(8,128)(2,1)S(1)} %collective-permute-done.23.inner, bf16[768,1024]{1,0:T(8,128)(2,1)S(1)} %bitcast.59), custom_call_target="tpu_custom_call" | custom-call | tf_op jit(solution)/shard_map/down/pallas_call | solution.py:432
  136.5 3.9 %collective-permute-start.22 = (bf16[32,1024]{1,0:T(8,128)(2,1)S(1)}, bf16[32,1024]{1,0:T(8,128)(2,1)S(1)}, u32[]{:S(2)}, u32[]{:S(2)}) collective-permute-start(bf16[32,1024]{1,0:T(8,128)(2,1)S(1)} %get-tuple-element.50), channel_id=1, source_target_pairs={{0,12},{1,13},{2,14},{3,15},{4,0},{5,1},{6,2},{7,3},{8,4},{9,5},{1... | collective-permute-start | bytes 196616 | tf_op jit(solution)/shard_map/ppermute | solution.py:289
  140.4 0.8 collective-permute-start.20
  141.5 1.4 collective-permute-done.22.m3
  142.9 4.4 %collective-permute-done.21.m2 = bf16[32,1024]{1,0:T(8,128)(2,1)S(1)} collective-permute-done((bf16[32,1024]{1,0:T(8,128)(2,1)S(1)}, bf16[32,1024]{1,0:T(8,128)(2,1)S(1)}, u32[]{:S(2)}, u32[]{:S(2)}) %collective-permute-start.21) | collective-permute-done | bytes 65568 | tf_op jit(solution)/shard_map/ppermute | solution.py:289
  147.3 1.5 collective-permute-start.25
  148.8 6.5 %collective-permute-done.25 = bf16[128,1024]{1,0:T(8,128)(2,1)S(1)} collective-permute-done((bf16[128,1024]{1,0:T(8,128)(2,1)S(1)}, bf16[128,1024]{1,0:T(8,128)(2,1)S(1)}, u32[]{:S(2)}, u32[]{:S(2)}) %collective-permute-start.25) | collective-permute-done | bytes 262176 | tf_op jit(solution)/shard_map/ppermute | solution.py:305
  155.4 1.2 collective-permute-start.29
  156.6 1.5 collective-permute-start.28
  158.1 1.9 %collective-permute-start.27 = (bf16[32,1024]{1,0:T(8,128)(2,1)S(1)}, bf16[32,1024]{1,0:T(8,128)(2,1)S(1)}, u32[]{:S(2)}, u32[]{:S(2)}) collective-permute-start(bf16[32,1024]{1,0:T(8,128)(2,1)S(1)} %get-tuple-element.48), channel_id=1, source_target_pairs={{0,20},{1,21},{2,22},{3,23},{4,24},{5,25},{6,26},{7,27},{8,28},{9,... | collective-permute-start | bytes 196616 | tf_op jit(solution)/shard_map/ppermute | solution.py:294
  160.0 1.5 collective-permute-start.26
  161.5 2.3 %collective-permute-done.28.o2 = bf16[32,1024]{1,0:T(8,128)(2,1)S(1)} collective-permute-done((bf16[32,1024]{1,0:T(8,128)(2,1)S(1)}, bf16[32,1024]{1,0:T(8,128)(2,1)S(1)}, u32[]{:S(2)}, u32[]{:S(2)}) %collective-permute-start.28) | collective-permute-done | bytes 65568 | tf_op jit(solution)/shard_map/ppermute | solution.py:294
  163.9 1.3 collective-permute-done.27.o1
  165.3 1.4 closing.1
  (75 shorter events, 1.5 us)
Async XLA Ops:
  0.6 20.1 %copy-start.6 = (bf16[1,64,2048]{2,1,0:T(8,128)(2,1)S(1)}, bf16[1,64,2048]{2,1,0:T(8,128)(2,1)}, u32[]{:S(2)}) copy-start(bf16[1,64,2048]{2,1,0:T(8,128)(2,1)} %param.10) | copy-start | bytes 786436
  0.6 15.1 %collective-permute-start.3 = (bf16[2048,128]{1,0:T(8,128)(2,1)}, bf16[2048,128]{1,0:T(8,128)(2,1)S(1)}, u32[]{:S(2)}, u32[]{:S(2)}) collective-permute-start(bf16[2048,128]{1,0:T(8,128)(2,1)} %w0.1), channel_id=1, source_target_pairs={{0,2},{1,3},{2,0},{3,1},{4,6},{5,7},{6,4},{7,5},{8,10},{9,11},{10,... | collective-permute-start | bytes 1572872 | tf_op jit(solution)/shard_map/ppermute | solution.py:305
  15.8 9.5 %collective-permute-start.5 = (bf16[2048,128]{1,0:T(8,128)(2,1)S(1)}, bf16[2048,128]{1,0:T(8,128)(2,1)S(1)}, u32[]{:S(2)}, u32[]{:S(2)}) collective-permute-start(bf16[2048,128]{1,0:T(8,128)(2,1)S(1)} %collective-permute-done.3.w2), channel_id=1, source_target_pairs={{0,1},{1,0},{2,3},{3,2},{4,5},{5,4},{6,7},{7,6},{8,9},{9,8},{10,11... | collective-permute-start | bytes 1572872 | tf_op jit(solution)/shard_map/ppermute | solution.py:305
  15.8 0.8 copy-start.2
  18.9 41.5 %collective-permute-start.6 = (bf16[384,1536]{1,0:T(8,128)(2,1)}, bf16[384,1536]{1,0:T(8,128)(2,1)}, u32[]{:S(2)}, u32[]{:S(2)}) collective-permute-start(bf16[384,1536]{1,0:T(8,128)(2,1)} %slice_bitcast_fusion.1), channel_id=1, source_target_pairs={{0,16},{16,0},{1,17},{17,1},{2,18},{18,2},{3,19},{19,3},{4,20},{20... | collective-permute-start | bytes 3538952 | tf_op jit(solution)/shard_map/ppermute | solution.py:286
  20.7 8.4 %copy-start.22 = (bf16[1,32,2048]{2,1,0:T(8,128)(2,1)S(1)}, bf16[1,32,2048]{2,1,0:T(8,128)(2,1)}, u32[]{:S(2)}) copy-start(bf16[1,32,2048]{2,1,0:T(8,128)(2,1)} %param.11) | copy-start | bytes 393220
  20.7 10.3 %collective-permute-start.2 = (bf16[64,2048]{1,0:T(8,128)(2,1)S(1)}, bf16[64,2048]{1,0:T(8,128)(2,1)S(1)}, u32[]{:S(2)}, u32[]{:S(2)}) collective-permute-start(bf16[64,2048]{1,0:T(8,128)(2,1)S(1)} %bitcast.61), channel_id=1, source_target_pairs={{0,12},{1,13},{2,14},{3,15},{4,0},{5,1},{6,2},{7,3},{8,4},{9,5},{1... | collective-permute-start | bytes 786440 | tf_op jit(solution)/shard_map/ppermute | solution.py:289
  24.3 23.8 %collective-permute-start.1 = (bf16[64,2048]{1,0:T(8,128)(2,1)S(1)}, bf16[64,2048]{1,0:T(8,128)(2,1)S(1)}, u32[]{:S(2)}, u32[]{:S(2)}) collective-permute-start(bf16[64,2048]{1,0:T(8,128)(2,1)S(1)} %bitcast.62), channel_id=1, source_target_pairs={{0,8},{1,9},{2,10},{3,11},{4,12},{5,13},{6,14},{7,15},{8,0},{9,1},... | collective-permute-start | bytes 786440 | tf_op jit(solution)/shard_map/ppermute | solution.py:289
  24.3 24.5 %collective-permute-start = (bf16[64,2048]{1,0:T(8,128)(2,1)S(1)}, bf16[64,2048]{1,0:T(8,128)(2,1)S(1)}, u32[]{:S(2)}, u32[]{:S(2)}) collective-permute-start(bf16[64,2048]{1,0:T(8,128)(2,1)S(1)} %bitcast.63), channel_id=1, source_target_pairs={{0,4},{1,5},{2,6},{3,7},{4,8},{5,9},{6,10},{7,11},{8,12},{9,13},{1... | collective-permute-start | bytes 786440 | tf_op jit(solution)/shard_map/ppermute | solution.py:289
  25.3 0.8 copy-start.4
  26.1 24.1 %collective-permute-start.4 = (bf16[2048,128]{1,0:T(8,128)(2,1)}, bf16[2048,128]{1,0:T(8,128)(2,1)}, u32[]{:S(2)}, u32[]{:S(2)}) collective-permute-start(bf16[2048,128]{1,0:T(8,128)(2,1)} %w0.1), channel_id=1, source_target_pairs={{0,1},{1,0},{2,3},{3,2},{4,5},{5,4},{6,7},{7,6},{8,9},{9,8},{10,11... | collective-permute-start | bytes 1572872 | tf_op jit(solution)/shard_map/ppermute | solution.py:305
  29.1 32.0 %copy-start.23 = (f32[1,32,8]{1,2,0:T(8,128)S(1)}, f32[1,32,8]{1,2,0:T(8,128)}, u32[]{:S(2)}) copy-start(f32[1,32,8]{1,2,0:T(8,128)} %param.15) | copy-start | bytes 3076
  31.1 0.7 copy-start.7
  31.8 26.8 %collective-permute-start.7 = (bf16[32,512]{1,0:T(8,128)(2,1)S(1)}, bf16[32,512]{1,0:T(8,128)(2,1)S(1)}, u32[]{:S(2)}, u32[]{:S(2)}) collective-permute-start(bf16[32,512]{1,0:T(8,128)(2,1)S(1)} %get-tuple-element.28), channel_id=1, source_target_pairs={{0,4},{1,5},{2,6},{3,7},{4,8},{5,9},{6,10},{7,11},{8,12},{9,13},{1... | collective-permute-start | bytes 98312 | tf_op jit(solution)/shard_map/ppermute | solution.py:289
  48.1 0.7 copy-start.9
  48.8 10.4 %collective-permute-start.8 = (bf16[32,512]{1,0:T(8,128)(2,1)S(1)}, bf16[32,512]{1,0:T(8,128)(2,1)S(1)}, u32[]{:S(2)}, u32[]{:S(2)}) collective-permute-start(bf16[32,512]{1,0:T(8,128)(2,1)S(1)} %get-tuple-element.29), channel_id=1, source_target_pairs={{0,8},{1,9},{2,10},{3,11},{4,12},{5,13},{6,14},{7,15},{8,0},{9,1},... | collective-permute-start | bytes 98312 | tf_op jit(solution)/shard_map/ppermute | solution.py:289
  48.8 0.7 copy-start.11
  49.5 10.3 %collective-permute-start.9 = (bf16[32,512]{1,0:T(8,128)(2,1)S(1)}, bf16[32,512]{1,0:T(8,128)(2,1)S(1)}, u32[]{:S(2)}, u32[]{:S(2)}) collective-permute-start(bf16[32,512]{1,0:T(8,128)(2,1)S(1)} %get-tuple-element.30), channel_id=1, source_target_pairs={{0,12},{1,13},{2,14},{3,15},{4,0},{5,1},{6,2},{7,3},{8,4},{9,5},{1... | collective-permute-start | bytes 98312 | tf_op jit(solution)/shard_map/ppermute | solution.py:289
  50.2 51.3 %copy-start = (bf16[1,1024,1536]{2,1,0:T(8,128)(2,1)S(1)}, bf16[1,1024,1536]{2,1,0:T(8,128)(2,1)}, u32[]{:S(2)}) copy-start(bf16[1,1024,1536]{2,1,0:T(8,128)(2,1)} %param.17) | copy-start | bytes 9437188
  50.3 1.2 copy-start.3
  51.4 1.0 copy-start.5
  52.5 0.9 copy-start.8
  53.4 0.9 copy-start.10
  54.4 0.9 copy-start.12
  55.3 46.2 %copy-start.20 = (f32[2048]{0:T(1024)S(1)}, f32[2048]{0:T(1024)}, u32[]{:S(2)}) copy-start(f32[2048]{0:T(1024)} %param.13) | copy-start | bytes 24580
  58.6 0.6 copy-start.14
  59.2 0.6 copy-start.16
  59.8 0.6 copy-start.18
  60.4 5.2 %collective-permute-start.10 = (bf16[128,512]{1,0:T(8,128)(2,1)}, bf16[128,512]{1,0:T(8,128)(2,1)S(1)}, u32[]{:S(2)}, u32[]{:S(2)}) collective-permute-start(bf16[128,512]{1,0:T(8,128)(2,1)} %get-tuple-element.31), channel_id=1, source_target_pairs={{0,16},{16,0},{1,17},{17,1},{2,18},{18,2},{3,19},{19,3},{4,20},{20... | collective-permute-start | bytes 393224 | tf_op jit(solution)/shard_map/ppermute | solution.py:286
  65.6 43.3 %collective-permute-start.17 = (bf16[640,1536]{1,0:T(8,128)(2,1)}, bf16[640,1536]{1,0:T(8,128)(2,1)}, u32[]{:S(2)}, u32[]{:S(2)}) collective-permute-start(bf16[640,1536]{1,0:T(8,128)(2,1)} %slice_bitcast_fusion), channel_id=1, source_target_pairs={{0,16},{16,0},{1,17},{17,1},{2,18},{18,2},{3,19},{19,3},{4,20},{20... | collective-permute-start | bytes 5898248 | tf_op jit(solution)/shard_map/ppermute | solution.py:286
  67.0 0.8 copy-start.13
  67.7 0.8 copy-start.15
  68.5 0.8 copy-start.17
  69.2 0.8 copy-start.19
  70.6 8.3 %collective-permute-start.13 = (bf16[144,512]{1,0:T(8,128)(2,1)S(1)}, bf16[144,512]{1,0:T(8,128)(2,1)S(1)}, u32[]{:S(2)}, u32[]{:S(2)}) collective-permute-start(bf16[144,512]{1,0:T(8,128)(2,1)S(1)} %stream.1), channel_id=1, source_target_pairs={{0,12},{1,13},{2,14},{3,15},{4,0},{5,1},{6,2},{7,3},{8,4},{9,5},{1... | collective-permute-start | bytes 442376 | tf_op jit(solution)/shard_map/ppermute | solution.py:289
  75.0 10.9 %collective-permute-start.12 = (bf16[144,512]{1,0:T(8,128)(2,1)S(1)}, bf16[144,512]{1,0:T(8,128)(2,1)S(1)}, u32[]{:S(2)}, u32[]{:S(2)}) collective-permute-start(bf16[144,512]{1,0:T(8,128)(2,1)S(1)} %stream.1), channel_id=1, source_target_pairs={{0,8},{1,9},{2,10},{3,11},{4,12},{5,13},{6,14},{7,15},{8,0},{9,1},... | collective-permute-start | bytes 442376 | tf_op jit(solution)/shard_map/ppermute | solution.py:289
  75.0 10.9 %collective-permute-start.11 = (bf16[144,512]{1,0:T(8,128)(2,1)S(1)}, bf16[144,512]{1,0:T(8,128)(2,1)S(1)}, u32[]{:S(2)}, u32[]{:S(2)}) collective-permute-start(bf16[144,512]{1,0:T(8,128)(2,1)S(1)} %stream.1), channel_id=1, source_target_pairs={{0,4},{1,5},{2,6},{3,7},{4,8},{5,9},{6,10},{7,11},{8,12},{9,13},{1... | collective-permute-start | bytes 442376 | tf_op jit(solution)/shard_map/ppermute | solution.py:289
  86.0 13.5 %collective-permute-start.14 = (bf16[4,144,512]{2,1,0:T(8,128)(2,1)S(1)}, bf16[4,144,512]{2,1,0:T(8,128)(2,1)S(1)}, u32[]{:S(2)}, u32[]{:S(2)}) collective-permute-start(bf16[4,144,512]{2,1,0:T(8,128)(2,1)S(1)} %pad_maximum_fusion.blocks), channel_id=1, source_target_pairs={{0,2},{1,3},{2,0},{3,1},{4,6},{5,7},{6,4},{7,5},{8,10},{9,11},{10,... | collective-permute-start | bytes 1769480 | tf_op jit(solution)/shard_map/ppermute | solution.py:305
  87.6 12.0 %collective-permute-start.15 = (bf16[4,144,512]{2,1,0:T(8,128)(2,1)S(1)}, bf16[4,144,512]{2,1,0:T(8,128)(2,1)S(1)}, u32[]{:S(2)}, u32[]{:S(2)}) collective-permute-start(bf16[4,144,512]{2,1,0:T(8,128)(2,1)S(1)} %pad_maximum_fusion.blocks), channel_id=1, source_target_pairs={{0,1},{1,0},{2,3},{3,2},{4,5},{5,4},{6,7},{7,6},{8,9},{9,8},{10,11... | collective-permute-start | bytes 1769480 | tf_op jit(solution)/shard_map/ppermute | solution.py:305
  99.6 2.0 %collective-permute-start.16 = (bf16[4,144,512]{2,1,0:T(8,128)(2,1)S(1)}, bf16[4,144,512]{2,1,0:T(8,128)(2,1)S(1)}, u32[]{:S(2)}, u32[]{:S(2)}) collective-permute-start(bf16[4,144,512]{2,1,0:T(8,128)(2,1)S(1)} %collective-permute-done.14.blocks_x), channel_id=1, source_target_pairs={{0,1},{1,0},{2,3},{3,2},{4,5},{5,4},{6,7},{7,6},{8,9},{9,8},{10,11... | collective-permute-start | bytes 1769480 | tf_op jit(solution)/shard_map/ppermute | solution.py:305
  108.9 3.7 %copy-start.1 = (bf16[1,768,1024]{2,1,0:T(8,128)(2,1)S(1)}, bf16[1,768,1024]{2,1,0:T(8,128)(2,1)}, u32[]{:S(2)}) copy-start(bf16[1,768,1024]{2,1,0:T(8,128)(2,1)} %param.18) | copy-start | bytes 4718596
  114.5 2.0 %collective-permute-start.18 = (bf16[256,1024]{1,0:T(8,128)(2,1)S(1)}, bf16[256,1024]{1,0:T(8,128)(2,1)S(1)}, u32[]{:S(2)}, u32[]{:S(2)}) collective-permute-start(bf16[256,1024]{1,0:T(8,128)(2,1)S(1)} %get-tuple-element.39), channel_id=1, source_target_pairs={{0,1},{1,0},{2,3},{3,2},{4,5},{5,4},{6,7},{7,6},{8,9},{9,8},{10,11... | collective-permute-start | bytes 1572872 | tf_op jit(solution)/shard_map/ppermute | solution.py:305
  114.6 20.0 %collective-permute-start.23 = (bf16[512,768]{1,0:T(8,128)(2,1)S(1)}, bf16[512,768]{1,0:T(8,128)(2,1)S(1)}, u32[]{:S(2)}, u32[]{:S(2)}) collective-permute-start(bf16[512,768]{1,0:T(8,128)(2,1)S(1)} %last_gate_up.1.inner), channel_id=1, source_target_pairs={{0,16},{16,0},{1,17},{17,1},{2,18},{18,2},{3,19},{19,3},{4,20},{20... | collective-permute-start | bytes 2359304 | tf_op jit(solution)/shard_map/ppermute | solution.py:286
  116.7 8.4 %collective-permute-start.19 = (bf16[128,1024]{1,0:T(8,128)(2,1)S(1)}, bf16[128,1024]{1,0:T(8,128)(2,1)S(1)}, u32[]{:S(2)}, u32[]{:S(2)}) collective-permute-start(bf16[128,1024]{1,0:T(8,128)(2,1)S(1)} %slice.25), channel_id=1, source_target_pairs={{0,2},{1,3},{2,0},{3,1},{4,6},{5,7},{6,4},{7,5},{8,10},{9,11},{10,... | collective-permute-start | bytes 786440 | tf_op jit(solution)/shard_map/ppermute | solution.py:305
  136.4 4.9 %collective-permute-start.24 = (bf16[256,1024]{1,0:T(8,128)(2,1)S(1)}, bf16[256,1024]{1,0:T(8,128)(2,1)S(1)}, u32[]{:S(2)}, u32[]{:S(2)}) collective-permute-start(bf16[256,1024]{1,0:T(8,128)(2,1)S(1)} %get-tuple-element.42), channel_id=1, source_target_pairs={{0,1},{1,0},{2,3},{3,2},{4,5},{5,4},{6,7},{7,6},{8,9},{9,8},{10,11... | collective-permute-start | bytes 1572872 | tf_op jit(solution)/shard_map/ppermute | solution.py:305
  136.5 28.8 %copy-start.21 = (f32[2048]{0:T(1024)S(1)}, f32[2048]{0:T(1024)}, u32[]{:S(2)}) copy-start(f32[2048]{0:T(1024)} %param.19) | copy-start | bytes 24580
  136.5 6.3 %collective-permute-start.22 = (bf16[32,1024]{1,0:T(8,128)(2,1)S(1)}, bf16[32,1024]{1,0:T(8,128)(2,1)S(1)}, u32[]{:S(2)}, u32[]{:S(2)}) collective-permute-start(bf16[32,1024]{1,0:T(8,128)(2,1)S(1)} %get-tuple-element.50), channel_id=1, source_target_pairs={{0,12},{1,13},{2,14},{3,15},{4,0},{5,1},{6,2},{7,3},{8,4},{9,5},{1... | collective-permute-start | bytes 196616 | tf_op jit(solution)/shard_map/ppermute | solution.py:289
  140.4 6.9 %collective-permute-start.21 = (bf16[32,1024]{1,0:T(8,128)(2,1)S(1)}, bf16[32,1024]{1,0:T(8,128)(2,1)S(1)}, u32[]{:S(2)}, u32[]{:S(2)}) collective-permute-start(bf16[32,1024]{1,0:T(8,128)(2,1)S(1)} %get-tuple-element.51), channel_id=1, source_target_pairs={{0,8},{1,9},{2,10},{3,11},{4,12},{5,13},{6,14},{7,15},{8,0},{9,1},... | collective-permute-start | bytes 196616 | tf_op jit(solution)/shard_map/ppermute | solution.py:289
  140.4 6.9 %collective-permute-start.20 = (bf16[32,1024]{1,0:T(8,128)(2,1)S(1)}, bf16[32,1024]{1,0:T(8,128)(2,1)S(1)}, u32[]{:S(2)}, u32[]{:S(2)}) collective-permute-start(bf16[32,1024]{1,0:T(8,128)(2,1)S(1)} %get-tuple-element.52), channel_id=1, source_target_pairs={{0,4},{1,5},{2,6},{3,7},{4,8},{5,9},{6,10},{7,11},{8,12},{9,13},{1... | collective-permute-start | bytes 196616 | tf_op jit(solution)/shard_map/ppermute | solution.py:289
  147.3 8.0 %collective-permute-start.25 = (bf16[128,1024]{1,0:T(8,128)(2,1)S(1)}, bf16[128,1024]{1,0:T(8,128)(2,1)S(1)}, u32[]{:S(2)}, u32[]{:S(2)}) collective-permute-start(bf16[128,1024]{1,0:T(8,128)(2,1)S(1)} %slice.27), channel_id=1, source_target_pairs={{0,2},{1,3},{2,0},{3,1},{4,6},{5,7},{6,4},{7,5},{8,10},{9,11},{10,... | collective-permute-start | bytes 786440 | tf_op jit(solution)/shard_map/ppermute | solution.py:305
  155.4 6.1 %collective-permute-start.29 = (bf16[32,1024]{1,0:T(8,128)(2,1)S(1)}, bf16[32,1024]{1,0:T(8,128)(2,1)S(1)}, u32[]{:S(2)}, u32[]{:S(2)}) collective-permute-start(bf16[32,1024]{1,0:T(8,128)(2,1)S(1)} %get-tuple-element.46), channel_id=1, source_target_pairs={{0,28},{1,29},{2,30},{3,31},{4,16},{5,17},{6,18},{7,19},{8,20},{9,... | collective-permute-start | bytes 196616 | tf_op jit(solution)/shard_map/ppermute | solution.py:294
  156.6 7.3 %collective-permute-start.28 = (bf16[32,1024]{1,0:T(8,128)(2,1)S(1)}, bf16[32,1024]{1,0:T(8,128)(2,1)S(1)}, u32[]{:S(2)}, u32[]{:S(2)}) collective-permute-start(bf16[32,1024]{1,0:T(8,128)(2,1)S(1)} %get-tuple-element.47), channel_id=1, source_target_pairs={{0,24},{1,25},{2,26},{3,27},{4,28},{5,29},{6,30},{7,31},{8,16},{9,... | collective-permute-start | bytes 196616 | tf_op jit(solution)/shard_map/ppermute | solution.py:294
  158.1 7.1 %collective-permute-start.27 = (bf16[32,1024]{1,0:T(8,128)(2,1)S(1)}, bf16[32,1024]{1,0:T(8,128)(2,1)S(1)}, u32[]{:S(2)}, u32[]{:S(2)}) collective-permute-start(bf16[32,1024]{1,0:T(8,128)(2,1)S(1)} %get-tuple-element.48), channel_id=1, source_target_pairs={{0,20},{1,21},{2,22},{3,23},{4,24},{5,25},{6,26},{7,27},{8,28},{9,... | collective-permute-start | bytes 196616 | tf_op jit(solution)/shard_map/ppermute | solution.py:294
  160.0 5.2 %collective-permute-start.26 = (bf16[32,1024]{1,0:T(8,128)(2,1)S(1)}, bf16[32,1024]{1,0:T(8,128)(2,1)S(1)}, u32[]{:S(2)}, u32[]{:S(2)}) collective-permute-start(bf16[32,1024]{1,0:T(8,128)(2,1)S(1)} %get-tuple-element.49), channel_id=1, source_target_pairs={{0,16},{1,17},{2,18},{3,19},{4,20},{5,21},{6,22},{7,23},{8,24},{9,... | collective-permute-start | bytes 196616 | tf_op jit(solution)/shard_map/ppermute | solution.py:294

commit v4 on v3

--- a/solution.py
+++ b/solution.py
@@ -148,44 +148,74 @@
     return jnp.dot(a, b, preferred_element_type=F32)
 
 
+def cost(flops, moved):
+    return pl.CostEstimate(flops=flops, bytes_accessed=moved, transcendentals=0)
+
+
 def kernel_params(mib):
     return pltpu.CompilerParams(vmem_limit_bytes=mib * MIB)
 
 
-def proj_kernel(place, a0, a1, a2, a3, w0, w1, w2, w3, keep_ref, send_ref, rows, part):
-    outer, inner, dp = place[0], place[1], place[2]
+def seat():
+    expert = lax.axis_index("expert")
+    return expert, lax.shift_right_logical(expert, 2), expert & 3, lax.axis_index("dp")
+
+
+def aligned(index, step):
+    return pl.ds(pl.multiple_of(index * step, step), step)
+
+
+def prepare_kernel(live, ids, logits, resid, share_ref, r0, r1, r2, r3):
+    expert, outer, inner, dp = seat()
+    rows, top = ids.shape
+    experts, lanes = share_ref.shape
+    value = logits[...]
+    value = jnp.exp(value - jnp.max(value, axis=1, keepdims=True))
+    probs = (value / jnp.sum(value, axis=1, keepdims=True)).astype(BF16).astype(F32)
+    probs = jnp.where(lax.broadcasted_iota(jnp.int32, (rows, top), 0) < live[0, 0], probs, 0.0)
+    names = lax.broadcasted_iota(jnp.int32, (rows, experts), 1)
+    table = jnp.zeros((rows, experts), F32)
+    for k in range(top):
+        table = table + jnp.where(ids[:, k : k + 1] == names, probs[:, k : k + 1], 0.0)
+    spots = lax.broadcasted_iota(jnp.int32, (rows, lanes), 1) - outer * rows
+    spots = (spots == lax.broadcasted_iota(jnp.int32, (rows, lanes), 0)).astype(F32).astype(BF16)
+    share_ref[...] = lax.dot_general(
+        table.astype(BF16), spots, (((0,), (0,)), ((), ())), preferred_element_type=F32
+    ).astype(BF16)
+    for s, r in enumerate((r0, r1, r2, r3)):
+        r[...] = resid[:, aligned((outer + s) & 3, lanes)]
+
+
+def proj_kernel(a0, a1, a2, a3, w0, w1, w2, w3, keep_ref, send_ref, rows, part):
+    expert, outer, inner, dp = seat()
     full = a0.shape[0]
     half = full // 2
     block = w0.shape[1]
     for s, a in enumerate((a0, a1, a2, a3)):
-        spot = lax.rem(outer + 4 - s, 4)
-        rows[pl.ds(pl.multiple_of(spot * full, full), full), :] = a[...]
+        rows[aligned(outer ^ s, full), :] = a[...]
     for j, w in enumerate((w0, w1, w2, w3)):
-        spot = pl.multiple_of((inner ^ j) * block, block)
-        part[:, pl.ds(spot, block)] = dot(rows[...], w[...]).astype(BF16)
+        part[:, aligned(inner ^ j, block)] = dot(rows[...], w[...]).astype(BF16)
     for spot in range(4):
-        mine = pl.multiple_of(spot * full + dp * half, half)
-        other = pl.multiple_of(spot * full + (1 - dp) * half, half)
-        keep_ref[spot * half : (spot + 1) * half, :] = part[pl.ds(mine, half), :]
-        send_ref[spot * half : (spot + 1) * half, :] = part[pl.ds(other, half), :]
-
-
-def stream_kernel(place, keep, arrived, r0, r1, r2, r3, share, block_ref):
-    outer = place[0]
+        keep_ref[spot * half : (spot + 1) * half, :] = part[aligned(2 * spot + dp, half), :]
+        send_ref[spot * half : (spot + 1) * half, :] = part[aligned(2 * spot + 1 - dp, half), :]
+
+
+def stream_kernel(keep, arrived, r0, r1, r2, r3, share, block_ref):
+    expert, outer, inner, dp = seat()
     count = keep.shape[0]
     small = r0.shape[0]
     for s, r in enumerate((r0, r1, r2, r3)):
-        rows = pl.ds(pl.multiple_of(lax.rem(outer + 4 - s, 4) * small, small), small)
+        rows = aligned((outer + 4 - s) & 3, small)
         product = keep[rows, :].astype(F32) + arrived[rows, :].astype(F32)
         block_ref[rows, :] = (r[...].astype(F32) + product).astype(BF16)
     block_ref[count:, :] = share[...]
 
 
 def first_gate_kernel(
-    place, blocks, blocks_x, blocks_c, blocks_cx, gain, ga, ua, gb, ub,
+    blocks, blocks_x, blocks_c, blocks_cx, gain, ga, ua, gb, ub,
     gate_ref, up_ref, last_ref, share_ref, own_ref, normed,
 ):
-    outer, inner, dp = place[0], place[1], place[2]
+    expert, outer, inner, dp = seat()
     step = pl.program_id(0)
     width = blocks.shape[2]
     count = share_ref.shape[0] // 4
@@ -197,27 +227,25 @@
 
     @pl.when(step == 0)
     def _():
-        expert = outer * 4 + inner
         picked = lax.broadcasted_iota(jnp.int32, (experts, count), 0) == expert
         diagonal = lax.broadcasted_iota(jnp.int32, (count, count), 0) == lax.broadcasted_iota(
             jnp.int32, (count, count), 1
         )
-        for j, group in enumerate((blocks, blocks_c, blocks_x, blocks_cx)):
+        for j, group in enumerate((blocks_x, blocks_cx, blocks, blocks_c)):
             rows = slice(j * count, (j + 1) * count)
             square = jnp.zeros((count, 1), F32)
             share = jnp.zeros((experts, count), F32)
             for s in range(4):
-                spot = lax.rem(outer + 4 - s, 4)
                 value = group[s, 0:count, :]
-                normed[rows, pl.ds(pl.multiple_of(spot * width, width), width)] = value
+                normed[rows, aligned((outer + 4 - s) & 3, width)] = value
                 value = value.astype(F32)
                 square = square + jnp.sum(value * value, axis=1, keepdims=True)
                 share = share + group[s, count : count + experts, 0:count].astype(F32)
             line = jnp.sum(jnp.where(picked, share, 0.0), axis=0, keepdims=True)
             column = jnp.sum(jnp.where(diagonal, line, 0.0), axis=1, keepdims=True)
             share_ref[rows, :] = jnp.broadcast_to(column, (count, share_ref.shape[1]))
-            if j == 0:
-                own_ref[...] = normed[pl.ds(pl.multiple_of(outer * small, small), small), :]
+            if j == 2:
+                own_ref[...] = normed[aligned(outer + 2 * (count // small), small), :]
             scale = lax.rsqrt(square / (4 * width) + 1e-06)
             for s in range(4):
                 cols = slice(s * width, (s + 1) * width)
@@ -225,36 +253,56 @@
                 normed[rows, cols] = (value * scale * gain[:, cols]).astype(BF16)
         last_ref[...] = normed[:, pl.ds(pl.multiple_of((1 - dp) * half + depth, 128), rest)]
 
-    mine = normed[:, pl.ds(pl.multiple_of(dp * half, half), half)]
+    mine = normed[:, aligned(dp, half)]
     early = normed[:, pl.ds(pl.multiple_of((1 - dp) * half, half), depth)]
     gate_ref[...] = dot(mine, ga[...]) + dot(early, gb[...])
     up_ref[...] = dot(mine, ua[...]) + dot(early, ub[...])
 
 
-def last_gate_kernel(gate, up, rows, share, gw, uw, inner_ref):
+def last_gate_kernel(gate, up, rows, share, gw, uw, far_ref, near_ref):
     g = gate[...] + dot(rows[...], gw[...])
     u = up[...] + dot(rows[...], uw[...])
-    inner_ref[...] = (g / (1.0 + jnp.exp(-g)) * u * share[:, 0:1]).astype(BF16)
-
-
-def down_kernel(inner, wd, keep_ref, send_ref):
-    count = inner.shape[0] // 4
-    value = dot(inner[...], wd[...]).astype(BF16)
-    for i in range(2):
-        keep_ref[i * count : (i + 1) * count, :] = value[2 * i * count : (2 * i + 1) * count]
-        send_ref[i * count : (i + 1) * count, :] = value[(2 * i + 1) * count : (2 * i + 2) * count]
-
-
-def tail_kernel(place, own, m0, m1, m2, m3, o0, o1, o2, o3, gain, stream_ref, normed_ref):
-    dp = place[2]
+    inner = (g / (1.0 + jnp.exp(-g)) * u * share[:, 0:1]).astype(BF16)
+    half = far_ref.shape[0]
+    far_ref[...] = inner[:half]
+    near_ref[...] = inner[half:]
+
+
+def down_both_kernel(far, near, wd, keep_far, keep_near, send_ref):
+    count = keep_far.shape[0]
+    value = dot(far[...], wd[...]).astype(BF16)
+    keep_far[...] = value[:count]
+    send_ref[0:count, :] = value[count:]
+    value = dot(near[...], wd[...]).astype(BF16)
+    keep_near[...] = value[:count]
+    send_ref[count : 2 * count, :] = value[count:]
+
+
+def down_kernel(rows, wd, keep_ref, send_ref):
+    count = keep_ref.shape[0]
+    value = dot(rows[...], wd[...]).astype(BF16)
+    keep_ref[...] = value[:count]
+    send_ref[...] = value[count:]
+
+
+def pieces_kernel(keep, core, far, p0, p1, p2, p3):
+    expert, outer, inner, dp = seat()
+    small = p0.shape[0]
+    for s, p in enumerate((p0, p1, p2, p3)):
+        rows = aligned((outer + s) & 3, small)
+        total = keep[rows, :].astype(F32) + core[rows, :].astype(F32)
+        p[...] = (total + far[rows, :].astype(F32)).astype(BF16)
+
+
+def tail_kernel(own, m0, m1, m2, m3, o0, o1, o2, o3, gain, stream_ref, normed_ref):
+    expert, outer, inner, dp = seat()
     half = m0.shape[1]
     for at, pieces in ((dp, (m0, m1, m2, m3)), (1 - dp, (o0, o1, o2, o3))):
-        cols = pl.ds(pl.multiple_of(at * half, half), half)
-        total = own[:, cols].astype(F32)
+        cols = aligned(at, half)
         mixture = pieces[0][...].astype(F32)
         for piece in pieces[1:]:
             mixture = mixture + piece[...].astype(F32)
-        stream_ref[:, cols] = (total + mixture).astype(BF16)
+        stream_ref[:, cols] = (own[:, cols].astype(F32) + mixture).astype(BF16)
     normed_ref[...] = rms_scale(stream_ref[...].astype(F32), gain[...]).astype(BF16)
 
 
@@ -276,11 +324,23 @@
     hidden = w_down.shape[1]
     half_width = w_down.shape[2]
     quarter = model_width // 4
-    dp = lax.axis_index("dp")
-    expert = lax.axis_index("expert")
-    outer, inner_at = expert // 4, expert % 4
-    place = jnp.stack([outer, inner_at, dp]).astype(jnp.int32)
     vmem, smem = whole_vmem(), whole_smem()
+
+    def shape_of(*shape, dtype=BF16):
+        return jax.ShapeDtypeStruct(shape, dtype)
+
+    def call(kernel, name, mib, outs, *args, scratch=(), first=vmem, flops=1_000_000):
+        moved = sum(math.prod(x.shape) * x.dtype.itemsize for x in (*args, *outs))
+        return pl.pallas_call(
+            kernel,
+            out_shape=outs,
+            in_specs=[first] + [vmem] * (len(args) - 1),
+            out_specs=tuple(vmem for _ in outs),
+            scratch_shapes=list(scratch),
+            compiler_params=kernel_params(mib),
+            cost_estimate=cost(flops, moved),
+            name=name,
+        )(*args)
 
     def swap_dp(x):
         return lax.ppermute(x, "dp", [(0, 1), (1, 0)])
@@ -304,56 +364,63 @@
     def swap_inner(x, j):
         return lax.ppermute(x, "expert", [(i, i ^ j) for i in range(expert_count)])
 
+    def swap_outer(x, s):
+        return lax.ppermute(x, "expert", [(i, i ^ (4 * s)) for i in range(expert_count)])
+
     def after(x, *results):
         return lax.optimization_barrier((x, *results))[0]
 
     depth = half_width * 3 // 8
-    early_piece = w_gate_up[0, :depth]
-    sent = after(attn[0], early_piece)
-    a = [attn[0]] + [shift_outer(sent, s) for s in (1, 2, 3)]
+    a = [attn[0], swap_outer(attn[0], 1), swap_outer(attn[0], 2)]
+    a.append(swap_outer(a[2], 1))
     w_x = swap_inner(w_out, 2)
-    gate_up_early = swap_dp(early_piece)
+    gate_up_early = swap_dp(w_gate_up[0, :depth])
     w_c = swap_inner(after(w_out, w_x), 1)
     w_cx = swap_inner(w_x, 1)
 
-    def resid_piece(s):
-        return lax.dynamic_slice_in_dim(resid[0], ((outer + s) % 4) * quarter, quarter, 1)
-
-    r = [resid_piece(0)] + [shift_outer(after(resid_piece(s), w_cx), s) for s in (1, 2, 3)]
-
-    probs = jax.nn.softmax(route_logits[0], axis=-1).astype(BF16)
-    alive = jnp.arange(rows_here, dtype=jnp.int32) < live_count[0, 0]
-    chosen = (
-        route_ids[0][None] == jnp.arange(expert_count, dtype=jnp.int32)[:, None, None]
-    ) & alive[None, :, None]
-    share = jnp.sum(jnp.where(chosen, probs.astype(F32)[None], 0.0), axis=2)
-    spots = jnp.arange(quarter // rows_here, dtype=jnp.int32) == outer
-    share = jnp.where(spots[None, :, None], share[:, None, :], 0.0)
-    share = share.reshape(expert_count, quarter).astype(BF16)
-
-    product = jax.ShapeDtypeStruct((4 * rows_here, quarter), BF16)
-    keep, send = pl.pallas_call(
+    piece = shape_of(rows_here, quarter)
+    share, *r = call(
+        prepare_kernel,
+        "prepare",
+        4,
+        (shape_of(expert_count, quarter), piece, piece, piece, piece),
+        live_count,
+        route_ids[0],
+        route_logits[0],
+        resid[0],
+        first=smem,
+    )
+    r = [r[0]] + [shift_outer(after(r[s], a[1]), s) for s in (1, 2, 3)]
+
+    product = shape_of(4 * rows_here, quarter)
+    keep, send = call(
         proj_kernel,
-        out_shape=(product, product),
-        in_specs=[smem] + [vmem] * 8,
-        out_specs=(vmem, vmem),
-        scratch_shapes=[
+        "projection",
+        8,
+        (product, product),
+        *a,
+        w_out,
+        w_c,
+        w_x,
+        w_cx,
+        flops=16 * rows_here * attn.shape[2] * quarter,
+        scratch=(
             pltpu.VMEM((8 * rows_here, attn.shape[2]), BF16),
             pltpu.VMEM((8 * rows_here, quarter), BF16),
-        ],
-        compiler_params=kernel_params(16),
-        name="projection",
-    )(place, *a, w_out, w_c, w_x, w_cx)
+        ),
+    )
     arrived = swap_dp(after(send, gate_up_early, *r[1:]))
     gate_up_late = swap_dp(after(w_gate_up[0, depth:], arrived))
-    block = pl.pallas_call(
+    (block,) = call(
         stream_kernel,
-        out_shape=jax.ShapeDtypeStruct((4 * rows_here + expert_count, quarter), BF16),
-        in_specs=[smem] + [vmem] * 7,
-        out_specs=vmem,
-        compiler_params=kernel_params(8),
-        name="stream",
-    )(place, keep, arrived, *r, share)
+        "stream",
+        4,
+        (shape_of(4 * rows_here + expert_count, quarter),),
+        keep,
+        arrived,
+        *r,
+        share,
+    )
 
     blocks = jnp.stack([block] + [shift_outer(block, s) for s in (1, 2, 3)])
     blocks_x = swap_inner(blocks, 2)
@@ -366,19 +433,18 @@
     block_spec = fixed(*blocks.shape)
     gate_cols = lambda k: pl.BlockSpec((k, unit), lambda i: (0, i))
     up_cols = lambda k: pl.BlockSpec((k, unit), lambda i: (0, i + steps))
-    out_cols = pl.BlockSpec((row_total, unit), lambda i: (0, i))
+    out_cols = lambda k: pl.BlockSpec((k, unit), lambda i: (0, i))
     gate, up, last_rows, share_rows, stream_own = pl.pallas_call(
         first_gate_kernel,
         grid=(steps,),
         out_shape=(
-            jax.ShapeDtypeStruct((row_total, hidden), F32),
-            jax.ShapeDtypeStruct((row_total, hidden), F32),
-            jax.ShapeDtypeStruct((row_total, half_width - depth), BF16),
-            jax.ShapeDtypeStruct((row_total, 128), F32),
-            jax.ShapeDtypeStruct((rows_here, model_width), BF16),
+            shape_of(row_total, hidden, dtype=F32),
+            shape_of(row_total, hidden, dtype=F32),
+            shape_of(row_total, half_width - depth),
+            shape_of(row_total, 128, dtype=F32),
+            shape_of(rows_here, model_width),
         ),
-        in_specs=[smem]
-        + [block_spec] * 4
+        in_specs=[block_spec] * 4
         + [
             fixed(1, model_width),
             gate_cols(half_width),
@@ -387,8 +453,8 @@
             up_cols(depth),
         ],
         out_specs=(
-            out_cols,
-            out_cols,
+            out_cols(row_total),
+            out_cols(row_total),
             fixed(row_total, half_width - depth),
             fixed(row_total, 128),
             fixed(rows_here, model_width),
@@ -396,8 +462,8 @@
         scratch_shapes=[pltpu.VMEM((row_total, model_width), BF16)],
         compiler_params=kernel_params(24),
         name="first_gate_up",
+        cost_estimate=cost(4 * row_total * (half_width + depth) * hidden, 12 * row_total * hidden),
     )(
-        place,
         blocks,
         blocks_x,
         blocks_c,
@@ -408,68 +474,77 @@
         gate_up_early,
         gate_up_early,
     )
-    inner = pl.pallas_call(
+    inner_half = shape_of(row_total // 2, hidden)
+    inner_far, inner_near = pl.pallas_call(
         last_gate_kernel,
         grid=(steps,),
-        out_shape=jax.ShapeDtypeStruct((row_total, hidden), BF16),
+        out_shape=(inner_half, inner_half),
         in_specs=[
-            out_cols,
-            out_cols,
+            out_cols(row_total),
+            out_cols(row_total),
             fixed(row_total, half_width - depth),
             fixed(row_total, 128),
             gate_cols(half_width - depth),
             up_cols(half_width - depth),
         ],
-        out_specs=out_cols,
+        out_specs=(out_cols(row_total // 2), out_cols(row_total // 2)),
         compiler_params=kernel_params(16),
         name="last_gate_up",
+        cost_estimate=cost(4 * row_total * (half_width - depth) * hidden, 14 * row_total * hidden),
     )(gate, up, last_rows, share_rows, gate_up_late, gate_up_late)
-    inner_other = swap_dp(inner)
+    far_other = swap_dp(inner_far)
+    near_other = swap_dp(inner_near)
+
+    count = row_total // 4
+    quarter_out = shape_of(count, half_width)
+    half_spec = fixed(row_total // 2, hidden)
+    wd_spec = pl.BlockSpec((hidden, unit), lambda i: (0, i))
 
     def down(rows):
-        out = jax.ShapeDtypeStruct((row_total // 2, half_width), BF16)
-        spec = pl.BlockSpec((row_total // 2, 256), lambda i: (0, i))
         return pl.pallas_call(
             down_kernel,
-            grid=(half_width // 256,),
-            out_shape=(out, out),
-            in_specs=[
-                fixed(row_total, hidden),
-                pl.BlockSpec((hidden, 256), lambda i: (0, i)),
-            ],
-            out_specs=(spec, spec),
-            compiler_params=kernel_params(12),
+            grid=(half_width // unit,),
+            out_shape=(quarter_out, quarter_out),
+            in_specs=[half_spec, wd_spec],
+            out_specs=(out_cols(count), out_cols(count)),
+            compiler_params=kernel_params(8),
             name="down",
+            cost_estimate=cost(row_total * hidden * half_width, 3 * row_total * half_width),
         )(rows, w_down[0])
 
     def add(x, y):
         return (x.astype(F32) + y.astype(F32)).astype(BF16)
 
-    def sum_inner(rows, *earlier):
-        keep, send = down(rows)
-        near = add(keep, swap_inner(send, 1))
-        count = near.shape[0] // 2
-        far = near[count:] if not earlier else after(near[count:], *earlier)
-        near = add(near[:count], swap_inner(far, 2))
-        return near.reshape(4, rows_here, half_width)
-
-    def outer_piece(near, s):
-        return lax.dynamic_index_in_dim(near, (outer + s) % 4, 0, keepdims=False)
-
-    near = sum_inner(inner)
-    mine = [outer_piece(near, 0)] + [shift_outer(outer_piece(near, s), s) for s in (1, 2, 3)]
-    near = sum_inner(after(inner_other, near), *mine[1:])
-    others = [cross_outer(outer_piece(near, s), s) for s in range(4)]
-
-    out = jax.ShapeDtypeStruct((rows_here, model_width), BF16)
-    stream_out, normed_out = pl.pallas_call(
-        tail_kernel,
-        out_shape=(out, out),
-        in_specs=[smem] + [vmem] * 10,
-        out_specs=(vmem, vmem),
-        compiler_params=kernel_params(8),
-        name="closing",
-    )(place, stream_own, *mine, *others, gain_final[None])
+    def pieces(keep, core, far):
+        out = shape_of(rows_here, half_width)
+        return call(pieces_kernel, "pieces", 4, (out, out, out, out), keep, core, far)
+
+    keep_far, keep_near, core_send = pl.pallas_call(
+        down_both_kernel,
+        grid=(half_width // unit,),
+        out_shape=(quarter_out, quarter_out, shape_of(2 * count, half_width)),
+        in_specs=[half_spec, half_spec, wd_spec],
+        out_specs=(out_cols(count), out_cols(count), out_cols(2 * count)),
+        compiler_params=kernel_params(12),
+        name="down_both",
+        cost_estimate=cost(2 * row_total * hidden * half_width, 4 * row_total * half_width),
+    )(inner_far, inner_near, w_down[0])
+    core = swap_inner(core_send, 1)
+    far = swap_inner(add(keep_far, core[:count]), 2)
+    ready = far
+    cut = pieces(keep_near, core[count:], far)
+    mine = [cut[0]] + [shift_outer(cut[s], s) for s in (1, 2, 3)]
+
+    keep_far, core_send = down(after(far_other, ready))
+    far = swap_inner(add(keep_far, swap_inner(core_send, 1)), 2)
+    keep_near, core_send = down(after(near_other, far, *mine[1:]))
+    cut = pieces(keep_near, swap_inner(core_send, 1), far)
+    others = [cross_outer(cut[s], s) for s in range(4)]
+
+    out = shape_of(rows_here, model_width)
+    stream_out, normed_out = call(
+        tail_kernel, "closing", 8, (out, out), stream_own, *mine, *others, gain_final[None]
+    )
     return (stream_out[None], normed_out[None])
 
 

time: 167 us -> 133 us (0.80)
  waiting for transfers between devices: 92.6 us -> 70.3 us
  local copies, waits for them, and re-layouts: 20 us -> 5.46 us
  starting transfers between devices: 32.8 us -> 38 us
    ppermute x12 -> x9, waiting for transfers between devices: 32.5 us -> 8.79 us  [shift_outer(): lax.ppermute(x, 'expert', [(i, (i + 4 * s) % expert_count) for i in range...]
    ppermute x10 -> x11, waiting for transfers between devices: 40.8 us -> 25.2 us  [swap_inner(): return lax.ppermute(x, 'expert', [(i, i ^ j) for i in range(expert_count)])]
    unnamed x48 -> x16, local copies, waits for them, and re-layouts: 13.7 us -> 2.88 us
    ppermute x4 -> x5, waiting for transfers between devices: 15.5 us -> 25.7 us  [swap_dp(): return lax.ppermute(x, 'dp', [(0, 1), (1, 0)])]
    ppermute x0 -> x3, waiting for transfers between devices: none -> 6.38 us  [swap_outer(): lax.ppermute(x, 'expert', [(i, i ^ 4 * s) for i in range(expert_count)])]
    ppermute x0 -> x3, starting transfers between devices: none -> 4.62 us  [swap_outer(): lax.ppermute(x, 'expert', [(i, i ^ 4 * s) for i in range(expert_count)])]
    squeeze x1, local copies, waits for them, and re-layouts: 2.98 us -> 0.13 us  [body_paired(): gate_up_late = swap_dp(after(w_gate_up[0, depth:], arrived))]
    ppermute x4 -> x5, starting transfers between devices: 3.35 us -> 5.2 us  [swap_dp(): return lax.ppermute(x, 'dp', [(0, 1), (1, 0)])]
  transfers between devices with their start and end apart: 30 -> 32, of which waited for: 18 -> 18; matrix products, arithmetic and copies ran while one was open for 5% -> 2% of each run, Pallas kernels for 6% -> 7%
where the time goes in v4:
time: 133 us
  waiting for transfers between devices  70.3 us (53%)
  starting transfers between devices  38 us (29%)
  Pallas kernels  17.5 us (13%)
  local copies, waits for them, and re-layouts  5.46 us (4%)
  between operations  1.49 us (1%)
    ppermute x5, waiting for transfers between devices, swap_dp(): return lax.ppermute(x, 'dp', [(0, 1), (1, 0)])  25.7 us
    ppermute x11, waiting for transfers between devices, swap_inner(): return lax.ppermute(x, 'expert', [(i, i ^ j) for i in range(expert_count)])  25.2 us
    ppermute x9, starting transfers between devices, shift_outer(): lax.ppermute(x, 'expert', [(i, (i + 4 * s) % expert_count) for i in range...  14.6 us
    ppermute x9, waiting for transfers between devices, shift_outer(): lax.ppermute(x, 'expert', [(i, (i + 4 * s) % expert_count) for i in range...  8.79 us
    ppermute x11, starting transfers between devices, swap_inner(): return lax.ppermute(x, 'expert', [(i, i ^ j) for i in range(expert_count)])  6.9 us
    ppermute x4, starting transfers between devices, cross_outer(): lax.ppermute(x, ('dp', 'expert'), [(d * expert_count + i, (1 - d) * exper...  6.69 us
    ppermute x3, waiting for transfers between devices, swap_outer(): lax.ppermute(x, 'expert', [(i, i ^ 4 * s) for i in range(expert_count)])  6.38 us
    pallas_call x1, Pallas kernels, body_paired(): pl.pallas_call(first_gate_kernel, grid=(steps,), out_shape=(shape_of(row_...  5.81 us
  transfers between devices with their start and end apart: 32, of which 18 were waited for; matrix products, arithmetic and copies ran while one was open for 2% of the time, Pallas kernels for 7%

profile of v4, /device:TPU:0, one launch (start us, length us, event | category | flops | bytes accessed | tf_op | source)
XLA Modules:
  0.0 132.9 jit_solution(9195221508621851121)
XLA Ops:
  0.6 2.4 %slice_bitcast_fusion.1 = bf16[384,1536]{1,0:T(8,128)(2,1)} fusion(bf16[1,1024,1536]{2,1,0:T(8,128)(2,1)} %param.17), kind=kLoop, calls=%fused_computation.1 | loop fusion | bytes 2359296 | tf_op jit(solution)/shard_map/squeeze | solution.py:377
  3.1 3.0 %collective-permute-start.6 = (bf16[384,1536]{1,0:T(8,128)(2,1)}, bf16[384,1536]{1,0:T(8,128)(2,1)}, u32[]{:S(2)}, u32[]{:S(2)}) collective-permute-start(bf16[384,1536]{1,0:T(8,128)(2,1)} %slice_bitcast_fusion.1), channel_id=1, source_target_pairs={{0,16},{16,0},{1,17},{17,1},{2,18},{18,2},{3,19},{19,3},{4,20},{20... | collective-permute-start | bytes 3538952 | tf_op jit(solution)/shard_map/ppermute | solution.py:346
  6.1 1.5 %collective-permute-start.3 = (bf16[2048,128]{1,0:T(8,128)(2,1)}, bf16[2048,128]{1,0:T(8,128)(2,1)}, u32[]{:S(2)}, u32[]{:S(2)}) collective-permute-start(bf16[2048,128]{1,0:T(8,128)(2,1)} %w0.1), channel_id=1, source_target_pairs={{0,2},{1,3},{2,0},{3,1},{4,6},{5,7},{6,4},{7,5},{8,10},{9,11},{10,... | collective-permute-start | bytes 1572872 | tf_op jit(solution)/shard_map/ppermute | solution.py:365
  7.5 2.6 %collective-permute-start.1 = (bf16[64,2048]{1,0:T(8,128)(2,1)S(1)}, bf16[64,2048]{1,0:T(8,128)(2,1)}, u32[]{:S(2)}, u32[]{:S(2)}) collective-permute-start(bf16[64,2048]{1,0:T(8,128)(2,1)S(1)} %bitcast.24), channel_id=1, source_target_pairs={{0,8},{1,9},{2,10},{3,11},{4,12},{5,13},{6,14},{7,15},{8,0},{9,1},... | collective-permute-start | bytes 786440 | tf_op jit(solution)/shard_map/ppermute | solution.py:368
  10.1 9.6 %collective-permute-done.3.w2 = bf16[2048,128]{1,0:T(8,128)(2,1)} collective-permute-done((bf16[2048,128]{1,0:T(8,128)(2,1)}, bf16[2048,128]{1,0:T(8,128)(2,1)}, u32[]{:S(2)}, u32[]{:S(2)}) %collective-permute-start.3) | collective-permute-done | bytes 524320 | tf_op jit(solution)/shard_map/ppermute | solution.py:365
  19.8 0.5 collective-permute-start.5
  20.3 1.6 %collective-permute-start = (bf16[64,2048]{1,0:T(8,128)(2,1)S(1)}, bf16[64,2048]{1,0:T(8,128)(2,1)}, u32[]{:S(2)}, u32[]{:S(2)}) collective-permute-start(bf16[64,2048]{1,0:T(8,128)(2,1)S(1)} %bitcast.25), channel_id=1, source_target_pairs={{0,4},{1,5},{2,6},{3,7},{4,0},{5,1},{6,2},{7,3},{8,12},{9,13},{10,... | collective-permute-start | bytes 786440 | tf_op jit(solution)/shard_map/ppermute | solution.py:368
  21.8 0.5 collective-permute-start.2
  22.9 0.8 copy.12
  23.7 1.4 %copy.13 = f32[1,32,8]{2,1,0:T(8,128)} copy(f32[1,32,8]{1,2,0:T(8,128)} %param.15) | data formatting | bytes 2048 | tf_op args[5]
  25.1 0.7 copy-done.4
  25.8 0.4 prepare.1
  26.2 3.3 %collective-permute-done.a1 = bf16[64,2048]{1,0:T(8,128)(2,1)} collective-permute-done((bf16[64,2048]{1,0:T(8,128)(2,1)S(1)}, bf16[64,2048]{1,0:T(8,128)(2,1)}, u32[]{:S(2)}, u32[]{:S(2)}) %collective-permute-start) | collective-permute-done | bytes 262176 | tf_op jit(solution)/shard_map/ppermute | solution.py:368
  29.5 1.6 %collective-permute-start.7 = (bf16[32,512]{1,0:T(8,128)(2,1)S(1)}, bf16[32,512]{1,0:T(8,128)(2,1)S(1)}, u32[]{:S(2)}, u32[]{:S(2)}) collective-permute-start(bf16[32,512]{1,0:T(8,128)(2,1)S(1)} %get-tuple-element.45), channel_id=1, source_target_pairs={{0,4},{1,5},{2,6},{3,7},{4,8},{5,9},{6,10},{7,11},{8,12},{9,13},{1... | collective-permute-start | bytes 98312 | tf_op jit(solution)/shard_map/ppermute | solution.py:349
  31.1 3.1 %collective-permute-done.2.a3 = bf16[64,2048]{1,0:T(8,128)(2,1)} collective-permute-done((bf16[64,2048]{1,0:T(8,128)(2,1)}, bf16[64,2048]{1,0:T(8,128)(2,1)}, u32[]{:S(2)}, u32[]{:S(2)}) %collective-permute-start.2) | collective-permute-done | bytes 262176 | tf_op jit(solution)/shard_map/ppermute | solution.py:368
  34.2 2.9 %collective-permute-start.8 = (bf16[32,512]{1,0:T(8,128)(2,1)S(1)}, bf16[32,512]{1,0:T(8,128)(2,1)S(1)}, u32[]{:S(2)}, u32[]{:S(2)}) collective-permute-start(bf16[32,512]{1,0:T(8,128)(2,1)S(1)} %get-tuple-element.47), channel_id=1, source_target_pairs={{0,8},{1,9},{2,10},{3,11},{4,12},{5,13},{6,14},{7,15},{8,0},{9,1},... | collective-permute-start | bytes 98312 | tf_op jit(solution)/shard_map/ppermute | solution.py:349
  37.1 1.3 %collective-permute-start.9 = (bf16[32,512]{1,0:T(8,128)(2,1)S(1)}, bf16[32,512]{1,0:T(8,128)(2,1)S(1)}, u32[]{:S(2)}, u32[]{:S(2)}) collective-permute-start(bf16[32,512]{1,0:T(8,128)(2,1)S(1)} %get-tuple-element.49), channel_id=1, source_target_pairs={{0,12},{1,13},{2,14},{3,15},{4,0},{5,1},{6,2},{7,3},{8,4},{9,5},{1... | collective-permute-start | bytes 98312 | tf_op jit(solution)/shard_map/ppermute | solution.py:349
  38.5 3.1 %projection.1 = (bf16[128,512]{1,0:T(8,128)(2,1)S(1)}, bf16[128,512]{1,0:T(8,128)(2,1)S(1)}) custom-call(bf16[64,2048]{1,0:T(8,128)(2,1)S(1)} %bitcast.26, bf16[64,2048]{1,0:T(8,128)(2,1)} %collective-permute-done.a1, bf16[64,2048]{1,0:T(8,128)(2,1)} %collective-permute-done.1.a2, bf16[64,2048]{1,0:T(8,128)(2,1)} %collective-permute-done.2.a3, ...), custom_call_target="tpu_custom_call" | custom-call | flops 536870912 | bytes 3407872 | tf_op jit(solution)/shard_map/projection/pallas_call | solution.py:334
  41.6 0.6 collective-permute-start.10
  42.2 0.1 slice_bitcast_fusion
  42.3 4.6 %collective-permute-done.10.arrived = bf16[128,512]{1,0:T(8,128)(2,1)S(1)} collective-permute-done((bf16[128,512]{1,0:T(8,128)(2,1)S(1)}, bf16[128,512]{1,0:T(8,128)(2,1)S(1)}, u32[]{:S(2)}, u32[]{:S(2)}) %collective-permute-start.10) | collective-permute-done | bytes 131104 | tf_op jit(solution)/shard_map/ppermute | solution.py:346
  47.0 0.5 collective-permute-start.17
  47.5 3.5 %collective-permute-start.13 = (bf16[144,512]{1,0:T(8,128)(2,1)S(1)}, bf16[144,512]{1,0:T(8,128)(2,1)S(1)}, u32[]{:S(2)}, u32[]{:S(2)}) collective-permute-start(bf16[144,512]{1,0:T(8,128)(2,1)S(1)} %stream.1), channel_id=1, source_target_pairs={{0,12},{1,13},{2,14},{3,15},{4,0},{5,1},{6,2},{7,3},{8,4},{9,5},{1... | collective-permute-start | bytes 442376 | tf_op jit(solution)/shard_map/ppermute | solution.py:349
  51.0 0.6 collective-permute-start.11
  51.6 3.5 %collective-permute-done.13 = bf16[144,512]{1,0:T(8,128)(2,1)S(1)} collective-permute-done((bf16[144,512]{1,0:T(8,128)(2,1)S(1)}, bf16[144,512]{1,0:T(8,128)(2,1)S(1)}, u32[]{:S(2)}, u32[]{:S(2)}) %collective-permute-start.13) | collective-permute-done | bytes 147488 | tf_op jit(solution)/shard_map/ppermute | solution.py:349
  55.1 4.9 %collective-permute-done.12 = bf16[144,512]{1,0:T(8,128)(2,1)S(1)} collective-permute-done((bf16[144,512]{1,0:T(8,128)(2,1)S(1)}, bf16[144,512]{1,0:T(8,128)(2,1)S(1)}, u32[]{:S(2)}, u32[]{:S(2)}) %collective-permute-start.12) | collective-permute-done | bytes 147488 | tf_op jit(solution)/shard_map/ppermute | solution.py:349
  60.0 0.1 pad_maximum_fusion.blocks
  60.1 1.6 %collective-permute-start.14 = (bf16[4,144,512]{2,1,0:T(8,128)(2,1)S(1)}, bf16[4,144,512]{2,1,0:T(8,128)(2,1)S(1)}, u32[]{:S(2)}, u32[]{:S(2)}) collective-permute-start(bf16[4,144,512]{2,1,0:T(8,128)(2,1)S(1)} %pad_maximum_fusion.blocks), channel_id=1, source_target_pairs={{0,2},{1,3},{2,0},{3,1},{4,6},{5,7},{6,4},{7,5},{8,10},{9,11},{10,... | collective-permute-start | bytes 1769480 | tf_op jit(solution)/shard_map/ppermute | solution.py:365
  61.7 9.8 %collective-permute-done.14.blocks_x = bf16[4,144,512]{2,1,0:T(8,128)(2,1)S(1)} collective-permute-done((bf16[4,144,512]{2,1,0:T(8,128)(2,1)S(1)}, bf16[4,144,512]{2,1,0:T(8,128)(2,1)S(1)}, u32[]{:S(2)}, u32[]{:S(2)}) %collective-permute-start.14) | collective-permute-done | bytes 589856 | tf_op jit(solution)/shard_map/ppermute | solution.py:365
  71.5 2.0 %collective-permute-done.16.blocks_cx = bf16[4,144,512]{2,1,0:T(8,128)(2,1)S(1)} collective-permute-done((bf16[4,144,512]{2,1,0:T(8,128)(2,1)S(1)}, bf16[4,144,512]{2,1,0:T(8,128)(2,1)S(1)}, u32[]{:S(2)}, u32[]{:S(2)}) %collective-permute-start.16) | collective-permute-done | bytes 589856 | tf_op jit(solution)/shard_map/ppermute | solution.py:365
  73.5 5.8 %first_gate_up.1 = (f32[512,768]{1,0:T(8,128)S(1)}, f32[512,768]{1,0:T(8,128)S(1)}, bf16[512,640]{1,0:T(8,128)(2,1)S(1)}, f32[512,128]{1,0:T(8,128)S(1)}, bf16[32,2048]{1,0:T(8,128)(2,1)S(1)}) custom-call(bf16[4,144,512]{2,1,0:T(8,128)(2,1)S(1)} %pad_maximum_fusion.blocks, bf16[4,144,512]{2,1,0:T(8,128)(2,1)S(1)} %collective-permute-done.14.blocks_x, ...), custom_call_target="tpu_custom_call" | custom-call | flops 2214592512 | bytes 4718592 | tf_op jit(solution)/shard_map/first_gate_up/pallas_call | solution.py:437
  79.3 9.5 %collective-permute-done.17.gw.uw = bf16[640,1536]{1,0:T(8,128)(2,1)S(1)} collective-permute-done((bf16[640,1536]{1,0:T(8,128)(2,1)S(1)}, bf16[640,1536]{1,0:T(8,128)(2,1)S(1)}, u32[]{:S(2)}, u32[]{:S(2)}) %collective-permute-start.17) | collective-permute-done | bytes 1966112 | tf_op jit(solution)/shard_map/ppermute | solution.py:346
  88.8 2.4 %last_gate_up.1 = (bf16[256,768]{1,0:T(8,128)(2,1)S(1)}, bf16[256,768]{1,0:T(8,128)(2,1)S(1)}) custom-call(f32[512,768]{1,0:T(8,128)S(1)} %get-tuple-element.54.gate, f32[512,768]{1,0:T(8,128)S(1)} %get-tuple-element.55.up, bf16[512,640]{1,0:T(8,128)(2,1)S(1)} %get-tuple-element.56.rows, f32[512,128]{1,0:T(8,128)S(1)} %get-tuple-element.57.share, ...), custom_call_target="tpu_custom_call" | custom-call | flops 1006632960 | bytes 5505024 | tf_op jit(solution)/shard_map/last_gate_up/pallas_call | solution.py:478
  91.2 1.8 %down_both.1 = (bf16[128,1024]{1,0:T(8,128)(2,1)S(1)}, bf16[128,1024]{1,0:T(8,128)(2,1)S(1)}, bf16[256,1024]{1,0:T(8,128)(2,1)S(1)}) custom-call(bf16[256,768]{1,0:T(8,128)(2,1)S(1)} %get-tuple-element.59.far, bf16[256,768]{1,0:T(8,128)(2,1)S(1)} %get-tuple-element.60.near, bf16[768,1024]{1,0:T(8,128)(2,1)S(1)} %bitcast.20), custom_call_target="tpu_custom_call" | custom-call | flops 805306368 | bytes 2097152 | tf_op jit(solution)/shard_map/down_both/pallas_call | solution.py:522
  93.0 0.1 collective-permute-start.18
  93.1 0.6 collective-permute-start.24
  93.7 1.3 collective-permute-done.18
  95.0 0.1 add_convert_fusion.1
  95.1 1.6 %collective-permute-start.19 = (bf16[128,1024]{1,0:T(8,128)(2,1)S(1)}, bf16[128,1024]{1,0:T(8,128)(2,1)S(1)}, u32[]{:S(2)}, u32[]{:S(2)}) collective-permute-start(bf16[128,1024]{1,0:T(8,128)(2,1)S(1)} %add_convert_fusion.1), channel_id=1, source_target_pairs={{0,2},{1,3},{2,0},{3,1},{4,6},{5,7},{6,4},{7,5},{8,10},{9,11},{10,... | collective-permute-start | bytes 786440 | tf_op jit(solution)/shard_map/ppermute | solution.py:365
  96.7 8.0 %collective-permute-done.24.rows = bf16[256,768]{1,0:T(8,128)(2,1)S(1)} collective-permute-done((bf16[256,768]{1,0:T(8,128)(2,1)S(1)}, bf16[256,768]{1,0:T(8,128)(2,1)S(1)}, u32[]{:S(2)}, u32[]{:S(2)}) %collective-permute-start.24) | collective-permute-done | bytes 393248 | tf_op jit(solution)/shard_map/ppermute | solution.py:346
  104.7 1.4 %down.2 = (bf16[128,1024]{1,0:T(8,128)(2,1)S(1)}, bf16[128,1024]{1,0:T(8,128)(2,1)S(1)}) custom-call(bf16[256,768]{1,0:T(8,128)(2,1)S(1)} %collective-permute-done.24.rows, bf16[768,1024]{1,0:T(8,128)(2,1)S(1)} %bitcast.21), custom_call_target="tpu_custom_call" | custom-call | flops 402653184 | bytes 1572864 | tf_op jit(solution)/shard_map/down/pallas_call | solution.py:504
  106.1 0.1 collective-permute-start.25
  106.1 0.6 collective-permute-start.23
  106.7 0.9 collective-permute-done.25
  107.7 0.1 add_convert_fusion
  107.7 1.6 %collective-permute-start.26 = (bf16[128,1024]{1,0:T(8,128)(2,1)S(1)}, bf16[128,1024]{1,0:T(8,128)(2,1)S(1)}, u32[]{:S(2)}, u32[]{:S(2)}) collective-permute-start(bf16[128,1024]{1,0:T(8,128)(2,1)S(1)} %add_convert_fusion), channel_id=1, source_target_pairs={{0,2},{1,3},{2,0},{3,1},{4,6},{5,7},{6,4},{7,5},{8,10},{9,11},{10,... | collective-permute-start | bytes 786440 | tf_op jit(solution)/shard_map/ppermute | solution.py:365
  109.3 0.1 pieces.2
  109.4 1.0 collective-permute-start.20
  110.4 2.1 %collective-permute-start.21 = (bf16[32,1024]{1,0:T(8,128)(2,1)S(1)}, bf16[32,1024]{1,0:T(8,128)(2,1)S(1)}, u32[]{:S(2)}, u32[]{:S(2)}) collective-permute-start(bf16[32,1024]{1,0:T(8,128)(2,1)S(1)} %get-tuple-element.66), channel_id=1, source_target_pairs={{0,8},{1,9},{2,10},{3,11},{4,12},{5,13},{6,14},{7,15},{8,0},{9,1},... | collective-permute-start | bytes 196616 | tf_op jit(solution)/shard_map/ppermute | solution.py:349
  112.6 1.5 %collective-permute-start.22 = (bf16[32,1024]{1,0:T(8,128)(2,1)S(1)}, bf16[32,1024]{1,0:T(8,128)(2,1)S(1)}, u32[]{:S(2)}, u32[]{:S(2)}) collective-permute-start(bf16[32,1024]{1,0:T(8,128)(2,1)S(1)} %get-tuple-element.67), channel_id=1, source_target_pairs={{0,12},{1,13},{2,14},{3,15},{4,0},{5,1},{6,2},{7,3},{8,4},{9,5},{1... | collective-permute-start | bytes 196616 | tf_op jit(solution)/shard_map/ppermute | solution.py:349
  114.1 3.6 %collective-permute-done.23.rows = bf16[256,768]{1,0:T(8,128)(2,1)S(1)} collective-permute-done((bf16[256,768]{1,0:T(8,128)(2,1)S(1)}, bf16[256,768]{1,0:T(8,128)(2,1)S(1)}, u32[]{:S(2)}, u32[]{:S(2)}) %collective-permute-start.23) | collective-permute-done | bytes 393248 | tf_op jit(solution)/shard_map/ppermute | solution.py:346
  117.7 0.4 collective-permute-done.21.m2
  118.1 1.4 %down.3 = (bf16[128,1024]{1,0:T(8,128)(2,1)S(1)}, bf16[128,1024]{1,0:T(8,128)(2,1)S(1)}) custom-call(bf16[256,768]{1,0:T(8,128)(2,1)S(1)} %collective-permute-done.23.rows, bf16[768,1024]{1,0:T(8,128)(2,1)S(1)} %bitcast.22), custom_call_target="tpu_custom_call" | custom-call | flops 402653184 | bytes 1572864 | tf_op jit(solution)/shard_map/down/pallas_call | solution.py:504
  119.5 0.1 collective-permute-start.27
  119.5 1.5 %collective-permute-done.27.core = bf16[128,1024]{1,0:T(8,128)(2,1)S(1)} collective-permute-done((bf16[128,1024]{1,0:T(8,128)(2,1)S(1)}, bf16[128,1024]{1,0:T(8,128)(2,1)S(1)}, u32[]{:S(2)}, u32[]{:S(2)}) %collective-permute-start.27) | collective-permute-done | bytes 262176 | tf_op jit(solution)/shard_map/ppermute | solution.py:365
  121.1 0.1 pieces.3
  121.2 0.7 collective-permute-start.28
  121.8 2.5 %collective-permute-start.29 = (bf16[32,1024]{1,0:T(8,128)(2,1)S(1)}, bf16[32,1024]{1,0:T(8,128)(2,1)S(1)}, u32[]{:S(2)}, u32[]{:S(2)}) collective-permute-start(bf16[32,1024]{1,0:T(8,128)(2,1)S(1)} %get-tuple-element.75), channel_id=1, source_target_pairs={{0,20},{1,21},{2,22},{3,23},{4,24},{5,25},{6,26},{7,27},{8,28},{9,... | collective-permute-start | bytes 196616 | tf_op jit(solution)/shard_map/ppermute | solution.py:354
  124.3 1.5 %collective-permute-start.30 = (bf16[32,1024]{1,0:T(8,128)(2,1)S(1)}, bf16[32,1024]{1,0:T(8,128)(2,1)S(1)}, u32[]{:S(2)}, u32[]{:S(2)}) collective-permute-start(bf16[32,1024]{1,0:T(8,128)(2,1)S(1)} %get-tuple-element.76), channel_id=1, source_target_pairs={{0,24},{1,25},{2,26},{3,27},{4,28},{5,29},{6,30},{7,31},{8,16},{9,... | collective-permute-start | bytes 196616 | tf_op jit(solution)/shard_map/ppermute | solution.py:354
  125.8 2.0 %collective-permute-start.31 = (bf16[32,1024]{1,0:T(8,128)(2,1)S(1)}, bf16[32,1024]{1,0:T(8,128)(2,1)S(1)}, u32[]{:S(2)}, u32[]{:S(2)}) collective-permute-start(bf16[32,1024]{1,0:T(8,128)(2,1)S(1)} %get-tuple-element.77), channel_id=1, source_target_pairs={{0,28},{1,29},{2,30},{3,31},{4,16},{5,17},{6,18},{7,19},{8,20},{9,... | collective-permute-start | bytes 196616 | tf_op jit(solution)/shard_map/ppermute | solution.py:354
  127.9 1.6 %collective-permute-done.29.o1 = bf16[32,1024]{1,0:T(8,128)(2,1)S(1)} collective-permute-done((bf16[32,1024]{1,0:T(8,128)(2,1)S(1)}, bf16[32,1024]{1,0:T(8,128)(2,1)S(1)}, u32[]{:S(2)}, u32[]{:S(2)}) %collective-permute-start.29) | collective-permute-done | bytes 65568 | tf_op jit(solution)/shard_map/ppermute | solution.py:354
  129.5 2.1 %collective-permute-done.30.o2 = bf16[32,1024]{1,0:T(8,128)(2,1)S(1)} collective-permute-done((bf16[32,1024]{1,0:T(8,128)(2,1)S(1)}, bf16[32,1024]{1,0:T(8,128)(2,1)S(1)}, u32[]{:S(2)}, u32[]{:S(2)}) %collective-permute-start.30) | collective-permute-done | bytes 65568 | tf_op jit(solution)/shard_map/ppermute | solution.py:354
  131.6 0.4 collective-permute-done.31.o3
  132.0 0.9 closing.1
  (33 shorter events, 0.2 us)
Async XLA Ops:
  0.6 6.9 %copy-start.2 = (bf16[1,64,2048]{2,1,0:T(8,128)(2,1)S(1)}, bf16[1,64,2048]{2,1,0:T(8,128)(2,1)}, u32[]{:S(2)}) copy-start(bf16[1,64,2048]{2,1,0:T(8,128)(2,1)} %param.10) | copy-start | bytes 786436
  0.6 24.4 %copy-start.3 = (bf16[1,32,2048]{2,1,0:T(8,128)(2,1)S(1)}, bf16[1,32,2048]{2,1,0:T(8,128)(2,1)}, u32[]{:S(2)}) copy-start(bf16[1,32,2048]{2,1,0:T(8,128)(2,1)} %param.11) | copy-start | bytes 393220
  3.1 39.1 %copy-start = (bf16[1,1024,1536]{2,1,0:T(8,128)(2,1)S(1)}, bf16[1,1024,1536]{2,1,0:T(8,128)(2,1)}, u32[]{:S(2)}) copy-start(bf16[1,1024,1536]{2,1,0:T(8,128)(2,1)} %param.17) | copy-start | bytes 9437188
  3.1 38.5 %collective-permute-start.6 = (bf16[384,1536]{1,0:T(8,128)(2,1)}, bf16[384,1536]{1,0:T(8,128)(2,1)}, u32[]{:S(2)}, u32[]{:S(2)}) collective-permute-start(bf16[384,1536]{1,0:T(8,128)(2,1)} %slice_bitcast_fusion.1), channel_id=1, source_target_pairs={{0,16},{16,0},{1,17},{17,1},{2,18},{18,2},{3,19},{19,3},{4,20},{20... | collective-permute-start | bytes 3538952 | tf_op jit(solution)/shard_map/ppermute | solution.py:346
  6.1 13.7 %collective-permute-start.3 = (bf16[2048,128]{1,0:T(8,128)(2,1)}, bf16[2048,128]{1,0:T(8,128)(2,1)}, u32[]{:S(2)}, u32[]{:S(2)}) collective-permute-start(bf16[2048,128]{1,0:T(8,128)(2,1)} %w0.1), channel_id=1, source_target_pairs={{0,2},{1,3},{2,0},{3,1},{4,6},{5,7},{6,4},{7,5},{8,10},{9,11},{10,... | collective-permute-start | bytes 1572872 | tf_op jit(solution)/shard_map/ppermute | solution.py:365
  7.5 14.3 %collective-permute-start.1 = (bf16[64,2048]{1,0:T(8,128)(2,1)S(1)}, bf16[64,2048]{1,0:T(8,128)(2,1)}, u32[]{:S(2)}, u32[]{:S(2)}) collective-permute-start(bf16[64,2048]{1,0:T(8,128)(2,1)S(1)} %bitcast.24), channel_id=1, source_target_pairs={{0,8},{1,9},{2,10},{3,11},{4,12},{5,13},{6,14},{7,15},{8,0},{9,1},... | collective-permute-start | bytes 786440 | tf_op jit(solution)/shard_map/ppermute | solution.py:368
  19.8 17.4 %collective-permute-start.4 = (bf16[2048,128]{1,0:T(8,128)(2,1)}, bf16[2048,128]{1,0:T(8,128)(2,1)}, u32[]{:S(2)}, u32[]{:S(2)}) collective-permute-start(bf16[2048,128]{1,0:T(8,128)(2,1)} %w0.1), channel_id=1, source_target_pairs={{0,1},{1,0},{2,3},{3,2},{4,5},{5,4},{6,7},{7,6},{8,9},{9,8},{10,11... | collective-permute-start | bytes 1572872 | tf_op jit(solution)/shard_map/ppermute | solution.py:365
  19.8 18.7 %collective-permute-start.5 = (bf16[2048,128]{1,0:T(8,128)(2,1)}, bf16[2048,128]{1,0:T(8,128)(2,1)}, u32[]{:S(2)}, u32[]{:S(2)}) collective-permute-start(bf16[2048,128]{1,0:T(8,128)(2,1)} %collective-permute-done.3.w2), channel_id=1, source_target_pairs={{0,1},{1,0},{2,3},{3,2},{4,5},{5,4},{6,7},{7,6},{8,9},{9,8},{10,11... | collective-permute-start | bytes 1572872 | tf_op jit(solution)/shard_map/ppermute | solution.py:365
  20.3 9.3 %collective-permute-start = (bf16[64,2048]{1,0:T(8,128)(2,1)S(1)}, bf16[64,2048]{1,0:T(8,128)(2,1)}, u32[]{:S(2)}, u32[]{:S(2)}) collective-permute-start(bf16[64,2048]{1,0:T(8,128)(2,1)S(1)} %bitcast.25), channel_id=1, source_target_pairs={{0,4},{1,5},{2,6},{3,7},{4,0},{5,1},{6,2},{7,3},{8,12},{9,13},{10,... | collective-permute-start | bytes 786440 | tf_op jit(solution)/shard_map/ppermute | solution.py:368
  21.8 12.4 %collective-permute-start.2 = (bf16[64,2048]{1,0:T(8,128)(2,1)}, bf16[64,2048]{1,0:T(8,128)(2,1)}, u32[]{:S(2)}, u32[]{:S(2)}) collective-permute-start(bf16[64,2048]{1,0:T(8,128)(2,1)} %collective-permute-done.1.a2), channel_id=1, source_target_pairs={{0,4},{1,5},{2,6},{3,7},{4,0},{5,1},{6,2},{7,3},{8,12},{9,13},{10,... | collective-permute-start | bytes 786440 | tf_op jit(solution)/shard_map/ppermute | solution.py:368
  25.1 0.7 copy-start.4
  29.5 12.0 %collective-permute-start.7 = (bf16[32,512]{1,0:T(8,128)(2,1)S(1)}, bf16[32,512]{1,0:T(8,128)(2,1)S(1)}, u32[]{:S(2)}, u32[]{:S(2)}) collective-permute-start(bf16[32,512]{1,0:T(8,128)(2,1)S(1)} %get-tuple-element.45), channel_id=1, source_target_pairs={{0,4},{1,5},{2,6},{3,7},{4,8},{5,9},{6,10},{7,11},{8,12},{9,13},{1... | collective-permute-start | bytes 98312 | tf_op jit(solution)/shard_map/ppermute | solution.py:349
  34.2 7.4 %collective-permute-start.8 = (bf16[32,512]{1,0:T(8,128)(2,1)S(1)}, bf16[32,512]{1,0:T(8,128)(2,1)S(1)}, u32[]{:S(2)}, u32[]{:S(2)}) collective-permute-start(bf16[32,512]{1,0:T(8,128)(2,1)S(1)} %get-tuple-element.47), channel_id=1, source_target_pairs={{0,8},{1,9},{2,10},{3,11},{4,12},{5,13},{6,14},{7,15},{8,0},{9,1},... | collective-permute-start | bytes 98312 | tf_op jit(solution)/shard_map/ppermute | solution.py:349
  37.1 4.5 %collective-permute-start.9 = (bf16[32,512]{1,0:T(8,128)(2,1)S(1)}, bf16[32,512]{1,0:T(8,128)(2,1)S(1)}, u32[]{:S(2)}, u32[]{:S(2)}) collective-permute-start(bf16[32,512]{1,0:T(8,128)(2,1)S(1)} %get-tuple-element.49), channel_id=1, source_target_pairs={{0,12},{1,13},{2,14},{3,15},{4,0},{5,1},{6,2},{7,3},{8,4},{9,5},{1... | collective-permute-start | bytes 98312 | tf_op jit(solution)/shard_map/ppermute | solution.py:349
  41.6 31.8 %copy-start.5 = (f32[2048]{0:T(1024)S(1)}, f32[2048]{0:T(1024)}, u32[]{:S(2)}) copy-start(f32[2048]{0:T(1024)} %param.13) | copy-start | bytes 24580
  41.6 5.3 %collective-permute-start.10 = (bf16[128,512]{1,0:T(8,128)(2,1)S(1)}, bf16[128,512]{1,0:T(8,128)(2,1)S(1)}, u32[]{:S(2)}, u32[]{:S(2)}) collective-permute-start(bf16[128,512]{1,0:T(8,128)(2,1)S(1)} %get-tuple-element.50), channel_id=1, source_target_pairs={{0,16},{16,0},{1,17},{17,1},{2,18},{18,2},{3,19},{19,3},{4,20},{20... | collective-permute-start | bytes 393224 | tf_op jit(solution)/shard_map/ppermute | solution.py:346
  47.0 41.8 %collective-permute-start.17 = (bf16[640,1536]{1,0:T(8,128)(2,1)S(1)}, bf16[640,1536]{1,0:T(8,128)(2,1)S(1)}, u32[]{:S(2)}, u32[]{:S(2)}) collective-permute-start(bf16[640,1536]{1,0:T(8,128)(2,1)S(1)} %slice_bitcast_fusion), channel_id=1, source_target_pairs={{0,16},{16,0},{1,17},{17,1},{2,18},{18,2},{3,19},{19,3},{4,20},{20... | collective-permute-start | bytes 5898248 | tf_op jit(solution)/shard_map/ppermute | solution.py:346
  47.5 7.5 %collective-permute-start.13 = (bf16[144,512]{1,0:T(8,128)(2,1)S(1)}, bf16[144,512]{1,0:T(8,128)(2,1)S(1)}, u32[]{:S(2)}, u32[]{:S(2)}) collective-permute-start(bf16[144,512]{1,0:T(8,128)(2,1)S(1)} %stream.1), channel_id=1, source_target_pairs={{0,12},{1,13},{2,14},{3,15},{4,0},{5,1},{6,2},{7,3},{8,4},{9,5},{1... | collective-permute-start | bytes 442376 | tf_op jit(solution)/shard_map/ppermute | solution.py:349
  51.0 9.0 %collective-permute-start.12 = (bf16[144,512]{1,0:T(8,128)(2,1)S(1)}, bf16[144,512]{1,0:T(8,128)(2,1)S(1)}, u32[]{:S(2)}, u32[]{:S(2)}) collective-permute-start(bf16[144,512]{1,0:T(8,128)(2,1)S(1)} %stream.1), channel_id=1, source_target_pairs={{0,8},{1,9},{2,10},{3,11},{4,12},{5,13},{6,14},{7,15},{8,0},{9,1},... | collective-permute-start | bytes 442376 | tf_op jit(solution)/shard_map/ppermute | solution.py:349
  51.0 9.0 %collective-permute-start.11 = (bf16[144,512]{1,0:T(8,128)(2,1)S(1)}, bf16[144,512]{1,0:T(8,128)(2,1)S(1)}, u32[]{:S(2)}, u32[]{:S(2)}) collective-permute-start(bf16[144,512]{1,0:T(8,128)(2,1)S(1)} %stream.1), channel_id=1, source_target_pairs={{0,4},{1,5},{2,6},{3,7},{4,8},{5,9},{6,10},{7,11},{8,12},{9,13},{1... | collective-permute-start | bytes 442376 | tf_op jit(solution)/shard_map/ppermute | solution.py:349
  60.1 11.3 %collective-permute-start.14 = (bf16[4,144,512]{2,1,0:T(8,128)(2,1)S(1)}, bf16[4,144,512]{2,1,0:T(8,128)(2,1)S(1)}, u32[]{:S(2)}, u32[]{:S(2)}) collective-permute-start(bf16[4,144,512]{2,1,0:T(8,128)(2,1)S(1)} %pad_maximum_fusion.blocks), channel_id=1, source_target_pairs={{0,2},{1,3},{2,0},{3,1},{4,6},{5,7},{6,4},{7,5},{8,10},{9,11},{10,... | collective-permute-start | bytes 1769480 | tf_op jit(solution)/shard_map/ppermute | solution.py:365
  61.7 9.8 %collective-permute-start.15 = (bf16[4,144,512]{2,1,0:T(8,128)(2,1)S(1)}, bf16[4,144,512]{2,1,0:T(8,128)(2,1)S(1)}, u32[]{:S(2)}, u32[]{:S(2)}) collective-permute-start(bf16[4,144,512]{2,1,0:T(8,128)(2,1)S(1)} %pad_maximum_fusion.blocks), channel_id=1, source_target_pairs={{0,1},{1,0},{2,3},{3,2},{4,5},{5,4},{6,7},{7,6},{8,9},{9,8},{10,11... | collective-permute-start | bytes 1769480 | tf_op jit(solution)/shard_map/ppermute | solution.py:365
  71.5 2.0 %collective-permute-start.16 = (bf16[4,144,512]{2,1,0:T(8,128)(2,1)S(1)}, bf16[4,144,512]{2,1,0:T(8,128)(2,1)S(1)}, u32[]{:S(2)}, u32[]{:S(2)}) collective-permute-start(bf16[4,144,512]{2,1,0:T(8,128)(2,1)S(1)} %collective-permute-done.14.blocks_x), channel_id=1, source_target_pairs={{0,1},{1,0},{2,3},{3,2},{4,5},{5,4},{6,7},{7,6},{8,9},{9,8},{10,11... | collective-permute-start | bytes 1769480 | tf_op jit(solution)/shard_map/ppermute | solution.py:365
  88.8 2.4 %copy-start.1 = (bf16[1,768,1024]{2,1,0:T(8,128)(2,1)S(1)}, bf16[1,768,1024]{2,1,0:T(8,128)(2,1)}, u32[]{:S(2)}) copy-start(bf16[1,768,1024]{2,1,0:T(8,128)(2,1)} %param.18) | copy-start | bytes 4718596
  93.0 2.0 %collective-permute-start.18 = (bf16[256,1024]{1,0:T(8,128)(2,1)S(1)}, bf16[256,1024]{1,0:T(8,128)(2,1)S(1)}, u32[]{:S(2)}, u32[]{:S(2)}) collective-permute-start(bf16[256,1024]{1,0:T(8,128)(2,1)S(1)} %get-tuple-element.62), channel_id=1, source_target_pairs={{0,1},{1,0},{2,3},{3,2},{4,5},{5,4},{6,7},{7,6},{8,9},{9,8},{10,11... | collective-permute-start | bytes 1572872 | tf_op jit(solution)/shard_map/ppermute | solution.py:365
  93.1 11.5 %collective-permute-start.24 = (bf16[256,768]{1,0:T(8,128)(2,1)S(1)}, bf16[256,768]{1,0:T(8,128)(2,1)S(1)}, u32[]{:S(2)}, u32[]{:S(2)}) collective-permute-start(bf16[256,768]{1,0:T(8,128)(2,1)S(1)} %get-tuple-element.59.far), channel_id=1, source_target_pairs={{0,16},{16,0},{1,17},{17,1},{2,18},{18,2},{3,19},{19,3},{4,20},{20... | collective-permute-start | bytes 1179656 | tf_op jit(solution)/shard_map/ppermute | solution.py:346
  95.1 9.6 %collective-permute-start.19 = (bf16[128,1024]{1,0:T(8,128)(2,1)S(1)}, bf16[128,1024]{1,0:T(8,128)(2,1)S(1)}, u32[]{:S(2)}, u32[]{:S(2)}) collective-permute-start(bf16[128,1024]{1,0:T(8,128)(2,1)S(1)} %add_convert_fusion.1), channel_id=1, source_target_pairs={{0,2},{1,3},{2,0},{3,1},{4,6},{5,7},{6,4},{7,5},{8,10},{9,11},{10,... | collective-permute-start | bytes 786440 | tf_op jit(solution)/shard_map/ppermute | solution.py:365
  106.1 1.6 %collective-permute-start.25 = (bf16[128,1024]{1,0:T(8,128)(2,1)S(1)}, bf16[128,1024]{1,0:T(8,128)(2,1)S(1)}, u32[]{:S(2)}, u32[]{:S(2)}) collective-permute-start(bf16[128,1024]{1,0:T(8,128)(2,1)S(1)} %get-tuple-element.70), channel_id=1, source_target_pairs={{0,1},{1,0},{2,3},{3,2},{4,5},{5,4},{6,7},{7,6},{8,9},{9,8},{10,11... | collective-permute-start | bytes 786440 | tf_op jit(solution)/shard_map/ppermute | solution.py:365
  106.1 11.5 %collective-permute-start.23 = (bf16[256,768]{1,0:T(8,128)(2,1)S(1)}, bf16[256,768]{1,0:T(8,128)(2,1)S(1)}, u32[]{:S(2)}, u32[]{:S(2)}) collective-permute-start(bf16[256,768]{1,0:T(8,128)(2,1)S(1)} %get-tuple-element.60.near), channel_id=1, source_target_pairs={{0,16},{16,0},{1,17},{17,1},{2,18},{18,2},{3,19},{19,3},{4,20},{20... | collective-permute-start | bytes 1179656 | tf_op jit(solution)/shard_map/ppermute | solution.py:346
  107.7 24.3 %copy-start.6 = (f32[2048]{0:T(1024)S(1)}, f32[2048]{0:T(1024)}, u32[]{:S(2)}) copy-start(f32[2048]{0:T(1024)} %param.19) | copy-start | bytes 24580
  107.7 10.3 %collective-permute-start.26 = (bf16[128,1024]{1,0:T(8,128)(2,1)S(1)}, bf16[128,1024]{1,0:T(8,128)(2,1)S(1)}, u32[]{:S(2)}, u32[]{:S(2)}) collective-permute-start(bf16[128,1024]{1,0:T(8,128)(2,1)S(1)} %add_convert_fusion), channel_id=1, source_target_pairs={{0,2},{1,3},{2,0},{3,1},{4,6},{5,7},{6,4},{7,5},{8,10},{9,11},{10,... | collective-permute-start | bytes 786440 | tf_op jit(solution)/shard_map/ppermute | solution.py:365
  109.4 8.2 %collective-permute-start.20 = (bf16[32,1024]{1,0:T(8,128)(2,1)S(1)}, bf16[32,1024]{1,0:T(8,128)(2,1)S(1)}, u32[]{:S(2)}, u32[]{:S(2)}) collective-permute-start(bf16[32,1024]{1,0:T(8,128)(2,1)S(1)} %get-tuple-element.65), channel_id=1, source_target_pairs={{0,4},{1,5},{2,6},{3,7},{4,8},{5,9},{6,10},{7,11},{8,12},{9,13},{1... | collective-permute-start | bytes 196616 | tf_op jit(solution)/shard_map/ppermute | solution.py:349
  110.4 7.6 %collective-permute-start.21 = (bf16[32,1024]{1,0:T(8,128)(2,1)S(1)}, bf16[32,1024]{1,0:T(8,128)(2,1)S(1)}, u32[]{:S(2)}, u32[]{:S(2)}) collective-permute-start(bf16[32,1024]{1,0:T(8,128)(2,1)S(1)} %get-tuple-element.66), channel_id=1, source_target_pairs={{0,8},{1,9},{2,10},{3,11},{4,12},{5,13},{6,14},{7,15},{8,0},{9,1},... | collective-permute-start | bytes 196616 | tf_op jit(solution)/shard_map/ppermute | solution.py:349
  112.6 5.5 %collective-permute-start.22 = (bf16[32,1024]{1,0:T(8,128)(2,1)S(1)}, bf16[32,1024]{1,0:T(8,128)(2,1)S(1)}, u32[]{:S(2)}, u32[]{:S(2)}) collective-permute-start(bf16[32,1024]{1,0:T(8,128)(2,1)S(1)} %get-tuple-element.67), channel_id=1, source_target_pairs={{0,12},{1,13},{2,14},{3,15},{4,0},{5,1},{6,2},{7,3},{8,4},{9,5},{1... | collective-permute-start | bytes 196616 | tf_op jit(solution)/shard_map/ppermute | solution.py:349
  119.5 1.6 %collective-permute-start.27 = (bf16[128,1024]{1,0:T(8,128)(2,1)S(1)}, bf16[128,1024]{1,0:T(8,128)(2,1)S(1)}, u32[]{:S(2)}, u32[]{:S(2)}) collective-permute-start(bf16[128,1024]{1,0:T(8,128)(2,1)S(1)} %get-tuple-element.73), channel_id=1, source_target_pairs={{0,1},{1,0},{2,3},{3,2},{4,5},{5,4},{6,7},{7,6},{8,9},{9,8},{10,11... | collective-permute-start | bytes 786440 | tf_op jit(solution)/shard_map/ppermute | solution.py:365
  121.2 6.7 %collective-permute-start.28 = (bf16[32,1024]{1,0:T(8,128)(2,1)S(1)}, bf16[32,1024]{1,0:T(8,128)(2,1)S(1)}, u32[]{:S(2)}, u32[]{:S(2)}) collective-permute-start(bf16[32,1024]{1,0:T(8,128)(2,1)S(1)} %get-tuple-element.74), channel_id=1, source_target_pairs={{0,16},{1,17},{2,18},{3,19},{4,20},{5,21},{6,22},{7,23},{8,24},{9,... | collective-permute-start | bytes 196616 | tf_op jit(solution)/shard_map/ppermute | solution.py:354
  121.8 7.7 %collective-permute-start.29 = (bf16[32,1024]{1,0:T(8,128)(2,1)S(1)}, bf16[32,1024]{1,0:T(8,128)(2,1)S(1)}, u32[]{:S(2)}, u32[]{:S(2)}) collective-permute-start(bf16[32,1024]{1,0:T(8,128)(2,1)S(1)} %get-tuple-element.75), channel_id=1, source_target_pairs={{0,20},{1,21},{2,22},{3,23},{4,24},{5,25},{6,26},{7,27},{8,28},{9,... | collective-permute-start | bytes 196616 | tf_op jit(solution)/shard_map/ppermute | solution.py:354
  124.3 7.3 %collective-permute-start.30 = (bf16[32,1024]{1,0:T(8,128)(2,1)S(1)}, bf16[32,1024]{1,0:T(8,128)(2,1)S(1)}, u32[]{:S(2)}, u32[]{:S(2)}) collective-permute-start(bf16[32,1024]{1,0:T(8,128)(2,1)S(1)} %get-tuple-element.76), channel_id=1, source_target_pairs={{0,24},{1,25},{2,26},{3,27},{4,28},{5,29},{6,30},{7,31},{8,16},{9,... | collective-permute-start | bytes 196616 | tf_op jit(solution)/shard_map/ppermute | solution.py:354
  125.8 6.2 %collective-permute-start.31 = (bf16[32,1024]{1,0:T(8,128)(2,1)S(1)}, bf16[32,1024]{1,0:T(8,128)(2,1)S(1)}, u32[]{:S(2)}, u32[]{:S(2)}) collective-permute-start(bf16[32,1024]{1,0:T(8,128)(2,1)S(1)} %get-tuple-element.77), channel_id=1, source_target_pairs={{0,28},{1,29},{2,30},{3,31},{4,16},{5,17},{6,18},{7,19},{8,20},{9,... | collective-permute-start | bytes 196616 | tf_op jit(solution)/shard_map/ppermute | solution.py:354

commit v5 on v4

--- a/solution.py
+++ b/solution.py
@@ -1,3 +1,4 @@
+import functools
 import math
 
 import jax
@@ -211,78 +212,105 @@
     block_ref[count:, :] = share[...]
 
 
+def piece_kernel(at, weights, out, semaphores):
+    width = out.shape[1] // 2
+    copies = [
+        pltpu.make_async_copy(
+            weights.at[:, pl.ds((2 * i + at) * width, width)],
+            out.at[:, pl.ds(i * width, width)],
+            semaphores.at[i],
+        )
+        for i in range(2)
+    ]
+    for copy in copies:
+        copy.start()
+    for copy in copies:
+        copy.wait()
+
+
+def swiglu(gate, up, share):
+    return (gate / (1.0 + jnp.exp(-gate)) * up * share).astype(BF16)
+
+
 def first_gate_kernel(
-    blocks, blocks_x, blocks_c, blocks_cx, gain, ga, ua, gb, ub,
-    gate_ref, up_ref, last_ref, share_ref, own_ref, normed,
+    blocks, blocks_x, blocks_c, blocks_cx, gain, own, early,
+    inner_ref, part_ref, other_ref, share_ref, own_ref, normed,
 ):
     expert, outer, inner, dp = seat()
-    step = pl.program_id(0)
     width = blocks.shape[2]
     count = share_ref.shape[0] // 4
     experts = blocks.shape[1] - count
     half = normed.shape[1] // 2
     small = own_ref.shape[0]
-    depth = gb.shape[0]
-    rest = half - depth
-
-    @pl.when(step == 0)
-    def _():
-        picked = lax.broadcasted_iota(jnp.int32, (experts, count), 0) == expert
-        diagonal = lax.broadcasted_iota(jnp.int32, (count, count), 0) == lax.broadcasted_iota(
-            jnp.int32, (count, count), 1
-        )
-        for j, group in enumerate((blocks_x, blocks_cx, blocks, blocks_c)):
-            rows = slice(j * count, (j + 1) * count)
-            square = jnp.zeros((count, 1), F32)
-            share = jnp.zeros((experts, count), F32)
-            for s in range(4):
-                value = group[s, 0:count, :]
-                normed[rows, aligned((outer + 4 - s) & 3, width)] = value
-                value = value.astype(F32)
-                square = square + jnp.sum(value * value, axis=1, keepdims=True)
-                share = share + group[s, count : count + experts, 0:count].astype(F32)
-            line = jnp.sum(jnp.where(picked, share, 0.0), axis=0, keepdims=True)
-            column = jnp.sum(jnp.where(diagonal, line, 0.0), axis=1, keepdims=True)
-            share_ref[rows, :] = jnp.broadcast_to(column, (count, share_ref.shape[1]))
-            if j == 2:
-                own_ref[...] = normed[aligned(outer + 2 * (count // small), small), :]
-            scale = lax.rsqrt(square / (4 * width) + 1e-06)
-            for s in range(4):
-                cols = slice(s * width, (s + 1) * width)
-                value = normed[rows, cols].astype(F32)
-                normed[rows, cols] = (value * scale * gain[:, cols]).astype(BF16)
-        last_ref[...] = normed[:, pl.ds(pl.multiple_of((1 - dp) * half + depth, 128), rest)]
+    cut = inner_ref.shape[1]
+    picked = lax.broadcasted_iota(jnp.int32, (experts, count), 0) == expert
+    diagonal = lax.broadcasted_iota(jnp.int32, (count, count), 0) == lax.broadcasted_iota(
+        jnp.int32, (count, count), 1
+    )
+    for j, group in enumerate((blocks_x, blocks_cx, blocks, blocks_c)):
+        rows = slice(j * count, (j + 1) * count)
+        square = jnp.zeros((count, 1), F32)
+        share = jnp.zeros((experts, count), F32)
+        for s in range(4):
+            value = group[s, 0:count, :]
+            normed[rows, aligned((outer + 4 - s) & 3, width)] = value
+            value = value.astype(F32)
+            square = square + jnp.sum(value * value, axis=1, keepdims=True)
+            share = share + group[s, count : count + experts, 0:count].astype(F32)
+        line = jnp.sum(jnp.where(picked, share, 0.0), axis=0, keepdims=True)
+        column = jnp.sum(jnp.where(diagonal, line, 0.0), axis=1, keepdims=True)
+        share_ref[rows, :] = jnp.broadcast_to(column, (count, share_ref.shape[1]))
+        if j == 2:
+            own_ref[...] = normed[aligned(outer + 2 * (count // small), small), :]
+        scale = lax.rsqrt(square / (4 * width) + 1e-06)
+        for s in range(4):
+            cols = slice(s * width, (s + 1) * width)
+            value = normed[rows, cols].astype(F32)
+            normed[rows, cols] = (value * scale * gain[:, cols]).astype(BF16)
+    other_ref[...] = normed[:, aligned(1 - dp, half)]
 
     mine = normed[:, aligned(dp, half)]
-    early = normed[:, pl.ds(pl.multiple_of((1 - dp) * half, half), depth)]
-    gate_ref[...] = dot(mine, ga[...]) + dot(early, gb[...])
-    up_ref[...] = dot(mine, ua[...]) + dot(early, ub[...])
-
-
-def last_gate_kernel(gate, up, rows, share, gw, uw, far_ref, near_ref):
-    g = gate[...] + dot(rows[...], gw[...])
-    u = up[...] + dot(rows[...], uw[...])
-    inner = (g / (1.0 + jnp.exp(-g)) * u * share[:, 0:1]).astype(BF16)
+    other = other_ref[...]
+    gate = dot(mine, own[:, 0:cut]) + dot(other, early[:, 0:cut])
+    up = dot(mine, own[:, 2 * cut : 3 * cut]) + dot(other, early[:, cut : 2 * cut])
+    inner_ref[...] = swiglu(gate, up, share_ref[:, 0:1])
+    part_ref[:, 0:cut] = dot(mine, own[:, cut : 2 * cut])
+    part_ref[:, cut : 2 * cut] = dot(mine, own[:, 3 * cut : 4 * cut])
+
+
+def last_gate_kernel(first, part, other, share, late, far_ref, near_ref):
+    cut = first.shape[1]
+    gate = part[:, 0:cut] + dot(other[...], late[:, 0:cut])
+    up = part[:, cut : 2 * cut] + dot(other[...], late[:, cut : 2 * cut])
+    value = swiglu(gate, up, share[:, 0:1])
     half = far_ref.shape[0]
-    far_ref[...] = inner[:half]
-    near_ref[...] = inner[half:]
+    far_ref[:, 0:cut] = first[0:half, :]
+    near_ref[:, 0:cut] = first[half:, :]
+    far_ref[:, cut : 2 * cut] = value[:half]
+    near_ref[:, cut : 2 * cut] = value[half:]
+
+
+def column_chunks(wd):
+    return [slice(at, at + 256) for at in range(0, wd.shape[1], 256)]
 
 
 def down_both_kernel(far, near, wd, keep_far, keep_near, send_ref):
     count = keep_far.shape[0]
-    value = dot(far[...], wd[...]).astype(BF16)
-    keep_far[...] = value[:count]
-    send_ref[0:count, :] = value[count:]
-    value = dot(near[...], wd[...]).astype(BF16)
-    keep_near[...] = value[:count]
-    send_ref[count : 2 * count, :] = value[count:]
+    for cols in column_chunks(wd):
+        value = dot(far[...], wd[:, cols]).astype(BF16)
+        keep_far[:, cols] = value[:count]
+        send_ref[0:count, cols] = value[count:]
+        value = dot(near[...], wd[:, cols]).astype(BF16)
+        keep_near[:, cols] = value[:count]
+        send_ref[count : 2 * count, cols] = value[count:]
 
 
 def down_kernel(rows, wd, keep_ref, send_ref):
     count = keep_ref.shape[0]
-    value = dot(rows[...], wd[...]).astype(BF16)
-    keep_ref[...] = value[:count]
-    send_ref[...] = value[count:]
+    for cols in column_chunks(wd):
+        value = dot(rows[...], wd[:, cols]).astype(BF16)
+        keep_ref[:, cols] = value[:count]
+        send_ref[:, cols] = value[count:]
 
 
 def pieces_kernel(keep, core, far, p0, p1, p2, p3):
@@ -370,11 +398,24 @@
     def after(x, *results):
         return lax.optimization_barrier((x, *results))[0]
 
-    depth = half_width * 3 // 8
+    def weight_piece(i):
+        return pl.pallas_call(
+            functools.partial(piece_kernel, i),
+            out_shape=shape_of(half_width, hidden),
+            in_specs=[pl.BlockSpec(memory_space=pl.ANY)],
+            out_specs=vmem,
+            scratch_shapes=[pltpu.SemaphoreType.DMA((2,))],
+            compiler_params=kernel_params(8),
+            cost_estimate=cost(1000, 4 * half_width * hidden),
+            name="weight_piece",
+        )(w_gate_up[0])
+
+    cut_width = hidden // 2
+    early_piece, late_piece = (weight_piece(i) for i in range(2))
     a = [attn[0], swap_outer(attn[0], 1), swap_outer(attn[0], 2)]
-    a.append(swap_outer(a[2], 1))
+    a.append(swap_outer(after(a[2], a[1]), 1))
     w_x = swap_inner(w_out, 2)
-    gate_up_early = swap_dp(w_gate_up[0, :depth])
+    gate_up_early = swap_dp(early_piece)
     w_c = swap_inner(after(w_out, w_x), 1)
     w_cx = swap_inner(w_x, 1)
 
@@ -409,8 +450,8 @@
             pltpu.VMEM((8 * rows_here, quarter), BF16),
         ),
     )
-    arrived = swap_dp(after(send, gate_up_early, *r[1:]))
-    gate_up_late = swap_dp(after(w_gate_up[0, depth:], arrived))
+    arrived = swap_dp(after(send, gate_up_early, late_piece, *r[1:]))
+    gate_up_late = swap_dp(after(late_piece, arrived))
     (block,) = call(
         stream_kernel,
         "stream",
@@ -427,90 +468,59 @@
     blocks_c = swap_inner(blocks, 1)
     blocks_cx = swap_inner(blocks_x, 1)
 
-    unit = 256
-    steps = hidden // unit
     row_total = 16 * rows_here
-    block_spec = fixed(*blocks.shape)
-    gate_cols = lambda k: pl.BlockSpec((k, unit), lambda i: (0, i))
-    up_cols = lambda k: pl.BlockSpec((k, unit), lambda i: (0, i + steps))
-    out_cols = lambda k: pl.BlockSpec((k, unit), lambda i: (0, i))
-    gate, up, last_rows, share_rows, stream_own = pl.pallas_call(
+    half_rows = row_total // 2
+    product_flops = 2 * row_total * half_width * hidden
+    inner_first, part, other_rows, share_rows, stream_own = call(
         first_gate_kernel,
-        grid=(steps,),
-        out_shape=(
+        "first_gate_up",
+        24,
+        (
+            shape_of(row_total, cut_width),
             shape_of(row_total, hidden, dtype=F32),
-            shape_of(row_total, hidden, dtype=F32),
-            shape_of(row_total, half_width - depth),
+            shape_of(row_total, half_width),
             shape_of(row_total, 128, dtype=F32),
             shape_of(rows_here, model_width),
         ),
-        in_specs=[block_spec] * 4
-        + [
-            fixed(1, model_width),
-            gate_cols(half_width),
-            up_cols(half_width),
-            gate_cols(depth),
-            up_cols(depth),
-        ],
-        out_specs=(
-            out_cols(row_total),
-            out_cols(row_total),
-            fixed(row_total, half_width - depth),
-            fixed(row_total, 128),
-            fixed(rows_here, model_width),
-        ),
-        scratch_shapes=[pltpu.VMEM((row_total, model_width), BF16)],
-        compiler_params=kernel_params(24),
-        name="first_gate_up",
-        cost_estimate=cost(4 * row_total * (half_width + depth) * hidden, 12 * row_total * hidden),
-    )(
         blocks,
         blocks_x,
         blocks_c,
         blocks_cx,
         gain_post[None],
         w_gate_up[0],
-        w_gate_up[0],
         gate_up_early,
-        gate_up_early,
-    )
-    inner_half = shape_of(row_total // 2, hidden)
-    inner_far, inner_near = pl.pallas_call(
+        flops=3 * product_flops,
+        scratch=(pltpu.VMEM((row_total, model_width), BF16),),
+    )
+    inner_half = shape_of(half_rows, hidden)
+    inner_far, inner_near = call(
         last_gate_kernel,
-        grid=(steps,),
-        out_shape=(inner_half, inner_half),
-        in_specs=[
-            out_cols(row_total),
-            out_cols(row_total),
-            fixed(row_total, half_width - depth),
-            fixed(row_total, 128),
-            gate_cols(half_width - depth),
-            up_cols(half_width - depth),
-        ],
-        out_specs=(out_cols(row_total // 2), out_cols(row_total // 2)),
-        compiler_params=kernel_params(16),
-        name="last_gate_up",
-        cost_estimate=cost(4 * row_total * (half_width - depth) * hidden, 14 * row_total * hidden),
-    )(gate, up, last_rows, share_rows, gate_up_late, gate_up_late)
+        "last_gate_up",
+        16,
+        (inner_half, inner_half),
+        inner_first,
+        part,
+        other_rows,
+        share_rows,
+        gate_up_late,
+        flops=product_flops,
+    )
     far_other = swap_dp(inner_far)
-    near_other = swap_dp(inner_near)
+    near_other = swap_dp(after(inner_near, far_other))
 
     count = row_total // 4
     quarter_out = shape_of(count, half_width)
-    half_spec = fixed(row_total // 2, hidden)
-    wd_spec = pl.BlockSpec((hidden, unit), lambda i: (0, i))
 
     def down(rows):
-        return pl.pallas_call(
+        return call(
             down_kernel,
-            grid=(half_width // unit,),
-            out_shape=(quarter_out, quarter_out),
-            in_specs=[half_spec, wd_spec],
-            out_specs=(out_cols(count), out_cols(count)),
-            compiler_params=kernel_params(8),
-            name="down",
-            cost_estimate=cost(row_total * hidden * half_width, 3 * row_total * half_width),
-        )(rows, w_down[0])
+            "down",
+            12,
+            (quarter_out, quarter_out),
+            rows,
+            w_down[0],
+            flops=product_flops // 2,
+        )
 
     def add(x, y):
         return (x.astype(F32) + y.astype(F32)).astype(BF16)
@@ -519,16 +529,16 @@
         out = shape_of(rows_here, half_width)
         return call(pieces_kernel, "pieces", 4, (out, out, out, out), keep, core, far)
 
-    keep_far, keep_near, core_send = pl.pallas_call(
+    keep_far, keep_near, core_send = call(
         down_both_kernel,
-        grid=(half_width // unit,),
-        out_shape=(quarter_out, quarter_out, shape_of(2 * count, half_width)),
-        in_specs=[half_spec, half_spec, wd_spec],
-        out_specs=(out_cols(count), out_cols(count), out_cols(2 * count)),
-        compiler_params=kernel_params(12),
-        name="down_both",
-        cost_estimate=cost(2 * row_total * hidden * half_width, 4 * row_total * half_width),
-    )(inner_far, inner_near, w_down[0])
+        "down_both",
+        16,
+        (quarter_out, quarter_out, shape_of(2 * count, half_width)),
+        inner_far,
+        inner_near,
+        w_down[0],
+        flops=product_flops,
+    )
     core = swap_inner(core_send, 1)
     far = swap_inner(add(keep_far, core[:count]), 2)
     ready = far

time: 133 us -> 126 us (0.947)
  waiting for transfers between devices: 70.3 us -> 58.5 us
  starting transfers between devices: 38 us -> 44.1 us
  Pallas kernels: 17.5 us -> 14.7 us
    pallas_call x5 -> x2, Pallas kernels: 12.8 us -> 0.36 us  [weight_piece(): pl.pallas_call(functools.partial(piece_kernel, i), out_shape=shape_of(hal...]
    pallas_call x6 -> x11, Pallas kernels: 4.65 us -> 14.3 us  [call(): pl.pallas_call(kernel, out_shape=outs, in_specs=[first] + [vmem] * (len(a...]
    ppermute x5, waiting for transfers between devices: 25.7 us -> 17 us  [swap_dp(): return lax.ppermute(x, 'dp', [(0, 1), (1, 0)])]
    ppermute x5, starting transfers between devices: 5.2 us -> 9.46 us  [swap_dp(): return lax.ppermute(x, 'dp', [(0, 1), (1, 0)])]
    ppermute x3, waiting for transfers between devices: 6.38 us -> 2.73 us  [swap_outer(): lax.ppermute(x, 'expert', [(i, i ^ 4 * s) for i in range(expert_count)])]
    unnamed x16 -> x22, local copies, waits for them, and re-layouts: 2.88 us -> 6.44 us
    squeeze x2 -> x0, local copies, waits for them, and re-layouts: 2.56 us -> none  [the longest x1 2.43 us: body_paired(): gate_up_early = swap_dp(w_gate_up[0, :depth])]
    ppermute x11, waiting for transfers between devices: 25.2 us -> 23.9 us  [swap_inner(): return lax.ppermute(x, 'expert', [(i, i ^ j) for i in range(expert_count)])]
  transfers between devices with their start and end apart: 32 -> 32, of which waited for: 18 -> 20; matrix products, arithmetic and copies ran while one was open for 2% -> 2% of each run, Pallas kernels for 7% -> 8%
where the time goes in v5:
time: 126 us; the launch traced here: 125 us
  waiting for transfers between devices  58.5 us (46%)
  starting transfers between devices  44.1 us (35%)
  Pallas kernels  14.7 us (12%)
  local copies, waits for them, and re-layouts  6.46 us (5%)
  between operations  1.48 us (1%)
    ppermute x11, waiting for transfers between devices, swap_inner(): return lax.ppermute(x, 'expert', [(i, i ^ j) for i in range(expert_count)])  23.9 us
    ppermute x5, waiting for transfers between devices, swap_dp(): return lax.ppermute(x, 'dp', [(0, 1), (1, 0)])  17 us
    ppermute x9, starting transfers between devices, shift_outer(): lax.ppermute(x, 'expert', [(i, (i + 4 * s) % expert_count) for i in range...  15.5 us
    pallas_call x11, Pallas kernels, call(): pl.pallas_call(kernel, out_shape=outs, in_specs=[first] + [vmem] * (len(a...  14.3 us
    ppermute x9, waiting for transfers between devices, shift_outer(): lax.ppermute(x, 'expert', [(i, (i + 4 * s) % expert_count) for i in range...  9.94 us
    ppermute x5, starting transfers between devices, swap_dp(): return lax.ppermute(x, 'dp', [(0, 1), (1, 0)])  9.46 us
    ppermute x11, starting transfers between devices, swap_inner(): return lax.ppermute(x, 'expert', [(i, i ^ j) for i in range(expert_count)])  6.89 us
    ppermute x4, starting transfers between devices, cross_outer(): lax.ppermute(x, ('dp', 'expert'), [(d * expert_count + i, (1 - d) * exper...  6.57 us
  transfers between devices with their start and end apart: 32, of which 20 were waited for; matrix products, arithmetic and copies ran while one was open for 2% of the time, Pallas kernels for 8%

profile of v5, /device:TPU:0, one launch (start us, length us, event | category | flops | bytes accessed | tf_op | source)
XLA Modules:
  0.0 125.4 jit_solution(10254215592127877988)
XLA Ops:
  0.6 1.9 %copy-done = bf16[1,1024,1536]{2,1,0:T(8,128)(2,1)S(1)} copy-done((bf16[1,1024,1536]{2,1,0:T(8,128)(2,1)S(1)}, bf16[1,1024,1536]{2,1,0:T(8,128)(2,1)}, u32[]{:S(2)}) %copy-start) | copy-done | bytes 3145752
  2.5 0.2 weight_piece.2
  2.7 3.0 %collective-permute-start.6 = (bf16[1024,768]{1,0:T(8,128)(2,1)S(1)}, bf16[1024,768]{1,0:T(8,128)(2,1)}, u32[]{:S(2)}, u32[]{:S(2)}) collective-permute-start(bf16[1024,768]{1,0:T(8,128)(2,1)S(1)} %weight_piece.2), channel_id=1, source_target_pairs={{0,16},{16,0},{1,17},{17,1},{2,18},{18,2},{3,19},{19,3},{4,20},{20... | collective-permute-start | bytes 4718600 | tf_op jit(solution)/shard_map/ppermute | solution.py:374
  5.7 1.5 %collective-permute-start.3 = (bf16[2048,128]{1,0:T(8,128)(2,1)}, bf16[2048,128]{1,0:T(8,128)(2,1)}, u32[]{:S(2)}, u32[]{:S(2)}) collective-permute-start(bf16[2048,128]{1,0:T(8,128)(2,1)} %w0.1), channel_id=1, source_target_pairs={{0,2},{1,3},{2,0},{3,1},{4,6},{5,7},{6,4},{7,5},{8,10},{9,11},{10,... | collective-permute-start | bytes 1572872 | tf_op jit(solution)/shard_map/ppermute | solution.py:393
  7.2 2.6 %collective-permute-start.1 = (bf16[64,2048]{1,0:T(8,128)(2,1)S(1)}, bf16[64,2048]{1,0:T(8,128)(2,1)}, u32[]{:S(2)}, u32[]{:S(2)}) collective-permute-start(bf16[64,2048]{1,0:T(8,128)(2,1)S(1)} %bitcast.21), channel_id=1, source_target_pairs={{0,8},{1,9},{2,10},{3,11},{4,12},{5,13},{6,14},{7,15},{8,0},{9,1},... | collective-permute-start | bytes 786440 | tf_op jit(solution)/shard_map/ppermute | solution.py:396
  9.8 1.6 %collective-permute-start = (bf16[64,2048]{1,0:T(8,128)(2,1)S(1)}, bf16[64,2048]{1,0:T(8,128)(2,1)S(1)}, u32[]{:S(2)}, u32[]{:S(2)}) collective-permute-start(bf16[64,2048]{1,0:T(8,128)(2,1)S(1)} %bitcast.22), channel_id=1, source_target_pairs={{0,4},{1,5},{2,6},{3,7},{4,0},{5,1},{6,2},{7,3},{8,12},{9,13},{10,... | collective-permute-start | bytes 786440 | tf_op jit(solution)/shard_map/ppermute | solution.py:396
  11.4 8.0 %collective-permute-done.3.w2 = bf16[2048,128]{1,0:T(8,128)(2,1)} collective-permute-done((bf16[2048,128]{1,0:T(8,128)(2,1)}, bf16[2048,128]{1,0:T(8,128)(2,1)}, u32[]{:S(2)}, u32[]{:S(2)}) %collective-permute-start.3) | collective-permute-done | bytes 524320 | tf_op jit(solution)/shard_map/ppermute | solution.py:393
  19.4 0.5 collective-permute-start.5
  20.0 1.5 %collective-permute-done.1.a2 = bf16[64,2048]{1,0:T(8,128)(2,1)} collective-permute-done((bf16[64,2048]{1,0:T(8,128)(2,1)S(1)}, bf16[64,2048]{1,0:T(8,128)(2,1)}, u32[]{:S(2)}, u32[]{:S(2)}) %collective-permute-start.1) | collective-permute-done | bytes 262176 | tf_op jit(solution)/shard_map/ppermute | solution.py:396
  21.5 0.1 collective-permute-done.a1
  21.5 0.7 copy-done.4
  22.3 1.4 %collective-permute-start.2 = (bf16[64,2048]{1,0:T(8,128)(2,1)}, bf16[64,2048]{1,0:T(8,128)(2,1)}, u32[]{:S(2)}, u32[]{:S(2)}) collective-permute-start(bf16[64,2048]{1,0:T(8,128)(2,1)} %collective-permute-done.1.a2), channel_id=1, source_target_pairs={{0,4},{1,5},{2,6},{3,7},{4,0},{5,1},{6,2},{7,3},{8,12},{9,13},{10,... | collective-permute-start | bytes 786440 | tf_op jit(solution)/shard_map/ppermute | solution.py:396
  23.7 0.2 weight_piece.3
  24.5 0.8 copy.12
  25.3 1.4 %copy.13 = f32[1,32,8]{2,1,0:T(8,128)} copy(f32[1,32,8]{1,2,0:T(8,128)} %param.15) | data formatting | bytes 2048 | tf_op args[5]
  26.7 0.7 copy-done.7
  27.4 0.4 prepare.1
  27.8 0.6 collective-permute-start.7
  28.4 1.1 collective-permute-done.2.a3
  29.6 3.7 %collective-permute-start.8 = (bf16[32,512]{1,0:T(8,128)(2,1)S(1)}, bf16[32,512]{1,0:T(8,128)(2,1)S(1)}, u32[]{:S(2)}, u32[]{:S(2)}) collective-permute-start(bf16[32,512]{1,0:T(8,128)(2,1)S(1)} %get-tuple-element.50), channel_id=1, source_target_pairs={{0,8},{1,9},{2,10},{3,11},{4,12},{5,13},{6,14},{7,15},{8,0},{9,1},... | collective-permute-start | bytes 98312 | tf_op jit(solution)/shard_map/ppermute | solution.py:377
  33.3 1.2 collective-permute-start.9
  34.5 0.9 copy-done.5
  35.4 3.1 %projection.1 = (bf16[128,512]{1,0:T(8,128)(2,1)S(1)}, bf16[128,512]{1,0:T(8,128)(2,1)S(1)}) custom-call(bf16[64,2048]{1,0:T(8,128)(2,1)S(1)} %bitcast.23, bf16[64,2048]{1,0:T(8,128)(2,1)S(1)} %copy-done.5, bf16[64,2048]{1,0:T(8,128)(2,1)} %collective-permute-done.1.a2, bf16[64,2048]{1,0:T(8,128)(2,1)} %collective-permute-done.2.a3, bf16[2048,128]{1,0:T(8,128)(2,1)} %w0.1, ...), custom_call_target="tpu_custom_call" | custom-call | flops 536870912 | bytes 3407872 | tf_op jit(solution)/shard_map/projection/pallas_call | solution.py:362
  38.6 1.6 %collective-permute-done.6.early = bf16[1024,768]{1,0:T(8,128)(2,1)} collective-permute-done((bf16[1024,768]{1,0:T(8,128)(2,1)S(1)}, bf16[1024,768]{1,0:T(8,128)(2,1)}, u32[]{:S(2)}, u32[]{:S(2)}) %collective-permute-start.6) | collective-permute-done | bytes 1572896 | tf_op jit(solution)/shard_map/ppermute | solution.py:374
  40.2 1.7 %collective-permute-start.10 = (bf16[128,512]{1,0:T(8,128)(2,1)S(1)}, bf16[128,512]{1,0:T(8,128)(2,1)S(1)}, u32[]{:S(2)}, u32[]{:S(2)}) collective-permute-start(bf16[128,512]{1,0:T(8,128)(2,1)S(1)} %get-tuple-element.53), channel_id=1, source_target_pairs={{0,16},{16,0},{1,17},{17,1},{2,18},{18,2},{3,19},{19,3},{4,20},{20... | collective-permute-start | bytes 393224 | tf_op jit(solution)/shard_map/ppermute | solution.py:374
  42.0 3.2 %collective-permute-done.10.arrived = bf16[128,512]{1,0:T(8,128)(2,1)S(1)} collective-permute-done((bf16[128,512]{1,0:T(8,128)(2,1)S(1)}, bf16[128,512]{1,0:T(8,128)(2,1)S(1)}, u32[]{:S(2)}, u32[]{:S(2)}) %collective-permute-start.10) | collective-permute-done | bytes 131104 | tf_op jit(solution)/shard_map/ppermute | solution.py:374
  45.3 3.9 %collective-permute-start.13 = (bf16[144,512]{1,0:T(8,128)(2,1)S(1)}, bf16[144,512]{1,0:T(8,128)(2,1)S(1)}, u32[]{:S(2)}, u32[]{:S(2)}) collective-permute-start(bf16[144,512]{1,0:T(8,128)(2,1)S(1)} %stream.1), channel_id=1, source_target_pairs={{0,12},{1,13},{2,14},{3,15},{4,0},{5,1},{6,2},{7,3},{8,4},{9,5},{1... | collective-permute-start | bytes 442376 | tf_op jit(solution)/shard_map/ppermute | solution.py:377
  49.1 1.0 collective-permute-start.11
  50.2 1.5 %collective-permute-start.17 = (bf16[1024,768]{1,0:T(8,128)(2,1)S(1)}, bf16[1024,768]{1,0:T(8,128)(2,1)S(1)}, u32[]{:S(2)}, u32[]{:S(2)}) collective-permute-start(bf16[1024,768]{1,0:T(8,128)(2,1)S(1)} %weight_piece.3), channel_id=1, source_target_pairs={{0,16},{16,0},{1,17},{17,1},{2,18},{18,2},{3,19},{19,3},{4,20},{20... | collective-permute-start | bytes 4718600 | tf_op jit(solution)/shard_map/ppermute | solution.py:374
  51.7 1.8 %collective-permute-done.13 = bf16[144,512]{1,0:T(8,128)(2,1)S(1)} collective-permute-done((bf16[144,512]{1,0:T(8,128)(2,1)S(1)}, bf16[144,512]{1,0:T(8,128)(2,1)S(1)}, u32[]{:S(2)}, u32[]{:S(2)}) %collective-permute-start.13) | collective-permute-done | bytes 147488 | tf_op jit(solution)/shard_map/ppermute | solution.py:377
  53.5 7.2 %collective-permute-done.12 = bf16[144,512]{1,0:T(8,128)(2,1)S(1)} collective-permute-done((bf16[144,512]{1,0:T(8,128)(2,1)S(1)}, bf16[144,512]{1,0:T(8,128)(2,1)S(1)}, u32[]{:S(2)}, u32[]{:S(2)}) %collective-permute-start.12) | collective-permute-done | bytes 147488 | tf_op jit(solution)/shard_map/ppermute | solution.py:377
  60.6 0.1 pad_maximum_fusion.blocks
  60.7 1.6 %collective-permute-start.14 = (bf16[4,144,512]{2,1,0:T(8,128)(2,1)S(1)}, bf16[4,144,512]{2,1,0:T(8,128)(2,1)S(1)}, u32[]{:S(2)}, u32[]{:S(2)}) collective-permute-start(bf16[4,144,512]{2,1,0:T(8,128)(2,1)S(1)} %pad_maximum_fusion.blocks), channel_id=1, source_target_pairs={{0,2},{1,3},{2,0},{3,1},{4,6},{5,7},{6,4},{7,5},{8,10},{9,11},{10,... | collective-permute-start | bytes 1769480 | tf_op jit(solution)/shard_map/ppermute | solution.py:393
  62.3 12.0 %collective-permute-done.14.blocks_x = bf16[4,144,512]{2,1,0:T(8,128)(2,1)S(1)} collective-permute-done((bf16[4,144,512]{2,1,0:T(8,128)(2,1)S(1)}, bf16[4,144,512]{2,1,0:T(8,128)(2,1)S(1)}, u32[]{:S(2)}, u32[]{:S(2)}) %collective-permute-start.14) | collective-permute-done | bytes 589856 | tf_op jit(solution)/shard_map/ppermute | solution.py:393
  74.2 2.0 %collective-permute-done.16.blocks_cx = bf16[4,144,512]{2,1,0:T(8,128)(2,1)S(1)} collective-permute-done((bf16[4,144,512]{2,1,0:T(8,128)(2,1)S(1)}, bf16[4,144,512]{2,1,0:T(8,128)(2,1)S(1)}, u32[]{:S(2)}, u32[]{:S(2)}) %collective-permute-start.16) | collective-permute-done | bytes 589856 | tf_op jit(solution)/shard_map/ppermute | solution.py:393
  76.2 6.1 %first_gate_up.1 = (bf16[512,384]{1,0:T(8,128)(2,1)S(1)}, f32[512,768]{1,0:T(8,128)S(1)}, bf16[512,1024]{1,0:T(8,128)(2,1)S(1)}, f32[512,128]{1,0:T(8,128)S(1)}, bf16[32,2048]{1,0:T(8,128)(2,1)S(1)}) custom-call(bf16[4,144,512]{2,1,0:T(8,128)(2,1)S(1)} %pad_maximum_fusion.blocks, bf16[4,144,512]{2,1,0:T(8,128)(2,1)S(1)} %collective-permute-done.14.blocks_x, ...), custom_call_target="tpu_custom_call" | custom-call | flops 2415919104 | bytes 10493952 | tf_op jit(solution)/shard_map/first_gate_up/pallas_call | solution.py:362
  82.3 1.1 collective-permute-done.17.late
  83.4 1.4 %last_gate_up.1 = (bf16[256,768]{1,0:T(8,128)(2,1)S(1)}, bf16[256,768]{1,0:T(8,128)(2,1)S(1)}) custom-call(bf16[512,384]{1,0:T(8,128)(2,1)S(1)} %get-tuple-element.57.first, f32[512,768]{1,0:T(8,128)S(1)} %get-tuple-element.58.part, bf16[512,1024]{1,0:T(8,128)(2,1)S(1)} %get-tuple-element.59.other, f32[512,128]{1,0:T(8,128)S(1)} %get-tuple-element.60.share, ...), custom_call_target="tpu_custom_call" | custom-call | flops 805306368 | bytes 5636096 | tf_op jit(solution)/shard_map/last_gate_up/pallas_call | solution.py:362
  84.8 1.0 down_both.1
  85.9 1.6 %collective-permute-start.23 = (bf16[256,768]{1,0:T(8,128)(2,1)S(1)}, bf16[256,768]{1,0:T(8,128)(2,1)S(1)}, u32[]{:S(2)}, u32[]{:S(2)}) collective-permute-start(bf16[256,768]{1,0:T(8,128)(2,1)S(1)} %get-tuple-element.62.far), channel_id=1, source_target_pairs={{0,16},{16,0},{1,17},{17,1},{2,18},{18,2},{3,19},{19,3},{4,20},{20... | collective-permute-start | bytes 1179656 | tf_op jit(solution)/shard_map/ppermute | solution.py:374
  87.5 0.3 collective-permute-done.18
  87.9 1.6 %collective-permute-start.19 = (bf16[128,1024]{1,0:T(8,128)(2,1)S(1)}, bf16[128,1024]{1,0:T(8,128)(2,1)S(1)}, u32[]{:S(2)}, u32[]{:S(2)}) collective-permute-start(bf16[128,1024]{1,0:T(8,128)(2,1)S(1)} %add_convert_fusion.1), channel_id=1, source_target_pairs={{0,2},{1,3},{2,0},{3,1},{4,6},{5,7},{6,4},{7,5},{8,10},{9,11},{10,... | collective-permute-start | bytes 786440 | tf_op jit(solution)/shard_map/ppermute | solution.py:393
  89.4 8.0 %collective-permute-done.23.rows = bf16[256,768]{1,0:T(8,128)(2,1)S(1)} collective-permute-done((bf16[256,768]{1,0:T(8,128)(2,1)S(1)}, bf16[256,768]{1,0:T(8,128)(2,1)S(1)}, u32[]{:S(2)}, u32[]{:S(2)}) %collective-permute-start.23) | collective-permute-done | bytes 393248 | tf_op jit(solution)/shard_map/ppermute | solution.py:374
  97.4 0.6 down.2
  98.1 1.6 %collective-permute-start.24 = (bf16[256,768]{1,0:T(8,128)(2,1)S(1)}, bf16[256,768]{1,0:T(8,128)(2,1)S(1)}, u32[]{:S(2)}, u32[]{:S(2)}) collective-permute-start(bf16[256,768]{1,0:T(8,128)(2,1)S(1)} %get-tuple-element.71.near), channel_id=1, source_target_pairs={{0,16},{16,0},{1,17},{17,1},{2,18},{18,2},{3,19},{19,3},{4,20},{20... | collective-permute-start | bytes 1179656 | tf_op jit(solution)/shard_map/ppermute | solution.py:374
  99.8 1.6 %collective-permute-start.26 = (bf16[128,1024]{1,0:T(8,128)(2,1)S(1)}, bf16[128,1024]{1,0:T(8,128)(2,1)S(1)}, u32[]{:S(2)}, u32[]{:S(2)}) collective-permute-start(bf16[128,1024]{1,0:T(8,128)(2,1)S(1)} %add_convert_fusion), channel_id=1, source_target_pairs={{0,2},{1,3},{2,0},{3,1},{4,6},{5,7},{6,4},{7,5},{8,10},{9,11},{10,... | collective-permute-start | bytes 786440 | tf_op jit(solution)/shard_map/ppermute | solution.py:393
  101.3 0.1 pieces.2
  101.5 2.5 %collective-permute-start.20 = (bf16[32,1024]{1,0:T(8,128)(2,1)S(1)}, bf16[32,1024]{1,0:T(8,128)(2,1)S(1)}, u32[]{:S(2)}, u32[]{:S(2)}) collective-permute-start(bf16[32,1024]{1,0:T(8,128)(2,1)S(1)} %get-tuple-element.68), channel_id=1, source_target_pairs={{0,4},{1,5},{2,6},{3,7},{4,8},{5,9},{6,10},{7,11},{8,12},{9,13},{1... | collective-permute-start | bytes 196616 | tf_op jit(solution)/shard_map/ppermute | solution.py:377
  104.0 1.2 collective-permute-start.21
  105.2 1.5 %collective-permute-start.22 = (bf16[32,1024]{1,0:T(8,128)(2,1)S(1)}, bf16[32,1024]{1,0:T(8,128)(2,1)S(1)}, u32[]{:S(2)}, u32[]{:S(2)}) collective-permute-start(bf16[32,1024]{1,0:T(8,128)(2,1)S(1)} %get-tuple-element.70), channel_id=1, source_target_pairs={{0,12},{1,13},{2,14},{3,15},{4,0},{5,1},{6,2},{7,3},{8,4},{9,5},{1... | collective-permute-start | bytes 196616 | tf_op jit(solution)/shard_map/ppermute | solution.py:377
  106.6 3.0 %collective-permute-done.24.rows = bf16[256,768]{1,0:T(8,128)(2,1)S(1)} collective-permute-done((bf16[256,768]{1,0:T(8,128)(2,1)S(1)}, bf16[256,768]{1,0:T(8,128)(2,1)S(1)}, u32[]{:S(2)}, u32[]{:S(2)}) %collective-permute-start.24) | collective-permute-done | bytes 393248 | tf_op jit(solution)/shard_map/ppermute | solution.py:374
  109.6 0.9 collective-permute-done.21.m2
  110.5 0.1 collective-permute-done.22.m3
  110.6 0.6 down.3
  111.3 1.5 %collective-permute-done.27.core = bf16[128,1024]{1,0:T(8,128)(2,1)S(1)} collective-permute-done((bf16[128,1024]{1,0:T(8,128)(2,1)S(1)}, bf16[128,1024]{1,0:T(8,128)(2,1)S(1)}, u32[]{:S(2)}, u32[]{:S(2)}) %collective-permute-start.27) | collective-permute-done | bytes 262176 | tf_op jit(solution)/shard_map/ppermute | solution.py:393
  112.8 0.1 pieces.3
  112.9 1.5 %collective-permute-start.28 = (bf16[32,1024]{1,0:T(8,128)(2,1)S(1)}, bf16[32,1024]{1,0:T(8,128)(2,1)S(1)}, u32[]{:S(2)}, u32[]{:S(2)}) collective-permute-start(bf16[32,1024]{1,0:T(8,128)(2,1)S(1)} %get-tuple-element.78), channel_id=1, source_target_pairs={{0,16},{1,17},{2,18},{3,19},{4,20},{5,21},{6,22},{7,23},{8,24},{9,... | collective-permute-start | bytes 196616 | tf_op jit(solution)/shard_map/ppermute | solution.py:382
  114.5 1.7 %collective-permute-start.29 = (bf16[32,1024]{1,0:T(8,128)(2,1)S(1)}, bf16[32,1024]{1,0:T(8,128)(2,1)S(1)}, u32[]{:S(2)}, u32[]{:S(2)}) collective-permute-start(bf16[32,1024]{1,0:T(8,128)(2,1)S(1)} %get-tuple-element.79), channel_id=1, source_target_pairs={{0,20},{1,21},{2,22},{3,23},{4,24},{5,25},{6,26},{7,27},{8,28},{9,... | collective-permute-start | bytes 196616 | tf_op jit(solution)/shard_map/ppermute | solution.py:382
  116.2 2.2 %collective-permute-start.30 = (bf16[32,1024]{1,0:T(8,128)(2,1)S(1)}, bf16[32,1024]{1,0:T(8,128)(2,1)S(1)}, u32[]{:S(2)}, u32[]{:S(2)}) collective-permute-start(bf16[32,1024]{1,0:T(8,128)(2,1)S(1)} %get-tuple-element.80), channel_id=1, source_target_pairs={{0,24},{1,25},{2,26},{3,27},{4,28},{5,29},{6,30},{7,31},{8,16},{9,... | collective-permute-start | bytes 196616 | tf_op jit(solution)/shard_map/ppermute | solution.py:382
  118.4 1.1 collective-permute-start.31
  119.5 2.4 %collective-permute-done.29.o1 = bf16[32,1024]{1,0:T(8,128)(2,1)S(1)} collective-permute-done((bf16[32,1024]{1,0:T(8,128)(2,1)S(1)}, bf16[32,1024]{1,0:T(8,128)(2,1)S(1)}, u32[]{:S(2)}, u32[]{:S(2)}) %collective-permute-start.29) | collective-permute-done | bytes 65568 | tf_op jit(solution)/shard_map/ppermute | solution.py:382
  121.9 2.0 %collective-permute-done.30.o2 = bf16[32,1024]{1,0:T(8,128)(2,1)S(1)} collective-permute-done((bf16[32,1024]{1,0:T(8,128)(2,1)S(1)}, bf16[32,1024]{1,0:T(8,128)(2,1)S(1)}, u32[]{:S(2)}, u32[]{:S(2)}) %collective-permute-start.30) | collective-permute-done | bytes 65568 | tf_op jit(solution)/shard_map/ppermute | solution.py:382
  123.9 0.6 collective-permute-done.31.o3
  124.5 0.9 closing.1
  (39 shorter events, 0.5 us)
Async XLA Ops:
  0.6 1.9 %copy-start = (bf16[1,1024,1536]{2,1,0:T(8,128)(2,1)S(1)}, bf16[1,1024,1536]{2,1,0:T(8,128)(2,1)}, u32[]{:S(2)}) copy-start(bf16[1,1024,1536]{2,1,0:T(8,128)(2,1)} %param.17) | copy-start | bytes 9437188
  2.5 4.7 %copy-start.3 = (bf16[1,64,2048]{2,1,0:T(8,128)(2,1)S(1)}, bf16[1,64,2048]{2,1,0:T(8,128)(2,1)}, u32[]{:S(2)}) copy-start(bf16[1,64,2048]{2,1,0:T(8,128)(2,1)} %param.10) | copy-start | bytes 786436
  2.7 37.5 %collective-permute-start.6 = (bf16[1024,768]{1,0:T(8,128)(2,1)S(1)}, bf16[1024,768]{1,0:T(8,128)(2,1)}, u32[]{:S(2)}, u32[]{:S(2)}) collective-permute-start(bf16[1024,768]{1,0:T(8,128)(2,1)S(1)} %weight_piece.2), channel_id=1, source_target_pairs={{0,16},{16,0},{1,17},{17,1},{2,18},{18,2},{3,19},{19,3},{4,20},{20... | collective-permute-start | bytes 4718600 | tf_op jit(solution)/shard_map/ppermute | solution.py:374
  5.7 13.7 %collective-permute-start.3 = (bf16[2048,128]{1,0:T(8,128)(2,1)}, bf16[2048,128]{1,0:T(8,128)(2,1)}, u32[]{:S(2)}, u32[]{:S(2)}) collective-permute-start(bf16[2048,128]{1,0:T(8,128)(2,1)} %w0.1), channel_id=1, source_target_pairs={{0,2},{1,3},{2,0},{3,1},{4,6},{5,7},{6,4},{7,5},{8,10},{9,11},{10,... | collective-permute-start | bytes 1572872 | tf_op jit(solution)/shard_map/ppermute | solution.py:393
  7.2 19.4 %copy-start.6 = (bf16[1,32,2048]{2,1,0:T(8,128)(2,1)S(1)}, bf16[1,32,2048]{2,1,0:T(8,128)(2,1)}, u32[]{:S(2)}) copy-start(bf16[1,32,2048]{2,1,0:T(8,128)(2,1)} %param.11) | copy-start | bytes 393220
  7.2 14.2 %collective-permute-start.1 = (bf16[64,2048]{1,0:T(8,128)(2,1)S(1)}, bf16[64,2048]{1,0:T(8,128)(2,1)}, u32[]{:S(2)}, u32[]{:S(2)}) collective-permute-start(bf16[64,2048]{1,0:T(8,128)(2,1)S(1)} %bitcast.21), channel_id=1, source_target_pairs={{0,8},{1,9},{2,10},{3,11},{4,12},{5,13},{6,14},{7,15},{8,0},{9,1},... | collective-permute-start | bytes 786440 | tf_op jit(solution)/shard_map/ppermute | solution.py:396
  9.8 11.7 %collective-permute-start = (bf16[64,2048]{1,0:T(8,128)(2,1)S(1)}, bf16[64,2048]{1,0:T(8,128)(2,1)S(1)}, u32[]{:S(2)}, u32[]{:S(2)}) collective-permute-start(bf16[64,2048]{1,0:T(8,128)(2,1)S(1)} %bitcast.22), channel_id=1, source_target_pairs={{0,4},{1,5},{2,6},{3,7},{4,0},{5,1},{6,2},{7,3},{8,12},{9,13},{10,... | collective-permute-start | bytes 786440 | tf_op jit(solution)/shard_map/ppermute | solution.py:396
  19.4 13.8 %collective-permute-start.4 = (bf16[2048,128]{1,0:T(8,128)(2,1)}, bf16[2048,128]{1,0:T(8,128)(2,1)}, u32[]{:S(2)}, u32[]{:S(2)}) collective-permute-start(bf16[2048,128]{1,0:T(8,128)(2,1)} %w0.1), channel_id=1, source_target_pairs={{0,1},{1,0},{2,3},{3,2},{4,5},{5,4},{6,7},{7,6},{8,9},{9,8},{10,11... | collective-permute-start | bytes 1572872 | tf_op jit(solution)/shard_map/ppermute | solution.py:393
  19.4 15.0 %collective-permute-start.5 = (bf16[2048,128]{1,0:T(8,128)(2,1)}, bf16[2048,128]{1,0:T(8,128)(2,1)}, u32[]{:S(2)}, u32[]{:S(2)}) collective-permute-start(bf16[2048,128]{1,0:T(8,128)(2,1)} %collective-permute-done.3.w2), channel_id=1, source_target_pairs={{0,1},{1,0},{2,3},{3,2},{4,5},{5,4},{6,7},{7,6},{8,9},{9,8},{10,11... | collective-permute-start | bytes 1572872 | tf_op jit(solution)/shard_map/ppermute | solution.py:393
  21.5 0.7 copy-start.4
  22.3 7.3 %collective-permute-start.2 = (bf16[64,2048]{1,0:T(8,128)(2,1)}, bf16[64,2048]{1,0:T(8,128)(2,1)}, u32[]{:S(2)}, u32[]{:S(2)}) collective-permute-start(bf16[64,2048]{1,0:T(8,128)(2,1)} %collective-permute-done.1.a2), channel_id=1, source_target_pairs={{0,4},{1,5},{2,6},{3,7},{4,0},{5,1},{6,2},{7,3},{8,12},{9,13},{10,... | collective-permute-start | bytes 786440 | tf_op jit(solution)/shard_map/ppermute | solution.py:396
  26.7 0.7 copy-start.7
  27.8 10.8 %collective-permute-start.7 = (bf16[32,512]{1,0:T(8,128)(2,1)S(1)}, bf16[32,512]{1,0:T(8,128)(2,1)S(1)}, u32[]{:S(2)}, u32[]{:S(2)}) collective-permute-start(bf16[32,512]{1,0:T(8,128)(2,1)S(1)} %get-tuple-element.48), channel_id=1, source_target_pairs={{0,4},{1,5},{2,6},{3,7},{4,8},{5,9},{6,10},{7,11},{8,12},{9,13},{1... | collective-permute-start | bytes 98312 | tf_op jit(solution)/shard_map/ppermute | solution.py:377
  29.6 9.0 %collective-permute-start.8 = (bf16[32,512]{1,0:T(8,128)(2,1)S(1)}, bf16[32,512]{1,0:T(8,128)(2,1)S(1)}, u32[]{:S(2)}, u32[]{:S(2)}) collective-permute-start(bf16[32,512]{1,0:T(8,128)(2,1)S(1)} %get-tuple-element.50), channel_id=1, source_target_pairs={{0,8},{1,9},{2,10},{3,11},{4,12},{5,13},{6,14},{7,15},{8,0},{9,1},... | collective-permute-start | bytes 98312 | tf_op jit(solution)/shard_map/ppermute | solution.py:377
  33.3 5.3 %collective-permute-start.9 = (bf16[32,512]{1,0:T(8,128)(2,1)S(1)}, bf16[32,512]{1,0:T(8,128)(2,1)S(1)}, u32[]{:S(2)}, u32[]{:S(2)}) collective-permute-start(bf16[32,512]{1,0:T(8,128)(2,1)S(1)} %get-tuple-element.52), channel_id=1, source_target_pairs={{0,12},{1,13},{2,14},{3,15},{4,0},{5,1},{6,2},{7,3},{8,4},{9,5},{1... | collective-permute-start | bytes 98312 | tf_op jit(solution)/shard_map/ppermute | solution.py:377
  34.5 1.0 copy-start.5
  35.4 40.8 %copy-start.1 = (bf16[1,1024,1536]{2,1,0:T(8,128)(2,1)S(1)}, bf16[1,1024,1536]{2,1,0:T(8,128)(2,1)}, u32[]{:S(2)}) copy-start(bf16[1,1024,1536]{2,1,0:T(8,128)(2,1)} %param.17) | copy-start | bytes 9437188
  38.6 37.7 %copy-start.9 = (f32[2048]{0:T(1024)S(1)}, f32[2048]{0:T(1024)}, u32[]{:S(2)}) copy-start(f32[2048]{0:T(1024)} %param.13) | copy-start | bytes 24580
  40.2 5.0 %collective-permute-start.10 = (bf16[128,512]{1,0:T(8,128)(2,1)S(1)}, bf16[128,512]{1,0:T(8,128)(2,1)S(1)}, u32[]{:S(2)}, u32[]{:S(2)}) collective-permute-start(bf16[128,512]{1,0:T(8,128)(2,1)S(1)} %get-tuple-element.53), channel_id=1, source_target_pairs={{0,16},{16,0},{1,17},{17,1},{2,18},{18,2},{3,19},{19,3},{4,20},{20... | collective-permute-start | bytes 393224 | tf_op jit(solution)/shard_map/ppermute | solution.py:374
  45.3 8.2 %collective-permute-start.13 = (bf16[144,512]{1,0:T(8,128)(2,1)S(1)}, bf16[144,512]{1,0:T(8,128)(2,1)S(1)}, u32[]{:S(2)}, u32[]{:S(2)}) collective-permute-start(bf16[144,512]{1,0:T(8,128)(2,1)S(1)} %stream.1), channel_id=1, source_target_pairs={{0,12},{1,13},{2,14},{3,15},{4,0},{5,1},{6,2},{7,3},{8,4},{9,5},{1... | collective-permute-start | bytes 442376 | tf_op jit(solution)/shard_map/ppermute | solution.py:377
  49.1 11.5 %collective-permute-start.12 = (bf16[144,512]{1,0:T(8,128)(2,1)S(1)}, bf16[144,512]{1,0:T(8,128)(2,1)S(1)}, u32[]{:S(2)}, u32[]{:S(2)}) collective-permute-start(bf16[144,512]{1,0:T(8,128)(2,1)S(1)} %stream.1), channel_id=1, source_target_pairs={{0,8},{1,9},{2,10},{3,11},{4,12},{5,13},{6,14},{7,15},{8,0},{9,1},... | collective-permute-start | bytes 442376 | tf_op jit(solution)/shard_map/ppermute | solution.py:377
  49.1 11.5 %collective-permute-start.11 = (bf16[144,512]{1,0:T(8,128)(2,1)S(1)}, bf16[144,512]{1,0:T(8,128)(2,1)S(1)}, u32[]{:S(2)}, u32[]{:S(2)}) collective-permute-start(bf16[144,512]{1,0:T(8,128)(2,1)S(1)} %stream.1), channel_id=1, source_target_pairs={{0,4},{1,5},{2,6},{3,7},{4,8},{5,9},{6,10},{7,11},{8,12},{9,13},{1... | collective-permute-start | bytes 442376 | tf_op jit(solution)/shard_map/ppermute | solution.py:377
  50.2 33.3 %collective-permute-start.17 = (bf16[1024,768]{1,0:T(8,128)(2,1)S(1)}, bf16[1024,768]{1,0:T(8,128)(2,1)S(1)}, u32[]{:S(2)}, u32[]{:S(2)}) collective-permute-start(bf16[1024,768]{1,0:T(8,128)(2,1)S(1)} %weight_piece.3), channel_id=1, source_target_pairs={{0,16},{16,0},{1,17},{17,1},{2,18},{18,2},{3,19},{19,3},{4,20},{20... | collective-permute-start | bytes 4718600 | tf_op jit(solution)/shard_map/ppermute | solution.py:374
  60.7 13.5 %collective-permute-start.14 = (bf16[4,144,512]{2,1,0:T(8,128)(2,1)S(1)}, bf16[4,144,512]{2,1,0:T(8,128)(2,1)S(1)}, u32[]{:S(2)}, u32[]{:S(2)}) collective-permute-start(bf16[4,144,512]{2,1,0:T(8,128)(2,1)S(1)} %pad_maximum_fusion.blocks), channel_id=1, source_target_pairs={{0,2},{1,3},{2,0},{3,1},{4,6},{5,7},{6,4},{7,5},{8,10},{9,11},{10,... | collective-permute-start | bytes 1769480 | tf_op jit(solution)/shard_map/ppermute | solution.py:393
  62.3 12.0 %collective-permute-start.15 = (bf16[4,144,512]{2,1,0:T(8,128)(2,1)S(1)}, bf16[4,144,512]{2,1,0:T(8,128)(2,1)S(1)}, u32[]{:S(2)}, u32[]{:S(2)}) collective-permute-start(bf16[4,144,512]{2,1,0:T(8,128)(2,1)S(1)} %pad_maximum_fusion.blocks), channel_id=1, source_target_pairs={{0,1},{1,0},{2,3},{3,2},{4,5},{5,4},{6,7},{7,6},{8,9},{9,8},{10,11... | collective-permute-start | bytes 1769480 | tf_op jit(solution)/shard_map/ppermute | solution.py:393
  74.2 2.0 %collective-permute-start.16 = (bf16[4,144,512]{2,1,0:T(8,128)(2,1)S(1)}, bf16[4,144,512]{2,1,0:T(8,128)(2,1)S(1)}, u32[]{:S(2)}, u32[]{:S(2)}) collective-permute-start(bf16[4,144,512]{2,1,0:T(8,128)(2,1)S(1)} %collective-permute-done.14.blocks_x), channel_id=1, source_target_pairs={{0,1},{1,0},{2,3},{3,2},{4,5},{5,4},{6,7},{7,6},{8,9},{9,8},{10,11... | collective-permute-start | bytes 1769480 | tf_op jit(solution)/shard_map/ppermute | solution.py:393
  83.4 1.4 %copy-start.2 = (bf16[1,768,1024]{2,1,0:T(8,128)(2,1)S(1)}, bf16[1,768,1024]{2,1,0:T(8,128)(2,1)}, u32[]{:S(2)}) copy-start(bf16[1,768,1024]{2,1,0:T(8,128)(2,1)} %param.18) | copy-start | bytes 4718596
  85.8 2.0 %collective-permute-start.18 = (bf16[256,1024]{1,0:T(8,128)(2,1)S(1)}, bf16[256,1024]{1,0:T(8,128)(2,1)S(1)}, u32[]{:S(2)}, u32[]{:S(2)}) collective-permute-start(bf16[256,1024]{1,0:T(8,128)(2,1)S(1)} %get-tuple-element.65), channel_id=1, source_target_pairs={{0,1},{1,0},{2,3},{3,2},{4,5},{5,4},{6,7},{7,6},{8,9},{9,8},{10,11... | collective-permute-start | bytes 1572872 | tf_op jit(solution)/shard_map/ppermute | solution.py:393
  85.9 11.5 %collective-permute-start.23 = (bf16[256,768]{1,0:T(8,128)(2,1)S(1)}, bf16[256,768]{1,0:T(8,128)(2,1)S(1)}, u32[]{:S(2)}, u32[]{:S(2)}) collective-permute-start(bf16[256,768]{1,0:T(8,128)(2,1)S(1)} %get-tuple-element.62.far), channel_id=1, source_target_pairs={{0,16},{16,0},{1,17},{17,1},{2,18},{18,2},{3,19},{19,3},{4,20},{20... | collective-permute-start | bytes 1179656 | tf_op jit(solution)/shard_map/ppermute | solution.py:374
  87.9 9.6 %collective-permute-start.19 = (bf16[128,1024]{1,0:T(8,128)(2,1)S(1)}, bf16[128,1024]{1,0:T(8,128)(2,1)S(1)}, u32[]{:S(2)}, u32[]{:S(2)}) collective-permute-start(bf16[128,1024]{1,0:T(8,128)(2,1)S(1)} %add_convert_fusion.1), channel_id=1, source_target_pairs={{0,2},{1,3},{2,0},{3,1},{4,6},{5,7},{6,4},{7,5},{8,10},{9,11},{10,... | collective-permute-start | bytes 786440 | tf_op jit(solution)/shard_map/ppermute | solution.py:393
  98.0 1.7 %collective-permute-start.25 = (bf16[128,1024]{1,0:T(8,128)(2,1)S(1)}, bf16[128,1024]{1,0:T(8,128)(2,1)S(1)}, u32[]{:S(2)}, u32[]{:S(2)}) collective-permute-start(bf16[128,1024]{1,0:T(8,128)(2,1)S(1)} %get-tuple-element.74), channel_id=1, source_target_pairs={{0,1},{1,0},{2,3},{3,2},{4,5},{5,4},{6,7},{7,6},{8,9},{9,8},{10,11... | collective-permute-start | bytes 786440 | tf_op jit(solution)/shard_map/ppermute | solution.py:393
  98.1 11.5 %collective-permute-start.24 = (bf16[256,768]{1,0:T(8,128)(2,1)S(1)}, bf16[256,768]{1,0:T(8,128)(2,1)S(1)}, u32[]{:S(2)}, u32[]{:S(2)}) collective-permute-start(bf16[256,768]{1,0:T(8,128)(2,1)S(1)} %get-tuple-element.71.near), channel_id=1, source_target_pairs={{0,16},{16,0},{1,17},{17,1},{2,18},{18,2},{3,19},{19,3},{4,20},{20... | collective-permute-start | bytes 1179656 | tf_op jit(solution)/shard_map/ppermute | solution.py:374
  99.8 10.9 %collective-permute-start.26 = (bf16[128,1024]{1,0:T(8,128)(2,1)S(1)}, bf16[128,1024]{1,0:T(8,128)(2,1)S(1)}, u32[]{:S(2)}, u32[]{:S(2)}) collective-permute-start(bf16[128,1024]{1,0:T(8,128)(2,1)S(1)} %add_convert_fusion), channel_id=1, source_target_pairs={{0,2},{1,3},{2,0},{3,1},{4,6},{5,7},{6,4},{7,5},{8,10},{9,11},{10,... | collective-permute-start | bytes 786440 | tf_op jit(solution)/shard_map/ppermute | solution.py:393
  101.5 23.1 %copy-start.8 = (f32[2048]{0:T(1024)S(1)}, f32[2048]{0:T(1024)}, u32[]{:S(2)}) copy-start(f32[2048]{0:T(1024)} %param.19) | copy-start | bytes 24580
  101.5 8.2 %collective-permute-start.20 = (bf16[32,1024]{1,0:T(8,128)(2,1)S(1)}, bf16[32,1024]{1,0:T(8,128)(2,1)S(1)}, u32[]{:S(2)}, u32[]{:S(2)}) collective-permute-start(bf16[32,1024]{1,0:T(8,128)(2,1)S(1)} %get-tuple-element.68), channel_id=1, source_target_pairs={{0,4},{1,5},{2,6},{3,7},{4,8},{5,9},{6,10},{7,11},{8,12},{9,13},{1... | collective-permute-start | bytes 196616 | tf_op jit(solution)/shard_map/ppermute | solution.py:377
  104.0 6.5 %collective-permute-start.21 = (bf16[32,1024]{1,0:T(8,128)(2,1)S(1)}, bf16[32,1024]{1,0:T(8,128)(2,1)S(1)}, u32[]{:S(2)}, u32[]{:S(2)}) collective-permute-start(bf16[32,1024]{1,0:T(8,128)(2,1)S(1)} %get-tuple-element.69), channel_id=1, source_target_pairs={{0,8},{1,9},{2,10},{3,11},{4,12},{5,13},{6,14},{7,15},{8,0},{9,1},... | collective-permute-start | bytes 196616 | tf_op jit(solution)/shard_map/ppermute | solution.py:377
  105.2 5.4 %collective-permute-start.22 = (bf16[32,1024]{1,0:T(8,128)(2,1)S(1)}, bf16[32,1024]{1,0:T(8,128)(2,1)S(1)}, u32[]{:S(2)}, u32[]{:S(2)}) collective-permute-start(bf16[32,1024]{1,0:T(8,128)(2,1)S(1)} %get-tuple-element.70), channel_id=1, source_target_pairs={{0,12},{1,13},{2,14},{3,15},{4,0},{5,1},{6,2},{7,3},{8,4},{9,5},{1... | collective-permute-start | bytes 196616 | tf_op jit(solution)/shard_map/ppermute | solution.py:377
  111.2 1.6 %collective-permute-start.27 = (bf16[128,1024]{1,0:T(8,128)(2,1)S(1)}, bf16[128,1024]{1,0:T(8,128)(2,1)S(1)}, u32[]{:S(2)}, u32[]{:S(2)}) collective-permute-start(bf16[128,1024]{1,0:T(8,128)(2,1)S(1)} %get-tuple-element.77), channel_id=1, source_target_pairs={{0,1},{1,0},{2,3},{3,2},{4,5},{5,4},{6,7},{7,6},{8,9},{9,8},{10,11... | collective-permute-start | bytes 786440 | tf_op jit(solution)/shard_map/ppermute | solution.py:393
  112.9 6.6 %collective-permute-start.28 = (bf16[32,1024]{1,0:T(8,128)(2,1)S(1)}, bf16[32,1024]{1,0:T(8,128)(2,1)S(1)}, u32[]{:S(2)}, u32[]{:S(2)}) collective-permute-start(bf16[32,1024]{1,0:T(8,128)(2,1)S(1)} %get-tuple-element.78), channel_id=1, source_target_pairs={{0,16},{1,17},{2,18},{3,19},{4,20},{5,21},{6,22},{7,23},{8,24},{9,... | collective-permute-start | bytes 196616 | tf_op jit(solution)/shard_map/ppermute | solution.py:382
  114.5 7.5 %collective-permute-start.29 = (bf16[32,1024]{1,0:T(8,128)(2,1)S(1)}, bf16[32,1024]{1,0:T(8,128)(2,1)S(1)}, u32[]{:S(2)}, u32[]{:S(2)}) collective-permute-start(bf16[32,1024]{1,0:T(8,128)(2,1)S(1)} %get-tuple-element.79), channel_id=1, source_target_pairs={{0,20},{1,21},{2,22},{3,23},{4,24},{5,25},{6,26},{7,27},{8,28},{9,... | collective-permute-start | bytes 196616 | tf_op jit(solution)/shard_map/ppermute | solution.py:382
  116.2 7.7 %collective-permute-start.30 = (bf16[32,1024]{1,0:T(8,128)(2,1)S(1)}, bf16[32,1024]{1,0:T(8,128)(2,1)S(1)}, u32[]{:S(2)}, u32[]{:S(2)}) collective-permute-start(bf16[32,1024]{1,0:T(8,128)(2,1)S(1)} %get-tuple-element.80), channel_id=1, source_target_pairs={{0,24},{1,25},{2,26},{3,27},{4,28},{5,29},{6,30},{7,31},{8,16},{9,... | collective-permute-start | bytes 196616 | tf_op jit(solution)/shard_map/ppermute | solution.py:382
  118.4 6.1 %collective-permute-start.31 = (bf16[32,1024]{1,0:T(8,128)(2,1)S(1)}, bf16[32,1024]{1,0:T(8,128)(2,1)S(1)}, u32[]{:S(2)}, u32[]{:S(2)}) collective-permute-start(bf16[32,1024]{1,0:T(8,128)(2,1)S(1)} %get-tuple-element.81), channel_id=1, source_target_pairs={{0,28},{1,29},{2,30},{3,31},{4,16},{5,17},{6,18},{7,19},{8,20},{9,... | collective-permute-start | bytes 196616 | tf_op jit(solution)/shard_map/ppermute | solution.py:382

commit v6 on v5

--- a/solution.py
+++ b/solution.py
@@ -149,8 +149,8 @@
     return jnp.dot(a, b, preferred_element_type=F32)
 
 
-def cost(flops, moved):
-    return pl.CostEstimate(flops=flops, bytes_accessed=moved, transcendentals=0)
+def small_cost():
+    return pl.CostEstimate(flops=1, bytes_accessed=1, transcendentals=0)
 
 
 def kernel_params(mib):
@@ -166,7 +166,16 @@
     return pl.ds(pl.multiple_of(index * step, step), step)
 
 
-def prepare_kernel(live, ids, logits, resid, share_ref, r0, r1, r2, r3):
+def cut_kernel(resid, r0, r1, r23):
+    expert, outer, inner, dp = seat()
+    rows, lanes = r0.shape
+    r0[...] = resid[:, aligned(outer, lanes)]
+    r1[...] = resid[:, aligned(outer ^ 1, lanes)]
+    for i in range(2):
+        r23[i * rows : (i + 1) * rows, :] = resid[:, aligned(outer ^ (2 + i), lanes)]
+
+
+def share_kernel(live, ids, logits, share_ref):
     expert, outer, inner, dp = seat()
     rows, top = ids.shape
     experts, lanes = share_ref.shape
@@ -183,8 +192,6 @@
     share_ref[...] = lax.dot_general(
         table.astype(BF16), spots, (((0,), (0,)), ((), ())), preferred_element_type=F32
     ).astype(BF16)
-    for s, r in enumerate((r0, r1, r2, r3)):
-        r[...] = resid[:, aligned((outer + s) & 3, lanes)]
 
 
 def proj_kernel(a0, a1, a2, a3, w0, w1, w2, w3, keep_ref, send_ref, rows, part):
@@ -201,14 +208,14 @@
         send_ref[spot * half : (spot + 1) * half, :] = part[aligned(2 * spot + 1 - dp, half), :]
 
 
-def stream_kernel(keep, arrived, r0, r1, r2, r3, share, block_ref):
+def stream_kernel(keep, arrived, r0, r13, r2, share, block_ref):
     expert, outer, inner, dp = seat()
     count = keep.shape[0]
     small = r0.shape[0]
-    for s, r in enumerate((r0, r1, r2, r3)):
-        rows = aligned((outer + 4 - s) & 3, small)
+    for s, r in enumerate((r0[...], r13[0:small, :], r2[0:small, :], r13[small:, :])):
+        rows = aligned(outer ^ s, small)
         product = keep[rows, :].astype(F32) + arrived[rows, :].astype(F32)
-        block_ref[rows, :] = (r[...].astype(F32) + product).astype(BF16)
+        block_ref[rows, :] = (r.astype(F32) + product).astype(BF16)
     block_ref[count:, :] = share[...]
 
 
@@ -232,45 +239,52 @@
     return (gate / (1.0 + jnp.exp(-gate)) * up * share).astype(BF16)
 
 
+def norm_kernel(b0, b1, b2, b3, gain, group_ref, own_ref):
+    expert, outer, inner, dp = seat()
+    count = group_ref.shape[0]
+    width = b0.shape[1]
+    experts = b0.shape[0] - count
+    small = own_ref.shape[0]
+    square = jnp.zeros((count, 1), F32)
+    share = jnp.zeros((experts, count), F32)
+    for s, b in enumerate((b0, b1, b2, b3)):
+        value = b[0:count, :]
+        group_ref[:, aligned((outer + 4 - s) & 3, width)] = value
+        value = value.astype(F32)
+        square = square + jnp.sum(value * value, axis=1, keepdims=True)
+        share = share + b[count : count + experts, 0:count].astype(F32)
+    own_ref[...] = group_ref[aligned(outer, small), 0 : 4 * width]
+    scale = lax.rsqrt(square / (4 * width) + 1e-06)
+    for s in range(4):
+        cols = slice(s * width, (s + 1) * width)
+        value = group_ref[:, cols].astype(F32)
+        group_ref[:, cols] = (value * scale * gain[:, cols]).astype(BF16)
+    lanes = (experts, 128)
+    spread = lax.broadcasted_iota(jnp.int32, lanes, 0) == lax.broadcasted_iota(jnp.int32, lanes, 1)
+    group_ref[:, 4 * width :] = lax.dot_general(
+        share.astype(BF16),
+        spread.astype(F32).astype(BF16),
+        (((0,), (0,)), ((), ())),
+        preferred_element_type=F32,
+    ).astype(BF16)
+
+
 def first_gate_kernel(
-    blocks, blocks_x, blocks_c, blocks_cx, gain, own, early,
-    inner_ref, part_ref, other_ref, share_ref, own_ref, normed,
+    group_x, group_cx, group, group_c, own, early, inner_ref, part_ref, other_ref, share_ref, mine_ref
 ):
     expert, outer, inner, dp = seat()
-    width = blocks.shape[2]
-    count = share_ref.shape[0] // 4
-    experts = blocks.shape[1] - count
-    half = normed.shape[1] // 2
-    small = own_ref.shape[0]
+    count = group.shape[0]
+    half = other_ref.shape[1]
     cut = inner_ref.shape[1]
-    picked = lax.broadcasted_iota(jnp.int32, (experts, count), 0) == expert
-    diagonal = lax.broadcasted_iota(jnp.int32, (count, count), 0) == lax.broadcasted_iota(
-        jnp.int32, (count, count), 1
-    )
-    for j, group in enumerate((blocks_x, blocks_cx, blocks, blocks_c)):
+    for j, g in enumerate((group_x, group_cx, group, group_c)):
         rows = slice(j * count, (j + 1) * count)
-        square = jnp.zeros((count, 1), F32)
-        share = jnp.zeros((experts, count), F32)
-        for s in range(4):
-            value = group[s, 0:count, :]
-            normed[rows, aligned((outer + 4 - s) & 3, width)] = value
-            value = value.astype(F32)
-            square = square + jnp.sum(value * value, axis=1, keepdims=True)
-            share = share + group[s, count : count + experts, 0:count].astype(F32)
-        line = jnp.sum(jnp.where(picked, share, 0.0), axis=0, keepdims=True)
-        column = jnp.sum(jnp.where(diagonal, line, 0.0), axis=1, keepdims=True)
-        share_ref[rows, :] = jnp.broadcast_to(column, (count, share_ref.shape[1]))
-        if j == 2:
-            own_ref[...] = normed[aligned(outer + 2 * (count // small), small), :]
-        scale = lax.rsqrt(square / (4 * width) + 1e-06)
-        for s in range(4):
-            cols = slice(s * width, (s + 1) * width)
-            value = normed[rows, cols].astype(F32)
-            normed[rows, cols] = (value * scale * gain[:, cols]).astype(BF16)
-    other_ref[...] = normed[:, aligned(1 - dp, half)]
-
-    mine = normed[:, aligned(dp, half)]
-    other = other_ref[...]
+        mine_ref[rows, :] = g[:, aligned(dp, half)]
+        other_ref[rows, :] = g[:, aligned(1 - dp, half)]
+        share = g[:, 2 * half : 2 * half + 128].astype(F32)
+        picked = lax.broadcasted_iota(jnp.int32, share.shape, 1) == expert
+        share = jnp.sum(jnp.where(picked, share, 0.0), axis=1, keepdims=True)
+        share_ref[rows, :] = jnp.broadcast_to(share, (count, 128))
+    mine, other = mine_ref[...], other_ref[...]
     gate = dot(mine, own[:, 0:cut]) + dot(other, early[:, 0:cut])
     up = dot(mine, own[:, 2 * cut : 3 * cut]) + dot(other, early[:, cut : 2 * cut])
     inner_ref[...] = swiglu(gate, up, share_ref[:, 0:1])
@@ -294,15 +308,9 @@
     return [slice(at, at + 256) for at in range(0, wd.shape[1], 256)]
 
 
-def down_both_kernel(far, near, wd, keep_far, keep_near, send_ref):
-    count = keep_far.shape[0]
-    for cols in column_chunks(wd):
-        value = dot(far[...], wd[:, cols]).astype(BF16)
-        keep_far[:, cols] = value[:count]
-        send_ref[0:count, cols] = value[count:]
-        value = dot(near[...], wd[:, cols]).astype(BF16)
-        keep_near[:, cols] = value[:count]
-        send_ref[count : 2 * count, cols] = value[count:]
+def down_both_kernel(far, near, wd, keep_far, keep_near, send_far, send_near):
+    down_kernel(far, wd, keep_far, send_far)
+    down_kernel(near, wd, keep_near, send_near)
 
 
 def down_kernel(rows, wd, keep_ref, send_ref):
@@ -322,10 +330,10 @@
         p[...] = (total + far[rows, :].astype(F32)).astype(BF16)
 
 
-def tail_kernel(own, m0, m1, m2, m3, o0, o1, o2, o3, gain, stream_ref, normed_ref):
+def tail_kernel(own, m0, o0, o1, o2, o3, gain, stream_ref, normed_ref):
     expert, outer, inner, dp = seat()
     half = m0.shape[1]
-    for at, pieces in ((dp, (m0, m1, m2, m3)), (1 - dp, (o0, o1, o2, o3))):
+    for at, pieces in ((dp, (m0,)), (1 - dp, (o0, o1, o2, o3))):
         cols = aligned(at, half)
         mixture = pieces[0][...].astype(F32)
         for piece in pieces[1:]:
@@ -357,8 +365,7 @@
     def shape_of(*shape, dtype=BF16):
         return jax.ShapeDtypeStruct(shape, dtype)
 
-    def call(kernel, name, mib, outs, *args, scratch=(), first=vmem, flops=1_000_000):
-        moved = sum(math.prod(x.shape) * x.dtype.itemsize for x in (*args, *outs))
+    def call(kernel, name, mib, outs, *args, scratch=(), first=vmem):
         return pl.pallas_call(
             kernel,
             out_shape=outs,
@@ -366,7 +373,7 @@
             out_specs=tuple(vmem for _ in outs),
             scratch_shapes=list(scratch),
             compiler_params=kernel_params(mib),
-            cost_estimate=cost(flops, moved),
+            cost_estimate=small_cost(),
             name=name,
         )(*args)
 
@@ -406,32 +413,34 @@
             out_specs=vmem,
             scratch_shapes=[pltpu.SemaphoreType.DMA((2,))],
             compiler_params=kernel_params(8),
-            cost_estimate=cost(1000, 4 * half_width * hidden),
+            cost_estimate=small_cost(),
             name="weight_piece",
         )(w_gate_up[0])
 
-    cut_width = hidden // 2
-    early_piece, late_piece = (weight_piece(i) for i in range(2))
-    a = [attn[0], swap_outer(attn[0], 1), swap_outer(attn[0], 2)]
-    a.append(swap_outer(after(a[2], a[1]), 1))
-    w_x = swap_inner(w_out, 2)
-    gate_up_early = swap_dp(early_piece)
-    w_c = swap_inner(after(w_out, w_x), 1)
-    w_cx = swap_inner(w_x, 1)
-
     piece = shape_of(rows_here, quarter)
-    share, *r = call(
-        prepare_kernel,
-        "prepare",
+    r_own, r_1, r_23 = call(
+        cut_kernel, "cut_resid", 4, (piece, piece, shape_of(2 * rows_here, quarter)), resid[0]
+    )
+    (share,) = call(
+        share_kernel,
+        "share",
         4,
-        (shape_of(expert_count, quarter), piece, piece, piece, piece),
+        (shape_of(expert_count, quarter),),
         live_count,
         route_ids[0],
         route_logits[0],
-        resid[0],
         first=smem,
     )
-    r = [r[0]] + [shift_outer(after(r[s], a[1]), s) for s in (1, 2, 3)]
+    cut_width = hidden // 2
+    early_piece, late_piece = (weight_piece(i) for i in range(2))
+    gate_up_early = swap_dp(early_piece)
+    a = [attn[0], swap_outer(attn[0], 1), swap_outer(attn[0], 2)]
+    w_x = swap_inner(w_out, 2)
+    r_2 = swap_outer(r_23, 2)
+    a.append(swap_outer(after(a[2], a[1], r_2), 1))
+    w_c = swap_inner(after(w_out, w_x), 1)
+    w_cx = swap_inner(w_x, 1)
+    r_13 = swap_outer(jnp.concatenate([r_1, r_2[rows_here:]], axis=0), 1)
 
     product = shape_of(4 * rows_here, quarter)
     keep, send = call(
@@ -444,13 +453,12 @@
         w_c,
         w_x,
         w_cx,
-        flops=16 * rows_here * attn.shape[2] * quarter,
         scratch=(
             pltpu.VMEM((8 * rows_here, attn.shape[2]), BF16),
             pltpu.VMEM((8 * rows_here, quarter), BF16),
         ),
     )
-    arrived = swap_dp(after(send, gate_up_early, late_piece, *r[1:]))
+    arrived = swap_dp(after(send, gate_up_early, late_piece, r_13, share))
     gate_up_late = swap_dp(after(late_piece, arrived))
     (block,) = call(
         stream_kernel,
@@ -459,19 +467,31 @@
         (shape_of(4 * rows_here + expert_count, quarter),),
         keep,
         arrived,
-        *r,
+        r_own,
+        r_13,
+        r_2,
         share,
     )
 
-    blocks = jnp.stack([block] + [shift_outer(block, s) for s in (1, 2, 3)])
-    blocks_x = swap_inner(blocks, 2)
-    blocks_c = swap_inner(blocks, 1)
-    blocks_cx = swap_inner(blocks_x, 1)
+    group, stream_own = call(
+        norm_kernel,
+        "norm",
+        8,
+        (
+            shape_of(4 * rows_here, model_width + 128),
+            shape_of(rows_here, model_width),
+        ),
+        block,
+        *(shift_outer(block, s) for s in (1, 2, 3)),
+        gain_post[None],
+    )
+    group_x = swap_inner(group, 2)
+    group_c = swap_inner(group, 1)
+    group_cx = swap_inner(group_x, 1)
 
     row_total = 16 * rows_here
     half_rows = row_total // 2
-    product_flops = 2 * row_total * half_width * hidden
-    inner_first, part, other_rows, share_rows, stream_own = call(
+    inner_first, part, other_rows, share_rows = call(
         first_gate_kernel,
         "first_gate_up",
         24,
@@ -480,17 +500,14 @@
             shape_of(row_total, hidden, dtype=F32),
             shape_of(row_total, half_width),
             shape_of(row_total, 128, dtype=F32),
-            shape_of(rows_here, model_width),
         ),
-        blocks,
-        blocks_x,
-        blocks_c,
-        blocks_cx,
-        gain_post[None],
+        group_x,
+        group_cx,
+        group,
+        group_c,
         w_gate_up[0],
         gate_up_early,
-        flops=3 * product_flops,
-        scratch=(pltpu.VMEM((row_total, model_width), BF16),),
+        scratch=(pltpu.VMEM((row_total, half_width), BF16),),
     )
     inner_half = shape_of(half_rows, hidden)
     inner_far, inner_near = call(
@@ -503,10 +520,9 @@
         other_rows,
         share_rows,
         gate_up_late,
-        flops=product_flops,
     )
     far_other = swap_dp(inner_far)
-    near_other = swap_dp(after(inner_near, far_other))
+    near_other = swap_dp(inner_near)
 
     count = row_total // 4
     quarter_out = shape_of(count, half_width)
@@ -519,7 +535,6 @@
             (quarter_out, quarter_out),
             rows,
             w_down[0],
-            flops=product_flops // 2,
         )
 
     def add(x, y):
@@ -529,26 +544,25 @@
         out = shape_of(rows_here, half_width)
         return call(pieces_kernel, "pieces", 4, (out, out, out, out), keep, core, far)
 
-    keep_far, keep_near, core_send = call(
+    keep_far, keep_near, send_far, send_near = call(
         down_both_kernel,
         "down_both",
         16,
-        (quarter_out, quarter_out, shape_of(2 * count, half_width)),
+        (quarter_out, quarter_out, quarter_out, quarter_out),
         inner_far,
         inner_near,
         w_down[0],
-        flops=product_flops,
-    )
-    core = swap_inner(core_send, 1)
-    far = swap_inner(add(keep_far, core[:count]), 2)
+    )
+    far = swap_inner(add(keep_far, swap_inner(send_far, 1)), 2)
     ready = far
-    cut = pieces(keep_near, core[count:], far)
-    mine = [cut[0]] + [shift_outer(cut[s], s) for s in (1, 2, 3)]
-
-    keep_far, core_send = down(after(far_other, ready))
-    far = swap_inner(add(keep_far, swap_inner(core_send, 1)), 2)
-    keep_near, core_send = down(after(near_other, far, *mine[1:]))
-    cut = pieces(keep_near, swap_inner(core_send, 1), far)
+    outer_groups = [[i + 4 * z for z in range(4)] for i in range(4)]
+    total = add(add(keep_near, swap_inner(send_near, 1)), far).reshape(4, rows_here, half_width)
+    mine = [lax.psum_scatter(total, "expert", scatter_dimension=0, axis_index_groups=outer_groups)]
+
+    keep_far, send_far = down(after(far_other, ready))
+    far = swap_inner(add(keep_far, swap_inner(send_far, 1)), 2)
+    keep_near, send_near = down(after(near_other, far))
+    cut = pieces(keep_near, swap_inner(send_near, 1), far)
     others = [cross_outer(cut[s], s) for s in range(4)]
 
     out = shape_of(rows_here, model_width)

time: 126 us -> 138 us (1.095)
  between operations: 1.48 us -> 14.9 us
  starting transfers between devices: 44.1 us -> 34.4 us
  waiting for transfers between devices: 58.5 us -> 63.3 us
  local copies, waits for them, and re-layouts: 6.46 us -> 9.08 us
  other arithmetic: 0.21 us -> 1.59 us
    ppermute x9 -> x3, starting transfers between devices: 15.5 us -> 4.67 us  [shift_outer(): lax.ppermute(x, 'expert', [(i, (i + 4 * s) % expert_count) for i in range...]
    ppermute x5, waiting for transfers between devices: 17 us -> 20.9 us  [swap_dp(): return lax.ppermute(x, 'dp', [(0, 1), (1, 0)])]
    ppermute x4, waiting for transfers between devices: 5.01 us -> 1.35 us  [cross_outer(): lax.ppermute(x, ('dp', 'expert'), [(d * expert_count + i, (1 - d) * exper...]
    ppermute x3 -> x5, waiting for transfers between devices: 2.73 us -> 6.13 us  [swap_outer(): lax.ppermute(x, 'expert', [(i, i ^ 4 * s) for i in range(expert_count)])]
    unnamed x22 -> x32, local copies, waits for them, and re-layouts: 6.44 us -> 9.08 us
    ppermute x5, starting transfers between devices: 9.46 us -> 7.53 us  [swap_dp(): return lax.ppermute(x, 'dp', [(0, 1), (1, 0)])]
    ppermute x4, starting transfers between devices: 6.57 us -> 8.13 us  [cross_outer(): lax.ppermute(x, ('dp', 'expert'), [(d * expert_count + i, (1 - d) * exper...]
    reduce_scatter x0 -> x1, waiting for transfers between devices: none -> 1.49 us  [body_paired(): lax.psum_scatter(total, 'expert', scatter_dimension=0, axis_index_groups=...]
  transfers between devices with their start and end apart: 32 -> 30, of which waited for: 20 -> 17; matrix products, arithmetic and copies ran while one was open for 2% -> 3% of each run, Pallas kernels for 8% -> 7%
where the time goes in v6:
time: 138 us
  waiting for transfers between devices  63.3 us (46%)
  starting transfers between devices  34.4 us (25%)
  between operations  14.9 us (11%)
  Pallas kernels  14.6 us (11%)
  local copies, waits for them, and re-layouts  9.08 us (7%)
  other arithmetic  1.59 us (1%)
    ppermute x12, waiting for transfers between devices, swap_inner(): return lax.ppermute(x, 'expert', [(i, i ^ j) for i in range(expert_count)])  23.2 us
    ppermute x5, waiting for transfers between devices, swap_dp(): return lax.ppermute(x, 'dp', [(0, 1), (1, 0)])  20.9 us
    pallas_call x12, Pallas kernels, call(): pl.pallas_call(kernel, out_shape=outs, in_specs=[first] + [vmem] * (len(a...  13.1 us
    ppermute x3, waiting for transfers between devices, shift_outer(): lax.ppermute(x, 'expert', [(i, (i + 4 * s) % expert_count) for i in range...  10.2 us
    unnamed x32, local copies, waits for them, and re-layouts  9.08 us
    ppermute x4, starting transfers between devices, cross_outer(): lax.ppermute(x, ('dp', 'expert'), [(d * expert_count + i, (1 - d) * exper...  8.13 us
    ppermute x5, starting transfers between devices, swap_dp(): return lax.ppermute(x, 'dp', [(0, 1), (1, 0)])  7.53 us
    ppermute x12, starting transfers between devices, swap_inner(): return lax.ppermute(x, 'expert', [(i, i ^ j) for i in range(expert_count)])  7.52 us
  transfers between devices with their start and end apart: 30, of which 17 were waited for; matrix products, arithmetic and copies ran while one was open for 3% of the time, Pallas kernels for 7%

profile of v6, /device:TPU:0, one launch (start us, length us, event | category | flops | bytes accessed | tf_op | source)
XLA Modules:
  0.0 137.8 jit_solution(6071466201979127599)
XLA Ops:
  7.2 1.9 %copy-done = bf16[1,1024,1536]{2,1,0:T(8,128)(2,1)S(1)} copy-done((bf16[1,1024,1536]{2,1,0:T(8,128)(2,1)S(1)}, bf16[1,1024,1536]{2,1,0:T(8,128)(2,1)}, u32[]{:S(2)}) %copy-start) | copy-done | bytes 3145752
  9.1 1.3 weight_piece.2
  10.4 3.0 %collective-permute-start.7 = (bf16[1024,768]{1,0:T(8,128)(2,1)}, bf16[1024,768]{1,0:T(8,128)(2,1)}, u32[]{:S(2)}, u32[]{:S(2)}) collective-permute-start(bf16[1024,768]{1,0:T(8,128)(2,1)} %weight_piece.2), channel_id=1, source_target_pairs={{0,16},{16,0},{1,17},{17,1},{2,18},{18,2},{3,19},{19,3},{4,20},{20... | collective-permute-start | bytes 4718600 | tf_op jit(solution)/shard_map/ppermute | solution.py:381
  13.5 1.5 %collective-permute-start.4 = (bf16[2048,128]{1,0:T(8,128)(2,1)}, bf16[2048,128]{1,0:T(8,128)(2,1)}, u32[]{:S(2)}, u32[]{:S(2)}) collective-permute-start(bf16[2048,128]{1,0:T(8,128)(2,1)} %w0.1), channel_id=1, source_target_pairs={{0,2},{1,3},{2,0},{3,1},{4,6},{5,7},{6,4},{7,5},{8,10},{9,11},{10,... | collective-permute-start | bytes 1572872 | tf_op jit(solution)/shard_map/ppermute | solution.py:400
  15.0 0.6 copy-done.11
  15.6 2.6 %collective-permute-start.2 = (bf16[64,512]{1,0:T(8,128)(2,1)S(1)}, bf16[64,512]{1,0:T(8,128)(2,1)S(1)}, u32[]{:S(2)}, u32[]{:S(2)}) collective-permute-start(bf16[64,512]{1,0:T(8,128)(2,1)S(1)} %get-tuple-element.35), channel_id=1, source_target_pairs={{0,8},{1,9},{2,10},{3,11},{4,12},{5,13},{6,14},{7,15},{8,0},{9,1},... | collective-permute-start | bytes 196616 | tf_op jit(solution)/shard_map/ppermute | solution.py:403
  18.2 0.3 collective-permute-start.1
  18.5 1.6 %collective-permute-start = (bf16[64,2048]{1,0:T(8,128)(2,1)S(1)}, bf16[64,2048]{1,0:T(8,128)(2,1)S(1)}, u32[]{:S(2)}, u32[]{:S(2)}) collective-permute-start(bf16[64,2048]{1,0:T(8,128)(2,1)S(1)} %bitcast.19), channel_id=1, source_target_pairs={{0,4},{1,5},{2,6},{3,7},{4,0},{5,1},{6,2},{7,3},{8,12},{9,13},{10,... | collective-permute-start | bytes 786440 | tf_op jit(solution)/shard_map/ppermute | solution.py:403
  20.1 7.1 %collective-permute-done.4.w2 = bf16[2048,128]{1,0:T(8,128)(2,1)} collective-permute-done((bf16[2048,128]{1,0:T(8,128)(2,1)}, bf16[2048,128]{1,0:T(8,128)(2,1)}, u32[]{:S(2)}, u32[]{:S(2)}) %collective-permute-start.4) | collective-permute-done | bytes 524320 | tf_op jit(solution)/shard_map/ppermute | solution.py:400
  27.2 0.5 collective-permute-start.6
  27.7 5.2 %collective-permute-done.1.a2 = bf16[64,2048]{1,0:T(8,128)(2,1)} collective-permute-done((bf16[64,2048]{1,0:T(8,128)(2,1)S(1)}, bf16[64,2048]{1,0:T(8,128)(2,1)}, u32[]{:S(2)}, u32[]{:S(2)}) %collective-permute-start.1) | collective-permute-done | bytes 262176 | tf_op jit(solution)/shard_map/ppermute | solution.py:403
  32.9 0.7 copy-done.6
  33.5 0.3 collective-permute-start.3
  33.8 0.6 pad_maximum_fusion
  34.4 1.8 %collective-permute-start.8 = (bf16[64,512]{1,0:T(8,128)(2,1)}, bf16[64,512]{1,0:T(8,128)(2,1)S(1)}, u32[]{:S(2)}, u32[]{:S(2)}) collective-permute-start(bf16[64,512]{1,0:T(8,128)(2,1)} %pad_maximum_fusion), channel_id=1, source_target_pairs={{0,4},{1,5},{2,6},{3,7},{4,0},{5,1},{6,2},{7,3},{8,12},{9,13},{10,... | collective-permute-start | bytes 196616 | tf_op jit(solution)/shard_map/ppermute | solution.py:403
  36.2 0.2 weight_piece.3
  36.4 1.1 copy-done.3
  38.2 0.8 copy.12
  39.0 1.4 copy.13
  40.3 0.7 copy-done.10
  41.1 0.4 share.1
  41.5 1.0 collective-permute-done.3.a3
  42.5 0.9 copy-done.7
  43.4 3.0 %projection.1 = (bf16[128,512]{1,0:T(8,128)(2,1)S(1)}, bf16[128,512]{1,0:T(8,128)(2,1)S(1)}) custom-call(bf16[64,2048]{1,0:T(8,128)(2,1)S(1)} %bitcast.20, bf16[64,2048]{1,0:T(8,128)(2,1)S(1)} %copy-done.7, bf16[64,2048]{1,0:T(8,128)(2,1)} %collective-permute-done.1.a2, bf16[64,2048]{1,0:T(8,128)(2,1)} %collective-permute-done.3.a3, bf16[2048,128]{1,0:T(8,128)(2,1)} %w0.1, ...), custom_call_target="tpu_custom_call" | custom-call | flops 1 | bytes 1 | tf_op jit(solution)/shard_map/projection/pallas_call | solution.py:369
  46.4 1.7 %collective-permute-done.7.early = bf16[1024,768]{1,0:T(8,128)(2,1)} collective-permute-done((bf16[1024,768]{1,0:T(8,128)(2,1)}, bf16[1024,768]{1,0:T(8,128)(2,1)}, u32[]{:S(2)}, u32[]{:S(2)}) %collective-permute-start.7) | collective-permute-done | bytes 1572896 | tf_op jit(solution)/shard_map/ppermute | solution.py:381
  48.2 1.7 %collective-permute-start.9 = (bf16[128,512]{1,0:T(8,128)(2,1)S(1)}, bf16[128,512]{1,0:T(8,128)(2,1)S(1)}, u32[]{:S(2)}, u32[]{:S(2)}) collective-permute-start(bf16[128,512]{1,0:T(8,128)(2,1)S(1)} %get-tuple-element.41), channel_id=1, source_target_pairs={{0,16},{16,0},{1,17},{17,1},{2,18},{18,2},{3,19},{19,3},{4,20},{20... | collective-permute-start | bytes 393224 | tf_op jit(solution)/shard_map/ppermute | solution.py:381
  49.9 3.2 %collective-permute-done.9.arrived = bf16[128,512]{1,0:T(8,128)(2,1)S(1)} collective-permute-done((bf16[128,512]{1,0:T(8,128)(2,1)S(1)}, bf16[128,512]{1,0:T(8,128)(2,1)S(1)}, u32[]{:S(2)}, u32[]{:S(2)}) %collective-permute-start.9) | collective-permute-done | bytes 131104 | tf_op jit(solution)/shard_map/ppermute | solution.py:381
  53.2 1.7 %collective-permute-start.16 = (bf16[1024,768]{1,0:T(8,128)(2,1)S(1)}, bf16[1024,768]{1,0:T(8,128)(2,1)S(1)}, u32[]{:S(2)}, u32[]{:S(2)}) collective-permute-start(bf16[1024,768]{1,0:T(8,128)(2,1)S(1)} %copy-done.4), channel_id=1, source_target_pairs={{0,16},{16,0},{1,17},{17,1},{2,18},{18,2},{3,19},{19,3},{4,20},{20... | collective-permute-start | bytes 4718600 | tf_op jit(solution)/shard_map/ppermute | solution.py:381
  55.0 3.7 %collective-permute-start.12 = (bf16[144,512]{1,0:T(8,128)(2,1)S(1)}, bf16[144,512]{1,0:T(8,128)(2,1)S(1)}, u32[]{:S(2)}, u32[]{:S(2)}) collective-permute-start(bf16[144,512]{1,0:T(8,128)(2,1)S(1)} %stream.1.b0), channel_id=1, source_target_pairs={{0,12},{1,13},{2,14},{3,15},{4,0},{5,1},{6,2},{7,3},{8,4},{9,5},{1... | collective-permute-start | bytes 442376 | tf_op jit(solution)/shard_map/ppermute | solution.py:384
  58.6 1.0 collective-permute-start.10
  59.6 3.0 %collective-permute-done.12.b3 = bf16[144,512]{1,0:T(8,128)(2,1)S(1)} collective-permute-done((bf16[144,512]{1,0:T(8,128)(2,1)S(1)}, bf16[144,512]{1,0:T(8,128)(2,1)S(1)}, u32[]{:S(2)}, u32[]{:S(2)}) %collective-permute-start.12) | collective-permute-done | bytes 147488 | tf_op jit(solution)/shard_map/ppermute | solution.py:384
  62.6 7.2 %collective-permute-done.11.b2 = bf16[144,512]{1,0:T(8,128)(2,1)S(1)} collective-permute-done((bf16[144,512]{1,0:T(8,128)(2,1)S(1)}, bf16[144,512]{1,0:T(8,128)(2,1)S(1)}, u32[]{:S(2)}, u32[]{:S(2)}) %collective-permute-start.11) | collective-permute-done | bytes 147488 | tf_op jit(solution)/shard_map/ppermute | solution.py:384
  69.8 0.3 norm.1
  70.1 1.6 %collective-permute-start.13 = (bf16[128,2176]{1,0:T(8,128)(2,1)S(1)}, bf16[128,2176]{1,0:T(8,128)(2,1)S(1)}, u32[]{:S(2)}, u32[]{:S(2)}) collective-permute-start(bf16[128,2176]{1,0:T(8,128)(2,1)S(1)} %get-tuple-element.44.group), channel_id=1, source_target_pairs={{0,2},{1,3},{2,0},{3,1},{4,6},{5,7},{6,4},{7,5},{8,10},{9,11},{10,... | collective-permute-start | bytes 1671176 | tf_op jit(solution)/shard_map/ppermute | solution.py:400
  71.7 11.3 %collective-permute-done.13.group_x = bf16[128,2176]{1,0:T(8,128)(2,1)S(1)} collective-permute-done((bf16[128,2176]{1,0:T(8,128)(2,1)S(1)}, bf16[128,2176]{1,0:T(8,128)(2,1)S(1)}, u32[]{:S(2)}, u32[]{:S(2)}) %collective-permute-start.13) | collective-permute-done | bytes 557088 | tf_op jit(solution)/shard_map/ppermute | solution.py:400
  83.0 2.0 %collective-permute-done.14.group_cx = bf16[128,2176]{1,0:T(8,128)(2,1)S(1)} collective-permute-done((bf16[128,2176]{1,0:T(8,128)(2,1)S(1)}, bf16[128,2176]{1,0:T(8,128)(2,1)S(1)}, u32[]{:S(2)}, u32[]{:S(2)}) %collective-permute-start.14) | collective-permute-done | bytes 557088 | tf_op jit(solution)/shard_map/ppermute | solution.py:400
  84.9 4.8 %first_gate_up.1 = (bf16[512,384]{1,0:T(8,128)(2,1)S(1)}, f32[512,768]{1,0:T(8,128)S(1)}, bf16[512,1024]{1,0:T(8,128)(2,1)S(1)}, f32[512,128]{1,0:T(8,128)S(1)}) custom-call(bf16[128,2176]{1,0:T(8,128)(2,1)S(1)} %collective-permute-done.13.group_x, bf16[128,2176]{1,0:T(8,128)(2,1)S(1)} %collective-permute-done.14.group_cx, ...), custom_call_target="tpu_custom_call" | custom-call | flops 1 | bytes 1 | tf_op jit(solution)/shard_map/first_gate_up/pallas_call | solution.py:369
  89.8 1.3 last_gate_up.1
  91.1 0.1 copy-done.2
  91.2 1.0 down_both.1
  92.2 0.2 collective-permute-start.18
  92.4 0.5 collective-permute-start.21
  92.9 0.9 collective-permute-done.18
  93.8 1.6 %collective-permute-start.19 = (bf16[128,1024]{1,0:T(8,128)(2,1)S(1)}, bf16[128,1024]{1,0:T(8,128)(2,1)S(1)}, u32[]{:S(2)}, u32[]{:S(2)}) collective-permute-start(bf16[128,1024]{1,0:T(8,128)(2,1)S(1)} %add_convert_fusion.2), channel_id=1, source_target_pairs={{0,2},{1,3},{2,0},{3,1},{4,6},{5,7},{6,4},{7,5},{8,10},{9,11},{10,... | collective-permute-start | bytes 786440 | tf_op jit(solution)/shard_map/ppermute | solution.py:400
  95.4 8.4 %collective-permute-done.21.rows = bf16[256,768]{1,0:T(8,128)(2,1)S(1)} collective-permute-done((bf16[256,768]{1,0:T(8,128)(2,1)S(1)}, bf16[256,768]{1,0:T(8,128)(2,1)S(1)}, u32[]{:S(2)}, u32[]{:S(2)}) %collective-permute-start.21) | collective-permute-done | bytes 393248 | tf_op jit(solution)/shard_map/ppermute | solution.py:381
  103.8 0.6 down.2
  104.3 0.1 collective-permute-start.22
  104.4 0.5 collective-permute-start.17
  104.9 0.5 collective-permute-start.20
  105.4 0.5 collective-permute-done.22
  106.0 1.6 %collective-permute-start.23 = (bf16[128,1024]{1,0:T(8,128)(2,1)S(1)}, bf16[128,1024]{1,0:T(8,128)(2,1)S(1)}, u32[]{:S(2)}, u32[]{:S(2)}) collective-permute-start(bf16[128,1024]{1,0:T(8,128)(2,1)S(1)} %add_convert_fusion), channel_id=1, source_target_pairs={{0,2},{1,3},{2,0},{3,1},{4,6},{5,7},{6,4},{7,5},{8,10},{9,11},{10,... | collective-permute-start | bytes 786440 | tf_op jit(solution)/shard_map/ppermute | solution.py:400
  107.6 0.8 add_convert_fusion.1
  108.4 7.6 %collective-permute-done.20.rows = bf16[256,768]{1,0:T(8,128)(2,1)S(1)} collective-permute-done((bf16[256,768]{1,0:T(8,128)(2,1)S(1)}, bf16[256,768]{1,0:T(8,128)(2,1)S(1)}, u32[]{:S(2)}, u32[]{:S(2)}) %collective-permute-start.20) | collective-permute-done | bytes 393248 | tf_op jit(solution)/shard_map/ppermute | solution.py:381
  116.0 0.6 down.3
  116.7 1.5 %collective-permute-done.24.core = bf16[128,1024]{1,0:T(8,128)(2,1)S(1)} collective-permute-done((bf16[128,1024]{1,0:T(8,128)(2,1)S(1)}, bf16[128,1024]{1,0:T(8,128)(2,1)S(1)}, u32[]{:S(2)}, u32[]{:S(2)}) %collective-permute-start.24) | collective-permute-done | bytes 262176 | tf_op jit(solution)/shard_map/ppermute | solution.py:400
  118.2 0.1 pieces.1
  118.3 0.6 collective-permute-start.25
  118.9 1.8 %collective-permute-start.26 = (bf16[32,1024]{1,0:T(8,128)(2,1)S(1)}, bf16[32,1024]{1,0:T(8,128)(2,1)S(1)}, u32[]{:S(2)}, u32[]{:S(2)}) collective-permute-start(bf16[32,1024]{1,0:T(8,128)(2,1)S(1)} %get-tuple-element.63), channel_id=1, source_target_pairs={{0,20},{1,21},{2,22},{3,23},{4,24},{5,25},{6,26},{7,27},{8,28},{9,... | collective-permute-start | bytes 196616 | tf_op jit(solution)/shard_map/ppermute | solution.py:389
  120.7 2.0 %collective-permute-start.27 = (bf16[32,1024]{1,0:T(8,128)(2,1)S(1)}, bf16[32,1024]{1,0:T(8,128)(2,1)S(1)}, u32[]{:S(2)}, u32[]{:S(2)}) collective-permute-start(bf16[32,1024]{1,0:T(8,128)(2,1)S(1)} %get-tuple-element.64), channel_id=1, source_target_pairs={{0,24},{1,25},{2,26},{3,27},{4,28},{5,29},{6,30},{7,31},{8,16},{9,... | collective-permute-start | bytes 196616 | tf_op jit(solution)/shard_map/ppermute | solution.py:389
  122.7 3.7 %collective-permute-start.28 = (bf16[32,1024]{1,0:T(8,128)(2,1)S(1)}, bf16[32,1024]{1,0:T(8,128)(2,1)S(1)}, u32[]{:S(2)}, u32[]{:S(2)}) collective-permute-start(bf16[32,1024]{1,0:T(8,128)(2,1)S(1)} %get-tuple-element.65), channel_id=1, source_target_pairs={{0,28},{1,29},{2,30},{3,31},{4,16},{5,17},{6,18},{7,19},{8,20},{9,... | collective-permute-start | bytes 196616 | tf_op jit(solution)/shard_map/ppermute | solution.py:389
  126.5 1.5 %reduce-scatter.2.cloned.1.call-done = bf16[1,32,1024]{2,1,0:T(8,128)(2,1)} async-done(((bf16[4,32,1024]{2,1,0:T(8,128)(2,1)}), bf16[1,32,1024]{2,1,0:T(8,128)(2,1)}) %reduce-scatter.2.cloned.1.call-update) | async-done | bytes 65552 | tf_op jit(solution)/shard_map/reduce_scatter | solution.py:560
  128.0 1.3 collective-permute-done.27.o2
  129.3 0.8 copy-done.9
  130.1 0.8 closing.1
  (48 shorter events, 0.5 us)
Async XLA Ops:
  7.2 120.8 %reduce-scatter.2.cloned.1.call-start = ((), (), s32[]{:S(2)}) async-start(), calls=%async_computation.1 | async-start | bytes 327680 | tf_op jit(solution)/shard_map/reduce_scatter | solution.py:560
  7.2 1.9 %copy-start = (bf16[1,1024,1536]{2,1,0:T(8,128)(2,1)S(1)}, bf16[1,1024,1536]{2,1,0:T(8,128)(2,1)}, u32[]{:S(2)}) copy-start(bf16[1,1024,1536]{2,1,0:T(8,128)(2,1)} %param.17) | copy-start | bytes 9437188
  9.1 5.9 %copy-start.8 = (bf16[1,32,2048]{2,1,0:T(8,128)(2,1)S(1)}, bf16[1,32,2048]{2,1,0:T(8,128)(2,1)}, u32[]{:S(2)}) copy-start(bf16[1,32,2048]{2,1,0:T(8,128)(2,1)} %param.11) | copy-start | bytes 393220
  9.1 9.1 %copy-start.5 = (bf16[1,64,2048]{2,1,0:T(8,128)(2,1)S(1)}, bf16[1,64,2048]{2,1,0:T(8,128)(2,1)}, u32[]{:S(2)}) copy-start(bf16[1,64,2048]{2,1,0:T(8,128)(2,1)} %param.10) | copy-start | bytes 786436
  9.1 27.1 %copy-start.1 = (bf16[1,1024,1536]{2,1,0:T(8,128)(2,1)S(1)}, bf16[1,1024,1536]{2,1,0:T(8,128)(2,1)}, u32[]{:S(2)}) copy-start(bf16[1,1024,1536]{2,1,0:T(8,128)(2,1)} %param.17) | copy-start | bytes 9437188
  10.4 37.7 %collective-permute-start.7 = (bf16[1024,768]{1,0:T(8,128)(2,1)}, bf16[1024,768]{1,0:T(8,128)(2,1)}, u32[]{:S(2)}, u32[]{:S(2)}) collective-permute-start(bf16[1024,768]{1,0:T(8,128)(2,1)} %weight_piece.2), channel_id=1, source_target_pairs={{0,16},{16,0},{1,17},{17,1},{2,18},{18,2},{3,19},{19,3},{4,20},{20... | collective-permute-start | bytes 4718600 | tf_op jit(solution)/shard_map/ppermute | solution.py:381
  13.5 13.7 %collective-permute-start.4 = (bf16[2048,128]{1,0:T(8,128)(2,1)}, bf16[2048,128]{1,0:T(8,128)(2,1)}, u32[]{:S(2)}, u32[]{:S(2)}) collective-permute-start(bf16[2048,128]{1,0:T(8,128)(2,1)} %w0.1), channel_id=1, source_target_pairs={{0,2},{1,3},{2,0},{3,1},{4,6},{5,7},{6,4},{7,5},{8,10},{9,11},{10,... | collective-permute-start | bytes 1572872 | tf_op jit(solution)/shard_map/ppermute | solution.py:400
  15.0 0.6 copy-start.11
  15.6 11.6 %collective-permute-start.2 = (bf16[64,512]{1,0:T(8,128)(2,1)S(1)}, bf16[64,512]{1,0:T(8,128)(2,1)S(1)}, u32[]{:S(2)}, u32[]{:S(2)}) collective-permute-start(bf16[64,512]{1,0:T(8,128)(2,1)S(1)} %get-tuple-element.35), channel_id=1, source_target_pairs={{0,8},{1,9},{2,10},{3,11},{4,12},{5,13},{6,14},{7,15},{8,0},{9,1},... | collective-permute-start | bytes 196616 | tf_op jit(solution)/shard_map/ppermute | solution.py:403
  18.2 14.7 %collective-permute-start.1 = (bf16[64,2048]{1,0:T(8,128)(2,1)S(1)}, bf16[64,2048]{1,0:T(8,128)(2,1)}, u32[]{:S(2)}, u32[]{:S(2)}) collective-permute-start(bf16[64,2048]{1,0:T(8,128)(2,1)S(1)} %bitcast.18), channel_id=1, source_target_pairs={{0,8},{1,9},{2,10},{3,11},{4,12},{5,13},{6,14},{7,15},{8,0},{9,1},... | collective-permute-start | bytes 786440 | tf_op jit(solution)/shard_map/ppermute | solution.py:403
  18.5 14.3 %collective-permute-start = (bf16[64,2048]{1,0:T(8,128)(2,1)S(1)}, bf16[64,2048]{1,0:T(8,128)(2,1)S(1)}, u32[]{:S(2)}, u32[]{:S(2)}) collective-permute-start(bf16[64,2048]{1,0:T(8,128)(2,1)S(1)} %bitcast.19), channel_id=1, source_target_pairs={{0,4},{1,5},{2,6},{3,7},{4,0},{5,1},{6,2},{7,3},{8,12},{9,13},{10,... | collective-permute-start | bytes 786440 | tf_op jit(solution)/shard_map/ppermute | solution.py:403
  27.2 15.3 %collective-permute-start.5 = (bf16[2048,128]{1,0:T(8,128)(2,1)}, bf16[2048,128]{1,0:T(8,128)(2,1)}, u32[]{:S(2)}, u32[]{:S(2)}) collective-permute-start(bf16[2048,128]{1,0:T(8,128)(2,1)} %w0.1), channel_id=1, source_target_pairs={{0,1},{1,0},{2,3},{3,2},{4,5},{5,4},{6,7},{7,6},{8,9},{9,8},{10,11... | collective-permute-start | bytes 1572872 | tf_op jit(solution)/shard_map/ppermute | solution.py:400
  27.2 15.3 %collective-permute-start.6 = (bf16[2048,128]{1,0:T(8,128)(2,1)}, bf16[2048,128]{1,0:T(8,128)(2,1)}, u32[]{:S(2)}, u32[]{:S(2)}) collective-permute-start(bf16[2048,128]{1,0:T(8,128)(2,1)} %collective-permute-done.4.w2), channel_id=1, source_target_pairs={{0,1},{1,0},{2,3},{3,2},{4,5},{5,4},{6,7},{7,6},{8,9},{9,8},{10,11... | collective-permute-start | bytes 1572872 | tf_op jit(solution)/shard_map/ppermute | solution.py:400
  32.9 0.7 copy-start.6
  33.5 8.9 %collective-permute-start.3 = (bf16[64,2048]{1,0:T(8,128)(2,1)}, bf16[64,2048]{1,0:T(8,128)(2,1)}, u32[]{:S(2)}, u32[]{:S(2)}) collective-permute-start(bf16[64,2048]{1,0:T(8,128)(2,1)} %collective-permute-done.1.a2), channel_id=1, source_target_pairs={{0,4},{1,5},{2,6},{3,7},{4,0},{5,1},{6,2},{7,3},{8,12},{9,13},{10,... | collective-permute-start | bytes 786440 | tf_op jit(solution)/shard_map/ppermute | solution.py:403
  34.4 12.0 %collective-permute-start.8 = (bf16[64,512]{1,0:T(8,128)(2,1)}, bf16[64,512]{1,0:T(8,128)(2,1)S(1)}, u32[]{:S(2)}, u32[]{:S(2)}) collective-permute-start(bf16[64,512]{1,0:T(8,128)(2,1)} %pad_maximum_fusion), channel_id=1, source_target_pairs={{0,4},{1,5},{2,6},{3,7},{4,0},{5,1},{6,2},{7,3},{8,12},{9,13},{10,... | collective-permute-start | bytes 196616 | tf_op jit(solution)/shard_map/ppermute | solution.py:403
  36.4 1.2 copy-start.3
  40.3 0.7 copy-start.10
  41.1 13.8 %copy-start.12 = (bf16[32,512]{1,0:T(8,128)(2,1)S(1)}, bf16[32,512]{1,0:T(8,128)(2,1)}, u32[]{:S(2)}) copy-start(bf16[32,512]{1,0:T(8,128)(2,1)} %copy-done.11) | copy-start | bytes 98308
  41.1 28.8 %copy-start.13 = (f32[2048]{0:T(1024)S(1)}, f32[2048]{0:T(1024)}, u32[]{:S(2)}) copy-start(f32[2048]{0:T(1024)} %param.13) | copy-start | bytes 24580
  41.5 11.6 %copy-start.4 = (bf16[1024,768]{1,0:T(8,128)(2,1)S(1)}, bf16[1024,768]{1,0:T(8,128)(2,1)}, u32[]{:S(2)}) copy-start(bf16[1024,768]{1,0:T(8,128)(2,1)} %copy-done.3) | copy-start | bytes 4718596
  42.5 1.0 copy-start.7
  48.2 5.0 %collective-permute-start.9 = (bf16[128,512]{1,0:T(8,128)(2,1)S(1)}, bf16[128,512]{1,0:T(8,128)(2,1)S(1)}, u32[]{:S(2)}, u32[]{:S(2)}) collective-permute-start(bf16[128,512]{1,0:T(8,128)(2,1)S(1)} %get-tuple-element.41), channel_id=1, source_target_pairs={{0,16},{16,0},{1,17},{17,1},{2,18},{18,2},{3,19},{19,3},{4,20},{20... | collective-permute-start | bytes 393224 | tf_op jit(solution)/shard_map/ppermute | solution.py:381
  53.2 36.6 %collective-permute-start.16 = (bf16[1024,768]{1,0:T(8,128)(2,1)S(1)}, bf16[1024,768]{1,0:T(8,128)(2,1)S(1)}, u32[]{:S(2)}, u32[]{:S(2)}) collective-permute-start(bf16[1024,768]{1,0:T(8,128)(2,1)S(1)} %copy-done.4), channel_id=1, source_target_pairs={{0,16},{16,0},{1,17},{17,1},{2,18},{18,2},{3,19},{19,3},{4,20},{20... | collective-permute-start | bytes 4718600 | tf_op jit(solution)/shard_map/ppermute | solution.py:381
  55.0 7.7 %collective-permute-start.12 = (bf16[144,512]{1,0:T(8,128)(2,1)S(1)}, bf16[144,512]{1,0:T(8,128)(2,1)S(1)}, u32[]{:S(2)}, u32[]{:S(2)}) collective-permute-start(bf16[144,512]{1,0:T(8,128)(2,1)S(1)} %stream.1.b0), channel_id=1, source_target_pairs={{0,12},{1,13},{2,14},{3,15},{4,0},{5,1},{6,2},{7,3},{8,4},{9,5},{1... | collective-permute-start | bytes 442376 | tf_op jit(solution)/shard_map/ppermute | solution.py:384
  58.6 11.2 %collective-permute-start.11 = (bf16[144,512]{1,0:T(8,128)(2,1)S(1)}, bf16[144,512]{1,0:T(8,128)(2,1)S(1)}, u32[]{:S(2)}, u32[]{:S(2)}) collective-permute-start(bf16[144,512]{1,0:T(8,128)(2,1)S(1)} %stream.1.b0), channel_id=1, source_target_pairs={{0,8},{1,9},{2,10},{3,11},{4,12},{5,13},{6,14},{7,15},{8,0},{9,1},... | collective-permute-start | bytes 442376 | tf_op jit(solution)/shard_map/ppermute | solution.py:384
  58.6 11.2 %collective-permute-start.10 = (bf16[144,512]{1,0:T(8,128)(2,1)S(1)}, bf16[144,512]{1,0:T(8,128)(2,1)S(1)}, u32[]{:S(2)}, u32[]{:S(2)}) collective-permute-start(bf16[144,512]{1,0:T(8,128)(2,1)S(1)} %stream.1.b0), channel_id=1, source_target_pairs={{0,4},{1,5},{2,6},{3,7},{4,8},{5,9},{6,10},{7,11},{8,12},{9,13},{1... | collective-permute-start | bytes 442376 | tf_op jit(solution)/shard_map/ppermute | solution.py:384
  70.1 12.8 %collective-permute-start.13 = (bf16[128,2176]{1,0:T(8,128)(2,1)S(1)}, bf16[128,2176]{1,0:T(8,128)(2,1)S(1)}, u32[]{:S(2)}, u32[]{:S(2)}) collective-permute-start(bf16[128,2176]{1,0:T(8,128)(2,1)S(1)} %get-tuple-element.44.group), channel_id=1, source_target_pairs={{0,2},{1,3},{2,0},{3,1},{4,6},{5,7},{6,4},{7,5},{8,10},{9,11},{10,... | collective-permute-start | bytes 1671176 | tf_op jit(solution)/shard_map/ppermute | solution.py:400
  71.7 11.3 %collective-permute-start.15 = (bf16[128,2176]{1,0:T(8,128)(2,1)S(1)}, bf16[128,2176]{1,0:T(8,128)(2,1)S(1)}, u32[]{:S(2)}, u32[]{:S(2)}) collective-permute-start(bf16[128,2176]{1,0:T(8,128)(2,1)S(1)} %get-tuple-element.44.group), channel_id=1, source_target_pairs={{0,1},{1,0},{2,3},{3,2},{4,5},{5,4},{6,7},{7,6},{8,9},{9,8},{10,11... | collective-permute-start | bytes 1671176 | tf_op jit(solution)/shard_map/ppermute | solution.py:400
  83.0 2.0 %collective-permute-start.14 = (bf16[128,2176]{1,0:T(8,128)(2,1)S(1)}, bf16[128,2176]{1,0:T(8,128)(2,1)S(1)}, u32[]{:S(2)}, u32[]{:S(2)}) collective-permute-start(bf16[128,2176]{1,0:T(8,128)(2,1)S(1)} %collective-permute-done.13.group_x), channel_id=1, source_target_pairs={{0,1},{1,0},{2,3},{3,2},{4,5},{5,4},{6,7},{7,6},{8,9},{9,8},{10,11... | collective-permute-start | bytes 1671176 | tf_op jit(solution)/shard_map/ppermute | solution.py:400
  89.8 1.4 %copy-start.2 = (bf16[1,768,1024]{2,1,0:T(8,128)(2,1)S(1)}, bf16[1,768,1024]{2,1,0:T(8,128)(2,1)}, u32[]{:S(2)}) copy-start(bf16[1,768,1024]{2,1,0:T(8,128)(2,1)} %param.18) | copy-start | bytes 4718596
  92.2 1.6 %collective-permute-start.18 = (bf16[128,1024]{1,0:T(8,128)(2,1)S(1)}, bf16[128,1024]{1,0:T(8,128)(2,1)S(1)}, u32[]{:S(2)}, u32[]{:S(2)}) collective-permute-start(bf16[128,1024]{1,0:T(8,128)(2,1)S(1)} %get-tuple-element.55), channel_id=1, source_target_pairs={{0,1},{1,0},{2,3},{3,2},{4,5},{5,4},{6,7},{7,6},{8,9},{9,8},{10,11... | collective-permute-start | bytes 786440 | tf_op jit(solution)/shard_map/ppermute | solution.py:400
  92.4 11.4 %collective-permute-start.21 = (bf16[256,768]{1,0:T(8,128)(2,1)S(1)}, bf16[256,768]{1,0:T(8,128)(2,1)S(1)}, u32[]{:S(2)}, u32[]{:S(2)}) collective-permute-start(bf16[256,768]{1,0:T(8,128)(2,1)S(1)} %get-tuple-element.50.far), channel_id=1, source_target_pairs={{0,16},{16,0},{1,17},{17,1},{2,18},{18,2},{3,19},{19,3},{4,20},{20... | collective-permute-start | bytes 1179656 | tf_op jit(solution)/shard_map/ppermute | solution.py:381
  93.8 9.9 %collective-permute-start.19 = (bf16[128,1024]{1,0:T(8,128)(2,1)S(1)}, bf16[128,1024]{1,0:T(8,128)(2,1)S(1)}, u32[]{:S(2)}, u32[]{:S(2)}) collective-permute-start(bf16[128,1024]{1,0:T(8,128)(2,1)S(1)} %add_convert_fusion.2), channel_id=1, source_target_pairs={{0,2},{1,3},{2,0},{3,1},{4,6},{5,7},{6,4},{7,5},{8,10},{9,11},{10,... | collective-permute-start | bytes 786440 | tf_op jit(solution)/shard_map/ppermute | solution.py:400
  104.3 1.6 %collective-permute-start.22 = (bf16[128,1024]{1,0:T(8,128)(2,1)S(1)}, bf16[128,1024]{1,0:T(8,128)(2,1)S(1)}, u32[]{:S(2)}, u32[]{:S(2)}) collective-permute-start(bf16[128,1024]{1,0:T(8,128)(2,1)S(1)} %get-tuple-element.58), channel_id=1, source_target_pairs={{0,1},{1,0},{2,3},{3,2},{4,5},{5,4},{6,7},{7,6},{8,9},{9,8},{10,11... | collective-permute-start | bytes 786440 | tf_op jit(solution)/shard_map/ppermute | solution.py:400
  104.4 3.2 %collective-permute-start.17 = (bf16[128,1024]{1,0:T(8,128)(2,1)S(1)}, bf16[128,1024]{1,0:T(8,128)(2,1)S(1)}, u32[]{:S(2)}, u32[]{:S(2)}) collective-permute-start(bf16[128,1024]{1,0:T(8,128)(2,1)S(1)} %get-tuple-element.53), channel_id=1, source_target_pairs={{0,1},{1,0},{2,3},{3,2},{4,5},{5,4},{6,7},{7,6},{8,9},{9,8},{10,11... | collective-permute-start | bytes 786440 | tf_op jit(solution)/shard_map/ppermute | solution.py:400
  104.9 11.1 %collective-permute-start.20 = (bf16[256,768]{1,0:T(8,128)(2,1)S(1)}, bf16[256,768]{1,0:T(8,128)(2,1)S(1)}, u32[]{:S(2)}, u32[]{:S(2)}) collective-permute-start(bf16[256,768]{1,0:T(8,128)(2,1)S(1)} %get-tuple-element.51.near), channel_id=1, source_target_pairs={{0,16},{16,0},{1,17},{17,1},{2,18},{18,2},{3,19},{19,3},{4,20},{20... | collective-permute-start | bytes 1179656 | tf_op jit(solution)/shard_map/ppermute | solution.py:381
  106.0 10.0 %collective-permute-start.23 = (bf16[128,1024]{1,0:T(8,128)(2,1)S(1)}, bf16[128,1024]{1,0:T(8,128)(2,1)S(1)}, u32[]{:S(2)}, u32[]{:S(2)}) collective-permute-start(bf16[128,1024]{1,0:T(8,128)(2,1)S(1)} %add_convert_fusion), channel_id=1, source_target_pairs={{0,2},{1,3},{2,0},{3,1},{4,6},{5,7},{6,4},{7,5},{8,10},{9,11},{10,... | collective-permute-start | bytes 786440 | tf_op jit(solution)/shard_map/ppermute | solution.py:400
  108.4 20.9 %copy-start.14 = (f32[2048]{0:T(1024)S(1)}, f32[2048]{0:T(1024)}, u32[]{:S(2)}) copy-start(f32[2048]{0:T(1024)} %param.19) | copy-start | bytes 24580
  116.6 1.6 %collective-permute-start.24 = (bf16[128,1024]{1,0:T(8,128)(2,1)S(1)}, bf16[128,1024]{1,0:T(8,128)(2,1)S(1)}, u32[]{:S(2)}, u32[]{:S(2)}) collective-permute-start(bf16[128,1024]{1,0:T(8,128)(2,1)S(1)} %get-tuple-element.61), channel_id=1, source_target_pairs={{0,1},{1,0},{2,3},{3,2},{4,5},{5,4},{6,7},{7,6},{8,9},{9,8},{10,11... | collective-permute-start | bytes 786440 | tf_op jit(solution)/shard_map/ppermute | solution.py:400
  118.3 9.6 %collective-permute-start.25 = (bf16[32,1024]{1,0:T(8,128)(2,1)S(1)}, bf16[32,1024]{1,0:T(8,128)(2,1)S(1)}, u32[]{:S(2)}, u32[]{:S(2)}) collective-permute-start(bf16[32,1024]{1,0:T(8,128)(2,1)S(1)} %get-tuple-element.62), channel_id=1, source_target_pairs={{0,16},{1,17},{2,18},{3,19},{4,20},{5,21},{6,22},{7,23},{8,24},{9,... | collective-permute-start | bytes 196616 | tf_op jit(solution)/shard_map/ppermute | solution.py:389
  118.9 9.1 %collective-permute-start.26 = (bf16[32,1024]{1,0:T(8,128)(2,1)S(1)}, bf16[32,1024]{1,0:T(8,128)(2,1)S(1)}, u32[]{:S(2)}, u32[]{:S(2)}) collective-permute-start(bf16[32,1024]{1,0:T(8,128)(2,1)S(1)} %get-tuple-element.63), channel_id=1, source_target_pairs={{0,20},{1,21},{2,22},{3,23},{4,24},{5,25},{6,26},{7,27},{8,28},{9,... | collective-permute-start | bytes 196616 | tf_op jit(solution)/shard_map/ppermute | solution.py:389
  120.7 8.5 %collective-permute-start.27 = (bf16[32,1024]{1,0:T(8,128)(2,1)S(1)}, bf16[32,1024]{1,0:T(8,128)(2,1)S(1)}, u32[]{:S(2)}, u32[]{:S(2)}) collective-permute-start(bf16[32,1024]{1,0:T(8,128)(2,1)S(1)} %get-tuple-element.64), channel_id=1, source_target_pairs={{0,24},{1,25},{2,26},{3,27},{4,28},{5,29},{6,30},{7,31},{8,16},{9,... | collective-permute-start | bytes 196616 | tf_op jit(solution)/shard_map/ppermute | solution.py:389
  122.7 6.6 %collective-permute-start.28 = (bf16[32,1024]{1,0:T(8,128)(2,1)S(1)}, bf16[32,1024]{1,0:T(8,128)(2,1)S(1)}, u32[]{:S(2)}, u32[]{:S(2)}) collective-permute-start(bf16[32,1024]{1,0:T(8,128)(2,1)S(1)} %get-tuple-element.65), channel_id=1, source_target_pairs={{0,28},{1,29},{2,30},{3,31},{4,16},{5,17},{6,18},{7,19},{8,20},{9,... | collective-permute-start | bytes 196616 | tf_op jit(solution)/shard_map/ppermute | solution.py:389
  129.3 0.8 copy-start.9
Sparse Core Ops, SparseCore 0:
  108.5 19.3 reduce-scatter.1

commit v7 on v6

--- a/solution.py
+++ b/solution.py
@@ -219,11 +219,11 @@
     block_ref[count:, :] = share[...]
 
 
-def piece_kernel(at, weights, out, semaphores):
+def piece_kernel(starts, weights, out, semaphores):
     width = out.shape[1] // 2
     copies = [
         pltpu.make_async_copy(
-            weights.at[:, pl.ds((2 * i + at) * width, width)],
+            weights.at[:, pl.ds(starts[i], width)],
             out.at[:, pl.ds(i * width, width)],
             semaphores.at[i],
         )
@@ -292,48 +292,65 @@
     part_ref[:, cut : 2 * cut] = dot(mine, own[:, 3 * cut : 4 * cut])
 
 
-def last_gate_kernel(first, part, other, share, late, far_ref, near_ref):
+def last_gate_kernel(first, part, other, share, *refs):
+    *late, far_ref, near_ref = refs
     cut = first.shape[1]
-    gate = part[:, 0:cut] + dot(other[...], late[:, 0:cut])
-    up = part[:, cut : 2 * cut] + dot(other[...], late[:, cut : 2 * cut])
-    value = swiglu(gate, up, share[:, 0:1])
     half = far_ref.shape[0]
     far_ref[:, 0:cut] = first[0:half, :]
     near_ref[:, 0:cut] = first[half:, :]
-    far_ref[:, cut : 2 * cut] = value[:half]
-    near_ref[:, cut : 2 * cut] = value[half:]
+    at = 0
+    for piece in late:
+        size = piece.shape[1] // 2
+        gate = part[:, at : at + size] + dot(other[...], piece[:, 0:size])
+        up = part[:, cut + at : cut + at + size] + dot(other[...], piece[:, size : 2 * size])
+        value = swiglu(gate, up, share[:, 0:1])
+        cols = slice(cut + at, cut + at + size)
+        far_ref[:, cols] = value[:half]
+        near_ref[:, cols] = value[half:]
+        at += size
 
 
 def column_chunks(wd):
     return [slice(at, at + 256) for at in range(0, wd.shape[1], 256)]
 
 
-def down_both_kernel(far, near, wd, keep_far, keep_near, send_far, send_near):
-    down_kernel(far, wd, keep_far, send_far)
-    down_kernel(near, wd, keep_near, send_near)
-
-
-def down_kernel(rows, wd, keep_ref, send_ref):
-    count = keep_ref.shape[0]
-    for cols in column_chunks(wd):
-        value = dot(rows[...], wd[:, cols]).astype(BF16)
-        keep_ref[:, cols] = value[:count]
-        send_ref[:, cols] = value[count:]
-
-
-def pieces_kernel(keep, core, far, p0, p1, p2, p3):
+def down_both_kernel(far, near, wd, keep_far, keep_near, far_a, far_b, near_a, near_b):
+    down_kernel(far, wd, keep_far, far_a, far_b)
+    down_kernel(near, wd, keep_near, near_a, near_b)
+
+
+def down_kernel(rows, wd, keep_ref, send_a, send_b):
+    count, side = send_a.shape
+    for at in range(0, wd.shape[1], 256):
+        value = dot(rows[...], wd[:, at : at + 256]).astype(BF16)
+        keep_ref[:, at : at + 256] = value[:count]
+        send = send_a if at < side else send_b
+        send[:, at % side : at % side + 256] = value[count:]
+
+
+def fold_kernel(keep, core_a, core_b, out):
+    side = core_a.shape[1]
+    for i, core in enumerate((core_a, core_b)):
+        cols = slice(i * side, (i + 1) * side)
+        out[:, cols] = (keep[:, cols].astype(F32) + core[...].astype(F32)).astype(BF16)
+
+
+def pieces_kernel(keep, core_a, core_b, far, p0, p1, p2, p3):
     expert, outer, inner, dp = seat()
     small = p0.shape[0]
     for s, p in enumerate((p0, p1, p2, p3)):
         rows = aligned((outer + s) & 3, small)
-        total = keep[rows, :].astype(F32) + core[rows, :].astype(F32)
-        p[...] = (total + far[rows, :].astype(F32)).astype(BF16)
-
-
-def tail_kernel(own, m0, o0, o1, o2, o3, gain, stream_ref, normed_ref):
+        side = core_a.shape[1]
+        for i, core in enumerate((core_a, core_b)):
+            cols = slice(i * side, (i + 1) * side)
+            total = keep[rows, cols].astype(F32) + core[rows, :].astype(F32)
+            p[:, cols] = (total + far[rows, cols].astype(F32)).astype(BF16)
+
+
+def tail_kernel(own, m0, m1, m2, m3, o0, o1, o2, o3, gain, stream_ref, normed_ref):
     expert, outer, inner, dp = seat()
     half = m0.shape[1]
-    for at, pieces in ((dp, (m0,)), (1 - dp, (o0, o1, o2, o3))):
+    for at, pieces in ((dp, (m0, m1, m2, m3)), (1 - dp, (o0, o1, o2, o3))):
         cols = aligned(at, half)
         mixture = pieces[0][...].astype(F32)
         for piece in pieces[1:]:
@@ -405,11 +422,11 @@
     def after(x, *results):
         return lax.optimization_barrier((x, *results))[0]
 
-    def weight_piece(i):
+    def weight_piece(first, size):
         return pl.pallas_call(
-            functools.partial(piece_kernel, i),
-            out_shape=shape_of(half_width, hidden),
-            in_specs=[pl.BlockSpec(memory_space=pl.ANY)],
+            functools.partial(piece_kernel, (first, hidden + first)),
+            out_shape=shape_of(half_width, 2 * size),
+            in_specs=[pl.BlockSpec(memory_space=pltpu.HBM)],
             out_specs=vmem,
             scratch_shapes=[pltpu.SemaphoreType.DMA((2,))],
             compiler_params=kernel_params(8),
@@ -432,12 +449,16 @@
         first=smem,
     )
     cut_width = hidden // 2
-    early_piece, late_piece = (weight_piece(i) for i in range(2))
+    early_piece = weight_piece(0, cut_width)
+    late_sizes = (cut_width * 384 // 384,)
+    late_pieces = [
+        weight_piece(cut_width + sum(late_sizes[:i]), size) for i, size in enumerate(late_sizes)
+    ]
     gate_up_early = swap_dp(early_piece)
     a = [attn[0], swap_outer(attn[0], 1), swap_outer(attn[0], 2)]
     w_x = swap_inner(w_out, 2)
     r_2 = swap_outer(r_23, 2)
-    a.append(swap_outer(after(a[2], a[1], r_2), 1))
+    a.append(swap_outer(after(a[2], a[1]), 1))
     w_c = swap_inner(after(w_out, w_x), 1)
     w_cx = swap_inner(w_x, 1)
     r_13 = swap_outer(jnp.concatenate([r_1, r_2[rows_here:]], axis=0), 1)
@@ -458,8 +479,8 @@
             pltpu.VMEM((8 * rows_here, quarter), BF16),
         ),
     )
-    arrived = swap_dp(after(send, gate_up_early, late_piece, r_13, share))
-    gate_up_late = swap_dp(after(late_piece, arrived))
+    arrived = swap_dp(after(send, gate_up_early, r_13, share, *late_pieces))
+    gate_up_late = [swap_dp(after(piece, arrived)) for piece in late_pieces]
     (block,) = call(
         stream_kernel,
         "stream",
@@ -473,19 +494,14 @@
         share,
     )
 
-    group, stream_own = call(
-        norm_kernel,
-        "norm",
-        8,
-        (
-            shape_of(4 * rows_here, model_width + 128),
-            shape_of(rows_here, model_width),
-        ),
-        block,
-        *(shift_outer(block, s) for s in (1, 2, 3)),
-        gain_post[None],
-    )
-    group_x = swap_inner(group, 2)
+    def norm(b0, b1, b2, b3):
+        outs = (shape_of(4 * rows_here, model_width + 128), shape_of(rows_here, model_width))
+        return call(norm_kernel, "norm", 8, outs, b0, b1, b2, b3, gain_post[None])
+
+    blocks = [block] + [shift_outer(block, s) for s in (1, 2, 3)]
+    group, stream_own = norm(*blocks)
+    blocks_x = [swap_inner(b, 2) for b in blocks]
+    group_x, unused = norm(*blocks_x)
     group_c = swap_inner(group, 1)
     group_cx = swap_inner(group_x, 1)
 
@@ -519,20 +535,21 @@
         part,
         other_rows,
         share_rows,
-        gate_up_late,
+        *gate_up_late,
     )
     far_other = swap_dp(inner_far)
     near_other = swap_dp(inner_near)
 
     count = row_total // 4
     quarter_out = shape_of(count, half_width)
+    half_out = shape_of(count, half_width // 2)
 
     def down(rows):
         return call(
             down_kernel,
             "down",
             12,
-            (quarter_out, quarter_out),
+            (quarter_out, half_out, half_out),
             rows,
             w_down[0],
         )
@@ -540,29 +557,34 @@
     def add(x, y):
         return (x.astype(F32) + y.astype(F32)).astype(BF16)
 
-    def pieces(keep, core, far):
+    def swap_cores(halves):
+        return [swap_inner(half, 1) for half in halves]
+
+    def fold(keep, halves):
+        return call(fold_kernel, "fold", 4, (quarter_out,), keep, *halves)[0]
+
+    def pieces(*args):
         out = shape_of(rows_here, half_width)
-        return call(pieces_kernel, "pieces", 4, (out, out, out, out), keep, core, far)
-
-    keep_far, keep_near, send_far, send_near = call(
+        return call(pieces_kernel, "pieces", 4, (out, out, out, out), *args)
+
+    keep_far, keep_near, *send = call(
         down_both_kernel,
         "down_both",
         16,
-        (quarter_out, quarter_out, quarter_out, quarter_out),
+        (quarter_out, quarter_out, half_out, half_out, half_out, half_out),
         inner_far,
         inner_near,
         w_down[0],
     )
-    far = swap_inner(add(keep_far, swap_inner(send_far, 1)), 2)
+    far = swap_inner(fold(keep_far, swap_cores(send[:2])), 2)
     ready = far
-    outer_groups = [[i + 4 * z for z in range(4)] for i in range(4)]
-    total = add(add(keep_near, swap_inner(send_near, 1)), far).reshape(4, rows_here, half_width)
-    mine = [lax.psum_scatter(total, "expert", scatter_dimension=0, axis_index_groups=outer_groups)]
-
-    keep_far, send_far = down(after(far_other, ready))
-    far = swap_inner(add(keep_far, swap_inner(send_far, 1)), 2)
-    keep_near, send_near = down(after(near_other, far))
-    cut = pieces(keep_near, swap_inner(send_near, 1), far)
+    cut = pieces(keep_near, *swap_cores(send[2:]), far)
+    mine = [cut[0]] + [shift_outer(cut[s], s) for s in (1, 2, 3)]
+
+    keep_far, *send = down(after(far_other, ready))
+    far = swap_inner(fold(keep_far, swap_cores(send)), 2)
+    keep_near, *send = down(after(near_other, *mine[1:]))
+    cut = pieces(keep_near, *swap_cores(send), far)
     others = [cross_outer(cut[s], s) for s in range(4)]
 
     out = shape_of(rows_here, model_width)

time: 138 us -> 126 us (0.913)
  between operations: 14.9 us -> 1.54 us
  starting transfers between devices: 34.4 us -> 39.8 us
  waiting for transfers between devices: 63.3 us -> 59.2 us
    ppermute x12 -> x19, waiting for transfers between devices: 23.2 us -> 16.6 us  [swap_inner(): return lax.ppermute(x, 'expert', [(i, i ^ j) for i in range(expert_count)])]
    ppermute x5, starting transfers between devices: 6.53 us -> 12.3 us  [swap_outer(): lax.ppermute(x, 'expert', [(i, i ^ 4 * s) for i in range(expert_count)])]
    ppermute x4, waiting for transfers between devices: 1.35 us -> 4.43 us  [cross_outer(): lax.ppermute(x, ('dp', 'expert'), [(d * expert_count + i, (1 - d) * exper...]
    ppermute x12 -> x19, starting transfers between devices: 7.52 us -> 9.85 us  [swap_inner(): return lax.ppermute(x, 'expert', [(i, i ^ j) for i in range(expert_count)])]
    ppermute x4, starting transfers between devices: 8.13 us -> 6.06 us  [cross_outer(): lax.ppermute(x, ('dp', 'expert'), [(d * expert_count + i, (1 - d) * exper...]
    ppermute x5, starting transfers between devices: 7.53 us -> 5.63 us  [swap_dp(): return lax.ppermute(x, 'dp', [(0, 1), (1, 0)])]
    reduce_scatter x1 -> x0, waiting for transfers between devices: 1.49 us -> none  [body_paired(): lax.psum_scatter(total, 'expert', scatter_dimension=0, axis_index_groups=...]
    ppermute x3 -> x6, waiting for transfers between devices: 10.2 us -> 11.7 us  [shift_outer(): lax.ppermute(x, 'expert', [(i, (i + 4 * s) % expert_count) for i in range...]
  transfers between devices with their start and end apart: 30 -> 39, of which waited for: 17 -> 26; matrix products, arithmetic and copies ran while one was open for 3% -> 2% of each run, Pallas kernels for 7% -> 9%
where the time goes in v7:
time: 126 us; the launch traced here: 125 us
  waiting for transfers between devices  59.2 us (47%)
  starting transfers between devices  39.8 us (32%)
  Pallas kernels  15.7 us (12%)
  local copies, waits for them, and re-layouts  8.32 us (7%)
  between operations  1.54 us (1%)
    ppermute x5, waiting for transfers between devices, swap_dp(): return lax.ppermute(x, 'dp', [(0, 1), (1, 0)])  21.7 us
    ppermute x19, waiting for transfers between devices, swap_inner(): return lax.ppermute(x, 'expert', [(i, i ^ j) for i in range(expert_count)])  16.6 us
    pallas_call x16, Pallas kernels, call(): pl.pallas_call(kernel, out_shape=outs, in_specs=[first] + [vmem] * (len(a...  14.2 us
    ppermute x5, starting transfers between devices, swap_outer(): lax.ppermute(x, 'expert', [(i, i ^ 4 * s) for i in range(expert_count)])  12.3 us
    ppermute x6, waiting for transfers between devices, shift_outer(): lax.ppermute(x, 'expert', [(i, (i + 4 * s) % expert_count) for i in range...  11.7 us
    ppermute x19, starting transfers between devices, swap_inner(): return lax.ppermute(x, 'expert', [(i, i ^ j) for i in range(expert_count)])  9.85 us
    unnamed x30, local copies, waits for them, and re-layouts  8.32 us
    ppermute x4, starting transfers between devices, cross_outer(): lax.ppermute(x, ('dp', 'expert'), [(d * expert_count + i, (1 - d) * exper...  6.06 us
  transfers between devices with their start and end apart: 39, of which 26 were waited for; matrix products, arithmetic and copies ran while one was open for 2% of the time, Pallas kernels for 9%

profile of v7, /device:TPU:0, one launch (start us, length us, event | category | flops | bytes accessed | tf_op | source)
XLA Modules:
  0.0 125.2 jit_solution(3889382081165485143)
XLA Ops:
  0.6 1.9 %copy-done = bf16[1,1024,1536]{2,1,0:T(8,128)(2,1)S(1)} copy-done((bf16[1,1024,1536]{2,1,0:T(8,128)(2,1)S(1)}, bf16[1,1024,1536]{2,1,0:T(8,128)(2,1)}, u32[]{:S(2)}) %copy-start) | copy-done | bytes 3145752
  2.5 1.3 %weight_piece.2 = bf16[1024,768]{1,0:T(8,128)(2,1)} custom-call(bf16[1024,1536]{1,0:T(8,128)(2,1)S(1)} %bitcast.10), custom_call_target="tpu_custom_call" | custom-call | flops 1 | bytes 1 | tf_op jit(solution)/shard_map/weight_piece/pallas_call | solution.py:426
  3.9 3.0 %collective-permute-start.6 = (bf16[1024,768]{1,0:T(8,128)(2,1)}, bf16[1024,768]{1,0:T(8,128)(2,1)}, u32[]{:S(2)}, u32[]{:S(2)}) collective-permute-start(bf16[1024,768]{1,0:T(8,128)(2,1)} %weight_piece.2), channel_id=1, source_target_pairs={{0,16},{16,0},{1,17},{17,1},{2,18},{18,2},{3,19},{19,3},{4,20},{20... | collective-permute-start | bytes 4718600 | tf_op jit(solution)/shard_map/ppermute | solution.py:398
  6.9 1.5 %collective-permute-start.3 = (bf16[2048,128]{1,0:T(8,128)(2,1)}, bf16[2048,128]{1,0:T(8,128)(2,1)}, u32[]{:S(2)}, u32[]{:S(2)}) collective-permute-start(bf16[2048,128]{1,0:T(8,128)(2,1)} %w0.1), channel_id=1, source_target_pairs={{0,2},{1,3},{2,0},{3,1},{4,6},{5,7},{6,4},{7,5},{8,10},{9,11},{10,... | collective-permute-start | bytes 1572872 | tf_op jit(solution)/shard_map/ppermute | solution.py:417
  8.4 2.6 %collective-permute-start.1 = (bf16[64,2048]{1,0:T(8,128)(2,1)S(1)}, bf16[64,2048]{1,0:T(8,128)(2,1)}, u32[]{:S(2)}, u32[]{:S(2)}) collective-permute-start(bf16[64,2048]{1,0:T(8,128)(2,1)S(1)} %bitcast.16), channel_id=1, source_target_pairs={{0,8},{1,9},{2,10},{3,11},{4,12},{5,13},{6,14},{7,15},{8,0},{9,1},... | collective-permute-start | bytes 786440 | tf_op jit(solution)/shard_map/ppermute | solution.py:420
  11.0 1.6 %collective-permute-start = (bf16[64,2048]{1,0:T(8,128)(2,1)S(1)}, bf16[64,2048]{1,0:T(8,128)(2,1)S(1)}, u32[]{:S(2)}, u32[]{:S(2)}) collective-permute-start(bf16[64,2048]{1,0:T(8,128)(2,1)S(1)} %bitcast.17), channel_id=1, source_target_pairs={{0,4},{1,5},{2,6},{3,7},{4,0},{5,1},{6,2},{7,3},{8,12},{9,13},{10,... | collective-permute-start | bytes 786440 | tf_op jit(solution)/shard_map/ppermute | solution.py:420
  12.6 8.0 %collective-permute-done.3.w2 = bf16[2048,128]{1,0:T(8,128)(2,1)} collective-permute-done((bf16[2048,128]{1,0:T(8,128)(2,1)}, bf16[2048,128]{1,0:T(8,128)(2,1)}, u32[]{:S(2)}, u32[]{:S(2)}) %collective-permute-start.3) | collective-permute-done | bytes 524320 | tf_op jit(solution)/shard_map/ppermute | solution.py:417
  20.6 0.5 collective-permute-start.5
  21.1 1.5 %collective-permute-done.1.a2 = bf16[64,2048]{1,0:T(8,128)(2,1)} collective-permute-done((bf16[64,2048]{1,0:T(8,128)(2,1)S(1)}, bf16[64,2048]{1,0:T(8,128)(2,1)}, u32[]{:S(2)}, u32[]{:S(2)}) %collective-permute-start.1) | collective-permute-done | bytes 262176 | tf_op jit(solution)/shard_map/ppermute | solution.py:420
  22.7 0.7 copy-done.6
  23.4 1.4 %collective-permute-start.2 = (bf16[64,2048]{1,0:T(8,128)(2,1)}, bf16[64,2048]{1,0:T(8,128)(2,1)}, u32[]{:S(2)}, u32[]{:S(2)}) collective-permute-start(bf16[64,2048]{1,0:T(8,128)(2,1)} %collective-permute-done.1.a2), channel_id=1, source_target_pairs={{0,4},{1,5},{2,6},{3,7},{4,0},{5,1},{6,2},{7,3},{8,12},{9,13},{10,... | collective-permute-start | bytes 786440 | tf_op jit(solution)/shard_map/ppermute | solution.py:420
  24.9 0.6 copy-done.11
  25.5 2.4 %collective-permute-start.7 = (bf16[64,512]{1,0:T(8,128)(2,1)S(1)}, bf16[64,512]{1,0:T(8,128)(2,1)S(1)}, u32[]{:S(2)}, u32[]{:S(2)}) collective-permute-start(bf16[64,512]{1,0:T(8,128)(2,1)S(1)} %get-tuple-element.49), channel_id=1, source_target_pairs={{0,8},{1,9},{2,10},{3,11},{4,12},{5,13},{6,14},{7,15},{8,0},{9,1},... | collective-permute-start | bytes 196616 | tf_op jit(solution)/shard_map/ppermute | solution.py:420
  27.9 3.2 %collective-permute-done.7.r2 = bf16[64,512]{1,0:T(8,128)(2,1)S(1)} collective-permute-done((bf16[64,512]{1,0:T(8,128)(2,1)S(1)}, bf16[64,512]{1,0:T(8,128)(2,1)S(1)}, u32[]{:S(2)}, u32[]{:S(2)}) %collective-permute-start.7) | collective-permute-done | bytes 65568 | tf_op jit(solution)/shard_map/ppermute | solution.py:420
  31.1 0.6 pad_maximum_fusion
  31.8 4.2 %collective-permute-start.8 = (bf16[64,512]{1,0:T(8,128)(2,1)}, bf16[64,512]{1,0:T(8,128)(2,1)S(1)}, u32[]{:S(2)}, u32[]{:S(2)}) collective-permute-start(bf16[64,512]{1,0:T(8,128)(2,1)} %pad_maximum_fusion), channel_id=1, source_target_pairs={{0,4},{1,5},{2,6},{3,7},{4,0},{5,1},{6,2},{7,3},{8,12},{9,13},{10,... | collective-permute-start | bytes 196616 | tf_op jit(solution)/shard_map/ppermute | solution.py:420
  36.2 1.2 copy-done.3
  38.0 0.8 copy.12
  38.8 1.4 %copy.13 = f32[1,32,8]{2,1,0:T(8,128)} copy(f32[1,32,8]{1,2,0:T(8,128)} %param.15) | data formatting | bytes 2048 | tf_op args[5]
  40.1 0.7 copy-done.9
  40.8 0.4 share.1
  41.3 1.1 copy-done.7
  42.4 3.0 %projection.1 = (bf16[128,512]{1,0:T(8,128)(2,1)S(1)}, bf16[128,512]{1,0:T(8,128)(2,1)S(1)}) custom-call(bf16[64,2048]{1,0:T(8,128)(2,1)S(1)} %bitcast.18, bf16[64,2048]{1,0:T(8,128)(2,1)S(1)} %copy-done.7, bf16[64,2048]{1,0:T(8,128)(2,1)} %collective-permute-done.1.a2, bf16[64,2048]{1,0:T(8,128)(2,1)} %collective-permute-done.2.a3, bf16[2048,128]{1,0:T(8,128)(2,1)} %w0.1, ...), custom_call_target="tpu_custom_call" | custom-call | flops 1 | bytes 1 | tf_op jit(solution)/shard_map/projection/pallas_call | solution.py:386
  45.4 0.6 collective-permute-start.9
  46.0 4.5 %collective-permute-done.9.arrived = bf16[128,512]{1,0:T(8,128)(2,1)S(1)} collective-permute-done((bf16[128,512]{1,0:T(8,128)(2,1)S(1)}, bf16[128,512]{1,0:T(8,128)(2,1)S(1)}, u32[]{:S(2)}, u32[]{:S(2)}) %collective-permute-start.9) | collective-permute-done | bytes 131104 | tf_op jit(solution)/shard_map/ppermute | solution.py:398
  50.5 0.5 collective-permute-start.19
  51.0 1.0 collective-permute-start.12
  52.0 0.5 collective-permute-start.11
  52.6 0.6 collective-permute-start.10
  53.1 1.4 %collective-permute-start.13 = (bf16[144,512]{1,0:T(8,128)(2,1)S(1)}, bf16[144,512]{1,0:T(8,128)(2,1)S(1)}, u32[]{:S(2)}, u32[]{:S(2)}) collective-permute-start(bf16[144,512]{1,0:T(8,128)(2,1)S(1)} %stream.1.b0), channel_id=1, source_target_pairs={{0,2},{1,3},{2,0},{3,1},{4,6},{5,7},{6,4},{7,5},{8,10},{9,11},{10,... | collective-permute-start | bytes 442376 | tf_op jit(solution)/shard_map/ppermute | solution.py:417
  54.5 2.7 %collective-permute-done.12.b3 = bf16[144,512]{1,0:T(8,128)(2,1)S(1)} collective-permute-done((bf16[144,512]{1,0:T(8,128)(2,1)S(1)}, bf16[144,512]{1,0:T(8,128)(2,1)S(1)}, u32[]{:S(2)}, u32[]{:S(2)}) %collective-permute-start.12) | collective-permute-done | bytes 147488 | tf_op jit(solution)/shard_map/ppermute | solution.py:401
  57.3 1.8 %collective-permute-start.16 = (bf16[144,512]{1,0:T(8,128)(2,1)S(1)}, bf16[144,512]{1,0:T(8,128)(2,1)S(1)}, u32[]{:S(2)}, u32[]{:S(2)}) collective-permute-start(bf16[144,512]{1,0:T(8,128)(2,1)S(1)} %collective-permute-done.12.b3), channel_id=1, source_target_pairs={{0,2},{1,3},{2,0},{3,1},{4,6},{5,7},{6,4},{7,5},{8,10},{9,11},{10,... | collective-permute-start | bytes 442376 | tf_op jit(solution)/shard_map/ppermute | solution.py:417
  59.1 4.8 %collective-permute-done.11.b2 = bf16[144,512]{1,0:T(8,128)(2,1)S(1)} collective-permute-done((bf16[144,512]{1,0:T(8,128)(2,1)S(1)}, bf16[144,512]{1,0:T(8,128)(2,1)S(1)}, u32[]{:S(2)}, u32[]{:S(2)}) %collective-permute-start.11) | collective-permute-done | bytes 147488 | tf_op jit(solution)/shard_map/ppermute | solution.py:401
  63.8 0.9 collective-permute-start.15
  64.7 1.2 collective-permute-start.14
  66.3 2.7 %collective-permute-done.15.b2 = bf16[144,512]{1,0:T(8,128)(2,1)S(1)} collective-permute-done((bf16[144,512]{1,0:T(8,128)(2,1)S(1)}, bf16[144,512]{1,0:T(8,128)(2,1)S(1)}, u32[]{:S(2)}, u32[]{:S(2)}) %collective-permute-start.15) | collective-permute-done | bytes 147488 | tf_op jit(solution)/shard_map/ppermute | solution.py:417
  69.0 1.6 %collective-permute-done.14.b1 = bf16[144,512]{1,0:T(8,128)(2,1)S(1)} collective-permute-done((bf16[144,512]{1,0:T(8,128)(2,1)S(1)}, bf16[144,512]{1,0:T(8,128)(2,1)S(1)}, u32[]{:S(2)}, u32[]{:S(2)}) %collective-permute-start.14) | collective-permute-done | bytes 147488 | tf_op jit(solution)/shard_map/ppermute | solution.py:417
  70.6 0.8 norm.3
  71.4 2.0 %collective-permute-done.17.group_cx = bf16[128,2176]{1,0:T(8,128)(2,1)S(1)} collective-permute-done((bf16[128,2176]{1,0:T(8,128)(2,1)S(1)}, bf16[128,2176]{1,0:T(8,128)(2,1)S(1)}, u32[]{:S(2)}, u32[]{:S(2)}) %collective-permute-start.17) | collective-permute-done | bytes 557088 | tf_op jit(solution)/shard_map/ppermute | solution.py:417
  73.3 4.8 %first_gate_up.1 = (bf16[512,384]{1,0:T(8,128)(2,1)S(1)}, f32[512,768]{1,0:T(8,128)S(1)}, bf16[512,1024]{1,0:T(8,128)(2,1)S(1)}, f32[512,128]{1,0:T(8,128)S(1)}) custom-call(bf16[128,2176]{1,0:T(8,128)(2,1)S(1)} %get-tuple-element.53.group_x, bf16[128,2176]{1,0:T(8,128)(2,1)S(1)} %collective-permute-done.17.group_cx, ...), custom_call_target="tpu_custom_call" | custom-call | flops 1 | bytes 1 | tf_op jit(solution)/shard_map/first_gate_up/pallas_call | solution.py:386
  78.2 6.7 %collective-permute-done.19.refs_0_ = bf16[1024,768]{1,0:T(8,128)(2,1)S(1)} collective-permute-done((bf16[1024,768]{1,0:T(8,128)(2,1)S(1)}, bf16[1024,768]{1,0:T(8,128)(2,1)S(1)}, u32[]{:S(2)}, u32[]{:S(2)}) %collective-permute-start.19) | collective-permute-done | bytes 1572896 | tf_op jit(solution)/shard_map/ppermute | solution.py:398
  84.8 1.4 %last_gate_up.1 = (bf16[256,768]{1,0:T(8,128)(2,1)S(1)}, bf16[256,768]{1,0:T(8,128)(2,1)S(1)}) custom-call(bf16[512,384]{1,0:T(8,128)(2,1)S(1)} %get-tuple-element.55.first, f32[512,768]{1,0:T(8,128)S(1)} %get-tuple-element.56.part, bf16[512,1024]{1,0:T(8,128)(2,1)S(1)} %get-tuple-element.57.other, f32[512,128]{1,0:T(8,128)S(1)} %get-tuple-element.58.share, ...), custom_call_target="tpu_custom_call" | custom-call | flops 1 | bytes 1 | tf_op jit(solution)/shard_map/last_gate_up/pallas_call | solution.py:386
  86.2 1.0 down_both.1
  87.3 0.5 collective-permute-start.23
  87.8 0.5 collective-permute-start.31
  89.0 1.0 collective-permute-start.28
  90.0 9.7 %collective-permute-done.31.rows = bf16[256,768]{1,0:T(8,128)(2,1)S(1)} collective-permute-done((bf16[256,768]{1,0:T(8,128)(2,1)S(1)}, bf16[256,768]{1,0:T(8,128)(2,1)S(1)}, u32[]{:S(2)}, u32[]{:S(2)}) %collective-permute-start.31) | collective-permute-done | bytes 393248 | tf_op jit(solution)/shard_map/ppermute | solution.py:398
  99.8 0.6 down.3
  100.4 0.5 collective-permute-start.33
  102.9 1.1 collective-permute-start.26
  104.0 2.5 %collective-permute-start.27 = (bf16[32,1024]{1,0:T(8,128)(2,1)S(1)}, bf16[32,1024]{1,0:T(8,128)(2,1)S(1)}, u32[]{:S(2)}, u32[]{:S(2)}) collective-permute-start(bf16[32,1024]{1,0:T(8,128)(2,1)S(1)} %get-tuple-element.71), channel_id=1, source_target_pairs={{0,12},{1,13},{2,14},{3,15},{4,0},{5,1},{6,2},{7,3},{8,4},{9,5},{1... | collective-permute-start | bytes 196616 | tf_op jit(solution)/shard_map/ppermute | solution.py:401
  106.5 0.8 collective-permute-done.28.rows
  107.3 2.1 %collective-permute-done.25.m1 = bf16[32,1024]{1,0:T(8,128)(2,1)S(1)} collective-permute-done((bf16[32,1024]{1,0:T(8,128)(2,1)S(1)}, bf16[32,1024]{1,0:T(8,128)(2,1)S(1)}, u32[]{:S(2)}, u32[]{:S(2)}) %collective-permute-start.25) | collective-permute-done | bytes 65568 | tf_op jit(solution)/shard_map/ppermute | solution.py:401
  109.5 2.0 %collective-permute-done.26.m2 = bf16[32,1024]{1,0:T(8,128)(2,1)S(1)} collective-permute-done((bf16[32,1024]{1,0:T(8,128)(2,1)S(1)}, bf16[32,1024]{1,0:T(8,128)(2,1)S(1)}, u32[]{:S(2)}, u32[]{:S(2)}) %collective-permute-start.26) | collective-permute-done | bytes 65568 | tf_op jit(solution)/shard_map/ppermute | solution.py:401
  111.5 0.6 down.2
  112.2 0.5 collective-permute-start.30
  112.6 0.8 collective-permute-done.29.core_a
  113.8 0.6 collective-permute-start.35
  114.4 2.3 %collective-permute-start.36 = (bf16[32,1024]{1,0:T(8,128)(2,1)S(1)}, bf16[32,1024]{1,0:T(8,128)(2,1)S(1)}, u32[]{:S(2)}, u32[]{:S(2)}) collective-permute-start(bf16[32,1024]{1,0:T(8,128)(2,1)S(1)} %get-tuple-element.81), channel_id=1, source_target_pairs={{0,20},{1,21},{2,22},{3,23},{4,24},{5,25},{6,26},{7,27},{8,28},{9,... | collective-permute-start | bytes 196616 | tf_op jit(solution)/shard_map/ppermute | solution.py:406
  116.7 1.2 collective-permute-start.37
  117.9 2.0 %collective-permute-start.38 = (bf16[32,1024]{1,0:T(8,128)(2,1)S(1)}, bf16[32,1024]{1,0:T(8,128)(2,1)S(1)}, u32[]{:S(2)}, u32[]{:S(2)}) collective-permute-start(bf16[32,1024]{1,0:T(8,128)(2,1)S(1)} %get-tuple-element.83), channel_id=1, source_target_pairs={{0,28},{1,29},{2,30},{3,31},{4,16},{5,17},{6,18},{7,19},{8,20},{9,... | collective-permute-start | bytes 196616 | tf_op jit(solution)/shard_map/ppermute | solution.py:406
  119.8 2.0 %collective-permute-done.36.o1 = bf16[32,1024]{1,0:T(8,128)(2,1)S(1)} collective-permute-done((bf16[32,1024]{1,0:T(8,128)(2,1)S(1)}, bf16[32,1024]{1,0:T(8,128)(2,1)S(1)}, u32[]{:S(2)}, u32[]{:S(2)}) %collective-permute-start.36) | collective-permute-done | bytes 65568 | tf_op jit(solution)/shard_map/ppermute | solution.py:406
  121.9 2.1 %collective-permute-done.37.o2 = bf16[32,1024]{1,0:T(8,128)(2,1)S(1)} collective-permute-done((bf16[32,1024]{1,0:T(8,128)(2,1)S(1)}, bf16[32,1024]{1,0:T(8,128)(2,1)S(1)}, u32[]{:S(2)}, u32[]{:S(2)}) %collective-permute-start.37) | collective-permute-done | bytes 65568 | tf_op jit(solution)/shard_map/ppermute | solution.py:406
  124.3 0.9 closing.1
  (64 shorter events, 4.3 us)
Async XLA Ops:
  0.6 1.9 %copy-start = (bf16[1,1024,1536]{2,1,0:T(8,128)(2,1)S(1)}, bf16[1,1024,1536]{2,1,0:T(8,128)(2,1)}, u32[]{:S(2)}) copy-start(bf16[1,1024,1536]{2,1,0:T(8,128)(2,1)} %param.17) | copy-start | bytes 9437188
  2.5 5.9 %copy-start.5 = (bf16[1,64,2048]{2,1,0:T(8,128)(2,1)S(1)}, bf16[1,64,2048]{2,1,0:T(8,128)(2,1)}, u32[]{:S(2)}) copy-start(bf16[1,64,2048]{2,1,0:T(8,128)(2,1)} %param.10) | copy-start | bytes 786436
  2.5 22.3 %copy-start.8 = (bf16[1,32,2048]{2,1,0:T(8,128)(2,1)S(1)}, bf16[1,32,2048]{2,1,0:T(8,128)(2,1)}, u32[]{:S(2)}) copy-start(bf16[1,32,2048]{2,1,0:T(8,128)(2,1)} %param.11) | copy-start | bytes 393220
  2.5 33.5 %copy-start.1 = (bf16[1,1024,1536]{2,1,0:T(8,128)(2,1)S(1)}, bf16[1,1024,1536]{2,1,0:T(8,128)(2,1)}, u32[]{:S(2)}) copy-start(bf16[1,1024,1536]{2,1,0:T(8,128)(2,1)} %param.17) | copy-start | bytes 9437188
  3.9 41.6 %collective-permute-start.6 = (bf16[1024,768]{1,0:T(8,128)(2,1)}, bf16[1024,768]{1,0:T(8,128)(2,1)}, u32[]{:S(2)}, u32[]{:S(2)}) collective-permute-start(bf16[1024,768]{1,0:T(8,128)(2,1)} %weight_piece.2), channel_id=1, source_target_pairs={{0,16},{16,0},{1,17},{17,1},{2,18},{18,2},{3,19},{19,3},{4,20},{20... | collective-permute-start | bytes 4718600 | tf_op jit(solution)/shard_map/ppermute | solution.py:398
  6.9 13.7 %collective-permute-start.3 = (bf16[2048,128]{1,0:T(8,128)(2,1)}, bf16[2048,128]{1,0:T(8,128)(2,1)}, u32[]{:S(2)}, u32[]{:S(2)}) collective-permute-start(bf16[2048,128]{1,0:T(8,128)(2,1)} %w0.1), channel_id=1, source_target_pairs={{0,2},{1,3},{2,0},{3,1},{4,6},{5,7},{6,4},{7,5},{8,10},{9,11},{10,... | collective-permute-start | bytes 1572872 | tf_op jit(solution)/shard_map/ppermute | solution.py:417
  8.4 14.2 %collective-permute-start.1 = (bf16[64,2048]{1,0:T(8,128)(2,1)S(1)}, bf16[64,2048]{1,0:T(8,128)(2,1)}, u32[]{:S(2)}, u32[]{:S(2)}) collective-permute-start(bf16[64,2048]{1,0:T(8,128)(2,1)S(1)} %bitcast.16), channel_id=1, source_target_pairs={{0,8},{1,9},{2,10},{3,11},{4,12},{5,13},{6,14},{7,15},{8,0},{9,1},... | collective-permute-start | bytes 786440 | tf_op jit(solution)/shard_map/ppermute | solution.py:420
  11.0 11.7 %collective-permute-start = (bf16[64,2048]{1,0:T(8,128)(2,1)S(1)}, bf16[64,2048]{1,0:T(8,128)(2,1)S(1)}, u32[]{:S(2)}, u32[]{:S(2)}) collective-permute-start(bf16[64,2048]{1,0:T(8,128)(2,1)S(1)} %bitcast.17), channel_id=1, source_target_pairs={{0,4},{1,5},{2,6},{3,7},{4,0},{5,1},{6,2},{7,3},{8,12},{9,13},{10,... | collective-permute-start | bytes 786440 | tf_op jit(solution)/shard_map/ppermute | solution.py:420
  20.6 20.7 %collective-permute-start.4 = (bf16[2048,128]{1,0:T(8,128)(2,1)}, bf16[2048,128]{1,0:T(8,128)(2,1)}, u32[]{:S(2)}, u32[]{:S(2)}) collective-permute-start(bf16[2048,128]{1,0:T(8,128)(2,1)} %w0.1), channel_id=1, source_target_pairs={{0,1},{1,0},{2,3},{3,2},{4,5},{5,4},{6,7},{7,6},{8,9},{9,8},{10,11... | collective-permute-start | bytes 1572872 | tf_op jit(solution)/shard_map/ppermute | solution.py:417
  20.6 20.7 %collective-permute-start.5 = (bf16[2048,128]{1,0:T(8,128)(2,1)}, bf16[2048,128]{1,0:T(8,128)(2,1)}, u32[]{:S(2)}, u32[]{:S(2)}) collective-permute-start(bf16[2048,128]{1,0:T(8,128)(2,1)} %collective-permute-done.3.w2), channel_id=1, source_target_pairs={{0,1},{1,0},{2,3},{3,2},{4,5},{5,4},{6,7},{7,6},{8,9},{9,8},{10,11... | collective-permute-start | bytes 1572872 | tf_op jit(solution)/shard_map/ppermute | solution.py:417
  22.7 0.7 copy-start.6
  23.4 17.9 %collective-permute-start.2 = (bf16[64,2048]{1,0:T(8,128)(2,1)}, bf16[64,2048]{1,0:T(8,128)(2,1)}, u32[]{:S(2)}, u32[]{:S(2)}) collective-permute-start(bf16[64,2048]{1,0:T(8,128)(2,1)} %collective-permute-done.1.a2), channel_id=1, source_target_pairs={{0,4},{1,5},{2,6},{3,7},{4,0},{5,1},{6,2},{7,3},{8,12},{9,13},{10,... | collective-permute-start | bytes 786440 | tf_op jit(solution)/shard_map/ppermute | solution.py:420
  24.8 0.6 copy-start.11
  25.5 5.7 %collective-permute-start.7 = (bf16[64,512]{1,0:T(8,128)(2,1)S(1)}, bf16[64,512]{1,0:T(8,128)(2,1)S(1)}, u32[]{:S(2)}, u32[]{:S(2)}) collective-permute-start(bf16[64,512]{1,0:T(8,128)(2,1)S(1)} %get-tuple-element.49), channel_id=1, source_target_pairs={{0,8},{1,9},{2,10},{3,11},{4,12},{5,13},{6,14},{7,15},{8,0},{9,1},... | collective-permute-start | bytes 196616 | tf_op jit(solution)/shard_map/ppermute | solution.py:420
  31.8 13.6 %collective-permute-start.8 = (bf16[64,512]{1,0:T(8,128)(2,1)}, bf16[64,512]{1,0:T(8,128)(2,1)S(1)}, u32[]{:S(2)}, u32[]{:S(2)}) collective-permute-start(bf16[64,512]{1,0:T(8,128)(2,1)} %pad_maximum_fusion), channel_id=1, source_target_pairs={{0,4},{1,5},{2,6},{3,7},{4,0},{5,1},{6,2},{7,3},{8,12},{9,13},{10,... | collective-permute-start | bytes 196616 | tf_op jit(solution)/shard_map/ppermute | solution.py:420
  36.2 1.2 copy-start.3
  40.1 0.7 copy-start.9
  40.8 10.1 %copy-start.12 = (bf16[32,512]{1,0:T(8,128)(2,1)S(1)}, bf16[32,512]{1,0:T(8,128)(2,1)}, u32[]{:S(2)}) copy-start(bf16[32,512]{1,0:T(8,128)(2,1)} %copy-done.11) | copy-start | bytes 98308
  40.8 25.0 %copy-start.10 = (f32[2048]{0:T(1024)S(1)}, f32[2048]{0:T(1024)}, u32[]{:S(2)}) copy-start(f32[2048]{0:T(1024)} %param.13) | copy-start | bytes 24580
  41.3 9.2 %copy-start.4 = (bf16[1024,768]{1,0:T(8,128)(2,1)S(1)}, bf16[1024,768]{1,0:T(8,128)(2,1)}, u32[]{:S(2)}) copy-start(bf16[1024,768]{1,0:T(8,128)(2,1)} %copy-done.3) | copy-start | bytes 4718596
  41.3 1.1 copy-start.7
  45.4 5.0 %collective-permute-start.9 = (bf16[128,512]{1,0:T(8,128)(2,1)S(1)}, bf16[128,512]{1,0:T(8,128)(2,1)S(1)}, u32[]{:S(2)}, u32[]{:S(2)}) collective-permute-start(bf16[128,512]{1,0:T(8,128)(2,1)S(1)} %get-tuple-element.50), channel_id=1, source_target_pairs={{0,16},{16,0},{1,17},{17,1},{2,18},{18,2},{3,19},{19,3},{4,20},{20... | collective-permute-start | bytes 393224 | tf_op jit(solution)/shard_map/ppermute | solution.py:398
  50.5 34.4 %collective-permute-start.19 = (bf16[1024,768]{1,0:T(8,128)(2,1)S(1)}, bf16[1024,768]{1,0:T(8,128)(2,1)S(1)}, u32[]{:S(2)}, u32[]{:S(2)}) collective-permute-start(bf16[1024,768]{1,0:T(8,128)(2,1)S(1)} %copy-done.4), channel_id=1, source_target_pairs={{0,16},{16,0},{1,17},{17,1},{2,18},{18,2},{3,19},{19,3},{4,20},{20... | collective-permute-start | bytes 4718600 | tf_op jit(solution)/shard_map/ppermute | solution.py:398
  51.0 6.2 %collective-permute-start.12 = (bf16[144,512]{1,0:T(8,128)(2,1)S(1)}, bf16[144,512]{1,0:T(8,128)(2,1)S(1)}, u32[]{:S(2)}, u32[]{:S(2)}) collective-permute-start(bf16[144,512]{1,0:T(8,128)(2,1)S(1)} %stream.1.b0), channel_id=1, source_target_pairs={{0,12},{1,13},{2,14},{3,15},{4,0},{5,1},{6,2},{7,3},{8,4},{9,5},{1... | collective-permute-start | bytes 442376 | tf_op jit(solution)/shard_map/ppermute | solution.py:401
  52.0 11.8 %collective-permute-start.11 = (bf16[144,512]{1,0:T(8,128)(2,1)S(1)}, bf16[144,512]{1,0:T(8,128)(2,1)S(1)}, u32[]{:S(2)}, u32[]{:S(2)}) collective-permute-start(bf16[144,512]{1,0:T(8,128)(2,1)S(1)} %stream.1.b0), channel_id=1, source_target_pairs={{0,8},{1,9},{2,10},{3,11},{4,12},{5,13},{6,14},{7,15},{8,0},{9,1},... | collective-permute-start | bytes 442376 | tf_op jit(solution)/shard_map/ppermute | solution.py:401
  52.6 12.2 %collective-permute-start.10 = (bf16[144,512]{1,0:T(8,128)(2,1)S(1)}, bf16[144,512]{1,0:T(8,128)(2,1)S(1)}, u32[]{:S(2)}, u32[]{:S(2)}) collective-permute-start(bf16[144,512]{1,0:T(8,128)(2,1)S(1)} %stream.1.b0), channel_id=1, source_target_pairs={{0,4},{1,5},{2,6},{3,7},{4,8},{5,9},{6,10},{7,11},{8,12},{9,13},{1... | collective-permute-start | bytes 442376 | tf_op jit(solution)/shard_map/ppermute | solution.py:401
  53.1 13.1 %collective-permute-start.13 = (bf16[144,512]{1,0:T(8,128)(2,1)S(1)}, bf16[144,512]{1,0:T(8,128)(2,1)S(1)}, u32[]{:S(2)}, u32[]{:S(2)}) collective-permute-start(bf16[144,512]{1,0:T(8,128)(2,1)S(1)} %stream.1.b0), channel_id=1, source_target_pairs={{0,2},{1,3},{2,0},{3,1},{4,6},{5,7},{6,4},{7,5},{8,10},{9,11},{10,... | collective-permute-start | bytes 442376 | tf_op jit(solution)/shard_map/ppermute | solution.py:417
  57.3 9.0 %collective-permute-start.16 = (bf16[144,512]{1,0:T(8,128)(2,1)S(1)}, bf16[144,512]{1,0:T(8,128)(2,1)S(1)}, u32[]{:S(2)}, u32[]{:S(2)}) collective-permute-start(bf16[144,512]{1,0:T(8,128)(2,1)S(1)} %collective-permute-done.12.b3), channel_id=1, source_target_pairs={{0,2},{1,3},{2,0},{3,1},{4,6},{5,7},{6,4},{7,5},{8,10},{9,11},{10,... | collective-permute-start | bytes 442376 | tf_op jit(solution)/shard_map/ppermute | solution.py:417
  63.8 5.1 %collective-permute-start.15 = (bf16[144,512]{1,0:T(8,128)(2,1)S(1)}, bf16[144,512]{1,0:T(8,128)(2,1)S(1)}, u32[]{:S(2)}, u32[]{:S(2)}) collective-permute-start(bf16[144,512]{1,0:T(8,128)(2,1)S(1)} %collective-permute-done.11.b2), channel_id=1, source_target_pairs={{0,2},{1,3},{2,0},{3,1},{4,6},{5,7},{6,4},{7,5},{8,10},{9,11},{10,... | collective-permute-start | bytes 442376 | tf_op jit(solution)/shard_map/ppermute | solution.py:417
  64.7 5.8 %collective-permute-start.14 = (bf16[144,512]{1,0:T(8,128)(2,1)S(1)}, bf16[144,512]{1,0:T(8,128)(2,1)S(1)}, u32[]{:S(2)}, u32[]{:S(2)}) collective-permute-start(bf16[144,512]{1,0:T(8,128)(2,1)S(1)} %collective-permute-done.10.b1), channel_id=1, source_target_pairs={{0,2},{1,3},{2,0},{3,1},{4,6},{5,7},{6,4},{7,5},{8,10},{9,11},{10,... | collective-permute-start | bytes 442376 | tf_op jit(solution)/shard_map/ppermute | solution.py:417
  66.2 5.2 %collective-permute-start.18 = (bf16[128,2176]{1,0:T(8,128)(2,1)S(1)}, bf16[128,2176]{1,0:T(8,128)(2,1)S(1)}, u32[]{:S(2)}, u32[]{:S(2)}) collective-permute-start(bf16[128,2176]{1,0:T(8,128)(2,1)S(1)} %get-tuple-element.54.group), channel_id=1, source_target_pairs={{0,1},{1,0},{2,3},{3,2},{4,5},{5,4},{6,7},{7,6},{8,9},{9,8},{10,11... | collective-permute-start | bytes 1671176 | tf_op jit(solution)/shard_map/ppermute | solution.py:417
  71.4 2.0 %collective-permute-start.17 = (bf16[128,2176]{1,0:T(8,128)(2,1)S(1)}, bf16[128,2176]{1,0:T(8,128)(2,1)S(1)}, u32[]{:S(2)}, u32[]{:S(2)}) collective-permute-start(bf16[128,2176]{1,0:T(8,128)(2,1)S(1)} %get-tuple-element.53.group_x), channel_id=1, source_target_pairs={{0,1},{1,0},{2,3},{3,2},{4,5},{5,4},{6,7},{7,6},{8,9},{9,8},{10,11... | collective-permute-start | bytes 1671176 | tf_op jit(solution)/shard_map/ppermute | solution.py:417
  84.8 1.4 %copy-start.2 = (bf16[1,768,1024]{2,1,0:T(8,128)(2,1)S(1)}, bf16[1,768,1024]{2,1,0:T(8,128)(2,1)}, u32[]{:S(2)}) copy-start(bf16[1,768,1024]{2,1,0:T(8,128)(2,1)} %param.18) | copy-start | bytes 4718596
  87.2 1.4 %collective-permute-start.22 = (bf16[128,512]{1,0:T(8,128)(2,1)S(1)}, bf16[128,512]{1,0:T(8,128)(2,1)S(1)}, u32[]{:S(2)}, u32[]{:S(2)}) collective-permute-start(bf16[128,512]{1,0:T(8,128)(2,1)S(1)} %get-tuple-element.66), channel_id=1, source_target_pairs={{0,1},{1,0},{2,3},{3,2},{4,5},{5,4},{6,7},{7,6},{8,9},{9,8},{10,11... | collective-permute-start | bytes 393224 | tf_op jit(solution)/shard_map/ppermute | solution.py:417
  87.3 1.5 %collective-permute-start.23 = (bf16[128,512]{1,0:T(8,128)(2,1)S(1)}, bf16[128,512]{1,0:T(8,128)(2,1)S(1)}, u32[]{:S(2)}, u32[]{:S(2)}) collective-permute-start(bf16[128,512]{1,0:T(8,128)(2,1)S(1)} %get-tuple-element.67), channel_id=1, source_target_pairs={{0,1},{1,0},{2,3},{3,2},{4,5},{5,4},{6,7},{7,6},{8,9},{9,8},{10,11... | collective-permute-start | bytes 393224 | tf_op jit(solution)/shard_map/ppermute | solution.py:417
  87.8 12.0 %collective-permute-start.31 = (bf16[256,768]{1,0:T(8,128)(2,1)S(1)}, bf16[256,768]{1,0:T(8,128)(2,1)S(1)}, u32[]{:S(2)}, u32[]{:S(2)}) collective-permute-start(bf16[256,768]{1,0:T(8,128)(2,1)S(1)} %get-tuple-element.60.far), channel_id=1, source_target_pairs={{0,16},{16,0},{1,17},{17,1},{2,18},{18,2},{3,19},{19,3},{4,20},{20... | collective-permute-start | bytes 1179656 | tf_op jit(solution)/shard_map/ppermute | solution.py:398
  88.9 10.9 %collective-permute-start.24 = (bf16[128,1024]{1,0:T(8,128)(2,1)S(1)}, bf16[128,1024]{1,0:T(8,128)(2,1)S(1)}, u32[]{:S(2)}, u32[]{:S(2)}) collective-permute-start(bf16[128,1024]{1,0:T(8,128)(2,1)S(1)} %fold.2), channel_id=1, source_target_pairs={{0,2},{1,3},{2,0},{3,1},{4,6},{5,7},{6,4},{7,5},{8,10},{9,11},{10,... | collective-permute-start | bytes 786440 | tf_op jit(solution)/shard_map/ppermute | solution.py:417
  89.0 18.3 %collective-permute-start.28 = (bf16[256,768]{1,0:T(8,128)(2,1)S(1)}, bf16[256,768]{1,0:T(8,128)(2,1)S(1)}, u32[]{:S(2)}, u32[]{:S(2)}) collective-permute-start(bf16[256,768]{1,0:T(8,128)(2,1)S(1)} %get-tuple-element.61.near), channel_id=1, source_target_pairs={{0,16},{16,0},{1,17},{17,1},{2,18},{18,2},{3,19},{19,3},{4,20},{20... | collective-permute-start | bytes 1179656 | tf_op jit(solution)/shard_map/ppermute | solution.py:398
  100.4 1.4 %collective-permute-start.32 = (bf16[128,512]{1,0:T(8,128)(2,1)S(1)}, bf16[128,512]{1,0:T(8,128)(2,1)S(1)}, u32[]{:S(2)}, u32[]{:S(2)}) collective-permute-start(bf16[128,512]{1,0:T(8,128)(2,1)S(1)} %get-tuple-element.78), channel_id=1, source_target_pairs={{0,1},{1,0},{2,3},{3,2},{4,5},{5,4},{6,7},{7,6},{8,9},{9,8},{10,11... | collective-permute-start | bytes 393224 | tf_op jit(solution)/shard_map/ppermute | solution.py:417
  100.4 1.5 %collective-permute-start.33 = (bf16[128,512]{1,0:T(8,128)(2,1)S(1)}, bf16[128,512]{1,0:T(8,128)(2,1)S(1)}, u32[]{:S(2)}, u32[]{:S(2)}) collective-permute-start(bf16[128,512]{1,0:T(8,128)(2,1)S(1)} %get-tuple-element.79), channel_id=1, source_target_pairs={{0,1},{1,0},{2,3},{3,2},{4,5},{5,4},{6,7},{7,6},{8,9},{9,8},{10,11... | collective-permute-start | bytes 393224 | tf_op jit(solution)/shard_map/ppermute | solution.py:417
  100.9 1.3 %collective-permute-start.20 = (bf16[128,512]{1,0:T(8,128)(2,1)S(1)}, bf16[128,512]{1,0:T(8,128)(2,1)S(1)}, u32[]{:S(2)}, u32[]{:S(2)}) collective-permute-start(bf16[128,512]{1,0:T(8,128)(2,1)S(1)} %get-tuple-element.63), channel_id=1, source_target_pairs={{0,1},{1,0},{2,3},{3,2},{4,5},{5,4},{6,7},{7,6},{8,9},{9,8},{10,11... | collective-permute-start | bytes 393224 | tf_op jit(solution)/shard_map/ppermute | solution.py:417
  101.0 1.5 %collective-permute-start.21 = (bf16[128,512]{1,0:T(8,128)(2,1)S(1)}, bf16[128,512]{1,0:T(8,128)(2,1)S(1)}, u32[]{:S(2)}, u32[]{:S(2)}) collective-permute-start(bf16[128,512]{1,0:T(8,128)(2,1)S(1)} %get-tuple-element.64), channel_id=1, source_target_pairs={{0,1},{1,0},{2,3},{3,2},{4,5},{5,4},{6,7},{7,6},{8,9},{9,8},{10,11... | collective-permute-start | bytes 393224 | tf_op jit(solution)/shard_map/ppermute | solution.py:417
  102.0 11.6 %collective-permute-start.34 = (bf16[128,1024]{1,0:T(8,128)(2,1)S(1)}, bf16[128,1024]{1,0:T(8,128)(2,1)S(1)}, u32[]{:S(2)}, u32[]{:S(2)}) collective-permute-start(bf16[128,1024]{1,0:T(8,128)(2,1)S(1)} %fold.3), channel_id=1, source_target_pairs={{0,2},{1,3},{2,0},{3,1},{4,6},{5,7},{6,4},{7,5},{8,10},{9,11},{10,... | collective-permute-start | bytes 786440 | tf_op jit(solution)/shard_map/ppermute | solution.py:417
  102.6 21.7 %copy-start.13 = (f32[2048]{0:T(1024)S(1)}, f32[2048]{0:T(1024)}, u32[]{:S(2)}) copy-start(f32[2048]{0:T(1024)} %param.19) | copy-start | bytes 24580
  102.6 6.9 %collective-permute-start.25 = (bf16[32,1024]{1,0:T(8,128)(2,1)S(1)}, bf16[32,1024]{1,0:T(8,128)(2,1)S(1)}, u32[]{:S(2)}, u32[]{:S(2)}) collective-permute-start(bf16[32,1024]{1,0:T(8,128)(2,1)S(1)} %get-tuple-element.69), channel_id=1, source_target_pairs={{0,4},{1,5},{2,6},{3,7},{4,8},{5,9},{6,10},{7,11},{8,12},{9,13},{1... | collective-permute-start | bytes 196616 | tf_op jit(solution)/shard_map/ppermute | solution.py:401
  102.9 8.6 %collective-permute-start.26 = (bf16[32,1024]{1,0:T(8,128)(2,1)S(1)}, bf16[32,1024]{1,0:T(8,128)(2,1)S(1)}, u32[]{:S(2)}, u32[]{:S(2)}) collective-permute-start(bf16[32,1024]{1,0:T(8,128)(2,1)S(1)} %get-tuple-element.70), channel_id=1, source_target_pairs={{0,8},{1,9},{2,10},{3,11},{4,12},{5,13},{6,14},{7,15},{8,0},{9,1},... | collective-permute-start | bytes 196616 | tf_op jit(solution)/shard_map/ppermute | solution.py:401
  104.0 7.5 %collective-permute-start.27 = (bf16[32,1024]{1,0:T(8,128)(2,1)S(1)}, bf16[32,1024]{1,0:T(8,128)(2,1)S(1)}, u32[]{:S(2)}, u32[]{:S(2)}) collective-permute-start(bf16[32,1024]{1,0:T(8,128)(2,1)S(1)} %get-tuple-element.71), channel_id=1, source_target_pairs={{0,12},{1,13},{2,14},{3,15},{4,0},{5,1},{6,2},{7,3},{8,4},{9,5},{1... | collective-permute-start | bytes 196616 | tf_op jit(solution)/shard_map/ppermute | solution.py:401
  112.1 1.4 %collective-permute-start.29 = (bf16[128,512]{1,0:T(8,128)(2,1)S(1)}, bf16[128,512]{1,0:T(8,128)(2,1)S(1)}, u32[]{:S(2)}, u32[]{:S(2)}) collective-permute-start(bf16[128,512]{1,0:T(8,128)(2,1)S(1)} %get-tuple-element.74), channel_id=1, source_target_pairs={{0,1},{1,0},{2,3},{3,2},{4,5},{5,4},{6,7},{7,6},{8,9},{9,8},{10,11... | collective-permute-start | bytes 393224 | tf_op jit(solution)/shard_map/ppermute | solution.py:417
  112.2 1.5 %collective-permute-start.30 = (bf16[128,512]{1,0:T(8,128)(2,1)S(1)}, bf16[128,512]{1,0:T(8,128)(2,1)S(1)}, u32[]{:S(2)}, u32[]{:S(2)}) collective-permute-start(bf16[128,512]{1,0:T(8,128)(2,1)S(1)} %get-tuple-element.75), channel_id=1, source_target_pairs={{0,1},{1,0},{2,3},{3,2},{4,5},{5,4},{6,7},{7,6},{8,9},{9,8},{10,11... | collective-permute-start | bytes 393224 | tf_op jit(solution)/shard_map/ppermute | solution.py:417
  113.8 6.1 %collective-permute-start.35 = (bf16[32,1024]{1,0:T(8,128)(2,1)S(1)}, bf16[32,1024]{1,0:T(8,128)(2,1)S(1)}, u32[]{:S(2)}, u32[]{:S(2)}) collective-permute-start(bf16[32,1024]{1,0:T(8,128)(2,1)S(1)} %get-tuple-element.80), channel_id=1, source_target_pairs={{0,16},{1,17},{2,18},{3,19},{4,20},{5,21},{6,22},{7,23},{8,24},{9,... | collective-permute-start | bytes 196616 | tf_op jit(solution)/shard_map/ppermute | solution.py:406
  114.4 7.5 %collective-permute-start.36 = (bf16[32,1024]{1,0:T(8,128)(2,1)S(1)}, bf16[32,1024]{1,0:T(8,128)(2,1)S(1)}, u32[]{:S(2)}, u32[]{:S(2)}) collective-permute-start(bf16[32,1024]{1,0:T(8,128)(2,1)S(1)} %get-tuple-element.81), channel_id=1, source_target_pairs={{0,20},{1,21},{2,22},{3,23},{4,24},{5,25},{6,26},{7,27},{8,28},{9,... | collective-permute-start | bytes 196616 | tf_op jit(solution)/shard_map/ppermute | solution.py:406
  116.7 7.3 %collective-permute-start.37 = (bf16[32,1024]{1,0:T(8,128)(2,1)S(1)}, bf16[32,1024]{1,0:T(8,128)(2,1)S(1)}, u32[]{:S(2)}, u32[]{:S(2)}) collective-permute-start(bf16[32,1024]{1,0:T(8,128)(2,1)S(1)} %get-tuple-element.82), channel_id=1, source_target_pairs={{0,24},{1,25},{2,26},{3,27},{4,28},{5,29},{6,30},{7,31},{8,16},{9,... | collective-permute-start | bytes 196616 | tf_op jit(solution)/shard_map/ppermute | solution.py:406
  117.9 6.4 %collective-permute-start.38 = (bf16[32,1024]{1,0:T(8,128)(2,1)S(1)}, bf16[32,1024]{1,0:T(8,128)(2,1)S(1)}, u32[]{:S(2)}, u32[]{:S(2)}) collective-permute-start(bf16[32,1024]{1,0:T(8,128)(2,1)S(1)} %get-tuple-element.83), channel_id=1, source_target_pairs={{0,28},{1,29},{2,30},{3,31},{4,16},{5,17},{6,18},{7,19},{8,20},{9,... | collective-permute-start | bytes 196616 | tf_op jit(solution)/shard_map/ppermute | solution.py:406

commit v8 on v7

--- a/solution.py
+++ b/solution.py
@@ -220,14 +220,15 @@
 
 
 def piece_kernel(starts, weights, out, semaphores):
-    width = out.shape[1] // 2
+    depth, width = out.shape[0] // 4, out.shape[1] // 2
     copies = [
         pltpu.make_async_copy(
-            weights.at[:, pl.ds(starts[i], width)],
-            out.at[:, pl.ds(i * width, width)],
-            semaphores.at[i],
+            weights.at[pl.ds(k * depth, depth), pl.ds(starts[i], width)],
+            out.at[pl.ds(k * depth, depth), pl.ds(i * width, width)],
+            semaphores.at[i, k],
         )
         for i in range(2)
+        for k in range(4)
     ]
     for copy in copies:
         copy.start()
@@ -422,14 +423,14 @@
     def after(x, *results):
         return lax.optimization_barrier((x, *results))[0]
 
-    def weight_piece(first, size):
+    def weight_piece(first, size, mib=8):
         return pl.pallas_call(
             functools.partial(piece_kernel, (first, hidden + first)),
             out_shape=shape_of(half_width, 2 * size),
-            in_specs=[pl.BlockSpec(memory_space=pltpu.HBM)],
-            out_specs=vmem,
-            scratch_shapes=[pltpu.SemaphoreType.DMA((2,))],
-            compiler_params=kernel_params(8),
+            in_specs=[pl.BlockSpec(memory_space=pl.ANY)],
+            out_specs=pl.BlockSpec(memory_space=pl.ANY),
+            scratch_shapes=[pltpu.SemaphoreType.DMA((2, 4))],
+            compiler_params=kernel_params(mib),
             cost_estimate=small_cost(),
             name="weight_piece",
         )(w_gate_up[0])
@@ -449,7 +450,7 @@
         first=smem,
     )
     cut_width = hidden // 2
-    early_piece = weight_piece(0, cut_width)
+    early_piece = weight_piece(0, cut_width, 60)
     late_sizes = (cut_width * 384 // 384,)
     late_pieces = [
         weight_piece(cut_width + sum(late_sizes[:i]), size) for i, size in enumerate(late_sizes)
@@ -458,8 +459,8 @@
     a = [attn[0], swap_outer(attn[0], 1), swap_outer(attn[0], 2)]
     w_x = swap_inner(w_out, 2)
     r_2 = swap_outer(r_23, 2)
-    a.append(swap_outer(after(a[2], a[1]), 1))
-    w_c = swap_inner(after(w_out, w_x), 1)
+    a.append(swap_outer(after(a[2], a[1], r_2), 1))
+    w_c = swap_inner(after(w_out, w_x, share, *late_pieces), 1)
     w_cx = swap_inner(w_x, 1)
     r_13 = swap_outer(jnp.concatenate([r_1, r_2[rows_here:]], axis=0), 1)
 
@@ -479,7 +480,7 @@
             pltpu.VMEM((8 * rows_here, quarter), BF16),
         ),
     )
-    arrived = swap_dp(after(send, gate_up_early, r_13, share, *late_pieces))
+    arrived = swap_dp(after(send, gate_up_early, r_13))
     gate_up_late = [swap_dp(after(piece, arrived)) for piece in late_pieces]
     (block,) = call(
         stream_kernel,

time: 126 us -> 170 us (1.35)
  Pallas kernels: 15.7 us -> 63.6 us
  local copies, waits for them, and re-layouts: 8.32 us -> 1.39 us
  starting transfers between devices: 39.8 us -> 44.6 us
    pallas_call x2, Pallas kernels: 1.5 us -> 49.1 us  [weight_piece(): pl.pallas_call(functools.partial(piece_kernel, (first, hidden + first)),...]
    unnamed x30 -> x24, local copies, waits for them, and re-layouts: 8.32 us -> 1.38 us
    ppermute x5, waiting for transfers between devices: 4.83 us -> 11.4 us  [swap_outer(): lax.ppermute(x, 'expert', [(i, i ^ 4 * s) for i in range(expert_count)])]
    ppermute x5, starting transfers between devices: 12.3 us -> 6.59 us  [swap_outer(): lax.ppermute(x, 'expert', [(i, i ^ 4 * s) for i in range(expert_count)])]
    ppermute x6, starting transfers between devices: 5.96 us -> 10.2 us  [shift_outer(): lax.ppermute(x, 'expert', [(i, (i + 4 * s) % expert_count) for i in range...]
    ppermute x19, waiting for transfers between devices: 16.6 us -> 12.5 us  [swap_inner(): return lax.ppermute(x, 'expert', [(i, i ^ j) for i in range(expert_count)])]
    ppermute x5, waiting for transfers between devices: 21.7 us -> 17.7 us  [swap_dp(): return lax.ppermute(x, 'dp', [(0, 1), (1, 0)])]
    ppermute x5, starting transfers between devices: 5.63 us -> 8.95 us  [swap_dp(): return lax.ppermute(x, 'dp', [(0, 1), (1, 0)])]
  transfers between devices with their start and end apart: 39 -> 39, of which waited for: 26 -> 22; matrix products, arithmetic and copies ran while one was open for 2% -> 1% of each run, Pallas kernels for 9% -> 7%
where the time goes in v8:
time: 170 us
  Pallas kernels  63.6 us (37%)
  waiting for transfers between devices  57.7 us (34%)
  starting transfers between devices  44.6 us (26%)
    pallas_call x2, Pallas kernels, weight_piece(): pl.pallas_call(functools.partial(piece_kernel, (first, hidden + first)),...  49.1 us
    ppermute x5, waiting for transfers between devices, swap_dp(): return lax.ppermute(x, 'dp', [(0, 1), (1, 0)])  17.7 us
    pallas_call x16, Pallas kernels, call(): pl.pallas_call(kernel, out_shape=outs, in_specs=[first] + [vmem] * (len(a...  14.5 us
    ppermute x19, waiting for transfers between devices, swap_inner(): return lax.ppermute(x, 'expert', [(i, i ^ j) for i in range(expert_count)])  12.5 us
    ppermute x19, starting transfers between devices, swap_inner(): return lax.ppermute(x, 'expert', [(i, i ^ j) for i in range(expert_count)])  12.3 us
    ppermute x5, waiting for transfers between devices, swap_outer(): lax.ppermute(x, 'expert', [(i, i ^ 4 * s) for i in range(expert_count)])  11.4 us
    ppermute x6, waiting for transfers between devices, shift_outer(): lax.ppermute(x, 'expert', [(i, (i + 4 * s) % expert_count) for i in range...  10.7 us
    ppermute x6, starting transfers between devices, shift_outer(): lax.ppermute(x, 'expert', [(i, (i + 4 * s) % expert_count) for i in range...  10.2 us
  transfers between devices with their start and end apart: 39, of which 22 were waited for; matrix products, arithmetic and copies ran while one was open for 1% of the time, Pallas kernels for 7%

profile of v8, /device:TPU:0, one launch (start us, length us, event | category | flops | bytes accessed | tf_op | source)
XLA Modules:
  0.0 169.5 jit_solution(7153403973392807872)
XLA Ops:
  0.7 48.8 %weight_piece.3 = bf16[1024,768]{1,0:T(8,128)(2,1)} custom-call(bf16[1024,1536]{1,0:T(8,128)(2,1)} %bitcast.10), custom_call_target="tpu_custom_call" | custom-call | flops 1 | bytes 1 | tf_op jit(solution)/shard_map/weight_piece/pallas_call | solution.py:427
  49.5 3.0 %collective-permute-start.7 = (bf16[1024,768]{1,0:T(8,128)(2,1)}, bf16[1024,768]{1,0:T(8,128)(2,1)}, u32[]{:S(2)}, u32[]{:S(2)}) collective-permute-start(bf16[1024,768]{1,0:T(8,128)(2,1)} %weight_piece.3), channel_id=1, source_target_pairs={{0,16},{16,0},{1,17},{17,1},{2,18},{18,2},{3,19},{19,3},{4,20},{20... | collective-permute-start | bytes 4718600 | tf_op jit(solution)/shard_map/ppermute | solution.py:399
  52.5 1.5 collective-permute-start.4
  54.0 0.6 cut_resid.1
  54.7 2.6 %collective-permute-start.2 = (bf16[64,512]{1,0:T(8,128)(2,1)}, bf16[64,512]{1,0:T(8,128)(2,1)S(1)}, u32[]{:S(2)}, u32[]{:S(2)}) collective-permute-start(bf16[64,512]{1,0:T(8,128)(2,1)} %get-tuple-element.44), channel_id=1, source_target_pairs={{0,8},{1,9},{2,10},{3,11},{4,12},{5,13},{6,14},{7,15},{8,0},{9,1},... | collective-permute-start | bytes 196616 | tf_op jit(solution)/shard_map/ppermute | solution.py:421
  57.3 0.3 collective-permute-start.1
  57.6 1.6 collective-permute-start
  59.2 0.2 weight_piece.2
  59.4 1.2 copy-done.2
  61.4 0.5 share.1
  61.9 4.4 %collective-permute-done.4.w2 = bf16[2048,128]{1,0:T(8,128)(2,1)} collective-permute-done((bf16[2048,128]{1,0:T(8,128)(2,1)}, bf16[2048,128]{1,0:T(8,128)(2,1)}, u32[]{:S(2)}, u32[]{:S(2)}) %collective-permute-start.4) | collective-permute-done | bytes 524320 | tf_op jit(solution)/shard_map/ppermute | solution.py:418
  66.2 0.5 collective-permute-start.5
  66.7 5.4 %collective-permute-done.1.a2 = bf16[64,2048]{1,0:T(8,128)(2,1)} collective-permute-done((bf16[64,2048]{1,0:T(8,128)(2,1)S(1)}, bf16[64,2048]{1,0:T(8,128)(2,1)}, u32[]{:S(2)}, u32[]{:S(2)}) %collective-permute-start.1) | collective-permute-done | bytes 262176 | tf_op jit(solution)/shard_map/ppermute | solution.py:421
  72.4 0.8 pad_maximum_fusion
  73.1 1.9 %collective-permute-start.8 = (bf16[64,512]{1,0:T(8,128)(2,1)S(1)}, bf16[64,512]{1,0:T(8,128)(2,1)S(1)}, u32[]{:S(2)}, u32[]{:S(2)}) collective-permute-start(bf16[64,512]{1,0:T(8,128)(2,1)S(1)} %pad_maximum_fusion), channel_id=1, source_target_pairs={{0,4},{1,5},{2,6},{3,7},{4,0},{5,1},{6,2},{7,3},{8,12},{9,13},{10,... | collective-permute-start | bytes 196616 | tf_op jit(solution)/shard_map/ppermute | solution.py:421
  75.0 6.0 %collective-permute-done.3.a3 = bf16[64,2048]{1,0:T(8,128)(2,1)S(1)} collective-permute-done((bf16[64,2048]{1,0:T(8,128)(2,1)}, bf16[64,2048]{1,0:T(8,128)(2,1)S(1)}, u32[]{:S(2)}, u32[]{:S(2)}) %collective-permute-start.3) | collective-permute-done | bytes 262176 | tf_op jit(solution)/shard_map/ppermute | solution.py:421
  81.0 2.7 %projection.1 = (bf16[128,512]{1,0:T(8,128)(2,1)S(1)}, bf16[128,512]{1,0:T(8,128)(2,1)S(1)}) custom-call(bf16[64,2048]{1,0:T(8,128)(2,1)S(1)} %bitcast.18, bf16[64,2048]{1,0:T(8,128)(2,1)} %collective-permute-done.a1, bf16[64,2048]{1,0:T(8,128)(2,1)} %collective-permute-done.1.a2, bf16[64,2048]{1,0:T(8,128)(2,1)S(1)} %collective-permute-done.3.a3, ...), custom_call_target="tpu_custom_call" | custom-call | flops 1 | bytes 1 | tf_op jit(solution)/shard_map/projection/pallas_call | solution.py:387
  83.7 3.5 %collective-permute-done.7.early = bf16[1024,768]{1,0:T(8,128)(2,1)} collective-permute-done((bf16[1024,768]{1,0:T(8,128)(2,1)}, bf16[1024,768]{1,0:T(8,128)(2,1)}, u32[]{:S(2)}, u32[]{:S(2)}) %collective-permute-start.7) | collective-permute-done | bytes 1572896 | tf_op jit(solution)/shard_map/ppermute | solution.py:399
  87.2 1.7 %collective-permute-start.9 = (bf16[128,512]{1,0:T(8,128)(2,1)S(1)}, bf16[128,512]{1,0:T(8,128)(2,1)S(1)}, u32[]{:S(2)}, u32[]{:S(2)}) collective-permute-start(bf16[128,512]{1,0:T(8,128)(2,1)S(1)} %get-tuple-element.50), channel_id=1, source_target_pairs={{0,16},{16,0},{1,17},{17,1},{2,18},{18,2},{3,19},{19,3},{4,20},{20... | collective-permute-start | bytes 393224 | tf_op jit(solution)/shard_map/ppermute | solution.py:399
  89.0 3.2 %collective-permute-done.9.arrived = bf16[128,512]{1,0:T(8,128)(2,1)S(1)} collective-permute-done((bf16[128,512]{1,0:T(8,128)(2,1)S(1)}, bf16[128,512]{1,0:T(8,128)(2,1)S(1)}, u32[]{:S(2)}, u32[]{:S(2)}) %collective-permute-start.9) | collective-permute-done | bytes 131104 | tf_op jit(solution)/shard_map/ppermute | solution.py:399
  92.2 1.7 %collective-permute-start.19 = (bf16[1024,768]{1,0:T(8,128)(2,1)S(1)}, bf16[1024,768]{1,0:T(8,128)(2,1)S(1)}, u32[]{:S(2)}, u32[]{:S(2)}) collective-permute-start(bf16[1024,768]{1,0:T(8,128)(2,1)S(1)} %copy-done.3), channel_id=1, source_target_pairs={{0,16},{16,0},{1,17},{17,1},{2,18},{18,2},{3,19},{19,3},{4,20},{20... | collective-permute-start | bytes 4718600 | tf_op jit(solution)/shard_map/ppermute | solution.py:399
  94.0 3.7 %collective-permute-start.12 = (bf16[144,512]{1,0:T(8,128)(2,1)S(1)}, bf16[144,512]{1,0:T(8,128)(2,1)S(1)}, u32[]{:S(2)}, u32[]{:S(2)}) collective-permute-start(bf16[144,512]{1,0:T(8,128)(2,1)S(1)} %stream.1.b0), channel_id=1, source_target_pairs={{0,12},{1,13},{2,14},{3,15},{4,0},{5,1},{6,2},{7,3},{8,4},{9,5},{1... | collective-permute-start | bytes 442376 | tf_op jit(solution)/shard_map/ppermute | solution.py:402
  97.7 1.0 collective-permute-start.10
  98.7 1.5 collective-permute-start.13
  100.2 1.5 collective-permute-done.12.b3
  101.7 1.5 collective-permute-start.16
  103.2 5.7 %collective-permute-done.11.b2 = bf16[144,512]{1,0:T(8,128)(2,1)S(1)} collective-permute-done((bf16[144,512]{1,0:T(8,128)(2,1)S(1)}, bf16[144,512]{1,0:T(8,128)(2,1)S(1)}, u32[]{:S(2)}, u32[]{:S(2)}) %collective-permute-start.11) | collective-permute-done | bytes 147488 | tf_op jit(solution)/shard_map/ppermute | solution.py:402
  108.9 1.5 collective-permute-start.15
  110.3 0.5 collective-permute-start.14
  110.9 0.3 norm.2
  111.3 3.1 %collective-permute-done.15.b2 = bf16[144,512]{1,0:T(8,128)(2,1)S(1)} collective-permute-done((bf16[144,512]{1,0:T(8,128)(2,1)S(1)}, bf16[144,512]{1,0:T(8,128)(2,1)S(1)}, u32[]{:S(2)}, u32[]{:S(2)}) %collective-permute-start.15) | collective-permute-done | bytes 147488 | tf_op jit(solution)/shard_map/ppermute | solution.py:418
  114.4 1.6 collective-permute-done.14.b1
  116.0 0.8 norm.3
  116.8 2.0 %collective-permute-done.17.group_cx = bf16[128,2176]{1,0:T(8,128)(2,1)S(1)} collective-permute-done((bf16[128,2176]{1,0:T(8,128)(2,1)S(1)}, bf16[128,2176]{1,0:T(8,128)(2,1)S(1)}, u32[]{:S(2)}, u32[]{:S(2)}) %collective-permute-start.17) | collective-permute-done | bytes 557088 | tf_op jit(solution)/shard_map/ppermute | solution.py:418
  118.7 4.8 %first_gate_up.1 = (bf16[512,384]{1,0:T(8,128)(2,1)S(1)}, f32[512,768]{1,0:T(8,128)S(1)}, bf16[512,1024]{1,0:T(8,128)(2,1)S(1)}, f32[512,128]{1,0:T(8,128)S(1)}) custom-call(bf16[128,2176]{1,0:T(8,128)(2,1)S(1)} %get-tuple-element.53.group_x, bf16[128,2176]{1,0:T(8,128)(2,1)S(1)} %collective-permute-done.17.group_cx, ...), custom_call_target="tpu_custom_call" | custom-call | flops 1 | bytes 1 | tf_op jit(solution)/shard_map/first_gate_up/pallas_call | solution.py:387
  123.6 3.1 %collective-permute-done.19.refs_0_ = bf16[1024,768]{1,0:T(8,128)(2,1)S(1)} collective-permute-done((bf16[1024,768]{1,0:T(8,128)(2,1)S(1)}, bf16[1024,768]{1,0:T(8,128)(2,1)S(1)}, u32[]{:S(2)}, u32[]{:S(2)}) %collective-permute-start.19) | collective-permute-done | bytes 1572896 | tf_op jit(solution)/shard_map/ppermute | solution.py:399
  126.6 1.4 last_gate_up.1
  128.0 1.0 down_both.1
  129.1 0.5 collective-permute-start.23
  129.6 1.4 collective-permute-start.31
  131.1 1.6 collective-permute-start.24
  132.7 1.0 collective-permute-start.28
  133.7 7.9 %collective-permute-done.31.rows = bf16[256,768]{1,0:T(8,128)(2,1)S(1)} collective-permute-done((bf16[256,768]{1,0:T(8,128)(2,1)S(1)}, bf16[256,768]{1,0:T(8,128)(2,1)S(1)}, u32[]{:S(2)}, u32[]{:S(2)}) %collective-permute-start.31) | collective-permute-done | bytes 393248 | tf_op jit(solution)/shard_map/ppermute | solution.py:399
  141.6 0.6 down.3
  142.3 0.5 collective-permute-start.33
  142.8 0.4 collective-permute-start.21
  143.3 0.3 collective-permute-done.32.core_a
  143.9 1.4 collective-permute-start.34
  145.4 1.6 collective-permute-start.25
  147.1 2.6 %collective-permute-start.26 = (bf16[32,1024]{1,0:T(8,128)(2,1)S(1)}, bf16[32,1024]{1,0:T(8,128)(2,1)S(1)}, u32[]{:S(2)}, u32[]{:S(2)}) collective-permute-start(bf16[32,1024]{1,0:T(8,128)(2,1)S(1)} %get-tuple-element.70), channel_id=1, source_target_pairs={{0,8},{1,9},{2,10},{3,11},{4,12},{5,13},{6,14},{7,15},{8,0},{9,1},... | collective-permute-start | bytes 196616 | tf_op jit(solution)/shard_map/ppermute | solution.py:402
  149.6 1.3 collective-permute-start.27
  151.0 0.8 collective-permute-done.25.m1
  151.8 2.5 %collective-permute-done.26.m2 = bf16[32,1024]{1,0:T(8,128)(2,1)S(1)} collective-permute-done((bf16[32,1024]{1,0:T(8,128)(2,1)S(1)}, bf16[32,1024]{1,0:T(8,128)(2,1)S(1)}, u32[]{:S(2)}, u32[]{:S(2)}) %collective-permute-start.26) | collective-permute-done | bytes 65568 | tf_op jit(solution)/shard_map/ppermute | solution.py:402
  154.5 0.6 down.2
  155.2 0.5 collective-permute-start.30
  155.7 0.8 collective-permute-done.29.core_a
  156.8 1.6 collective-permute-start.35
  158.4 1.6 collective-permute-start.36
  160.0 2.8 %collective-permute-start.37 = (bf16[32,1024]{1,0:T(8,128)(2,1)S(1)}, bf16[32,1024]{1,0:T(8,128)(2,1)S(1)}, u32[]{:S(2)}, u32[]{:S(2)}) collective-permute-start(bf16[32,1024]{1,0:T(8,128)(2,1)S(1)} %get-tuple-element.82), channel_id=1, source_target_pairs={{0,24},{1,25},{2,26},{3,27},{4,28},{5,29},{6,30},{7,31},{8,16},{9,... | collective-permute-start | bytes 196616 | tf_op jit(solution)/shard_map/ppermute | solution.py:407
  162.8 0.5 collective-permute-start.38
  163.3 2.7 %collective-permute-done.36.o1 = bf16[32,1024]{1,0:T(8,128)(2,1)S(1)} collective-permute-done((bf16[32,1024]{1,0:T(8,128)(2,1)S(1)}, bf16[32,1024]{1,0:T(8,128)(2,1)S(1)}, u32[]{:S(2)}, u32[]{:S(2)}) %collective-permute-start.36) | collective-permute-done | bytes 65568 | tf_op jit(solution)/shard_map/ppermute | solution.py:407
  166.0 2.1 %collective-permute-done.37.o2 = bf16[32,1024]{1,0:T(8,128)(2,1)S(1)} collective-permute-done((bf16[32,1024]{1,0:T(8,128)(2,1)S(1)}, bf16[32,1024]{1,0:T(8,128)(2,1)S(1)}, u32[]{:S(2)}, u32[]{:S(2)}) %collective-permute-start.37) | collective-permute-done | bytes 65568 | tf_op jit(solution)/shard_map/ppermute | solution.py:407
  168.1 0.6 collective-permute-done.38.o3
  168.7 0.9 closing.1
  (58 shorter events, 1.8 us)
Async XLA Ops:
  0.6 53.4 %copy-start.5 = (bf16[1,32,2048]{2,1,0:T(8,128)(2,1)S(1)}, bf16[1,32,2048]{2,1,0:T(8,128)(2,1)}, u32[]{:S(2)}) copy-start(bf16[1,32,2048]{2,1,0:T(8,128)(2,1)} %param.11) | copy-start | bytes 393220
  0.6 56.6 %copy-start.4 = (bf16[1,64,2048]{2,1,0:T(8,128)(2,1)S(1)}, bf16[1,64,2048]{2,1,0:T(8,128)(2,1)}, u32[]{:S(2)}) copy-start(bf16[1,64,2048]{2,1,0:T(8,128)(2,1)} %param.10) | copy-start | bytes 786436
  0.6 58.5 %copy-start = (bf16[1,1024,1536]{2,1,0:T(8,128)(2,1)S(1)}, bf16[1,1024,1536]{2,1,0:T(8,128)(2,1)}, u32[]{:S(2)}) copy-start(bf16[1,1024,1536]{2,1,0:T(8,128)(2,1)} %param.17) | copy-start | bytes 9437188
  49.5 37.7 %collective-permute-start.7 = (bf16[1024,768]{1,0:T(8,128)(2,1)}, bf16[1024,768]{1,0:T(8,128)(2,1)}, u32[]{:S(2)}, u32[]{:S(2)}) collective-permute-start(bf16[1024,768]{1,0:T(8,128)(2,1)} %weight_piece.3), channel_id=1, source_target_pairs={{0,16},{16,0},{1,17},{17,1},{2,18},{18,2},{3,19},{19,3},{4,20},{20... | collective-permute-start | bytes 4718600 | tf_op jit(solution)/shard_map/ppermute | solution.py:399
  52.5 13.7 %collective-permute-start.4 = (bf16[2048,128]{1,0:T(8,128)(2,1)}, bf16[2048,128]{1,0:T(8,128)(2,1)}, u32[]{:S(2)}, u32[]{:S(2)}) collective-permute-start(bf16[2048,128]{1,0:T(8,128)(2,1)} %w0.1), channel_id=1, source_target_pairs={{0,2},{1,3},{2,0},{3,1},{4,6},{5,7},{6,4},{7,5},{8,10},{9,11},{10,... | collective-permute-start | bytes 1572872 | tf_op jit(solution)/shard_map/ppermute | solution.py:418
  54.7 4.8 %copy-start.7 = (bf16[32,512]{1,0:T(8,128)(2,1)}, bf16[32,512]{1,0:T(8,128)(2,1)S(1)}, u32[]{:S(2)}) copy-start(bf16[32,512]{1,0:T(8,128)(2,1)S(1)} %get-tuple-element.49) | copy-start | bytes 98308
  54.7 11.6 %collective-permute-start.2 = (bf16[64,512]{1,0:T(8,128)(2,1)}, bf16[64,512]{1,0:T(8,128)(2,1)S(1)}, u32[]{:S(2)}, u32[]{:S(2)}) collective-permute-start(bf16[64,512]{1,0:T(8,128)(2,1)} %get-tuple-element.44), channel_id=1, source_target_pairs={{0,8},{1,9},{2,10},{3,11},{4,12},{5,13},{6,14},{7,15},{8,0},{9,1},... | collective-permute-start | bytes 196616 | tf_op jit(solution)/shard_map/ppermute | solution.py:421
  57.2 4.0 %copy-start.9 = (s32[1,32,8]{1,2,0:T(8,128)S(1)}, s32[1,32,8]{1,2,0:T(8,128)}, u32[]{:S(2)}) copy-start(s32[1,32,8]{1,2,0:T(8,128)} %param.14) | copy-start | bytes 3076
  57.2 4.1 %copy-start.10 = (f32[1,32,8]{1,2,0:T(8,128)S(1)}, f32[1,32,8]{1,2,0:T(8,128)}, u32[]{:S(2)}) copy-start(f32[1,32,8]{1,2,0:T(8,128)} %param.15) | copy-start | bytes 3076
  57.3 14.9 %collective-permute-start.1 = (bf16[64,2048]{1,0:T(8,128)(2,1)S(1)}, bf16[64,2048]{1,0:T(8,128)(2,1)}, u32[]{:S(2)}, u32[]{:S(2)}) collective-permute-start(bf16[64,2048]{1,0:T(8,128)(2,1)S(1)} %bitcast.16), channel_id=1, source_target_pairs={{0,8},{1,9},{2,10},{3,11},{4,12},{5,13},{6,14},{7,15},{8,0},{9,1},... | collective-permute-start | bytes 786440 | tf_op jit(solution)/shard_map/ppermute | solution.py:421
  57.6 14.5 %collective-permute-start = (bf16[64,2048]{1,0:T(8,128)(2,1)S(1)}, bf16[64,2048]{1,0:T(8,128)(2,1)}, u32[]{:S(2)}, u32[]{:S(2)}) collective-permute-start(bf16[64,2048]{1,0:T(8,128)(2,1)S(1)} %bitcast.17), channel_id=1, source_target_pairs={{0,4},{1,5},{2,6},{3,7},{4,0},{5,1},{6,2},{7,3},{8,12},{9,13},{10,... | collective-permute-start | bytes 786440 | tf_op jit(solution)/shard_map/ppermute | solution.py:421
  59.4 1.2 copy-start.2
  66.2 14.8 %collective-permute-start.6 = (bf16[2048,128]{1,0:T(8,128)(2,1)}, bf16[2048,128]{1,0:T(8,128)(2,1)S(1)}, u32[]{:S(2)}, u32[]{:S(2)}) collective-permute-start(bf16[2048,128]{1,0:T(8,128)(2,1)} %collective-permute-done.4.w2), channel_id=1, source_target_pairs={{0,1},{1,0},{2,3},{3,2},{4,5},{5,4},{6,7},{7,6},{8,9},{9,8},{10,11... | collective-permute-start | bytes 1572872 | tf_op jit(solution)/shard_map/ppermute | solution.py:418
  66.2 14.7 %collective-permute-start.5 = (bf16[2048,128]{1,0:T(8,128)(2,1)}, bf16[2048,128]{1,0:T(8,128)(2,1)S(1)}, u32[]{:S(2)}, u32[]{:S(2)}) collective-permute-start(bf16[2048,128]{1,0:T(8,128)(2,1)} %w0.1), channel_id=1, source_target_pairs={{0,1},{1,0},{2,3},{3,2},{4,5},{5,4},{6,7},{7,6},{8,9},{9,8},{10,11... | collective-permute-start | bytes 1572872 | tf_op jit(solution)/shard_map/ppermute | solution.py:418
  72.1 8.8 %collective-permute-start.3 = (bf16[64,2048]{1,0:T(8,128)(2,1)}, bf16[64,2048]{1,0:T(8,128)(2,1)S(1)}, u32[]{:S(2)}, u32[]{:S(2)}) collective-permute-start(bf16[64,2048]{1,0:T(8,128)(2,1)} %collective-permute-done.1.a2), channel_id=1, source_target_pairs={{0,4},{1,5},{2,6},{3,7},{4,0},{5,1},{6,2},{7,3},{8,12},{9,13},{10,... | collective-permute-start | bytes 786440 | tf_op jit(solution)/shard_map/ppermute | solution.py:421
  73.1 19.1 %copy-start.3 = (bf16[1024,768]{1,0:T(8,128)(2,1)S(1)}, bf16[1024,768]{1,0:T(8,128)(2,1)}, u32[]{:S(2)}) copy-start(bf16[1024,768]{1,0:T(8,128)(2,1)} %copy-done.2) | copy-start | bytes 4718596
  73.1 37.8 %copy-start.6 = (f32[2048]{0:T(1024)S(1)}, f32[2048]{0:T(1024)}, u32[]{:S(2)}) copy-start(f32[2048]{0:T(1024)} %param.13) | copy-start | bytes 24580
  73.1 10.6 %collective-permute-start.8 = (bf16[64,512]{1,0:T(8,128)(2,1)S(1)}, bf16[64,512]{1,0:T(8,128)(2,1)S(1)}, u32[]{:S(2)}, u32[]{:S(2)}) collective-permute-start(bf16[64,512]{1,0:T(8,128)(2,1)S(1)} %pad_maximum_fusion), channel_id=1, source_target_pairs={{0,4},{1,5},{2,6},{3,7},{4,0},{5,1},{6,2},{7,3},{8,12},{9,13},{10,... | collective-permute-start | bytes 196616 | tf_op jit(solution)/shard_map/ppermute | solution.py:421
  87.2 5.0 %collective-permute-start.9 = (bf16[128,512]{1,0:T(8,128)(2,1)S(1)}, bf16[128,512]{1,0:T(8,128)(2,1)S(1)}, u32[]{:S(2)}, u32[]{:S(2)}) collective-permute-start(bf16[128,512]{1,0:T(8,128)(2,1)S(1)} %get-tuple-element.50), channel_id=1, source_target_pairs={{0,16},{16,0},{1,17},{17,1},{2,18},{18,2},{3,19},{19,3},{4,20},{20... | collective-permute-start | bytes 393224 | tf_op jit(solution)/shard_map/ppermute | solution.py:399
  92.2 34.4 %collective-permute-start.19 = (bf16[1024,768]{1,0:T(8,128)(2,1)S(1)}, bf16[1024,768]{1,0:T(8,128)(2,1)S(1)}, u32[]{:S(2)}, u32[]{:S(2)}) collective-permute-start(bf16[1024,768]{1,0:T(8,128)(2,1)S(1)} %copy-done.3), channel_id=1, source_target_pairs={{0,16},{16,0},{1,17},{17,1},{2,18},{18,2},{3,19},{19,3},{4,20},{20... | collective-permute-start | bytes 4718600 | tf_op jit(solution)/shard_map/ppermute | solution.py:399
  94.0 7.7 %collective-permute-start.12 = (bf16[144,512]{1,0:T(8,128)(2,1)S(1)}, bf16[144,512]{1,0:T(8,128)(2,1)S(1)}, u32[]{:S(2)}, u32[]{:S(2)}) collective-permute-start(bf16[144,512]{1,0:T(8,128)(2,1)S(1)} %stream.1.b0), channel_id=1, source_target_pairs={{0,12},{1,13},{2,14},{3,15},{4,0},{5,1},{6,2},{7,3},{8,4},{9,5},{1... | collective-permute-start | bytes 442376 | tf_op jit(solution)/shard_map/ppermute | solution.py:402
  97.7 11.2 %collective-permute-start.11 = (bf16[144,512]{1,0:T(8,128)(2,1)S(1)}, bf16[144,512]{1,0:T(8,128)(2,1)S(1)}, u32[]{:S(2)}, u32[]{:S(2)}) collective-permute-start(bf16[144,512]{1,0:T(8,128)(2,1)S(1)} %stream.1.b0), channel_id=1, source_target_pairs={{0,8},{1,9},{2,10},{3,11},{4,12},{5,13},{6,14},{7,15},{8,0},{9,1},... | collective-permute-start | bytes 442376 | tf_op jit(solution)/shard_map/ppermute | solution.py:402
  97.7 12.7 %collective-permute-start.10 = (bf16[144,512]{1,0:T(8,128)(2,1)S(1)}, bf16[144,512]{1,0:T(8,128)(2,1)S(1)}, u32[]{:S(2)}, u32[]{:S(2)}) collective-permute-start(bf16[144,512]{1,0:T(8,128)(2,1)S(1)} %stream.1.b0), channel_id=1, source_target_pairs={{0,4},{1,5},{2,6},{3,7},{4,8},{5,9},{6,10},{7,11},{8,12},{9,13},{1... | collective-permute-start | bytes 442376 | tf_op jit(solution)/shard_map/ppermute | solution.py:402
  98.7 12.5 %collective-permute-start.13 = (bf16[144,512]{1,0:T(8,128)(2,1)S(1)}, bf16[144,512]{1,0:T(8,128)(2,1)S(1)}, u32[]{:S(2)}, u32[]{:S(2)}) collective-permute-start(bf16[144,512]{1,0:T(8,128)(2,1)S(1)} %stream.1.b0), channel_id=1, source_target_pairs={{0,2},{1,3},{2,0},{3,1},{4,6},{5,7},{6,4},{7,5},{8,10},{9,11},{10,... | collective-permute-start | bytes 442376 | tf_op jit(solution)/shard_map/ppermute | solution.py:418
  101.7 9.6 %collective-permute-start.16 = (bf16[144,512]{1,0:T(8,128)(2,1)S(1)}, bf16[144,512]{1,0:T(8,128)(2,1)S(1)}, u32[]{:S(2)}, u32[]{:S(2)}) collective-permute-start(bf16[144,512]{1,0:T(8,128)(2,1)S(1)} %collective-permute-done.12.b3), channel_id=1, source_target_pairs={{0,2},{1,3},{2,0},{3,1},{4,6},{5,7},{6,4},{7,5},{8,10},{9,11},{10,... | collective-permute-start | bytes 442376 | tf_op jit(solution)/shard_map/ppermute | solution.py:418
  108.9 5.6 %collective-permute-start.15 = (bf16[144,512]{1,0:T(8,128)(2,1)S(1)}, bf16[144,512]{1,0:T(8,128)(2,1)S(1)}, u32[]{:S(2)}, u32[]{:S(2)}) collective-permute-start(bf16[144,512]{1,0:T(8,128)(2,1)S(1)} %collective-permute-done.11.b2), channel_id=1, source_target_pairs={{0,2},{1,3},{2,0},{3,1},{4,6},{5,7},{6,4},{7,5},{8,10},{9,11},{10,... | collective-permute-start | bytes 442376 | tf_op jit(solution)/shard_map/ppermute | solution.py:418
  110.3 5.6 %collective-permute-start.14 = (bf16[144,512]{1,0:T(8,128)(2,1)S(1)}, bf16[144,512]{1,0:T(8,128)(2,1)S(1)}, u32[]{:S(2)}, u32[]{:S(2)}) collective-permute-start(bf16[144,512]{1,0:T(8,128)(2,1)S(1)} %collective-permute-done.10.b1), channel_id=1, source_target_pairs={{0,2},{1,3},{2,0},{3,1},{4,6},{5,7},{6,4},{7,5},{8,10},{9,11},{10,... | collective-permute-start | bytes 442376 | tf_op jit(solution)/shard_map/ppermute | solution.py:418
  111.2 5.6 %collective-permute-start.18 = (bf16[128,2176]{1,0:T(8,128)(2,1)S(1)}, bf16[128,2176]{1,0:T(8,128)(2,1)S(1)}, u32[]{:S(2)}, u32[]{:S(2)}) collective-permute-start(bf16[128,2176]{1,0:T(8,128)(2,1)S(1)} %get-tuple-element.54.group), channel_id=1, source_target_pairs={{0,1},{1,0},{2,3},{3,2},{4,5},{5,4},{6,7},{7,6},{8,9},{9,8},{10,11... | collective-permute-start | bytes 1671176 | tf_op jit(solution)/shard_map/ppermute | solution.py:418
  116.8 2.0 %collective-permute-start.17 = (bf16[128,2176]{1,0:T(8,128)(2,1)S(1)}, bf16[128,2176]{1,0:T(8,128)(2,1)S(1)}, u32[]{:S(2)}, u32[]{:S(2)}) collective-permute-start(bf16[128,2176]{1,0:T(8,128)(2,1)S(1)} %get-tuple-element.53.group_x), channel_id=1, source_target_pairs={{0,1},{1,0},{2,3},{3,2},{4,5},{5,4},{6,7},{7,6},{8,9},{9,8},{10,11... | collective-permute-start | bytes 1671176 | tf_op jit(solution)/shard_map/ppermute | solution.py:418
  126.6 1.4 copy-start.1
  129.0 2.0 %collective-permute-start.22 = (bf16[128,512]{1,0:T(8,128)(2,1)S(1)}, bf16[128,512]{1,0:T(8,128)(2,1)S(1)}, u32[]{:S(2)}, u32[]{:S(2)}) collective-permute-start(bf16[128,512]{1,0:T(8,128)(2,1)S(1)} %get-tuple-element.66), channel_id=1, source_target_pairs={{0,1},{1,0},{2,3},{3,2},{4,5},{5,4},{6,7},{7,6},{8,9},{9,8},{10,11... | collective-permute-start | bytes 393224 | tf_op jit(solution)/shard_map/ppermute | solution.py:418
  129.1 1.9 %collective-permute-start.23 = (bf16[128,512]{1,0:T(8,128)(2,1)S(1)}, bf16[128,512]{1,0:T(8,128)(2,1)S(1)}, u32[]{:S(2)}, u32[]{:S(2)}) collective-permute-start(bf16[128,512]{1,0:T(8,128)(2,1)S(1)} %get-tuple-element.67), channel_id=1, source_target_pairs={{0,1},{1,0},{2,3},{3,2},{4,5},{5,4},{6,7},{7,6},{8,9},{9,8},{10,11... | collective-permute-start | bytes 393224 | tf_op jit(solution)/shard_map/ppermute | solution.py:418
  129.6 12.0 %collective-permute-start.31 = (bf16[256,768]{1,0:T(8,128)(2,1)S(1)}, bf16[256,768]{1,0:T(8,128)(2,1)S(1)}, u32[]{:S(2)}, u32[]{:S(2)}) collective-permute-start(bf16[256,768]{1,0:T(8,128)(2,1)S(1)} %get-tuple-element.60.far), channel_id=1, source_target_pairs={{0,16},{16,0},{1,17},{17,1},{2,18},{18,2},{3,19},{19,3},{4,20},{20... | collective-permute-start | bytes 1179656 | tf_op jit(solution)/shard_map/ppermute | solution.py:399
  131.1 10.5 %collective-permute-start.24 = (bf16[128,1024]{1,0:T(8,128)(2,1)S(1)}, bf16[128,1024]{1,0:T(8,128)(2,1)S(1)}, u32[]{:S(2)}, u32[]{:S(2)}) collective-permute-start(bf16[128,1024]{1,0:T(8,128)(2,1)S(1)} %fold.2), channel_id=1, source_target_pairs={{0,2},{1,3},{2,0},{3,1},{4,6},{5,7},{6,4},{7,5},{8,10},{9,11},{10,... | collective-permute-start | bytes 786440 | tf_op jit(solution)/shard_map/ppermute | solution.py:418
  132.7 18.3 %collective-permute-start.28 = (bf16[256,768]{1,0:T(8,128)(2,1)S(1)}, bf16[256,768]{1,0:T(8,128)(2,1)S(1)}, u32[]{:S(2)}, u32[]{:S(2)}) collective-permute-start(bf16[256,768]{1,0:T(8,128)(2,1)S(1)} %get-tuple-element.61.near), channel_id=1, source_target_pairs={{0,16},{16,0},{1,17},{17,1},{2,18},{18,2},{3,19},{19,3},{4,20},{20... | collective-permute-start | bytes 1179656 | tf_op jit(solution)/shard_map/ppermute | solution.py:399
  142.2 1.4 collective-permute-start.32
  142.3 1.5 collective-permute-start.33
  142.8 2.5 %collective-permute-start.20 = (bf16[128,512]{1,0:T(8,128)(2,1)S(1)}, bf16[128,512]{1,0:T(8,128)(2,1)S(1)}, u32[]{:S(2)}, u32[]{:S(2)}) collective-permute-start(bf16[128,512]{1,0:T(8,128)(2,1)S(1)} %get-tuple-element.63), channel_id=1, source_target_pairs={{0,1},{1,0},{2,3},{3,2},{4,5},{5,4},{6,7},{7,6},{8,9},{9,8},{10,11... | collective-permute-start | bytes 393224 | tf_op jit(solution)/shard_map/ppermute | solution.py:418
  142.8 2.5 %collective-permute-start.21 = (bf16[128,512]{1,0:T(8,128)(2,1)S(1)}, bf16[128,512]{1,0:T(8,128)(2,1)S(1)}, u32[]{:S(2)}, u32[]{:S(2)}) collective-permute-start(bf16[128,512]{1,0:T(8,128)(2,1)S(1)} %get-tuple-element.64), channel_id=1, source_target_pairs={{0,1},{1,0},{2,3},{3,2},{4,5},{5,4},{6,7},{7,6},{8,9},{9,8},{10,11... | collective-permute-start | bytes 393224 | tf_op jit(solution)/shard_map/ppermute | solution.py:418
  143.9 12.9 %collective-permute-start.34 = (bf16[128,1024]{1,0:T(8,128)(2,1)S(1)}, bf16[128,1024]{1,0:T(8,128)(2,1)S(1)}, u32[]{:S(2)}, u32[]{:S(2)}) collective-permute-start(bf16[128,1024]{1,0:T(8,128)(2,1)S(1)} %fold.3), channel_id=1, source_target_pairs={{0,2},{1,3},{2,0},{3,1},{4,6},{5,7},{6,4},{7,5},{8,10},{9,11},{10,... | collective-permute-start | bytes 786440 | tf_op jit(solution)/shard_map/ppermute | solution.py:418
  145.4 23.3 %copy-start.8 = (f32[2048]{0:T(1024)S(1)}, f32[2048]{0:T(1024)}, u32[]{:S(2)}) copy-start(f32[2048]{0:T(1024)} %param.19) | copy-start | bytes 24580
  145.4 6.4 %collective-permute-start.25 = (bf16[32,1024]{1,0:T(8,128)(2,1)S(1)}, bf16[32,1024]{1,0:T(8,128)(2,1)S(1)}, u32[]{:S(2)}, u32[]{:S(2)}) collective-permute-start(bf16[32,1024]{1,0:T(8,128)(2,1)S(1)} %get-tuple-element.69), channel_id=1, source_target_pairs={{0,4},{1,5},{2,6},{3,7},{4,8},{5,9},{6,10},{7,11},{8,12},{9,13},{1... | collective-permute-start | bytes 196616 | tf_op jit(solution)/shard_map/ppermute | solution.py:402
  147.1 7.3 %collective-permute-start.26 = (bf16[32,1024]{1,0:T(8,128)(2,1)S(1)}, bf16[32,1024]{1,0:T(8,128)(2,1)S(1)}, u32[]{:S(2)}, u32[]{:S(2)}) collective-permute-start(bf16[32,1024]{1,0:T(8,128)(2,1)S(1)} %get-tuple-element.70), channel_id=1, source_target_pairs={{0,8},{1,9},{2,10},{3,11},{4,12},{5,13},{6,14},{7,15},{8,0},{9,1},... | collective-permute-start | bytes 196616 | tf_op jit(solution)/shard_map/ppermute | solution.py:402
  149.6 4.9 %collective-permute-start.27 = (bf16[32,1024]{1,0:T(8,128)(2,1)S(1)}, bf16[32,1024]{1,0:T(8,128)(2,1)S(1)}, u32[]{:S(2)}, u32[]{:S(2)}) collective-permute-start(bf16[32,1024]{1,0:T(8,128)(2,1)S(1)} %get-tuple-element.71), channel_id=1, source_target_pairs={{0,12},{1,13},{2,14},{3,15},{4,0},{5,1},{6,2},{7,3},{8,4},{9,5},{1... | collective-permute-start | bytes 196616 | tf_op jit(solution)/shard_map/ppermute | solution.py:402
  155.1 1.4 collective-permute-start.29
  155.2 1.5 collective-permute-start.30
  156.8 6.5 %collective-permute-start.35 = (bf16[32,1024]{1,0:T(8,128)(2,1)S(1)}, bf16[32,1024]{1,0:T(8,128)(2,1)S(1)}, u32[]{:S(2)}, u32[]{:S(2)}) collective-permute-start(bf16[32,1024]{1,0:T(8,128)(2,1)S(1)} %get-tuple-element.80), channel_id=1, source_target_pairs={{0,16},{1,17},{2,18},{3,19},{4,20},{5,21},{6,22},{7,23},{8,24},{9,... | collective-permute-start | bytes 196616 | tf_op jit(solution)/shard_map/ppermute | solution.py:407
  158.4 7.6 %collective-permute-start.36 = (bf16[32,1024]{1,0:T(8,128)(2,1)S(1)}, bf16[32,1024]{1,0:T(8,128)(2,1)S(1)}, u32[]{:S(2)}, u32[]{:S(2)}) collective-permute-start(bf16[32,1024]{1,0:T(8,128)(2,1)S(1)} %get-tuple-element.81), channel_id=1, source_target_pairs={{0,20},{1,21},{2,22},{3,23},{4,24},{5,25},{6,26},{7,27},{8,28},{9,... | collective-permute-start | bytes 196616 | tf_op jit(solution)/shard_map/ppermute | solution.py:407
  160.0 8.1 %collective-permute-start.37 = (bf16[32,1024]{1,0:T(8,128)(2,1)S(1)}, bf16[32,1024]{1,0:T(8,128)(2,1)S(1)}, u32[]{:S(2)}, u32[]{:S(2)}) collective-permute-start(bf16[32,1024]{1,0:T(8,128)(2,1)S(1)} %get-tuple-element.82), channel_id=1, source_target_pairs={{0,24},{1,25},{2,26},{3,27},{4,28},{5,29},{6,30},{7,31},{8,16},{9,... | collective-permute-start | bytes 196616 | tf_op jit(solution)/shard_map/ppermute | solution.py:407
  162.8 5.9 %collective-permute-start.38 = (bf16[32,1024]{1,0:T(8,128)(2,1)S(1)}, bf16[32,1024]{1,0:T(8,128)(2,1)S(1)}, u32[]{:S(2)}, u32[]{:S(2)}) collective-permute-start(bf16[32,1024]{1,0:T(8,128)(2,1)S(1)} %get-tuple-element.83), channel_id=1, source_target_pairs={{0,28},{1,29},{2,30},{3,31},{4,16},{5,17},{6,18},{7,19},{8,20},{9,... | collective-permute-start | bytes 196616 | tf_op jit(solution)/shard_map/ppermute | solution.py:407

commit v9 on v8

--- a/solution.py
+++ b/solution.py
@@ -270,9 +270,8 @@
     ).astype(BF16)
 
 
-def first_gate_kernel(
-    group_x, group_cx, group, group_c, own, early, inner_ref, part_ref, other_ref, share_ref, mine_ref
-):
+def first_gate_kernel(group_x, group_cx, group, group_c, own, *refs):
+    *early, inner_ref, part_ref, other_ref, share_ref, mine_ref = refs
     expert, outer, inner, dp = seat()
     count = group.shape[0]
     half = other_ref.shape[1]
@@ -286,9 +285,13 @@
         share = jnp.sum(jnp.where(picked, share, 0.0), axis=1, keepdims=True)
         share_ref[rows, :] = jnp.broadcast_to(share, (count, 128))
     mine, other = mine_ref[...], other_ref[...]
-    gate = dot(mine, own[:, 0:cut]) + dot(other, early[:, 0:cut])
-    up = dot(mine, own[:, 2 * cut : 3 * cut]) + dot(other, early[:, cut : 2 * cut])
-    inner_ref[...] = swiglu(gate, up, share_ref[:, 0:1])
+    at = 0
+    for piece in early:
+        size = piece.shape[1] // 2
+        gate = dot(mine, own[:, at : at + size]) + dot(other, piece[:, 0:size])
+        up = dot(mine, own[:, 2 * cut + at : 2 * cut + at + size]) + dot(other, piece[:, size:])
+        inner_ref[:, at : at + size] = swiglu(gate, up, share_ref[:, 0:1])
+        at += size
     part_ref[:, 0:cut] = dot(mine, own[:, cut : 2 * cut])
     part_ref[:, cut : 2 * cut] = dot(mine, own[:, 3 * cut : 4 * cut])
 
@@ -423,17 +426,20 @@
     def after(x, *results):
         return lax.optimization_barrier((x, *results))[0]
 
-    def weight_piece(first, size, mib=8):
+    def weight_piece(first, size):
         return pl.pallas_call(
             functools.partial(piece_kernel, (first, hidden + first)),
             out_shape=shape_of(half_width, 2 * size),
             in_specs=[pl.BlockSpec(memory_space=pl.ANY)],
-            out_specs=pl.BlockSpec(memory_space=pl.ANY),
+            out_specs=vmem,
             scratch_shapes=[pltpu.SemaphoreType.DMA((2, 4))],
-            compiler_params=kernel_params(mib),
+            compiler_params=kernel_params(8),
             cost_estimate=small_cost(),
             name="weight_piece",
         )(w_gate_up[0])
+
+    def weight_pieces(first, sizes):
+        return [weight_piece(first + sum(sizes[:i]), size) for i, size in enumerate(sizes)]
 
     piece = shape_of(rows_here, quarter)
     r_own, r_1, r_23 = call(
@@ -450,12 +456,9 @@
         first=smem,
     )
     cut_width = hidden // 2
-    early_piece = weight_piece(0, cut_width, 60)
-    late_sizes = (cut_width * 384 // 384,)
-    late_pieces = [
-        weight_piece(cut_width + sum(late_sizes[:i]), size) for i, size in enumerate(late_sizes)
-    ]
-    gate_up_early = swap_dp(early_piece)
+    early_pieces = weight_pieces(0, (cut_width * 384 // 384,))
+    late_pieces = weight_pieces(cut_width, (cut_width * 384 // 384,))
+    gate_up_early = [swap_dp(piece) for piece in early_pieces]
     a = [attn[0], swap_outer(attn[0], 1), swap_outer(attn[0], 2)]
     w_x = swap_inner(w_out, 2)
     r_2 = swap_outer(r_23, 2)
@@ -480,7 +483,7 @@
             pltpu.VMEM((8 * rows_here, quarter), BF16),
         ),
     )
-    arrived = swap_dp(after(send, gate_up_early, r_13))
+    arrived = swap_dp(after(send, gate_up_early[0], r_13))
     gate_up_late = [swap_dp(after(piece, arrived)) for piece in late_pieces]
     (block,) = call(
         stream_kernel,
@@ -523,7 +526,7 @@
         group,
         group_c,
         w_gate_up[0],
-        gate_up_early,
+        *gate_up_early,
         scratch=(pltpu.VMEM((row_total, half_width), BF16),),
     )
     inner_half = shape_of(half_rows, hidden)

time: 170 us -> 124 us (0.73)
  Pallas kernels: 63.6 us -> 14.9 us
  waiting for transfers between devices: 57.7 us -> 59.5 us
    pallas_call x2, Pallas kernels: 49.1 us -> 1.68 us  [weight_piece(): pl.pallas_call(functools.partial(piece_kernel, (first, hidden + first)),...]
  transfers between devices with their start and end apart: 39 -> 39, of which waited for: 22 -> 22; matrix products, arithmetic and copies ran while one was open for 1% -> 1% of each run, Pallas kernels for 7% -> 8%
where the time goes in v9:
time: 124 us
  waiting for transfers between devices  59.5 us (48%)
  starting transfers between devices  44.5 us (36%)
  Pallas kernels  14.9 us (12%)
  local copies, waits for them, and re-layouts  2.72 us (2%)
  between operations  1.49 us (1%)
    ppermute x5, waiting for transfers between devices, swap_dp(): return lax.ppermute(x, 'dp', [(0, 1), (1, 0)])  18.3 us
    pallas_call x16, Pallas kernels, call(): pl.pallas_call(kernel, out_shape=outs, in_specs=[first] + [vmem] * (len(a...  13.2 us
    ppermute x19, waiting for transfers between devices, swap_inner(): return lax.ppermute(x, 'expert', [(i, i ^ j) for i in range(expert_count)])  13.1 us
    ppermute x19, starting transfers between devices, swap_inner(): return lax.ppermute(x, 'expert', [(i, i ^ j) for i in range(expert_count)])  12.3 us
    ppermute x5, waiting for transfers between devices, swap_outer(): lax.ppermute(x, 'expert', [(i, i ^ 4 * s) for i in range(expert_count)])  12.1 us
    ppermute x6, waiting for transfers between devices, shift_outer(): lax.ppermute(x, 'expert', [(i, (i + 4 * s) % expert_count) for i in range...  10.7 us
    ppermute x6, starting transfers between devices, shift_outer(): lax.ppermute(x, 'expert', [(i, (i + 4 * s) % expert_count) for i in range...  10.2 us
    ppermute x5, starting transfers between devices, swap_dp(): return lax.ppermute(x, 'dp', [(0, 1), (1, 0)])  8.95 us
  transfers between devices with their start and end apart: 39, of which 22 were waited for; matrix products, arithmetic and copies ran while one was open for 1% of the time, Pallas kernels for 8%

profile of v9, /device:TPU:0, one launch (start us, length us, event | category | flops | bytes accessed | tf_op | source)
XLA Modules:
  0.0 123.8 jit_solution(5242941222455306175)
XLA Ops:
  0.6 1.9 %copy-done = bf16[1,1024,1536]{2,1,0:T(8,128)(2,1)S(1)} copy-done((bf16[1,1024,1536]{2,1,0:T(8,128)(2,1)S(1)}, bf16[1,1024,1536]{2,1,0:T(8,128)(2,1)}, u32[]{:S(2)}) %copy-start) | copy-done | bytes 3145752
  2.5 1.4 %weight_piece.3 = bf16[1024,768]{1,0:T(8,128)(2,1)} custom-call(bf16[1024,1536]{1,0:T(8,128)(2,1)S(1)} %bitcast.10), custom_call_target="tpu_custom_call" | custom-call | flops 1 | bytes 1 | tf_op jit(solution)/shard_map/weight_piece/pallas_call | solution.py:430
  4.0 3.0 %collective-permute-start.7 = (bf16[1024,768]{1,0:T(8,128)(2,1)}, bf16[1024,768]{1,0:T(8,128)(2,1)S(1)}, u32[]{:S(2)}, u32[]{:S(2)}) collective-permute-start(bf16[1024,768]{1,0:T(8,128)(2,1)} %weight_piece.3), channel_id=1, source_target_pairs={{0,16},{16,0},{1,17},{17,1},{2,18},{18,2},{3,19},{19,3},{4,20},{20... | collective-permute-start | bytes 4718600 | tf_op jit(solution)/shard_map/ppermute | solution.py:402
  7.0 1.5 %collective-permute-start.4 = (bf16[2048,128]{1,0:T(8,128)(2,1)}, bf16[2048,128]{1,0:T(8,128)(2,1)}, u32[]{:S(2)}, u32[]{:S(2)}) collective-permute-start(bf16[2048,128]{1,0:T(8,128)(2,1)} %w0.1), channel_id=1, source_target_pairs={{0,2},{1,3},{2,0},{3,1},{4,6},{5,7},{6,4},{7,5},{8,10},{9,11},{10,... | collective-permute-start | bytes 1572872 | tf_op jit(solution)/shard_map/ppermute | solution.py:421
  8.5 0.6 cut_resid.1
  9.1 0.6 copy-done.6
  9.7 2.6 %collective-permute-start.2 = (bf16[64,512]{1,0:T(8,128)(2,1)}, bf16[64,512]{1,0:T(8,128)(2,1)S(1)}, u32[]{:S(2)}, u32[]{:S(2)}) collective-permute-start(bf16[64,512]{1,0:T(8,128)(2,1)} %get-tuple-element.44), channel_id=1, source_target_pairs={{0,8},{1,9},{2,10},{3,11},{4,12},{5,13},{6,14},{7,15},{8,0},{9,1},... | collective-permute-start | bytes 196616 | tf_op jit(solution)/shard_map/ppermute | solution.py:424
  12.3 0.3 collective-permute-start.1
  12.7 1.6 %collective-permute-start = (bf16[64,2048]{1,0:T(8,128)(2,1)S(1)}, bf16[64,2048]{1,0:T(8,128)(2,1)}, u32[]{:S(2)}, u32[]{:S(2)}) collective-permute-start(bf16[64,2048]{1,0:T(8,128)(2,1)S(1)} %bitcast.17), channel_id=1, source_target_pairs={{0,4},{1,5},{2,6},{3,7},{4,0},{5,1},{6,2},{7,3},{8,12},{9,13},{10,... | collective-permute-start | bytes 786440 | tf_op jit(solution)/shard_map/ppermute | solution.py:424
  15.3 0.5 share.1
  15.8 4.9 %collective-permute-done.4.w2 = bf16[2048,128]{1,0:T(8,128)(2,1)} collective-permute-done((bf16[2048,128]{1,0:T(8,128)(2,1)}, bf16[2048,128]{1,0:T(8,128)(2,1)}, u32[]{:S(2)}, u32[]{:S(2)}) %collective-permute-start.4) | collective-permute-done | bytes 524320 | tf_op jit(solution)/shard_map/ppermute | solution.py:421
  20.7 0.5 collective-permute-start.5
  21.2 6.0 %collective-permute-done.1.a2 = bf16[64,2048]{1,0:T(8,128)(2,1)} collective-permute-done((bf16[64,2048]{1,0:T(8,128)(2,1)S(1)}, bf16[64,2048]{1,0:T(8,128)(2,1)}, u32[]{:S(2)}, u32[]{:S(2)}) %collective-permute-start.1) | collective-permute-done | bytes 262176 | tf_op jit(solution)/shard_map/ppermute | solution.py:424
  27.4 0.8 pad_maximum_fusion
  28.2 1.8 %collective-permute-start.8 = (bf16[64,512]{1,0:T(8,128)(2,1)S(1)}, bf16[64,512]{1,0:T(8,128)(2,1)S(1)}, u32[]{:S(2)}, u32[]{:S(2)}) collective-permute-start(bf16[64,512]{1,0:T(8,128)(2,1)S(1)} %pad_maximum_fusion), channel_id=1, source_target_pairs={{0,4},{1,5},{2,6},{3,7},{4,0},{5,1},{6,2},{7,3},{8,12},{9,13},{10,... | collective-permute-start | bytes 196616 | tf_op jit(solution)/shard_map/ppermute | solution.py:424
  30.0 6.0 %collective-permute-done.3.a3 = bf16[64,2048]{1,0:T(8,128)(2,1)S(1)} collective-permute-done((bf16[64,2048]{1,0:T(8,128)(2,1)}, bf16[64,2048]{1,0:T(8,128)(2,1)S(1)}, u32[]{:S(2)}, u32[]{:S(2)}) %collective-permute-start.3) | collective-permute-done | bytes 262176 | tf_op jit(solution)/shard_map/ppermute | solution.py:424
  36.1 2.8 %projection.1 = (bf16[128,512]{1,0:T(8,128)(2,1)S(1)}, bf16[128,512]{1,0:T(8,128)(2,1)S(1)}) custom-call(bf16[64,2048]{1,0:T(8,128)(2,1)S(1)} %bitcast.18, bf16[64,2048]{1,0:T(8,128)(2,1)} %collective-permute-done.a1, bf16[64,2048]{1,0:T(8,128)(2,1)} %collective-permute-done.1.a2, bf16[64,2048]{1,0:T(8,128)(2,1)S(1)} %collective-permute-done.3.a3, ...), custom_call_target="tpu_custom_call" | custom-call | flops 1 | bytes 1 | tf_op jit(solution)/shard_map/projection/pallas_call | solution.py:390
  38.9 2.7 %collective-permute-done.7.refs_0_ = bf16[1024,768]{1,0:T(8,128)(2,1)S(1)} collective-permute-done((bf16[1024,768]{1,0:T(8,128)(2,1)}, bf16[1024,768]{1,0:T(8,128)(2,1)S(1)}, u32[]{:S(2)}, u32[]{:S(2)}) %collective-permute-start.7) | collective-permute-done | bytes 1572896 | tf_op jit(solution)/shard_map/ppermute | solution.py:402
  41.6 1.7 %collective-permute-start.9 = (bf16[128,512]{1,0:T(8,128)(2,1)S(1)}, bf16[128,512]{1,0:T(8,128)(2,1)S(1)}, u32[]{:S(2)}, u32[]{:S(2)}) collective-permute-start(bf16[128,512]{1,0:T(8,128)(2,1)S(1)} %get-tuple-element.50), channel_id=1, source_target_pairs={{0,16},{16,0},{1,17},{17,1},{2,18},{18,2},{3,19},{19,3},{4,20},{20... | collective-permute-start | bytes 393224 | tf_op jit(solution)/shard_map/ppermute | solution.py:402
  43.3 3.2 %collective-permute-done.9.arrived = bf16[128,512]{1,0:T(8,128)(2,1)S(1)} collective-permute-done((bf16[128,512]{1,0:T(8,128)(2,1)S(1)}, bf16[128,512]{1,0:T(8,128)(2,1)S(1)}, u32[]{:S(2)}, u32[]{:S(2)}) %collective-permute-start.9) | collective-permute-done | bytes 131104 | tf_op jit(solution)/shard_map/ppermute | solution.py:402
  46.6 1.7 %collective-permute-start.19 = (bf16[1024,768]{1,0:T(8,128)(2,1)S(1)}, bf16[1024,768]{1,0:T(8,128)(2,1)S(1)}, u32[]{:S(2)}, u32[]{:S(2)}) collective-permute-start(bf16[1024,768]{1,0:T(8,128)(2,1)S(1)} %weight_piece.2), channel_id=1, source_target_pairs={{0,16},{16,0},{1,17},{17,1},{2,18},{18,2},{3,19},{19,3},{4,20},{20... | collective-permute-start | bytes 4718600 | tf_op jit(solution)/shard_map/ppermute | solution.py:402
  48.4 3.7 %collective-permute-start.12 = (bf16[144,512]{1,0:T(8,128)(2,1)S(1)}, bf16[144,512]{1,0:T(8,128)(2,1)S(1)}, u32[]{:S(2)}, u32[]{:S(2)}) collective-permute-start(bf16[144,512]{1,0:T(8,128)(2,1)S(1)} %stream.1.b0), channel_id=1, source_target_pairs={{0,12},{1,13},{2,14},{3,15},{4,0},{5,1},{6,2},{7,3},{8,4},{9,5},{1... | collective-permute-start | bytes 442376 | tf_op jit(solution)/shard_map/ppermute | solution.py:405
  52.0 1.0 collective-permute-start.10
  53.0 1.5 %collective-permute-start.13 = (bf16[144,512]{1,0:T(8,128)(2,1)S(1)}, bf16[144,512]{1,0:T(8,128)(2,1)S(1)}, u32[]{:S(2)}, u32[]{:S(2)}) collective-permute-start(bf16[144,512]{1,0:T(8,128)(2,1)S(1)} %stream.1.b0), channel_id=1, source_target_pairs={{0,2},{1,3},{2,0},{3,1},{4,6},{5,7},{6,4},{7,5},{8,10},{9,11},{10,... | collective-permute-start | bytes 442376 | tf_op jit(solution)/shard_map/ppermute | solution.py:421
  54.5 1.5 %collective-permute-done.12.b3 = bf16[144,512]{1,0:T(8,128)(2,1)S(1)} collective-permute-done((bf16[144,512]{1,0:T(8,128)(2,1)S(1)}, bf16[144,512]{1,0:T(8,128)(2,1)S(1)}, u32[]{:S(2)}, u32[]{:S(2)}) %collective-permute-start.12) | collective-permute-done | bytes 147488 | tf_op jit(solution)/shard_map/ppermute | solution.py:405
  56.0 1.5 %collective-permute-start.16 = (bf16[144,512]{1,0:T(8,128)(2,1)S(1)}, bf16[144,512]{1,0:T(8,128)(2,1)S(1)}, u32[]{:S(2)}, u32[]{:S(2)}) collective-permute-start(bf16[144,512]{1,0:T(8,128)(2,1)S(1)} %collective-permute-done.12.b3), channel_id=1, source_target_pairs={{0,2},{1,3},{2,0},{3,1},{4,6},{5,7},{6,4},{7,5},{8,10},{9,11},{10,... | collective-permute-start | bytes 442376 | tf_op jit(solution)/shard_map/ppermute | solution.py:421
  57.5 5.7 %collective-permute-done.11.b2 = bf16[144,512]{1,0:T(8,128)(2,1)S(1)} collective-permute-done((bf16[144,512]{1,0:T(8,128)(2,1)S(1)}, bf16[144,512]{1,0:T(8,128)(2,1)S(1)}, u32[]{:S(2)}, u32[]{:S(2)}) %collective-permute-start.11) | collective-permute-done | bytes 147488 | tf_op jit(solution)/shard_map/ppermute | solution.py:405
  63.2 1.5 %collective-permute-start.15 = (bf16[144,512]{1,0:T(8,128)(2,1)S(1)}, bf16[144,512]{1,0:T(8,128)(2,1)S(1)}, u32[]{:S(2)}, u32[]{:S(2)}) collective-permute-start(bf16[144,512]{1,0:T(8,128)(2,1)S(1)} %collective-permute-done.11.b2), channel_id=1, source_target_pairs={{0,2},{1,3},{2,0},{3,1},{4,6},{5,7},{6,4},{7,5},{8,10},{9,11},{10,... | collective-permute-start | bytes 442376 | tf_op jit(solution)/shard_map/ppermute | solution.py:421
  64.7 0.5 collective-permute-start.14
  65.3 0.3 norm.2
  65.7 3.1 %collective-permute-done.15.b2 = bf16[144,512]{1,0:T(8,128)(2,1)S(1)} collective-permute-done((bf16[144,512]{1,0:T(8,128)(2,1)S(1)}, bf16[144,512]{1,0:T(8,128)(2,1)S(1)}, u32[]{:S(2)}, u32[]{:S(2)}) %collective-permute-start.15) | collective-permute-done | bytes 147488 | tf_op jit(solution)/shard_map/ppermute | solution.py:421
  68.8 1.6 %collective-permute-done.14.b1 = bf16[144,512]{1,0:T(8,128)(2,1)S(1)} collective-permute-done((bf16[144,512]{1,0:T(8,128)(2,1)S(1)}, bf16[144,512]{1,0:T(8,128)(2,1)S(1)}, u32[]{:S(2)}, u32[]{:S(2)}) %collective-permute-start.14) | collective-permute-done | bytes 147488 | tf_op jit(solution)/shard_map/ppermute | solution.py:421
  70.4 0.8 norm.3
  71.2 2.0 %collective-permute-done.17.group_cx = bf16[128,2176]{1,0:T(8,128)(2,1)S(1)} collective-permute-done((bf16[128,2176]{1,0:T(8,128)(2,1)S(1)}, bf16[128,2176]{1,0:T(8,128)(2,1)S(1)}, u32[]{:S(2)}, u32[]{:S(2)}) %collective-permute-start.17) | collective-permute-done | bytes 557088 | tf_op jit(solution)/shard_map/ppermute | solution.py:421
  73.1 3.4 %first_gate_up.1 = (bf16[512,384]{1,0:T(8,128)(2,1)S(1)}, f32[512,768]{1,0:T(8,128)S(1)}, bf16[512,1024]{1,0:T(8,128)(2,1)S(1)}, f32[512,128]{1,0:T(8,128)S(1)}) custom-call(bf16[128,2176]{1,0:T(8,128)(2,1)S(1)} %get-tuple-element.53.group_x, bf16[128,2176]{1,0:T(8,128)(2,1)S(1)} %collective-permute-done.17.group_cx, ...), custom_call_target="tpu_custom_call" | custom-call | flops 1 | bytes 1 | tf_op jit(solution)/shard_map/first_gate_up/pallas_call | solution.py:390
  76.5 4.5 %collective-permute-done.19.refs_0_ = bf16[1024,768]{1,0:T(8,128)(2,1)S(1)} collective-permute-done((bf16[1024,768]{1,0:T(8,128)(2,1)S(1)}, bf16[1024,768]{1,0:T(8,128)(2,1)S(1)}, u32[]{:S(2)}, u32[]{:S(2)}) %collective-permute-start.19) | collective-permute-done | bytes 1572896 | tf_op jit(solution)/shard_map/ppermute | solution.py:402
  81.0 1.4 %last_gate_up.1 = (bf16[256,768]{1,0:T(8,128)(2,1)S(1)}, bf16[256,768]{1,0:T(8,128)(2,1)S(1)}) custom-call(bf16[512,384]{1,0:T(8,128)(2,1)S(1)} %get-tuple-element.55.first, f32[512,768]{1,0:T(8,128)S(1)} %get-tuple-element.56.part, bf16[512,1024]{1,0:T(8,128)(2,1)S(1)} %get-tuple-element.57.other, f32[512,128]{1,0:T(8,128)S(1)} %get-tuple-element.58.share, ...), custom_call_target="tpu_custom_call" | custom-call | flops 1 | bytes 1 | tf_op jit(solution)/shard_map/last_gate_up/pallas_call | solution.py:390
  82.4 1.0 down_both.1
  83.5 0.5 collective-permute-start.23
  84.0 1.4 %collective-permute-start.31 = (bf16[256,768]{1,0:T(8,128)(2,1)S(1)}, bf16[256,768]{1,0:T(8,128)(2,1)S(1)}, u32[]{:S(2)}, u32[]{:S(2)}) collective-permute-start(bf16[256,768]{1,0:T(8,128)(2,1)S(1)} %get-tuple-element.60.far), channel_id=1, source_target_pairs={{0,16},{16,0},{1,17},{17,1},{2,18},{18,2},{3,19},{19,3},{4,20},{20... | collective-permute-start | bytes 1179656 | tf_op jit(solution)/shard_map/ppermute | solution.py:402
  85.5 1.6 %collective-permute-start.24 = (bf16[128,1024]{1,0:T(8,128)(2,1)S(1)}, bf16[128,1024]{1,0:T(8,128)(2,1)S(1)}, u32[]{:S(2)}, u32[]{:S(2)}) collective-permute-start(bf16[128,1024]{1,0:T(8,128)(2,1)S(1)} %fold.2), channel_id=1, source_target_pairs={{0,2},{1,3},{2,0},{3,1},{4,6},{5,7},{6,4},{7,5},{8,10},{9,11},{10,... | collective-permute-start | bytes 786440 | tf_op jit(solution)/shard_map/ppermute | solution.py:421
  87.0 1.0 collective-permute-start.28
  88.0 7.9 %collective-permute-done.31.rows = bf16[256,768]{1,0:T(8,128)(2,1)S(1)} collective-permute-done((bf16[256,768]{1,0:T(8,128)(2,1)S(1)}, bf16[256,768]{1,0:T(8,128)(2,1)S(1)}, u32[]{:S(2)}, u32[]{:S(2)}) %collective-permute-start.31) | collective-permute-done | bytes 393248 | tf_op jit(solution)/shard_map/ppermute | solution.py:402
  95.9 0.6 down.3
  96.6 0.5 collective-permute-start.33
  97.2 0.4 collective-permute-start.21
  97.6 0.3 collective-permute-done.32.core_a
  98.2 1.5 %collective-permute-start.34 = (bf16[128,1024]{1,0:T(8,128)(2,1)S(1)}, bf16[128,1024]{1,0:T(8,128)(2,1)S(1)}, u32[]{:S(2)}, u32[]{:S(2)}) collective-permute-start(bf16[128,1024]{1,0:T(8,128)(2,1)S(1)} %fold.3), channel_id=1, source_target_pairs={{0,2},{1,3},{2,0},{3,1},{4,6},{5,7},{6,4},{7,5},{8,10},{9,11},{10,... | collective-permute-start | bytes 786440 | tf_op jit(solution)/shard_map/ppermute | solution.py:421
  99.8 1.6 %collective-permute-start.25 = (bf16[32,1024]{1,0:T(8,128)(2,1)S(1)}, bf16[32,1024]{1,0:T(8,128)(2,1)S(1)}, u32[]{:S(2)}, u32[]{:S(2)}) collective-permute-start(bf16[32,1024]{1,0:T(8,128)(2,1)S(1)} %get-tuple-element.69), channel_id=1, source_target_pairs={{0,4},{1,5},{2,6},{3,7},{4,8},{5,9},{6,10},{7,11},{8,12},{9,13},{1... | collective-permute-start | bytes 196616 | tf_op jit(solution)/shard_map/ppermute | solution.py:405
  101.4 2.6 %collective-permute-start.26 = (bf16[32,1024]{1,0:T(8,128)(2,1)S(1)}, bf16[32,1024]{1,0:T(8,128)(2,1)S(1)}, u32[]{:S(2)}, u32[]{:S(2)}) collective-permute-start(bf16[32,1024]{1,0:T(8,128)(2,1)S(1)} %get-tuple-element.70), channel_id=1, source_target_pairs={{0,8},{1,9},{2,10},{3,11},{4,12},{5,13},{6,14},{7,15},{8,0},{9,1},... | collective-permute-start | bytes 196616 | tf_op jit(solution)/shard_map/ppermute | solution.py:405
  104.0 1.3 %collective-permute-start.27 = (bf16[32,1024]{1,0:T(8,128)(2,1)S(1)}, bf16[32,1024]{1,0:T(8,128)(2,1)S(1)}, u32[]{:S(2)}, u32[]{:S(2)}) collective-permute-start(bf16[32,1024]{1,0:T(8,128)(2,1)S(1)} %get-tuple-element.71), channel_id=1, source_target_pairs={{0,12},{1,13},{2,14},{3,15},{4,0},{5,1},{6,2},{7,3},{8,4},{9,5},{1... | collective-permute-start | bytes 196616 | tf_op jit(solution)/shard_map/ppermute | solution.py:405
  105.3 0.8 collective-permute-done.25.m1
  106.2 2.5 %collective-permute-done.26.m2 = bf16[32,1024]{1,0:T(8,128)(2,1)S(1)} collective-permute-done((bf16[32,1024]{1,0:T(8,128)(2,1)S(1)}, bf16[32,1024]{1,0:T(8,128)(2,1)S(1)}, u32[]{:S(2)}, u32[]{:S(2)}) %collective-permute-start.26) | collective-permute-done | bytes 65568 | tf_op jit(solution)/shard_map/ppermute | solution.py:405
  108.9 0.6 down.2
  109.5 0.5 collective-permute-start.30
  110.0 0.8 collective-permute-done.29.core_a
  111.1 1.6 %collective-permute-start.35 = (bf16[32,1024]{1,0:T(8,128)(2,1)S(1)}, bf16[32,1024]{1,0:T(8,128)(2,1)S(1)}, u32[]{:S(2)}, u32[]{:S(2)}) collective-permute-start(bf16[32,1024]{1,0:T(8,128)(2,1)S(1)} %get-tuple-element.80), channel_id=1, source_target_pairs={{0,16},{1,17},{2,18},{3,19},{4,20},{5,21},{6,22},{7,23},{8,24},{9,... | collective-permute-start | bytes 196616 | tf_op jit(solution)/shard_map/ppermute | solution.py:410
  112.7 1.6 %collective-permute-start.36 = (bf16[32,1024]{1,0:T(8,128)(2,1)S(1)}, bf16[32,1024]{1,0:T(8,128)(2,1)S(1)}, u32[]{:S(2)}, u32[]{:S(2)}) collective-permute-start(bf16[32,1024]{1,0:T(8,128)(2,1)S(1)} %get-tuple-element.81), channel_id=1, source_target_pairs={{0,20},{1,21},{2,22},{3,23},{4,24},{5,25},{6,26},{7,27},{8,28},{9,... | collective-permute-start | bytes 196616 | tf_op jit(solution)/shard_map/ppermute | solution.py:410
  114.3 2.8 %collective-permute-start.37 = (bf16[32,1024]{1,0:T(8,128)(2,1)S(1)}, bf16[32,1024]{1,0:T(8,128)(2,1)S(1)}, u32[]{:S(2)}, u32[]{:S(2)}) collective-permute-start(bf16[32,1024]{1,0:T(8,128)(2,1)S(1)} %get-tuple-element.82), channel_id=1, source_target_pairs={{0,24},{1,25},{2,26},{3,27},{4,28},{5,29},{6,30},{7,31},{8,16},{9,... | collective-permute-start | bytes 196616 | tf_op jit(solution)/shard_map/ppermute | solution.py:410
  117.1 0.5 collective-permute-start.38
  117.6 2.6 %collective-permute-done.36.o1 = bf16[32,1024]{1,0:T(8,128)(2,1)S(1)} collective-permute-done((bf16[32,1024]{1,0:T(8,128)(2,1)S(1)}, bf16[32,1024]{1,0:T(8,128)(2,1)S(1)}, u32[]{:S(2)}, u32[]{:S(2)}) %collective-permute-start.36) | collective-permute-done | bytes 65568 | tf_op jit(solution)/shard_map/ppermute | solution.py:410
  120.3 2.1 %collective-permute-done.37.o2 = bf16[32,1024]{1,0:T(8,128)(2,1)S(1)} collective-permute-done((bf16[32,1024]{1,0:T(8,128)(2,1)S(1)}, bf16[32,1024]{1,0:T(8,128)(2,1)S(1)}, u32[]{:S(2)}, u32[]{:S(2)}) %collective-permute-start.37) | collective-permute-done | bytes 65568 | tf_op jit(solution)/shard_map/ppermute | solution.py:410
  122.4 0.6 collective-permute-done.38.o3
  123.0 0.9 closing.1
  (56 shorter events, 2.0 us)
Async XLA Ops:
  0.6 1.9 %copy-start = (bf16[1,1024,1536]{2,1,0:T(8,128)(2,1)S(1)}, bf16[1,1024,1536]{2,1,0:T(8,128)(2,1)}, u32[]{:S(2)}) copy-start(bf16[1,1024,1536]{2,1,0:T(8,128)(2,1)} %param.17) | copy-start | bytes 9437188
  2.5 6.0 %copy-start.4 = (bf16[1,32,2048]{2,1,0:T(8,128)(2,1)S(1)}, bf16[1,32,2048]{2,1,0:T(8,128)(2,1)}, u32[]{:S(2)}) copy-start(bf16[1,32,2048]{2,1,0:T(8,128)(2,1)} %param.11) | copy-start | bytes 393220
  2.5 9.8 %copy-start.3 = (bf16[1,64,2048]{2,1,0:T(8,128)(2,1)S(1)}, bf16[1,64,2048]{2,1,0:T(8,128)(2,1)}, u32[]{:S(2)}) copy-start(bf16[1,64,2048]{2,1,0:T(8,128)(2,1)} %param.10) | copy-start | bytes 786436
  4.0 37.6 %collective-permute-start.7 = (bf16[1024,768]{1,0:T(8,128)(2,1)}, bf16[1024,768]{1,0:T(8,128)(2,1)S(1)}, u32[]{:S(2)}, u32[]{:S(2)}) collective-permute-start(bf16[1024,768]{1,0:T(8,128)(2,1)} %weight_piece.3), channel_id=1, source_target_pairs={{0,16},{16,0},{1,17},{17,1},{2,18},{18,2},{3,19},{19,3},{4,20},{20... | collective-permute-start | bytes 4718600 | tf_op jit(solution)/shard_map/ppermute | solution.py:402
  7.0 13.7 %collective-permute-start.4 = (bf16[2048,128]{1,0:T(8,128)(2,1)}, bf16[2048,128]{1,0:T(8,128)(2,1)}, u32[]{:S(2)}, u32[]{:S(2)}) collective-permute-start(bf16[2048,128]{1,0:T(8,128)(2,1)} %w0.1), channel_id=1, source_target_pairs={{0,2},{1,3},{2,0},{3,1},{4,6},{5,7},{6,4},{7,5},{8,10},{9,11},{10,... | collective-permute-start | bytes 1572872 | tf_op jit(solution)/shard_map/ppermute | solution.py:421
  9.1 0.6 copy-start.6
  9.7 11.0 %collective-permute-start.2 = (bf16[64,512]{1,0:T(8,128)(2,1)}, bf16[64,512]{1,0:T(8,128)(2,1)S(1)}, u32[]{:S(2)}, u32[]{:S(2)}) collective-permute-start(bf16[64,512]{1,0:T(8,128)(2,1)} %get-tuple-element.44), channel_id=1, source_target_pairs={{0,8},{1,9},{2,10},{3,11},{4,12},{5,13},{6,14},{7,15},{8,0},{9,1},... | collective-permute-start | bytes 196616 | tf_op jit(solution)/shard_map/ppermute | solution.py:424
  12.3 2.8 %copy-start.8 = (s32[1,32,8]{1,2,0:T(8,128)S(1)}, s32[1,32,8]{1,2,0:T(8,128)}, u32[]{:S(2)}) copy-start(s32[1,32,8]{1,2,0:T(8,128)} %param.14) | copy-start | bytes 3076
  12.3 2.9 %copy-start.9 = (f32[1,32,8]{1,2,0:T(8,128)S(1)}, f32[1,32,8]{1,2,0:T(8,128)}, u32[]{:S(2)}) copy-start(f32[1,32,8]{1,2,0:T(8,128)} %param.15) | copy-start | bytes 3076
  12.3 14.9 %collective-permute-start.1 = (bf16[64,2048]{1,0:T(8,128)(2,1)S(1)}, bf16[64,2048]{1,0:T(8,128)(2,1)}, u32[]{:S(2)}, u32[]{:S(2)}) collective-permute-start(bf16[64,2048]{1,0:T(8,128)(2,1)S(1)} %bitcast.16), channel_id=1, source_target_pairs={{0,8},{1,9},{2,10},{3,11},{4,12},{5,13},{6,14},{7,15},{8,0},{9,1},... | collective-permute-start | bytes 786440 | tf_op jit(solution)/shard_map/ppermute | solution.py:424
  12.7 14.5 %collective-permute-start = (bf16[64,2048]{1,0:T(8,128)(2,1)S(1)}, bf16[64,2048]{1,0:T(8,128)(2,1)}, u32[]{:S(2)}, u32[]{:S(2)}) collective-permute-start(bf16[64,2048]{1,0:T(8,128)(2,1)S(1)} %bitcast.17), channel_id=1, source_target_pairs={{0,4},{1,5},{2,6},{3,7},{4,0},{5,1},{6,2},{7,3},{8,12},{9,13},{10,... | collective-permute-start | bytes 786440 | tf_op jit(solution)/shard_map/ppermute | solution.py:424
  20.7 15.4 %collective-permute-start.6 = (bf16[2048,128]{1,0:T(8,128)(2,1)}, bf16[2048,128]{1,0:T(8,128)(2,1)S(1)}, u32[]{:S(2)}, u32[]{:S(2)}) collective-permute-start(bf16[2048,128]{1,0:T(8,128)(2,1)} %collective-permute-done.4.w2), channel_id=1, source_target_pairs={{0,1},{1,0},{2,3},{3,2},{4,5},{5,4},{6,7},{7,6},{8,9},{9,8},{10,11... | collective-permute-start | bytes 1572872 | tf_op jit(solution)/shard_map/ppermute | solution.py:421
  20.7 15.4 %collective-permute-start.5 = (bf16[2048,128]{1,0:T(8,128)(2,1)}, bf16[2048,128]{1,0:T(8,128)(2,1)S(1)}, u32[]{:S(2)}, u32[]{:S(2)}) collective-permute-start(bf16[2048,128]{1,0:T(8,128)(2,1)} %w0.1), channel_id=1, source_target_pairs={{0,1},{1,0},{2,3},{3,2},{4,5},{5,4},{6,7},{7,6},{8,9},{9,8},{10,11... | collective-permute-start | bytes 1572872 | tf_op jit(solution)/shard_map/ppermute | solution.py:421
  27.2 8.8 %collective-permute-start.3 = (bf16[64,2048]{1,0:T(8,128)(2,1)}, bf16[64,2048]{1,0:T(8,128)(2,1)S(1)}, u32[]{:S(2)}, u32[]{:S(2)}) collective-permute-start(bf16[64,2048]{1,0:T(8,128)(2,1)} %collective-permute-done.1.a2), channel_id=1, source_target_pairs={{0,4},{1,5},{2,6},{3,7},{4,0},{5,1},{6,2},{7,3},{8,12},{9,13},{10,... | collective-permute-start | bytes 786440 | tf_op jit(solution)/shard_map/ppermute | solution.py:424
  28.2 37.0 %copy-start.5 = (f32[2048]{0:T(1024)S(1)}, f32[2048]{0:T(1024)}, u32[]{:S(2)}) copy-start(f32[2048]{0:T(1024)} %param.13) | copy-start | bytes 24580
  28.2 10.7 %collective-permute-start.8 = (bf16[64,512]{1,0:T(8,128)(2,1)S(1)}, bf16[64,512]{1,0:T(8,128)(2,1)S(1)}, u32[]{:S(2)}, u32[]{:S(2)}) collective-permute-start(bf16[64,512]{1,0:T(8,128)(2,1)S(1)} %pad_maximum_fusion), channel_id=1, source_target_pairs={{0,4},{1,5},{2,6},{3,7},{4,0},{5,1},{6,2},{7,3},{8,12},{9,13},{10,... | collective-permute-start | bytes 196616 | tf_op jit(solution)/shard_map/ppermute | solution.py:424
  36.1 37.0 %copy-start.1 = (bf16[1,1024,1536]{2,1,0:T(8,128)(2,1)S(1)}, bf16[1,1024,1536]{2,1,0:T(8,128)(2,1)}, u32[]{:S(2)}) copy-start(bf16[1,1024,1536]{2,1,0:T(8,128)(2,1)} %param.17) | copy-start | bytes 9437188
  41.6 5.0 %collective-permute-start.9 = (bf16[128,512]{1,0:T(8,128)(2,1)S(1)}, bf16[128,512]{1,0:T(8,128)(2,1)S(1)}, u32[]{:S(2)}, u32[]{:S(2)}) collective-permute-start(bf16[128,512]{1,0:T(8,128)(2,1)S(1)} %get-tuple-element.50), channel_id=1, source_target_pairs={{0,16},{16,0},{1,17},{17,1},{2,18},{18,2},{3,19},{19,3},{4,20},{20... | collective-permute-start | bytes 393224 | tf_op jit(solution)/shard_map/ppermute | solution.py:402
  46.6 34.4 %collective-permute-start.19 = (bf16[1024,768]{1,0:T(8,128)(2,1)S(1)}, bf16[1024,768]{1,0:T(8,128)(2,1)S(1)}, u32[]{:S(2)}, u32[]{:S(2)}) collective-permute-start(bf16[1024,768]{1,0:T(8,128)(2,1)S(1)} %weight_piece.2), channel_id=1, source_target_pairs={{0,16},{16,0},{1,17},{17,1},{2,18},{18,2},{3,19},{19,3},{4,20},{20... | collective-permute-start | bytes 4718600 | tf_op jit(solution)/shard_map/ppermute | solution.py:402
  48.4 7.7 %collective-permute-start.12 = (bf16[144,512]{1,0:T(8,128)(2,1)S(1)}, bf16[144,512]{1,0:T(8,128)(2,1)S(1)}, u32[]{:S(2)}, u32[]{:S(2)}) collective-permute-start(bf16[144,512]{1,0:T(8,128)(2,1)S(1)} %stream.1.b0), channel_id=1, source_target_pairs={{0,12},{1,13},{2,14},{3,15},{4,0},{5,1},{6,2},{7,3},{8,4},{9,5},{1... | collective-permute-start | bytes 442376 | tf_op jit(solution)/shard_map/ppermute | solution.py:405
  52.0 11.2 %collective-permute-start.11 = (bf16[144,512]{1,0:T(8,128)(2,1)S(1)}, bf16[144,512]{1,0:T(8,128)(2,1)S(1)}, u32[]{:S(2)}, u32[]{:S(2)}) collective-permute-start(bf16[144,512]{1,0:T(8,128)(2,1)S(1)} %stream.1.b0), channel_id=1, source_target_pairs={{0,8},{1,9},{2,10},{3,11},{4,12},{5,13},{6,14},{7,15},{8,0},{9,1},... | collective-permute-start | bytes 442376 | tf_op jit(solution)/shard_map/ppermute | solution.py:405
  52.0 12.7 %collective-permute-start.10 = (bf16[144,512]{1,0:T(8,128)(2,1)S(1)}, bf16[144,512]{1,0:T(8,128)(2,1)S(1)}, u32[]{:S(2)}, u32[]{:S(2)}) collective-permute-start(bf16[144,512]{1,0:T(8,128)(2,1)S(1)} %stream.1.b0), channel_id=1, source_target_pairs={{0,4},{1,5},{2,6},{3,7},{4,8},{5,9},{6,10},{7,11},{8,12},{9,13},{1... | collective-permute-start | bytes 442376 | tf_op jit(solution)/shard_map/ppermute | solution.py:405
  53.0 12.5 %collective-permute-start.13 = (bf16[144,512]{1,0:T(8,128)(2,1)S(1)}, bf16[144,512]{1,0:T(8,128)(2,1)S(1)}, u32[]{:S(2)}, u32[]{:S(2)}) collective-permute-start(bf16[144,512]{1,0:T(8,128)(2,1)S(1)} %stream.1.b0), channel_id=1, source_target_pairs={{0,2},{1,3},{2,0},{3,1},{4,6},{5,7},{6,4},{7,5},{8,10},{9,11},{10,... | collective-permute-start | bytes 442376 | tf_op jit(solution)/shard_map/ppermute | solution.py:421
  56.0 9.6 %collective-permute-start.16 = (bf16[144,512]{1,0:T(8,128)(2,1)S(1)}, bf16[144,512]{1,0:T(8,128)(2,1)S(1)}, u32[]{:S(2)}, u32[]{:S(2)}) collective-permute-start(bf16[144,512]{1,0:T(8,128)(2,1)S(1)} %collective-permute-done.12.b3), channel_id=1, source_target_pairs={{0,2},{1,3},{2,0},{3,1},{4,6},{5,7},{6,4},{7,5},{8,10},{9,11},{10,... | collective-permute-start | bytes 442376 | tf_op jit(solution)/shard_map/ppermute | solution.py:421
  63.2 5.6 %collective-permute-start.15 = (bf16[144,512]{1,0:T(8,128)(2,1)S(1)}, bf16[144,512]{1,0:T(8,128)(2,1)S(1)}, u32[]{:S(2)}, u32[]{:S(2)}) collective-permute-start(bf16[144,512]{1,0:T(8,128)(2,1)S(1)} %collective-permute-done.11.b2), channel_id=1, source_target_pairs={{0,2},{1,3},{2,0},{3,1},{4,6},{5,7},{6,4},{7,5},{8,10},{9,11},{10,... | collective-permute-start | bytes 442376 | tf_op jit(solution)/shard_map/ppermute | solution.py:421
  64.7 5.6 %collective-permute-start.14 = (bf16[144,512]{1,0:T(8,128)(2,1)S(1)}, bf16[144,512]{1,0:T(8,128)(2,1)S(1)}, u32[]{:S(2)}, u32[]{:S(2)}) collective-permute-start(bf16[144,512]{1,0:T(8,128)(2,1)S(1)} %collective-permute-done.10.b1), channel_id=1, source_target_pairs={{0,2},{1,3},{2,0},{3,1},{4,6},{5,7},{6,4},{7,5},{8,10},{9,11},{10,... | collective-permute-start | bytes 442376 | tf_op jit(solution)/shard_map/ppermute | solution.py:421
  65.6 5.6 %collective-permute-start.18 = (bf16[128,2176]{1,0:T(8,128)(2,1)S(1)}, bf16[128,2176]{1,0:T(8,128)(2,1)S(1)}, u32[]{:S(2)}, u32[]{:S(2)}) collective-permute-start(bf16[128,2176]{1,0:T(8,128)(2,1)S(1)} %get-tuple-element.54.group), channel_id=1, source_target_pairs={{0,1},{1,0},{2,3},{3,2},{4,5},{5,4},{6,7},{7,6},{8,9},{9,8},{10,11... | collective-permute-start | bytes 1671176 | tf_op jit(solution)/shard_map/ppermute | solution.py:421
  71.1 2.0 %collective-permute-start.17 = (bf16[128,2176]{1,0:T(8,128)(2,1)S(1)}, bf16[128,2176]{1,0:T(8,128)(2,1)S(1)}, u32[]{:S(2)}, u32[]{:S(2)}) collective-permute-start(bf16[128,2176]{1,0:T(8,128)(2,1)S(1)} %get-tuple-element.53.group_x), channel_id=1, source_target_pairs={{0,1},{1,0},{2,3},{3,2},{4,5},{5,4},{6,7},{7,6},{8,9},{9,8},{10,11... | collective-permute-start | bytes 1671176 | tf_op jit(solution)/shard_map/ppermute | solution.py:421
  81.0 1.4 %copy-start.2 = (bf16[1,768,1024]{2,1,0:T(8,128)(2,1)S(1)}, bf16[1,768,1024]{2,1,0:T(8,128)(2,1)}, u32[]{:S(2)}) copy-start(bf16[1,768,1024]{2,1,0:T(8,128)(2,1)} %param.18) | copy-start | bytes 4718596
  83.4 2.0 %collective-permute-start.22 = (bf16[128,512]{1,0:T(8,128)(2,1)S(1)}, bf16[128,512]{1,0:T(8,128)(2,1)S(1)}, u32[]{:S(2)}, u32[]{:S(2)}) collective-permute-start(bf16[128,512]{1,0:T(8,128)(2,1)S(1)} %get-tuple-element.66), channel_id=1, source_target_pairs={{0,1},{1,0},{2,3},{3,2},{4,5},{5,4},{6,7},{7,6},{8,9},{9,8},{10,11... | collective-permute-start | bytes 393224 | tf_op jit(solution)/shard_map/ppermute | solution.py:421
  83.5 1.9 %collective-permute-start.23 = (bf16[128,512]{1,0:T(8,128)(2,1)S(1)}, bf16[128,512]{1,0:T(8,128)(2,1)S(1)}, u32[]{:S(2)}, u32[]{:S(2)}) collective-permute-start(bf16[128,512]{1,0:T(8,128)(2,1)S(1)} %get-tuple-element.67), channel_id=1, source_target_pairs={{0,1},{1,0},{2,3},{3,2},{4,5},{5,4},{6,7},{7,6},{8,9},{9,8},{10,11... | collective-permute-start | bytes 393224 | tf_op jit(solution)/shard_map/ppermute | solution.py:421
  84.0 12.0 %collective-permute-start.31 = (bf16[256,768]{1,0:T(8,128)(2,1)S(1)}, bf16[256,768]{1,0:T(8,128)(2,1)S(1)}, u32[]{:S(2)}, u32[]{:S(2)}) collective-permute-start(bf16[256,768]{1,0:T(8,128)(2,1)S(1)} %get-tuple-element.60.far), channel_id=1, source_target_pairs={{0,16},{16,0},{1,17},{17,1},{2,18},{18,2},{3,19},{19,3},{4,20},{20... | collective-permute-start | bytes 1179656 | tf_op jit(solution)/shard_map/ppermute | solution.py:402
  85.5 10.5 %collective-permute-start.24 = (bf16[128,1024]{1,0:T(8,128)(2,1)S(1)}, bf16[128,1024]{1,0:T(8,128)(2,1)S(1)}, u32[]{:S(2)}, u32[]{:S(2)}) collective-permute-start(bf16[128,1024]{1,0:T(8,128)(2,1)S(1)} %fold.2), channel_id=1, source_target_pairs={{0,2},{1,3},{2,0},{3,1},{4,6},{5,7},{6,4},{7,5},{8,10},{9,11},{10,... | collective-permute-start | bytes 786440 | tf_op jit(solution)/shard_map/ppermute | solution.py:421
  87.0 18.3 %collective-permute-start.28 = (bf16[256,768]{1,0:T(8,128)(2,1)S(1)}, bf16[256,768]{1,0:T(8,128)(2,1)S(1)}, u32[]{:S(2)}, u32[]{:S(2)}) collective-permute-start(bf16[256,768]{1,0:T(8,128)(2,1)S(1)} %get-tuple-element.61.near), channel_id=1, source_target_pairs={{0,16},{16,0},{1,17},{17,1},{2,18},{18,2},{3,19},{19,3},{4,20},{20... | collective-permute-start | bytes 1179656 | tf_op jit(solution)/shard_map/ppermute | solution.py:402
  96.5 1.4 %collective-permute-start.32 = (bf16[128,512]{1,0:T(8,128)(2,1)S(1)}, bf16[128,512]{1,0:T(8,128)(2,1)S(1)}, u32[]{:S(2)}, u32[]{:S(2)}) collective-permute-start(bf16[128,512]{1,0:T(8,128)(2,1)S(1)} %get-tuple-element.78), channel_id=1, source_target_pairs={{0,1},{1,0},{2,3},{3,2},{4,5},{5,4},{6,7},{7,6},{8,9},{9,8},{10,11... | collective-permute-start | bytes 393224 | tf_op jit(solution)/shard_map/ppermute | solution.py:421
  96.6 1.5 %collective-permute-start.33 = (bf16[128,512]{1,0:T(8,128)(2,1)S(1)}, bf16[128,512]{1,0:T(8,128)(2,1)S(1)}, u32[]{:S(2)}, u32[]{:S(2)}) collective-permute-start(bf16[128,512]{1,0:T(8,128)(2,1)S(1)} %get-tuple-element.79), channel_id=1, source_target_pairs={{0,1},{1,0},{2,3},{3,2},{4,5},{5,4},{6,7},{7,6},{8,9},{9,8},{10,11... | collective-permute-start | bytes 393224 | tf_op jit(solution)/shard_map/ppermute | solution.py:421
  97.1 2.6 %collective-permute-start.20 = (bf16[128,512]{1,0:T(8,128)(2,1)S(1)}, bf16[128,512]{1,0:T(8,128)(2,1)S(1)}, u32[]{:S(2)}, u32[]{:S(2)}) collective-permute-start(bf16[128,512]{1,0:T(8,128)(2,1)S(1)} %get-tuple-element.63), channel_id=1, source_target_pairs={{0,1},{1,0},{2,3},{3,2},{4,5},{5,4},{6,7},{7,6},{8,9},{9,8},{10,11... | collective-permute-start | bytes 393224 | tf_op jit(solution)/shard_map/ppermute | solution.py:421
  97.2 2.5 %collective-permute-start.21 = (bf16[128,512]{1,0:T(8,128)(2,1)S(1)}, bf16[128,512]{1,0:T(8,128)(2,1)S(1)}, u32[]{:S(2)}, u32[]{:S(2)}) collective-permute-start(bf16[128,512]{1,0:T(8,128)(2,1)S(1)} %get-tuple-element.64), channel_id=1, source_target_pairs={{0,1},{1,0},{2,3},{3,2},{4,5},{5,4},{6,7},{7,6},{8,9},{9,8},{10,11... | collective-permute-start | bytes 393224 | tf_op jit(solution)/shard_map/ppermute | solution.py:421
  98.2 12.9 %collective-permute-start.34 = (bf16[128,1024]{1,0:T(8,128)(2,1)S(1)}, bf16[128,1024]{1,0:T(8,128)(2,1)S(1)}, u32[]{:S(2)}, u32[]{:S(2)}) collective-permute-start(bf16[128,1024]{1,0:T(8,128)(2,1)S(1)} %fold.3), channel_id=1, source_target_pairs={{0,2},{1,3},{2,0},{3,1},{4,6},{5,7},{6,4},{7,5},{8,10},{9,11},{10,... | collective-permute-start | bytes 786440 | tf_op jit(solution)/shard_map/ppermute | solution.py:421
  99.8 23.2 %copy-start.7 = (f32[2048]{0:T(1024)S(1)}, f32[2048]{0:T(1024)}, u32[]{:S(2)}) copy-start(f32[2048]{0:T(1024)} %param.19) | copy-start | bytes 24580
  99.8 6.4 %collective-permute-start.25 = (bf16[32,1024]{1,0:T(8,128)(2,1)S(1)}, bf16[32,1024]{1,0:T(8,128)(2,1)S(1)}, u32[]{:S(2)}, u32[]{:S(2)}) collective-permute-start(bf16[32,1024]{1,0:T(8,128)(2,1)S(1)} %get-tuple-element.69), channel_id=1, source_target_pairs={{0,4},{1,5},{2,6},{3,7},{4,8},{5,9},{6,10},{7,11},{8,12},{9,13},{1... | collective-permute-start | bytes 196616 | tf_op jit(solution)/shard_map/ppermute | solution.py:405
  101.4 7.3 %collective-permute-start.26 = (bf16[32,1024]{1,0:T(8,128)(2,1)S(1)}, bf16[32,1024]{1,0:T(8,128)(2,1)S(1)}, u32[]{:S(2)}, u32[]{:S(2)}) collective-permute-start(bf16[32,1024]{1,0:T(8,128)(2,1)S(1)} %get-tuple-element.70), channel_id=1, source_target_pairs={{0,8},{1,9},{2,10},{3,11},{4,12},{5,13},{6,14},{7,15},{8,0},{9,1},... | collective-permute-start | bytes 196616 | tf_op jit(solution)/shard_map/ppermute | solution.py:405
  104.0 4.9 %collective-permute-start.27 = (bf16[32,1024]{1,0:T(8,128)(2,1)S(1)}, bf16[32,1024]{1,0:T(8,128)(2,1)S(1)}, u32[]{:S(2)}, u32[]{:S(2)}) collective-permute-start(bf16[32,1024]{1,0:T(8,128)(2,1)S(1)} %get-tuple-element.71), channel_id=1, source_target_pairs={{0,12},{1,13},{2,14},{3,15},{4,0},{5,1},{6,2},{7,3},{8,4},{9,5},{1... | collective-permute-start | bytes 196616 | tf_op jit(solution)/shard_map/ppermute | solution.py:405
  109.4 1.4 %collective-permute-start.29 = (bf16[128,512]{1,0:T(8,128)(2,1)S(1)}, bf16[128,512]{1,0:T(8,128)(2,1)S(1)}, u32[]{:S(2)}, u32[]{:S(2)}) collective-permute-start(bf16[128,512]{1,0:T(8,128)(2,1)S(1)} %get-tuple-element.74), channel_id=1, source_target_pairs={{0,1},{1,0},{2,3},{3,2},{4,5},{5,4},{6,7},{7,6},{8,9},{9,8},{10,11... | collective-permute-start | bytes 393224 | tf_op jit(solution)/shard_map/ppermute | solution.py:421
  109.5 1.5 %collective-permute-start.30 = (bf16[128,512]{1,0:T(8,128)(2,1)S(1)}, bf16[128,512]{1,0:T(8,128)(2,1)S(1)}, u32[]{:S(2)}, u32[]{:S(2)}) collective-permute-start(bf16[128,512]{1,0:T(8,128)(2,1)S(1)} %get-tuple-element.75), channel_id=1, source_target_pairs={{0,1},{1,0},{2,3},{3,2},{4,5},{5,4},{6,7},{7,6},{8,9},{9,8},{10,11... | collective-permute-start | bytes 393224 | tf_op jit(solution)/shard_map/ppermute | solution.py:421
  111.1 6.5 %collective-permute-start.35 = (bf16[32,1024]{1,0:T(8,128)(2,1)S(1)}, bf16[32,1024]{1,0:T(8,128)(2,1)S(1)}, u32[]{:S(2)}, u32[]{:S(2)}) collective-permute-start(bf16[32,1024]{1,0:T(8,128)(2,1)S(1)} %get-tuple-element.80), channel_id=1, source_target_pairs={{0,16},{1,17},{2,18},{3,19},{4,20},{5,21},{6,22},{7,23},{8,24},{9,... | collective-permute-start | bytes 196616 | tf_op jit(solution)/shard_map/ppermute | solution.py:410
  112.7 7.6 %collective-permute-start.36 = (bf16[32,1024]{1,0:T(8,128)(2,1)S(1)}, bf16[32,1024]{1,0:T(8,128)(2,1)S(1)}, u32[]{:S(2)}, u32[]{:S(2)}) collective-permute-start(bf16[32,1024]{1,0:T(8,128)(2,1)S(1)} %get-tuple-element.81), channel_id=1, source_target_pairs={{0,20},{1,21},{2,22},{3,23},{4,24},{5,25},{6,26},{7,27},{8,28},{9,... | collective-permute-start | bytes 196616 | tf_op jit(solution)/shard_map/ppermute | solution.py:410
  114.3 8.1 %collective-permute-start.37 = (bf16[32,1024]{1,0:T(8,128)(2,1)S(1)}, bf16[32,1024]{1,0:T(8,128)(2,1)S(1)}, u32[]{:S(2)}, u32[]{:S(2)}) collective-permute-start(bf16[32,1024]{1,0:T(8,128)(2,1)S(1)} %get-tuple-element.82), channel_id=1, source_target_pairs={{0,24},{1,25},{2,26},{3,27},{4,28},{5,29},{6,30},{7,31},{8,16},{9,... | collective-permute-start | bytes 196616 | tf_op jit(solution)/shard_map/ppermute | solution.py:410
  117.1 5.9 %collective-permute-start.38 = (bf16[32,1024]{1,0:T(8,128)(2,1)S(1)}, bf16[32,1024]{1,0:T(8,128)(2,1)S(1)}, u32[]{:S(2)}, u32[]{:S(2)}) collective-permute-start(bf16[32,1024]{1,0:T(8,128)(2,1)S(1)} %get-tuple-element.83), channel_id=1, source_target_pairs={{0,28},{1,29},{2,30},{3,31},{4,16},{5,17},{6,18},{7,19},{8,20},{9,... | collective-permute-start | bytes 196616 | tf_op jit(solution)/shard_map/ppermute | solution.py:410

commit v10 on v9

--- a/solution.py
+++ b/solution.py
@@ -318,47 +318,71 @@
     return [slice(at, at + 256) for at in range(0, wd.shape[1], 256)]
 
 
-def down_both_kernel(far, near, wd, keep_far, keep_near, far_a, far_b, near_a, near_b):
-    down_kernel(far, wd, keep_far, far_a, far_b)
-    down_kernel(near, wd, keep_near, near_a, near_b)
-
-
-def down_kernel(rows, wd, keep_ref, send_a, send_b):
-    count, side = send_a.shape
+def down_both_kernel(far, near, wd, keep_far, *refs):
+    *sends, keep_near, rows = refs
+    half = len(sends) // 2
+    down_kernel(far, wd, keep_far, *sends[:half], rows)
+    down_kernel(near, wd, keep_near, *sends[half:], rows)
+
+
+def down_kernel(block, wd, keep_ref, *refs):
+    *sends, rows = refs
+    expert, outer, inner, dp = seat()
+    core = inner & 1
+    count, side = sends[0].shape
+    small = count // 4
+    for i in range(2):
+        for j in range(2):
+            kept = aligned(4 * j + ((outer + 2 * core + i) & 3), small)
+            sent = aligned(4 * (1 - j) + ((outer + 2 - 2 * core + i) & 3), small)
+            at = (2 * i + j) * small
+            rows[at : at + small, :] = block[kept, :]
+            rows[count + at : count + at + small, :] = block[sent, :]
     for at in range(0, wd.shape[1], 256):
         value = dot(rows[...], wd[:, at : at + 256]).astype(BF16)
         keep_ref[:, at : at + 256] = value[:count]
-        send = send_a if at < side else send_b
-        send[:, at % side : at % side + 256] = value[count:]
-
-
-def fold_kernel(keep, core_a, core_b, out):
-    side = core_a.shape[1]
-    for i, core in enumerate((core_a, core_b)):
-        cols = slice(i * side, (i + 1) * side)
-        out[:, cols] = (keep[:, cols].astype(F32) + core[...].astype(F32)).astype(BF16)
-
-
-def pieces_kernel(keep, core_a, core_b, far, p0, p1, p2, p3):
-    expert, outer, inner, dp = seat()
-    small = p0.shape[0]
-    for s, p in enumerate((p0, p1, p2, p3)):
-        rows = aligned((outer + s) & 3, small)
-        side = core_a.shape[1]
-        for i, core in enumerate((core_a, core_b)):
-            cols = slice(i * side, (i + 1) * side)
-            total = keep[rows, cols].astype(F32) + core[rows, :].astype(F32)
-            p[:, cols] = (total + far[rows, cols].astype(F32)).astype(BF16)
-
-
-def tail_kernel(own, m0, m1, m2, m3, o0, o1, o2, o3, gain, stream_ref, normed_ref):
-    expert, outer, inner, dp = seat()
-    half = m0.shape[1]
-    for at, pieces in ((dp, (m0, m1, m2, m3)), (1 - dp, (o0, o1, o2, o3))):
+        sends[at // side][:, at % side : at % side + 256] = value[count:]
+
+
+def added(keep, cores, cols):
+    side = cores[0].shape[1]
+    return keep[:, cols].astype(F32) + cores[cols.start // side][:, cols.start % side : cols.start % side + 256].astype(F32)
+
+
+def fold_kernel(keep, *refs):
+    *cores, out = refs
+    for at in range(0, keep.shape[1], 256):
+        cols = slice(at, at + 256)
+        out[:, cols] = added(keep, cores, cols).astype(BF16)
+
+
+def pieces_kernel(far, keep, *refs):
+    *cores, first, second = refs
+    half = first.shape[0]
+    for at in range(0, keep.shape[1], 256):
+        cols = slice(at, at + 256)
+        total = (added(keep, cores, cols) + far[:, cols].astype(F32)).astype(BF16)
+        first[:, cols] = total[:half]
+        second[:, cols] = total[half:]
+
+
+def gather_kernel(own, a0, a1, b0, b1, keep_ref, send_ref):
+    expert, outer, inner, dp = seat()
+    small = own.shape[0] // 2
+    start = jnp.where((inner & 1) == 0, own[...].astype(F32), a0[...].astype(F32))
+    for i, total in enumerate((start + a1[...].astype(F32), b0[...].astype(F32) + b1[...].astype(F32))):
+        rows = slice(i * small, (i + 1) * small)
+        keep_ref[rows, :] = total[:small]
+        send_ref[rows, :] = total[small:].astype(BF16)
+
+
+def tail_kernel(own, keep, core, gain, stream_ref, normed_ref):
+    expert, outer, inner, dp = seat()
+    small, half = own.shape[0], keep.shape[1]
+    for i, at in enumerate((dp, 1 - dp)):
+        rows = slice(i * small, (i + 1) * small)
         cols = aligned(at, half)
-        mixture = pieces[0][...].astype(F32)
-        for piece in pieces[1:]:
-            mixture = mixture + piece[...].astype(F32)
+        mixture = keep[rows, :] + core[rows, :].astype(F32)
         stream_ref[:, cols] = (own[:, cols].astype(F32) + mixture).astype(BF16)
     normed_ref[...] = rms_scale(stream_ref[...].astype(F32), gain[...]).astype(BF16)
 
@@ -406,16 +430,14 @@
             x, "expert", [(i, (i + 4 * s) % expert_count) for i in range(expert_count)]
         )
 
-    def cross_outer(x, s):
-        return lax.ppermute(
-            x,
-            ("dp", "expert"),
-            [
-                (d * expert_count + i, (1 - d) * expert_count + (i + 4 * s) % expert_count)
-                for d in range(2)
-                for i in range(expert_count)
-            ],
-        )
+    def send_outer(x, i, cross):
+        pairs = []
+        for at in range(2 * expert_count):
+            d, e = divmod(at, expert_count)
+            step = 2 * (e % 2) + i
+            if step or cross:
+                pairs.append((at, (d ^ cross) * expert_count + (e + 4 * step) % expert_count))
+        return lax.ppermute(x, ("dp", "expert"), pairs)
 
     def swap_inner(x, j):
         return lax.ppermute(x, "expert", [(i, i ^ j) for i in range(expert_count)])
@@ -426,20 +448,17 @@
     def after(x, *results):
         return lax.optimization_barrier((x, *results))[0]
 
-    def weight_piece(first, size):
+    def weight_piece(first, size, mib=8):
         return pl.pallas_call(
             functools.partial(piece_kernel, (first, hidden + first)),
             out_shape=shape_of(half_width, 2 * size),
             in_specs=[pl.BlockSpec(memory_space=pl.ANY)],
             out_specs=vmem,
             scratch_shapes=[pltpu.SemaphoreType.DMA((2, 4))],
-            compiler_params=kernel_params(8),
+            compiler_params=kernel_params(mib),
             cost_estimate=small_cost(),
             name="weight_piece",
         )(w_gate_up[0])
-
-    def weight_pieces(first, sizes):
-        return [weight_piece(first + sum(sizes[:i]), size) for i, size in enumerate(sizes)]
 
     piece = shape_of(rows_here, quarter)
     r_own, r_1, r_23 = call(
@@ -456,8 +475,8 @@
         first=smem,
     )
     cut_width = hidden // 2
-    early_pieces = weight_pieces(0, (cut_width * 384 // 384,))
-    late_pieces = weight_pieces(cut_width, (cut_width * 384 // 384,))
+    early_pieces = [weight_piece(0, cut_width, 58)]
+    late_pieces = [weight_piece(cut_width, hidden - cut_width)]
     gate_up_early = [swap_dp(piece) for piece in early_pieces]
     a = [attn[0], swap_outer(attn[0], 1), swap_outer(attn[0], 2)]
     w_x = swap_inner(w_out, 2)
@@ -546,20 +565,17 @@
 
     count = row_total // 4
     quarter_out = shape_of(count, half_width)
-    half_out = shape_of(count, half_width // 2)
-
-    def down(rows):
-        return call(
-            down_kernel,
-            "down",
-            12,
-            (quarter_out, half_out, half_out),
-            rows,
-            w_down[0],
+
+    def parts_of(many):
+        return (shape_of(count, half_width // many),) * many
+
+    scratch = (pltpu.VMEM((half_rows, hidden), BF16),)
+
+    def down(rows, many):
+        keep, *send = call(
+            down_kernel, "down", 12, (quarter_out, *parts_of(many)), rows, w_down[0], scratch=scratch
         )
-
-    def add(x, y):
-        return (x.astype(F32) + y.astype(F32)).astype(BF16)
+        return keep, send
 
     def swap_cores(halves):
         return [swap_inner(half, 1) for half in halves]
@@ -567,33 +583,38 @@
     def fold(keep, halves):
         return call(fold_kernel, "fold", 4, (quarter_out,), keep, *halves)[0]
 
-    def pieces(*args):
-        out = shape_of(rows_here, half_width)
-        return call(pieces_kernel, "pieces", 4, (out, out, out, out), *args)
-
-    keep_far, keep_near, *send = call(
-        down_both_kernel,
-        "down_both",
-        16,
-        (quarter_out, quarter_out, half_out, half_out, half_out, half_out),
-        inner_far,
-        inner_near,
-        w_down[0],
+    def pieces(far, keep, send):
+        outs = (shape_of(2 * rows_here, half_width),) * 2
+        return call(pieces_kernel, "pieces", 4, outs, far, keep, *swap_cores(send))
+
+    outs = (quarter_out, *parts_of(2), *parts_of(2), quarter_out)
+    keep_far, *send, keep_near = call(
+        down_both_kernel, "down_both", 16, outs, inner_far, inner_near, w_down[0], scratch=scratch
     )
     far = swap_inner(fold(keep_far, swap_cores(send[:2])), 2)
     ready = far
-    cut = pieces(keep_near, *swap_cores(send[2:]), far)
-    mine = [cut[0]] + [shift_outer(cut[s], s) for s in (1, 2, 3)]
-
-    keep_far, *send = down(after(far_other, ready))
+    own, second = pieces(far, keep_near, send[2:])
+    mine = [send_outer(own, 0, False), send_outer(second, 1, False)]
+
+    keep_far, send = down(after(far_other, ready), 2)
     far = swap_inner(fold(keep_far, swap_cores(send)), 2)
-    keep_near, *send = down(after(near_other, *mine[1:]))
-    cut = pieces(keep_near, *swap_cores(send), far)
-    others = [cross_outer(cut[s], s) for s in range(4)]
-
+    keep_near, send = down(near_other, 2)
+    cut = pieces(far, after(keep_near, *mine), send)
+    others = [send_outer(cut[i], i, True) for i in range(2)]
+
+    sums = shape_of(2 * rows_here, half_width)
+    keep, send = call(
+        gather_kernel,
+        "gather",
+        4,
+        (shape_of(2 * rows_here, half_width, dtype=F32), sums),
+        own,
+        *mine,
+        *others,
+    )
     out = shape_of(rows_here, model_width)
     stream_out, normed_out = call(
-        tail_kernel, "closing", 8, (out, out), stream_own, *mine, *others, gain_final[None]
+        tail_kernel, "closing", 8, (out, out), stream_own, keep, swap_inner(send, 1), gain_final[None]
     )
     return (stream_out[None], normed_out[None])
 

time: 124 us -> 121 us (0.976)
  starting transfers between devices: 44.5 us -> 38.6 us
  Pallas kernels: 14.9 us -> 17.6 us
    ppermute x6 -> x3, starting transfers between devices: 10.2 us -> 4.67 us  [shift_outer(): lax.ppermute(x, 'expert', [(i, (i + 4 * s) % expert_count) for i in range...]
    ppermute x4, waiting for transfers between devices: 5.34 us -> 10.2 us  [send_outer(): return lax.ppermute(x, ('dp', 'expert'), pairs)]
    ppermute x6 -> x3, waiting for transfers between devices: 10.7 us -> 7.19 us  [shift_outer(): lax.ppermute(x, 'expert', [(i, (i + 4 * s) % expert_count) for i in range...]
    ppermute x4, starting transfers between devices: 6.49 us -> 4.25 us  [send_outer(): return lax.ppermute(x, ('dp', 'expert'), pairs)]
    ppermute x19 -> x20, starting transfers between devices: 12.3 us -> 14.2 us  [swap_inner(): return lax.ppermute(x, 'expert', [(i, i ^ j) for i in range(expert_count)])]
    pallas_call x2, Pallas kernels: 1.68 us -> 3.06 us  [weight_piece(): pl.pallas_call(functools.partial(piece_kernel, (first, hidden + first)),...]
    pallas_call x16 -> x17, Pallas kernels: 13.2 us -> 14.6 us  [call(): pl.pallas_call(kernel, out_shape=outs, in_specs=[first] + [vmem] * (len(a...]
    ppermute x19 -> x20, waiting for transfers between devices: 13.1 us -> 11.8 us  [swap_inner(): return lax.ppermute(x, 'expert', [(i, i ^ j) for i in range(expert_count)])]
  transfers between devices with their start and end apart: 39 -> 37, of which waited for: 22 -> 19; matrix products, arithmetic and copies ran while one was open for 1% -> 1% of each run, Pallas kernels for 8% -> 10%
where the time goes in v10:
time: 121 us; the launch traced here: 120 us
  waiting for transfers between devices  59.6 us (49%)
  starting transfers between devices  38.6 us (32%)
  Pallas kernels  17.6 us (15%)
  local copies, waits for them, and re-layouts  2.06 us (2%)
  between operations  1.54 us (1%)
    ppermute x5, waiting for transfers between devices, swap_dp(): return lax.ppermute(x, 'dp', [(0, 1), (1, 0)])  19 us
    pallas_call x17, Pallas kernels, call(): pl.pallas_call(kernel, out_shape=outs, in_specs=[first] + [vmem] * (len(a...  14.6 us
    ppermute x20, starting transfers between devices, swap_inner(): return lax.ppermute(x, 'expert', [(i, i ^ j) for i in range(expert_count)])  14.2 us
    ppermute x20, waiting for transfers between devices, swap_inner(): return lax.ppermute(x, 'expert', [(i, i ^ j) for i in range(expert_count)])  11.8 us
    ppermute x5, waiting for transfers between devices, swap_outer(): lax.ppermute(x, 'expert', [(i, i ^ 4 * s) for i in range(expert_count)])  11.4 us
    ppermute x4, waiting for transfers between devices, send_outer(): return lax.ppermute(x, ('dp', 'expert'), pairs)  10.2 us
    ppermute x5, starting transfers between devices, swap_dp(): return lax.ppermute(x, 'dp', [(0, 1), (1, 0)])  8.95 us
    ppermute x3, waiting for transfers between devices, shift_outer(): lax.ppermute(x, 'expert', [(i, (i + 4 * s) % expert_count) for i in range...  7.19 us
  transfers between devices with their start and end apart: 37, of which 19 were waited for; matrix products, arithmetic and copies ran while one was open for 1% of the time, Pallas kernels for 10%

profile of v10, /device:TPU:0, one launch (start us, length us, event | category | flops | bytes accessed | tf_op | source)
XLA Modules:
  0.0 120.2 jit_solution(16270331159480907501)
XLA Ops:
  0.7 2.8 %weight_piece.3 = bf16[1024,768]{1,0:T(8,128)(2,1)} custom-call(bf16[1024,1536]{1,0:T(8,128)(2,1)} %bitcast.10), custom_call_target="tpu_custom_call" | custom-call | flops 1 | bytes 1 | tf_op jit(solution)/shard_map/weight_piece/pallas_call | solution.py:452
  3.5 3.0 %collective-permute-start.7 = (bf16[1024,768]{1,0:T(8,128)(2,1)}, bf16[1024,768]{1,0:T(8,128)(2,1)}, u32[]{:S(2)}, u32[]{:S(2)}) collective-permute-start(bf16[1024,768]{1,0:T(8,128)(2,1)} %weight_piece.3), channel_id=1, source_target_pairs={{0,16},{16,0},{1,17},{17,1},{2,18},{18,2},{3,19},{19,3},{4,20},{20... | collective-permute-start | bytes 4718600 | tf_op jit(solution)/shard_map/ppermute | solution.py:426
  6.5 1.5 %collective-permute-start.4 = (bf16[2048,128]{1,0:T(8,128)(2,1)}, bf16[2048,128]{1,0:T(8,128)(2,1)}, u32[]{:S(2)}, u32[]{:S(2)}) collective-permute-start(bf16[2048,128]{1,0:T(8,128)(2,1)} %w0.1), channel_id=1, source_target_pairs={{0,2},{1,3},{2,0},{3,1},{4,6},{5,7},{6,4},{7,5},{8,10},{9,11},{10,... | collective-permute-start | bytes 1572872 | tf_op jit(solution)/shard_map/ppermute | solution.py:443
  8.0 0.6 cut_resid.1
  8.6 2.6 %collective-permute-start.2 = (bf16[64,512]{1,0:T(8,128)(2,1)}, bf16[64,512]{1,0:T(8,128)(2,1)S(1)}, u32[]{:S(2)}, u32[]{:S(2)}) collective-permute-start(bf16[64,512]{1,0:T(8,128)(2,1)} %get-tuple-element.42), channel_id=1, source_target_pairs={{0,8},{1,9},{2,10},{3,11},{4,12},{5,13},{6,14},{7,15},{8,0},{9,1},... | collective-permute-start | bytes 196616 | tf_op jit(solution)/shard_map/ppermute | solution.py:446
  11.2 0.3 collective-permute-start.1
  11.6 1.6 %collective-permute-start = (bf16[64,2048]{1,0:T(8,128)(2,1)S(1)}, bf16[64,2048]{1,0:T(8,128)(2,1)}, u32[]{:S(2)}, u32[]{:S(2)}) collective-permute-start(bf16[64,2048]{1,0:T(8,128)(2,1)S(1)} %bitcast.17), channel_id=1, source_target_pairs={{0,4},{1,5},{2,6},{3,7},{4,0},{5,1},{6,2},{7,3},{8,12},{9,13},{10,... | collective-permute-start | bytes 786440 | tf_op jit(solution)/shard_map/ppermute | solution.py:446
  13.2 0.2 weight_piece.2
  13.4 1.2 copy-done.2
  15.3 0.8 copy.13
  16.1 0.4 share.1
  16.5 3.7 %collective-permute-done.4.w2 = bf16[2048,128]{1,0:T(8,128)(2,1)} collective-permute-done((bf16[2048,128]{1,0:T(8,128)(2,1)}, bf16[2048,128]{1,0:T(8,128)(2,1)}, u32[]{:S(2)}, u32[]{:S(2)}) %collective-permute-start.4) | collective-permute-done | bytes 524320 | tf_op jit(solution)/shard_map/ppermute | solution.py:443
  20.2 0.5 collective-permute-start.5
  20.7 5.4 %collective-permute-done.1.a2 = bf16[64,2048]{1,0:T(8,128)(2,1)} collective-permute-done((bf16[64,2048]{1,0:T(8,128)(2,1)S(1)}, bf16[64,2048]{1,0:T(8,128)(2,1)}, u32[]{:S(2)}, u32[]{:S(2)}) %collective-permute-start.1) | collective-permute-done | bytes 262176 | tf_op jit(solution)/shard_map/ppermute | solution.py:446
  26.1 0.2 collective-permute-start.3
  26.3 0.8 pad_maximum_fusion
  27.1 1.9 %collective-permute-start.8 = (bf16[64,512]{1,0:T(8,128)(2,1)S(1)}, bf16[64,512]{1,0:T(8,128)(2,1)S(1)}, u32[]{:S(2)}, u32[]{:S(2)}) collective-permute-start(bf16[64,512]{1,0:T(8,128)(2,1)S(1)} %pad_maximum_fusion), channel_id=1, source_target_pairs={{0,4},{1,5},{2,6},{3,7},{4,0},{5,1},{6,2},{7,3},{8,12},{9,13},{10,... | collective-permute-start | bytes 196616 | tf_op jit(solution)/shard_map/ppermute | solution.py:446
  29.0 6.0 %collective-permute-done.3.a3 = bf16[64,2048]{1,0:T(8,128)(2,1)S(1)} collective-permute-done((bf16[64,2048]{1,0:T(8,128)(2,1)}, bf16[64,2048]{1,0:T(8,128)(2,1)S(1)}, u32[]{:S(2)}, u32[]{:S(2)}) %collective-permute-start.3) | collective-permute-done | bytes 262176 | tf_op jit(solution)/shard_map/ppermute | solution.py:446
  35.0 2.7 %projection.1 = (bf16[128,512]{1,0:T(8,128)(2,1)S(1)}, bf16[128,512]{1,0:T(8,128)(2,1)S(1)}) custom-call(bf16[64,2048]{1,0:T(8,128)(2,1)S(1)} %bitcast.18, bf16[64,2048]{1,0:T(8,128)(2,1)} %collective-permute-done.a1, bf16[64,2048]{1,0:T(8,128)(2,1)} %collective-permute-done.1.a2, bf16[64,2048]{1,0:T(8,128)(2,1)S(1)} %collective-permute-done.3.a3, ...), custom_call_target="tpu_custom_call" | custom-call | flops 1 | bytes 1 | tf_op jit(solution)/shard_map/projection/pallas_call | solution.py:414
  37.7 3.6 %collective-permute-done.7.refs_0_ = bf16[1024,768]{1,0:T(8,128)(2,1)} collective-permute-done((bf16[1024,768]{1,0:T(8,128)(2,1)}, bf16[1024,768]{1,0:T(8,128)(2,1)}, u32[]{:S(2)}, u32[]{:S(2)}) %collective-permute-start.7) | collective-permute-done | bytes 1572896 | tf_op jit(solution)/shard_map/ppermute | solution.py:426
  41.2 1.7 %collective-permute-start.9 = (bf16[128,512]{1,0:T(8,128)(2,1)S(1)}, bf16[128,512]{1,0:T(8,128)(2,1)S(1)}, u32[]{:S(2)}, u32[]{:S(2)}) collective-permute-start(bf16[128,512]{1,0:T(8,128)(2,1)S(1)} %get-tuple-element.48), channel_id=1, source_target_pairs={{0,16},{16,0},{1,17},{17,1},{2,18},{18,2},{3,19},{19,3},{4,20},{20... | collective-permute-start | bytes 393224 | tf_op jit(solution)/shard_map/ppermute | solution.py:426
  43.0 3.2 %collective-permute-done.9.arrived = bf16[128,512]{1,0:T(8,128)(2,1)S(1)} collective-permute-done((bf16[128,512]{1,0:T(8,128)(2,1)S(1)}, bf16[128,512]{1,0:T(8,128)(2,1)S(1)}, u32[]{:S(2)}, u32[]{:S(2)}) %collective-permute-start.9) | collective-permute-done | bytes 131104 | tf_op jit(solution)/shard_map/ppermute | solution.py:426
  46.2 1.7 %collective-permute-start.19 = (bf16[1024,768]{1,0:T(8,128)(2,1)S(1)}, bf16[1024,768]{1,0:T(8,128)(2,1)S(1)}, u32[]{:S(2)}, u32[]{:S(2)}) collective-permute-start(bf16[1024,768]{1,0:T(8,128)(2,1)S(1)} %copy-done.3), channel_id=1, source_target_pairs={{0,16},{16,0},{1,17},{17,1},{2,18},{18,2},{3,19},{19,3},{4,20},{20... | collective-permute-start | bytes 4718600 | tf_op jit(solution)/shard_map/ppermute | solution.py:426
  48.0 3.7 %collective-permute-start.12 = (bf16[144,512]{1,0:T(8,128)(2,1)S(1)}, bf16[144,512]{1,0:T(8,128)(2,1)S(1)}, u32[]{:S(2)}, u32[]{:S(2)}) collective-permute-start(bf16[144,512]{1,0:T(8,128)(2,1)S(1)} %stream.1.b0), channel_id=1, source_target_pairs={{0,12},{1,13},{2,14},{3,15},{4,0},{5,1},{6,2},{7,3},{8,4},{9,5},{1... | collective-permute-start | bytes 442376 | tf_op jit(solution)/shard_map/ppermute | solution.py:429
  51.7 1.0 collective-permute-start.10
  52.7 1.5 %collective-permute-start.13 = (bf16[144,512]{1,0:T(8,128)(2,1)S(1)}, bf16[144,512]{1,0:T(8,128)(2,1)S(1)}, u32[]{:S(2)}, u32[]{:S(2)}) collective-permute-start(bf16[144,512]{1,0:T(8,128)(2,1)S(1)} %stream.1.b0), channel_id=1, source_target_pairs={{0,2},{1,3},{2,0},{3,1},{4,6},{5,7},{6,4},{7,5},{8,10},{9,11},{10,... | collective-permute-start | bytes 442376 | tf_op jit(solution)/shard_map/ppermute | solution.py:443
  54.2 1.5 %collective-permute-done.12.b3 = bf16[144,512]{1,0:T(8,128)(2,1)S(1)} collective-permute-done((bf16[144,512]{1,0:T(8,128)(2,1)S(1)}, bf16[144,512]{1,0:T(8,128)(2,1)S(1)}, u32[]{:S(2)}, u32[]{:S(2)}) %collective-permute-start.12) | collective-permute-done | bytes 147488 | tf_op jit(solution)/shard_map/ppermute | solution.py:429
  55.7 1.5 %collective-permute-start.16 = (bf16[144,512]{1,0:T(8,128)(2,1)S(1)}, bf16[144,512]{1,0:T(8,128)(2,1)S(1)}, u32[]{:S(2)}, u32[]{:S(2)}) collective-permute-start(bf16[144,512]{1,0:T(8,128)(2,1)S(1)} %collective-permute-done.12.b3), channel_id=1, source_target_pairs={{0,2},{1,3},{2,0},{3,1},{4,6},{5,7},{6,4},{7,5},{8,10},{9,11},{10,... | collective-permute-start | bytes 442376 | tf_op jit(solution)/shard_map/ppermute | solution.py:443
  57.2 5.7 %collective-permute-done.11.b2 = bf16[144,512]{1,0:T(8,128)(2,1)S(1)} collective-permute-done((bf16[144,512]{1,0:T(8,128)(2,1)S(1)}, bf16[144,512]{1,0:T(8,128)(2,1)S(1)}, u32[]{:S(2)}, u32[]{:S(2)}) %collective-permute-start.11) | collective-permute-done | bytes 147488 | tf_op jit(solution)/shard_map/ppermute | solution.py:429
  62.8 1.5 %collective-permute-start.15 = (bf16[144,512]{1,0:T(8,128)(2,1)S(1)}, bf16[144,512]{1,0:T(8,128)(2,1)S(1)}, u32[]{:S(2)}, u32[]{:S(2)}) collective-permute-start(bf16[144,512]{1,0:T(8,128)(2,1)S(1)} %collective-permute-done.11.b2), channel_id=1, source_target_pairs={{0,2},{1,3},{2,0},{3,1},{4,6},{5,7},{6,4},{7,5},{8,10},{9,11},{10,... | collective-permute-start | bytes 442376 | tf_op jit(solution)/shard_map/ppermute | solution.py:443
  64.3 0.5 collective-permute-start.14
  64.9 0.3 norm.2
  65.3 3.1 %collective-permute-done.15.b2 = bf16[144,512]{1,0:T(8,128)(2,1)S(1)} collective-permute-done((bf16[144,512]{1,0:T(8,128)(2,1)S(1)}, bf16[144,512]{1,0:T(8,128)(2,1)S(1)}, u32[]{:S(2)}, u32[]{:S(2)}) %collective-permute-start.15) | collective-permute-done | bytes 147488 | tf_op jit(solution)/shard_map/ppermute | solution.py:443
  68.4 1.6 %collective-permute-done.14.b1 = bf16[144,512]{1,0:T(8,128)(2,1)S(1)} collective-permute-done((bf16[144,512]{1,0:T(8,128)(2,1)S(1)}, bf16[144,512]{1,0:T(8,128)(2,1)S(1)}, u32[]{:S(2)}, u32[]{:S(2)}) %collective-permute-start.14) | collective-permute-done | bytes 147488 | tf_op jit(solution)/shard_map/ppermute | solution.py:443
  70.0 0.8 norm.3
  70.8 2.0 %collective-permute-done.17.group_cx = bf16[128,2176]{1,0:T(8,128)(2,1)S(1)} collective-permute-done((bf16[128,2176]{1,0:T(8,128)(2,1)S(1)}, bf16[128,2176]{1,0:T(8,128)(2,1)S(1)}, u32[]{:S(2)}, u32[]{:S(2)}) %collective-permute-start.17) | collective-permute-done | bytes 557088 | tf_op jit(solution)/shard_map/ppermute | solution.py:443
  72.7 4.8 %first_gate_up.1 = (bf16[512,384]{1,0:T(8,128)(2,1)S(1)}, f32[512,768]{1,0:T(8,128)S(1)}, bf16[512,1024]{1,0:T(8,128)(2,1)S(1)}, f32[512,128]{1,0:T(8,128)S(1)}) custom-call(bf16[128,2176]{1,0:T(8,128)(2,1)S(1)} %get-tuple-element.51.group_x, bf16[128,2176]{1,0:T(8,128)(2,1)S(1)} %collective-permute-done.17.group_cx, ...), custom_call_target="tpu_custom_call" | custom-call | flops 1 | bytes 1 | tf_op jit(solution)/shard_map/first_gate_up/pallas_call | solution.py:414
  77.6 3.1 %collective-permute-done.19.refs_0_ = bf16[1024,768]{1,0:T(8,128)(2,1)S(1)} collective-permute-done((bf16[1024,768]{1,0:T(8,128)(2,1)S(1)}, bf16[1024,768]{1,0:T(8,128)(2,1)S(1)}, u32[]{:S(2)}, u32[]{:S(2)}) %collective-permute-start.19) | collective-permute-done | bytes 1572896 | tf_op jit(solution)/shard_map/ppermute | solution.py:426
  80.6 1.4 %last_gate_up.1 = (bf16[256,768]{1,0:T(8,128)(2,1)S(1)}, bf16[256,768]{1,0:T(8,128)(2,1)S(1)}) custom-call(bf16[512,384]{1,0:T(8,128)(2,1)S(1)} %get-tuple-element.53.first, f32[512,768]{1,0:T(8,128)S(1)} %get-tuple-element.54.part, bf16[512,1024]{1,0:T(8,128)(2,1)S(1)} %get-tuple-element.55.other, f32[512,128]{1,0:T(8,128)S(1)} %get-tuple-element.56.share, ...), custom_call_target="tpu_custom_call" | custom-call | flops 1 | bytes 1 | tf_op jit(solution)/shard_map/last_gate_up/pallas_call | solution.py:414
  82.0 1.0 down_both.1
  83.1 0.5 collective-permute-start.21
  83.6 1.4 %collective-permute-start.27 = (bf16[256,768]{1,0:T(8,128)(2,1)S(1)}, bf16[256,768]{1,0:T(8,128)(2,1)S(1)}, u32[]{:S(2)}, u32[]{:S(2)}) collective-permute-start(bf16[256,768]{1,0:T(8,128)(2,1)S(1)} %get-tuple-element.58.far), channel_id=1, source_target_pairs={{0,16},{16,0},{1,17},{17,1},{2,18},{18,2},{3,19},{19,3},{4,20},{20... | collective-permute-start | bytes 1179656 | tf_op jit(solution)/shard_map/ppermute | solution.py:426
  85.1 1.6 %collective-permute-start.22 = (bf16[128,1024]{1,0:T(8,128)(2,1)S(1)}, bf16[128,1024]{1,0:T(8,128)(2,1)S(1)}, u32[]{:S(2)}, u32[]{:S(2)}) collective-permute-start(bf16[128,1024]{1,0:T(8,128)(2,1)S(1)} %fold.2), channel_id=1, source_target_pairs={{0,2},{1,3},{2,0},{3,1},{4,6},{5,7},{6,4},{7,5},{8,10},{9,11},{10,... | collective-permute-start | bytes 786440 | tf_op jit(solution)/shard_map/ppermute | solution.py:443
  86.7 1.0 collective-permute-start.31
  87.7 7.9 %collective-permute-done.27.block = bf16[256,768]{1,0:T(8,128)(2,1)S(1)} collective-permute-done((bf16[256,768]{1,0:T(8,128)(2,1)S(1)}, bf16[256,768]{1,0:T(8,128)(2,1)S(1)}, u32[]{:S(2)}, u32[]{:S(2)}) %collective-permute-start.27) | collective-permute-done | bytes 393248 | tf_op jit(solution)/shard_map/ppermute | solution.py:426
  95.6 0.6 down.2
  96.2 0.5 collective-permute-start.29
  96.8 0.4 collective-permute-start.24
  97.3 0.3 collective-permute-done.28.refs_0_
  97.6 0.2 collective-permute-done.29.refs_1_
  97.8 1.4 %collective-permute-start.30 = (bf16[128,1024]{1,0:T(8,128)(2,1)S(1)}, bf16[128,1024]{1,0:T(8,128)(2,1)S(1)}, u32[]{:S(2)}, u32[]{:S(2)}) collective-permute-start(bf16[128,1024]{1,0:T(8,128)(2,1)S(1)} %fold.3), channel_id=1, source_target_pairs={{0,2},{1,3},{2,0},{3,1},{4,6},{5,7},{6,4},{7,5},{8,10},{9,11},{10,... | collective-permute-start | bytes 786440 | tf_op jit(solution)/shard_map/ppermute | solution.py:443
  99.4 1.6 %collective-permute-start.26 = (bf16[64,1024]{1,0:T(8,128)(2,1)S(1)}, bf16[64,1024]{1,0:T(8,128)(2,1)S(1)}, u32[]{:S(2)}, u32[]{:S(2)}) collective-permute-start(bf16[64,1024]{1,0:T(8,128)(2,1)S(1)} %get-tuple-element.67), channel_id=1, source_target_pairs={{0,4},{1,13},{2,6},{3,15},{4,8},{5,1},{6,10},{7,3},{8,12},{9,5},{1... | collective-permute-start | bytes 393224 | tf_op jit(solution)/shard_map/ppermute | solution.py:440
  101.0 0.8 collective-permute-start.25
  101.8 1.3 %collective-permute-done.31.block = bf16[256,768]{1,0:T(8,128)(2,1)S(1)} collective-permute-done((bf16[256,768]{1,0:T(8,128)(2,1)S(1)}, bf16[256,768]{1,0:T(8,128)(2,1)S(1)}, u32[]{:S(2)}, u32[]{:S(2)}) %collective-permute-start.31) | collective-permute-done | bytes 393248 | tf_op jit(solution)/shard_map/ppermute | solution.py:426
  103.1 0.6 down.3
  103.7 1.8 %collective-permute-start.32 = (bf16[128,512]{1,0:T(8,128)(2,1)S(1)}, bf16[128,512]{1,0:T(8,128)(2,1)S(1)}, u32[]{:S(2)}, u32[]{:S(2)}) collective-permute-start(bf16[128,512]{1,0:T(8,128)(2,1)S(1)} %get-tuple-element.74), channel_id=1, source_target_pairs={{0,1},{1,0},{2,3},{3,2},{4,5},{5,4},{6,7},{7,6},{8,9},{9,8},{10,11... | collective-permute-start | bytes 393224 | tf_op jit(solution)/shard_map/ppermute | solution.py:443
  105.6 2.0 %collective-permute-done.26.a1 = bf16[64,1024]{1,0:T(8,128)(2,1)S(1)} collective-permute-done((bf16[64,1024]{1,0:T(8,128)(2,1)S(1)}, bf16[64,1024]{1,0:T(8,128)(2,1)S(1)}, u32[]{:S(2)}, u32[]{:S(2)}) %collective-permute-start.26) | collective-permute-done | bytes 131104 | tf_op jit(solution)/shard_map/ppermute | solution.py:440
  107.7 1.6 %collective-permute-start.34 = (bf16[64,1024]{1,0:T(8,128)(2,1)S(1)}, bf16[64,1024]{1,0:T(8,128)(2,1)S(1)}, u32[]{:S(2)}, u32[]{:S(2)}) collective-permute-start(bf16[64,1024]{1,0:T(8,128)(2,1)S(1)} %get-tuple-element.76), channel_id=1, source_target_pairs={{0,16},{1,25},{2,18},{3,27},{4,20},{5,29},{6,22},{7,31},{8,24},{9,... | collective-permute-start | bytes 393224 | tf_op jit(solution)/shard_map/ppermute | solution.py:440
  109.3 0.2 collective-permute-start.35
  109.5 3.2 %collective-permute-done.34.b0 = bf16[64,1024]{1,0:T(8,128)(2,1)S(1)} collective-permute-done((bf16[64,1024]{1,0:T(8,128)(2,1)S(1)}, bf16[64,1024]{1,0:T(8,128)(2,1)S(1)}, u32[]{:S(2)}, u32[]{:S(2)}) %collective-permute-start.34) | collective-permute-done | bytes 131104 | tf_op jit(solution)/shard_map/ppermute | solution.py:440
  112.7 5.0 %collective-permute-done.35.b1 = bf16[64,1024]{1,0:T(8,128)(2,1)S(1)} collective-permute-done((bf16[64,1024]{1,0:T(8,128)(2,1)S(1)}, bf16[64,1024]{1,0:T(8,128)(2,1)S(1)}, u32[]{:S(2)}, u32[]{:S(2)}) %collective-permute-start.35) | collective-permute-done | bytes 131104 | tf_op jit(solution)/shard_map/ppermute | solution.py:440
  117.8 0.5 collective-permute-start.36
  118.4 1.0 collective-permute-done.36.core
  119.4 0.8 closing.1
  (53 shorter events, 1.1 us)
Async XLA Ops:
  0.6 7.4 %copy-start.5 = (bf16[1,32,2048]{2,1,0:T(8,128)(2,1)S(1)}, bf16[1,32,2048]{2,1,0:T(8,128)(2,1)}, u32[]{:S(2)}) copy-start(bf16[1,32,2048]{2,1,0:T(8,128)(2,1)} %param.11) | copy-start | bytes 393220
  0.6 10.6 %copy-start.4 = (bf16[1,64,2048]{2,1,0:T(8,128)(2,1)S(1)}, bf16[1,64,2048]{2,1,0:T(8,128)(2,1)}, u32[]{:S(2)}) copy-start(bf16[1,64,2048]{2,1,0:T(8,128)(2,1)} %param.10) | copy-start | bytes 786436
  0.6 12.5 %copy-start = (bf16[1,1024,1536]{2,1,0:T(8,128)(2,1)S(1)}, bf16[1,1024,1536]{2,1,0:T(8,128)(2,1)}, u32[]{:S(2)}) copy-start(bf16[1,1024,1536]{2,1,0:T(8,128)(2,1)} %param.17) | copy-start | bytes 9437188
  3.5 37.7 %collective-permute-start.7 = (bf16[1024,768]{1,0:T(8,128)(2,1)}, bf16[1024,768]{1,0:T(8,128)(2,1)}, u32[]{:S(2)}, u32[]{:S(2)}) collective-permute-start(bf16[1024,768]{1,0:T(8,128)(2,1)} %weight_piece.3), channel_id=1, source_target_pairs={{0,16},{16,0},{1,17},{17,1},{2,18},{18,2},{3,19},{19,3},{4,20},{20... | collective-permute-start | bytes 4718600 | tf_op jit(solution)/shard_map/ppermute | solution.py:426
  6.5 13.7 %collective-permute-start.4 = (bf16[2048,128]{1,0:T(8,128)(2,1)}, bf16[2048,128]{1,0:T(8,128)(2,1)}, u32[]{:S(2)}, u32[]{:S(2)}) collective-permute-start(bf16[2048,128]{1,0:T(8,128)(2,1)} %w0.1), channel_id=1, source_target_pairs={{0,2},{1,3},{2,0},{3,1},{4,6},{5,7},{6,4},{7,5},{8,10},{9,11},{10,... | collective-permute-start | bytes 1572872 | tf_op jit(solution)/shard_map/ppermute | solution.py:443
  8.6 4.8 %copy-start.7 = (bf16[32,512]{1,0:T(8,128)(2,1)}, bf16[32,512]{1,0:T(8,128)(2,1)S(1)}, u32[]{:S(2)}) copy-start(bf16[32,512]{1,0:T(8,128)(2,1)S(1)} %get-tuple-element.47) | copy-start | bytes 98308
  8.6 11.6 %collective-permute-start.2 = (bf16[64,512]{1,0:T(8,128)(2,1)}, bf16[64,512]{1,0:T(8,128)(2,1)S(1)}, u32[]{:S(2)}, u32[]{:S(2)}) collective-permute-start(bf16[64,512]{1,0:T(8,128)(2,1)} %get-tuple-element.42), channel_id=1, source_target_pairs={{0,8},{1,9},{2,10},{3,11},{4,12},{5,13},{6,14},{7,15},{8,0},{9,1},... | collective-permute-start | bytes 196616 | tf_op jit(solution)/shard_map/ppermute | solution.py:446
  11.2 4.0 %copy-start.9 = (s32[1,32,8]{1,2,0:T(8,128)S(1)}, s32[1,32,8]{1,2,0:T(8,128)}, u32[]{:S(2)}) copy-start(s32[1,32,8]{1,2,0:T(8,128)} %param.14) | copy-start | bytes 3076
  11.2 14.9 %collective-permute-start.1 = (bf16[64,2048]{1,0:T(8,128)(2,1)S(1)}, bf16[64,2048]{1,0:T(8,128)(2,1)}, u32[]{:S(2)}, u32[]{:S(2)}) collective-permute-start(bf16[64,2048]{1,0:T(8,128)(2,1)S(1)} %bitcast.16), channel_id=1, source_target_pairs={{0,8},{1,9},{2,10},{3,11},{4,12},{5,13},{6,14},{7,15},{8,0},{9,1},... | collective-permute-start | bytes 786440 | tf_op jit(solution)/shard_map/ppermute | solution.py:446
  11.6 14.5 %collective-permute-start = (bf16[64,2048]{1,0:T(8,128)(2,1)S(1)}, bf16[64,2048]{1,0:T(8,128)(2,1)}, u32[]{:S(2)}, u32[]{:S(2)}) collective-permute-start(bf16[64,2048]{1,0:T(8,128)(2,1)S(1)} %bitcast.17), channel_id=1, source_target_pairs={{0,4},{1,5},{2,6},{3,7},{4,0},{5,1},{6,2},{7,3},{8,12},{9,13},{10,... | collective-permute-start | bytes 786440 | tf_op jit(solution)/shard_map/ppermute | solution.py:446
  13.4 1.2 copy-start.2
  20.2 14.7 %collective-permute-start.6 = (bf16[2048,128]{1,0:T(8,128)(2,1)}, bf16[2048,128]{1,0:T(8,128)(2,1)S(1)}, u32[]{:S(2)}, u32[]{:S(2)}) collective-permute-start(bf16[2048,128]{1,0:T(8,128)(2,1)} %collective-permute-done.4.w2), channel_id=1, source_target_pairs={{0,1},{1,0},{2,3},{3,2},{4,5},{5,4},{6,7},{7,6},{8,9},{9,8},{10,11... | collective-permute-start | bytes 1572872 | tf_op jit(solution)/shard_map/ppermute | solution.py:443
  20.2 14.7 %collective-permute-start.5 = (bf16[2048,128]{1,0:T(8,128)(2,1)}, bf16[2048,128]{1,0:T(8,128)(2,1)S(1)}, u32[]{:S(2)}, u32[]{:S(2)}) collective-permute-start(bf16[2048,128]{1,0:T(8,128)(2,1)} %w0.1), channel_id=1, source_target_pairs={{0,1},{1,0},{2,3},{3,2},{4,5},{5,4},{6,7},{7,6},{8,9},{9,8},{10,11... | collective-permute-start | bytes 1572872 | tf_op jit(solution)/shard_map/ppermute | solution.py:443
  26.1 8.8 %collective-permute-start.3 = (bf16[64,2048]{1,0:T(8,128)(2,1)}, bf16[64,2048]{1,0:T(8,128)(2,1)S(1)}, u32[]{:S(2)}, u32[]{:S(2)}) collective-permute-start(bf16[64,2048]{1,0:T(8,128)(2,1)} %collective-permute-done.1.a2), channel_id=1, source_target_pairs={{0,4},{1,5},{2,6},{3,7},{4,0},{5,1},{6,2},{7,3},{8,12},{9,13},{10,... | collective-permute-start | bytes 786440 | tf_op jit(solution)/shard_map/ppermute | solution.py:446
  27.1 19.1 %copy-start.3 = (bf16[1024,768]{1,0:T(8,128)(2,1)S(1)}, bf16[1024,768]{1,0:T(8,128)(2,1)}, u32[]{:S(2)}) copy-start(bf16[1024,768]{1,0:T(8,128)(2,1)} %copy-done.2) | copy-start | bytes 4718596
  27.1 37.8 %copy-start.6 = (f32[2048]{0:T(1024)S(1)}, f32[2048]{0:T(1024)}, u32[]{:S(2)}) copy-start(f32[2048]{0:T(1024)} %param.13) | copy-start | bytes 24580
  27.1 10.5 %collective-permute-start.8 = (bf16[64,512]{1,0:T(8,128)(2,1)S(1)}, bf16[64,512]{1,0:T(8,128)(2,1)S(1)}, u32[]{:S(2)}, u32[]{:S(2)}) collective-permute-start(bf16[64,512]{1,0:T(8,128)(2,1)S(1)} %pad_maximum_fusion), channel_id=1, source_target_pairs={{0,4},{1,5},{2,6},{3,7},{4,0},{5,1},{6,2},{7,3},{8,12},{9,13},{10,... | collective-permute-start | bytes 196616 | tf_op jit(solution)/shard_map/ppermute | solution.py:446
  41.2 5.0 %collective-permute-start.9 = (bf16[128,512]{1,0:T(8,128)(2,1)S(1)}, bf16[128,512]{1,0:T(8,128)(2,1)S(1)}, u32[]{:S(2)}, u32[]{:S(2)}) collective-permute-start(bf16[128,512]{1,0:T(8,128)(2,1)S(1)} %get-tuple-element.48), channel_id=1, source_target_pairs={{0,16},{16,0},{1,17},{17,1},{2,18},{18,2},{3,19},{19,3},{4,20},{20... | collective-permute-start | bytes 393224 | tf_op jit(solution)/shard_map/ppermute | solution.py:426
  46.2 34.4 %collective-permute-start.19 = (bf16[1024,768]{1,0:T(8,128)(2,1)S(1)}, bf16[1024,768]{1,0:T(8,128)(2,1)S(1)}, u32[]{:S(2)}, u32[]{:S(2)}) collective-permute-start(bf16[1024,768]{1,0:T(8,128)(2,1)S(1)} %copy-done.3), channel_id=1, source_target_pairs={{0,16},{16,0},{1,17},{17,1},{2,18},{18,2},{3,19},{19,3},{4,20},{20... | collective-permute-start | bytes 4718600 | tf_op jit(solution)/shard_map/ppermute | solution.py:426
  48.0 7.7 %collective-permute-start.12 = (bf16[144,512]{1,0:T(8,128)(2,1)S(1)}, bf16[144,512]{1,0:T(8,128)(2,1)S(1)}, u32[]{:S(2)}, u32[]{:S(2)}) collective-permute-start(bf16[144,512]{1,0:T(8,128)(2,1)S(1)} %stream.1.b0), channel_id=1, source_target_pairs={{0,12},{1,13},{2,14},{3,15},{4,0},{5,1},{6,2},{7,3},{8,4},{9,5},{1... | collective-permute-start | bytes 442376 | tf_op jit(solution)/shard_map/ppermute | solution.py:429
  51.7 11.2 %collective-permute-start.11 = (bf16[144,512]{1,0:T(8,128)(2,1)S(1)}, bf16[144,512]{1,0:T(8,128)(2,1)S(1)}, u32[]{:S(2)}, u32[]{:S(2)}) collective-permute-start(bf16[144,512]{1,0:T(8,128)(2,1)S(1)} %stream.1.b0), channel_id=1, source_target_pairs={{0,8},{1,9},{2,10},{3,11},{4,12},{5,13},{6,14},{7,15},{8,0},{9,1},... | collective-permute-start | bytes 442376 | tf_op jit(solution)/shard_map/ppermute | solution.py:429
  51.7 12.7 %collective-permute-start.10 = (bf16[144,512]{1,0:T(8,128)(2,1)S(1)}, bf16[144,512]{1,0:T(8,128)(2,1)S(1)}, u32[]{:S(2)}, u32[]{:S(2)}) collective-permute-start(bf16[144,512]{1,0:T(8,128)(2,1)S(1)} %stream.1.b0), channel_id=1, source_target_pairs={{0,4},{1,5},{2,6},{3,7},{4,8},{5,9},{6,10},{7,11},{8,12},{9,13},{1... | collective-permute-start | bytes 442376 | tf_op jit(solution)/shard_map/ppermute | solution.py:429
  52.7 12.5 %collective-permute-start.13 = (bf16[144,512]{1,0:T(8,128)(2,1)S(1)}, bf16[144,512]{1,0:T(8,128)(2,1)S(1)}, u32[]{:S(2)}, u32[]{:S(2)}) collective-permute-start(bf16[144,512]{1,0:T(8,128)(2,1)S(1)} %stream.1.b0), channel_id=1, source_target_pairs={{0,2},{1,3},{2,0},{3,1},{4,6},{5,7},{6,4},{7,5},{8,10},{9,11},{10,... | collective-permute-start | bytes 442376 | tf_op jit(solution)/shard_map/ppermute | solution.py:443
  55.7 9.6 %collective-permute-start.16 = (bf16[144,512]{1,0:T(8,128)(2,1)S(1)}, bf16[144,512]{1,0:T(8,128)(2,1)S(1)}, u32[]{:S(2)}, u32[]{:S(2)}) collective-permute-start(bf16[144,512]{1,0:T(8,128)(2,1)S(1)} %collective-permute-done.12.b3), channel_id=1, source_target_pairs={{0,2},{1,3},{2,0},{3,1},{4,6},{5,7},{6,4},{7,5},{8,10},{9,11},{10,... | collective-permute-start | bytes 442376 | tf_op jit(solution)/shard_map/ppermute | solution.py:443
  62.8 5.6 %collective-permute-start.15 = (bf16[144,512]{1,0:T(8,128)(2,1)S(1)}, bf16[144,512]{1,0:T(8,128)(2,1)S(1)}, u32[]{:S(2)}, u32[]{:S(2)}) collective-permute-start(bf16[144,512]{1,0:T(8,128)(2,1)S(1)} %collective-permute-done.11.b2), channel_id=1, source_target_pairs={{0,2},{1,3},{2,0},{3,1},{4,6},{5,7},{6,4},{7,5},{8,10},{9,11},{10,... | collective-permute-start | bytes 442376 | tf_op jit(solution)/shard_map/ppermute | solution.py:443
  64.3 5.6 %collective-permute-start.14 = (bf16[144,512]{1,0:T(8,128)(2,1)S(1)}, bf16[144,512]{1,0:T(8,128)(2,1)S(1)}, u32[]{:S(2)}, u32[]{:S(2)}) collective-permute-start(bf16[144,512]{1,0:T(8,128)(2,1)S(1)} %collective-permute-done.10.b1), channel_id=1, source_target_pairs={{0,2},{1,3},{2,0},{3,1},{4,6},{5,7},{6,4},{7,5},{8,10},{9,11},{10,... | collective-permute-start | bytes 442376 | tf_op jit(solution)/shard_map/ppermute | solution.py:443
  65.2 5.6 %collective-permute-start.18 = (bf16[128,2176]{1,0:T(8,128)(2,1)S(1)}, bf16[128,2176]{1,0:T(8,128)(2,1)S(1)}, u32[]{:S(2)}, u32[]{:S(2)}) collective-permute-start(bf16[128,2176]{1,0:T(8,128)(2,1)S(1)} %get-tuple-element.52.group), channel_id=1, source_target_pairs={{0,1},{1,0},{2,3},{3,2},{4,5},{5,4},{6,7},{7,6},{8,9},{9,8},{10,11... | collective-permute-start | bytes 1671176 | tf_op jit(solution)/shard_map/ppermute | solution.py:443
  70.8 2.0 %collective-permute-start.17 = (bf16[128,2176]{1,0:T(8,128)(2,1)S(1)}, bf16[128,2176]{1,0:T(8,128)(2,1)S(1)}, u32[]{:S(2)}, u32[]{:S(2)}) collective-permute-start(bf16[128,2176]{1,0:T(8,128)(2,1)S(1)} %get-tuple-element.51.group_x), channel_id=1, source_target_pairs={{0,1},{1,0},{2,3},{3,2},{4,5},{5,4},{6,7},{7,6},{8,9},{9,8},{10,11... | collective-permute-start | bytes 1671176 | tf_op jit(solution)/shard_map/ppermute | solution.py:443
  80.6 1.4 %copy-start.1 = (bf16[1,768,1024]{2,1,0:T(8,128)(2,1)S(1)}, bf16[1,768,1024]{2,1,0:T(8,128)(2,1)}, u32[]{:S(2)}) copy-start(bf16[1,768,1024]{2,1,0:T(8,128)(2,1)} %param.18) | copy-start | bytes 4718596
  83.0 2.0 %collective-permute-start.20 = (bf16[128,512]{1,0:T(8,128)(2,1)S(1)}, bf16[128,512]{1,0:T(8,128)(2,1)S(1)}, u32[]{:S(2)}, u32[]{:S(2)}) collective-permute-start(bf16[128,512]{1,0:T(8,128)(2,1)S(1)} %get-tuple-element.61), channel_id=1, source_target_pairs={{0,1},{1,0},{2,3},{3,2},{4,5},{5,4},{6,7},{7,6},{8,9},{9,8},{10,11... | collective-permute-start | bytes 393224 | tf_op jit(solution)/shard_map/ppermute | solution.py:443
  83.1 1.9 %collective-permute-start.21 = (bf16[128,512]{1,0:T(8,128)(2,1)S(1)}, bf16[128,512]{1,0:T(8,128)(2,1)S(1)}, u32[]{:S(2)}, u32[]{:S(2)}) collective-permute-start(bf16[128,512]{1,0:T(8,128)(2,1)S(1)} %get-tuple-element.62), channel_id=1, source_target_pairs={{0,1},{1,0},{2,3},{3,2},{4,5},{5,4},{6,7},{7,6},{8,9},{9,8},{10,11... | collective-permute-start | bytes 393224 | tf_op jit(solution)/shard_map/ppermute | solution.py:443
  83.6 12.0 %collective-permute-start.27 = (bf16[256,768]{1,0:T(8,128)(2,1)S(1)}, bf16[256,768]{1,0:T(8,128)(2,1)S(1)}, u32[]{:S(2)}, u32[]{:S(2)}) collective-permute-start(bf16[256,768]{1,0:T(8,128)(2,1)S(1)} %get-tuple-element.58.far), channel_id=1, source_target_pairs={{0,16},{16,0},{1,17},{17,1},{2,18},{18,2},{3,19},{19,3},{4,20},{20... | collective-permute-start | bytes 1179656 | tf_op jit(solution)/shard_map/ppermute | solution.py:426
  85.1 10.5 %collective-permute-start.22 = (bf16[128,1024]{1,0:T(8,128)(2,1)S(1)}, bf16[128,1024]{1,0:T(8,128)(2,1)S(1)}, u32[]{:S(2)}, u32[]{:S(2)}) collective-permute-start(bf16[128,1024]{1,0:T(8,128)(2,1)S(1)} %fold.2), channel_id=1, source_target_pairs={{0,2},{1,3},{2,0},{3,1},{4,6},{5,7},{6,4},{7,5},{8,10},{9,11},{10,... | collective-permute-start | bytes 786440 | tf_op jit(solution)/shard_map/ppermute | solution.py:443
  86.7 16.5 %collective-permute-start.31 = (bf16[256,768]{1,0:T(8,128)(2,1)S(1)}, bf16[256,768]{1,0:T(8,128)(2,1)S(1)}, u32[]{:S(2)}, u32[]{:S(2)}) collective-permute-start(bf16[256,768]{1,0:T(8,128)(2,1)S(1)} %get-tuple-element.59.near), channel_id=1, source_target_pairs={{0,16},{16,0},{1,17},{17,1},{2,18},{18,2},{3,19},{19,3},{4,20},{20... | collective-permute-start | bytes 1179656 | tf_op jit(solution)/shard_map/ppermute | solution.py:426
  96.2 1.4 %collective-permute-start.28 = (bf16[128,512]{1,0:T(8,128)(2,1)S(1)}, bf16[128,512]{1,0:T(8,128)(2,1)S(1)}, u32[]{:S(2)}, u32[]{:S(2)}) collective-permute-start(bf16[128,512]{1,0:T(8,128)(2,1)S(1)} %get-tuple-element.70), channel_id=1, source_target_pairs={{0,1},{1,0},{2,3},{3,2},{4,5},{5,4},{6,7},{7,6},{8,9},{9,8},{10,11... | collective-permute-start | bytes 393224 | tf_op jit(solution)/shard_map/ppermute | solution.py:443
  96.2 1.5 %collective-permute-start.29 = (bf16[128,512]{1,0:T(8,128)(2,1)S(1)}, bf16[128,512]{1,0:T(8,128)(2,1)S(1)}, u32[]{:S(2)}, u32[]{:S(2)}) collective-permute-start(bf16[128,512]{1,0:T(8,128)(2,1)S(1)} %get-tuple-element.71), channel_id=1, source_target_pairs={{0,1},{1,0},{2,3},{3,2},{4,5},{5,4},{6,7},{7,6},{8,9},{9,8},{10,11... | collective-permute-start | bytes 393224 | tf_op jit(solution)/shard_map/ppermute | solution.py:443
  96.7 2.5 %collective-permute-start.23 = (bf16[128,512]{1,0:T(8,128)(2,1)S(1)}, bf16[128,512]{1,0:T(8,128)(2,1)S(1)}, u32[]{:S(2)}, u32[]{:S(2)}) collective-permute-start(bf16[128,512]{1,0:T(8,128)(2,1)S(1)} %get-tuple-element.64), channel_id=1, source_target_pairs={{0,1},{1,0},{2,3},{3,2},{4,5},{5,4},{6,7},{7,6},{8,9},{9,8},{10,11... | collective-permute-start | bytes 393224 | tf_op jit(solution)/shard_map/ppermute | solution.py:443
  96.8 2.5 %collective-permute-start.24 = (bf16[128,512]{1,0:T(8,128)(2,1)S(1)}, bf16[128,512]{1,0:T(8,128)(2,1)S(1)}, u32[]{:S(2)}, u32[]{:S(2)}) collective-permute-start(bf16[128,512]{1,0:T(8,128)(2,1)S(1)} %get-tuple-element.65), channel_id=1, source_target_pairs={{0,1},{1,0},{2,3},{3,2},{4,5},{5,4},{6,7},{7,6},{8,9},{9,8},{10,11... | collective-permute-start | bytes 393224 | tf_op jit(solution)/shard_map/ppermute | solution.py:443
  97.8 9.7 %collective-permute-start.30 = (bf16[128,1024]{1,0:T(8,128)(2,1)S(1)}, bf16[128,1024]{1,0:T(8,128)(2,1)S(1)}, u32[]{:S(2)}, u32[]{:S(2)}) collective-permute-start(bf16[128,1024]{1,0:T(8,128)(2,1)S(1)} %fold.3), channel_id=1, source_target_pairs={{0,2},{1,3},{2,0},{3,1},{4,6},{5,7},{6,4},{7,5},{8,10},{9,11},{10,... | collective-permute-start | bytes 786440 | tf_op jit(solution)/shard_map/ppermute | solution.py:443
  99.4 8.2 %collective-permute-start.26 = (bf16[64,1024]{1,0:T(8,128)(2,1)S(1)}, bf16[64,1024]{1,0:T(8,128)(2,1)S(1)}, u32[]{:S(2)}, u32[]{:S(2)}) collective-permute-start(bf16[64,1024]{1,0:T(8,128)(2,1)S(1)} %get-tuple-element.67), channel_id=1, source_target_pairs={{0,4},{1,13},{2,6},{3,15},{4,8},{5,1},{6,10},{7,3},{8,12},{9,5},{1... | collective-permute-start | bytes 393224 | tf_op jit(solution)/shard_map/ppermute | solution.py:440
  101.0 18.3 %copy-start.8 = (f32[2048]{0:T(1024)S(1)}, f32[2048]{0:T(1024)}, u32[]{:S(2)}) copy-start(f32[2048]{0:T(1024)} %param.19) | copy-start | bytes 24580
  101.0 6.5 %collective-permute-start.25 = (bf16[64,1024]{1,0:T(8,128)(2,1)S(1)}, bf16[64,1024]{1,0:T(8,128)(2,1)S(1)}, u32[]{:S(2)}, u32[]{:S(2)}) collective-permute-start(bf16[64,1024]{1,0:T(8,128)(2,1)S(1)} %get-tuple-element.66.own), channel_id=1, source_target_pairs={{1,9},{3,11},{5,13},{7,15},{9,1},{11,3},{13,5},{15,7},{17,25},{19,... | collective-permute-start | bytes 393224 | tf_op jit(solution)/shard_map/ppermute | solution.py:440
  103.7 3.9 %collective-permute-start.32 = (bf16[128,512]{1,0:T(8,128)(2,1)S(1)}, bf16[128,512]{1,0:T(8,128)(2,1)S(1)}, u32[]{:S(2)}, u32[]{:S(2)}) collective-permute-start(bf16[128,512]{1,0:T(8,128)(2,1)S(1)} %get-tuple-element.74), channel_id=1, source_target_pairs={{0,1},{1,0},{2,3},{3,2},{4,5},{5,4},{6,7},{7,6},{8,9},{9,8},{10,11... | collective-permute-start | bytes 393224 | tf_op jit(solution)/shard_map/ppermute | solution.py:443
  105.5 2.1 %collective-permute-start.33 = (bf16[128,512]{1,0:T(8,128)(2,1)S(1)}, bf16[128,512]{1,0:T(8,128)(2,1)S(1)}, u32[]{:S(2)}, u32[]{:S(2)}) collective-permute-start(bf16[128,512]{1,0:T(8,128)(2,1)S(1)} %get-tuple-element.75), channel_id=1, source_target_pairs={{0,1},{1,0},{2,3},{3,2},{4,5},{5,4},{6,7},{7,6},{8,9},{9,8},{10,11... | collective-permute-start | bytes 393224 | tf_op jit(solution)/shard_map/ppermute | solution.py:443
  107.7 5.0 %collective-permute-start.34 = (bf16[64,1024]{1,0:T(8,128)(2,1)S(1)}, bf16[64,1024]{1,0:T(8,128)(2,1)S(1)}, u32[]{:S(2)}, u32[]{:S(2)}) collective-permute-start(bf16[64,1024]{1,0:T(8,128)(2,1)S(1)} %get-tuple-element.76), channel_id=1, source_target_pairs={{0,16},{1,25},{2,18},{3,27},{4,20},{5,29},{6,22},{7,31},{8,24},{9,... | collective-permute-start | bytes 393224 | tf_op jit(solution)/shard_map/ppermute | solution.py:440
  109.3 8.5 %collective-permute-start.35 = (bf16[64,1024]{1,0:T(8,128)(2,1)S(1)}, bf16[64,1024]{1,0:T(8,128)(2,1)S(1)}, u32[]{:S(2)}, u32[]{:S(2)}) collective-permute-start(bf16[64,1024]{1,0:T(8,128)(2,1)S(1)} %get-tuple-element.77), channel_id=1, source_target_pairs={{0,20},{1,29},{2,22},{3,31},{4,24},{5,17},{6,26},{7,19},{8,28},{9,... | collective-permute-start | bytes 393224 | tf_op jit(solution)/shard_map/ppermute | solution.py:440
  117.8 1.5 %collective-permute-start.36 = (bf16[64,1024]{1,0:T(8,128)(2,1)S(1)}, bf16[64,1024]{1,0:T(8,128)(2,1)S(1)}, u32[]{:S(2)}, u32[]{:S(2)}) collective-permute-start(bf16[64,1024]{1,0:T(8,128)(2,1)S(1)} %get-tuple-element.79), channel_id=1, source_target_pairs={{0,1},{1,0},{2,3},{3,2},{4,5},{5,4},{6,7},{7,6},{8,9},{9,8},{10,11... | collective-permute-start | bytes 393224 | tf_op jit(solution)/shard_map/ppermute | solution.py:443

commit v11 on v10

--- a/solution.py
+++ b/solution.py
@@ -220,7 +220,8 @@
 
 
 def piece_kernel(starts, weights, out, semaphores):
-    depth, width = out.shape[0] // 4, out.shape[1] // 2
+    parts = semaphores.shape[1]
+    depth, width = out.shape[0] // parts, out.shape[1] // 2
     copies = [
         pltpu.make_async_copy(
             weights.at[pl.ds(k * depth, depth), pl.ds(starts[i], width)],
@@ -228,7 +229,7 @@
             semaphores.at[i, k],
         )
         for i in range(2)
-        for k in range(4)
+        for k in range(parts)
     ]
     for copy in copies:
         copy.start()
@@ -454,7 +455,7 @@
             out_shape=shape_of(half_width, 2 * size),
             in_specs=[pl.BlockSpec(memory_space=pl.ANY)],
             out_specs=vmem,
-            scratch_shapes=[pltpu.SemaphoreType.DMA((2, 4))],
+            scratch_shapes=[pltpu.SemaphoreType.DMA((2, 16))],
             compiler_params=kernel_params(mib),
             cost_estimate=small_cost(),
             name="weight_piece",
@@ -502,14 +503,14 @@
             pltpu.VMEM((8 * rows_here, quarter), BF16),
         ),
     )
-    arrived = swap_dp(after(send, gate_up_early[0], r_13))
+    arrived = swap_dp(after(send, r_13))
     gate_up_late = [swap_dp(after(piece, arrived)) for piece in late_pieces]
     (block,) = call(
         stream_kernel,
         "stream",
         4,
         (shape_of(4 * rows_here + expert_count, quarter),),
-        keep,
+        after(keep, *gate_up_early),
         arrived,
         r_own,
         r_13,

time: 121 us -> 120 us (level)
  starting transfers between devices: 38.6 us -> 33.7 us
  waiting for transfers between devices: 59.6 us -> 62.5 us
    ppermute x5, waiting for transfers between devices: 11.4 us -> 15.3 us  [swap_outer(): lax.ppermute(x, 'expert', [(i, i ^ 4 * s) for i in range(expert_count)])]
    ppermute x20, waiting for transfers between devices: 11.8 us -> 8.66 us  [swap_inner(): return lax.ppermute(x, 'expert', [(i, i ^ j) for i in range(expert_count)])]
    ppermute x20, starting transfers between devices: 14.2 us -> 11 us  [swap_inner(): return lax.ppermute(x, 'expert', [(i, i ^ j) for i in range(expert_count)])]
    ppermute x3, waiting for transfers between devices: 7.19 us -> 9.95 us  [shift_outer(): lax.ppermute(x, 'expert', [(i, (i + 4 * s) % expert_count) for i in range...]
    ppermute x5, starting transfers between devices: 8.95 us -> 6.21 us  [swap_dp(): return lax.ppermute(x, 'dp', [(0, 1), (1, 0)])]
    ppermute x4, waiting for transfers between devices: 10.2 us -> 8.9 us  [send_outer(): return lax.ppermute(x, ('dp', 'expert'), pairs)]
    unnamed x22 -> x24, local copies, waits for them, and re-layouts: 2.06 us -> 3.11 us
  transfers between devices with their start and end apart: 37 -> 37, of which waited for: 19 -> 18; matrix products, arithmetic and copies ran while one was open for 1% -> 1% of each run, Pallas kernels for 10% -> 12%
where the time goes in v11:
time: 120 us; the launch traced here: 119 us
  waiting for transfers between devices  62.5 us (52%)
  starting transfers between devices  33.7 us (28%)
  Pallas kernels  17.9 us (15%)
  local copies, waits for them, and re-layouts  3.11 us (3%)
  between operations  1.52 us (1%)
    ppermute x5, waiting for transfers between devices, swap_dp(): return lax.ppermute(x, 'dp', [(0, 1), (1, 0)])  19.7 us
    ppermute x5, waiting for transfers between devices, swap_outer(): lax.ppermute(x, 'expert', [(i, i ^ 4 * s) for i in range(expert_count)])  15.3 us
    pallas_call x17, Pallas kernels, call(): pl.pallas_call(kernel, out_shape=outs, in_specs=[first] + [vmem] * (len(a...  14.4 us
    ppermute x20, starting transfers between devices, swap_inner(): return lax.ppermute(x, 'expert', [(i, i ^ j) for i in range(expert_count)])  11 us
    ppermute x3, waiting for transfers between devices, shift_outer(): lax.ppermute(x, 'expert', [(i, (i + 4 * s) % expert_count) for i in range...  9.95 us
    ppermute x4, waiting for transfers between devices, send_outer(): return lax.ppermute(x, ('dp', 'expert'), pairs)  8.9 us
    ppermute x20, waiting for transfers between devices, swap_inner(): return lax.ppermute(x, 'expert', [(i, i ^ j) for i in range(expert_count)])  8.66 us
    ppermute x5, starting transfers between devices, swap_outer(): lax.ppermute(x, 'expert', [(i, i ^ 4 * s) for i in range(expert_count)])  6.53 us
  transfers between devices with their start and end apart: 37, of which 18 were waited for; matrix products, arithmetic and copies ran while one was open for 1% of the time, Pallas kernels for 12%

profile of v11, /device:TPU:0, one launch (start us, length us, event | category | flops | bytes accessed | tf_op | source)
XLA Modules:
  0.0 119.5 jit_solution(8808919026886198192)
XLA Ops:
  0.6 3.0 %collective-permute-start.4 = (bf16[2048,128]{1,0:T(8,128)(2,1)}, bf16[2048,128]{1,0:T(8,128)(2,1)}, u32[]{:S(2)}, u32[]{:S(2)}) collective-permute-start(bf16[2048,128]{1,0:T(8,128)(2,1)} %w0.1), channel_id=1, source_target_pairs={{0,2},{1,3},{2,0},{3,1},{4,6},{5,7},{6,4},{7,5},{8,10},{9,11},{10,... | collective-permute-start | bytes 1572872 | tf_op jit(solution)/shard_map/ppermute | solution.py:444
  3.6 3.0 %weight_piece.3 = bf16[1024,768]{1,0:T(8,128)(2,1)} custom-call(bf16[1024,1536]{1,0:T(8,128)(2,1)} %bitcast.10), custom_call_target="tpu_custom_call" | custom-call | flops 1 | bytes 1 | tf_op jit(solution)/shard_map/weight_piece/pallas_call | solution.py:453
  6.6 1.6 %collective-permute-start.7 = (bf16[1024,768]{1,0:T(8,128)(2,1)}, bf16[1024,768]{1,0:T(8,128)(2,1)}, u32[]{:S(2)}, u32[]{:S(2)}) collective-permute-start(bf16[1024,768]{1,0:T(8,128)(2,1)} %weight_piece.3), channel_id=1, source_target_pairs={{0,16},{16,0},{1,17},{17,1},{2,18},{18,2},{3,19},{19,3},{4,20},{20... | collective-permute-start | bytes 4718600 | tf_op jit(solution)/shard_map/ppermute | solution.py:427
  8.2 0.6 cut_resid.1
  8.9 2.6 %collective-permute-start.2 = (bf16[64,512]{1,0:T(8,128)(2,1)}, bf16[64,512]{1,0:T(8,128)(2,1)S(1)}, u32[]{:S(2)}, u32[]{:S(2)}) collective-permute-start(bf16[64,512]{1,0:T(8,128)(2,1)} %get-tuple-element.43), channel_id=1, source_target_pairs={{0,8},{1,9},{2,10},{3,11},{4,12},{5,13},{6,14},{7,15},{8,0},{9,1},... | collective-permute-start | bytes 196616 | tf_op jit(solution)/shard_map/ppermute | solution.py:447
  11.4 0.3 collective-permute-start.1
  11.8 1.6 %collective-permute-start = (bf16[64,2048]{1,0:T(8,128)(2,1)S(1)}, bf16[64,2048]{1,0:T(8,128)(2,1)}, u32[]{:S(2)}, u32[]{:S(2)}) collective-permute-start(bf16[64,2048]{1,0:T(8,128)(2,1)S(1)} %bitcast.17), channel_id=1, source_target_pairs={{0,4},{1,5},{2,6},{3,7},{4,0},{5,1},{6,2},{7,3},{8,12},{9,13},{10,... | collective-permute-start | bytes 786440 | tf_op jit(solution)/shard_map/ppermute | solution.py:447
  13.4 0.6 weight_piece.2
  13.9 1.2 copy-done.2
  15.8 0.8 copy.13
  16.6 0.4 share.1
  17.1 2.3 %collective-permute-done.2.r2 = bf16[64,512]{1,0:T(8,128)(2,1)S(1)} collective-permute-done((bf16[64,512]{1,0:T(8,128)(2,1)}, bf16[64,512]{1,0:T(8,128)(2,1)S(1)}, u32[]{:S(2)}, u32[]{:S(2)}) %collective-permute-start.2) | collective-permute-done | bytes 65568 | tf_op jit(solution)/shard_map/ppermute | solution.py:447
  19.4 6.9 %collective-permute-done.1.a2 = bf16[64,2048]{1,0:T(8,128)(2,1)} collective-permute-done((bf16[64,2048]{1,0:T(8,128)(2,1)S(1)}, bf16[64,2048]{1,0:T(8,128)(2,1)}, u32[]{:S(2)}, u32[]{:S(2)}) %collective-permute-start.1) | collective-permute-done | bytes 262176 | tf_op jit(solution)/shard_map/ppermute | solution.py:447
  26.3 0.2 collective-permute-start.3
  26.6 0.8 pad_maximum_fusion
  27.3 1.8 %collective-permute-start.8 = (bf16[64,512]{1,0:T(8,128)(2,1)S(1)}, bf16[64,512]{1,0:T(8,128)(2,1)S(1)}, u32[]{:S(2)}, u32[]{:S(2)}) collective-permute-start(bf16[64,512]{1,0:T(8,128)(2,1)S(1)} %pad_maximum_fusion), channel_id=1, source_target_pairs={{0,4},{1,5},{2,6},{3,7},{4,0},{5,1},{6,2},{7,3},{8,12},{9,13},{10,... | collective-permute-start | bytes 196616 | tf_op jit(solution)/shard_map/ppermute | solution.py:447
  29.1 6.0 %collective-permute-done.3.a3 = bf16[64,2048]{1,0:T(8,128)(2,1)S(1)} collective-permute-done((bf16[64,2048]{1,0:T(8,128)(2,1)}, bf16[64,2048]{1,0:T(8,128)(2,1)S(1)}, u32[]{:S(2)}, u32[]{:S(2)}) %collective-permute-start.3) | collective-permute-done | bytes 262176 | tf_op jit(solution)/shard_map/ppermute | solution.py:447
  35.2 1.0 copy-done.4
  36.2 2.5 %projection.1 = (bf16[128,512]{1,0:T(8,128)(2,1)S(1)}, bf16[128,512]{1,0:T(8,128)(2,1)S(1)}) custom-call(bf16[64,2048]{1,0:T(8,128)(2,1)S(1)} %bitcast.18, bf16[64,2048]{1,0:T(8,128)(2,1)} %collective-permute-done.a1, bf16[64,2048]{1,0:T(8,128)(2,1)} %collective-permute-done.1.a2, bf16[64,2048]{1,0:T(8,128)(2,1)S(1)} %collective-permute-done.3.a3, ...), custom_call_target="tpu_custom_call" | custom-call | flops 1 | bytes 1 | tf_op jit(solution)/shard_map/projection/pallas_call | solution.py:415
  38.8 0.6 collective-permute-start.9
  39.3 6.2 %collective-permute-done.9.arrived = bf16[128,512]{1,0:T(8,128)(2,1)S(1)} collective-permute-done((bf16[128,512]{1,0:T(8,128)(2,1)S(1)}, bf16[128,512]{1,0:T(8,128)(2,1)S(1)}, u32[]{:S(2)}, u32[]{:S(2)}) %collective-permute-start.9) | collective-permute-done | bytes 131104 | tf_op jit(solution)/shard_map/ppermute | solution.py:427
  45.6 1.5 %collective-permute-start.19 = (bf16[1024,768]{1,0:T(8,128)(2,1)S(1)}, bf16[1024,768]{1,0:T(8,128)(2,1)S(1)}, u32[]{:S(2)}, u32[]{:S(2)}) collective-permute-start(bf16[1024,768]{1,0:T(8,128)(2,1)S(1)} %copy-done.3), channel_id=1, source_target_pairs={{0,16},{16,0},{1,17},{17,1},{2,18},{18,2},{3,19},{19,3},{4,20},{20... | collective-permute-start | bytes 4718600 | tf_op jit(solution)/shard_map/ppermute | solution.py:427
  47.2 3.7 %collective-permute-start.12 = (bf16[144,512]{1,0:T(8,128)(2,1)S(1)}, bf16[144,512]{1,0:T(8,128)(2,1)S(1)}, u32[]{:S(2)}, u32[]{:S(2)}) collective-permute-start(bf16[144,512]{1,0:T(8,128)(2,1)S(1)} %stream.1.b0), channel_id=1, source_target_pairs={{0,12},{1,13},{2,14},{3,15},{4,0},{5,1},{6,2},{7,3},{8,4},{9,5},{1... | collective-permute-start | bytes 442376 | tf_op jit(solution)/shard_map/ppermute | solution.py:430
  50.8 1.0 collective-permute-start.10
  51.8 0.5 collective-permute-start.13
  52.4 2.8 %collective-permute-done.12.b3 = bf16[144,512]{1,0:T(8,128)(2,1)S(1)} collective-permute-done((bf16[144,512]{1,0:T(8,128)(2,1)S(1)}, bf16[144,512]{1,0:T(8,128)(2,1)S(1)}, u32[]{:S(2)}, u32[]{:S(2)}) %collective-permute-start.12) | collective-permute-done | bytes 147488 | tf_op jit(solution)/shard_map/ppermute | solution.py:430
  55.1 0.5 collective-permute-start.16
  55.7 7.2 %collective-permute-done.11.b2 = bf16[144,512]{1,0:T(8,128)(2,1)S(1)} collective-permute-done((bf16[144,512]{1,0:T(8,128)(2,1)S(1)}, bf16[144,512]{1,0:T(8,128)(2,1)S(1)}, u32[]{:S(2)}, u32[]{:S(2)}) %collective-permute-start.11) | collective-permute-done | bytes 147488 | tf_op jit(solution)/shard_map/ppermute | solution.py:430
  62.8 0.5 collective-permute-start.15
  63.4 1.5 %collective-permute-start.14 = (bf16[144,512]{1,0:T(8,128)(2,1)S(1)}, bf16[144,512]{1,0:T(8,128)(2,1)S(1)}, u32[]{:S(2)}, u32[]{:S(2)}) collective-permute-start(bf16[144,512]{1,0:T(8,128)(2,1)S(1)} %collective-permute-done.10.b1), channel_id=1, source_target_pairs={{0,2},{1,3},{2,0},{3,1},{4,6},{5,7},{6,4},{7,5},{8,10},{9,11},{10,... | collective-permute-start | bytes 442376 | tf_op jit(solution)/shard_map/ppermute | solution.py:444
  64.9 0.3 norm.2
  65.3 3.6 %collective-permute-done.15.b2 = bf16[144,512]{1,0:T(8,128)(2,1)S(1)} collective-permute-done((bf16[144,512]{1,0:T(8,128)(2,1)S(1)}, bf16[144,512]{1,0:T(8,128)(2,1)S(1)}, u32[]{:S(2)}, u32[]{:S(2)}) %collective-permute-start.15) | collective-permute-done | bytes 147488 | tf_op jit(solution)/shard_map/ppermute | solution.py:444
  68.9 1.6 %collective-permute-done.14.b1 = bf16[144,512]{1,0:T(8,128)(2,1)S(1)} collective-permute-done((bf16[144,512]{1,0:T(8,128)(2,1)S(1)}, bf16[144,512]{1,0:T(8,128)(2,1)S(1)}, u32[]{:S(2)}, u32[]{:S(2)}) %collective-permute-start.14) | collective-permute-done | bytes 147488 | tf_op jit(solution)/shard_map/ppermute | solution.py:444
  70.5 0.8 norm.3
  71.3 2.0 %collective-permute-done.17.group_cx = bf16[128,2176]{1,0:T(8,128)(2,1)S(1)} collective-permute-done((bf16[128,2176]{1,0:T(8,128)(2,1)S(1)}, bf16[128,2176]{1,0:T(8,128)(2,1)S(1)}, u32[]{:S(2)}, u32[]{:S(2)}) %collective-permute-start.17) | collective-permute-done | bytes 557088 | tf_op jit(solution)/shard_map/ppermute | solution.py:444
  73.2 4.8 %first_gate_up.1 = (bf16[512,384]{1,0:T(8,128)(2,1)S(1)}, f32[512,768]{1,0:T(8,128)S(1)}, bf16[512,1024]{1,0:T(8,128)(2,1)S(1)}, f32[512,128]{1,0:T(8,128)S(1)}) custom-call(bf16[128,2176]{1,0:T(8,128)(2,1)S(1)} %get-tuple-element.53.group_x, bf16[128,2176]{1,0:T(8,128)(2,1)S(1)} %collective-permute-done.17.group_cx, ...), custom_call_target="tpu_custom_call" | custom-call | flops 1 | bytes 1 | tf_op jit(solution)/shard_map/first_gate_up/pallas_call | solution.py:415
  78.1 2.5 %collective-permute-done.19.refs_0_ = bf16[1024,768]{1,0:T(8,128)(2,1)S(1)} collective-permute-done((bf16[1024,768]{1,0:T(8,128)(2,1)S(1)}, bf16[1024,768]{1,0:T(8,128)(2,1)S(1)}, u32[]{:S(2)}, u32[]{:S(2)}) %collective-permute-start.19) | collective-permute-done | bytes 1572896 | tf_op jit(solution)/shard_map/ppermute | solution.py:427
  80.6 1.4 %last_gate_up.1 = (bf16[256,768]{1,0:T(8,128)(2,1)S(1)}, bf16[256,768]{1,0:T(8,128)(2,1)S(1)}) custom-call(bf16[512,384]{1,0:T(8,128)(2,1)S(1)} %get-tuple-element.55.first, f32[512,768]{1,0:T(8,128)S(1)} %get-tuple-element.56.part, bf16[512,1024]{1,0:T(8,128)(2,1)S(1)} %get-tuple-element.57.other, f32[512,128]{1,0:T(8,128)S(1)} %get-tuple-element.58.share, ...), custom_call_target="tpu_custom_call" | custom-call | flops 1 | bytes 1 | tf_op jit(solution)/shard_map/last_gate_up/pallas_call | solution.py:415
  82.0 1.0 down_both.1
  83.1 0.5 collective-permute-start.21
  83.6 1.5 %collective-permute-start.27 = (bf16[256,768]{1,0:T(8,128)(2,1)S(1)}, bf16[256,768]{1,0:T(8,128)(2,1)S(1)}, u32[]{:S(2)}, u32[]{:S(2)}) collective-permute-start(bf16[256,768]{1,0:T(8,128)(2,1)S(1)} %get-tuple-element.60.far), channel_id=1, source_target_pairs={{0,16},{16,0},{1,17},{17,1},{2,18},{18,2},{3,19},{19,3},{4,20},{20... | collective-permute-start | bytes 1179656 | tf_op jit(solution)/shard_map/ppermute | solution.py:427
  85.2 0.6 collective-permute-start.22
  85.8 1.0 collective-permute-start.31
  86.8 8.7 %collective-permute-done.27.block = bf16[256,768]{1,0:T(8,128)(2,1)S(1)} collective-permute-done((bf16[256,768]{1,0:T(8,128)(2,1)S(1)}, bf16[256,768]{1,0:T(8,128)(2,1)S(1)}, u32[]{:S(2)}, u32[]{:S(2)}) %collective-permute-start.27) | collective-permute-done | bytes 393248 | tf_op jit(solution)/shard_map/ppermute | solution.py:427
  95.6 0.6 down.2
  96.2 0.5 collective-permute-start.29
  96.8 0.4 collective-permute-start.24
  97.2 0.3 collective-permute-done.28.refs_0_
  97.6 0.2 collective-permute-done.29.refs_1_
  97.8 0.6 collective-permute-start.30
  98.4 0.1 pieces.2
  98.5 1.6 %collective-permute-start.26 = (bf16[64,1024]{1,0:T(8,128)(2,1)S(1)}, bf16[64,1024]{1,0:T(8,128)(2,1)S(1)}, u32[]{:S(2)}, u32[]{:S(2)}) collective-permute-start(bf16[64,1024]{1,0:T(8,128)(2,1)S(1)} %get-tuple-element.69), channel_id=1, source_target_pairs={{0,4},{1,13},{2,6},{3,15},{4,8},{5,1},{6,10},{7,3},{8,12},{9,5},{1... | collective-permute-start | bytes 393224 | tf_op jit(solution)/shard_map/ppermute | solution.py:441
  100.2 0.8 collective-permute-start.25
  101.0 2.1 %collective-permute-done.31.block = bf16[256,768]{1,0:T(8,128)(2,1)S(1)} collective-permute-done((bf16[256,768]{1,0:T(8,128)(2,1)S(1)}, bf16[256,768]{1,0:T(8,128)(2,1)S(1)}, u32[]{:S(2)}, u32[]{:S(2)}) %collective-permute-start.31) | collective-permute-done | bytes 393248 | tf_op jit(solution)/shard_map/ppermute | solution.py:427
  103.1 0.6 down.3
  103.7 1.1 collective-permute-start.32
  104.9 1.8 %collective-permute-done.26.a1 = bf16[64,1024]{1,0:T(8,128)(2,1)S(1)} collective-permute-done((bf16[64,1024]{1,0:T(8,128)(2,1)S(1)}, bf16[64,1024]{1,0:T(8,128)(2,1)S(1)}, u32[]{:S(2)}, u32[]{:S(2)}) %collective-permute-start.26) | collective-permute-done | bytes 131104 | tf_op jit(solution)/shard_map/ppermute | solution.py:441
  106.8 1.6 %collective-permute-start.34 = (bf16[64,1024]{1,0:T(8,128)(2,1)S(1)}, bf16[64,1024]{1,0:T(8,128)(2,1)S(1)}, u32[]{:S(2)}, u32[]{:S(2)}) collective-permute-start(bf16[64,1024]{1,0:T(8,128)(2,1)S(1)} %get-tuple-element.78), channel_id=1, source_target_pairs={{0,16},{1,25},{2,18},{3,27},{4,20},{5,29},{6,22},{7,31},{8,24},{9,... | collective-permute-start | bytes 393224 | tf_op jit(solution)/shard_map/ppermute | solution.py:441
  108.4 1.2 %collective-permute-start.35 = (bf16[64,1024]{1,0:T(8,128)(2,1)S(1)}, bf16[64,1024]{1,0:T(8,128)(2,1)S(1)}, u32[]{:S(2)}, u32[]{:S(2)}) collective-permute-start(bf16[64,1024]{1,0:T(8,128)(2,1)S(1)} %get-tuple-element.79), channel_id=1, source_target_pairs={{0,20},{1,29},{2,22},{3,31},{4,24},{5,17},{6,26},{7,19},{8,28},{9,... | collective-permute-start | bytes 393224 | tf_op jit(solution)/shard_map/ppermute | solution.py:441
  109.6 2.2 %collective-permute-done.34.b0 = bf16[64,1024]{1,0:T(8,128)(2,1)S(1)} collective-permute-done((bf16[64,1024]{1,0:T(8,128)(2,1)S(1)}, bf16[64,1024]{1,0:T(8,128)(2,1)S(1)}, u32[]{:S(2)}, u32[]{:S(2)}) %collective-permute-start.34) | collective-permute-done | bytes 131104 | tf_op jit(solution)/shard_map/ppermute | solution.py:441
  111.9 4.8 %collective-permute-done.35.b1 = bf16[64,1024]{1,0:T(8,128)(2,1)S(1)} collective-permute-done((bf16[64,1024]{1,0:T(8,128)(2,1)S(1)}, bf16[64,1024]{1,0:T(8,128)(2,1)S(1)}, u32[]{:S(2)}, u32[]{:S(2)}) %collective-permute-start.35) | collective-permute-done | bytes 131104 | tf_op jit(solution)/shard_map/ppermute | solution.py:441
  116.8 0.9 collective-permute-start.36
  117.6 1.0 collective-permute-done.36.core
  118.6 0.8 closing.1
  (55 shorter events, 1.0 us)
Async XLA Ops:
  0.6 16.4 %collective-permute-start.4 = (bf16[2048,128]{1,0:T(8,128)(2,1)}, bf16[2048,128]{1,0:T(8,128)(2,1)}, u32[]{:S(2)}, u32[]{:S(2)}) collective-permute-start(bf16[2048,128]{1,0:T(8,128)(2,1)} %w0.1), channel_id=1, source_target_pairs={{0,2},{1,3},{2,0},{3,1},{4,6},{5,7},{6,4},{7,5},{8,10},{9,11},{10,... | collective-permute-start | bytes 1572872 | tf_op jit(solution)/shard_map/ppermute | solution.py:444
  3.6 4.6 %copy-start.6 = (bf16[1,32,2048]{2,1,0:T(8,128)(2,1)S(1)}, bf16[1,32,2048]{2,1,0:T(8,128)(2,1)}, u32[]{:S(2)}) copy-start(bf16[1,32,2048]{2,1,0:T(8,128)(2,1)} %param.11) | copy-start | bytes 393220
  3.6 7.8 %copy-start.5 = (bf16[1,64,2048]{2,1,0:T(8,128)(2,1)S(1)}, bf16[1,64,2048]{2,1,0:T(8,128)(2,1)}, u32[]{:S(2)}) copy-start(bf16[1,64,2048]{2,1,0:T(8,128)(2,1)} %param.10) | copy-start | bytes 786436
  3.6 9.7 %copy-start = (bf16[1,1024,1536]{2,1,0:T(8,128)(2,1)S(1)}, bf16[1,1024,1536]{2,1,0:T(8,128)(2,1)}, u32[]{:S(2)}) copy-start(bf16[1,1024,1536]{2,1,0:T(8,128)(2,1)} %param.17) | copy-start | bytes 9437188
  6.6 40.5 %collective-permute-start.7 = (bf16[1024,768]{1,0:T(8,128)(2,1)}, bf16[1024,768]{1,0:T(8,128)(2,1)}, u32[]{:S(2)}, u32[]{:S(2)}) collective-permute-start(bf16[1024,768]{1,0:T(8,128)(2,1)} %weight_piece.3), channel_id=1, source_target_pairs={{0,16},{16,0},{1,17},{17,1},{2,18},{18,2},{3,19},{19,3},{4,20},{20... | collective-permute-start | bytes 4718600 | tf_op jit(solution)/shard_map/ppermute | solution.py:427
  8.9 5.1 %copy-start.8 = (bf16[32,512]{1,0:T(8,128)(2,1)}, bf16[32,512]{1,0:T(8,128)(2,1)S(1)}, u32[]{:S(2)}) copy-start(bf16[32,512]{1,0:T(8,128)(2,1)S(1)} %get-tuple-element.49) | copy-start | bytes 98308
  8.9 10.5 %collective-permute-start.2 = (bf16[64,512]{1,0:T(8,128)(2,1)}, bf16[64,512]{1,0:T(8,128)(2,1)S(1)}, u32[]{:S(2)}, u32[]{:S(2)}) collective-permute-start(bf16[64,512]{1,0:T(8,128)(2,1)} %get-tuple-element.43), channel_id=1, source_target_pairs={{0,8},{1,9},{2,10},{3,11},{4,12},{5,13},{6,14},{7,15},{8,0},{9,1},... | collective-permute-start | bytes 196616 | tf_op jit(solution)/shard_map/ppermute | solution.py:447
  11.4 4.3 %copy-start.10 = (s32[1,32,8]{1,2,0:T(8,128)S(1)}, s32[1,32,8]{1,2,0:T(8,128)}, u32[]{:S(2)}) copy-start(s32[1,32,8]{1,2,0:T(8,128)} %param.14) | copy-start | bytes 3076
  11.4 14.9 %collective-permute-start.1 = (bf16[64,2048]{1,0:T(8,128)(2,1)S(1)}, bf16[64,2048]{1,0:T(8,128)(2,1)}, u32[]{:S(2)}, u32[]{:S(2)}) collective-permute-start(bf16[64,2048]{1,0:T(8,128)(2,1)S(1)} %bitcast.16), channel_id=1, source_target_pairs={{0,8},{1,9},{2,10},{3,11},{4,12},{5,13},{6,14},{7,15},{8,0},{9,1},... | collective-permute-start | bytes 786440 | tf_op jit(solution)/shard_map/ppermute | solution.py:447
  11.8 14.5 %collective-permute-start = (bf16[64,2048]{1,0:T(8,128)(2,1)S(1)}, bf16[64,2048]{1,0:T(8,128)(2,1)}, u32[]{:S(2)}, u32[]{:S(2)}) collective-permute-start(bf16[64,2048]{1,0:T(8,128)(2,1)S(1)} %bitcast.17), channel_id=1, source_target_pairs={{0,4},{1,5},{2,6},{3,7},{4,0},{5,1},{6,2},{7,3},{8,12},{9,13},{10,... | collective-permute-start | bytes 786440 | tf_op jit(solution)/shard_map/ppermute | solution.py:447
  13.9 1.2 copy-start.2
  17.1 18.1 %collective-permute-start.6 = (bf16[2048,128]{1,0:T(8,128)(2,1)}, bf16[2048,128]{1,0:T(8,128)(2,1)S(1)}, u32[]{:S(2)}, u32[]{:S(2)}) collective-permute-start(bf16[2048,128]{1,0:T(8,128)(2,1)} %collective-permute-done.4.w2), channel_id=1, source_target_pairs={{0,1},{1,0},{2,3},{3,2},{4,5},{5,4},{6,7},{7,6},{8,9},{9,8},{10,11... | collective-permute-start | bytes 1572872 | tf_op jit(solution)/shard_map/ppermute | solution.py:444
  19.4 15.8 %collective-permute-start.5 = (bf16[2048,128]{1,0:T(8,128)(2,1)}, bf16[2048,128]{1,0:T(8,128)(2,1)S(1)}, u32[]{:S(2)}, u32[]{:S(2)}) collective-permute-start(bf16[2048,128]{1,0:T(8,128)(2,1)} %w0.1), channel_id=1, source_target_pairs={{0,1},{1,0},{2,3},{3,2},{4,5},{5,4},{6,7},{7,6},{8,9},{9,8},{10,11... | collective-permute-start | bytes 1572872 | tf_op jit(solution)/shard_map/ppermute | solution.py:444
  26.3 8.8 %collective-permute-start.3 = (bf16[64,2048]{1,0:T(8,128)(2,1)}, bf16[64,2048]{1,0:T(8,128)(2,1)S(1)}, u32[]{:S(2)}, u32[]{:S(2)}) collective-permute-start(bf16[64,2048]{1,0:T(8,128)(2,1)} %collective-permute-done.1.a2), channel_id=1, source_target_pairs={{0,4},{1,5},{2,6},{3,7},{4,0},{5,1},{6,2},{7,3},{8,12},{9,13},{10,... | collective-permute-start | bytes 786440 | tf_op jit(solution)/shard_map/ppermute | solution.py:447
  26.6 38.3 %copy-start.7 = (f32[2048]{0:T(1024)S(1)}, f32[2048]{0:T(1024)}, u32[]{:S(2)}) copy-start(f32[2048]{0:T(1024)} %param.13) | copy-start | bytes 24580
  27.3 18.2 %copy-start.3 = (bf16[1024,768]{1,0:T(8,128)(2,1)S(1)}, bf16[1024,768]{1,0:T(8,128)(2,1)}, u32[]{:S(2)}) copy-start(bf16[1024,768]{1,0:T(8,128)(2,1)} %copy-done.2) | copy-start | bytes 4718596
  27.3 11.4 %collective-permute-start.8 = (bf16[64,512]{1,0:T(8,128)(2,1)S(1)}, bf16[64,512]{1,0:T(8,128)(2,1)S(1)}, u32[]{:S(2)}, u32[]{:S(2)}) collective-permute-start(bf16[64,512]{1,0:T(8,128)(2,1)S(1)} %pad_maximum_fusion), channel_id=1, source_target_pairs={{0,4},{1,5},{2,6},{3,7},{4,0},{5,1},{6,2},{7,3},{8,12},{9,13},{10,... | collective-permute-start | bytes 196616 | tf_op jit(solution)/shard_map/ppermute | solution.py:447
  35.2 1.0 copy-start.4
  38.8 6.8 %collective-permute-start.9 = (bf16[128,512]{1,0:T(8,128)(2,1)S(1)}, bf16[128,512]{1,0:T(8,128)(2,1)S(1)}, u32[]{:S(2)}, u32[]{:S(2)}) collective-permute-start(bf16[128,512]{1,0:T(8,128)(2,1)S(1)} %get-tuple-element.50), channel_id=1, source_target_pairs={{0,16},{16,0},{1,17},{17,1},{2,18},{18,2},{3,19},{19,3},{4,20},{20... | collective-permute-start | bytes 393224 | tf_op jit(solution)/shard_map/ppermute | solution.py:427
  45.6 35.1 %collective-permute-start.19 = (bf16[1024,768]{1,0:T(8,128)(2,1)S(1)}, bf16[1024,768]{1,0:T(8,128)(2,1)S(1)}, u32[]{:S(2)}, u32[]{:S(2)}) collective-permute-start(bf16[1024,768]{1,0:T(8,128)(2,1)S(1)} %copy-done.3), channel_id=1, source_target_pairs={{0,16},{16,0},{1,17},{17,1},{2,18},{18,2},{3,19},{19,3},{4,20},{20... | collective-permute-start | bytes 4718600 | tf_op jit(solution)/shard_map/ppermute | solution.py:427
  47.2 8.0 %collective-permute-start.12 = (bf16[144,512]{1,0:T(8,128)(2,1)S(1)}, bf16[144,512]{1,0:T(8,128)(2,1)S(1)}, u32[]{:S(2)}, u32[]{:S(2)}) collective-permute-start(bf16[144,512]{1,0:T(8,128)(2,1)S(1)} %stream.1.b0), channel_id=1, source_target_pairs={{0,12},{1,13},{2,14},{3,15},{4,0},{5,1},{6,2},{7,3},{8,4},{9,5},{1... | collective-permute-start | bytes 442376 | tf_op jit(solution)/shard_map/ppermute | solution.py:430
  50.8 12.0 %collective-permute-start.11 = (bf16[144,512]{1,0:T(8,128)(2,1)S(1)}, bf16[144,512]{1,0:T(8,128)(2,1)S(1)}, u32[]{:S(2)}, u32[]{:S(2)}) collective-permute-start(bf16[144,512]{1,0:T(8,128)(2,1)S(1)} %stream.1.b0), channel_id=1, source_target_pairs={{0,8},{1,9},{2,10},{3,11},{4,12},{5,13},{6,14},{7,15},{8,0},{9,1},... | collective-permute-start | bytes 442376 | tf_op jit(solution)/shard_map/ppermute | solution.py:430
  50.8 12.6 %collective-permute-start.10 = (bf16[144,512]{1,0:T(8,128)(2,1)S(1)}, bf16[144,512]{1,0:T(8,128)(2,1)S(1)}, u32[]{:S(2)}, u32[]{:S(2)}) collective-permute-start(bf16[144,512]{1,0:T(8,128)(2,1)S(1)} %stream.1.b0), channel_id=1, source_target_pairs={{0,4},{1,5},{2,6},{3,7},{4,8},{5,9},{6,10},{7,11},{8,12},{9,13},{1... | collective-permute-start | bytes 442376 | tf_op jit(solution)/shard_map/ppermute | solution.py:430
  51.8 13.4 %collective-permute-start.13 = (bf16[144,512]{1,0:T(8,128)(2,1)S(1)}, bf16[144,512]{1,0:T(8,128)(2,1)S(1)}, u32[]{:S(2)}, u32[]{:S(2)}) collective-permute-start(bf16[144,512]{1,0:T(8,128)(2,1)S(1)} %stream.1.b0), channel_id=1, source_target_pairs={{0,2},{1,3},{2,0},{3,1},{4,6},{5,7},{6,4},{7,5},{8,10},{9,11},{10,... | collective-permute-start | bytes 442376 | tf_op jit(solution)/shard_map/ppermute | solution.py:444
  55.1 10.2 %collective-permute-start.16 = (bf16[144,512]{1,0:T(8,128)(2,1)S(1)}, bf16[144,512]{1,0:T(8,128)(2,1)S(1)}, u32[]{:S(2)}, u32[]{:S(2)}) collective-permute-start(bf16[144,512]{1,0:T(8,128)(2,1)S(1)} %collective-permute-done.12.b3), channel_id=1, source_target_pairs={{0,2},{1,3},{2,0},{3,1},{4,6},{5,7},{6,4},{7,5},{8,10},{9,11},{10,... | collective-permute-start | bytes 442376 | tf_op jit(solution)/shard_map/ppermute | solution.py:444
  62.8 6.1 %collective-permute-start.15 = (bf16[144,512]{1,0:T(8,128)(2,1)S(1)}, bf16[144,512]{1,0:T(8,128)(2,1)S(1)}, u32[]{:S(2)}, u32[]{:S(2)}) collective-permute-start(bf16[144,512]{1,0:T(8,128)(2,1)S(1)} %collective-permute-done.11.b2), channel_id=1, source_target_pairs={{0,2},{1,3},{2,0},{3,1},{4,6},{5,7},{6,4},{7,5},{8,10},{9,11},{10,... | collective-permute-start | bytes 442376 | tf_op jit(solution)/shard_map/ppermute | solution.py:444
  63.4 7.1 %collective-permute-start.14 = (bf16[144,512]{1,0:T(8,128)(2,1)S(1)}, bf16[144,512]{1,0:T(8,128)(2,1)S(1)}, u32[]{:S(2)}, u32[]{:S(2)}) collective-permute-start(bf16[144,512]{1,0:T(8,128)(2,1)S(1)} %collective-permute-done.10.b1), channel_id=1, source_target_pairs={{0,2},{1,3},{2,0},{3,1},{4,6},{5,7},{6,4},{7,5},{8,10},{9,11},{10,... | collective-permute-start | bytes 442376 | tf_op jit(solution)/shard_map/ppermute | solution.py:444
  65.2 6.1 %collective-permute-start.18 = (bf16[128,2176]{1,0:T(8,128)(2,1)S(1)}, bf16[128,2176]{1,0:T(8,128)(2,1)S(1)}, u32[]{:S(2)}, u32[]{:S(2)}) collective-permute-start(bf16[128,2176]{1,0:T(8,128)(2,1)S(1)} %get-tuple-element.54.group), channel_id=1, source_target_pairs={{0,1},{1,0},{2,3},{3,2},{4,5},{5,4},{6,7},{7,6},{8,9},{9,8},{10,11... | collective-permute-start | bytes 1671176 | tf_op jit(solution)/shard_map/ppermute | solution.py:444
  71.3 2.0 %collective-permute-start.17 = (bf16[128,2176]{1,0:T(8,128)(2,1)S(1)}, bf16[128,2176]{1,0:T(8,128)(2,1)S(1)}, u32[]{:S(2)}, u32[]{:S(2)}) collective-permute-start(bf16[128,2176]{1,0:T(8,128)(2,1)S(1)} %get-tuple-element.53.group_x), channel_id=1, source_target_pairs={{0,1},{1,0},{2,3},{3,2},{4,5},{5,4},{6,7},{7,6},{8,9},{9,8},{10,11... | collective-permute-start | bytes 1671176 | tf_op jit(solution)/shard_map/ppermute | solution.py:444
  80.6 1.4 %copy-start.1 = (bf16[1,768,1024]{2,1,0:T(8,128)(2,1)S(1)}, bf16[1,768,1024]{2,1,0:T(8,128)(2,1)}, u32[]{:S(2)}) copy-start(bf16[1,768,1024]{2,1,0:T(8,128)(2,1)} %param.18) | copy-start | bytes 4718596
  83.0 2.1 %collective-permute-start.20 = (bf16[128,512]{1,0:T(8,128)(2,1)S(1)}, bf16[128,512]{1,0:T(8,128)(2,1)S(1)}, u32[]{:S(2)}, u32[]{:S(2)}) collective-permute-start(bf16[128,512]{1,0:T(8,128)(2,1)S(1)} %get-tuple-element.63), channel_id=1, source_target_pairs={{0,1},{1,0},{2,3},{3,2},{4,5},{5,4},{6,7},{7,6},{8,9},{9,8},{10,11... | collective-permute-start | bytes 393224 | tf_op jit(solution)/shard_map/ppermute | solution.py:444
  83.1 2.0 %collective-permute-start.21 = (bf16[128,512]{1,0:T(8,128)(2,1)S(1)}, bf16[128,512]{1,0:T(8,128)(2,1)S(1)}, u32[]{:S(2)}, u32[]{:S(2)}) collective-permute-start(bf16[128,512]{1,0:T(8,128)(2,1)S(1)} %get-tuple-element.64), channel_id=1, source_target_pairs={{0,1},{1,0},{2,3},{3,2},{4,5},{5,4},{6,7},{7,6},{8,9},{9,8},{10,11... | collective-permute-start | bytes 393224 | tf_op jit(solution)/shard_map/ppermute | solution.py:444
  83.6 12.0 %collective-permute-start.27 = (bf16[256,768]{1,0:T(8,128)(2,1)S(1)}, bf16[256,768]{1,0:T(8,128)(2,1)S(1)}, u32[]{:S(2)}, u32[]{:S(2)}) collective-permute-start(bf16[256,768]{1,0:T(8,128)(2,1)S(1)} %get-tuple-element.60.far), channel_id=1, source_target_pairs={{0,16},{16,0},{1,17},{17,1},{2,18},{18,2},{3,19},{19,3},{4,20},{20... | collective-permute-start | bytes 1179656 | tf_op jit(solution)/shard_map/ppermute | solution.py:427
  85.2 10.4 %collective-permute-start.22 = (bf16[128,1024]{1,0:T(8,128)(2,1)S(1)}, bf16[128,1024]{1,0:T(8,128)(2,1)S(1)}, u32[]{:S(2)}, u32[]{:S(2)}) collective-permute-start(bf16[128,1024]{1,0:T(8,128)(2,1)S(1)} %fold.2), channel_id=1, source_target_pairs={{0,2},{1,3},{2,0},{3,1},{4,6},{5,7},{6,4},{7,5},{8,10},{9,11},{10,... | collective-permute-start | bytes 786440 | tf_op jit(solution)/shard_map/ppermute | solution.py:444
  85.8 17.3 %collective-permute-start.31 = (bf16[256,768]{1,0:T(8,128)(2,1)S(1)}, bf16[256,768]{1,0:T(8,128)(2,1)S(1)}, u32[]{:S(2)}, u32[]{:S(2)}) collective-permute-start(bf16[256,768]{1,0:T(8,128)(2,1)S(1)} %get-tuple-element.61.near), channel_id=1, source_target_pairs={{0,16},{16,0},{1,17},{17,1},{2,18},{18,2},{3,19},{19,3},{4,20},{20... | collective-permute-start | bytes 1179656 | tf_op jit(solution)/shard_map/ppermute | solution.py:427
  96.2 1.4 %collective-permute-start.28 = (bf16[128,512]{1,0:T(8,128)(2,1)S(1)}, bf16[128,512]{1,0:T(8,128)(2,1)S(1)}, u32[]{:S(2)}, u32[]{:S(2)}) collective-permute-start(bf16[128,512]{1,0:T(8,128)(2,1)S(1)} %get-tuple-element.72), channel_id=1, source_target_pairs={{0,1},{1,0},{2,3},{3,2},{4,5},{5,4},{6,7},{7,6},{8,9},{9,8},{10,11... | collective-permute-start | bytes 393224 | tf_op jit(solution)/shard_map/ppermute | solution.py:444
  96.2 1.5 %collective-permute-start.29 = (bf16[128,512]{1,0:T(8,128)(2,1)S(1)}, bf16[128,512]{1,0:T(8,128)(2,1)S(1)}, u32[]{:S(2)}, u32[]{:S(2)}) collective-permute-start(bf16[128,512]{1,0:T(8,128)(2,1)S(1)} %get-tuple-element.73), channel_id=1, source_target_pairs={{0,1},{1,0},{2,3},{3,2},{4,5},{5,4},{6,7},{7,6},{8,9},{9,8},{10,11... | collective-permute-start | bytes 393224 | tf_op jit(solution)/shard_map/ppermute | solution.py:444
  96.7 1.7 %collective-permute-start.23 = (bf16[128,512]{1,0:T(8,128)(2,1)S(1)}, bf16[128,512]{1,0:T(8,128)(2,1)S(1)}, u32[]{:S(2)}, u32[]{:S(2)}) collective-permute-start(bf16[128,512]{1,0:T(8,128)(2,1)S(1)} %get-tuple-element.66), channel_id=1, source_target_pairs={{0,1},{1,0},{2,3},{3,2},{4,5},{5,4},{6,7},{7,6},{8,9},{9,8},{10,11... | collective-permute-start | bytes 393224 | tf_op jit(solution)/shard_map/ppermute | solution.py:444
  96.8 1.6 %collective-permute-start.24 = (bf16[128,512]{1,0:T(8,128)(2,1)S(1)}, bf16[128,512]{1,0:T(8,128)(2,1)S(1)}, u32[]{:S(2)}, u32[]{:S(2)}) collective-permute-start(bf16[128,512]{1,0:T(8,128)(2,1)S(1)} %get-tuple-element.67), channel_id=1, source_target_pairs={{0,1},{1,0},{2,3},{3,2},{4,5},{5,4},{6,7},{7,6},{8,9},{9,8},{10,11... | collective-permute-start | bytes 393224 | tf_op jit(solution)/shard_map/ppermute | solution.py:444
  97.8 8.9 %collective-permute-start.30 = (bf16[128,1024]{1,0:T(8,128)(2,1)S(1)}, bf16[128,1024]{1,0:T(8,128)(2,1)S(1)}, u32[]{:S(2)}, u32[]{:S(2)}) collective-permute-start(bf16[128,1024]{1,0:T(8,128)(2,1)S(1)} %fold.3), channel_id=1, source_target_pairs={{0,2},{1,3},{2,0},{3,1},{4,6},{5,7},{6,4},{7,5},{8,10},{9,11},{10,... | collective-permute-start | bytes 786440 | tf_op jit(solution)/shard_map/ppermute | solution.py:444
  98.5 8.2 %collective-permute-start.26 = (bf16[64,1024]{1,0:T(8,128)(2,1)S(1)}, bf16[64,1024]{1,0:T(8,128)(2,1)S(1)}, u32[]{:S(2)}, u32[]{:S(2)}) collective-permute-start(bf16[64,1024]{1,0:T(8,128)(2,1)S(1)} %get-tuple-element.69), channel_id=1, source_target_pairs={{0,4},{1,13},{2,6},{3,15},{4,8},{5,1},{6,10},{7,3},{8,12},{9,5},{1... | collective-permute-start | bytes 393224 | tf_op jit(solution)/shard_map/ppermute | solution.py:441
  100.2 18.4 %copy-start.9 = (f32[2048]{0:T(1024)S(1)}, f32[2048]{0:T(1024)}, u32[]{:S(2)}) copy-start(f32[2048]{0:T(1024)} %param.19) | copy-start | bytes 24580
  100.2 6.5 %collective-permute-start.25 = (bf16[64,1024]{1,0:T(8,128)(2,1)S(1)}, bf16[64,1024]{1,0:T(8,128)(2,1)S(1)}, u32[]{:S(2)}, u32[]{:S(2)}) collective-permute-start(bf16[64,1024]{1,0:T(8,128)(2,1)S(1)} %get-tuple-element.68.own), channel_id=1, source_target_pairs={{1,9},{3,11},{5,13},{7,15},{9,1},{11,3},{13,5},{15,7},{17,25},{19,... | collective-permute-start | bytes 393224 | tf_op jit(solution)/shard_map/ppermute | solution.py:441
  103.7 3.0 %collective-permute-start.32 = (bf16[128,512]{1,0:T(8,128)(2,1)S(1)}, bf16[128,512]{1,0:T(8,128)(2,1)S(1)}, u32[]{:S(2)}, u32[]{:S(2)}) collective-permute-start(bf16[128,512]{1,0:T(8,128)(2,1)S(1)} %get-tuple-element.76), channel_id=1, source_target_pairs={{0,1},{1,0},{2,3},{3,2},{4,5},{5,4},{6,7},{7,6},{8,9},{9,8},{10,11... | collective-permute-start | bytes 393224 | tf_op jit(solution)/shard_map/ppermute | solution.py:444
  104.8 1.9 %collective-permute-start.33 = (bf16[128,512]{1,0:T(8,128)(2,1)S(1)}, bf16[128,512]{1,0:T(8,128)(2,1)S(1)}, u32[]{:S(2)}, u32[]{:S(2)}) collective-permute-start(bf16[128,512]{1,0:T(8,128)(2,1)S(1)} %get-tuple-element.77), channel_id=1, source_target_pairs={{0,1},{1,0},{2,3},{3,2},{4,5},{5,4},{6,7},{7,6},{8,9},{9,8},{10,11... | collective-permute-start | bytes 393224 | tf_op jit(solution)/shard_map/ppermute | solution.py:444
  106.8 5.0 %collective-permute-start.34 = (bf16[64,1024]{1,0:T(8,128)(2,1)S(1)}, bf16[64,1024]{1,0:T(8,128)(2,1)S(1)}, u32[]{:S(2)}, u32[]{:S(2)}) collective-permute-start(bf16[64,1024]{1,0:T(8,128)(2,1)S(1)} %get-tuple-element.78), channel_id=1, source_target_pairs={{0,16},{1,25},{2,18},{3,27},{4,20},{5,29},{6,22},{7,31},{8,24},{9,... | collective-permute-start | bytes 393224 | tf_op jit(solution)/shard_map/ppermute | solution.py:441
  108.4 8.3 %collective-permute-start.35 = (bf16[64,1024]{1,0:T(8,128)(2,1)S(1)}, bf16[64,1024]{1,0:T(8,128)(2,1)S(1)}, u32[]{:S(2)}, u32[]{:S(2)}) collective-permute-start(bf16[64,1024]{1,0:T(8,128)(2,1)S(1)} %get-tuple-element.79), channel_id=1, source_target_pairs={{0,20},{1,29},{2,22},{3,31},{4,24},{5,17},{6,26},{7,19},{8,28},{9,... | collective-permute-start | bytes 393224 | tf_op jit(solution)/shard_map/ppermute | solution.py:441
  116.8 1.8 %collective-permute-start.36 = (bf16[64,1024]{1,0:T(8,128)(2,1)S(1)}, bf16[64,1024]{1,0:T(8,128)(2,1)S(1)}, u32[]{:S(2)}, u32[]{:S(2)}) collective-permute-start(bf16[64,1024]{1,0:T(8,128)(2,1)S(1)} %get-tuple-element.81), channel_id=1, source_target_pairs={{0,1},{1,0},{2,3},{3,2},{4,5},{5,4},{6,7},{7,6},{8,9},{9,8},{10,11... | collective-permute-start | bytes 393224 | tf_op jit(solution)/shard_map/ppermute | solution.py:444

commit v12 on v10

--- a/solution.py
+++ b/solution.py
@@ -219,17 +219,21 @@
     block_ref[count:, :] = share[...]
 
 
-def piece_kernel(starts, weights, out, semaphores):
-    depth, width = out.shape[0] // 4, out.shape[1] // 2
-    copies = [
-        pltpu.make_async_copy(
-            weights.at[pl.ds(k * depth, depth), pl.ds(starts[i], width)],
-            out.at[pl.ds(k * depth, depth), pl.ds(i * width, width)],
-            semaphores.at[i, k],
-        )
-        for i in range(2)
-        for k in range(4)
-    ]
+def piece_kernel(starts, weights, *refs):
+    *outs, semaphores = refs
+    copies = []
+    at = 0
+    for k, out in enumerate(outs):
+        depth, width = out.shape[0], out.shape[1] // 2
+        for i in range(2):
+            copies.append(
+                pltpu.make_async_copy(
+                    weights.at[pl.ds(at, depth), pl.ds(starts[i], width)],
+                    out.at[:, pl.ds(i * width, width)],
+                    semaphores.at[i, k],
+                )
+            )
+        at += depth
     for copy in copies:
         copy.start()
     for copy in copies:
@@ -270,8 +274,9 @@
     ).astype(BF16)
 
 
-def first_gate_kernel(group_x, group_cx, group, group_c, own, *refs):
-    *early, inner_ref, part_ref, other_ref, share_ref, mine_ref = refs
+def first_gate_kernel(
+    group_x, group_cx, group, group_c, own, early, inner_ref, part_ref, other_ref, share_ref, mine_ref
+):
     expert, outer, inner, dp = seat()
     count = group.shape[0]
     half = other_ref.shape[1]
@@ -285,13 +290,9 @@
         share = jnp.sum(jnp.where(picked, share, 0.0), axis=1, keepdims=True)
         share_ref[rows, :] = jnp.broadcast_to(share, (count, 128))
     mine, other = mine_ref[...], other_ref[...]
-    at = 0
-    for piece in early:
-        size = piece.shape[1] // 2
-        gate = dot(mine, own[:, at : at + size]) + dot(other, piece[:, 0:size])
-        up = dot(mine, own[:, 2 * cut + at : 2 * cut + at + size]) + dot(other, piece[:, size:])
-        inner_ref[:, at : at + size] = swiglu(gate, up, share_ref[:, 0:1])
-        at += size
+    gate = dot(mine, own[:, 0:cut]) + dot(other, early[:, 0:cut])
+    up = dot(mine, own[:, 2 * cut : 3 * cut]) + dot(other, early[:, cut : 2 * cut])
+    inner_ref[...] = swiglu(gate, up, share_ref[:, 0:1])
     part_ref[:, 0:cut] = dot(mine, own[:, cut : 2 * cut])
     part_ref[:, cut : 2 * cut] = dot(mine, own[:, 3 * cut : 4 * cut])
 
@@ -300,22 +301,18 @@
     *late, far_ref, near_ref = refs
     cut = first.shape[1]
     half = far_ref.shape[0]
+    gate, up = part[:, 0:cut], part[:, cut : 2 * cut]
+    at = 0
+    for piece in late:
+        rows = other[:, at : at + piece.shape[0]]
+        gate = gate + dot(rows, piece[:, 0:cut])
+        up = up + dot(rows, piece[:, cut : 2 * cut])
+        at += piece.shape[0]
+    value = swiglu(gate, up, share[:, 0:1])
     far_ref[:, 0:cut] = first[0:half, :]
     near_ref[:, 0:cut] = first[half:, :]
-    at = 0
-    for piece in late:
-        size = piece.shape[1] // 2
-        gate = part[:, at : at + size] + dot(other[...], piece[:, 0:size])
-        up = part[:, cut + at : cut + at + size] + dot(other[...], piece[:, size : 2 * size])
-        value = swiglu(gate, up, share[:, 0:1])
-        cols = slice(cut + at, cut + at + size)
-        far_ref[:, cols] = value[:half]
-        near_ref[:, cols] = value[half:]
-        at += size
-
-
-def column_chunks(wd):
-    return [slice(at, at + 256) for at in range(0, wd.shape[1], 256)]
+    far_ref[:, cut : 2 * cut] = value[:half]
+    near_ref[:, cut : 2 * cut] = value[half:]
 
 
 def down_both_kernel(far, near, wd, keep_far, *refs):
@@ -448,14 +445,14 @@
     def after(x, *results):
         return lax.optimization_barrier((x, *results))[0]
 
-    def weight_piece(first, size, mib=8):
+    def weight_piece(first, size, depths):
         return pl.pallas_call(
             functools.partial(piece_kernel, (first, hidden + first)),
-            out_shape=shape_of(half_width, 2 * size),
+            out_shape=tuple(shape_of(depth, 2 * size) for depth in depths),
             in_specs=[pl.BlockSpec(memory_space=pl.ANY)],
-            out_specs=vmem,
-            scratch_shapes=[pltpu.SemaphoreType.DMA((2, 4))],
-            compiler_params=kernel_params(mib),
+            out_specs=tuple(vmem for _ in depths),
+            scratch_shapes=[pltpu.SemaphoreType.DMA((2, len(depths)))],
+            compiler_params=kernel_params(8),
             cost_estimate=small_cost(),
             name="weight_piece",
         )(w_gate_up[0])
@@ -475,9 +472,9 @@
         first=smem,
     )
     cut_width = hidden // 2
-    early_pieces = [weight_piece(0, cut_width, 58)]
-    late_pieces = [weight_piece(cut_width, hidden - cut_width)]
-    gate_up_early = [swap_dp(piece) for piece in early_pieces]
+    early_piece = weight_piece(0, cut_width, (half_width,))[0]
+    late_pieces = weight_piece(cut_width, cut_width, (half_width * 640 // 1024, half_width * 384 // 1024))
+    gate_up_early = swap_dp(early_piece)
     a = [attn[0], swap_outer(attn[0], 1), swap_outer(attn[0], 2)]
     w_x = swap_inner(w_out, 2)
     r_2 = swap_outer(r_23, 2)
@@ -492,7 +489,8 @@
         "projection",
         8,
         (product, product),
-        *a,
+        *a[:3],
+        after(a[3], r_13),
         w_out,
         w_c,
         w_x,
@@ -502,14 +500,14 @@
             pltpu.VMEM((8 * rows_here, quarter), BF16),
         ),
     )
-    arrived = swap_dp(after(send, gate_up_early[0], r_13))
-    gate_up_late = [swap_dp(after(piece, arrived)) for piece in late_pieces]
+    arrived = swap_dp(send)
+    gate_up_late = [swap_dp(after(piece, send)) for piece in late_pieces]
     (block,) = call(
         stream_kernel,
         "stream",
         4,
         (shape_of(4 * rows_here + expert_count, quarter),),
-        keep,
+        after(keep, gate_up_early),
         arrived,
         r_own,
         r_13,
@@ -545,7 +543,7 @@
         group,
         group_c,
         w_gate_up[0],
-        *gate_up_early,
+        gate_up_early,
         scratch=(pltpu.VMEM((row_total, half_width), BF16),),
     )
     inner_half = shape_of(half_rows, hidden)

time: 121 us -> 117 us (0.967)
  Pallas kernels: 17.6 us -> 13.8 us
  waiting for transfers between devices: 59.6 us -> 56.4 us
  local copies, waits for them, and re-layouts: 2.06 us -> 4.58 us
    ppermute x5 -> x6, waiting for transfers between devices: 19 us -> 16.1 us  [swap_dp(): return lax.ppermute(x, 'dp', [(0, 1), (1, 0)])]
    pallas_call x2, Pallas kernels: 3.06 us -> 0.39 us  [weight_piece(): pl.pallas_call(functools.partial(piece_kernel, (first, hidden + first)),...]
    unnamed x22 -> x28, local copies, waits for them, and re-layouts: 2.06 us -> 4.57 us
    ppermute x20, waiting for transfers between devices: 11.8 us -> 10.4 us  [swap_inner(): return lax.ppermute(x, 'expert', [(i, i ^ j) for i in range(expert_count)])]
    ppermute x20, starting transfers between devices: 14.2 us -> 15.4 us  [swap_inner(): return lax.ppermute(x, 'expert', [(i, i ^ j) for i in range(expert_count)])]
    ppermute x5 -> x6, starting transfers between devices: 8.95 us -> 9.03 us  [swap_dp(): return lax.ppermute(x, 'dp', [(0, 1), (1, 0)])]
  transfers between devices with their start and end apart: 37 -> 38, of which waited for: 19 -> 19; matrix products, arithmetic and copies ran while one was open for 1% -> 1% of each run, Pallas kernels for 10% -> 9%
where the time goes in v12:
time: 117 us
  waiting for transfers between devices  56.4 us (48%)
  starting transfers between devices  39.6 us (34%)
  Pallas kernels  13.8 us (12%)
  local copies, waits for them, and re-layouts  4.58 us (4%)
  between operations  1.54 us (1%)
    ppermute x6, waiting for transfers between devices, swap_dp(): return lax.ppermute(x, 'dp', [(0, 1), (1, 0)])  16.1 us
    ppermute x20, starting transfers between devices, swap_inner(): return lax.ppermute(x, 'expert', [(i, i ^ j) for i in range(expert_count)])  15.4 us
    pallas_call x17, Pallas kernels, call(): pl.pallas_call(kernel, out_shape=outs, in_specs=[first] + [vmem] * (len(a...  13.4 us
    ppermute x5, waiting for transfers between devices, swap_outer(): lax.ppermute(x, 'expert', [(i, i ^ 4 * s) for i in range(expert_count)])  12.1 us
    ppermute x20, waiting for transfers between devices, swap_inner(): return lax.ppermute(x, 'expert', [(i, i ^ j) for i in range(expert_count)])  10.4 us
    ppermute x4, waiting for transfers between devices, send_outer(): return lax.ppermute(x, ('dp', 'expert'), pairs)  10.2 us
    ppermute x6, starting transfers between devices, swap_dp(): return lax.ppermute(x, 'dp', [(0, 1), (1, 0)])  9.03 us
    ppermute x3, waiting for transfers between devices, shift_outer(): lax.ppermute(x, 'expert', [(i, (i + 4 * s) % expert_count) for i in range...  7.64 us
  transfers between devices with their start and end apart: 38, of which 19 were waited for; matrix products, arithmetic and copies ran while one was open for 1% of the time, Pallas kernels for 9%

profile of v12, /device:TPU:0, one launch (start us, length us, event | category | flops | bytes accessed | tf_op | source)
XLA Modules:
  0.0 116.6 jit_solution(5368476248067918039)
XLA Ops:
  0.6 1.9 %copy-done = bf16[1,1024,1536]{2,1,0:T(8,128)(2,1)S(1)} copy-done((bf16[1,1024,1536]{2,1,0:T(8,128)(2,1)S(1)}, bf16[1,1024,1536]{2,1,0:T(8,128)(2,1)}, u32[]{:S(2)}) %copy-start) | copy-done | bytes 3145752
  2.7 3.0 %collective-permute-start.8 = (bf16[1024,768]{1,0:T(8,128)(2,1)S(1)}, bf16[1024,768]{1,0:T(8,128)(2,1)S(1)}, u32[]{:S(2)}, u32[]{:S(2)}) collective-permute-start(bf16[1024,768]{1,0:T(8,128)(2,1)S(1)} %weight_piece.3), channel_id=1, source_target_pairs={{0,16},{16,0},{1,17},{17,1},{2,18},{18,2},{3,19},{19,3},{4,20},{20... | collective-permute-start | bytes 4718600 | tf_op jit(solution)/shard_map/ppermute | solution.py:423
  5.7 1.5 %collective-permute-start.5 = (bf16[2048,128]{1,0:T(8,128)(2,1)}, bf16[2048,128]{1,0:T(8,128)(2,1)}, u32[]{:S(2)}, u32[]{:S(2)}) collective-permute-start(bf16[2048,128]{1,0:T(8,128)(2,1)} %w0.1), channel_id=1, source_target_pairs={{0,2},{1,3},{2,0},{3,1},{4,6},{5,7},{6,4},{7,5},{8,10},{9,11},{10,... | collective-permute-start | bytes 1572872 | tf_op jit(solution)/shard_map/ppermute | solution.py:440
  7.2 0.6 cut_resid.1
  7.9 2.6 %collective-permute-start.2 = (bf16[64,512]{1,0:T(8,128)(2,1)}, bf16[64,512]{1,0:T(8,128)(2,1)S(1)}, u32[]{:S(2)}, u32[]{:S(2)}) collective-permute-start(bf16[64,512]{1,0:T(8,128)(2,1)} %get-tuple-element.46), channel_id=1, source_target_pairs={{0,8},{1,9},{2,10},{3,11},{4,12},{5,13},{6,14},{7,15},{8,0},{9,1},... | collective-permute-start | bytes 196616 | tf_op jit(solution)/shard_map/ppermute | solution.py:443
  10.5 0.3 collective-permute-start.1
  10.8 1.6 %collective-permute-start = (bf16[64,2048]{1,0:T(8,128)(2,1)S(1)}, bf16[64,2048]{1,0:T(8,128)(2,1)}, u32[]{:S(2)}, u32[]{:S(2)}) collective-permute-start(bf16[64,2048]{1,0:T(8,128)(2,1)S(1)} %bitcast.17), channel_id=1, source_target_pairs={{0,4},{1,5},{2,6},{3,7},{4,0},{5,1},{6,2},{7,3},{8,12},{9,13},{10,... | collective-permute-start | bytes 786440 | tf_op jit(solution)/shard_map/ppermute | solution.py:443
  12.6 1.0 copy-done.8
  13.6 0.8 copy-done.10
  15.2 0.8 copy.13
  15.9 0.4 share.1
  16.4 3.1 %collective-permute-done.5.w2 = bf16[2048,128]{1,0:T(8,128)(2,1)} collective-permute-done((bf16[2048,128]{1,0:T(8,128)(2,1)}, bf16[2048,128]{1,0:T(8,128)(2,1)}, u32[]{:S(2)}, u32[]{:S(2)}) %collective-permute-start.5) | collective-permute-done | bytes 524320 | tf_op jit(solution)/shard_map/ppermute | solution.py:440
  19.5 0.5 collective-permute-start.6
  20.0 5.4 %collective-permute-done.1.a2 = bf16[64,2048]{1,0:T(8,128)(2,1)} collective-permute-done((bf16[64,2048]{1,0:T(8,128)(2,1)S(1)}, bf16[64,2048]{1,0:T(8,128)(2,1)}, u32[]{:S(2)}, u32[]{:S(2)}) %collective-permute-start.1) | collective-permute-done | bytes 262176 | tf_op jit(solution)/shard_map/ppermute | solution.py:443
  25.4 0.2 collective-permute-start.3
  25.6 0.8 pad_maximum_fusion
  26.4 1.9 %collective-permute-start.4 = (bf16[64,512]{1,0:T(8,128)(2,1)S(1)}, bf16[64,512]{1,0:T(8,128)(2,1)S(1)}, u32[]{:S(2)}, u32[]{:S(2)}) collective-permute-start(bf16[64,512]{1,0:T(8,128)(2,1)S(1)} %pad_maximum_fusion), channel_id=1, source_target_pairs={{0,4},{1,5},{2,6},{3,7},{4,0},{5,1},{6,2},{7,3},{8,12},{9,13},{10,... | collective-permute-start | bytes 196616 | tf_op jit(solution)/shard_map/ppermute | solution.py:443
  28.2 6.7 %collective-permute-done.4.r13 = bf16[64,512]{1,0:T(8,128)(2,1)S(1)} collective-permute-done((bf16[64,512]{1,0:T(8,128)(2,1)S(1)}, bf16[64,512]{1,0:T(8,128)(2,1)S(1)}, u32[]{:S(2)}, u32[]{:S(2)}) %collective-permute-start.4) | collective-permute-done | bytes 65568 | tf_op jit(solution)/shard_map/ppermute | solution.py:443
  34.9 2.8 %projection.1 = (bf16[128,512]{1,0:T(8,128)(2,1)S(1)}, bf16[128,512]{1,0:T(8,128)(2,1)S(1)}) custom-call(bf16[64,2048]{1,0:T(8,128)(2,1)S(1)} %bitcast.18, bf16[64,2048]{1,0:T(8,128)(2,1)} %collective-permute-done.a1, bf16[64,2048]{1,0:T(8,128)(2,1)} %collective-permute-done.1.a2, bf16[64,2048]{1,0:T(8,128)(2,1)S(1)} %collective-permute-done.3.a3, ...), custom_call_target="tpu_custom_call" | custom-call | flops 1 | bytes 1 | tf_op jit(solution)/shard_map/projection/pallas_call | solution.py:411
  37.8 0.6 collective-permute-start.9
  38.3 1.5 %collective-permute-start.19 = (bf16[640,768]{1,0:T(8,128)(2,1)S(1)}, bf16[640,768]{1,0:T(8,128)(2,1)S(1)}, u32[]{:S(2)}, u32[]{:S(2)}) collective-permute-start(bf16[640,768]{1,0:T(8,128)(2,1)S(1)} %copy-done.9), channel_id=1, source_target_pairs={{0,16},{16,0},{1,17},{17,1},{2,18},{18,2},{3,19},{19,3},{4,20},{20... | collective-permute-start | bytes 2949128 | tf_op jit(solution)/shard_map/ppermute | solution.py:423
  39.9 1.1 collective-permute-done.8.early
  41.0 3.3 %collective-permute-done.9.arrived = bf16[128,512]{1,0:T(8,128)(2,1)S(1)} collective-permute-done((bf16[128,512]{1,0:T(8,128)(2,1)S(1)}, bf16[128,512]{1,0:T(8,128)(2,1)S(1)}, u32[]{:S(2)}, u32[]{:S(2)}) %collective-permute-start.9) | collective-permute-done | bytes 131104 | tf_op jit(solution)/shard_map/ppermute | solution.py:423
  44.3 3.5 %collective-permute-start.12 = (bf16[144,512]{1,0:T(8,128)(2,1)S(1)}, bf16[144,512]{1,0:T(8,128)(2,1)S(1)}, u32[]{:S(2)}, u32[]{:S(2)}) collective-permute-start(bf16[144,512]{1,0:T(8,128)(2,1)S(1)} %stream.1.b0), channel_id=1, source_target_pairs={{0,12},{1,13},{2,14},{3,15},{4,0},{5,1},{6,2},{7,3},{8,4},{9,5},{1... | collective-permute-start | bytes 442376 | tf_op jit(solution)/shard_map/ppermute | solution.py:426
  47.8 0.8 collective-permute-start.10
  48.7 1.9 %collective-permute-start.13 = (bf16[144,512]{1,0:T(8,128)(2,1)S(1)}, bf16[144,512]{1,0:T(8,128)(2,1)S(1)}, u32[]{:S(2)}, u32[]{:S(2)}) collective-permute-start(bf16[144,512]{1,0:T(8,128)(2,1)S(1)} %stream.1.b0), channel_id=1, source_target_pairs={{0,2},{1,3},{2,0},{3,1},{4,6},{5,7},{6,4},{7,5},{8,10},{9,11},{10,... | collective-permute-start | bytes 442376 | tf_op jit(solution)/shard_map/ppermute | solution.py:440
  50.5 1.6 %collective-permute-done.12.b3 = bf16[144,512]{1,0:T(8,128)(2,1)S(1)} collective-permute-done((bf16[144,512]{1,0:T(8,128)(2,1)S(1)}, bf16[144,512]{1,0:T(8,128)(2,1)S(1)}, u32[]{:S(2)}, u32[]{:S(2)}) %collective-permute-start.12) | collective-permute-done | bytes 147488 | tf_op jit(solution)/shard_map/ppermute | solution.py:426
  52.1 1.7 %collective-permute-start.16 = (bf16[144,512]{1,0:T(8,128)(2,1)S(1)}, bf16[144,512]{1,0:T(8,128)(2,1)S(1)}, u32[]{:S(2)}, u32[]{:S(2)}) collective-permute-start(bf16[144,512]{1,0:T(8,128)(2,1)S(1)} %collective-permute-done.12.b3), channel_id=1, source_target_pairs={{0,2},{1,3},{2,0},{3,1},{4,6},{5,7},{6,4},{7,5},{8,10},{9,11},{10,... | collective-permute-start | bytes 442376 | tf_op jit(solution)/shard_map/ppermute | solution.py:440
  53.8 6.0 %collective-permute-done.11.b2 = bf16[144,512]{1,0:T(8,128)(2,1)S(1)} collective-permute-done((bf16[144,512]{1,0:T(8,128)(2,1)S(1)}, bf16[144,512]{1,0:T(8,128)(2,1)S(1)}, u32[]{:S(2)}, u32[]{:S(2)}) %collective-permute-start.11) | collective-permute-done | bytes 147488 | tf_op jit(solution)/shard_map/ppermute | solution.py:426
  59.9 1.1 collective-permute-start.15
  61.0 0.9 collective-permute-start.14
  61.9 1.2 collective-permute-start.20
  63.1 0.3 norm.2
  63.5 2.3 %collective-permute-done.15.b2 = bf16[144,512]{1,0:T(8,128)(2,1)S(1)} collective-permute-done((bf16[144,512]{1,0:T(8,128)(2,1)S(1)}, bf16[144,512]{1,0:T(8,128)(2,1)S(1)}, u32[]{:S(2)}, u32[]{:S(2)}) %collective-permute-start.15) | collective-permute-done | bytes 147488 | tf_op jit(solution)/shard_map/ppermute | solution.py:440
  65.8 1.6 %collective-permute-done.14.b1 = bf16[144,512]{1,0:T(8,128)(2,1)S(1)} collective-permute-done((bf16[144,512]{1,0:T(8,128)(2,1)S(1)}, bf16[144,512]{1,0:T(8,128)(2,1)S(1)}, u32[]{:S(2)}, u32[]{:S(2)}) %collective-permute-start.14) | collective-permute-done | bytes 147488 | tf_op jit(solution)/shard_map/ppermute | solution.py:440
  67.3 0.8 norm.3
  68.1 2.0 %collective-permute-done.17.group_cx = bf16[128,2176]{1,0:T(8,128)(2,1)S(1)} collective-permute-done((bf16[128,2176]{1,0:T(8,128)(2,1)S(1)}, bf16[128,2176]{1,0:T(8,128)(2,1)S(1)}, u32[]{:S(2)}, u32[]{:S(2)}) %collective-permute-start.17) | collective-permute-done | bytes 557088 | tf_op jit(solution)/shard_map/ppermute | solution.py:440
  70.1 3.4 %first_gate_up.1 = (bf16[512,384]{1,0:T(8,128)(2,1)S(1)}, f32[512,768]{1,0:T(8,128)S(1)}, bf16[512,1024]{1,0:T(8,128)(2,1)S(1)}, f32[512,128]{1,0:T(8,128)S(1)}) custom-call(bf16[128,2176]{1,0:T(8,128)(2,1)S(1)} %get-tuple-element.58.group_x, bf16[128,2176]{1,0:T(8,128)(2,1)S(1)} %collective-permute-done.17.group_cx, ...), custom_call_target="tpu_custom_call" | custom-call | flops 1 | bytes 1 | tf_op jit(solution)/shard_map/first_gate_up/pallas_call | solution.py:411
  73.5 3.1 %collective-permute-done.20.refs_1_ = bf16[384,768]{1,0:T(8,128)(2,1)S(1)} collective-permute-done((bf16[384,768]{1,0:T(8,128)(2,1)S(1)}, bf16[384,768]{1,0:T(8,128)(2,1)S(1)}, u32[]{:S(2)}, u32[]{:S(2)}) %collective-permute-start.20) | collective-permute-done | bytes 589856 | tf_op jit(solution)/shard_map/ppermute | solution.py:423
  76.7 1.5 %last_gate_up.1 = (bf16[256,768]{1,0:T(8,128)(2,1)S(1)}, bf16[256,768]{1,0:T(8,128)(2,1)S(1)}) custom-call(bf16[512,384]{1,0:T(8,128)(2,1)S(1)} %get-tuple-element.60.first, f32[512,768]{1,0:T(8,128)S(1)} %get-tuple-element.61.part, bf16[512,1024]{1,0:T(8,128)(2,1)S(1)} %get-tuple-element.62.other, f32[512,128]{1,0:T(8,128)S(1)} %get-tuple-element.63.share, ...), custom_call_target="tpu_custom_call" | custom-call | flops 1 | bytes 1 | tf_op jit(solution)/shard_map/last_gate_up/pallas_call | solution.py:411
  78.2 1.0 down_both.1
  79.2 0.5 collective-permute-start.22
  79.7 1.7 %collective-permute-start.28 = (bf16[256,768]{1,0:T(8,128)(2,1)S(1)}, bf16[256,768]{1,0:T(8,128)(2,1)S(1)}, u32[]{:S(2)}, u32[]{:S(2)}) collective-permute-start(bf16[256,768]{1,0:T(8,128)(2,1)S(1)} %get-tuple-element.66.far), channel_id=1, source_target_pairs={{0,16},{16,0},{1,17},{17,1},{2,18},{18,2},{3,19},{19,3},{4,20},{20... | collective-permute-start | bytes 1179656 | tf_op jit(solution)/shard_map/ppermute | solution.py:423
  81.5 1.6 %collective-permute-start.23 = (bf16[128,1024]{1,0:T(8,128)(2,1)S(1)}, bf16[128,1024]{1,0:T(8,128)(2,1)S(1)}, u32[]{:S(2)}, u32[]{:S(2)}) collective-permute-start(bf16[128,1024]{1,0:T(8,128)(2,1)S(1)} %fold.2), channel_id=1, source_target_pairs={{0,2},{1,3},{2,0},{3,1},{4,6},{5,7},{6,4},{7,5},{8,10},{9,11},{10,... | collective-permute-start | bytes 786440 | tf_op jit(solution)/shard_map/ppermute | solution.py:440
  83.1 1.0 collective-permute-start.32
  84.1 7.6 %collective-permute-done.28.block = bf16[256,768]{1,0:T(8,128)(2,1)S(1)} collective-permute-done((bf16[256,768]{1,0:T(8,128)(2,1)S(1)}, bf16[256,768]{1,0:T(8,128)(2,1)S(1)}, u32[]{:S(2)}, u32[]{:S(2)}) %collective-permute-start.28) | collective-permute-done | bytes 393248 | tf_op jit(solution)/shard_map/ppermute | solution.py:423
  91.7 0.6 down.2
  92.4 0.5 collective-permute-start.30
  92.9 0.4 collective-permute-start.25
  93.4 0.3 collective-permute-done.29.refs_0_
  94.0 1.8 %collective-permute-start.31 = (bf16[128,1024]{1,0:T(8,128)(2,1)S(1)}, bf16[128,1024]{1,0:T(8,128)(2,1)S(1)}, u32[]{:S(2)}, u32[]{:S(2)}) collective-permute-start(bf16[128,1024]{1,0:T(8,128)(2,1)S(1)} %fold.3), channel_id=1, source_target_pairs={{0,2},{1,3},{2,0},{3,1},{4,6},{5,7},{6,4},{7,5},{8,10},{9,11},{10,... | collective-permute-start | bytes 786440 | tf_op jit(solution)/shard_map/ppermute | solution.py:440
  95.8 1.6 %collective-permute-start.27 = (bf16[64,1024]{1,0:T(8,128)(2,1)S(1)}, bf16[64,1024]{1,0:T(8,128)(2,1)S(1)}, u32[]{:S(2)}, u32[]{:S(2)}) collective-permute-start(bf16[64,1024]{1,0:T(8,128)(2,1)S(1)} %get-tuple-element.75), channel_id=1, source_target_pairs={{0,4},{1,13},{2,6},{3,15},{4,8},{5,1},{6,10},{7,3},{8,12},{9,5},{1... | collective-permute-start | bytes 393224 | tf_op jit(solution)/shard_map/ppermute | solution.py:437
  97.5 0.8 collective-permute-start.26
  98.3 1.0 collective-permute-done.32.block
  99.2 0.6 down.3
  99.8 2.1 %collective-permute-start.33 = (bf16[128,512]{1,0:T(8,128)(2,1)S(1)}, bf16[128,512]{1,0:T(8,128)(2,1)S(1)}, u32[]{:S(2)}, u32[]{:S(2)}) collective-permute-start(bf16[128,512]{1,0:T(8,128)(2,1)S(1)} %get-tuple-element.82), channel_id=1, source_target_pairs={{0,1},{1,0},{2,3},{3,2},{4,5},{5,4},{6,7},{7,6},{8,9},{9,8},{10,11... | collective-permute-start | bytes 393224 | tf_op jit(solution)/shard_map/ppermute | solution.py:440
  102.1 2.0 %collective-permute-done.27.a1 = bf16[64,1024]{1,0:T(8,128)(2,1)S(1)} collective-permute-done((bf16[64,1024]{1,0:T(8,128)(2,1)S(1)}, bf16[64,1024]{1,0:T(8,128)(2,1)S(1)}, u32[]{:S(2)}, u32[]{:S(2)}) %collective-permute-start.27) | collective-permute-done | bytes 131104 | tf_op jit(solution)/shard_map/ppermute | solution.py:437
  104.1 1.6 %collective-permute-start.35 = (bf16[64,1024]{1,0:T(8,128)(2,1)S(1)}, bf16[64,1024]{1,0:T(8,128)(2,1)S(1)}, u32[]{:S(2)}, u32[]{:S(2)}) collective-permute-start(bf16[64,1024]{1,0:T(8,128)(2,1)S(1)} %get-tuple-element.84), channel_id=1, source_target_pairs={{0,16},{1,25},{2,18},{3,27},{4,20},{5,29},{6,22},{7,31},{8,24},{9,... | collective-permute-start | bytes 393224 | tf_op jit(solution)/shard_map/ppermute | solution.py:437
  105.7 0.2 collective-permute-start.36
  106.0 3.2 %collective-permute-done.35.b0 = bf16[64,1024]{1,0:T(8,128)(2,1)S(1)} collective-permute-done((bf16[64,1024]{1,0:T(8,128)(2,1)S(1)}, bf16[64,1024]{1,0:T(8,128)(2,1)S(1)}, u32[]{:S(2)}, u32[]{:S(2)}) %collective-permute-start.35) | collective-permute-done | bytes 131104 | tf_op jit(solution)/shard_map/ppermute | solution.py:437
  109.2 5.0 %collective-permute-done.36.b1 = bf16[64,1024]{1,0:T(8,128)(2,1)S(1)} collective-permute-done((bf16[64,1024]{1,0:T(8,128)(2,1)S(1)}, bf16[64,1024]{1,0:T(8,128)(2,1)S(1)}, u32[]{:S(2)}, u32[]{:S(2)}) %collective-permute-start.36) | collective-permute-done | bytes 131104 | tf_op jit(solution)/shard_map/ppermute | solution.py:437
  114.3 0.5 collective-permute-start.37
  114.8 1.0 collective-permute-done.37.core
  115.8 0.8 closing.1
  (61 shorter events, 1.6 us)
Async XLA Ops:
  0.6 1.9 %copy-start = (bf16[1,1024,1536]{2,1,0:T(8,128)(2,1)S(1)}, bf16[1,1024,1536]{2,1,0:T(8,128)(2,1)}, u32[]{:S(2)}) copy-start(bf16[1,1024,1536]{2,1,0:T(8,128)(2,1)} %param.17) | copy-start | bytes 9437188
  2.5 4.7 %copy-start.4 = (bf16[1,32,2048]{2,1,0:T(8,128)(2,1)S(1)}, bf16[1,32,2048]{2,1,0:T(8,128)(2,1)}, u32[]{:S(2)}) copy-start(bf16[1,32,2048]{2,1,0:T(8,128)(2,1)} %param.11) | copy-start | bytes 393220
  2.5 7.9 %copy-start.3 = (bf16[1,64,2048]{2,1,0:T(8,128)(2,1)S(1)}, bf16[1,64,2048]{2,1,0:T(8,128)(2,1)}, u32[]{:S(2)}) copy-start(bf16[1,64,2048]{2,1,0:T(8,128)(2,1)} %param.10) | copy-start | bytes 786436
  2.7 38.3 %collective-permute-start.8 = (bf16[1024,768]{1,0:T(8,128)(2,1)S(1)}, bf16[1024,768]{1,0:T(8,128)(2,1)S(1)}, u32[]{:S(2)}, u32[]{:S(2)}) collective-permute-start(bf16[1024,768]{1,0:T(8,128)(2,1)S(1)} %weight_piece.3), channel_id=1, source_target_pairs={{0,16},{16,0},{1,17},{17,1},{2,18},{18,2},{3,19},{19,3},{4,20},{20... | collective-permute-start | bytes 4718600 | tf_op jit(solution)/shard_map/ppermute | solution.py:423
  5.7 13.7 %collective-permute-start.5 = (bf16[2048,128]{1,0:T(8,128)(2,1)}, bf16[2048,128]{1,0:T(8,128)(2,1)}, u32[]{:S(2)}, u32[]{:S(2)}) collective-permute-start(bf16[2048,128]{1,0:T(8,128)(2,1)} %w0.1), channel_id=1, source_target_pairs={{0,2},{1,3},{2,0},{3,1},{4,6},{5,7},{6,4},{7,5},{8,10},{9,11},{10,... | collective-permute-start | bytes 1572872 | tf_op jit(solution)/shard_map/ppermute | solution.py:440
  7.9 4.7 %copy-start.6 = (bf16[32,512]{1,0:T(8,128)(2,1)}, bf16[32,512]{1,0:T(8,128)(2,1)S(1)}, u32[]{:S(2)}) copy-start(bf16[32,512]{1,0:T(8,128)(2,1)S(1)} %get-tuple-element.48) | copy-start | bytes 98308
  7.9 11.6 %collective-permute-start.2 = (bf16[64,512]{1,0:T(8,128)(2,1)}, bf16[64,512]{1,0:T(8,128)(2,1)S(1)}, u32[]{:S(2)}, u32[]{:S(2)}) collective-permute-start(bf16[64,512]{1,0:T(8,128)(2,1)} %get-tuple-element.46), channel_id=1, source_target_pairs={{0,8},{1,9},{2,10},{3,11},{4,12},{5,13},{6,14},{7,15},{8,0},{9,1},... | collective-permute-start | bytes 196616 | tf_op jit(solution)/shard_map/ppermute | solution.py:443
  10.5 4.6 %copy-start.12 = (s32[1,32,8]{1,2,0:T(8,128)S(1)}, s32[1,32,8]{1,2,0:T(8,128)}, u32[]{:S(2)}) copy-start(s32[1,32,8]{1,2,0:T(8,128)} %param.14) | copy-start | bytes 3076
  10.5 14.9 %collective-permute-start.1 = (bf16[64,2048]{1,0:T(8,128)(2,1)S(1)}, bf16[64,2048]{1,0:T(8,128)(2,1)}, u32[]{:S(2)}, u32[]{:S(2)}) collective-permute-start(bf16[64,2048]{1,0:T(8,128)(2,1)S(1)} %bitcast.16), channel_id=1, source_target_pairs={{0,8},{1,9},{2,10},{3,11},{4,12},{5,13},{6,14},{7,15},{8,0},{9,1},... | collective-permute-start | bytes 786440 | tf_op jit(solution)/shard_map/ppermute | solution.py:443
  10.8 14.5 %collective-permute-start = (bf16[64,2048]{1,0:T(8,128)(2,1)S(1)}, bf16[64,2048]{1,0:T(8,128)(2,1)}, u32[]{:S(2)}, u32[]{:S(2)}) collective-permute-start(bf16[64,2048]{1,0:T(8,128)(2,1)S(1)} %bitcast.17), channel_id=1, source_target_pairs={{0,4},{1,5},{2,6},{3,7},{4,0},{5,1},{6,2},{7,3},{8,12},{9,13},{10,... | collective-permute-start | bytes 786440 | tf_op jit(solution)/shard_map/ppermute | solution.py:443
  12.6 1.0 copy-start.8
  13.6 0.8 copy-start.10
  19.4 15.4 %collective-permute-start.7 = (bf16[2048,128]{1,0:T(8,128)(2,1)}, bf16[2048,128]{1,0:T(8,128)(2,1)S(1)}, u32[]{:S(2)}, u32[]{:S(2)}) collective-permute-start(bf16[2048,128]{1,0:T(8,128)(2,1)} %collective-permute-done.5.w2), channel_id=1, source_target_pairs={{0,1},{1,0},{2,3},{3,2},{4,5},{5,4},{6,7},{7,6},{8,9},{9,8},{10,11... | collective-permute-start | bytes 1572872 | tf_op jit(solution)/shard_map/ppermute | solution.py:440
  19.5 15.4 %collective-permute-start.6 = (bf16[2048,128]{1,0:T(8,128)(2,1)}, bf16[2048,128]{1,0:T(8,128)(2,1)S(1)}, u32[]{:S(2)}, u32[]{:S(2)}) collective-permute-start(bf16[2048,128]{1,0:T(8,128)(2,1)} %w0.1), channel_id=1, source_target_pairs={{0,1},{1,0},{2,3},{3,2},{4,5},{5,4},{6,7},{7,6},{8,9},{9,8},{10,11... | collective-permute-start | bytes 1572872 | tf_op jit(solution)/shard_map/ppermute | solution.py:440
  25.4 9.5 %collective-permute-start.3 = (bf16[64,2048]{1,0:T(8,128)(2,1)}, bf16[64,2048]{1,0:T(8,128)(2,1)S(1)}, u32[]{:S(2)}, u32[]{:S(2)}) collective-permute-start(bf16[64,2048]{1,0:T(8,128)(2,1)} %collective-permute-done.1.a2), channel_id=1, source_target_pairs={{0,4},{1,5},{2,6},{3,7},{4,0},{5,1},{6,2},{7,3},{8,12},{9,13},{10,... | collective-permute-start | bytes 786440 | tf_op jit(solution)/shard_map/ppermute | solution.py:443
  26.3 12.0 %copy-start.9 = (bf16[640,768]{1,0:T(8,128)(2,1)S(1)}, bf16[640,768]{1,0:T(8,128)(2,1)}, u32[]{:S(2)}) copy-start(bf16[640,768]{1,0:T(8,128)(2,1)} %copy-done.8) | copy-start | bytes 2949124
  26.3 35.6 %copy-start.11 = (bf16[384,768]{1,0:T(8,128)(2,1)S(1)}, bf16[384,768]{1,0:T(8,128)(2,1)}, u32[]{:S(2)}) copy-start(bf16[384,768]{1,0:T(8,128)(2,1)} %copy-done.10) | copy-start | bytes 1769476
  26.4 36.7 %copy-start.5 = (f32[2048]{0:T(1024)S(1)}, f32[2048]{0:T(1024)}, u32[]{:S(2)}) copy-start(f32[2048]{0:T(1024)} %param.13) | copy-start | bytes 24580
  26.4 8.5 %collective-permute-start.4 = (bf16[64,512]{1,0:T(8,128)(2,1)S(1)}, bf16[64,512]{1,0:T(8,128)(2,1)S(1)}, u32[]{:S(2)}, u32[]{:S(2)}) collective-permute-start(bf16[64,512]{1,0:T(8,128)(2,1)S(1)} %pad_maximum_fusion), channel_id=1, source_target_pairs={{0,4},{1,5},{2,6},{3,7},{4,0},{5,1},{6,2},{7,3},{8,12},{9,13},{10,... | collective-permute-start | bytes 196616 | tf_op jit(solution)/shard_map/ppermute | solution.py:443
  34.9 35.2 %copy-start.1 = (bf16[1,1024,1536]{2,1,0:T(8,128)(2,1)S(1)}, bf16[1,1024,1536]{2,1,0:T(8,128)(2,1)}, u32[]{:S(2)}) copy-start(bf16[1,1024,1536]{2,1,0:T(8,128)(2,1)} %param.17) | copy-start | bytes 9437188
  37.8 6.5 %collective-permute-start.9 = (bf16[128,512]{1,0:T(8,128)(2,1)S(1)}, bf16[128,512]{1,0:T(8,128)(2,1)S(1)}, u32[]{:S(2)}, u32[]{:S(2)}) collective-permute-start(bf16[128,512]{1,0:T(8,128)(2,1)S(1)} %get-tuple-element.55), channel_id=1, source_target_pairs={{0,16},{16,0},{1,17},{17,1},{2,18},{18,2},{3,19},{19,3},{4,20},{20... | collective-permute-start | bytes 393224 | tf_op jit(solution)/shard_map/ppermute | solution.py:423
  38.3 38.3 %collective-permute-start.19 = (bf16[640,768]{1,0:T(8,128)(2,1)S(1)}, bf16[640,768]{1,0:T(8,128)(2,1)S(1)}, u32[]{:S(2)}, u32[]{:S(2)}) collective-permute-start(bf16[640,768]{1,0:T(8,128)(2,1)S(1)} %copy-done.9), channel_id=1, source_target_pairs={{0,16},{16,0},{1,17},{17,1},{2,18},{18,2},{3,19},{19,3},{4,20},{20... | collective-permute-start | bytes 2949128 | tf_op jit(solution)/shard_map/ppermute | solution.py:423
  44.3 7.8 %collective-permute-start.12 = (bf16[144,512]{1,0:T(8,128)(2,1)S(1)}, bf16[144,512]{1,0:T(8,128)(2,1)S(1)}, u32[]{:S(2)}, u32[]{:S(2)}) collective-permute-start(bf16[144,512]{1,0:T(8,128)(2,1)S(1)} %stream.1.b0), channel_id=1, source_target_pairs={{0,12},{1,13},{2,14},{3,15},{4,0},{5,1},{6,2},{7,3},{8,4},{9,5},{1... | collective-permute-start | bytes 442376 | tf_op jit(solution)/shard_map/ppermute | solution.py:426
  47.8 12.0 %collective-permute-start.11 = (bf16[144,512]{1,0:T(8,128)(2,1)S(1)}, bf16[144,512]{1,0:T(8,128)(2,1)S(1)}, u32[]{:S(2)}, u32[]{:S(2)}) collective-permute-start(bf16[144,512]{1,0:T(8,128)(2,1)S(1)} %stream.1.b0), channel_id=1, source_target_pairs={{0,8},{1,9},{2,10},{3,11},{4,12},{5,13},{6,14},{7,15},{8,0},{9,1},... | collective-permute-start | bytes 442376 | tf_op jit(solution)/shard_map/ppermute | solution.py:426
  47.8 13.2 %collective-permute-start.10 = (bf16[144,512]{1,0:T(8,128)(2,1)S(1)}, bf16[144,512]{1,0:T(8,128)(2,1)S(1)}, u32[]{:S(2)}, u32[]{:S(2)}) collective-permute-start(bf16[144,512]{1,0:T(8,128)(2,1)S(1)} %stream.1.b0), channel_id=1, source_target_pairs={{0,4},{1,5},{2,6},{3,7},{4,8},{5,9},{6,10},{7,11},{8,12},{9,13},{1... | collective-permute-start | bytes 442376 | tf_op jit(solution)/shard_map/ppermute | solution.py:426
  48.7 13.2 %collective-permute-start.13 = (bf16[144,512]{1,0:T(8,128)(2,1)S(1)}, bf16[144,512]{1,0:T(8,128)(2,1)S(1)}, u32[]{:S(2)}, u32[]{:S(2)}) collective-permute-start(bf16[144,512]{1,0:T(8,128)(2,1)S(1)} %stream.1.b0), channel_id=1, source_target_pairs={{0,2},{1,3},{2,0},{3,1},{4,6},{5,7},{6,4},{7,5},{8,10},{9,11},{10,... | collective-permute-start | bytes 442376 | tf_op jit(solution)/shard_map/ppermute | solution.py:440
  52.1 11.3 %collective-permute-start.16 = (bf16[144,512]{1,0:T(8,128)(2,1)S(1)}, bf16[144,512]{1,0:T(8,128)(2,1)S(1)}, u32[]{:S(2)}, u32[]{:S(2)}) collective-permute-start(bf16[144,512]{1,0:T(8,128)(2,1)S(1)} %collective-permute-done.12.b3), channel_id=1, source_target_pairs={{0,2},{1,3},{2,0},{3,1},{4,6},{5,7},{6,4},{7,5},{8,10},{9,11},{10,... | collective-permute-start | bytes 442376 | tf_op jit(solution)/shard_map/ppermute | solution.py:440
  59.9 5.9 %collective-permute-start.15 = (bf16[144,512]{1,0:T(8,128)(2,1)S(1)}, bf16[144,512]{1,0:T(8,128)(2,1)S(1)}, u32[]{:S(2)}, u32[]{:S(2)}) collective-permute-start(bf16[144,512]{1,0:T(8,128)(2,1)S(1)} %collective-permute-done.11.b2), channel_id=1, source_target_pairs={{0,2},{1,3},{2,0},{3,1},{4,6},{5,7},{6,4},{7,5},{8,10},{9,11},{10,... | collective-permute-start | bytes 442376 | tf_op jit(solution)/shard_map/ppermute | solution.py:440
  61.0 6.3 %collective-permute-start.14 = (bf16[144,512]{1,0:T(8,128)(2,1)S(1)}, bf16[144,512]{1,0:T(8,128)(2,1)S(1)}, u32[]{:S(2)}, u32[]{:S(2)}) collective-permute-start(bf16[144,512]{1,0:T(8,128)(2,1)S(1)} %collective-permute-done.10.b1), channel_id=1, source_target_pairs={{0,2},{1,3},{2,0},{3,1},{4,6},{5,7},{6,4},{7,5},{8,10},{9,11},{10,... | collective-permute-start | bytes 442376 | tf_op jit(solution)/shard_map/ppermute | solution.py:440
  61.9 14.7 %collective-permute-start.20 = (bf16[384,768]{1,0:T(8,128)(2,1)S(1)}, bf16[384,768]{1,0:T(8,128)(2,1)S(1)}, u32[]{:S(2)}, u32[]{:S(2)}) collective-permute-start(bf16[384,768]{1,0:T(8,128)(2,1)S(1)} %copy-done.11), channel_id=1, source_target_pairs={{0,16},{16,0},{1,17},{17,1},{2,18},{18,2},{3,19},{19,3},{4,20},{20... | collective-permute-start | bytes 1769480 | tf_op jit(solution)/shard_map/ppermute | solution.py:423
  63.4 4.7 %collective-permute-start.18 = (bf16[128,2176]{1,0:T(8,128)(2,1)S(1)}, bf16[128,2176]{1,0:T(8,128)(2,1)S(1)}, u32[]{:S(2)}, u32[]{:S(2)}) collective-permute-start(bf16[128,2176]{1,0:T(8,128)(2,1)S(1)} %get-tuple-element.59.group), channel_id=1, source_target_pairs={{0,1},{1,0},{2,3},{3,2},{4,5},{5,4},{6,7},{7,6},{8,9},{9,8},{10,11... | collective-permute-start | bytes 1671176 | tf_op jit(solution)/shard_map/ppermute | solution.py:440
  68.1 2.0 %collective-permute-start.17 = (bf16[128,2176]{1,0:T(8,128)(2,1)S(1)}, bf16[128,2176]{1,0:T(8,128)(2,1)S(1)}, u32[]{:S(2)}, u32[]{:S(2)}) collective-permute-start(bf16[128,2176]{1,0:T(8,128)(2,1)S(1)} %get-tuple-element.58.group_x), channel_id=1, source_target_pairs={{0,1},{1,0},{2,3},{3,2},{4,5},{5,4},{6,7},{7,6},{8,9},{9,8},{10,11... | collective-permute-start | bytes 1671176 | tf_op jit(solution)/shard_map/ppermute | solution.py:440
  76.7 1.5 %copy-start.2 = (bf16[1,768,1024]{2,1,0:T(8,128)(2,1)S(1)}, bf16[1,768,1024]{2,1,0:T(8,128)(2,1)}, u32[]{:S(2)}) copy-start(bf16[1,768,1024]{2,1,0:T(8,128)(2,1)} %param.18) | copy-start | bytes 4718596
  79.1 2.3 %collective-permute-start.21 = (bf16[128,512]{1,0:T(8,128)(2,1)S(1)}, bf16[128,512]{1,0:T(8,128)(2,1)S(1)}, u32[]{:S(2)}, u32[]{:S(2)}) collective-permute-start(bf16[128,512]{1,0:T(8,128)(2,1)S(1)} %get-tuple-element.69), channel_id=1, source_target_pairs={{0,1},{1,0},{2,3},{3,2},{4,5},{5,4},{6,7},{7,6},{8,9},{9,8},{10,11... | collective-permute-start | bytes 393224 | tf_op jit(solution)/shard_map/ppermute | solution.py:440
  79.2 2.2 %collective-permute-start.22 = (bf16[128,512]{1,0:T(8,128)(2,1)S(1)}, bf16[128,512]{1,0:T(8,128)(2,1)S(1)}, u32[]{:S(2)}, u32[]{:S(2)}) collective-permute-start(bf16[128,512]{1,0:T(8,128)(2,1)S(1)} %get-tuple-element.70), channel_id=1, source_target_pairs={{0,1},{1,0},{2,3},{3,2},{4,5},{5,4},{6,7},{7,6},{8,9},{9,8},{10,11... | collective-permute-start | bytes 393224 | tf_op jit(solution)/shard_map/ppermute | solution.py:440
  79.7 12.0 %collective-permute-start.28 = (bf16[256,768]{1,0:T(8,128)(2,1)S(1)}, bf16[256,768]{1,0:T(8,128)(2,1)S(1)}, u32[]{:S(2)}, u32[]{:S(2)}) collective-permute-start(bf16[256,768]{1,0:T(8,128)(2,1)S(1)} %get-tuple-element.66.far), channel_id=1, source_target_pairs={{0,16},{16,0},{1,17},{17,1},{2,18},{18,2},{3,19},{19,3},{4,20},{20... | collective-permute-start | bytes 1179656 | tf_op jit(solution)/shard_map/ppermute | solution.py:423
  81.5 10.1 %collective-permute-start.23 = (bf16[128,1024]{1,0:T(8,128)(2,1)S(1)}, bf16[128,1024]{1,0:T(8,128)(2,1)S(1)}, u32[]{:S(2)}, u32[]{:S(2)}) collective-permute-start(bf16[128,1024]{1,0:T(8,128)(2,1)S(1)} %fold.2), channel_id=1, source_target_pairs={{0,2},{1,3},{2,0},{3,1},{4,6},{5,7},{6,4},{7,5},{8,10},{9,11},{10,... | collective-permute-start | bytes 786440 | tf_op jit(solution)/shard_map/ppermute | solution.py:440
  83.1 16.1 %collective-permute-start.32 = (bf16[256,768]{1,0:T(8,128)(2,1)S(1)}, bf16[256,768]{1,0:T(8,128)(2,1)S(1)}, u32[]{:S(2)}, u32[]{:S(2)}) collective-permute-start(bf16[256,768]{1,0:T(8,128)(2,1)S(1)} %get-tuple-element.67.near), channel_id=1, source_target_pairs={{0,16},{16,0},{1,17},{17,1},{2,18},{18,2},{3,19},{19,3},{4,20},{20... | collective-permute-start | bytes 1179656 | tf_op jit(solution)/shard_map/ppermute | solution.py:423
  92.3 1.4 %collective-permute-start.29 = (bf16[128,512]{1,0:T(8,128)(2,1)S(1)}, bf16[128,512]{1,0:T(8,128)(2,1)S(1)}, u32[]{:S(2)}, u32[]{:S(2)}) collective-permute-start(bf16[128,512]{1,0:T(8,128)(2,1)S(1)} %get-tuple-element.78), channel_id=1, source_target_pairs={{0,1},{1,0},{2,3},{3,2},{4,5},{5,4},{6,7},{7,6},{8,9},{9,8},{10,11... | collective-permute-start | bytes 393224 | tf_op jit(solution)/shard_map/ppermute | solution.py:440
  92.4 1.5 %collective-permute-start.30 = (bf16[128,512]{1,0:T(8,128)(2,1)S(1)}, bf16[128,512]{1,0:T(8,128)(2,1)S(1)}, u32[]{:S(2)}, u32[]{:S(2)}) collective-permute-start(bf16[128,512]{1,0:T(8,128)(2,1)S(1)} %get-tuple-element.79), channel_id=1, source_target_pairs={{0,1},{1,0},{2,3},{3,2},{4,5},{5,4},{6,7},{7,6},{8,9},{9,8},{10,11... | collective-permute-start | bytes 393224 | tf_op jit(solution)/shard_map/ppermute | solution.py:440
  92.9 2.9 %collective-permute-start.24 = (bf16[128,512]{1,0:T(8,128)(2,1)S(1)}, bf16[128,512]{1,0:T(8,128)(2,1)S(1)}, u32[]{:S(2)}, u32[]{:S(2)}) collective-permute-start(bf16[128,512]{1,0:T(8,128)(2,1)S(1)} %get-tuple-element.72), channel_id=1, source_target_pairs={{0,1},{1,0},{2,3},{3,2},{4,5},{5,4},{6,7},{7,6},{8,9},{9,8},{10,11... | collective-permute-start | bytes 393224 | tf_op jit(solution)/shard_map/ppermute | solution.py:440
  92.9 2.8 %collective-permute-start.25 = (bf16[128,512]{1,0:T(8,128)(2,1)S(1)}, bf16[128,512]{1,0:T(8,128)(2,1)S(1)}, u32[]{:S(2)}, u32[]{:S(2)}) collective-permute-start(bf16[128,512]{1,0:T(8,128)(2,1)S(1)} %get-tuple-element.73), channel_id=1, source_target_pairs={{0,1},{1,0},{2,3},{3,2},{4,5},{5,4},{6,7},{7,6},{8,9},{9,8},{10,11... | collective-permute-start | bytes 393224 | tf_op jit(solution)/shard_map/ppermute | solution.py:440
  94.0 10.1 %collective-permute-start.31 = (bf16[128,1024]{1,0:T(8,128)(2,1)S(1)}, bf16[128,1024]{1,0:T(8,128)(2,1)S(1)}, u32[]{:S(2)}, u32[]{:S(2)}) collective-permute-start(bf16[128,1024]{1,0:T(8,128)(2,1)S(1)} %fold.3), channel_id=1, source_target_pairs={{0,2},{1,3},{2,0},{3,1},{4,6},{5,7},{6,4},{7,5},{8,10},{9,11},{10,... | collective-permute-start | bytes 786440 | tf_op jit(solution)/shard_map/ppermute | solution.py:440
  95.8 8.2 %collective-permute-start.27 = (bf16[64,1024]{1,0:T(8,128)(2,1)S(1)}, bf16[64,1024]{1,0:T(8,128)(2,1)S(1)}, u32[]{:S(2)}, u32[]{:S(2)}) collective-permute-start(bf16[64,1024]{1,0:T(8,128)(2,1)S(1)} %get-tuple-element.75), channel_id=1, source_target_pairs={{0,4},{1,13},{2,6},{3,15},{4,8},{5,1},{6,10},{7,3},{8,12},{9,5},{1... | collective-permute-start | bytes 393224 | tf_op jit(solution)/shard_map/ppermute | solution.py:437
  97.5 18.3 %copy-start.7 = (f32[2048]{0:T(1024)S(1)}, f32[2048]{0:T(1024)}, u32[]{:S(2)}) copy-start(f32[2048]{0:T(1024)} %param.19) | copy-start | bytes 24580
  97.5 6.5 %collective-permute-start.26 = (bf16[64,1024]{1,0:T(8,128)(2,1)S(1)}, bf16[64,1024]{1,0:T(8,128)(2,1)S(1)}, u32[]{:S(2)}, u32[]{:S(2)}) collective-permute-start(bf16[64,1024]{1,0:T(8,128)(2,1)S(1)} %get-tuple-element.74.own), channel_id=1, source_target_pairs={{1,9},{3,11},{5,13},{7,15},{9,1},{11,3},{13,5},{15,7},{17,25},{19,... | collective-permute-start | bytes 393224 | tf_op jit(solution)/shard_map/ppermute | solution.py:437
  99.8 4.2 %collective-permute-start.33 = (bf16[128,512]{1,0:T(8,128)(2,1)S(1)}, bf16[128,512]{1,0:T(8,128)(2,1)S(1)}, u32[]{:S(2)}, u32[]{:S(2)}) collective-permute-start(bf16[128,512]{1,0:T(8,128)(2,1)S(1)} %get-tuple-element.82), channel_id=1, source_target_pairs={{0,1},{1,0},{2,3},{3,2},{4,5},{5,4},{6,7},{7,6},{8,9},{9,8},{10,11... | collective-permute-start | bytes 393224 | tf_op jit(solution)/shard_map/ppermute | solution.py:440
  102.0 2.1 %collective-permute-start.34 = (bf16[128,512]{1,0:T(8,128)(2,1)S(1)}, bf16[128,512]{1,0:T(8,128)(2,1)S(1)}, u32[]{:S(2)}, u32[]{:S(2)}) collective-permute-start(bf16[128,512]{1,0:T(8,128)(2,1)S(1)} %get-tuple-element.83), channel_id=1, source_target_pairs={{0,1},{1,0},{2,3},{3,2},{4,5},{5,4},{6,7},{7,6},{8,9},{9,8},{10,11... | collective-permute-start | bytes 393224 | tf_op jit(solution)/shard_map/ppermute | solution.py:440
  104.1 5.0 %collective-permute-start.35 = (bf16[64,1024]{1,0:T(8,128)(2,1)S(1)}, bf16[64,1024]{1,0:T(8,128)(2,1)S(1)}, u32[]{:S(2)}, u32[]{:S(2)}) collective-permute-start(bf16[64,1024]{1,0:T(8,128)(2,1)S(1)} %get-tuple-element.84), channel_id=1, source_target_pairs={{0,16},{1,25},{2,18},{3,27},{4,20},{5,29},{6,22},{7,31},{8,24},{9,... | collective-permute-start | bytes 393224 | tf_op jit(solution)/shard_map/ppermute | solution.py:437
  105.7 8.5 %collective-permute-start.36 = (bf16[64,1024]{1,0:T(8,128)(2,1)S(1)}, bf16[64,1024]{1,0:T(8,128)(2,1)S(1)}, u32[]{:S(2)}, u32[]{:S(2)}) collective-permute-start(bf16[64,1024]{1,0:T(8,128)(2,1)S(1)} %get-tuple-element.85), channel_id=1, source_target_pairs={{0,20},{1,29},{2,22},{3,31},{4,24},{5,17},{6,26},{7,19},{8,28},{9,... | collective-permute-start | bytes 393224 | tf_op jit(solution)/shard_map/ppermute | solution.py:437
  114.3 1.5 %collective-permute-start.37 = (bf16[64,1024]{1,0:T(8,128)(2,1)S(1)}, bf16[64,1024]{1,0:T(8,128)(2,1)S(1)}, u32[]{:S(2)}, u32[]{:S(2)}) collective-permute-start(bf16[64,1024]{1,0:T(8,128)(2,1)S(1)} %get-tuple-element.87), channel_id=1, source_target_pairs={{0,1},{1,0},{2,3},{3,2},{4,5},{5,4},{6,7},{7,6},{8,9},{9,8},{10,11... | collective-permute-start | bytes 393224 | tf_op jit(solution)/shard_map/ppermute | solution.py:440

commit v13 on v12

--- a/solution.py
+++ b/solution.py
@@ -590,12 +590,12 @@
         down_both_kernel, "down_both", 16, outs, inner_far, inner_near, w_down[0], scratch=scratch
     )
     far = swap_inner(fold(keep_far, swap_cores(send[:2])), 2)
-    ready = far
+    first_far = far
     own, second = pieces(far, keep_near, send[2:])
     mine = [send_outer(own, 0, False), send_outer(second, 1, False)]
 
-    keep_far, send = down(after(far_other, ready), 2)
-    far = swap_inner(fold(keep_far, swap_cores(send)), 2)
+    keep_far, send = down(far_other, 2)
+    far = swap_inner(fold(after(keep_far, own), swap_cores(send)), 2)
     keep_near, send = down(near_other, 2)
     cut = pieces(far, after(keep_near, *mine), send)
     others = [send_outer(cut[i], i, True) for i in range(2)]

time: 117 us -> 116 us (level)
    ppermute x6, waiting for transfers between devices: 16.1 us -> 11.9 us  [swap_dp(): return lax.ppermute(x, 'dp', [(0, 1), (1, 0)])]
    ppermute x20, waiting for transfers between devices: 10.4 us -> 12.2 us  [swap_inner(): return lax.ppermute(x, 'expert', [(i, i ^ j) for i in range(expert_count)])]
    ppermute x4, waiting for transfers between devices: 10.2 us -> 11.6 us  [send_outer(): return lax.ppermute(x, ('dp', 'expert'), pairs)]
    ppermute x20, starting transfers between devices: 15.4 us -> 16.6 us  [swap_inner(): return lax.ppermute(x, 'expert', [(i, i ^ j) for i in range(expert_count)])]
  transfers between devices with their start and end apart: 38 -> 38, of which waited for: 19 -> 21; matrix products, arithmetic and copies ran while one was open for 1% -> 1% of each run, Pallas kernels for 9% -> 10%
where the time goes in v13:
time: 116 us
  waiting for transfers between devices  55.4 us (48%)
  starting transfers between devices  40.1 us (35%)
  Pallas kernels  13.8 us (12%)
  local copies, waits for them, and re-layouts  4.58 us (4%)
  between operations  1.55 us (1%)
    ppermute x20, starting transfers between devices, swap_inner(): return lax.ppermute(x, 'expert', [(i, i ^ j) for i in range(expert_count)])  16.6 us
    pallas_call x17, Pallas kernels, call(): pl.pallas_call(kernel, out_shape=outs, in_specs=[first] + [vmem] * (len(a...  13.4 us
    ppermute x20, waiting for transfers between devices, swap_inner(): return lax.ppermute(x, 'expert', [(i, i ^ j) for i in range(expert_count)])  12.2 us
    ppermute x5, waiting for transfers between devices, swap_outer(): lax.ppermute(x, 'expert', [(i, i ^ 4 * s) for i in range(expert_count)])  12.1 us
    ppermute x6, waiting for transfers between devices, swap_dp(): return lax.ppermute(x, 'dp', [(0, 1), (1, 0)])  11.9 us
    ppermute x4, waiting for transfers between devices, send_outer(): return lax.ppermute(x, ('dp', 'expert'), pairs)  11.6 us
    ppermute x6, starting transfers between devices, swap_dp(): return lax.ppermute(x, 'dp', [(0, 1), (1, 0)])  8.59 us
    ppermute x3, waiting for transfers between devices, shift_outer(): lax.ppermute(x, 'expert', [(i, (i + 4 * s) % expert_count) for i in range...  7.64 us
  transfers between devices with their start and end apart: 38, of which 21 were waited for; matrix products, arithmetic and copies ran while one was open for 1% of the time, Pallas kernels for 10%

profile of v13, /device:TPU:0, one launch (start us, length us, event | category | flops | bytes accessed | tf_op | source)
XLA Modules:
  0.0 116.1 jit_solution(13563975296780839600)
XLA Ops:
  0.6 1.9 %copy-done = bf16[1,1024,1536]{2,1,0:T(8,128)(2,1)S(1)} copy-done((bf16[1,1024,1536]{2,1,0:T(8,128)(2,1)S(1)}, bf16[1,1024,1536]{2,1,0:T(8,128)(2,1)}, u32[]{:S(2)}) %copy-start) | copy-done | bytes 3145752
  2.7 3.0 %collective-permute-start.8 = (bf16[1024,768]{1,0:T(8,128)(2,1)S(1)}, bf16[1024,768]{1,0:T(8,128)(2,1)S(1)}, u32[]{:S(2)}, u32[]{:S(2)}) collective-permute-start(bf16[1024,768]{1,0:T(8,128)(2,1)S(1)} %weight_piece.3), channel_id=1, source_target_pairs={{0,16},{16,0},{1,17},{17,1},{2,18},{18,2},{3,19},{19,3},{4,20},{20... | collective-permute-start | bytes 4718600 | tf_op jit(solution)/shard_map/ppermute | solution.py:423
  5.7 1.5 %collective-permute-start.5 = (bf16[2048,128]{1,0:T(8,128)(2,1)}, bf16[2048,128]{1,0:T(8,128)(2,1)}, u32[]{:S(2)}, u32[]{:S(2)}) collective-permute-start(bf16[2048,128]{1,0:T(8,128)(2,1)} %w0.1), channel_id=1, source_target_pairs={{0,2},{1,3},{2,0},{3,1},{4,6},{5,7},{6,4},{7,5},{8,10},{9,11},{10,... | collective-permute-start | bytes 1572872 | tf_op jit(solution)/shard_map/ppermute | solution.py:440
  7.2 0.6 cut_resid.1
  7.9 2.6 %collective-permute-start.2 = (bf16[64,512]{1,0:T(8,128)(2,1)}, bf16[64,512]{1,0:T(8,128)(2,1)S(1)}, u32[]{:S(2)}, u32[]{:S(2)}) collective-permute-start(bf16[64,512]{1,0:T(8,128)(2,1)} %get-tuple-element.46), channel_id=1, source_target_pairs={{0,8},{1,9},{2,10},{3,11},{4,12},{5,13},{6,14},{7,15},{8,0},{9,1},... | collective-permute-start | bytes 196616 | tf_op jit(solution)/shard_map/ppermute | solution.py:443
  10.5 0.3 collective-permute-start.1
  10.8 1.6 %collective-permute-start = (bf16[64,2048]{1,0:T(8,128)(2,1)S(1)}, bf16[64,2048]{1,0:T(8,128)(2,1)}, u32[]{:S(2)}, u32[]{:S(2)}) collective-permute-start(bf16[64,2048]{1,0:T(8,128)(2,1)S(1)} %bitcast.17), channel_id=1, source_target_pairs={{0,4},{1,5},{2,6},{3,7},{4,0},{5,1},{6,2},{7,3},{8,12},{9,13},{10,... | collective-permute-start | bytes 786440 | tf_op jit(solution)/shard_map/ppermute | solution.py:443
  12.4 0.2 weight_piece.2
  12.6 1.0 copy-done.8
  13.6 0.8 copy-done.10
  15.2 0.8 copy.13
  15.9 0.4 share.1
  16.4 3.1 %collective-permute-done.5.w2 = bf16[2048,128]{1,0:T(8,128)(2,1)} collective-permute-done((bf16[2048,128]{1,0:T(8,128)(2,1)}, bf16[2048,128]{1,0:T(8,128)(2,1)}, u32[]{:S(2)}, u32[]{:S(2)}) %collective-permute-start.5) | collective-permute-done | bytes 524320 | tf_op jit(solution)/shard_map/ppermute | solution.py:440
  19.5 0.5 collective-permute-start.6
  20.0 5.4 %collective-permute-done.1.a2 = bf16[64,2048]{1,0:T(8,128)(2,1)} collective-permute-done((bf16[64,2048]{1,0:T(8,128)(2,1)S(1)}, bf16[64,2048]{1,0:T(8,128)(2,1)}, u32[]{:S(2)}, u32[]{:S(2)}) %collective-permute-start.1) | collective-permute-done | bytes 262176 | tf_op jit(solution)/shard_map/ppermute | solution.py:443
  25.4 0.2 collective-permute-start.3
  25.6 0.8 pad_maximum_fusion
  26.4 1.9 %collective-permute-start.4 = (bf16[64,512]{1,0:T(8,128)(2,1)S(1)}, bf16[64,512]{1,0:T(8,128)(2,1)S(1)}, u32[]{:S(2)}, u32[]{:S(2)}) collective-permute-start(bf16[64,512]{1,0:T(8,128)(2,1)S(1)} %pad_maximum_fusion), channel_id=1, source_target_pairs={{0,4},{1,5},{2,6},{3,7},{4,0},{5,1},{6,2},{7,3},{8,12},{9,13},{10,... | collective-permute-start | bytes 196616 | tf_op jit(solution)/shard_map/ppermute | solution.py:443
  28.2 6.7 %collective-permute-done.4.r13 = bf16[64,512]{1,0:T(8,128)(2,1)S(1)} collective-permute-done((bf16[64,512]{1,0:T(8,128)(2,1)S(1)}, bf16[64,512]{1,0:T(8,128)(2,1)S(1)}, u32[]{:S(2)}, u32[]{:S(2)}) %collective-permute-start.4) | collective-permute-done | bytes 65568 | tf_op jit(solution)/shard_map/ppermute | solution.py:443
  34.9 2.8 %projection.1 = (bf16[128,512]{1,0:T(8,128)(2,1)S(1)}, bf16[128,512]{1,0:T(8,128)(2,1)S(1)}) custom-call(bf16[64,2048]{1,0:T(8,128)(2,1)S(1)} %bitcast.18, bf16[64,2048]{1,0:T(8,128)(2,1)} %collective-permute-done.a1, bf16[64,2048]{1,0:T(8,128)(2,1)} %collective-permute-done.1.a2, bf16[64,2048]{1,0:T(8,128)(2,1)S(1)} %collective-permute-done.3.a3, ...), custom_call_target="tpu_custom_call" | custom-call | flops 1 | bytes 1 | tf_op jit(solution)/shard_map/projection/pallas_call | solution.py:411
  37.8 0.6 collective-permute-start.9
  38.3 1.5 %collective-permute-start.19 = (bf16[640,768]{1,0:T(8,128)(2,1)S(1)}, bf16[640,768]{1,0:T(8,128)(2,1)S(1)}, u32[]{:S(2)}, u32[]{:S(2)}) collective-permute-start(bf16[640,768]{1,0:T(8,128)(2,1)S(1)} %copy-done.9), channel_id=1, source_target_pairs={{0,16},{16,0},{1,17},{17,1},{2,18},{18,2},{3,19},{19,3},{4,20},{20... | collective-permute-start | bytes 2949128 | tf_op jit(solution)/shard_map/ppermute | solution.py:423
  39.9 1.1 collective-permute-done.8.early
  41.0 3.3 %collective-permute-done.9.arrived = bf16[128,512]{1,0:T(8,128)(2,1)S(1)} collective-permute-done((bf16[128,512]{1,0:T(8,128)(2,1)S(1)}, bf16[128,512]{1,0:T(8,128)(2,1)S(1)}, u32[]{:S(2)}, u32[]{:S(2)}) %collective-permute-start.9) | collective-permute-done | bytes 131104 | tf_op jit(solution)/shard_map/ppermute | solution.py:423
  44.3 3.5 %collective-permute-start.12 = (bf16[144,512]{1,0:T(8,128)(2,1)S(1)}, bf16[144,512]{1,0:T(8,128)(2,1)S(1)}, u32[]{:S(2)}, u32[]{:S(2)}) collective-permute-start(bf16[144,512]{1,0:T(8,128)(2,1)S(1)} %stream.1.b0), channel_id=1, source_target_pairs={{0,12},{1,13},{2,14},{3,15},{4,0},{5,1},{6,2},{7,3},{8,4},{9,5},{1... | collective-permute-start | bytes 442376 | tf_op jit(solution)/shard_map/ppermute | solution.py:426
  47.8 0.8 collective-permute-start.10
  48.7 1.9 %collective-permute-start.13 = (bf16[144,512]{1,0:T(8,128)(2,1)S(1)}, bf16[144,512]{1,0:T(8,128)(2,1)S(1)}, u32[]{:S(2)}, u32[]{:S(2)}) collective-permute-start(bf16[144,512]{1,0:T(8,128)(2,1)S(1)} %stream.1.b0), channel_id=1, source_target_pairs={{0,2},{1,3},{2,0},{3,1},{4,6},{5,7},{6,4},{7,5},{8,10},{9,11},{10,... | collective-permute-start | bytes 442376 | tf_op jit(solution)/shard_map/ppermute | solution.py:440
  50.5 1.6 %collective-permute-done.12.b3 = bf16[144,512]{1,0:T(8,128)(2,1)S(1)} collective-permute-done((bf16[144,512]{1,0:T(8,128)(2,1)S(1)}, bf16[144,512]{1,0:T(8,128)(2,1)S(1)}, u32[]{:S(2)}, u32[]{:S(2)}) %collective-permute-start.12) | collective-permute-done | bytes 147488 | tf_op jit(solution)/shard_map/ppermute | solution.py:426
  52.1 1.7 %collective-permute-start.16 = (bf16[144,512]{1,0:T(8,128)(2,1)S(1)}, bf16[144,512]{1,0:T(8,128)(2,1)S(1)}, u32[]{:S(2)}, u32[]{:S(2)}) collective-permute-start(bf16[144,512]{1,0:T(8,128)(2,1)S(1)} %collective-permute-done.12.b3), channel_id=1, source_target_pairs={{0,2},{1,3},{2,0},{3,1},{4,6},{5,7},{6,4},{7,5},{8,10},{9,11},{10,... | collective-permute-start | bytes 442376 | tf_op jit(solution)/shard_map/ppermute | solution.py:440
  53.8 6.0 %collective-permute-done.11.b2 = bf16[144,512]{1,0:T(8,128)(2,1)S(1)} collective-permute-done((bf16[144,512]{1,0:T(8,128)(2,1)S(1)}, bf16[144,512]{1,0:T(8,128)(2,1)S(1)}, u32[]{:S(2)}, u32[]{:S(2)}) %collective-permute-start.11) | collective-permute-done | bytes 147488 | tf_op jit(solution)/shard_map/ppermute | solution.py:426
  59.9 1.1 collective-permute-start.15
  61.0 0.9 collective-permute-start.14
  61.9 1.2 collective-permute-start.20
  63.1 0.3 norm.2
  63.5 2.3 %collective-permute-done.15.b2 = bf16[144,512]{1,0:T(8,128)(2,1)S(1)} collective-permute-done((bf16[144,512]{1,0:T(8,128)(2,1)S(1)}, bf16[144,512]{1,0:T(8,128)(2,1)S(1)}, u32[]{:S(2)}, u32[]{:S(2)}) %collective-permute-start.15) | collective-permute-done | bytes 147488 | tf_op jit(solution)/shard_map/ppermute | solution.py:440
  65.8 1.6 %collective-permute-done.14.b1 = bf16[144,512]{1,0:T(8,128)(2,1)S(1)} collective-permute-done((bf16[144,512]{1,0:T(8,128)(2,1)S(1)}, bf16[144,512]{1,0:T(8,128)(2,1)S(1)}, u32[]{:S(2)}, u32[]{:S(2)}) %collective-permute-start.14) | collective-permute-done | bytes 147488 | tf_op jit(solution)/shard_map/ppermute | solution.py:440
  67.3 0.8 norm.3
  68.1 2.0 %collective-permute-done.17.group_cx = bf16[128,2176]{1,0:T(8,128)(2,1)S(1)} collective-permute-done((bf16[128,2176]{1,0:T(8,128)(2,1)S(1)}, bf16[128,2176]{1,0:T(8,128)(2,1)S(1)}, u32[]{:S(2)}, u32[]{:S(2)}) %collective-permute-start.17) | collective-permute-done | bytes 557088 | tf_op jit(solution)/shard_map/ppermute | solution.py:440
  70.1 3.4 %first_gate_up.1 = (bf16[512,384]{1,0:T(8,128)(2,1)S(1)}, f32[512,768]{1,0:T(8,128)S(1)}, bf16[512,1024]{1,0:T(8,128)(2,1)S(1)}, f32[512,128]{1,0:T(8,128)S(1)}) custom-call(bf16[128,2176]{1,0:T(8,128)(2,1)S(1)} %get-tuple-element.58.group_x, bf16[128,2176]{1,0:T(8,128)(2,1)S(1)} %collective-permute-done.17.group_cx, ...), custom_call_target="tpu_custom_call" | custom-call | flops 1 | bytes 1 | tf_op jit(solution)/shard_map/first_gate_up/pallas_call | solution.py:411
  73.5 3.1 %collective-permute-done.20.refs_1_ = bf16[384,768]{1,0:T(8,128)(2,1)S(1)} collective-permute-done((bf16[384,768]{1,0:T(8,128)(2,1)S(1)}, bf16[384,768]{1,0:T(8,128)(2,1)S(1)}, u32[]{:S(2)}, u32[]{:S(2)}) %collective-permute-start.20) | collective-permute-done | bytes 589856 | tf_op jit(solution)/shard_map/ppermute | solution.py:423
  76.7 1.5 %last_gate_up.1 = (bf16[256,768]{1,0:T(8,128)(2,1)S(1)}, bf16[256,768]{1,0:T(8,128)(2,1)S(1)}) custom-call(bf16[512,384]{1,0:T(8,128)(2,1)S(1)} %get-tuple-element.60.first, f32[512,768]{1,0:T(8,128)S(1)} %get-tuple-element.61.part, bf16[512,1024]{1,0:T(8,128)(2,1)S(1)} %get-tuple-element.62.other, f32[512,128]{1,0:T(8,128)S(1)} %get-tuple-element.63.share, ...), custom_call_target="tpu_custom_call" | custom-call | flops 1 | bytes 1 | tf_op jit(solution)/shard_map/last_gate_up/pallas_call | solution.py:411
  78.1 1.8 %collective-permute-start.28 = (bf16[256,768]{1,0:T(8,128)(2,1)S(1)}, bf16[256,768]{1,0:T(8,128)(2,1)S(1)}, u32[]{:S(2)}, u32[]{:S(2)}) collective-permute-start(bf16[256,768]{1,0:T(8,128)(2,1)S(1)} %get-tuple-element.66.far), channel_id=1, source_target_pairs={{0,16},{16,0},{1,17},{17,1},{2,18},{18,2},{3,19},{19,3},{4,20},{20... | collective-permute-start | bytes 1179656 | tf_op jit(solution)/shard_map/ppermute | solution.py:423
  80.0 1.0 down_both.1
  81.0 0.5 collective-permute-start.22
  81.5 0.8 collective-permute-done.21.refs_0_
  82.6 1.6 %collective-permute-start.23 = (bf16[128,1024]{1,0:T(8,128)(2,1)S(1)}, bf16[128,1024]{1,0:T(8,128)(2,1)S(1)}, u32[]{:S(2)}, u32[]{:S(2)}) collective-permute-start(bf16[128,1024]{1,0:T(8,128)(2,1)S(1)} %fold.2), channel_id=1, source_target_pairs={{0,2},{1,3},{2,0},{3,1},{4,6},{5,7},{6,4},{7,5},{8,10},{9,11},{10,... | collective-permute-start | bytes 786440 | tf_op jit(solution)/shard_map/ppermute | solution.py:440
  84.2 0.5 collective-permute-start.32
  84.7 0.5 collective-permute-start.25
  85.2 4.3 %collective-permute-done.28.block = bf16[256,768]{1,0:T(8,128)(2,1)S(1)} collective-permute-done((bf16[256,768]{1,0:T(8,128)(2,1)S(1)}, bf16[256,768]{1,0:T(8,128)(2,1)S(1)}, u32[]{:S(2)}, u32[]{:S(2)}) %collective-permute-start.28) | collective-permute-done | bytes 393248 | tf_op jit(solution)/shard_map/ppermute | solution.py:423
  89.5 0.6 down.2
  90.2 0.5 collective-permute-start.30
  90.7 0.5 collective-permute-done.23.far
  91.3 0.2 collective-permute-done.29.refs_0_
  91.8 2.5 %collective-permute-start.31 = (bf16[128,1024]{1,0:T(8,128)(2,1)S(1)}, bf16[128,1024]{1,0:T(8,128)(2,1)S(1)}, u32[]{:S(2)}, u32[]{:S(2)}) collective-permute-start(bf16[128,1024]{1,0:T(8,128)(2,1)S(1)} %fold.3), channel_id=1, source_target_pairs={{0,2},{1,3},{2,0},{3,1},{4,6},{5,7},{6,4},{7,5},{8,10},{9,11},{10,... | collective-permute-start | bytes 786440 | tf_op jit(solution)/shard_map/ppermute | solution.py:440
  94.3 0.7 collective-permute-start.26
  95.0 1.6 %collective-permute-start.27 = (bf16[64,1024]{1,0:T(8,128)(2,1)S(1)}, bf16[64,1024]{1,0:T(8,128)(2,1)S(1)}, u32[]{:S(2)}, u32[]{:S(2)}) collective-permute-start(bf16[64,1024]{1,0:T(8,128)(2,1)S(1)} %get-tuple-element.75), channel_id=1, source_target_pairs={{0,4},{1,13},{2,6},{3,15},{4,8},{5,1},{6,10},{7,3},{8,12},{9,5},{1... | collective-permute-start | bytes 393224 | tf_op jit(solution)/shard_map/ppermute | solution.py:437
  96.6 0.6 down.3
  97.2 3.1 %collective-permute-start.33 = (bf16[128,512]{1,0:T(8,128)(2,1)S(1)}, bf16[128,512]{1,0:T(8,128)(2,1)S(1)}, u32[]{:S(2)}, u32[]{:S(2)}) collective-permute-start(bf16[128,512]{1,0:T(8,128)(2,1)S(1)} %get-tuple-element.82), channel_id=1, source_target_pairs={{0,1},{1,0},{2,3},{3,2},{4,5},{5,4},{6,7},{7,6},{8,9},{9,8},{10,11... | collective-permute-start | bytes 393224 | tf_op jit(solution)/shard_map/ppermute | solution.py:440
  100.4 2.5 %collective-permute-done.27.a1 = bf16[64,1024]{1,0:T(8,128)(2,1)S(1)} collective-permute-done((bf16[64,1024]{1,0:T(8,128)(2,1)S(1)}, bf16[64,1024]{1,0:T(8,128)(2,1)S(1)}, u32[]{:S(2)}, u32[]{:S(2)}) %collective-permute-start.27) | collective-permute-done | bytes 131104 | tf_op jit(solution)/shard_map/ppermute | solution.py:437
  103.1 1.6 %collective-permute-start.35 = (bf16[64,1024]{1,0:T(8,128)(2,1)S(1)}, bf16[64,1024]{1,0:T(8,128)(2,1)S(1)}, u32[]{:S(2)}, u32[]{:S(2)}) collective-permute-start(bf16[64,1024]{1,0:T(8,128)(2,1)S(1)} %get-tuple-element.84), channel_id=1, source_target_pairs={{0,16},{1,25},{2,18},{3,27},{4,20},{5,29},{6,22},{7,31},{8,24},{9,... | collective-permute-start | bytes 393224 | tf_op jit(solution)/shard_map/ppermute | solution.py:437
  104.7 3.4 %collective-permute-done.35.b0 = bf16[64,1024]{1,0:T(8,128)(2,1)S(1)} collective-permute-done((bf16[64,1024]{1,0:T(8,128)(2,1)S(1)}, bf16[64,1024]{1,0:T(8,128)(2,1)S(1)}, u32[]{:S(2)}, u32[]{:S(2)}) %collective-permute-start.35) | collective-permute-done | bytes 131104 | tf_op jit(solution)/shard_map/ppermute | solution.py:437
  108.1 5.7 %collective-permute-done.36.b1 = bf16[64,1024]{1,0:T(8,128)(2,1)S(1)} collective-permute-done((bf16[64,1024]{1,0:T(8,128)(2,1)S(1)}, bf16[64,1024]{1,0:T(8,128)(2,1)S(1)}, u32[]{:S(2)}, u32[]{:S(2)}) %collective-permute-start.36) | collective-permute-done | bytes 131104 | tf_op jit(solution)/shard_map/ppermute | solution.py:437
  113.9 1.3 %collective-permute-done.37.core = bf16[64,1024]{1,0:T(8,128)(2,1)S(1)} collective-permute-done((bf16[64,1024]{1,0:T(8,128)(2,1)S(1)}, bf16[64,1024]{1,0:T(8,128)(2,1)S(1)}, u32[]{:S(2)}, u32[]{:S(2)}) %collective-permute-start.37) | collective-permute-done | bytes 131104 | tf_op jit(solution)/shard_map/ppermute | solution.py:440
  115.3 0.8 closing.1
  (61 shorter events, 1.6 us)
Async XLA Ops:
  0.6 1.9 %copy-start = (bf16[1,1024,1536]{2,1,0:T(8,128)(2,1)S(1)}, bf16[1,1024,1536]{2,1,0:T(8,128)(2,1)}, u32[]{:S(2)}) copy-start(bf16[1,1024,1536]{2,1,0:T(8,128)(2,1)} %param.17) | copy-start | bytes 9437188
  2.5 4.7 %copy-start.4 = (bf16[1,32,2048]{2,1,0:T(8,128)(2,1)S(1)}, bf16[1,32,2048]{2,1,0:T(8,128)(2,1)}, u32[]{:S(2)}) copy-start(bf16[1,32,2048]{2,1,0:T(8,128)(2,1)} %param.11) | copy-start | bytes 393220
  2.5 7.9 %copy-start.3 = (bf16[1,64,2048]{2,1,0:T(8,128)(2,1)S(1)}, bf16[1,64,2048]{2,1,0:T(8,128)(2,1)}, u32[]{:S(2)}) copy-start(bf16[1,64,2048]{2,1,0:T(8,128)(2,1)} %param.10) | copy-start | bytes 786436
  2.7 38.3 %collective-permute-start.8 = (bf16[1024,768]{1,0:T(8,128)(2,1)S(1)}, bf16[1024,768]{1,0:T(8,128)(2,1)S(1)}, u32[]{:S(2)}, u32[]{:S(2)}) collective-permute-start(bf16[1024,768]{1,0:T(8,128)(2,1)S(1)} %weight_piece.3), channel_id=1, source_target_pairs={{0,16},{16,0},{1,17},{17,1},{2,18},{18,2},{3,19},{19,3},{4,20},{20... | collective-permute-start | bytes 4718600 | tf_op jit(solution)/shard_map/ppermute | solution.py:423
  5.7 13.7 %collective-permute-start.5 = (bf16[2048,128]{1,0:T(8,128)(2,1)}, bf16[2048,128]{1,0:T(8,128)(2,1)}, u32[]{:S(2)}, u32[]{:S(2)}) collective-permute-start(bf16[2048,128]{1,0:T(8,128)(2,1)} %w0.1), channel_id=1, source_target_pairs={{0,2},{1,3},{2,0},{3,1},{4,6},{5,7},{6,4},{7,5},{8,10},{9,11},{10,... | collective-permute-start | bytes 1572872 | tf_op jit(solution)/shard_map/ppermute | solution.py:440
  7.9 4.7 %copy-start.6 = (bf16[32,512]{1,0:T(8,128)(2,1)}, bf16[32,512]{1,0:T(8,128)(2,1)S(1)}, u32[]{:S(2)}) copy-start(bf16[32,512]{1,0:T(8,128)(2,1)S(1)} %get-tuple-element.48) | copy-start | bytes 98308
  7.9 11.6 %collective-permute-start.2 = (bf16[64,512]{1,0:T(8,128)(2,1)}, bf16[64,512]{1,0:T(8,128)(2,1)S(1)}, u32[]{:S(2)}, u32[]{:S(2)}) collective-permute-start(bf16[64,512]{1,0:T(8,128)(2,1)} %get-tuple-element.46), channel_id=1, source_target_pairs={{0,8},{1,9},{2,10},{3,11},{4,12},{5,13},{6,14},{7,15},{8,0},{9,1},... | collective-permute-start | bytes 196616 | tf_op jit(solution)/shard_map/ppermute | solution.py:443
  10.5 4.6 %copy-start.12 = (s32[1,32,8]{1,2,0:T(8,128)S(1)}, s32[1,32,8]{1,2,0:T(8,128)}, u32[]{:S(2)}) copy-start(s32[1,32,8]{1,2,0:T(8,128)} %param.14) | copy-start | bytes 3076
  10.5 14.9 %collective-permute-start.1 = (bf16[64,2048]{1,0:T(8,128)(2,1)S(1)}, bf16[64,2048]{1,0:T(8,128)(2,1)}, u32[]{:S(2)}, u32[]{:S(2)}) collective-permute-start(bf16[64,2048]{1,0:T(8,128)(2,1)S(1)} %bitcast.16), channel_id=1, source_target_pairs={{0,8},{1,9},{2,10},{3,11},{4,12},{5,13},{6,14},{7,15},{8,0},{9,1},... | collective-permute-start | bytes 786440 | tf_op jit(solution)/shard_map/ppermute | solution.py:443
  10.8 14.5 %collective-permute-start = (bf16[64,2048]{1,0:T(8,128)(2,1)S(1)}, bf16[64,2048]{1,0:T(8,128)(2,1)}, u32[]{:S(2)}, u32[]{:S(2)}) collective-permute-start(bf16[64,2048]{1,0:T(8,128)(2,1)S(1)} %bitcast.17), channel_id=1, source_target_pairs={{0,4},{1,5},{2,6},{3,7},{4,0},{5,1},{6,2},{7,3},{8,12},{9,13},{10,... | collective-permute-start | bytes 786440 | tf_op jit(solution)/shard_map/ppermute | solution.py:443
  12.6 1.0 copy-start.8
  13.6 0.8 copy-start.10
  19.4 15.4 %collective-permute-start.7 = (bf16[2048,128]{1,0:T(8,128)(2,1)}, bf16[2048,128]{1,0:T(8,128)(2,1)S(1)}, u32[]{:S(2)}, u32[]{:S(2)}) collective-permute-start(bf16[2048,128]{1,0:T(8,128)(2,1)} %collective-permute-done.5.w2), channel_id=1, source_target_pairs={{0,1},{1,0},{2,3},{3,2},{4,5},{5,4},{6,7},{7,6},{8,9},{9,8},{10,11... | collective-permute-start | bytes 1572872 | tf_op jit(solution)/shard_map/ppermute | solution.py:440
  19.5 15.4 %collective-permute-start.6 = (bf16[2048,128]{1,0:T(8,128)(2,1)}, bf16[2048,128]{1,0:T(8,128)(2,1)S(1)}, u32[]{:S(2)}, u32[]{:S(2)}) collective-permute-start(bf16[2048,128]{1,0:T(8,128)(2,1)} %w0.1), channel_id=1, source_target_pairs={{0,1},{1,0},{2,3},{3,2},{4,5},{5,4},{6,7},{7,6},{8,9},{9,8},{10,11... | collective-permute-start | bytes 1572872 | tf_op jit(solution)/shard_map/ppermute | solution.py:440
  25.4 9.5 %collective-permute-start.3 = (bf16[64,2048]{1,0:T(8,128)(2,1)}, bf16[64,2048]{1,0:T(8,128)(2,1)S(1)}, u32[]{:S(2)}, u32[]{:S(2)}) collective-permute-start(bf16[64,2048]{1,0:T(8,128)(2,1)} %collective-permute-done.1.a2), channel_id=1, source_target_pairs={{0,4},{1,5},{2,6},{3,7},{4,0},{5,1},{6,2},{7,3},{8,12},{9,13},{10,... | collective-permute-start | bytes 786440 | tf_op jit(solution)/shard_map/ppermute | solution.py:443
  26.3 12.0 %copy-start.9 = (bf16[640,768]{1,0:T(8,128)(2,1)S(1)}, bf16[640,768]{1,0:T(8,128)(2,1)}, u32[]{:S(2)}) copy-start(bf16[640,768]{1,0:T(8,128)(2,1)} %copy-done.8) | copy-start | bytes 2949124
  26.3 35.6 %copy-start.11 = (bf16[384,768]{1,0:T(8,128)(2,1)S(1)}, bf16[384,768]{1,0:T(8,128)(2,1)}, u32[]{:S(2)}) copy-start(bf16[384,768]{1,0:T(8,128)(2,1)} %copy-done.10) | copy-start | bytes 1769476
  26.4 36.7 %copy-start.5 = (f32[2048]{0:T(1024)S(1)}, f32[2048]{0:T(1024)}, u32[]{:S(2)}) copy-start(f32[2048]{0:T(1024)} %param.13) | copy-start | bytes 24580
  26.4 8.5 %collective-permute-start.4 = (bf16[64,512]{1,0:T(8,128)(2,1)S(1)}, bf16[64,512]{1,0:T(8,128)(2,1)S(1)}, u32[]{:S(2)}, u32[]{:S(2)}) collective-permute-start(bf16[64,512]{1,0:T(8,128)(2,1)S(1)} %pad_maximum_fusion), channel_id=1, source_target_pairs={{0,4},{1,5},{2,6},{3,7},{4,0},{5,1},{6,2},{7,3},{8,12},{9,13},{10,... | collective-permute-start | bytes 196616 | tf_op jit(solution)/shard_map/ppermute | solution.py:443
  34.9 35.2 %copy-start.1 = (bf16[1,1024,1536]{2,1,0:T(8,128)(2,1)S(1)}, bf16[1,1024,1536]{2,1,0:T(8,128)(2,1)}, u32[]{:S(2)}) copy-start(bf16[1,1024,1536]{2,1,0:T(8,128)(2,1)} %param.17) | copy-start | bytes 9437188
  37.8 6.5 %collective-permute-start.9 = (bf16[128,512]{1,0:T(8,128)(2,1)S(1)}, bf16[128,512]{1,0:T(8,128)(2,1)S(1)}, u32[]{:S(2)}, u32[]{:S(2)}) collective-permute-start(bf16[128,512]{1,0:T(8,128)(2,1)S(1)} %get-tuple-element.55), channel_id=1, source_target_pairs={{0,16},{16,0},{1,17},{17,1},{2,18},{18,2},{3,19},{19,3},{4,20},{20... | collective-permute-start | bytes 393224 | tf_op jit(solution)/shard_map/ppermute | solution.py:423
  38.3 38.3 %collective-permute-start.19 = (bf16[640,768]{1,0:T(8,128)(2,1)S(1)}, bf16[640,768]{1,0:T(8,128)(2,1)S(1)}, u32[]{:S(2)}, u32[]{:S(2)}) collective-permute-start(bf16[640,768]{1,0:T(8,128)(2,1)S(1)} %copy-done.9), channel_id=1, source_target_pairs={{0,16},{16,0},{1,17},{17,1},{2,18},{18,2},{3,19},{19,3},{4,20},{20... | collective-permute-start | bytes 2949128 | tf_op jit(solution)/shard_map/ppermute | solution.py:423
  44.3 7.8 %collective-permute-start.12 = (bf16[144,512]{1,0:T(8,128)(2,1)S(1)}, bf16[144,512]{1,0:T(8,128)(2,1)S(1)}, u32[]{:S(2)}, u32[]{:S(2)}) collective-permute-start(bf16[144,512]{1,0:T(8,128)(2,1)S(1)} %stream.1.b0), channel_id=1, source_target_pairs={{0,12},{1,13},{2,14},{3,15},{4,0},{5,1},{6,2},{7,3},{8,4},{9,5},{1... | collective-permute-start | bytes 442376 | tf_op jit(solution)/shard_map/ppermute | solution.py:426
  47.8 12.0 %collective-permute-start.11 = (bf16[144,512]{1,0:T(8,128)(2,1)S(1)}, bf16[144,512]{1,0:T(8,128)(2,1)S(1)}, u32[]{:S(2)}, u32[]{:S(2)}) collective-permute-start(bf16[144,512]{1,0:T(8,128)(2,1)S(1)} %stream.1.b0), channel_id=1, source_target_pairs={{0,8},{1,9},{2,10},{3,11},{4,12},{5,13},{6,14},{7,15},{8,0},{9,1},... | collective-permute-start | bytes 442376 | tf_op jit(solution)/shard_map/ppermute | solution.py:426
  47.8 13.2 %collective-permute-start.10 = (bf16[144,512]{1,0:T(8,128)(2,1)S(1)}, bf16[144,512]{1,0:T(8,128)(2,1)S(1)}, u32[]{:S(2)}, u32[]{:S(2)}) collective-permute-start(bf16[144,512]{1,0:T(8,128)(2,1)S(1)} %stream.1.b0), channel_id=1, source_target_pairs={{0,4},{1,5},{2,6},{3,7},{4,8},{5,9},{6,10},{7,11},{8,12},{9,13},{1... | collective-permute-start | bytes 442376 | tf_op jit(solution)/shard_map/ppermute | solution.py:426
  48.7 13.2 %collective-permute-start.13 = (bf16[144,512]{1,0:T(8,128)(2,1)S(1)}, bf16[144,512]{1,0:T(8,128)(2,1)S(1)}, u32[]{:S(2)}, u32[]{:S(2)}) collective-permute-start(bf16[144,512]{1,0:T(8,128)(2,1)S(1)} %stream.1.b0), channel_id=1, source_target_pairs={{0,2},{1,3},{2,0},{3,1},{4,6},{5,7},{6,4},{7,5},{8,10},{9,11},{10,... | collective-permute-start | bytes 442376 | tf_op jit(solution)/shard_map/ppermute | solution.py:440
  52.1 11.3 %collective-permute-start.16 = (bf16[144,512]{1,0:T(8,128)(2,1)S(1)}, bf16[144,512]{1,0:T(8,128)(2,1)S(1)}, u32[]{:S(2)}, u32[]{:S(2)}) collective-permute-start(bf16[144,512]{1,0:T(8,128)(2,1)S(1)} %collective-permute-done.12.b3), channel_id=1, source_target_pairs={{0,2},{1,3},{2,0},{3,1},{4,6},{5,7},{6,4},{7,5},{8,10},{9,11},{10,... | collective-permute-start | bytes 442376 | tf_op jit(solution)/shard_map/ppermute | solution.py:440
  59.9 5.9 %collective-permute-start.15 = (bf16[144,512]{1,0:T(8,128)(2,1)S(1)}, bf16[144,512]{1,0:T(8,128)(2,1)S(1)}, u32[]{:S(2)}, u32[]{:S(2)}) collective-permute-start(bf16[144,512]{1,0:T(8,128)(2,1)S(1)} %collective-permute-done.11.b2), channel_id=1, source_target_pairs={{0,2},{1,3},{2,0},{3,1},{4,6},{5,7},{6,4},{7,5},{8,10},{9,11},{10,... | collective-permute-start | bytes 442376 | tf_op jit(solution)/shard_map/ppermute | solution.py:440
  61.0 6.3 %collective-permute-start.14 = (bf16[144,512]{1,0:T(8,128)(2,1)S(1)}, bf16[144,512]{1,0:T(8,128)(2,1)S(1)}, u32[]{:S(2)}, u32[]{:S(2)}) collective-permute-start(bf16[144,512]{1,0:T(8,128)(2,1)S(1)} %collective-permute-done.10.b1), channel_id=1, source_target_pairs={{0,2},{1,3},{2,0},{3,1},{4,6},{5,7},{6,4},{7,5},{8,10},{9,11},{10,... | collective-permute-start | bytes 442376 | tf_op jit(solution)/shard_map/ppermute | solution.py:440
  61.9 14.7 %collective-permute-start.20 = (bf16[384,768]{1,0:T(8,128)(2,1)S(1)}, bf16[384,768]{1,0:T(8,128)(2,1)S(1)}, u32[]{:S(2)}, u32[]{:S(2)}) collective-permute-start(bf16[384,768]{1,0:T(8,128)(2,1)S(1)} %copy-done.11), channel_id=1, source_target_pairs={{0,16},{16,0},{1,17},{17,1},{2,18},{18,2},{3,19},{19,3},{4,20},{20... | collective-permute-start | bytes 1769480 | tf_op jit(solution)/shard_map/ppermute | solution.py:423
  63.4 4.7 %collective-permute-start.18 = (bf16[128,2176]{1,0:T(8,128)(2,1)S(1)}, bf16[128,2176]{1,0:T(8,128)(2,1)S(1)}, u32[]{:S(2)}, u32[]{:S(2)}) collective-permute-start(bf16[128,2176]{1,0:T(8,128)(2,1)S(1)} %get-tuple-element.59.group), channel_id=1, source_target_pairs={{0,1},{1,0},{2,3},{3,2},{4,5},{5,4},{6,7},{7,6},{8,9},{9,8},{10,11... | collective-permute-start | bytes 1671176 | tf_op jit(solution)/shard_map/ppermute | solution.py:440
  68.1 2.0 %collective-permute-start.17 = (bf16[128,2176]{1,0:T(8,128)(2,1)S(1)}, bf16[128,2176]{1,0:T(8,128)(2,1)S(1)}, u32[]{:S(2)}, u32[]{:S(2)}) collective-permute-start(bf16[128,2176]{1,0:T(8,128)(2,1)S(1)} %get-tuple-element.58.group_x), channel_id=1, source_target_pairs={{0,1},{1,0},{2,3},{3,2},{4,5},{5,4},{6,7},{7,6},{8,9},{9,8},{10,11... | collective-permute-start | bytes 1671176 | tf_op jit(solution)/shard_map/ppermute | solution.py:440
  76.7 3.3 %copy-start.2 = (bf16[1,768,1024]{2,1,0:T(8,128)(2,1)S(1)}, bf16[1,768,1024]{2,1,0:T(8,128)(2,1)}, u32[]{:S(2)}) copy-start(bf16[1,768,1024]{2,1,0:T(8,128)(2,1)} %param.18) | copy-start | bytes 4718596
  78.1 11.4 %collective-permute-start.28 = (bf16[256,768]{1,0:T(8,128)(2,1)S(1)}, bf16[256,768]{1,0:T(8,128)(2,1)S(1)}, u32[]{:S(2)}, u32[]{:S(2)}) collective-permute-start(bf16[256,768]{1,0:T(8,128)(2,1)S(1)} %get-tuple-element.66.far), channel_id=1, source_target_pairs={{0,16},{16,0},{1,17},{17,1},{2,18},{18,2},{3,19},{19,3},{4,20},{20... | collective-permute-start | bytes 1179656 | tf_op jit(solution)/shard_map/ppermute | solution.py:423
  80.9 1.4 %collective-permute-start.21 = (bf16[128,512]{1,0:T(8,128)(2,1)S(1)}, bf16[128,512]{1,0:T(8,128)(2,1)S(1)}, u32[]{:S(2)}, u32[]{:S(2)}) collective-permute-start(bf16[128,512]{1,0:T(8,128)(2,1)S(1)} %get-tuple-element.69), channel_id=1, source_target_pairs={{0,1},{1,0},{2,3},{3,2},{4,5},{5,4},{6,7},{7,6},{8,9},{9,8},{10,11... | collective-permute-start | bytes 393224 | tf_op jit(solution)/shard_map/ppermute | solution.py:440
  81.0 1.5 %collective-permute-start.22 = (bf16[128,512]{1,0:T(8,128)(2,1)S(1)}, bf16[128,512]{1,0:T(8,128)(2,1)S(1)}, u32[]{:S(2)}, u32[]{:S(2)}) collective-permute-start(bf16[128,512]{1,0:T(8,128)(2,1)S(1)} %get-tuple-element.70), channel_id=1, source_target_pairs={{0,1},{1,0},{2,3},{3,2},{4,5},{5,4},{6,7},{7,6},{8,9},{9,8},{10,11... | collective-permute-start | bytes 393224 | tf_op jit(solution)/shard_map/ppermute | solution.py:440
  82.6 8.6 %collective-permute-start.23 = (bf16[128,1024]{1,0:T(8,128)(2,1)S(1)}, bf16[128,1024]{1,0:T(8,128)(2,1)S(1)}, u32[]{:S(2)}, u32[]{:S(2)}) collective-permute-start(bf16[128,1024]{1,0:T(8,128)(2,1)S(1)} %fold.2), channel_id=1, source_target_pairs={{0,2},{1,3},{2,0},{3,1},{4,6},{5,7},{6,4},{7,5},{8,10},{9,11},{10,... | collective-permute-start | bytes 786440 | tf_op jit(solution)/shard_map/ppermute | solution.py:440
  84.2 12.4 %collective-permute-start.32 = (bf16[256,768]{1,0:T(8,128)(2,1)S(1)}, bf16[256,768]{1,0:T(8,128)(2,1)S(1)}, u32[]{:S(2)}, u32[]{:S(2)}) collective-permute-start(bf16[256,768]{1,0:T(8,128)(2,1)S(1)} %get-tuple-element.67.near), channel_id=1, source_target_pairs={{0,16},{16,0},{1,17},{17,1},{2,18},{18,2},{3,19},{19,3},{4,20},{20... | collective-permute-start | bytes 1179656 | tf_op jit(solution)/shard_map/ppermute | solution.py:423
  84.7 5.5 %collective-permute-start.24 = (bf16[128,512]{1,0:T(8,128)(2,1)S(1)}, bf16[128,512]{1,0:T(8,128)(2,1)S(1)}, u32[]{:S(2)}, u32[]{:S(2)}) collective-permute-start(bf16[128,512]{1,0:T(8,128)(2,1)S(1)} %get-tuple-element.72), channel_id=1, source_target_pairs={{0,1},{1,0},{2,3},{3,2},{4,5},{5,4},{6,7},{7,6},{8,9},{9,8},{10,11... | collective-permute-start | bytes 393224 | tf_op jit(solution)/shard_map/ppermute | solution.py:440
  84.7 6.0 %collective-permute-start.25 = (bf16[128,512]{1,0:T(8,128)(2,1)S(1)}, bf16[128,512]{1,0:T(8,128)(2,1)S(1)}, u32[]{:S(2)}, u32[]{:S(2)}) collective-permute-start(bf16[128,512]{1,0:T(8,128)(2,1)S(1)} %get-tuple-element.73), channel_id=1, source_target_pairs={{0,1},{1,0},{2,3},{3,2},{4,5},{5,4},{6,7},{7,6},{8,9},{9,8},{10,11... | collective-permute-start | bytes 393224 | tf_op jit(solution)/shard_map/ppermute | solution.py:440
  90.1 1.4 %collective-permute-start.29 = (bf16[128,512]{1,0:T(8,128)(2,1)S(1)}, bf16[128,512]{1,0:T(8,128)(2,1)S(1)}, u32[]{:S(2)}, u32[]{:S(2)}) collective-permute-start(bf16[128,512]{1,0:T(8,128)(2,1)S(1)} %get-tuple-element.78), channel_id=1, source_target_pairs={{0,1},{1,0},{2,3},{3,2},{4,5},{5,4},{6,7},{7,6},{8,9},{9,8},{10,11... | collective-permute-start | bytes 393224 | tf_op jit(solution)/shard_map/ppermute | solution.py:440
  90.2 1.5 %collective-permute-start.30 = (bf16[128,512]{1,0:T(8,128)(2,1)S(1)}, bf16[128,512]{1,0:T(8,128)(2,1)S(1)}, u32[]{:S(2)}, u32[]{:S(2)}) collective-permute-start(bf16[128,512]{1,0:T(8,128)(2,1)S(1)} %get-tuple-element.79), channel_id=1, source_target_pairs={{0,1},{1,0},{2,3},{3,2},{4,5},{5,4},{6,7},{7,6},{8,9},{9,8},{10,11... | collective-permute-start | bytes 393224 | tf_op jit(solution)/shard_map/ppermute | solution.py:440
  91.8 11.2 %collective-permute-start.31 = (bf16[128,1024]{1,0:T(8,128)(2,1)S(1)}, bf16[128,1024]{1,0:T(8,128)(2,1)S(1)}, u32[]{:S(2)}, u32[]{:S(2)}) collective-permute-start(bf16[128,1024]{1,0:T(8,128)(2,1)S(1)} %fold.3), channel_id=1, source_target_pairs={{0,2},{1,3},{2,0},{3,1},{4,6},{5,7},{6,4},{7,5},{8,10},{9,11},{10,... | collective-permute-start | bytes 786440 | tf_op jit(solution)/shard_map/ppermute | solution.py:440
  94.3 8.7 %collective-permute-start.26 = (bf16[64,1024]{1,0:T(8,128)(2,1)S(1)}, bf16[64,1024]{1,0:T(8,128)(2,1)S(1)}, u32[]{:S(2)}, u32[]{:S(2)}) collective-permute-start(bf16[64,1024]{1,0:T(8,128)(2,1)S(1)} %get-tuple-element.74.own), channel_id=1, source_target_pairs={{1,9},{3,11},{5,13},{7,15},{9,1},{11,3},{13,5},{15,7},{17,25},{19,... | collective-permute-start | bytes 393224 | tf_op jit(solution)/shard_map/ppermute | solution.py:437
  95.0 20.3 %copy-start.7 = (f32[2048]{0:T(1024)S(1)}, f32[2048]{0:T(1024)}, u32[]{:S(2)}) copy-start(f32[2048]{0:T(1024)} %param.19) | copy-start | bytes 24580
  95.0 8.0 %collective-permute-start.27 = (bf16[64,1024]{1,0:T(8,128)(2,1)S(1)}, bf16[64,1024]{1,0:T(8,128)(2,1)S(1)}, u32[]{:S(2)}, u32[]{:S(2)}) collective-permute-start(bf16[64,1024]{1,0:T(8,128)(2,1)S(1)} %get-tuple-element.75), channel_id=1, source_target_pairs={{0,4},{1,13},{2,6},{3,15},{4,8},{5,1},{6,10},{7,3},{8,12},{9,5},{1... | collective-permute-start | bytes 393224 | tf_op jit(solution)/shard_map/ppermute | solution.py:437
  97.2 5.7 %collective-permute-start.33 = (bf16[128,512]{1,0:T(8,128)(2,1)S(1)}, bf16[128,512]{1,0:T(8,128)(2,1)S(1)}, u32[]{:S(2)}, u32[]{:S(2)}) collective-permute-start(bf16[128,512]{1,0:T(8,128)(2,1)S(1)} %get-tuple-element.82), channel_id=1, source_target_pairs={{0,1},{1,0},{2,3},{3,2},{4,5},{5,4},{6,7},{7,6},{8,9},{9,8},{10,11... | collective-permute-start | bytes 393224 | tf_op jit(solution)/shard_map/ppermute | solution.py:440
  100.3 2.6 %collective-permute-start.34 = (bf16[128,512]{1,0:T(8,128)(2,1)S(1)}, bf16[128,512]{1,0:T(8,128)(2,1)S(1)}, u32[]{:S(2)}, u32[]{:S(2)}) collective-permute-start(bf16[128,512]{1,0:T(8,128)(2,1)S(1)} %get-tuple-element.83), channel_id=1, source_target_pairs={{0,1},{1,0},{2,3},{3,2},{4,5},{5,4},{6,7},{7,6},{8,9},{9,8},{10,11... | collective-permute-start | bytes 393224 | tf_op jit(solution)/shard_map/ppermute | solution.py:440
  103.1 5.0 %collective-permute-start.35 = (bf16[64,1024]{1,0:T(8,128)(2,1)S(1)}, bf16[64,1024]{1,0:T(8,128)(2,1)S(1)}, u32[]{:S(2)}, u32[]{:S(2)}) collective-permute-start(bf16[64,1024]{1,0:T(8,128)(2,1)S(1)} %get-tuple-element.84), channel_id=1, source_target_pairs={{0,16},{1,25},{2,18},{3,27},{4,20},{5,29},{6,22},{7,31},{8,24},{9,... | collective-permute-start | bytes 393224 | tf_op jit(solution)/shard_map/ppermute | solution.py:437
  104.7 9.1 %collective-permute-start.36 = (bf16[64,1024]{1,0:T(8,128)(2,1)S(1)}, bf16[64,1024]{1,0:T(8,128)(2,1)S(1)}, u32[]{:S(2)}, u32[]{:S(2)}) collective-permute-start(bf16[64,1024]{1,0:T(8,128)(2,1)S(1)} %get-tuple-element.85), channel_id=1, source_target_pairs={{0,20},{1,29},{2,22},{3,31},{4,24},{5,17},{6,26},{7,19},{8,28},{9,... | collective-permute-start | bytes 393224 | tf_op jit(solution)/shard_map/ppermute | solution.py:437
  113.9 1.4 %collective-permute-start.37 = (bf16[64,1024]{1,0:T(8,128)(2,1)S(1)}, bf16[64,1024]{1,0:T(8,128)(2,1)S(1)}, u32[]{:S(2)}, u32[]{:S(2)}) collective-permute-start(bf16[64,1024]{1,0:T(8,128)(2,1)S(1)} %get-tuple-element.87), channel_id=1, source_target_pairs={{0,1},{1,0},{2,3},{3,2},{4,5},{5,4},{6,7},{7,6},{8,9},{9,8},{10,11... | collective-permute-start | bytes 393224 | tf_op jit(solution)/shard_map/ppermute | solution.py:440

commit v14 on v13

--- a/solution.py
+++ b/solution.py
@@ -275,12 +275,13 @@
 
 
 def first_gate_kernel(
-    group_x, group_cx, group, group_c, own, early, inner_ref, part_ref, other_ref, share_ref, mine_ref
+    group_x, group_cx, group, group_c, own, early,
+    first_ref, second_ref, part_ref, other_ref, share_ref, mine_ref,
 ):
     expert, outer, inner, dp = seat()
     count = group.shape[0]
     half = other_ref.shape[1]
-    cut = inner_ref.shape[1]
+    cut = first_ref.shape[1]
     for j, g in enumerate((group_x, group_cx, group, group_c)):
         rows = slice(j * count, (j + 1) * count)
         mine_ref[rows, :] = g[:, aligned(dp, half)]
@@ -292,15 +293,16 @@
     mine, other = mine_ref[...], other_ref[...]
     gate = dot(mine, own[:, 0:cut]) + dot(other, early[:, 0:cut])
     up = dot(mine, own[:, 2 * cut : 3 * cut]) + dot(other, early[:, cut : 2 * cut])
-    inner_ref[...] = swiglu(gate, up, share_ref[:, 0:1])
+    inner = swiglu(gate, up, share_ref[:, 0:1])
+    first_ref[...] = inner[: 3 * count]
+    second_ref[...] = inner[3 * count :]
     part_ref[:, 0:cut] = dot(mine, own[:, cut : 2 * cut])
     part_ref[:, cut : 2 * cut] = dot(mine, own[:, 3 * cut : 4 * cut])
 
 
-def last_gate_kernel(first, part, other, share, *refs):
-    *late, far_ref, near_ref = refs
-    cut = first.shape[1]
-    half = far_ref.shape[0]
+def last_gate_kernel(second, part, other, share, *refs):
+    *late, far_ref, rest_ref = refs
+    count, cut = second.shape
     gate, up = part[:, 0:cut], part[:, cut : 2 * cut]
     at = 0
     for piece in late:
@@ -309,36 +311,59 @@
         up = up + dot(rows, piece[:, cut : 2 * cut])
         at += piece.shape[0]
     value = swiglu(gate, up, share[:, 0:1])
-    far_ref[:, 0:cut] = first[0:half, :]
-    near_ref[:, 0:cut] = first[half:, :]
-    far_ref[:, cut : 2 * cut] = value[:half]
-    near_ref[:, cut : 2 * cut] = value[half:]
-
-
-def down_both_kernel(far, near, wd, keep_far, *refs):
-    *sends, keep_near, rows = refs
-    half = len(sends) // 2
-    down_kernel(far, wd, keep_far, *sends[:half], rows)
-    down_kernel(near, wd, keep_near, *sends[half:], rows)
-
-
-def down_kernel(block, wd, keep_ref, *refs):
-    *sends, rows = refs
+    far_ref[...] = value[: 2 * count]
+    rest_ref[0:count, :] = second[...]
+    rest_ref[count:, :] = value[2 * count :]
+
+
+def down_rows(pieces, wd, keep_ref, sends, rows):
     expert, outer, inner, dp = seat()
     core = inner & 1
     count, side = sends[0].shape
     small = count // 4
-    for i in range(2):
-        for j in range(2):
-            kept = aligned(4 * j + ((outer + 2 * core + i) & 3), small)
-            sent = aligned(4 * (1 - j) + ((outer + 2 - 2 * core + i) & 3), small)
-            at = (2 * i + j) * small
-            rows[at : at + small, :] = block[kept, :]
-            rows[count + at : count + at + small, :] = block[sent, :]
+    for h, places in enumerate(pieces):
+        cut = places[0][0].shape[1]
+        cols = slice(h * cut, (h + 1) * cut)
+        for i in range(2):
+            for j in range(2):
+                ref, start = places[j]
+                kept = aligned(start // small + ((outer + 2 * core + i) & 3), small)
+                at = (2 * i + j) * small
+                rows[at : at + small, cols] = ref[kept, :]
+                ref, start = places[1 - j]
+                sent = aligned(start // small + ((outer + 2 - 2 * core + i) & 3), small)
+                rows[count + at : count + at + small, cols] = ref[sent, :]
     for at in range(0, wd.shape[1], 256):
         value = dot(rows[...], wd[:, at : at + 256]).astype(BF16)
         keep_ref[:, at : at + 256] = value[:count]
         sends[at // side][:, at % side : at % side + 256] = value[count:]
+
+
+def far_places(first, far):
+    count = far.shape[0] // 2
+    return ((first, 0), (first, count)), ((far, 0), (far, count))
+
+
+def near_places(first, rest):
+    count = rest.shape[0] // 3
+    return ((first, 2 * count), (rest, 0)), ((rest, count), (rest, 2 * count))
+
+
+def down_both_kernel(first, far, rest, wd, keep_far, *refs):
+    *sends, keep_near, rows = refs
+    half = len(sends) // 2
+    down_rows(far_places(first, far), wd, keep_far, sends[:half], rows)
+    down_rows(near_places(first, rest), wd, keep_near, sends[half:], rows)
+
+
+def down_far_kernel(first, far, wd, keep_ref, *refs):
+    *sends, rows = refs
+    down_rows(far_places(first, far), wd, keep_ref, sends, rows)
+
+
+def down_near_kernel(first, rest, wd, keep_ref, *refs):
+    *sends, rows = refs
+    down_rows(near_places(first, rest), wd, keep_ref, sends, rows)
 
 
 def added(keep, cores, cols):
@@ -528,12 +553,13 @@
 
     row_total = 16 * rows_here
     half_rows = row_total // 2
-    inner_first, part, other_rows, share_rows = call(
+    inner_first, inner_second, part, other_rows, share_rows = call(
         first_gate_kernel,
         "first_gate_up",
         24,
         (
-            shape_of(row_total, cut_width),
+            shape_of(row_total * 3 // 4, cut_width),
+            shape_of(row_total // 4, cut_width),
             shape_of(row_total, hidden, dtype=F32),
             shape_of(row_total, half_width),
             shape_of(row_total, 128, dtype=F32),
@@ -546,20 +572,20 @@
         gate_up_early,
         scratch=(pltpu.VMEM((row_total, half_width), BF16),),
     )
-    inner_half = shape_of(half_rows, hidden)
-    inner_far, inner_near = call(
+    inner_far, inner_rest = call(
         last_gate_kernel,
         "last_gate_up",
         16,
-        (inner_half, inner_half),
-        inner_first,
+        (shape_of(half_rows, cut_width), shape_of(row_total * 3 // 4, cut_width)),
+        inner_second,
         part,
         other_rows,
         share_rows,
         *gate_up_late,
     )
+    first_other = swap_dp(inner_first)
     far_other = swap_dp(inner_far)
-    near_other = swap_dp(inner_near)
+    rest_other = swap_dp(inner_rest)
 
     count = row_total // 4
     quarter_out = shape_of(count, half_width)
@@ -569,9 +595,9 @@
 
     scratch = (pltpu.VMEM((half_rows, hidden), BF16),)
 
-    def down(rows, many):
+    def down(kernel, rows, many):
         keep, *send = call(
-            down_kernel, "down", 12, (quarter_out, *parts_of(many)), rows, w_down[0], scratch=scratch
+            kernel, "down", 12, (quarter_out, *parts_of(many)), first_other, rows, w_down[0], scratch=scratch
         )
         return keep, send
 
@@ -587,16 +613,16 @@
 
     outs = (quarter_out, *parts_of(2), *parts_of(2), quarter_out)
     keep_far, *send, keep_near = call(
-        down_both_kernel, "down_both", 16, outs, inner_far, inner_near, w_down[0], scratch=scratch
+        down_both_kernel, "down_both", 16, outs, inner_first, inner_far, inner_rest, w_down[0], scratch=scratch
     )
     far = swap_inner(fold(keep_far, swap_cores(send[:2])), 2)
     first_far = far
     own, second = pieces(far, keep_near, send[2:])
     mine = [send_outer(own, 0, False), send_outer(second, 1, False)]
 
-    keep_far, send = down(far_other, 2)
+    keep_far, send = down(down_far_kernel, far_other, 2)
     far = swap_inner(fold(after(keep_far, own), swap_cores(send)), 2)
-    keep_near, send = down(near_other, 2)
+    keep_near, send = down(down_near_kernel, rest_other, 2)
     cut = pieces(far, after(keep_near, *mine), send)
     others = [send_outer(cut[i], i, True) for i in range(2)]
 

time: 116 us -> 115 us (level)
  waiting for transfers between devices: 55.4 us -> 52.5 us
  starting transfers between devices: 40.1 us -> 41.7 us
    ppermute x6 -> x7, starting transfers between devices: 8.59 us -> 10.7 us  [swap_dp(): return lax.ppermute(x, 'dp', [(0, 1), (1, 0)])]
    ppermute x6 -> x7, waiting for transfers between devices: 11.9 us -> 9.83 us  [swap_dp(): return lax.ppermute(x, 'dp', [(0, 1), (1, 0)])]
  transfers between devices with their start and end apart: 38 -> 39, of which waited for: 21 -> 18; matrix products, arithmetic and copies ran while one was open for 1% -> 1% of each run, Pallas kernels for 10% -> 11%
where the time goes in v14:
time: 115 us
  waiting for transfers between devices  52.5 us (46%)
  starting transfers between devices  41.7 us (36%)
  Pallas kernels  13.7 us (12%)
  local copies, waits for them, and re-layouts  4.58 us (4%)
  between operations  1.56 us (1%)
    ppermute x20, starting transfers between devices, swap_inner(): return lax.ppermute(x, 'expert', [(i, i ^ j) for i in range(expert_count)])  15.6 us
    pallas_call x17, Pallas kernels, call(): pl.pallas_call(kernel, out_shape=outs, in_specs=[first] + [vmem] * (len(a...  13.4 us
    ppermute x5, waiting for transfers between devices, swap_outer(): lax.ppermute(x, 'expert', [(i, i ^ 4 * s) for i in range(expert_count)])  12.1 us
    ppermute x20, waiting for transfers between devices, swap_inner(): return lax.ppermute(x, 'expert', [(i, i ^ j) for i in range(expert_count)])  11.6 us
    ppermute x4, waiting for transfers between devices, send_outer(): return lax.ppermute(x, ('dp', 'expert'), pairs)  11.4 us
    ppermute x7, starting transfers between devices, swap_dp(): return lax.ppermute(x, 'dp', [(0, 1), (1, 0)])  10.7 us
    ppermute x7, waiting for transfers between devices, swap_dp(): return lax.ppermute(x, 'dp', [(0, 1), (1, 0)])  9.83 us
    ppermute x3, waiting for transfers between devices, shift_outer(): lax.ppermute(x, 'expert', [(i, (i + 4 * s) % expert_count) for i in range...  7.64 us
  transfers between devices with their start and end apart: 39, of which 18 were waited for; matrix products, arithmetic and copies ran while one was open for 1% of the time, Pallas kernels for 11%

profile of v14, /device:TPU:0, one launch (start us, length us, event | category | flops | bytes accessed | tf_op | source)
XLA Modules:
  0.0 114.9 jit_solution(18189145535676848415)
XLA Ops:
  0.6 1.9 %copy-done = bf16[1,1024,1536]{2,1,0:T(8,128)(2,1)S(1)} copy-done((bf16[1,1024,1536]{2,1,0:T(8,128)(2,1)S(1)}, bf16[1,1024,1536]{2,1,0:T(8,128)(2,1)}, u32[]{:S(2)}) %copy-start) | copy-done | bytes 3145752
  2.5 0.2 weight_piece.3
  2.7 3.0 %collective-permute-start.8 = (bf16[1024,768]{1,0:T(8,128)(2,1)S(1)}, bf16[1024,768]{1,0:T(8,128)(2,1)S(1)}, u32[]{:S(2)}, u32[]{:S(2)}) collective-permute-start(bf16[1024,768]{1,0:T(8,128)(2,1)S(1)} %weight_piece.3), channel_id=1, source_target_pairs={{0,16},{16,0},{1,17},{17,1},{2,18},{18,2},{3,19},{19,3},{4,20},{20... | collective-permute-start | bytes 4718600 | tf_op jit(solution)/shard_map/ppermute | solution.py:448
  5.7 1.5 %collective-permute-start.5 = (bf16[2048,128]{1,0:T(8,128)(2,1)}, bf16[2048,128]{1,0:T(8,128)(2,1)}, u32[]{:S(2)}, u32[]{:S(2)}) collective-permute-start(bf16[2048,128]{1,0:T(8,128)(2,1)} %w0.1), channel_id=1, source_target_pairs={{0,2},{1,3},{2,0},{3,1},{4,6},{5,7},{6,4},{7,5},{8,10},{9,11},{10,... | collective-permute-start | bytes 1572872 | tf_op jit(solution)/shard_map/ppermute | solution.py:465
  7.2 0.6 cut_resid.1
  7.9 2.6 %collective-permute-start.2 = (bf16[64,512]{1,0:T(8,128)(2,1)}, bf16[64,512]{1,0:T(8,128)(2,1)S(1)}, u32[]{:S(2)}, u32[]{:S(2)}) collective-permute-start(bf16[64,512]{1,0:T(8,128)(2,1)} %get-tuple-element.47), channel_id=1, source_target_pairs={{0,8},{1,9},{2,10},{3,11},{4,12},{5,13},{6,14},{7,15},{8,0},{9,1},... | collective-permute-start | bytes 196616 | tf_op jit(solution)/shard_map/ppermute | solution.py:468
  10.5 0.3 collective-permute-start.1
  10.8 1.6 %collective-permute-start = (bf16[64,2048]{1,0:T(8,128)(2,1)S(1)}, bf16[64,2048]{1,0:T(8,128)(2,1)}, u32[]{:S(2)}, u32[]{:S(2)}) collective-permute-start(bf16[64,2048]{1,0:T(8,128)(2,1)S(1)} %bitcast.17), channel_id=1, source_target_pairs={{0,4},{1,5},{2,6},{3,7},{4,0},{5,1},{6,2},{7,3},{8,12},{9,13},{10,... | collective-permute-start | bytes 786440 | tf_op jit(solution)/shard_map/ppermute | solution.py:468
  12.4 0.2 weight_piece.2
  12.6 1.0 copy-done.8
  13.6 0.8 copy-done.10
  15.2 0.8 copy.13
  15.9 0.4 share.1
  16.4 3.1 %collective-permute-done.5.w2 = bf16[2048,128]{1,0:T(8,128)(2,1)} collective-permute-done((bf16[2048,128]{1,0:T(8,128)(2,1)}, bf16[2048,128]{1,0:T(8,128)(2,1)}, u32[]{:S(2)}, u32[]{:S(2)}) %collective-permute-start.5) | collective-permute-done | bytes 524320 | tf_op jit(solution)/shard_map/ppermute | solution.py:465
  19.5 0.5 collective-permute-start.6
  20.0 5.4 %collective-permute-done.1.a2 = bf16[64,2048]{1,0:T(8,128)(2,1)} collective-permute-done((bf16[64,2048]{1,0:T(8,128)(2,1)S(1)}, bf16[64,2048]{1,0:T(8,128)(2,1)}, u32[]{:S(2)}, u32[]{:S(2)}) %collective-permute-start.1) | collective-permute-done | bytes 262176 | tf_op jit(solution)/shard_map/ppermute | solution.py:468
  25.4 0.2 collective-permute-start.3
  25.6 0.8 pad_maximum_fusion
  26.4 1.9 %collective-permute-start.4 = (bf16[64,512]{1,0:T(8,128)(2,1)S(1)}, bf16[64,512]{1,0:T(8,128)(2,1)S(1)}, u32[]{:S(2)}, u32[]{:S(2)}) collective-permute-start(bf16[64,512]{1,0:T(8,128)(2,1)S(1)} %pad_maximum_fusion), channel_id=1, source_target_pairs={{0,4},{1,5},{2,6},{3,7},{4,0},{5,1},{6,2},{7,3},{8,12},{9,13},{10,... | collective-permute-start | bytes 196616 | tf_op jit(solution)/shard_map/ppermute | solution.py:468
  28.2 6.7 %collective-permute-done.4.r13 = bf16[64,512]{1,0:T(8,128)(2,1)S(1)} collective-permute-done((bf16[64,512]{1,0:T(8,128)(2,1)S(1)}, bf16[64,512]{1,0:T(8,128)(2,1)S(1)}, u32[]{:S(2)}, u32[]{:S(2)}) %collective-permute-start.4) | collective-permute-done | bytes 65568 | tf_op jit(solution)/shard_map/ppermute | solution.py:468
  34.9 2.8 %projection.1 = (bf16[128,512]{1,0:T(8,128)(2,1)S(1)}, bf16[128,512]{1,0:T(8,128)(2,1)S(1)}) custom-call(bf16[64,2048]{1,0:T(8,128)(2,1)S(1)} %bitcast.18, bf16[64,2048]{1,0:T(8,128)(2,1)} %collective-permute-done.a1, bf16[64,2048]{1,0:T(8,128)(2,1)} %collective-permute-done.1.a2, bf16[64,2048]{1,0:T(8,128)(2,1)S(1)} %collective-permute-done.3.a3, ...), custom_call_target="tpu_custom_call" | custom-call | flops 1 | bytes 1 | tf_op jit(solution)/shard_map/projection/pallas_call | solution.py:436
  37.8 0.6 collective-permute-start.9
  38.3 1.5 %collective-permute-start.19 = (bf16[640,768]{1,0:T(8,128)(2,1)S(1)}, bf16[640,768]{1,0:T(8,128)(2,1)S(1)}, u32[]{:S(2)}, u32[]{:S(2)}) collective-permute-start(bf16[640,768]{1,0:T(8,128)(2,1)S(1)} %copy-done.9), channel_id=1, source_target_pairs={{0,16},{16,0},{1,17},{17,1},{2,18},{18,2},{3,19},{19,3},{4,20},{20... | collective-permute-start | bytes 2949128 | tf_op jit(solution)/shard_map/ppermute | solution.py:448
  39.9 1.1 collective-permute-done.8.early
  41.0 3.3 %collective-permute-done.9.arrived = bf16[128,512]{1,0:T(8,128)(2,1)S(1)} collective-permute-done((bf16[128,512]{1,0:T(8,128)(2,1)S(1)}, bf16[128,512]{1,0:T(8,128)(2,1)S(1)}, u32[]{:S(2)}, u32[]{:S(2)}) %collective-permute-start.9) | collective-permute-done | bytes 131104 | tf_op jit(solution)/shard_map/ppermute | solution.py:448
  44.3 3.5 %collective-permute-start.12 = (bf16[144,512]{1,0:T(8,128)(2,1)S(1)}, bf16[144,512]{1,0:T(8,128)(2,1)S(1)}, u32[]{:S(2)}, u32[]{:S(2)}) collective-permute-start(bf16[144,512]{1,0:T(8,128)(2,1)S(1)} %stream.1.b0), channel_id=1, source_target_pairs={{0,12},{1,13},{2,14},{3,15},{4,0},{5,1},{6,2},{7,3},{8,4},{9,5},{1... | collective-permute-start | bytes 442376 | tf_op jit(solution)/shard_map/ppermute | solution.py:451
  47.8 0.8 collective-permute-start.10
  48.7 1.9 %collective-permute-start.13 = (bf16[144,512]{1,0:T(8,128)(2,1)S(1)}, bf16[144,512]{1,0:T(8,128)(2,1)S(1)}, u32[]{:S(2)}, u32[]{:S(2)}) collective-permute-start(bf16[144,512]{1,0:T(8,128)(2,1)S(1)} %stream.1.b0), channel_id=1, source_target_pairs={{0,2},{1,3},{2,0},{3,1},{4,6},{5,7},{6,4},{7,5},{8,10},{9,11},{10,... | collective-permute-start | bytes 442376 | tf_op jit(solution)/shard_map/ppermute | solution.py:465
  50.5 1.6 %collective-permute-done.12.b3 = bf16[144,512]{1,0:T(8,128)(2,1)S(1)} collective-permute-done((bf16[144,512]{1,0:T(8,128)(2,1)S(1)}, bf16[144,512]{1,0:T(8,128)(2,1)S(1)}, u32[]{:S(2)}, u32[]{:S(2)}) %collective-permute-start.12) | collective-permute-done | bytes 147488 | tf_op jit(solution)/shard_map/ppermute | solution.py:451
  52.1 1.7 %collective-permute-start.16 = (bf16[144,512]{1,0:T(8,128)(2,1)S(1)}, bf16[144,512]{1,0:T(8,128)(2,1)S(1)}, u32[]{:S(2)}, u32[]{:S(2)}) collective-permute-start(bf16[144,512]{1,0:T(8,128)(2,1)S(1)} %collective-permute-done.12.b3), channel_id=1, source_target_pairs={{0,2},{1,3},{2,0},{3,1},{4,6},{5,7},{6,4},{7,5},{8,10},{9,11},{10,... | collective-permute-start | bytes 442376 | tf_op jit(solution)/shard_map/ppermute | solution.py:465
  53.8 6.0 %collective-permute-done.11.b2 = bf16[144,512]{1,0:T(8,128)(2,1)S(1)} collective-permute-done((bf16[144,512]{1,0:T(8,128)(2,1)S(1)}, bf16[144,512]{1,0:T(8,128)(2,1)S(1)}, u32[]{:S(2)}, u32[]{:S(2)}) %collective-permute-start.11) | collective-permute-done | bytes 147488 | tf_op jit(solution)/shard_map/ppermute | solution.py:451
  59.9 1.1 collective-permute-start.15
  61.0 0.9 collective-permute-start.14
  61.9 1.2 %collective-permute-start.20 = (bf16[384,768]{1,0:T(8,128)(2,1)S(1)}, bf16[384,768]{1,0:T(8,128)(2,1)S(1)}, u32[]{:S(2)}, u32[]{:S(2)}) collective-permute-start(bf16[384,768]{1,0:T(8,128)(2,1)S(1)} %copy-done.11), channel_id=1, source_target_pairs={{0,16},{16,0},{1,17},{17,1},{2,18},{18,2},{3,19},{19,3},{4,20},{20... | collective-permute-start | bytes 1769480 | tf_op jit(solution)/shard_map/ppermute | solution.py:448
  63.1 0.3 norm.2
  63.5 2.3 %collective-permute-done.15.b2 = bf16[144,512]{1,0:T(8,128)(2,1)S(1)} collective-permute-done((bf16[144,512]{1,0:T(8,128)(2,1)S(1)}, bf16[144,512]{1,0:T(8,128)(2,1)S(1)}, u32[]{:S(2)}, u32[]{:S(2)}) %collective-permute-start.15) | collective-permute-done | bytes 147488 | tf_op jit(solution)/shard_map/ppermute | solution.py:465
  65.8 1.6 %collective-permute-done.14.b1 = bf16[144,512]{1,0:T(8,128)(2,1)S(1)} collective-permute-done((bf16[144,512]{1,0:T(8,128)(2,1)S(1)}, bf16[144,512]{1,0:T(8,128)(2,1)S(1)}, u32[]{:S(2)}, u32[]{:S(2)}) %collective-permute-start.14) | collective-permute-done | bytes 147488 | tf_op jit(solution)/shard_map/ppermute | solution.py:465
  67.3 0.8 norm.3
  68.1 2.0 %collective-permute-done.17.group_cx = bf16[128,2176]{1,0:T(8,128)(2,1)S(1)} collective-permute-done((bf16[128,2176]{1,0:T(8,128)(2,1)S(1)}, bf16[128,2176]{1,0:T(8,128)(2,1)S(1)}, u32[]{:S(2)}, u32[]{:S(2)}) %collective-permute-start.17) | collective-permute-done | bytes 557088 | tf_op jit(solution)/shard_map/ppermute | solution.py:465
  70.1 3.4 %first_gate_up.1 = (bf16[384,384]{1,0:T(8,128)(2,1)S(1)}, bf16[128,384]{1,0:T(8,128)(2,1)S(1)}, f32[512,768]{1,0:T(8,128)S(1)}, bf16[512,1024]{1,0:T(8,128)(2,1)S(1)}, f32[512,128]{1,0:T(8,128)S(1)}) custom-call(bf16[128,2176]{1,0:T(8,128)(2,1)S(1)} %get-tuple-element.59.group_x, bf16[128,2176]{1,0:T(8,128)(2,1)S(1)} %collective-permute-done.17.group_cx, ...), custom_call_target="tpu_custom_call" | custom-call | flops 1 | bytes 1 | tf_op jit(solution)/shard_map/first_gate_up/pallas_call | solution.py:436
  73.5 0.9 collective-permute-start.28
  74.4 2.6 %collective-permute-done.20.refs_1_ = bf16[384,768]{1,0:T(8,128)(2,1)S(1)} collective-permute-done((bf16[384,768]{1,0:T(8,128)(2,1)S(1)}, bf16[384,768]{1,0:T(8,128)(2,1)S(1)}, u32[]{:S(2)}, u32[]{:S(2)}) %collective-permute-start.20) | collective-permute-done | bytes 589856 | tf_op jit(solution)/shard_map/ppermute | solution.py:448
  77.1 1.5 %last_gate_up.1 = (bf16[256,384]{1,0:T(8,128)(2,1)S(1)}, bf16[384,384]{1,0:T(8,128)(2,1)S(1)}) custom-call(bf16[128,384]{1,0:T(8,128)(2,1)S(1)} %get-tuple-element.62.second, f32[512,768]{1,0:T(8,128)S(1)} %get-tuple-element.63.part, bf16[512,1024]{1,0:T(8,128)(2,1)S(1)} %get-tuple-element.64.other, f32[512,128]{1,0:T(8,128)S(1)} %get-tuple-element.65.share, ...), custom_call_target="tpu_custom_call" | custom-call | flops 1 | bytes 1 | tf_op jit(solution)/shard_map/last_gate_up/pallas_call | solution.py:436
  78.5 1.0 down_both.1
  79.6 0.5 collective-permute-start.22
  80.1 2.5 %collective-permute-start.29 = (bf16[256,384]{1,0:T(8,128)(2,1)S(1)}, bf16[256,384]{1,0:T(8,128)(2,1)S(1)}, u32[]{:S(2)}, u32[]{:S(2)}) collective-permute-start(bf16[256,384]{1,0:T(8,128)(2,1)S(1)} %get-tuple-element.68.far), channel_id=1, source_target_pairs={{0,16},{16,0},{1,17},{17,1},{2,18},{18,2},{3,19},{19,3},{4,20},{20... | collective-permute-start | bytes 589832 | tf_op jit(solution)/shard_map/ppermute | solution.py:448
  82.7 1.6 %collective-permute-start.23 = (bf16[128,1024]{1,0:T(8,128)(2,1)S(1)}, bf16[128,1024]{1,0:T(8,128)(2,1)S(1)}, u32[]{:S(2)}, u32[]{:S(2)}) collective-permute-start(bf16[128,1024]{1,0:T(8,128)(2,1)S(1)} %fold.2), channel_id=1, source_target_pairs={{0,2},{1,3},{2,0},{3,1},{4,6},{5,7},{6,4},{7,5},{8,10},{9,11},{10,... | collective-permute-start | bytes 786440 | tf_op jit(solution)/shard_map/ppermute | solution.py:465
  84.2 1.1 collective-permute-start.33
  85.3 2.8 %collective-permute-done.29.far = bf16[256,384]{1,0:T(8,128)(2,1)S(1)} collective-permute-done((bf16[256,384]{1,0:T(8,128)(2,1)S(1)}, bf16[256,384]{1,0:T(8,128)(2,1)S(1)}, u32[]{:S(2)}, u32[]{:S(2)}) %collective-permute-start.29) | collective-permute-done | bytes 196640 | tf_op jit(solution)/shard_map/ppermute | solution.py:448
  88.1 0.6 down.2
  88.7 0.6 collective-permute-start.30
  89.4 1.3 %collective-permute-done.23.far = bf16[128,1024]{1,0:T(8,128)(2,1)S(1)} collective-permute-done((bf16[128,1024]{1,0:T(8,128)(2,1)S(1)}, bf16[128,1024]{1,0:T(8,128)(2,1)S(1)}, u32[]{:S(2)}, u32[]{:S(2)}) %collective-permute-start.23) | collective-permute-done | bytes 262176 | tf_op jit(solution)/shard_map/ppermute | solution.py:465
  91.0 2.0 %collective-permute-start.32 = (bf16[128,1024]{1,0:T(8,128)(2,1)S(1)}, bf16[128,1024]{1,0:T(8,128)(2,1)S(1)}, u32[]{:S(2)}, u32[]{:S(2)}) collective-permute-start(bf16[128,1024]{1,0:T(8,128)(2,1)S(1)} %fold.3), channel_id=1, source_target_pairs={{0,2},{1,3},{2,0},{3,1},{4,6},{5,7},{6,4},{7,5},{8,10},{9,11},{10,... | collective-permute-start | bytes 786440 | tf_op jit(solution)/shard_map/ppermute | solution.py:465
  93.0 0.7 collective-permute-start.26
  93.7 1.6 %collective-permute-start.27 = (bf16[64,1024]{1,0:T(8,128)(2,1)S(1)}, bf16[64,1024]{1,0:T(8,128)(2,1)S(1)}, u32[]{:S(2)}, u32[]{:S(2)}) collective-permute-start(bf16[64,1024]{1,0:T(8,128)(2,1)S(1)} %get-tuple-element.77), channel_id=1, source_target_pairs={{0,4},{1,13},{2,6},{3,15},{4,8},{5,1},{6,10},{7,3},{8,12},{9,5},{1... | collective-permute-start | bytes 393224 | tf_op jit(solution)/shard_map/ppermute | solution.py:462
  95.3 0.6 down.3
  95.9 3.0 %collective-permute-start.34 = (bf16[128,512]{1,0:T(8,128)(2,1)S(1)}, bf16[128,512]{1,0:T(8,128)(2,1)S(1)}, u32[]{:S(2)}, u32[]{:S(2)}) collective-permute-start(bf16[128,512]{1,0:T(8,128)(2,1)S(1)} %get-tuple-element.84), channel_id=1, source_target_pairs={{0,1},{1,0},{2,3},{3,2},{4,5},{5,4},{6,7},{7,6},{8,9},{9,8},{10,11... | collective-permute-start | bytes 393224 | tf_op jit(solution)/shard_map/ppermute | solution.py:465
  99.0 2.9 %collective-permute-done.27.a1 = bf16[64,1024]{1,0:T(8,128)(2,1)S(1)} collective-permute-done((bf16[64,1024]{1,0:T(8,128)(2,1)S(1)}, bf16[64,1024]{1,0:T(8,128)(2,1)S(1)}, u32[]{:S(2)}, u32[]{:S(2)}) %collective-permute-start.27) | collective-permute-done | bytes 131104 | tf_op jit(solution)/shard_map/ppermute | solution.py:462
  101.9 1.6 %collective-permute-start.36 = (bf16[64,1024]{1,0:T(8,128)(2,1)S(1)}, bf16[64,1024]{1,0:T(8,128)(2,1)S(1)}, u32[]{:S(2)}, u32[]{:S(2)}) collective-permute-start(bf16[64,1024]{1,0:T(8,128)(2,1)S(1)} %get-tuple-element.86), channel_id=1, source_target_pairs={{0,16},{1,25},{2,18},{3,27},{4,20},{5,29},{6,22},{7,31},{8,24},{9,... | collective-permute-start | bytes 393224 | tf_op jit(solution)/shard_map/ppermute | solution.py:462
  103.5 0.5 collective-permute-start.37
  104.0 2.9 %collective-permute-done.36.b0 = bf16[64,1024]{1,0:T(8,128)(2,1)S(1)} collective-permute-done((bf16[64,1024]{1,0:T(8,128)(2,1)S(1)}, bf16[64,1024]{1,0:T(8,128)(2,1)S(1)}, u32[]{:S(2)}, u32[]{:S(2)}) %collective-permute-start.36) | collective-permute-done | bytes 131104 | tf_op jit(solution)/shard_map/ppermute | solution.py:462
  107.0 5.6 %collective-permute-done.37.b1 = bf16[64,1024]{1,0:T(8,128)(2,1)S(1)} collective-permute-done((bf16[64,1024]{1,0:T(8,128)(2,1)S(1)}, bf16[64,1024]{1,0:T(8,128)(2,1)S(1)}, u32[]{:S(2)}, u32[]{:S(2)}) %collective-permute-start.37) | collective-permute-done | bytes 131104 | tf_op jit(solution)/shard_map/ppermute | solution.py:462
  112.7 1.3 %collective-permute-done.38.core = bf16[64,1024]{1,0:T(8,128)(2,1)S(1)} collective-permute-done((bf16[64,1024]{1,0:T(8,128)(2,1)S(1)}, bf16[64,1024]{1,0:T(8,128)(2,1)S(1)}, u32[]{:S(2)}, u32[]{:S(2)}) %collective-permute-start.38) | collective-permute-done | bytes 131104 | tf_op jit(solution)/shard_map/ppermute | solution.py:465
  114.1 0.8 closing.1
  (63 shorter events, 1.1 us)
Async XLA Ops:
  0.6 1.9 %copy-start = (bf16[1,1024,1536]{2,1,0:T(8,128)(2,1)S(1)}, bf16[1,1024,1536]{2,1,0:T(8,128)(2,1)}, u32[]{:S(2)}) copy-start(bf16[1,1024,1536]{2,1,0:T(8,128)(2,1)} %param.17) | copy-start | bytes 9437188
  2.5 4.7 %copy-start.4 = (bf16[1,32,2048]{2,1,0:T(8,128)(2,1)S(1)}, bf16[1,32,2048]{2,1,0:T(8,128)(2,1)}, u32[]{:S(2)}) copy-start(bf16[1,32,2048]{2,1,0:T(8,128)(2,1)} %param.11) | copy-start | bytes 393220
  2.5 7.9 %copy-start.3 = (bf16[1,64,2048]{2,1,0:T(8,128)(2,1)S(1)}, bf16[1,64,2048]{2,1,0:T(8,128)(2,1)}, u32[]{:S(2)}) copy-start(bf16[1,64,2048]{2,1,0:T(8,128)(2,1)} %param.10) | copy-start | bytes 786436
  2.7 38.3 %collective-permute-start.8 = (bf16[1024,768]{1,0:T(8,128)(2,1)S(1)}, bf16[1024,768]{1,0:T(8,128)(2,1)S(1)}, u32[]{:S(2)}, u32[]{:S(2)}) collective-permute-start(bf16[1024,768]{1,0:T(8,128)(2,1)S(1)} %weight_piece.3), channel_id=1, source_target_pairs={{0,16},{16,0},{1,17},{17,1},{2,18},{18,2},{3,19},{19,3},{4,20},{20... | collective-permute-start | bytes 4718600 | tf_op jit(solution)/shard_map/ppermute | solution.py:448
  5.7 13.7 %collective-permute-start.5 = (bf16[2048,128]{1,0:T(8,128)(2,1)}, bf16[2048,128]{1,0:T(8,128)(2,1)}, u32[]{:S(2)}, u32[]{:S(2)}) collective-permute-start(bf16[2048,128]{1,0:T(8,128)(2,1)} %w0.1), channel_id=1, source_target_pairs={{0,2},{1,3},{2,0},{3,1},{4,6},{5,7},{6,4},{7,5},{8,10},{9,11},{10,... | collective-permute-start | bytes 1572872 | tf_op jit(solution)/shard_map/ppermute | solution.py:465
  7.9 4.7 %copy-start.6 = (bf16[32,512]{1,0:T(8,128)(2,1)}, bf16[32,512]{1,0:T(8,128)(2,1)S(1)}, u32[]{:S(2)}) copy-start(bf16[32,512]{1,0:T(8,128)(2,1)S(1)} %get-tuple-element.49) | copy-start | bytes 98308
  7.9 11.6 %collective-permute-start.2 = (bf16[64,512]{1,0:T(8,128)(2,1)}, bf16[64,512]{1,0:T(8,128)(2,1)S(1)}, u32[]{:S(2)}, u32[]{:S(2)}) collective-permute-start(bf16[64,512]{1,0:T(8,128)(2,1)} %get-tuple-element.47), channel_id=1, source_target_pairs={{0,8},{1,9},{2,10},{3,11},{4,12},{5,13},{6,14},{7,15},{8,0},{9,1},... | collective-permute-start | bytes 196616 | tf_op jit(solution)/shard_map/ppermute | solution.py:468
  10.5 4.6 %copy-start.12 = (s32[1,32,8]{1,2,0:T(8,128)S(1)}, s32[1,32,8]{1,2,0:T(8,128)}, u32[]{:S(2)}) copy-start(s32[1,32,8]{1,2,0:T(8,128)} %param.14) | copy-start | bytes 3076
  10.5 14.9 %collective-permute-start.1 = (bf16[64,2048]{1,0:T(8,128)(2,1)S(1)}, bf16[64,2048]{1,0:T(8,128)(2,1)}, u32[]{:S(2)}, u32[]{:S(2)}) collective-permute-start(bf16[64,2048]{1,0:T(8,128)(2,1)S(1)} %bitcast.16), channel_id=1, source_target_pairs={{0,8},{1,9},{2,10},{3,11},{4,12},{5,13},{6,14},{7,15},{8,0},{9,1},... | collective-permute-start | bytes 786440 | tf_op jit(solution)/shard_map/ppermute | solution.py:468
  10.8 14.5 %collective-permute-start = (bf16[64,2048]{1,0:T(8,128)(2,1)S(1)}, bf16[64,2048]{1,0:T(8,128)(2,1)}, u32[]{:S(2)}, u32[]{:S(2)}) collective-permute-start(bf16[64,2048]{1,0:T(8,128)(2,1)S(1)} %bitcast.17), channel_id=1, source_target_pairs={{0,4},{1,5},{2,6},{3,7},{4,0},{5,1},{6,2},{7,3},{8,12},{9,13},{10,... | collective-permute-start | bytes 786440 | tf_op jit(solution)/shard_map/ppermute | solution.py:468
  12.6 1.0 copy-start.8
  13.6 0.8 copy-start.10
  19.4 15.4 %collective-permute-start.7 = (bf16[2048,128]{1,0:T(8,128)(2,1)}, bf16[2048,128]{1,0:T(8,128)(2,1)S(1)}, u32[]{:S(2)}, u32[]{:S(2)}) collective-permute-start(bf16[2048,128]{1,0:T(8,128)(2,1)} %collective-permute-done.5.w2), channel_id=1, source_target_pairs={{0,1},{1,0},{2,3},{3,2},{4,5},{5,4},{6,7},{7,6},{8,9},{9,8},{10,11... | collective-permute-start | bytes 1572872 | tf_op jit(solution)/shard_map/ppermute | solution.py:465
  19.5 15.4 %collective-permute-start.6 = (bf16[2048,128]{1,0:T(8,128)(2,1)}, bf16[2048,128]{1,0:T(8,128)(2,1)S(1)}, u32[]{:S(2)}, u32[]{:S(2)}) collective-permute-start(bf16[2048,128]{1,0:T(8,128)(2,1)} %w0.1), channel_id=1, source_target_pairs={{0,1},{1,0},{2,3},{3,2},{4,5},{5,4},{6,7},{7,6},{8,9},{9,8},{10,11... | collective-permute-start | bytes 1572872 | tf_op jit(solution)/shard_map/ppermute | solution.py:465
  25.4 9.5 %collective-permute-start.3 = (bf16[64,2048]{1,0:T(8,128)(2,1)}, bf16[64,2048]{1,0:T(8,128)(2,1)S(1)}, u32[]{:S(2)}, u32[]{:S(2)}) collective-permute-start(bf16[64,2048]{1,0:T(8,128)(2,1)} %collective-permute-done.1.a2), channel_id=1, source_target_pairs={{0,4},{1,5},{2,6},{3,7},{4,0},{5,1},{6,2},{7,3},{8,12},{9,13},{10,... | collective-permute-start | bytes 786440 | tf_op jit(solution)/shard_map/ppermute | solution.py:468
  26.3 12.0 %copy-start.9 = (bf16[640,768]{1,0:T(8,128)(2,1)S(1)}, bf16[640,768]{1,0:T(8,128)(2,1)}, u32[]{:S(2)}) copy-start(bf16[640,768]{1,0:T(8,128)(2,1)} %copy-done.8) | copy-start | bytes 2949124
  26.3 35.6 %copy-start.11 = (bf16[384,768]{1,0:T(8,128)(2,1)S(1)}, bf16[384,768]{1,0:T(8,128)(2,1)}, u32[]{:S(2)}) copy-start(bf16[384,768]{1,0:T(8,128)(2,1)} %copy-done.10) | copy-start | bytes 1769476
  26.4 36.7 %copy-start.5 = (f32[2048]{0:T(1024)S(1)}, f32[2048]{0:T(1024)}, u32[]{:S(2)}) copy-start(f32[2048]{0:T(1024)} %param.13) | copy-start | bytes 24580
  26.4 8.5 %collective-permute-start.4 = (bf16[64,512]{1,0:T(8,128)(2,1)S(1)}, bf16[64,512]{1,0:T(8,128)(2,1)S(1)}, u32[]{:S(2)}, u32[]{:S(2)}) collective-permute-start(bf16[64,512]{1,0:T(8,128)(2,1)S(1)} %pad_maximum_fusion), channel_id=1, source_target_pairs={{0,4},{1,5},{2,6},{3,7},{4,0},{5,1},{6,2},{7,3},{8,12},{9,13},{10,... | collective-permute-start | bytes 196616 | tf_op jit(solution)/shard_map/ppermute | solution.py:468
  34.9 35.2 %copy-start.1 = (bf16[1,1024,1536]{2,1,0:T(8,128)(2,1)S(1)}, bf16[1,1024,1536]{2,1,0:T(8,128)(2,1)}, u32[]{:S(2)}) copy-start(bf16[1,1024,1536]{2,1,0:T(8,128)(2,1)} %param.17) | copy-start | bytes 9437188
  37.8 6.5 %collective-permute-start.9 = (bf16[128,512]{1,0:T(8,128)(2,1)S(1)}, bf16[128,512]{1,0:T(8,128)(2,1)S(1)}, u32[]{:S(2)}, u32[]{:S(2)}) collective-permute-start(bf16[128,512]{1,0:T(8,128)(2,1)S(1)} %get-tuple-element.56), channel_id=1, source_target_pairs={{0,16},{16,0},{1,17},{17,1},{2,18},{18,2},{3,19},{19,3},{4,20},{20... | collective-permute-start | bytes 393224 | tf_op jit(solution)/shard_map/ppermute | solution.py:448
  38.3 38.7 %collective-permute-start.19 = (bf16[640,768]{1,0:T(8,128)(2,1)S(1)}, bf16[640,768]{1,0:T(8,128)(2,1)S(1)}, u32[]{:S(2)}, u32[]{:S(2)}) collective-permute-start(bf16[640,768]{1,0:T(8,128)(2,1)S(1)} %copy-done.9), channel_id=1, source_target_pairs={{0,16},{16,0},{1,17},{17,1},{2,18},{18,2},{3,19},{19,3},{4,20},{20... | collective-permute-start | bytes 2949128 | tf_op jit(solution)/shard_map/ppermute | solution.py:448
  44.3 7.8 %collective-permute-start.12 = (bf16[144,512]{1,0:T(8,128)(2,1)S(1)}, bf16[144,512]{1,0:T(8,128)(2,1)S(1)}, u32[]{:S(2)}, u32[]{:S(2)}) collective-permute-start(bf16[144,512]{1,0:T(8,128)(2,1)S(1)} %stream.1.b0), channel_id=1, source_target_pairs={{0,12},{1,13},{2,14},{3,15},{4,0},{5,1},{6,2},{7,3},{8,4},{9,5},{1... | collective-permute-start | bytes 442376 | tf_op jit(solution)/shard_map/ppermute | solution.py:451
  47.8 12.0 %collective-permute-start.11 = (bf16[144,512]{1,0:T(8,128)(2,1)S(1)}, bf16[144,512]{1,0:T(8,128)(2,1)S(1)}, u32[]{:S(2)}, u32[]{:S(2)}) collective-permute-start(bf16[144,512]{1,0:T(8,128)(2,1)S(1)} %stream.1.b0), channel_id=1, source_target_pairs={{0,8},{1,9},{2,10},{3,11},{4,12},{5,13},{6,14},{7,15},{8,0},{9,1},... | collective-permute-start | bytes 442376 | tf_op jit(solution)/shard_map/ppermute | solution.py:451
  47.8 13.2 %collective-permute-start.10 = (bf16[144,512]{1,0:T(8,128)(2,1)S(1)}, bf16[144,512]{1,0:T(8,128)(2,1)S(1)}, u32[]{:S(2)}, u32[]{:S(2)}) collective-permute-start(bf16[144,512]{1,0:T(8,128)(2,1)S(1)} %stream.1.b0), channel_id=1, source_target_pairs={{0,4},{1,5},{2,6},{3,7},{4,8},{5,9},{6,10},{7,11},{8,12},{9,13},{1... | collective-permute-start | bytes 442376 | tf_op jit(solution)/shard_map/ppermute | solution.py:451
  48.7 13.2 %collective-permute-start.13 = (bf16[144,512]{1,0:T(8,128)(2,1)S(1)}, bf16[144,512]{1,0:T(8,128)(2,1)S(1)}, u32[]{:S(2)}, u32[]{:S(2)}) collective-permute-start(bf16[144,512]{1,0:T(8,128)(2,1)S(1)} %stream.1.b0), channel_id=1, source_target_pairs={{0,2},{1,3},{2,0},{3,1},{4,6},{5,7},{6,4},{7,5},{8,10},{9,11},{10,... | collective-permute-start | bytes 442376 | tf_op jit(solution)/shard_map/ppermute | solution.py:465
  52.1 11.3 %collective-permute-start.16 = (bf16[144,512]{1,0:T(8,128)(2,1)S(1)}, bf16[144,512]{1,0:T(8,128)(2,1)S(1)}, u32[]{:S(2)}, u32[]{:S(2)}) collective-permute-start(bf16[144,512]{1,0:T(8,128)(2,1)S(1)} %collective-permute-done.12.b3), channel_id=1, source_target_pairs={{0,2},{1,3},{2,0},{3,1},{4,6},{5,7},{6,4},{7,5},{8,10},{9,11},{10,... | collective-permute-start | bytes 442376 | tf_op jit(solution)/shard_map/ppermute | solution.py:465
  59.9 5.9 %collective-permute-start.15 = (bf16[144,512]{1,0:T(8,128)(2,1)S(1)}, bf16[144,512]{1,0:T(8,128)(2,1)S(1)}, u32[]{:S(2)}, u32[]{:S(2)}) collective-permute-start(bf16[144,512]{1,0:T(8,128)(2,1)S(1)} %collective-permute-done.11.b2), channel_id=1, source_target_pairs={{0,2},{1,3},{2,0},{3,1},{4,6},{5,7},{6,4},{7,5},{8,10},{9,11},{10,... | collective-permute-start | bytes 442376 | tf_op jit(solution)/shard_map/ppermute | solution.py:465
  61.0 6.3 %collective-permute-start.14 = (bf16[144,512]{1,0:T(8,128)(2,1)S(1)}, bf16[144,512]{1,0:T(8,128)(2,1)S(1)}, u32[]{:S(2)}, u32[]{:S(2)}) collective-permute-start(bf16[144,512]{1,0:T(8,128)(2,1)S(1)} %collective-permute-done.10.b1), channel_id=1, source_target_pairs={{0,2},{1,3},{2,0},{3,1},{4,6},{5,7},{6,4},{7,5},{8,10},{9,11},{10,... | collective-permute-start | bytes 442376 | tf_op jit(solution)/shard_map/ppermute | solution.py:465
  61.9 15.1 %collective-permute-start.20 = (bf16[384,768]{1,0:T(8,128)(2,1)S(1)}, bf16[384,768]{1,0:T(8,128)(2,1)S(1)}, u32[]{:S(2)}, u32[]{:S(2)}) collective-permute-start(bf16[384,768]{1,0:T(8,128)(2,1)S(1)} %copy-done.11), channel_id=1, source_target_pairs={{0,16},{16,0},{1,17},{17,1},{2,18},{18,2},{3,19},{19,3},{4,20},{20... | collective-permute-start | bytes 1769480 | tf_op jit(solution)/shard_map/ppermute | solution.py:448
  63.4 4.7 %collective-permute-start.18 = (bf16[128,2176]{1,0:T(8,128)(2,1)S(1)}, bf16[128,2176]{1,0:T(8,128)(2,1)S(1)}, u32[]{:S(2)}, u32[]{:S(2)}) collective-permute-start(bf16[128,2176]{1,0:T(8,128)(2,1)S(1)} %get-tuple-element.60.group), channel_id=1, source_target_pairs={{0,1},{1,0},{2,3},{3,2},{4,5},{5,4},{6,7},{7,6},{8,9},{9,8},{10,11... | collective-permute-start | bytes 1671176 | tf_op jit(solution)/shard_map/ppermute | solution.py:465
  68.1 2.0 %collective-permute-start.17 = (bf16[128,2176]{1,0:T(8,128)(2,1)S(1)}, bf16[128,2176]{1,0:T(8,128)(2,1)S(1)}, u32[]{:S(2)}, u32[]{:S(2)}) collective-permute-start(bf16[128,2176]{1,0:T(8,128)(2,1)S(1)} %get-tuple-element.59.group_x), channel_id=1, source_target_pairs={{0,1},{1,0},{2,3},{3,2},{4,5},{5,4},{6,7},{7,6},{8,9},{9,8},{10,11... | collective-permute-start | bytes 1671176 | tf_op jit(solution)/shard_map/ppermute | solution.py:465
  73.5 14.6 %collective-permute-start.28 = (bf16[384,384]{1,0:T(8,128)(2,1)S(1)}, bf16[384,384]{1,0:T(8,128)(2,1)S(1)}, u32[]{:S(2)}, u32[]{:S(2)}) collective-permute-start(bf16[384,384]{1,0:T(8,128)(2,1)S(1)} %get-tuple-element.61.first), channel_id=1, source_target_pairs={{0,16},{16,0},{1,17},{17,1},{2,18},{18,2},{3,19},{19,3},{4,20},{20... | collective-permute-start | bytes 884744 | tf_op jit(solution)/shard_map/ppermute | solution.py:448
  77.1 1.5 %copy-start.2 = (bf16[1,768,1024]{2,1,0:T(8,128)(2,1)S(1)}, bf16[1,768,1024]{2,1,0:T(8,128)(2,1)}, u32[]{:S(2)}) copy-start(bf16[1,768,1024]{2,1,0:T(8,128)(2,1)} %param.18) | copy-start | bytes 4718596
  79.5 3.1 %collective-permute-start.21 = (bf16[128,512]{1,0:T(8,128)(2,1)S(1)}, bf16[128,512]{1,0:T(8,128)(2,1)S(1)}, u32[]{:S(2)}, u32[]{:S(2)}) collective-permute-start(bf16[128,512]{1,0:T(8,128)(2,1)S(1)} %get-tuple-element.71), channel_id=1, source_target_pairs={{0,1},{1,0},{2,3},{3,2},{4,5},{5,4},{6,7},{7,6},{8,9},{9,8},{10,11... | collective-permute-start | bytes 393224 | tf_op jit(solution)/shard_map/ppermute | solution.py:465
  79.6 3.0 %collective-permute-start.22 = (bf16[128,512]{1,0:T(8,128)(2,1)S(1)}, bf16[128,512]{1,0:T(8,128)(2,1)S(1)}, u32[]{:S(2)}, u32[]{:S(2)}) collective-permute-start(bf16[128,512]{1,0:T(8,128)(2,1)S(1)} %get-tuple-element.72), channel_id=1, source_target_pairs={{0,1},{1,0},{2,3},{3,2},{4,5},{5,4},{6,7},{7,6},{8,9},{9,8},{10,11... | collective-permute-start | bytes 393224 | tf_op jit(solution)/shard_map/ppermute | solution.py:465
  80.1 8.0 %collective-permute-start.29 = (bf16[256,384]{1,0:T(8,128)(2,1)S(1)}, bf16[256,384]{1,0:T(8,128)(2,1)S(1)}, u32[]{:S(2)}, u32[]{:S(2)}) collective-permute-start(bf16[256,384]{1,0:T(8,128)(2,1)S(1)} %get-tuple-element.68.far), channel_id=1, source_target_pairs={{0,16},{16,0},{1,17},{17,1},{2,18},{18,2},{3,19},{19,3},{4,20},{20... | collective-permute-start | bytes 589832 | tf_op jit(solution)/shard_map/ppermute | solution.py:448
  82.7 8.1 %collective-permute-start.23 = (bf16[128,1024]{1,0:T(8,128)(2,1)S(1)}, bf16[128,1024]{1,0:T(8,128)(2,1)S(1)}, u32[]{:S(2)}, u32[]{:S(2)}) collective-permute-start(bf16[128,1024]{1,0:T(8,128)(2,1)S(1)} %fold.2), channel_id=1, source_target_pairs={{0,2},{1,3},{2,0},{3,1},{4,6},{5,7},{6,4},{7,5},{8,10},{9,11},{10,... | collective-permute-start | bytes 786440 | tf_op jit(solution)/shard_map/ppermute | solution.py:465
  84.2 5.0 %collective-permute-start.24 = (bf16[128,512]{1,0:T(8,128)(2,1)S(1)}, bf16[128,512]{1,0:T(8,128)(2,1)S(1)}, u32[]{:S(2)}, u32[]{:S(2)}) collective-permute-start(bf16[128,512]{1,0:T(8,128)(2,1)S(1)} %get-tuple-element.74), channel_id=1, source_target_pairs={{0,1},{1,0},{2,3},{3,2},{4,5},{5,4},{6,7},{7,6},{8,9},{9,8},{10,11... | collective-permute-start | bytes 393224 | tf_op jit(solution)/shard_map/ppermute | solution.py:465
  84.2 11.0 %collective-permute-start.33 = (bf16[384,384]{1,0:T(8,128)(2,1)S(1)}, bf16[384,384]{1,0:T(8,128)(2,1)S(1)}, u32[]{:S(2)}, u32[]{:S(2)}) collective-permute-start(bf16[384,384]{1,0:T(8,128)(2,1)S(1)} %get-tuple-element.69.rest), channel_id=1, source_target_pairs={{0,16},{16,0},{1,17},{17,1},{2,18},{18,2},{3,19},{19,3},{4,20},{20... | collective-permute-start | bytes 884744 | tf_op jit(solution)/shard_map/ppermute | solution.py:448
  88.1 1.3 %collective-permute-start.25 = (bf16[128,512]{1,0:T(8,128)(2,1)S(1)}, bf16[128,512]{1,0:T(8,128)(2,1)S(1)}, u32[]{:S(2)}, u32[]{:S(2)}) collective-permute-start(bf16[128,512]{1,0:T(8,128)(2,1)S(1)} %get-tuple-element.75), channel_id=1, source_target_pairs={{0,1},{1,0},{2,3},{3,2},{4,5},{5,4},{6,7},{7,6},{8,9},{9,8},{10,11... | collective-permute-start | bytes 393224 | tf_op jit(solution)/shard_map/ppermute | solution.py:465
  88.7 2.2 %collective-permute-start.30 = (bf16[128,512]{1,0:T(8,128)(2,1)S(1)}, bf16[128,512]{1,0:T(8,128)(2,1)S(1)}, u32[]{:S(2)}, u32[]{:S(2)}) collective-permute-start(bf16[128,512]{1,0:T(8,128)(2,1)S(1)} %get-tuple-element.80), channel_id=1, source_target_pairs={{0,1},{1,0},{2,3},{3,2},{4,5},{5,4},{6,7},{7,6},{8,9},{9,8},{10,11... | collective-permute-start | bytes 393224 | tf_op jit(solution)/shard_map/ppermute | solution.py:465
  89.3 1.6 %collective-permute-start.31 = (bf16[128,512]{1,0:T(8,128)(2,1)S(1)}, bf16[128,512]{1,0:T(8,128)(2,1)S(1)}, u32[]{:S(2)}, u32[]{:S(2)}) collective-permute-start(bf16[128,512]{1,0:T(8,128)(2,1)S(1)} %get-tuple-element.81), channel_id=1, source_target_pairs={{0,1},{1,0},{2,3},{3,2},{4,5},{5,4},{6,7},{7,6},{8,9},{9,8},{10,11... | collective-permute-start | bytes 393224 | tf_op jit(solution)/shard_map/ppermute | solution.py:465
  91.0 10.9 %collective-permute-start.32 = (bf16[128,1024]{1,0:T(8,128)(2,1)S(1)}, bf16[128,1024]{1,0:T(8,128)(2,1)S(1)}, u32[]{:S(2)}, u32[]{:S(2)}) collective-permute-start(bf16[128,1024]{1,0:T(8,128)(2,1)S(1)} %fold.3), channel_id=1, source_target_pairs={{0,2},{1,3},{2,0},{3,1},{4,6},{5,7},{6,4},{7,5},{8,10},{9,11},{10,... | collective-permute-start | bytes 786440 | tf_op jit(solution)/shard_map/ppermute | solution.py:465
  93.0 8.8 %collective-permute-start.26 = (bf16[64,1024]{1,0:T(8,128)(2,1)S(1)}, bf16[64,1024]{1,0:T(8,128)(2,1)S(1)}, u32[]{:S(2)}, u32[]{:S(2)}) collective-permute-start(bf16[64,1024]{1,0:T(8,128)(2,1)S(1)} %get-tuple-element.76.own), channel_id=1, source_target_pairs={{1,9},{3,11},{5,13},{7,15},{9,1},{11,3},{13,5},{15,7},{17,25},{19,... | collective-permute-start | bytes 393224 | tf_op jit(solution)/shard_map/ppermute | solution.py:462
  93.7 20.4 %copy-start.7 = (f32[2048]{0:T(1024)S(1)}, f32[2048]{0:T(1024)}, u32[]{:S(2)}) copy-start(f32[2048]{0:T(1024)} %param.19) | copy-start | bytes 24580
  93.7 8.1 %collective-permute-start.27 = (bf16[64,1024]{1,0:T(8,128)(2,1)S(1)}, bf16[64,1024]{1,0:T(8,128)(2,1)S(1)}, u32[]{:S(2)}, u32[]{:S(2)}) collective-permute-start(bf16[64,1024]{1,0:T(8,128)(2,1)S(1)} %get-tuple-element.77), channel_id=1, source_target_pairs={{0,4},{1,13},{2,6},{3,15},{4,8},{5,1},{6,10},{7,3},{8,12},{9,5},{1... | collective-permute-start | bytes 393224 | tf_op jit(solution)/shard_map/ppermute | solution.py:462
  95.9 6.0 %collective-permute-start.34 = (bf16[128,512]{1,0:T(8,128)(2,1)S(1)}, bf16[128,512]{1,0:T(8,128)(2,1)S(1)}, u32[]{:S(2)}, u32[]{:S(2)}) collective-permute-start(bf16[128,512]{1,0:T(8,128)(2,1)S(1)} %get-tuple-element.84), channel_id=1, source_target_pairs={{0,1},{1,0},{2,3},{3,2},{4,5},{5,4},{6,7},{7,6},{8,9},{9,8},{10,11... | collective-permute-start | bytes 393224 | tf_op jit(solution)/shard_map/ppermute | solution.py:465
  98.9 3.0 %collective-permute-start.35 = (bf16[128,512]{1,0:T(8,128)(2,1)S(1)}, bf16[128,512]{1,0:T(8,128)(2,1)S(1)}, u32[]{:S(2)}, u32[]{:S(2)}) collective-permute-start(bf16[128,512]{1,0:T(8,128)(2,1)S(1)} %get-tuple-element.85), channel_id=1, source_target_pairs={{0,1},{1,0},{2,3},{3,2},{4,5},{5,4},{6,7},{7,6},{8,9},{9,8},{10,11... | collective-permute-start | bytes 393224 | tf_op jit(solution)/shard_map/ppermute | solution.py:465
  101.9 5.0 %collective-permute-start.36 = (bf16[64,1024]{1,0:T(8,128)(2,1)S(1)}, bf16[64,1024]{1,0:T(8,128)(2,1)S(1)}, u32[]{:S(2)}, u32[]{:S(2)}) collective-permute-start(bf16[64,1024]{1,0:T(8,128)(2,1)S(1)} %get-tuple-element.86), channel_id=1, source_target_pairs={{0,16},{1,25},{2,18},{3,27},{4,20},{5,29},{6,22},{7,31},{8,24},{9,... | collective-permute-start | bytes 393224 | tf_op jit(solution)/shard_map/ppermute | solution.py:462
  103.5 9.0 %collective-permute-start.37 = (bf16[64,1024]{1,0:T(8,128)(2,1)S(1)}, bf16[64,1024]{1,0:T(8,128)(2,1)S(1)}, u32[]{:S(2)}, u32[]{:S(2)}) collective-permute-start(bf16[64,1024]{1,0:T(8,128)(2,1)S(1)} %get-tuple-element.87), channel_id=1, source_target_pairs={{0,20},{1,29},{2,22},{3,31},{4,24},{5,17},{6,26},{7,19},{8,28},{9,... | collective-permute-start | bytes 393224 | tf_op jit(solution)/shard_map/ppermute | solution.py:462
  112.6 1.4 %collective-permute-start.38 = (bf16[64,1024]{1,0:T(8,128)(2,1)S(1)}, bf16[64,1024]{1,0:T(8,128)(2,1)S(1)}, u32[]{:S(2)}, u32[]{:S(2)}) collective-permute-start(bf16[64,1024]{1,0:T(8,128)(2,1)S(1)} %get-tuple-element.89), channel_id=1, source_target_pairs={{0,1},{1,0},{2,3},{3,2},{4,5},{5,4},{6,7},{7,6},{8,9},{9,8},{10,11... | collective-permute-start | bytes 393224 | tf_op jit(solution)/shard_map/ppermute | solution.py:465

commit v15 on v14

--- a/solution.py
+++ b/solution.py
@@ -327,11 +327,11 @@
         for i in range(2):
             for j in range(2):
                 ref, start = places[j]
-                kept = aligned(start // small + ((outer + 2 * core + i) & 3), small)
+                kept = aligned(start // small + ((outer + 3 - core - 2 * i) & 3), small)
                 at = (2 * i + j) * small
                 rows[at : at + small, cols] = ref[kept, :]
                 ref, start = places[1 - j]
-                sent = aligned(start // small + ((outer + 2 - 2 * core + i) & 3), small)
+                sent = aligned(start // small + ((outer + 2 + core - 2 * i) & 3), small)
                 rows[count + at : count + at + small, cols] = ref[sent, :]
     for at in range(0, wd.shape[1], 256):
         value = dot(rows[...], wd[:, at : at + 256]).astype(BF16)
@@ -347,13 +347,6 @@
 def near_places(first, rest):
     count = rest.shape[0] // 3
     return ((first, 2 * count), (rest, 0)), ((rest, count), (rest, 2 * count))
-
-
-def down_both_kernel(first, far, rest, wd, keep_far, *refs):
-    *sends, keep_near, rows = refs
-    half = len(sends) // 2
-    down_rows(far_places(first, far), wd, keep_far, sends[:half], rows)
-    down_rows(near_places(first, rest), wd, keep_near, sends[half:], rows)
 
 
 def down_far_kernel(first, far, wd, keep_ref, *refs):
@@ -391,8 +384,8 @@
 def gather_kernel(own, a0, a1, b0, b1, keep_ref, send_ref):
     expert, outer, inner, dp = seat()
     small = own.shape[0] // 2
-    start = jnp.where((inner & 1) == 0, own[...].astype(F32), a0[...].astype(F32))
-    for i, total in enumerate((start + a1[...].astype(F32), b0[...].astype(F32) + b1[...].astype(F32))):
+    last = jnp.where((inner & 1) == 1, own[...].astype(F32), a1[...].astype(F32))
+    for i, total in enumerate((a0[...].astype(F32) + last, b0[...].astype(F32) + b1[...].astype(F32))):
         rows = slice(i * small, (i + 1) * small)
         keep_ref[rows, :] = total[:small]
         send_ref[rows, :] = total[small:].astype(BF16)
@@ -456,7 +449,7 @@
         pairs = []
         for at in range(2 * expert_count):
             d, e = divmod(at, expert_count)
-            step = 2 * (e % 2) + i
+            step = 3 - e % 2 - 2 * i
             if step or cross:
                 pairs.append((at, (d ^ cross) * expert_count + (e + 4 * step) % expert_count))
         return lax.ppermute(x, ("dp", "expert"), pairs)
@@ -595,9 +588,9 @@
 
     scratch = (pltpu.VMEM((half_rows, hidden), BF16),)
 
-    def down(kernel, rows, many):
+    def down(kernel, first, rows, many):
         keep, *send = call(
-            kernel, "down", 12, (quarter_out, *parts_of(many)), first_other, rows, w_down[0], scratch=scratch
+            kernel, "down", 12, (quarter_out, *parts_of(many)), first, rows, w_down[0], scratch=scratch
         )
         return keep, send
 
@@ -611,18 +604,15 @@
         outs = (shape_of(2 * rows_here, half_width),) * 2
         return call(pieces_kernel, "pieces", 4, outs, far, keep, *swap_cores(send))
 
-    outs = (quarter_out, *parts_of(2), *parts_of(2), quarter_out)
-    keep_far, *send, keep_near = call(
-        down_both_kernel, "down_both", 16, outs, inner_first, inner_far, inner_rest, w_down[0], scratch=scratch
-    )
-    far = swap_inner(fold(keep_far, swap_cores(send[:2])), 2)
-    first_far = far
-    own, second = pieces(far, keep_near, send[2:])
-    mine = [send_outer(own, 0, False), send_outer(second, 1, False)]
-
-    keep_far, send = down(down_far_kernel, far_other, 2)
+    keep_far, send = down(down_far_kernel, inner_first, inner_far, 2)
+    far = swap_inner(fold(keep_far, swap_cores(send)), 2)
+    keep_near, send = down(down_near_kernel, inner_first, inner_rest, 2)
+    first, own = pieces(far, keep_near, send)
+    mine = [send_outer(first, 0, False), send_outer(own, 1, False)]
+
+    keep_far, send = down(down_far_kernel, first_other, far_other, 2)
     far = swap_inner(fold(after(keep_far, own), swap_cores(send)), 2)
-    keep_near, send = down(down_near_kernel, rest_other, 2)
+    keep_near, send = down(down_near_kernel, first_other, rest_other, 2)
     cut = pieces(far, after(keep_near, *mine), send)
     others = [send_outer(cut[i], i, True) for i in range(2)]
 

time: 115 us -> 117 us (1.017)
  starting transfers between devices: 41.7 us -> 44.9 us
  waiting for transfers between devices: 52.5 us -> 51.1 us
    ppermute x4, starting transfers between devices: 4.36 us -> 10 us  [send_outer(): return lax.ppermute(x, ('dp', 'expert'), pairs)]
    ppermute x20, starting transfers between devices: 15.6 us -> 13.2 us  [swap_inner(): return lax.ppermute(x, 'expert', [(i, i ^ j) for i in range(expert_count)])]
    pallas_call x17 -> x18, Pallas kernels: 13.4 us -> 13.5 us  [call(): pl.pallas_call(kernel, out_shape=outs, in_specs=[first] + [vmem] * (len(a...]
where the time goes in v15:
time: 117 us
  waiting for transfers between devices  51.1 us (44%)
  starting transfers between devices  44.9 us (38%)
  Pallas kernels  13.9 us (12%)
  local copies, waits for them, and re-layouts  4.6 us (4%)
  between operations  1.58 us (1%)
    pallas_call x18, Pallas kernels, call(): pl.pallas_call(kernel, out_shape=outs, in_specs=[first] + [vmem] * (len(a...  13.5 us
    ppermute x20, starting transfers between devices, swap_inner(): return lax.ppermute(x, 'expert', [(i, i ^ j) for i in range(expert_count)])  13.2 us
    ppermute x5, waiting for transfers between devices, swap_outer(): lax.ppermute(x, 'expert', [(i, i ^ 4 * s) for i in range(expert_count)])  12.1 us
    ppermute x20, waiting for transfers between devices, swap_inner(): return lax.ppermute(x, 'expert', [(i, i ^ j) for i in range(expert_count)])  12 us
    ppermute x7, starting transfers between devices, swap_dp(): return lax.ppermute(x, 'dp', [(0, 1), (1, 0)])  10.8 us
    ppermute x4, waiting for transfers between devices, send_outer(): return lax.ppermute(x, ('dp', 'expert'), pairs)  10.6 us
    ppermute x4, starting transfers between devices, send_outer(): return lax.ppermute(x, ('dp', 'expert'), pairs)  10 us
    ppermute x7, waiting for transfers between devices, swap_dp(): return lax.ppermute(x, 'dp', [(0, 1), (1, 0)])  8.81 us
  transfers between devices with their start and end apart: 39, of which 18 were waited for; matrix products, arithmetic and copies ran while one was open for 1% of the time, Pallas kernels for 11%

profile of v15, /device:TPU:0, one launch (start us, length us, event | category | flops | bytes accessed | tf_op | source)
XLA Modules:
  0.0 116.9 jit_solution(281096752632836498)
XLA Ops:
  0.6 1.9 %copy-done = bf16[1,1024,1536]{2,1,0:T(8,128)(2,1)S(1)} copy-done((bf16[1,1024,1536]{2,1,0:T(8,128)(2,1)S(1)}, bf16[1,1024,1536]{2,1,0:T(8,128)(2,1)}, u32[]{:S(2)}) %copy-start) | copy-done | bytes 3145752
  2.5 0.2 weight_piece.3
  2.7 3.0 %collective-permute-start.8 = (bf16[1024,768]{1,0:T(8,128)(2,1)S(1)}, bf16[1024,768]{1,0:T(8,128)(2,1)S(1)}, u32[]{:S(2)}, u32[]{:S(2)}) collective-permute-start(bf16[1024,768]{1,0:T(8,128)(2,1)S(1)} %weight_piece.3), channel_id=1, source_target_pairs={{0,16},{16,0},{1,17},{17,1},{2,18},{18,2},{3,19},{19,3},{4,20},{20... | collective-permute-start | bytes 4718600 | tf_op jit(solution)/shard_map/ppermute | solution.py:441
  5.7 1.5 %collective-permute-start.5 = (bf16[2048,128]{1,0:T(8,128)(2,1)}, bf16[2048,128]{1,0:T(8,128)(2,1)}, u32[]{:S(2)}, u32[]{:S(2)}) collective-permute-start(bf16[2048,128]{1,0:T(8,128)(2,1)} %w0.1), channel_id=1, source_target_pairs={{0,2},{1,3},{2,0},{3,1},{4,6},{5,7},{6,4},{7,5},{8,10},{9,11},{10,... | collective-permute-start | bytes 1572872 | tf_op jit(solution)/shard_map/ppermute | solution.py:458
  7.2 0.6 cut_resid.1
  7.9 2.6 %collective-permute-start.2 = (bf16[64,512]{1,0:T(8,128)(2,1)}, bf16[64,512]{1,0:T(8,128)(2,1)S(1)}, u32[]{:S(2)}, u32[]{:S(2)}) collective-permute-start(bf16[64,512]{1,0:T(8,128)(2,1)} %get-tuple-element.47), channel_id=1, source_target_pairs={{0,8},{1,9},{2,10},{3,11},{4,12},{5,13},{6,14},{7,15},{8,0},{9,1},... | collective-permute-start | bytes 196616 | tf_op jit(solution)/shard_map/ppermute | solution.py:461
  10.5 0.3 collective-permute-start.1
  10.8 1.6 %collective-permute-start = (bf16[64,2048]{1,0:T(8,128)(2,1)S(1)}, bf16[64,2048]{1,0:T(8,128)(2,1)}, u32[]{:S(2)}, u32[]{:S(2)}) collective-permute-start(bf16[64,2048]{1,0:T(8,128)(2,1)S(1)} %bitcast.18), channel_id=1, source_target_pairs={{0,4},{1,5},{2,6},{3,7},{4,0},{5,1},{6,2},{7,3},{8,12},{9,13},{10,... | collective-permute-start | bytes 786440 | tf_op jit(solution)/shard_map/ppermute | solution.py:461
  12.4 0.2 weight_piece.2
  12.6 1.0 copy-done.8
  13.6 0.8 copy-done.10
  15.2 0.8 copy.13
  15.9 0.4 share.1
  16.4 3.0 %collective-permute-done.5.w2 = bf16[2048,128]{1,0:T(8,128)(2,1)} collective-permute-done((bf16[2048,128]{1,0:T(8,128)(2,1)}, bf16[2048,128]{1,0:T(8,128)(2,1)}, u32[]{:S(2)}, u32[]{:S(2)}) %collective-permute-start.5) | collective-permute-done | bytes 524320 | tf_op jit(solution)/shard_map/ppermute | solution.py:458
  19.5 0.5 collective-permute-start.6
  20.0 5.4 %collective-permute-done.1.a2 = bf16[64,2048]{1,0:T(8,128)(2,1)} collective-permute-done((bf16[64,2048]{1,0:T(8,128)(2,1)S(1)}, bf16[64,2048]{1,0:T(8,128)(2,1)}, u32[]{:S(2)}, u32[]{:S(2)}) %collective-permute-start.1) | collective-permute-done | bytes 262176 | tf_op jit(solution)/shard_map/ppermute | solution.py:461
  25.4 0.2 collective-permute-start.3
  25.6 0.8 pad_maximum_fusion
  26.4 1.9 %collective-permute-start.4 = (bf16[64,512]{1,0:T(8,128)(2,1)S(1)}, bf16[64,512]{1,0:T(8,128)(2,1)S(1)}, u32[]{:S(2)}, u32[]{:S(2)}) collective-permute-start(bf16[64,512]{1,0:T(8,128)(2,1)S(1)} %pad_maximum_fusion), channel_id=1, source_target_pairs={{0,4},{1,5},{2,6},{3,7},{4,0},{5,1},{6,2},{7,3},{8,12},{9,13},{10,... | collective-permute-start | bytes 196616 | tf_op jit(solution)/shard_map/ppermute | solution.py:461
  28.2 6.7 %collective-permute-done.4.r13 = bf16[64,512]{1,0:T(8,128)(2,1)S(1)} collective-permute-done((bf16[64,512]{1,0:T(8,128)(2,1)S(1)}, bf16[64,512]{1,0:T(8,128)(2,1)S(1)}, u32[]{:S(2)}, u32[]{:S(2)}) %collective-permute-start.4) | collective-permute-done | bytes 65568 | tf_op jit(solution)/shard_map/ppermute | solution.py:461
  34.9 2.8 %projection.1 = (bf16[128,512]{1,0:T(8,128)(2,1)S(1)}, bf16[128,512]{1,0:T(8,128)(2,1)S(1)}) custom-call(bf16[64,2048]{1,0:T(8,128)(2,1)S(1)} %bitcast.19, bf16[64,2048]{1,0:T(8,128)(2,1)} %collective-permute-done.a1, bf16[64,2048]{1,0:T(8,128)(2,1)} %collective-permute-done.1.a2, bf16[64,2048]{1,0:T(8,128)(2,1)S(1)} %collective-permute-done.3.a3, ...), custom_call_target="tpu_custom_call" | custom-call | flops 1 | bytes 1 | tf_op jit(solution)/shard_map/projection/pallas_call | solution.py:429
  37.8 0.6 collective-permute-start.9
  38.3 1.5 %collective-permute-start.19 = (bf16[640,768]{1,0:T(8,128)(2,1)S(1)}, bf16[640,768]{1,0:T(8,128)(2,1)S(1)}, u32[]{:S(2)}, u32[]{:S(2)}) collective-permute-start(bf16[640,768]{1,0:T(8,128)(2,1)S(1)} %copy-done.9), channel_id=1, source_target_pairs={{0,16},{16,0},{1,17},{17,1},{2,18},{18,2},{3,19},{19,3},{4,20},{20... | collective-permute-start | bytes 2949128 | tf_op jit(solution)/shard_map/ppermute | solution.py:441
  39.9 1.1 collective-permute-done.8.early
  41.0 3.3 %collective-permute-done.9.arrived = bf16[128,512]{1,0:T(8,128)(2,1)S(1)} collective-permute-done((bf16[128,512]{1,0:T(8,128)(2,1)S(1)}, bf16[128,512]{1,0:T(8,128)(2,1)S(1)}, u32[]{:S(2)}, u32[]{:S(2)}) %collective-permute-start.9) | collective-permute-done | bytes 131104 | tf_op jit(solution)/shard_map/ppermute | solution.py:441
  44.3 3.5 %collective-permute-start.12 = (bf16[144,512]{1,0:T(8,128)(2,1)S(1)}, bf16[144,512]{1,0:T(8,128)(2,1)S(1)}, u32[]{:S(2)}, u32[]{:S(2)}) collective-permute-start(bf16[144,512]{1,0:T(8,128)(2,1)S(1)} %stream.1.b0), channel_id=1, source_target_pairs={{0,12},{1,13},{2,14},{3,15},{4,0},{5,1},{6,2},{7,3},{8,4},{9,5},{1... | collective-permute-start | bytes 442376 | tf_op jit(solution)/shard_map/ppermute | solution.py:444
  47.8 0.8 collective-permute-start.10
  48.7 1.9 %collective-permute-start.13 = (bf16[144,512]{1,0:T(8,128)(2,1)S(1)}, bf16[144,512]{1,0:T(8,128)(2,1)S(1)}, u32[]{:S(2)}, u32[]{:S(2)}) collective-permute-start(bf16[144,512]{1,0:T(8,128)(2,1)S(1)} %stream.1.b0), channel_id=1, source_target_pairs={{0,2},{1,3},{2,0},{3,1},{4,6},{5,7},{6,4},{7,5},{8,10},{9,11},{10,... | collective-permute-start | bytes 442376 | tf_op jit(solution)/shard_map/ppermute | solution.py:458
  50.5 1.6 %collective-permute-done.12.b3 = bf16[144,512]{1,0:T(8,128)(2,1)S(1)} collective-permute-done((bf16[144,512]{1,0:T(8,128)(2,1)S(1)}, bf16[144,512]{1,0:T(8,128)(2,1)S(1)}, u32[]{:S(2)}, u32[]{:S(2)}) %collective-permute-start.12) | collective-permute-done | bytes 147488 | tf_op jit(solution)/shard_map/ppermute | solution.py:444
  52.1 1.7 %collective-permute-start.16 = (bf16[144,512]{1,0:T(8,128)(2,1)S(1)}, bf16[144,512]{1,0:T(8,128)(2,1)S(1)}, u32[]{:S(2)}, u32[]{:S(2)}) collective-permute-start(bf16[144,512]{1,0:T(8,128)(2,1)S(1)} %collective-permute-done.12.b3), channel_id=1, source_target_pairs={{0,2},{1,3},{2,0},{3,1},{4,6},{5,7},{6,4},{7,5},{8,10},{9,11},{10,... | collective-permute-start | bytes 442376 | tf_op jit(solution)/shard_map/ppermute | solution.py:458
  53.8 6.0 %collective-permute-done.11.b2 = bf16[144,512]{1,0:T(8,128)(2,1)S(1)} collective-permute-done((bf16[144,512]{1,0:T(8,128)(2,1)S(1)}, bf16[144,512]{1,0:T(8,128)(2,1)S(1)}, u32[]{:S(2)}, u32[]{:S(2)}) %collective-permute-start.11) | collective-permute-done | bytes 147488 | tf_op jit(solution)/shard_map/ppermute | solution.py:444
  59.9 1.1 collective-permute-start.15
  61.0 0.9 collective-permute-start.14
  61.9 1.2 collective-permute-start.20
  63.1 0.3 norm.2
  63.5 2.3 %collective-permute-done.15.b2 = bf16[144,512]{1,0:T(8,128)(2,1)S(1)} collective-permute-done((bf16[144,512]{1,0:T(8,128)(2,1)S(1)}, bf16[144,512]{1,0:T(8,128)(2,1)S(1)}, u32[]{:S(2)}, u32[]{:S(2)}) %collective-permute-start.15) | collective-permute-done | bytes 147488 | tf_op jit(solution)/shard_map/ppermute | solution.py:458
  65.8 1.6 %collective-permute-done.14.b1 = bf16[144,512]{1,0:T(8,128)(2,1)S(1)} collective-permute-done((bf16[144,512]{1,0:T(8,128)(2,1)S(1)}, bf16[144,512]{1,0:T(8,128)(2,1)S(1)}, u32[]{:S(2)}, u32[]{:S(2)}) %collective-permute-start.14) | collective-permute-done | bytes 147488 | tf_op jit(solution)/shard_map/ppermute | solution.py:458
  67.3 0.8 norm.3
  68.1 2.0 %collective-permute-done.17.group_cx = bf16[128,2176]{1,0:T(8,128)(2,1)S(1)} collective-permute-done((bf16[128,2176]{1,0:T(8,128)(2,1)S(1)}, bf16[128,2176]{1,0:T(8,128)(2,1)S(1)}, u32[]{:S(2)}, u32[]{:S(2)}) %collective-permute-start.17) | collective-permute-done | bytes 557088 | tf_op jit(solution)/shard_map/ppermute | solution.py:458
  70.1 3.4 %first_gate_up.1 = (bf16[384,384]{1,0:T(8,128)(2,1)S(1)}, bf16[128,384]{1,0:T(8,128)(2,1)S(1)}, f32[512,768]{1,0:T(8,128)S(1)}, bf16[512,1024]{1,0:T(8,128)(2,1)S(1)}, f32[512,128]{1,0:T(8,128)S(1)}) custom-call(bf16[128,2176]{1,0:T(8,128)(2,1)S(1)} %get-tuple-element.59.group_x, bf16[128,2176]{1,0:T(8,128)(2,1)S(1)} %collective-permute-done.17.group_cx, ...), custom_call_target="tpu_custom_call" | custom-call | flops 1 | bytes 1 | tf_op jit(solution)/shard_map/first_gate_up/pallas_call | solution.py:429
  73.5 0.9 collective-permute-start.28
  74.4 2.6 %collective-permute-done.20.refs_1_ = bf16[384,768]{1,0:T(8,128)(2,1)S(1)} collective-permute-done((bf16[384,768]{1,0:T(8,128)(2,1)S(1)}, bf16[384,768]{1,0:T(8,128)(2,1)S(1)}, u32[]{:S(2)}, u32[]{:S(2)}) %collective-permute-start.20) | collective-permute-done | bytes 589856 | tf_op jit(solution)/shard_map/ppermute | solution.py:441
  77.1 1.5 %last_gate_up.1 = (bf16[256,384]{1,0:T(8,128)(2,1)S(1)}, bf16[384,384]{1,0:T(8,128)(2,1)S(1)}) custom-call(bf16[128,384]{1,0:T(8,128)(2,1)S(1)} %get-tuple-element.62.second, f32[512,768]{1,0:T(8,128)S(1)} %get-tuple-element.63.part, bf16[512,1024]{1,0:T(8,128)(2,1)S(1)} %get-tuple-element.64.other, f32[512,128]{1,0:T(8,128)S(1)} %get-tuple-element.65.share, ...), custom_call_target="tpu_custom_call" | custom-call | flops 1 | bytes 1 | tf_op jit(solution)/shard_map/last_gate_up/pallas_call | solution.py:429
  78.5 0.6 down.4
  79.2 0.5 collective-permute-start.22
  79.7 2.5 %collective-permute-start.29 = (bf16[256,384]{1,0:T(8,128)(2,1)S(1)}, bf16[256,384]{1,0:T(8,128)(2,1)S(1)}, u32[]{:S(2)}, u32[]{:S(2)}) collective-permute-start(bf16[256,384]{1,0:T(8,128)(2,1)S(1)} %get-tuple-element.68.far), channel_id=1, source_target_pairs={{0,16},{16,0},{1,17},{17,1},{2,18},{18,2},{3,19},{19,3},{4,20},{20... | collective-permute-start | bytes 589832 | tf_op jit(solution)/shard_map/ppermute | solution.py:441
  82.3 1.6 %collective-permute-start.23 = (bf16[128,1024]{1,0:T(8,128)(2,1)S(1)}, bf16[128,1024]{1,0:T(8,128)(2,1)S(1)}, u32[]{:S(2)}, u32[]{:S(2)}) collective-permute-start(bf16[128,1024]{1,0:T(8,128)(2,1)S(1)} %fold.2), channel_id=1, source_target_pairs={{0,2},{1,3},{2,0},{3,1},{4,6},{5,7},{6,4},{7,5},{8,10},{9,11},{10,... | collective-permute-start | bytes 786440 | tf_op jit(solution)/shard_map/ppermute | solution.py:458
  83.8 0.6 down.5
  84.5 1.1 collective-permute-start.33
  85.6 1.8 %collective-permute-done.29.far = bf16[256,384]{1,0:T(8,128)(2,1)S(1)} collective-permute-done((bf16[256,384]{1,0:T(8,128)(2,1)S(1)}, bf16[256,384]{1,0:T(8,128)(2,1)S(1)}, u32[]{:S(2)}, u32[]{:S(2)}) %collective-permute-start.29) | collective-permute-done | bytes 196640 | tf_op jit(solution)/shard_map/ppermute | solution.py:441
  87.3 0.6 down.6
  87.9 0.6 collective-permute-start.30
  88.7 1.7 %collective-permute-done.23.far = bf16[128,1024]{1,0:T(8,128)(2,1)S(1)} collective-permute-done((bf16[128,1024]{1,0:T(8,128)(2,1)S(1)}, bf16[128,1024]{1,0:T(8,128)(2,1)S(1)}, u32[]{:S(2)}, u32[]{:S(2)}) %collective-permute-start.23) | collective-permute-done | bytes 262176 | tf_op jit(solution)/shard_map/ppermute | solution.py:458
  90.5 2.0 %collective-permute-start.32 = (bf16[128,1024]{1,0:T(8,128)(2,1)S(1)}, bf16[128,1024]{1,0:T(8,128)(2,1)S(1)}, u32[]{:S(2)}, u32[]{:S(2)}) collective-permute-start(bf16[128,1024]{1,0:T(8,128)(2,1)S(1)} %fold.3), channel_id=1, source_target_pairs={{0,2},{1,3},{2,0},{3,1},{4,6},{5,7},{6,4},{7,5},{8,10},{9,11},{10,... | collective-permute-start | bytes 786440 | tf_op jit(solution)/shard_map/ppermute | solution.py:458
  92.6 3.5 %collective-permute-start.27 = (bf16[64,1024]{1,0:T(8,128)(2,1)S(1)}, bf16[64,1024]{1,0:T(8,128)(2,1)S(1)}, u32[]{:S(2)}, u32[]{:S(2)}) collective-permute-start(bf16[64,1024]{1,0:T(8,128)(2,1)S(1)} %get-tuple-element.76.own), channel_id=1, source_target_pairs={{0,4},{2,6},{4,8},{6,10},{8,12},{10,14},{12,0},{14,2},{16,20},{18,... | collective-permute-start | bytes 393224 | tf_op jit(solution)/shard_map/ppermute | solution.py:455
  96.1 2.3 %collective-permute-start.26 = (bf16[64,1024]{1,0:T(8,128)(2,1)S(1)}, bf16[64,1024]{1,0:T(8,128)(2,1)S(1)}, u32[]{:S(2)}, u32[]{:S(2)}) collective-permute-start(bf16[64,1024]{1,0:T(8,128)(2,1)S(1)} %get-tuple-element.77), channel_id=1, source_target_pairs={{0,12},{1,9},{2,14},{3,11},{4,0},{5,13},{6,2},{7,15},{8,4},{9,1},{... | collective-permute-start | bytes 393224 | tf_op jit(solution)/shard_map/ppermute | solution.py:455
  98.4 0.6 down.7
  99.0 0.5 collective-permute-start.35
  99.5 3.0 %collective-permute-done.26.a0 = bf16[64,1024]{1,0:T(8,128)(2,1)S(1)} collective-permute-done((bf16[64,1024]{1,0:T(8,128)(2,1)S(1)}, bf16[64,1024]{1,0:T(8,128)(2,1)S(1)}, u32[]{:S(2)}, u32[]{:S(2)}) %collective-permute-start.26) | collective-permute-done | bytes 131104 | tf_op jit(solution)/shard_map/ppermute | solution.py:455
  102.6 4.2 %collective-permute-start.36 = (bf16[64,1024]{1,0:T(8,128)(2,1)S(1)}, bf16[64,1024]{1,0:T(8,128)(2,1)S(1)}, u32[]{:S(2)}, u32[]{:S(2)}) collective-permute-start(bf16[64,1024]{1,0:T(8,128)(2,1)S(1)} %get-tuple-element.86), channel_id=1, source_target_pairs={{0,28},{1,25},{2,30},{3,27},{4,16},{5,29},{6,18},{7,31},{8,20},{9,... | collective-permute-start | bytes 393224 | tf_op jit(solution)/shard_map/ppermute | solution.py:455
  106.9 2.5 %collective-permute-done.36.b0 = bf16[64,1024]{1,0:T(8,128)(2,1)S(1)} collective-permute-done((bf16[64,1024]{1,0:T(8,128)(2,1)S(1)}, bf16[64,1024]{1,0:T(8,128)(2,1)S(1)}, u32[]{:S(2)}, u32[]{:S(2)}) %collective-permute-start.36) | collective-permute-done | bytes 131104 | tf_op jit(solution)/shard_map/ppermute | solution.py:455
  109.4 5.1 %collective-permute-done.37.b1 = bf16[64,1024]{1,0:T(8,128)(2,1)S(1)} collective-permute-done((bf16[64,1024]{1,0:T(8,128)(2,1)S(1)}, bf16[64,1024]{1,0:T(8,128)(2,1)S(1)}, u32[]{:S(2)}, u32[]{:S(2)}) %collective-permute-start.37) | collective-permute-done | bytes 131104 | tf_op jit(solution)/shard_map/ppermute | solution.py:455
  114.7 1.3 %collective-permute-done.38.core = bf16[64,1024]{1,0:T(8,128)(2,1)S(1)} collective-permute-done((bf16[64,1024]{1,0:T(8,128)(2,1)S(1)}, bf16[64,1024]{1,0:T(8,128)(2,1)S(1)}, u32[]{:S(2)}, u32[]{:S(2)}) %collective-permute-start.38) | collective-permute-done | bytes 131104 | tf_op jit(solution)/shard_map/ppermute | solution.py:458
  116.0 0.8 closing.1
  (64 shorter events, 1.2 us)
Async XLA Ops:
  0.6 1.9 %copy-start = (bf16[1,1024,1536]{2,1,0:T(8,128)(2,1)S(1)}, bf16[1,1024,1536]{2,1,0:T(8,128)(2,1)}, u32[]{:S(2)}) copy-start(bf16[1,1024,1536]{2,1,0:T(8,128)(2,1)} %param.17) | copy-start | bytes 9437188
  2.5 4.7 %copy-start.4 = (bf16[1,32,2048]{2,1,0:T(8,128)(2,1)S(1)}, bf16[1,32,2048]{2,1,0:T(8,128)(2,1)}, u32[]{:S(2)}) copy-start(bf16[1,32,2048]{2,1,0:T(8,128)(2,1)} %param.11) | copy-start | bytes 393220
  2.5 7.9 %copy-start.3 = (bf16[1,64,2048]{2,1,0:T(8,128)(2,1)S(1)}, bf16[1,64,2048]{2,1,0:T(8,128)(2,1)}, u32[]{:S(2)}) copy-start(bf16[1,64,2048]{2,1,0:T(8,128)(2,1)} %param.10) | copy-start | bytes 786436
  2.7 38.3 %collective-permute-start.8 = (bf16[1024,768]{1,0:T(8,128)(2,1)S(1)}, bf16[1024,768]{1,0:T(8,128)(2,1)S(1)}, u32[]{:S(2)}, u32[]{:S(2)}) collective-permute-start(bf16[1024,768]{1,0:T(8,128)(2,1)S(1)} %weight_piece.3), channel_id=1, source_target_pairs={{0,16},{16,0},{1,17},{17,1},{2,18},{18,2},{3,19},{19,3},{4,20},{20... | collective-permute-start | bytes 4718600 | tf_op jit(solution)/shard_map/ppermute | solution.py:441
  5.7 13.7 %collective-permute-start.5 = (bf16[2048,128]{1,0:T(8,128)(2,1)}, bf16[2048,128]{1,0:T(8,128)(2,1)}, u32[]{:S(2)}, u32[]{:S(2)}) collective-permute-start(bf16[2048,128]{1,0:T(8,128)(2,1)} %w0.1), channel_id=1, source_target_pairs={{0,2},{1,3},{2,0},{3,1},{4,6},{5,7},{6,4},{7,5},{8,10},{9,11},{10,... | collective-permute-start | bytes 1572872 | tf_op jit(solution)/shard_map/ppermute | solution.py:458
  7.9 4.7 %copy-start.6 = (bf16[32,512]{1,0:T(8,128)(2,1)}, bf16[32,512]{1,0:T(8,128)(2,1)S(1)}, u32[]{:S(2)}) copy-start(bf16[32,512]{1,0:T(8,128)(2,1)S(1)} %get-tuple-element.49) | copy-start | bytes 98308
  7.9 11.6 %collective-permute-start.2 = (bf16[64,512]{1,0:T(8,128)(2,1)}, bf16[64,512]{1,0:T(8,128)(2,1)S(1)}, u32[]{:S(2)}, u32[]{:S(2)}) collective-permute-start(bf16[64,512]{1,0:T(8,128)(2,1)} %get-tuple-element.47), channel_id=1, source_target_pairs={{0,8},{1,9},{2,10},{3,11},{4,12},{5,13},{6,14},{7,15},{8,0},{9,1},... | collective-permute-start | bytes 196616 | tf_op jit(solution)/shard_map/ppermute | solution.py:461
  10.5 4.6 %copy-start.12 = (s32[1,32,8]{1,2,0:T(8,128)S(1)}, s32[1,32,8]{1,2,0:T(8,128)}, u32[]{:S(2)}) copy-start(s32[1,32,8]{1,2,0:T(8,128)} %param.14) | copy-start | bytes 3076
  10.5 14.9 %collective-permute-start.1 = (bf16[64,2048]{1,0:T(8,128)(2,1)S(1)}, bf16[64,2048]{1,0:T(8,128)(2,1)}, u32[]{:S(2)}, u32[]{:S(2)}) collective-permute-start(bf16[64,2048]{1,0:T(8,128)(2,1)S(1)} %bitcast.17), channel_id=1, source_target_pairs={{0,8},{1,9},{2,10},{3,11},{4,12},{5,13},{6,14},{7,15},{8,0},{9,1},... | collective-permute-start | bytes 786440 | tf_op jit(solution)/shard_map/ppermute | solution.py:461
  10.8 14.5 %collective-permute-start = (bf16[64,2048]{1,0:T(8,128)(2,1)S(1)}, bf16[64,2048]{1,0:T(8,128)(2,1)}, u32[]{:S(2)}, u32[]{:S(2)}) collective-permute-start(bf16[64,2048]{1,0:T(8,128)(2,1)S(1)} %bitcast.18), channel_id=1, source_target_pairs={{0,4},{1,5},{2,6},{3,7},{4,0},{5,1},{6,2},{7,3},{8,12},{9,13},{10,... | collective-permute-start | bytes 786440 | tf_op jit(solution)/shard_map/ppermute | solution.py:461
  12.6 1.0 copy-start.8
  13.6 0.8 copy-start.10
  19.4 15.4 %collective-permute-start.7 = (bf16[2048,128]{1,0:T(8,128)(2,1)}, bf16[2048,128]{1,0:T(8,128)(2,1)S(1)}, u32[]{:S(2)}, u32[]{:S(2)}) collective-permute-start(bf16[2048,128]{1,0:T(8,128)(2,1)} %collective-permute-done.5.w2), channel_id=1, source_target_pairs={{0,1},{1,0},{2,3},{3,2},{4,5},{5,4},{6,7},{7,6},{8,9},{9,8},{10,11... | collective-permute-start | bytes 1572872 | tf_op jit(solution)/shard_map/ppermute | solution.py:458
  19.5 15.4 %collective-permute-start.6 = (bf16[2048,128]{1,0:T(8,128)(2,1)}, bf16[2048,128]{1,0:T(8,128)(2,1)S(1)}, u32[]{:S(2)}, u32[]{:S(2)}) collective-permute-start(bf16[2048,128]{1,0:T(8,128)(2,1)} %w0.1), channel_id=1, source_target_pairs={{0,1},{1,0},{2,3},{3,2},{4,5},{5,4},{6,7},{7,6},{8,9},{9,8},{10,11... | collective-permute-start | bytes 1572872 | tf_op jit(solution)/shard_map/ppermute | solution.py:458
  25.4 9.5 %collective-permute-start.3 = (bf16[64,2048]{1,0:T(8,128)(2,1)}, bf16[64,2048]{1,0:T(8,128)(2,1)S(1)}, u32[]{:S(2)}, u32[]{:S(2)}) collective-permute-start(bf16[64,2048]{1,0:T(8,128)(2,1)} %collective-permute-done.1.a2), channel_id=1, source_target_pairs={{0,4},{1,5},{2,6},{3,7},{4,0},{5,1},{6,2},{7,3},{8,12},{9,13},{10,... | collective-permute-start | bytes 786440 | tf_op jit(solution)/shard_map/ppermute | solution.py:461
  26.3 12.0 %copy-start.9 = (bf16[640,768]{1,0:T(8,128)(2,1)S(1)}, bf16[640,768]{1,0:T(8,128)(2,1)}, u32[]{:S(2)}) copy-start(bf16[640,768]{1,0:T(8,128)(2,1)} %copy-done.8) | copy-start | bytes 2949124
  26.3 35.6 %copy-start.11 = (bf16[384,768]{1,0:T(8,128)(2,1)S(1)}, bf16[384,768]{1,0:T(8,128)(2,1)}, u32[]{:S(2)}) copy-start(bf16[384,768]{1,0:T(8,128)(2,1)} %copy-done.10) | copy-start | bytes 1769476
  26.4 36.7 %copy-start.5 = (f32[2048]{0:T(1024)S(1)}, f32[2048]{0:T(1024)}, u32[]{:S(2)}) copy-start(f32[2048]{0:T(1024)} %param.13) | copy-start | bytes 24580
  26.4 8.5 %collective-permute-start.4 = (bf16[64,512]{1,0:T(8,128)(2,1)S(1)}, bf16[64,512]{1,0:T(8,128)(2,1)S(1)}, u32[]{:S(2)}, u32[]{:S(2)}) collective-permute-start(bf16[64,512]{1,0:T(8,128)(2,1)S(1)} %pad_maximum_fusion), channel_id=1, source_target_pairs={{0,4},{1,5},{2,6},{3,7},{4,0},{5,1},{6,2},{7,3},{8,12},{9,13},{10,... | collective-permute-start | bytes 196616 | tf_op jit(solution)/shard_map/ppermute | solution.py:461
  34.9 35.2 %copy-start.1 = (bf16[1,1024,1536]{2,1,0:T(8,128)(2,1)S(1)}, bf16[1,1024,1536]{2,1,0:T(8,128)(2,1)}, u32[]{:S(2)}) copy-start(bf16[1,1024,1536]{2,1,0:T(8,128)(2,1)} %param.17) | copy-start | bytes 9437188
  37.8 6.5 %collective-permute-start.9 = (bf16[128,512]{1,0:T(8,128)(2,1)S(1)}, bf16[128,512]{1,0:T(8,128)(2,1)S(1)}, u32[]{:S(2)}, u32[]{:S(2)}) collective-permute-start(bf16[128,512]{1,0:T(8,128)(2,1)S(1)} %get-tuple-element.56), channel_id=1, source_target_pairs={{0,16},{16,0},{1,17},{17,1},{2,18},{18,2},{3,19},{19,3},{4,20},{20... | collective-permute-start | bytes 393224 | tf_op jit(solution)/shard_map/ppermute | solution.py:441
  38.3 38.7 %collective-permute-start.19 = (bf16[640,768]{1,0:T(8,128)(2,1)S(1)}, bf16[640,768]{1,0:T(8,128)(2,1)S(1)}, u32[]{:S(2)}, u32[]{:S(2)}) collective-permute-start(bf16[640,768]{1,0:T(8,128)(2,1)S(1)} %copy-done.9), channel_id=1, source_target_pairs={{0,16},{16,0},{1,17},{17,1},{2,18},{18,2},{3,19},{19,3},{4,20},{20... | collective-permute-start | bytes 2949128 | tf_op jit(solution)/shard_map/ppermute | solution.py:441
  44.3 7.8 %collective-permute-start.12 = (bf16[144,512]{1,0:T(8,128)(2,1)S(1)}, bf16[144,512]{1,0:T(8,128)(2,1)S(1)}, u32[]{:S(2)}, u32[]{:S(2)}) collective-permute-start(bf16[144,512]{1,0:T(8,128)(2,1)S(1)} %stream.1.b0), channel_id=1, source_target_pairs={{0,12},{1,13},{2,14},{3,15},{4,0},{5,1},{6,2},{7,3},{8,4},{9,5},{1... | collective-permute-start | bytes 442376 | tf_op jit(solution)/shard_map/ppermute | solution.py:444
  47.8 12.0 %collective-permute-start.11 = (bf16[144,512]{1,0:T(8,128)(2,1)S(1)}, bf16[144,512]{1,0:T(8,128)(2,1)S(1)}, u32[]{:S(2)}, u32[]{:S(2)}) collective-permute-start(bf16[144,512]{1,0:T(8,128)(2,1)S(1)} %stream.1.b0), channel_id=1, source_target_pairs={{0,8},{1,9},{2,10},{3,11},{4,12},{5,13},{6,14},{7,15},{8,0},{9,1},... | collective-permute-start | bytes 442376 | tf_op jit(solution)/shard_map/ppermute | solution.py:444
  47.8 13.2 %collective-permute-start.10 = (bf16[144,512]{1,0:T(8,128)(2,1)S(1)}, bf16[144,512]{1,0:T(8,128)(2,1)S(1)}, u32[]{:S(2)}, u32[]{:S(2)}) collective-permute-start(bf16[144,512]{1,0:T(8,128)(2,1)S(1)} %stream.1.b0), channel_id=1, source_target_pairs={{0,4},{1,5},{2,6},{3,7},{4,8},{5,9},{6,10},{7,11},{8,12},{9,13},{1... | collective-permute-start | bytes 442376 | tf_op jit(solution)/shard_map/ppermute | solution.py:444
  48.7 13.2 %collective-permute-start.13 = (bf16[144,512]{1,0:T(8,128)(2,1)S(1)}, bf16[144,512]{1,0:T(8,128)(2,1)S(1)}, u32[]{:S(2)}, u32[]{:S(2)}) collective-permute-start(bf16[144,512]{1,0:T(8,128)(2,1)S(1)} %stream.1.b0), channel_id=1, source_target_pairs={{0,2},{1,3},{2,0},{3,1},{4,6},{5,7},{6,4},{7,5},{8,10},{9,11},{10,... | collective-permute-start | bytes 442376 | tf_op jit(solution)/shard_map/ppermute | solution.py:458
  52.1 11.3 %collective-permute-start.16 = (bf16[144,512]{1,0:T(8,128)(2,1)S(1)}, bf16[144,512]{1,0:T(8,128)(2,1)S(1)}, u32[]{:S(2)}, u32[]{:S(2)}) collective-permute-start(bf16[144,512]{1,0:T(8,128)(2,1)S(1)} %collective-permute-done.12.b3), channel_id=1, source_target_pairs={{0,2},{1,3},{2,0},{3,1},{4,6},{5,7},{6,4},{7,5},{8,10},{9,11},{10,... | collective-permute-start | bytes 442376 | tf_op jit(solution)/shard_map/ppermute | solution.py:458
  59.9 5.9 %collective-permute-start.15 = (bf16[144,512]{1,0:T(8,128)(2,1)S(1)}, bf16[144,512]{1,0:T(8,128)(2,1)S(1)}, u32[]{:S(2)}, u32[]{:S(2)}) collective-permute-start(bf16[144,512]{1,0:T(8,128)(2,1)S(1)} %collective-permute-done.11.b2), channel_id=1, source_target_pairs={{0,2},{1,3},{2,0},{3,1},{4,6},{5,7},{6,4},{7,5},{8,10},{9,11},{10,... | collective-permute-start | bytes 442376 | tf_op jit(solution)/shard_map/ppermute | solution.py:458
  61.0 6.3 %collective-permute-start.14 = (bf16[144,512]{1,0:T(8,128)(2,1)S(1)}, bf16[144,512]{1,0:T(8,128)(2,1)S(1)}, u32[]{:S(2)}, u32[]{:S(2)}) collective-permute-start(bf16[144,512]{1,0:T(8,128)(2,1)S(1)} %collective-permute-done.10.b1), channel_id=1, source_target_pairs={{0,2},{1,3},{2,0},{3,1},{4,6},{5,7},{6,4},{7,5},{8,10},{9,11},{10,... | collective-permute-start | bytes 442376 | tf_op jit(solution)/shard_map/ppermute | solution.py:458
  61.9 15.1 %collective-permute-start.20 = (bf16[384,768]{1,0:T(8,128)(2,1)S(1)}, bf16[384,768]{1,0:T(8,128)(2,1)S(1)}, u32[]{:S(2)}, u32[]{:S(2)}) collective-permute-start(bf16[384,768]{1,0:T(8,128)(2,1)S(1)} %copy-done.11), channel_id=1, source_target_pairs={{0,16},{16,0},{1,17},{17,1},{2,18},{18,2},{3,19},{19,3},{4,20},{20... | collective-permute-start | bytes 1769480 | tf_op jit(solution)/shard_map/ppermute | solution.py:441
  63.4 4.7 %collective-permute-start.18 = (bf16[128,2176]{1,0:T(8,128)(2,1)S(1)}, bf16[128,2176]{1,0:T(8,128)(2,1)S(1)}, u32[]{:S(2)}, u32[]{:S(2)}) collective-permute-start(bf16[128,2176]{1,0:T(8,128)(2,1)S(1)} %get-tuple-element.60.group), channel_id=1, source_target_pairs={{0,1},{1,0},{2,3},{3,2},{4,5},{5,4},{6,7},{7,6},{8,9},{9,8},{10,11... | collective-permute-start | bytes 1671176 | tf_op jit(solution)/shard_map/ppermute | solution.py:458
  68.1 2.0 %collective-permute-start.17 = (bf16[128,2176]{1,0:T(8,128)(2,1)S(1)}, bf16[128,2176]{1,0:T(8,128)(2,1)S(1)}, u32[]{:S(2)}, u32[]{:S(2)}) collective-permute-start(bf16[128,2176]{1,0:T(8,128)(2,1)S(1)} %get-tuple-element.59.group_x), channel_id=1, source_target_pairs={{0,1},{1,0},{2,3},{3,2},{4,5},{5,4},{6,7},{7,6},{8,9},{9,8},{10,11... | collective-permute-start | bytes 1671176 | tf_op jit(solution)/shard_map/ppermute | solution.py:458
  73.5 13.8 %collective-permute-start.28 = (bf16[384,384]{1,0:T(8,128)(2,1)S(1)}, bf16[384,384]{1,0:T(8,128)(2,1)S(1)}, u32[]{:S(2)}, u32[]{:S(2)}) collective-permute-start(bf16[384,384]{1,0:T(8,128)(2,1)S(1)} %get-tuple-element.61.first), channel_id=1, source_target_pairs={{0,16},{16,0},{1,17},{17,1},{2,18},{18,2},{3,19},{19,3},{4,20},{20... | collective-permute-start | bytes 884744 | tf_op jit(solution)/shard_map/ppermute | solution.py:441
  77.1 1.5 %copy-start.2 = (bf16[1,768,1024]{2,1,0:T(8,128)(2,1)S(1)}, bf16[1,768,1024]{2,1,0:T(8,128)(2,1)}, u32[]{:S(2)}) copy-start(bf16[1,768,1024]{2,1,0:T(8,128)(2,1)} %param.18) | copy-start | bytes 4718596
  79.1 3.1 %collective-permute-start.21 = (bf16[128,512]{1,0:T(8,128)(2,1)S(1)}, bf16[128,512]{1,0:T(8,128)(2,1)S(1)}, u32[]{:S(2)}, u32[]{:S(2)}) collective-permute-start(bf16[128,512]{1,0:T(8,128)(2,1)S(1)} %get-tuple-element.70), channel_id=1, source_target_pairs={{0,1},{1,0},{2,3},{3,2},{4,5},{5,4},{6,7},{7,6},{8,9},{9,8},{10,11... | collective-permute-start | bytes 393224 | tf_op jit(solution)/shard_map/ppermute | solution.py:458
  79.2 3.0 %collective-permute-start.22 = (bf16[128,512]{1,0:T(8,128)(2,1)S(1)}, bf16[128,512]{1,0:T(8,128)(2,1)S(1)}, u32[]{:S(2)}, u32[]{:S(2)}) collective-permute-start(bf16[128,512]{1,0:T(8,128)(2,1)S(1)} %get-tuple-element.71), channel_id=1, source_target_pairs={{0,1},{1,0},{2,3},{3,2},{4,5},{5,4},{6,7},{7,6},{8,9},{9,8},{10,11... | collective-permute-start | bytes 393224 | tf_op jit(solution)/shard_map/ppermute | solution.py:458
  79.7 7.6 %collective-permute-start.29 = (bf16[256,384]{1,0:T(8,128)(2,1)S(1)}, bf16[256,384]{1,0:T(8,128)(2,1)S(1)}, u32[]{:S(2)}, u32[]{:S(2)}) collective-permute-start(bf16[256,384]{1,0:T(8,128)(2,1)S(1)} %get-tuple-element.68.far), channel_id=1, source_target_pairs={{0,16},{16,0},{1,17},{17,1},{2,18},{18,2},{3,19},{19,3},{4,20},{20... | collective-permute-start | bytes 589832 | tf_op jit(solution)/shard_map/ppermute | solution.py:441
  82.3 8.1 %collective-permute-start.23 = (bf16[128,1024]{1,0:T(8,128)(2,1)S(1)}, bf16[128,1024]{1,0:T(8,128)(2,1)S(1)}, u32[]{:S(2)}, u32[]{:S(2)}) collective-permute-start(bf16[128,1024]{1,0:T(8,128)(2,1)S(1)} %fold.2), channel_id=1, source_target_pairs={{0,2},{1,3},{2,0},{3,1},{4,6},{5,7},{6,4},{7,5},{8,10},{9,11},{10,... | collective-permute-start | bytes 786440 | tf_op jit(solution)/shard_map/ppermute | solution.py:458
  84.4 4.1 %collective-permute-start.24 = (bf16[128,512]{1,0:T(8,128)(2,1)S(1)}, bf16[128,512]{1,0:T(8,128)(2,1)S(1)}, u32[]{:S(2)}, u32[]{:S(2)}) collective-permute-start(bf16[128,512]{1,0:T(8,128)(2,1)S(1)} %get-tuple-element.74), channel_id=1, source_target_pairs={{0,1},{1,0},{2,3},{3,2},{4,5},{5,4},{6,7},{7,6},{8,9},{9,8},{10,11... | collective-permute-start | bytes 393224 | tf_op jit(solution)/shard_map/ppermute | solution.py:458
  84.5 13.9 %collective-permute-start.33 = (bf16[384,384]{1,0:T(8,128)(2,1)S(1)}, bf16[384,384]{1,0:T(8,128)(2,1)S(1)}, u32[]{:S(2)}, u32[]{:S(2)}) collective-permute-start(bf16[384,384]{1,0:T(8,128)(2,1)S(1)} %get-tuple-element.72.rest), channel_id=1, source_target_pairs={{0,16},{16,0},{1,17},{17,1},{2,18},{18,2},{3,19},{19,3},{4,20},{20... | collective-permute-start | bytes 884744 | tf_op jit(solution)/shard_map/ppermute | solution.py:441
  87.3 1.3 %collective-permute-start.25 = (bf16[128,512]{1,0:T(8,128)(2,1)S(1)}, bf16[128,512]{1,0:T(8,128)(2,1)S(1)}, u32[]{:S(2)}, u32[]{:S(2)}) collective-permute-start(bf16[128,512]{1,0:T(8,128)(2,1)S(1)} %get-tuple-element.75), channel_id=1, source_target_pairs={{0,1},{1,0},{2,3},{3,2},{4,5},{5,4},{6,7},{7,6},{8,9},{9,8},{10,11... | collective-permute-start | bytes 393224 | tf_op jit(solution)/shard_map/ppermute | solution.py:458
  87.9 2.5 %collective-permute-start.30 = (bf16[128,512]{1,0:T(8,128)(2,1)S(1)}, bf16[128,512]{1,0:T(8,128)(2,1)S(1)}, u32[]{:S(2)}, u32[]{:S(2)}) collective-permute-start(bf16[128,512]{1,0:T(8,128)(2,1)S(1)} %get-tuple-element.80), channel_id=1, source_target_pairs={{0,1},{1,0},{2,3},{3,2},{4,5},{5,4},{6,7},{7,6},{8,9},{9,8},{10,11... | collective-permute-start | bytes 393224 | tf_op jit(solution)/shard_map/ppermute | solution.py:458
  88.5 2.0 %collective-permute-start.31 = (bf16[128,512]{1,0:T(8,128)(2,1)S(1)}, bf16[128,512]{1,0:T(8,128)(2,1)S(1)}, u32[]{:S(2)}, u32[]{:S(2)}) collective-permute-start(bf16[128,512]{1,0:T(8,128)(2,1)S(1)} %get-tuple-element.81), channel_id=1, source_target_pairs={{0,1},{1,0},{2,3},{3,2},{4,5},{5,4},{6,7},{7,6},{8,9},{9,8},{10,11... | collective-permute-start | bytes 393224 | tf_op jit(solution)/shard_map/ppermute | solution.py:458
  90.5 12.0 %collective-permute-start.32 = (bf16[128,1024]{1,0:T(8,128)(2,1)S(1)}, bf16[128,1024]{1,0:T(8,128)(2,1)S(1)}, u32[]{:S(2)}, u32[]{:S(2)}) collective-permute-start(bf16[128,1024]{1,0:T(8,128)(2,1)S(1)} %fold.3), channel_id=1, source_target_pairs={{0,2},{1,3},{2,0},{3,1},{4,6},{5,7},{6,4},{7,5},{8,10},{9,11},{10,... | collective-permute-start | bytes 786440 | tf_op jit(solution)/shard_map/ppermute | solution.py:458
  92.6 9.9 %collective-permute-start.27 = (bf16[64,1024]{1,0:T(8,128)(2,1)S(1)}, bf16[64,1024]{1,0:T(8,128)(2,1)S(1)}, u32[]{:S(2)}, u32[]{:S(2)}) collective-permute-start(bf16[64,1024]{1,0:T(8,128)(2,1)S(1)} %get-tuple-element.76.own), channel_id=1, source_target_pairs={{0,4},{2,6},{4,8},{6,10},{8,12},{10,14},{12,0},{14,2},{16,20},{18,... | collective-permute-start | bytes 393224 | tf_op jit(solution)/shard_map/ppermute | solution.py:455
  96.1 20.0 %copy-start.7 = (f32[2048]{0:T(1024)S(1)}, f32[2048]{0:T(1024)}, u32[]{:S(2)}) copy-start(f32[2048]{0:T(1024)} %param.19) | copy-start | bytes 24580
  96.1 6.4 %collective-permute-start.26 = (bf16[64,1024]{1,0:T(8,128)(2,1)S(1)}, bf16[64,1024]{1,0:T(8,128)(2,1)S(1)}, u32[]{:S(2)}, u32[]{:S(2)}) collective-permute-start(bf16[64,1024]{1,0:T(8,128)(2,1)S(1)} %get-tuple-element.77), channel_id=1, source_target_pairs={{0,12},{1,9},{2,14},{3,11},{4,0},{5,13},{6,2},{7,15},{8,4},{9,1},{... | collective-permute-start | bytes 393224 | tf_op jit(solution)/shard_map/ppermute | solution.py:455
  99.0 3.5 %collective-permute-start.34 = (bf16[128,512]{1,0:T(8,128)(2,1)S(1)}, bf16[128,512]{1,0:T(8,128)(2,1)S(1)}, u32[]{:S(2)}, u32[]{:S(2)}) collective-permute-start(bf16[128,512]{1,0:T(8,128)(2,1)S(1)} %get-tuple-element.84), channel_id=1, source_target_pairs={{0,1},{1,0},{2,3},{3,2},{4,5},{5,4},{6,7},{7,6},{8,9},{9,8},{10,11... | collective-permute-start | bytes 393224 | tf_op jit(solution)/shard_map/ppermute | solution.py:458
  99.0 3.5 %collective-permute-start.35 = (bf16[128,512]{1,0:T(8,128)(2,1)S(1)}, bf16[128,512]{1,0:T(8,128)(2,1)S(1)}, u32[]{:S(2)}, u32[]{:S(2)}) collective-permute-start(bf16[128,512]{1,0:T(8,128)(2,1)S(1)} %get-tuple-element.85), channel_id=1, source_target_pairs={{0,1},{1,0},{2,3},{3,2},{4,5},{5,4},{6,7},{7,6},{8,9},{9,8},{10,11... | collective-permute-start | bytes 393224 | tf_op jit(solution)/shard_map/ppermute | solution.py:458
  102.6 6.8 %collective-permute-start.36 = (bf16[64,1024]{1,0:T(8,128)(2,1)S(1)}, bf16[64,1024]{1,0:T(8,128)(2,1)S(1)}, u32[]{:S(2)}, u32[]{:S(2)}) collective-permute-start(bf16[64,1024]{1,0:T(8,128)(2,1)S(1)} %get-tuple-element.86), channel_id=1, source_target_pairs={{0,28},{1,25},{2,30},{3,27},{4,16},{5,29},{6,18},{7,31},{8,20},{9,... | collective-permute-start | bytes 393224 | tf_op jit(solution)/shard_map/ppermute | solution.py:455
  106.9 7.7 %collective-permute-start.37 = (bf16[64,1024]{1,0:T(8,128)(2,1)S(1)}, bf16[64,1024]{1,0:T(8,128)(2,1)S(1)}, u32[]{:S(2)}, u32[]{:S(2)}) collective-permute-start(bf16[64,1024]{1,0:T(8,128)(2,1)S(1)} %get-tuple-element.87), channel_id=1, source_target_pairs={{0,20},{1,17},{2,22},{3,19},{4,24},{5,21},{6,26},{7,23},{8,28},{9,... | collective-permute-start | bytes 393224 | tf_op jit(solution)/shard_map/ppermute | solution.py:455
  114.6 1.4 %collective-permute-start.38 = (bf16[64,1024]{1,0:T(8,128)(2,1)S(1)}, bf16[64,1024]{1,0:T(8,128)(2,1)S(1)}, u32[]{:S(2)}, u32[]{:S(2)}) collective-permute-start(bf16[64,1024]{1,0:T(8,128)(2,1)S(1)} %get-tuple-element.89), channel_id=1, source_target_pairs={{0,1},{1,0},{2,3},{3,2},{4,5},{5,4},{6,7},{7,6},{8,9},{9,8},{10,11... | collective-permute-start | bytes 393224 | tf_op jit(solution)/shard_map/ppermute | solution.py:458

commit v16 on v14

--- a/solution.py
+++ b/solution.py
@@ -254,7 +254,7 @@
     share = jnp.zeros((experts, count), F32)
     for s, b in enumerate((b0, b1, b2, b3)):
         value = b[0:count, :]
-        group_ref[:, aligned((outer + 4 - s) & 3, width)] = value
+        group_ref[:, aligned(outer ^ s, width)] = value
         value = value.astype(F32)
         square = square + jnp.sum(value * value, axis=1, keepdims=True)
         share = share + b[count : count + experts, 0:count].astype(F32)
@@ -327,11 +327,11 @@
         for i in range(2):
             for j in range(2):
                 ref, start = places[j]
-                kept = aligned(start // small + ((outer + 2 * core + i) & 3), small)
+                kept = aligned(start // small + (outer ^ (2 * core + i)), small)
                 at = (2 * i + j) * small
                 rows[at : at + small, cols] = ref[kept, :]
                 ref, start = places[1 - j]
-                sent = aligned(start // small + ((outer + 2 - 2 * core + i) & 3), small)
+                sent = aligned(start // small + (outer ^ (2 - 2 * core + i)), small)
                 rows[count + at : count + at + small, cols] = ref[sent, :]
     for at in range(0, wd.shape[1], 256):
         value = dot(rows[...], wd[:, at : at + 256]).astype(BF16)
@@ -447,18 +447,13 @@
     def swap_dp(x):
         return lax.ppermute(x, "dp", [(0, 1), (1, 0)])
 
-    def shift_outer(x, s):
-        return lax.ppermute(
-            x, "expert", [(i, (i + 4 * s) % expert_count) for i in range(expert_count)]
-        )
-
     def send_outer(x, i, cross):
         pairs = []
         for at in range(2 * expert_count):
             d, e = divmod(at, expert_count)
             step = 2 * (e % 2) + i
             if step or cross:
-                pairs.append((at, (d ^ cross) * expert_count + (e + 4 * step) % expert_count))
+                pairs.append((at, (d ^ cross) * expert_count + (e ^ (4 * step))))
         return lax.ppermute(x, ("dp", "expert"), pairs)
 
     def swap_inner(x, j):
@@ -544,7 +539,7 @@
         outs = (shape_of(4 * rows_here, model_width + 128), shape_of(rows_here, model_width))
         return call(norm_kernel, "norm", 8, outs, b0, b1, b2, b3, gain_post[None])
 
-    blocks = [block] + [shift_outer(block, s) for s in (1, 2, 3)]
+    blocks = [block] + [swap_outer(block, s) for s in (1, 2, 3)]
     group, stream_own = norm(*blocks)
     blocks_x = [swap_inner(b, 2) for b in blocks]
     group_x, unused = norm(*blocks_x)

time: 115 us -> 116 us (level)
  starting transfers between devices: 41.7 us -> 48 us
  waiting for transfers between devices: 52.5 us -> 47.3 us
    ppermute x3 -> x0, waiting for transfers between devices: 7.64 us -> none  [shift_outer(): lax.ppermute(x, 'expert', [(i, (i + 4 * s) % expert_count) for i in range...]
    ppermute x5 -> x8, waiting for transfers between devices: 12.1 us -> 19.2 us  [swap_outer(): lax.ppermute(x, 'expert', [(i, i ^ 4 * s) for i in range(expert_count)])]
    ppermute x20, starting transfers between devices: 15.6 us -> 21.2 us  [swap_inner(): return lax.ppermute(x, 'expert', [(i, i ^ j) for i in range(expert_count)])]
    ppermute x4, waiting for transfers between devices: 11.4 us -> 6.02 us  [send_outer(): return lax.ppermute(x, ('dp', 'expert'), pairs)]
    ppermute x5 -> x8, starting transfers between devices: 6.59 us -> 11 us  [swap_outer(): lax.ppermute(x, 'expert', [(i, i ^ 4 * s) for i in range(expert_count)])]
    ppermute x3 -> x0, starting transfers between devices: 4.36 us -> none  [shift_outer(): lax.ppermute(x, 'expert', [(i, (i + 4 * s) % expert_count) for i in range...]
  transfers between devices with their start and end apart: 39 -> 39, of which waited for: 18 -> 19; matrix products, arithmetic and copies ran while one was open for 1% -> 1% of each run, Pallas kernels for 11% -> 11%
where the time goes in v16:
time: 116 us
  starting transfers between devices  48 us (41%)
  waiting for transfers between devices  47.3 us (41%)
  Pallas kernels  13.9 us (12%)
  local copies, waits for them, and re-layouts  4.58 us (4%)
  between operations  1.54 us (1%)
    ppermute x20, starting transfers between devices, swap_inner(): return lax.ppermute(x, 'expert', [(i, i ^ j) for i in range(expert_count)])  21.2 us
    ppermute x8, waiting for transfers between devices, swap_outer(): lax.ppermute(x, 'expert', [(i, i ^ 4 * s) for i in range(expert_count)])  19.2 us
    pallas_call x17, Pallas kernels, call(): pl.pallas_call(kernel, out_shape=outs, in_specs=[first] + [vmem] * (len(a...  13.5 us
    ppermute x20, waiting for transfers between devices, swap_inner(): return lax.ppermute(x, 'expert', [(i, i ^ j) for i in range(expert_count)])  11.9 us
    ppermute x8, starting transfers between devices, swap_outer(): lax.ppermute(x, 'expert', [(i, i ^ 4 * s) for i in range(expert_count)])  11 us
    ppermute x7, starting transfers between devices, swap_dp(): return lax.ppermute(x, 'dp', [(0, 1), (1, 0)])  11 us
    ppermute x7, waiting for transfers between devices, swap_dp(): return lax.ppermute(x, 'dp', [(0, 1), (1, 0)])  10.3 us
    ppermute x4, waiting for transfers between devices, send_outer(): return lax.ppermute(x, ('dp', 'expert'), pairs)  6.02 us
  transfers between devices with their start and end apart: 39, of which 19 were waited for; matrix products, arithmetic and copies ran while one was open for 1% of the time, Pallas kernels for 11%

profile of v16, /device:TPU:0, one launch (start us, length us, event | category | flops | bytes accessed | tf_op | source)
XLA Modules:
  0.0 116.1 jit_solution(11082904483037505489)
XLA Ops:
  0.6 1.9 %copy-done = bf16[1,1024,1536]{2,1,0:T(8,128)(2,1)S(1)} copy-done((bf16[1,1024,1536]{2,1,0:T(8,128)(2,1)S(1)}, bf16[1,1024,1536]{2,1,0:T(8,128)(2,1)}, u32[]{:S(2)}) %copy-start) | copy-done | bytes 3145752
  2.7 3.0 %collective-permute-start.8 = (bf16[1024,768]{1,0:T(8,128)(2,1)S(1)}, bf16[1024,768]{1,0:T(8,128)(2,1)S(1)}, u32[]{:S(2)}, u32[]{:S(2)}) collective-permute-start(bf16[1024,768]{1,0:T(8,128)(2,1)S(1)} %weight_piece.3), channel_id=1, source_target_pairs={{0,16},{16,0},{1,17},{17,1},{2,18},{18,2},{3,19},{19,3},{4,20},{20... | collective-permute-start | bytes 4718600 | tf_op jit(solution)/shard_map/ppermute | solution.py:448
  5.7 1.5 %collective-permute-start.5 = (bf16[2048,128]{1,0:T(8,128)(2,1)}, bf16[2048,128]{1,0:T(8,128)(2,1)}, u32[]{:S(2)}, u32[]{:S(2)}) collective-permute-start(bf16[2048,128]{1,0:T(8,128)(2,1)} %w0.1), channel_id=1, source_target_pairs={{0,2},{1,3},{2,0},{3,1},{4,6},{5,7},{6,4},{7,5},{8,10},{9,11},{10,... | collective-permute-start | bytes 1572872 | tf_op jit(solution)/shard_map/ppermute | solution.py:460
  7.2 0.6 cut_resid.1
  7.9 2.6 %collective-permute-start.2 = (bf16[64,512]{1,0:T(8,128)(2,1)}, bf16[64,512]{1,0:T(8,128)(2,1)S(1)}, u32[]{:S(2)}, u32[]{:S(2)}) collective-permute-start(bf16[64,512]{1,0:T(8,128)(2,1)} %get-tuple-element.47), channel_id=1, source_target_pairs={{0,8},{1,9},{2,10},{3,11},{4,12},{5,13},{6,14},{7,15},{8,0},{9,1},... | collective-permute-start | bytes 196616 | tf_op jit(solution)/shard_map/ppermute | solution.py:463
  10.5 0.3 collective-permute-start.1
  10.8 1.6 %collective-permute-start = (bf16[64,2048]{1,0:T(8,128)(2,1)S(1)}, bf16[64,2048]{1,0:T(8,128)(2,1)}, u32[]{:S(2)}, u32[]{:S(2)}) collective-permute-start(bf16[64,2048]{1,0:T(8,128)(2,1)S(1)} %bitcast.17), channel_id=1, source_target_pairs={{0,4},{1,5},{2,6},{3,7},{4,0},{5,1},{6,2},{7,3},{8,12},{9,13},{10,... | collective-permute-start | bytes 786440 | tf_op jit(solution)/shard_map/ppermute | solution.py:463
  12.6 1.0 copy-done.8
  13.6 0.8 copy-done.10
  15.2 0.8 copy.13
  15.9 0.4 share.1
  16.4 3.1 %collective-permute-done.5.w2 = bf16[2048,128]{1,0:T(8,128)(2,1)} collective-permute-done((bf16[2048,128]{1,0:T(8,128)(2,1)}, bf16[2048,128]{1,0:T(8,128)(2,1)}, u32[]{:S(2)}, u32[]{:S(2)}) %collective-permute-start.5) | collective-permute-done | bytes 524320 | tf_op jit(solution)/shard_map/ppermute | solution.py:460
  19.5 0.5 collective-permute-start.6
  20.0 5.4 %collective-permute-done.1.a2 = bf16[64,2048]{1,0:T(8,128)(2,1)} collective-permute-done((bf16[64,2048]{1,0:T(8,128)(2,1)S(1)}, bf16[64,2048]{1,0:T(8,128)(2,1)}, u32[]{:S(2)}, u32[]{:S(2)}) %collective-permute-start.1) | collective-permute-done | bytes 262176 | tf_op jit(solution)/shard_map/ppermute | solution.py:463
  25.4 0.2 collective-permute-start.3
  25.6 0.8 pad_maximum_fusion
  26.4 1.9 %collective-permute-start.4 = (bf16[64,512]{1,0:T(8,128)(2,1)S(1)}, bf16[64,512]{1,0:T(8,128)(2,1)S(1)}, u32[]{:S(2)}, u32[]{:S(2)}) collective-permute-start(bf16[64,512]{1,0:T(8,128)(2,1)S(1)} %pad_maximum_fusion), channel_id=1, source_target_pairs={{0,4},{1,5},{2,6},{3,7},{4,0},{5,1},{6,2},{7,3},{8,12},{9,13},{10,... | collective-permute-start | bytes 196616 | tf_op jit(solution)/shard_map/ppermute | solution.py:463
  28.2 6.7 %collective-permute-done.4.r13 = bf16[64,512]{1,0:T(8,128)(2,1)S(1)} collective-permute-done((bf16[64,512]{1,0:T(8,128)(2,1)S(1)}, bf16[64,512]{1,0:T(8,128)(2,1)S(1)}, u32[]{:S(2)}, u32[]{:S(2)}) %collective-permute-start.4) | collective-permute-done | bytes 65568 | tf_op jit(solution)/shard_map/ppermute | solution.py:463
  34.9 2.8 %projection.1 = (bf16[128,512]{1,0:T(8,128)(2,1)S(1)}, bf16[128,512]{1,0:T(8,128)(2,1)S(1)}) custom-call(bf16[64,2048]{1,0:T(8,128)(2,1)S(1)} %bitcast.18, bf16[64,2048]{1,0:T(8,128)(2,1)} %collective-permute-done.a1, bf16[64,2048]{1,0:T(8,128)(2,1)} %collective-permute-done.1.a2, bf16[64,2048]{1,0:T(8,128)(2,1)S(1)} %collective-permute-done.3.a3, ...), custom_call_target="tpu_custom_call" | custom-call | flops 1 | bytes 1 | tf_op jit(solution)/shard_map/projection/pallas_call | solution.py:436
  37.8 0.6 collective-permute-start.9
  38.3 1.5 %collective-permute-start.19 = (bf16[640,768]{1,0:T(8,128)(2,1)S(1)}, bf16[640,768]{1,0:T(8,128)(2,1)S(1)}, u32[]{:S(2)}, u32[]{:S(2)}) collective-permute-start(bf16[640,768]{1,0:T(8,128)(2,1)S(1)} %copy-done.9), channel_id=1, source_target_pairs={{0,16},{16,0},{1,17},{17,1},{2,18},{18,2},{3,19},{19,3},{4,20},{20... | collective-permute-start | bytes 2949128 | tf_op jit(solution)/shard_map/ppermute | solution.py:448
  39.9 1.1 collective-permute-done.8.early
  41.0 3.3 %collective-permute-done.9.arrived = bf16[128,512]{1,0:T(8,128)(2,1)S(1)} collective-permute-done((bf16[128,512]{1,0:T(8,128)(2,1)S(1)}, bf16[128,512]{1,0:T(8,128)(2,1)S(1)}, u32[]{:S(2)}, u32[]{:S(2)}) %collective-permute-start.9) | collective-permute-done | bytes 131104 | tf_op jit(solution)/shard_map/ppermute | solution.py:448
  44.3 3.5 %collective-permute-start.12 = (bf16[144,512]{1,0:T(8,128)(2,1)S(1)}, bf16[144,512]{1,0:T(8,128)(2,1)S(1)}, u32[]{:S(2)}, u32[]{:S(2)}) collective-permute-start(bf16[144,512]{1,0:T(8,128)(2,1)S(1)} %stream.1.b0), channel_id=1, source_target_pairs={{0,12},{1,13},{2,14},{3,15},{4,8},{5,9},{6,10},{7,11},{8,4},{9,5},... | collective-permute-start | bytes 442376 | tf_op jit(solution)/shard_map/ppermute | solution.py:463
  47.9 0.9 collective-permute-start.10
  48.8 1.6 %collective-permute-start.13 = (bf16[144,512]{1,0:T(8,128)(2,1)S(1)}, bf16[144,512]{1,0:T(8,128)(2,1)S(1)}, u32[]{:S(2)}, u32[]{:S(2)}) collective-permute-start(bf16[144,512]{1,0:T(8,128)(2,1)S(1)} %stream.1.b0), channel_id=1, source_target_pairs={{0,2},{1,3},{2,0},{3,1},{4,6},{5,7},{6,4},{7,5},{8,10},{9,11},{10,... | collective-permute-start | bytes 442376 | tf_op jit(solution)/shard_map/ppermute | solution.py:460
  50.3 2.6 %collective-permute-done.12.b3 = bf16[144,512]{1,0:T(8,128)(2,1)S(1)} collective-permute-done((bf16[144,512]{1,0:T(8,128)(2,1)S(1)}, bf16[144,512]{1,0:T(8,128)(2,1)S(1)}, u32[]{:S(2)}, u32[]{:S(2)}) %collective-permute-start.12) | collective-permute-done | bytes 147488 | tf_op jit(solution)/shard_map/ppermute | solution.py:463
  53.0 1.3 %collective-permute-start.16 = (bf16[144,512]{1,0:T(8,128)(2,1)S(1)}, bf16[144,512]{1,0:T(8,128)(2,1)S(1)}, u32[]{:S(2)}, u32[]{:S(2)}) collective-permute-start(bf16[144,512]{1,0:T(8,128)(2,1)S(1)} %collective-permute-done.12.b3), channel_id=1, source_target_pairs={{0,2},{1,3},{2,0},{3,1},{4,6},{5,7},{6,4},{7,5},{8,10},{9,11},{10,... | collective-permute-start | bytes 442376 | tf_op jit(solution)/shard_map/ppermute | solution.py:460
  54.2 4.5 %collective-permute-done.11.b2 = bf16[144,512]{1,0:T(8,128)(2,1)S(1)} collective-permute-done((bf16[144,512]{1,0:T(8,128)(2,1)S(1)}, bf16[144,512]{1,0:T(8,128)(2,1)S(1)}, u32[]{:S(2)}, u32[]{:S(2)}) %collective-permute-start.11) | collective-permute-done | bytes 147488 | tf_op jit(solution)/shard_map/ppermute | solution.py:463
  58.7 1.3 %collective-permute-start.15 = (bf16[144,512]{1,0:T(8,128)(2,1)S(1)}, bf16[144,512]{1,0:T(8,128)(2,1)S(1)}, u32[]{:S(2)}, u32[]{:S(2)}) collective-permute-start(bf16[144,512]{1,0:T(8,128)(2,1)S(1)} %collective-permute-done.11.b2), channel_id=1, source_target_pairs={{0,2},{1,3},{2,0},{3,1},{4,6},{5,7},{6,4},{7,5},{8,10},{9,11},{10,... | collective-permute-start | bytes 442376 | tf_op jit(solution)/shard_map/ppermute | solution.py:460
  60.0 0.7 collective-permute-start.14
  60.8 1.3 %collective-permute-start.20 = (bf16[384,768]{1,0:T(8,128)(2,1)S(1)}, bf16[384,768]{1,0:T(8,128)(2,1)S(1)}, u32[]{:S(2)}, u32[]{:S(2)}) collective-permute-start(bf16[384,768]{1,0:T(8,128)(2,1)S(1)} %copy-done.11), channel_id=1, source_target_pairs={{0,16},{16,0},{1,17},{17,1},{2,18},{18,2},{3,19},{19,3},{4,20},{20... | collective-permute-start | bytes 1769480 | tf_op jit(solution)/shard_map/ppermute | solution.py:448
  62.1 0.3 norm.2
  62.5 2.6 %collective-permute-done.15.b2 = bf16[144,512]{1,0:T(8,128)(2,1)S(1)} collective-permute-done((bf16[144,512]{1,0:T(8,128)(2,1)S(1)}, bf16[144,512]{1,0:T(8,128)(2,1)S(1)}, u32[]{:S(2)}, u32[]{:S(2)}) %collective-permute-start.15) | collective-permute-done | bytes 147488 | tf_op jit(solution)/shard_map/ppermute | solution.py:460
  65.2 1.6 %collective-permute-done.14.b1 = bf16[144,512]{1,0:T(8,128)(2,1)S(1)} collective-permute-done((bf16[144,512]{1,0:T(8,128)(2,1)S(1)}, bf16[144,512]{1,0:T(8,128)(2,1)S(1)}, u32[]{:S(2)}, u32[]{:S(2)}) %collective-permute-start.14) | collective-permute-done | bytes 147488 | tf_op jit(solution)/shard_map/ppermute | solution.py:460
  66.7 0.9 norm.3
  67.6 2.0 %collective-permute-done.17.group_cx = bf16[128,2176]{1,0:T(8,128)(2,1)S(1)} collective-permute-done((bf16[128,2176]{1,0:T(8,128)(2,1)S(1)}, bf16[128,2176]{1,0:T(8,128)(2,1)S(1)}, u32[]{:S(2)}, u32[]{:S(2)}) %collective-permute-start.17) | collective-permute-done | bytes 557088 | tf_op jit(solution)/shard_map/ppermute | solution.py:460
  69.6 3.4 %first_gate_up.1 = (bf16[384,384]{1,0:T(8,128)(2,1)S(1)}, bf16[128,384]{1,0:T(8,128)(2,1)S(1)}, f32[512,768]{1,0:T(8,128)S(1)}, bf16[512,1024]{1,0:T(8,128)(2,1)S(1)}, f32[512,128]{1,0:T(8,128)S(1)}) custom-call(bf16[128,2176]{1,0:T(8,128)(2,1)S(1)} %get-tuple-element.59.group_x, bf16[128,2176]{1,0:T(8,128)(2,1)S(1)} %collective-permute-done.17.group_cx, ...), custom_call_target="tpu_custom_call" | custom-call | flops 1 | bytes 1 | tf_op jit(solution)/shard_map/first_gate_up/pallas_call | solution.py:436
  73.0 1.4 %collective-permute-start.28 = (bf16[384,384]{1,0:T(8,128)(2,1)S(1)}, bf16[384,384]{1,0:T(8,128)(2,1)S(1)}, u32[]{:S(2)}, u32[]{:S(2)}) collective-permute-start(bf16[384,384]{1,0:T(8,128)(2,1)S(1)} %get-tuple-element.61.first), channel_id=1, source_target_pairs={{0,16},{16,0},{1,17},{17,1},{2,18},{18,2},{3,19},{19,3},{4,20},{20... | collective-permute-start | bytes 884744 | tf_op jit(solution)/shard_map/ppermute | solution.py:448
  74.4 3.1 %collective-permute-done.20.refs_1_ = bf16[384,768]{1,0:T(8,128)(2,1)S(1)} collective-permute-done((bf16[384,768]{1,0:T(8,128)(2,1)S(1)}, bf16[384,768]{1,0:T(8,128)(2,1)S(1)}, u32[]{:S(2)}, u32[]{:S(2)}) %collective-permute-start.20) | collective-permute-done | bytes 589856 | tf_op jit(solution)/shard_map/ppermute | solution.py:448
  77.4 1.5 %last_gate_up.1 = (bf16[256,384]{1,0:T(8,128)(2,1)S(1)}, bf16[384,384]{1,0:T(8,128)(2,1)S(1)}) custom-call(bf16[128,384]{1,0:T(8,128)(2,1)S(1)} %get-tuple-element.62.second, f32[512,768]{1,0:T(8,128)S(1)} %get-tuple-element.63.part, bf16[512,1024]{1,0:T(8,128)(2,1)S(1)} %get-tuple-element.64.other, f32[512,128]{1,0:T(8,128)S(1)} %get-tuple-element.65.share, ...), custom_call_target="tpu_custom_call" | custom-call | flops 1 | bytes 1 | tf_op jit(solution)/shard_map/last_gate_up/pallas_call | solution.py:436
  78.9 1.0 down_both.1
  80.0 0.5 collective-permute-start.22
  80.5 2.1 %collective-permute-start.29 = (bf16[256,384]{1,0:T(8,128)(2,1)S(1)}, bf16[256,384]{1,0:T(8,128)(2,1)S(1)}, u32[]{:S(2)}, u32[]{:S(2)}) collective-permute-start(bf16[256,384]{1,0:T(8,128)(2,1)S(1)} %get-tuple-element.68.far), channel_id=1, source_target_pairs={{0,16},{16,0},{1,17},{17,1},{2,18},{18,2},{3,19},{19,3},{4,20},{20... | collective-permute-start | bytes 589832 | tf_op jit(solution)/shard_map/ppermute | solution.py:448
  82.7 1.6 %collective-permute-start.23 = (bf16[128,1024]{1,0:T(8,128)(2,1)S(1)}, bf16[128,1024]{1,0:T(8,128)(2,1)S(1)}, u32[]{:S(2)}, u32[]{:S(2)}) collective-permute-start(bf16[128,1024]{1,0:T(8,128)(2,1)S(1)} %fold.2), channel_id=1, source_target_pairs={{0,2},{1,3},{2,0},{3,1},{4,6},{5,7},{6,4},{7,5},{8,10},{9,11},{10,... | collective-permute-start | bytes 786440 | tf_op jit(solution)/shard_map/ppermute | solution.py:460
  84.2 1.1 collective-permute-start.33
  85.3 2.8 %collective-permute-done.29.far = bf16[256,384]{1,0:T(8,128)(2,1)S(1)} collective-permute-done((bf16[256,384]{1,0:T(8,128)(2,1)S(1)}, bf16[256,384]{1,0:T(8,128)(2,1)S(1)}, u32[]{:S(2)}, u32[]{:S(2)}) %collective-permute-start.29) | collective-permute-done | bytes 196640 | tf_op jit(solution)/shard_map/ppermute | solution.py:448
  88.1 0.6 down.2
  88.7 0.6 collective-permute-start.30
  89.4 1.3 %collective-permute-done.23.far = bf16[128,1024]{1,0:T(8,128)(2,1)S(1)} collective-permute-done((bf16[128,1024]{1,0:T(8,128)(2,1)S(1)}, bf16[128,1024]{1,0:T(8,128)(2,1)S(1)}, u32[]{:S(2)}, u32[]{:S(2)}) %collective-permute-start.23) | collective-permute-done | bytes 262176 | tf_op jit(solution)/shard_map/ppermute | solution.py:460
  91.0 2.0 %collective-permute-start.32 = (bf16[128,1024]{1,0:T(8,128)(2,1)S(1)}, bf16[128,1024]{1,0:T(8,128)(2,1)S(1)}, u32[]{:S(2)}, u32[]{:S(2)}) collective-permute-start(bf16[128,1024]{1,0:T(8,128)(2,1)S(1)} %fold.3), channel_id=1, source_target_pairs={{0,2},{1,3},{2,0},{3,1},{4,6},{5,7},{6,4},{7,5},{8,10},{9,11},{10,... | collective-permute-start | bytes 786440 | tf_op jit(solution)/shard_map/ppermute | solution.py:460
  93.0 0.7 collective-permute-start.26
  93.7 1.6 %collective-permute-start.27 = (bf16[64,1024]{1,0:T(8,128)(2,1)S(1)}, bf16[64,1024]{1,0:T(8,128)(2,1)S(1)}, u32[]{:S(2)}, u32[]{:S(2)}) collective-permute-start(bf16[64,1024]{1,0:T(8,128)(2,1)S(1)} %get-tuple-element.77), channel_id=1, source_target_pairs={{0,4},{1,13},{2,6},{3,15},{4,0},{5,9},{6,2},{7,11},{8,12},{9,5},{1... | collective-permute-start | bytes 393224 | tf_op jit(solution)/shard_map/ppermute | solution.py:457
  95.3 0.6 down.3
  95.9 3.0 %collective-permute-start.34 = (bf16[128,512]{1,0:T(8,128)(2,1)S(1)}, bf16[128,512]{1,0:T(8,128)(2,1)S(1)}, u32[]{:S(2)}, u32[]{:S(2)}) collective-permute-start(bf16[128,512]{1,0:T(8,128)(2,1)S(1)} %get-tuple-element.84), channel_id=1, source_target_pairs={{0,1},{1,0},{2,3},{3,2},{4,5},{5,4},{6,7},{7,6},{8,9},{9,8},{10,11... | collective-permute-start | bytes 393224 | tf_op jit(solution)/shard_map/ppermute | solution.py:460
  99.0 1.0 collective-permute-done.27.a1
  100.0 0.2 collective-permute-done.35.refs_1_
  100.3 1.6 %collective-permute-start.36 = (bf16[64,1024]{1,0:T(8,128)(2,1)S(1)}, bf16[64,1024]{1,0:T(8,128)(2,1)S(1)}, u32[]{:S(2)}, u32[]{:S(2)}) collective-permute-start(bf16[64,1024]{1,0:T(8,128)(2,1)S(1)} %get-tuple-element.86), channel_id=1, source_target_pairs={{0,16},{1,25},{2,18},{3,27},{4,20},{5,29},{6,22},{7,31},{8,24},{9,... | collective-permute-start | bytes 393224 | tf_op jit(solution)/shard_map/ppermute | solution.py:457
  101.9 0.9 collective-permute-start.37
  102.8 2.5 %collective-permute-done.36.b0 = bf16[64,1024]{1,0:T(8,128)(2,1)S(1)} collective-permute-done((bf16[64,1024]{1,0:T(8,128)(2,1)S(1)}, bf16[64,1024]{1,0:T(8,128)(2,1)S(1)}, u32[]{:S(2)}, u32[]{:S(2)}) %collective-permute-start.36) | collective-permute-done | bytes 131104 | tf_op jit(solution)/shard_map/ppermute | solution.py:457
  105.4 2.4 %collective-permute-done.37.b1 = bf16[64,1024]{1,0:T(8,128)(2,1)S(1)} collective-permute-done((bf16[64,1024]{1,0:T(8,128)(2,1)S(1)}, bf16[64,1024]{1,0:T(8,128)(2,1)S(1)}, u32[]{:S(2)}, u32[]{:S(2)}) %collective-permute-start.37) | collective-permute-done | bytes 131104 | tf_op jit(solution)/shard_map/ppermute | solution.py:457
  107.9 6.3 %collective-permute-start.38 = (bf16[64,1024]{1,0:T(8,128)(2,1)S(1)}, bf16[64,1024]{1,0:T(8,128)(2,1)S(1)}, u32[]{:S(2)}, u32[]{:S(2)}) collective-permute-start(bf16[64,1024]{1,0:T(8,128)(2,1)S(1)} %get-tuple-element.89), channel_id=1, source_target_pairs={{0,1},{1,0},{2,3},{3,2},{4,5},{5,4},{6,7},{7,6},{8,9},{9,8},{10,11... | collective-permute-start | bytes 393224 | tf_op jit(solution)/shard_map/ppermute | solution.py:460
  114.2 1.0 collective-permute-done.38.core
  115.2 0.8 closing.1
  (63 shorter events, 1.5 us)
Async XLA Ops:
  0.6 1.9 %copy-start = (bf16[1,1024,1536]{2,1,0:T(8,128)(2,1)S(1)}, bf16[1,1024,1536]{2,1,0:T(8,128)(2,1)}, u32[]{:S(2)}) copy-start(bf16[1,1024,1536]{2,1,0:T(8,128)(2,1)} %param.17) | copy-start | bytes 9437188
  2.5 4.7 %copy-start.4 = (bf16[1,32,2048]{2,1,0:T(8,128)(2,1)S(1)}, bf16[1,32,2048]{2,1,0:T(8,128)(2,1)}, u32[]{:S(2)}) copy-start(bf16[1,32,2048]{2,1,0:T(8,128)(2,1)} %param.11) | copy-start | bytes 393220
  2.5 7.9 %copy-start.3 = (bf16[1,64,2048]{2,1,0:T(8,128)(2,1)S(1)}, bf16[1,64,2048]{2,1,0:T(8,128)(2,1)}, u32[]{:S(2)}) copy-start(bf16[1,64,2048]{2,1,0:T(8,128)(2,1)} %param.10) | copy-start | bytes 786436
  2.7 38.3 %collective-permute-start.8 = (bf16[1024,768]{1,0:T(8,128)(2,1)S(1)}, bf16[1024,768]{1,0:T(8,128)(2,1)S(1)}, u32[]{:S(2)}, u32[]{:S(2)}) collective-permute-start(bf16[1024,768]{1,0:T(8,128)(2,1)S(1)} %weight_piece.3), channel_id=1, source_target_pairs={{0,16},{16,0},{1,17},{17,1},{2,18},{18,2},{3,19},{19,3},{4,20},{20... | collective-permute-start | bytes 4718600 | tf_op jit(solution)/shard_map/ppermute | solution.py:448
  5.7 13.7 %collective-permute-start.5 = (bf16[2048,128]{1,0:T(8,128)(2,1)}, bf16[2048,128]{1,0:T(8,128)(2,1)}, u32[]{:S(2)}, u32[]{:S(2)}) collective-permute-start(bf16[2048,128]{1,0:T(8,128)(2,1)} %w0.1), channel_id=1, source_target_pairs={{0,2},{1,3},{2,0},{3,1},{4,6},{5,7},{6,4},{7,5},{8,10},{9,11},{10,... | collective-permute-start | bytes 1572872 | tf_op jit(solution)/shard_map/ppermute | solution.py:460
  7.9 4.7 %copy-start.6 = (bf16[32,512]{1,0:T(8,128)(2,1)}, bf16[32,512]{1,0:T(8,128)(2,1)S(1)}, u32[]{:S(2)}) copy-start(bf16[32,512]{1,0:T(8,128)(2,1)S(1)} %get-tuple-element.49) | copy-start | bytes 98308
  7.9 11.6 %collective-permute-start.2 = (bf16[64,512]{1,0:T(8,128)(2,1)}, bf16[64,512]{1,0:T(8,128)(2,1)S(1)}, u32[]{:S(2)}, u32[]{:S(2)}) collective-permute-start(bf16[64,512]{1,0:T(8,128)(2,1)} %get-tuple-element.47), channel_id=1, source_target_pairs={{0,8},{1,9},{2,10},{3,11},{4,12},{5,13},{6,14},{7,15},{8,0},{9,1},... | collective-permute-start | bytes 196616 | tf_op jit(solution)/shard_map/ppermute | solution.py:463
  10.5 4.6 %copy-start.12 = (s32[1,32,8]{1,2,0:T(8,128)S(1)}, s32[1,32,8]{1,2,0:T(8,128)}, u32[]{:S(2)}) copy-start(s32[1,32,8]{1,2,0:T(8,128)} %param.14) | copy-start | bytes 3076
  10.5 14.9 %collective-permute-start.1 = (bf16[64,2048]{1,0:T(8,128)(2,1)S(1)}, bf16[64,2048]{1,0:T(8,128)(2,1)}, u32[]{:S(2)}, u32[]{:S(2)}) collective-permute-start(bf16[64,2048]{1,0:T(8,128)(2,1)S(1)} %bitcast.16), channel_id=1, source_target_pairs={{0,8},{1,9},{2,10},{3,11},{4,12},{5,13},{6,14},{7,15},{8,0},{9,1},... | collective-permute-start | bytes 786440 | tf_op jit(solution)/shard_map/ppermute | solution.py:463
  10.8 14.5 %collective-permute-start = (bf16[64,2048]{1,0:T(8,128)(2,1)S(1)}, bf16[64,2048]{1,0:T(8,128)(2,1)}, u32[]{:S(2)}, u32[]{:S(2)}) collective-permute-start(bf16[64,2048]{1,0:T(8,128)(2,1)S(1)} %bitcast.17), channel_id=1, source_target_pairs={{0,4},{1,5},{2,6},{3,7},{4,0},{5,1},{6,2},{7,3},{8,12},{9,13},{10,... | collective-permute-start | bytes 786440 | tf_op jit(solution)/shard_map/ppermute | solution.py:463
  12.6 1.0 copy-start.8
  13.6 0.8 copy-start.10
  19.4 15.4 %collective-permute-start.7 = (bf16[2048,128]{1,0:T(8,128)(2,1)}, bf16[2048,128]{1,0:T(8,128)(2,1)S(1)}, u32[]{:S(2)}, u32[]{:S(2)}) collective-permute-start(bf16[2048,128]{1,0:T(8,128)(2,1)} %collective-permute-done.5.w2), channel_id=1, source_target_pairs={{0,1},{1,0},{2,3},{3,2},{4,5},{5,4},{6,7},{7,6},{8,9},{9,8},{10,11... | collective-permute-start | bytes 1572872 | tf_op jit(solution)/shard_map/ppermute | solution.py:460
  19.5 15.4 %collective-permute-start.6 = (bf16[2048,128]{1,0:T(8,128)(2,1)}, bf16[2048,128]{1,0:T(8,128)(2,1)S(1)}, u32[]{:S(2)}, u32[]{:S(2)}) collective-permute-start(bf16[2048,128]{1,0:T(8,128)(2,1)} %w0.1), channel_id=1, source_target_pairs={{0,1},{1,0},{2,3},{3,2},{4,5},{5,4},{6,7},{7,6},{8,9},{9,8},{10,11... | collective-permute-start | bytes 1572872 | tf_op jit(solution)/shard_map/ppermute | solution.py:460
  25.4 9.5 %collective-permute-start.3 = (bf16[64,2048]{1,0:T(8,128)(2,1)}, bf16[64,2048]{1,0:T(8,128)(2,1)S(1)}, u32[]{:S(2)}, u32[]{:S(2)}) collective-permute-start(bf16[64,2048]{1,0:T(8,128)(2,1)} %collective-permute-done.1.a2), channel_id=1, source_target_pairs={{0,4},{1,5},{2,6},{3,7},{4,0},{5,1},{6,2},{7,3},{8,12},{9,13},{10,... | collective-permute-start | bytes 786440 | tf_op jit(solution)/shard_map/ppermute | solution.py:463
  26.3 12.0 %copy-start.9 = (bf16[640,768]{1,0:T(8,128)(2,1)S(1)}, bf16[640,768]{1,0:T(8,128)(2,1)}, u32[]{:S(2)}) copy-start(bf16[640,768]{1,0:T(8,128)(2,1)} %copy-done.8) | copy-start | bytes 2949124
  26.3 34.4 %copy-start.11 = (bf16[384,768]{1,0:T(8,128)(2,1)S(1)}, bf16[384,768]{1,0:T(8,128)(2,1)}, u32[]{:S(2)}) copy-start(bf16[384,768]{1,0:T(8,128)(2,1)} %copy-done.10) | copy-start | bytes 1769476
  26.4 35.7 %copy-start.5 = (f32[2048]{0:T(1024)S(1)}, f32[2048]{0:T(1024)}, u32[]{:S(2)}) copy-start(f32[2048]{0:T(1024)} %param.13) | copy-start | bytes 24580
  26.4 8.5 %collective-permute-start.4 = (bf16[64,512]{1,0:T(8,128)(2,1)S(1)}, bf16[64,512]{1,0:T(8,128)(2,1)S(1)}, u32[]{:S(2)}, u32[]{:S(2)}) collective-permute-start(bf16[64,512]{1,0:T(8,128)(2,1)S(1)} %pad_maximum_fusion), channel_id=1, source_target_pairs={{0,4},{1,5},{2,6},{3,7},{4,0},{5,1},{6,2},{7,3},{8,12},{9,13},{10,... | collective-permute-start | bytes 196616 | tf_op jit(solution)/shard_map/ppermute | solution.py:463
  34.9 34.7 %copy-start.1 = (bf16[1,1024,1536]{2,1,0:T(8,128)(2,1)S(1)}, bf16[1,1024,1536]{2,1,0:T(8,128)(2,1)}, u32[]{:S(2)}) copy-start(bf16[1,1024,1536]{2,1,0:T(8,128)(2,1)} %param.17) | copy-start | bytes 9437188
  37.8 6.5 %collective-permute-start.9 = (bf16[128,512]{1,0:T(8,128)(2,1)S(1)}, bf16[128,512]{1,0:T(8,128)(2,1)S(1)}, u32[]{:S(2)}, u32[]{:S(2)}) collective-permute-start(bf16[128,512]{1,0:T(8,128)(2,1)S(1)} %get-tuple-element.56), channel_id=1, source_target_pairs={{0,16},{16,0},{1,17},{17,1},{2,18},{18,2},{3,19},{19,3},{4,20},{20... | collective-permute-start | bytes 393224 | tf_op jit(solution)/shard_map/ppermute | solution.py:448
  38.3 39.1 %collective-permute-start.19 = (bf16[640,768]{1,0:T(8,128)(2,1)S(1)}, bf16[640,768]{1,0:T(8,128)(2,1)S(1)}, u32[]{:S(2)}, u32[]{:S(2)}) collective-permute-start(bf16[640,768]{1,0:T(8,128)(2,1)S(1)} %copy-done.9), channel_id=1, source_target_pairs={{0,16},{16,0},{1,17},{17,1},{2,18},{18,2},{3,19},{19,3},{4,20},{20... | collective-permute-start | bytes 2949128 | tf_op jit(solution)/shard_map/ppermute | solution.py:448
  44.3 8.6 %collective-permute-start.12 = (bf16[144,512]{1,0:T(8,128)(2,1)S(1)}, bf16[144,512]{1,0:T(8,128)(2,1)S(1)}, u32[]{:S(2)}, u32[]{:S(2)}) collective-permute-start(bf16[144,512]{1,0:T(8,128)(2,1)S(1)} %stream.1.b0), channel_id=1, source_target_pairs={{0,12},{1,13},{2,14},{3,15},{4,8},{5,9},{6,10},{7,11},{8,4},{9,5},... | collective-permute-start | bytes 442376 | tf_op jit(solution)/shard_map/ppermute | solution.py:463
  47.8 10.9 %collective-permute-start.11 = (bf16[144,512]{1,0:T(8,128)(2,1)S(1)}, bf16[144,512]{1,0:T(8,128)(2,1)S(1)}, u32[]{:S(2)}, u32[]{:S(2)}) collective-permute-start(bf16[144,512]{1,0:T(8,128)(2,1)S(1)} %stream.1.b0), channel_id=1, source_target_pairs={{0,8},{1,9},{2,10},{3,11},{4,12},{5,13},{6,14},{7,15},{8,0},{9,1},... | collective-permute-start | bytes 442376 | tf_op jit(solution)/shard_map/ppermute | solution.py:463
  47.9 12.2 %collective-permute-start.10 = (bf16[144,512]{1,0:T(8,128)(2,1)S(1)}, bf16[144,512]{1,0:T(8,128)(2,1)S(1)}, u32[]{:S(2)}, u32[]{:S(2)}) collective-permute-start(bf16[144,512]{1,0:T(8,128)(2,1)S(1)} %stream.1.b0), channel_id=1, source_target_pairs={{0,4},{1,5},{2,6},{3,7},{4,0},{5,1},{6,2},{7,3},{8,12},{9,13},{10,... | collective-permute-start | bytes 442376 | tf_op jit(solution)/shard_map/ppermute | solution.py:463
  48.8 12.0 %collective-permute-start.13 = (bf16[144,512]{1,0:T(8,128)(2,1)S(1)}, bf16[144,512]{1,0:T(8,128)(2,1)S(1)}, u32[]{:S(2)}, u32[]{:S(2)}) collective-permute-start(bf16[144,512]{1,0:T(8,128)(2,1)S(1)} %stream.1.b0), channel_id=1, source_target_pairs={{0,2},{1,3},{2,0},{3,1},{4,6},{5,7},{6,4},{7,5},{8,10},{9,11},{10,... | collective-permute-start | bytes 442376 | tf_op jit(solution)/shard_map/ppermute | solution.py:460
  53.0 9.5 %collective-permute-start.16 = (bf16[144,512]{1,0:T(8,128)(2,1)S(1)}, bf16[144,512]{1,0:T(8,128)(2,1)S(1)}, u32[]{:S(2)}, u32[]{:S(2)}) collective-permute-start(bf16[144,512]{1,0:T(8,128)(2,1)S(1)} %collective-permute-done.12.b3), channel_id=1, source_target_pairs={{0,2},{1,3},{2,0},{3,1},{4,6},{5,7},{6,4},{7,5},{8,10},{9,11},{10,... | collective-permute-start | bytes 442376 | tf_op jit(solution)/shard_map/ppermute | solution.py:460
  58.7 6.4 %collective-permute-start.15 = (bf16[144,512]{1,0:T(8,128)(2,1)S(1)}, bf16[144,512]{1,0:T(8,128)(2,1)S(1)}, u32[]{:S(2)}, u32[]{:S(2)}) collective-permute-start(bf16[144,512]{1,0:T(8,128)(2,1)S(1)} %collective-permute-done.11.b2), channel_id=1, source_target_pairs={{0,2},{1,3},{2,0},{3,1},{4,6},{5,7},{6,4},{7,5},{8,10},{9,11},{10,... | collective-permute-start | bytes 442376 | tf_op jit(solution)/shard_map/ppermute | solution.py:460
  60.0 6.7 %collective-permute-start.14 = (bf16[144,512]{1,0:T(8,128)(2,1)S(1)}, bf16[144,512]{1,0:T(8,128)(2,1)S(1)}, u32[]{:S(2)}, u32[]{:S(2)}) collective-permute-start(bf16[144,512]{1,0:T(8,128)(2,1)S(1)} %collective-permute-done.10.b1), channel_id=1, source_target_pairs={{0,2},{1,3},{2,0},{3,1},{4,6},{5,7},{6,4},{7,5},{8,10},{9,11},{10,... | collective-permute-start | bytes 442376 | tf_op jit(solution)/shard_map/ppermute | solution.py:460
  60.8 16.7 %collective-permute-start.20 = (bf16[384,768]{1,0:T(8,128)(2,1)S(1)}, bf16[384,768]{1,0:T(8,128)(2,1)S(1)}, u32[]{:S(2)}, u32[]{:S(2)}) collective-permute-start(bf16[384,768]{1,0:T(8,128)(2,1)S(1)} %copy-done.11), channel_id=1, source_target_pairs={{0,16},{16,0},{1,17},{17,1},{2,18},{18,2},{3,19},{19,3},{4,20},{20... | collective-permute-start | bytes 1769480 | tf_op jit(solution)/shard_map/ppermute | solution.py:448
  62.4 5.2 %collective-permute-start.18 = (bf16[128,2176]{1,0:T(8,128)(2,1)S(1)}, bf16[128,2176]{1,0:T(8,128)(2,1)S(1)}, u32[]{:S(2)}, u32[]{:S(2)}) collective-permute-start(bf16[128,2176]{1,0:T(8,128)(2,1)S(1)} %get-tuple-element.60.group), channel_id=1, source_target_pairs={{0,1},{1,0},{2,3},{3,2},{4,5},{5,4},{6,7},{7,6},{8,9},{9,8},{10,11... | collective-permute-start | bytes 1671176 | tf_op jit(solution)/shard_map/ppermute | solution.py:460
  67.6 2.0 %collective-permute-start.17 = (bf16[128,2176]{1,0:T(8,128)(2,1)S(1)}, bf16[128,2176]{1,0:T(8,128)(2,1)S(1)}, u32[]{:S(2)}, u32[]{:S(2)}) collective-permute-start(bf16[128,2176]{1,0:T(8,128)(2,1)S(1)} %get-tuple-element.59.group_x), channel_id=1, source_target_pairs={{0,1},{1,0},{2,3},{3,2},{4,5},{5,4},{6,7},{7,6},{8,9},{9,8},{10,11... | collective-permute-start | bytes 1671176 | tf_op jit(solution)/shard_map/ppermute | solution.py:460
  73.0 15.1 %collective-permute-start.28 = (bf16[384,384]{1,0:T(8,128)(2,1)S(1)}, bf16[384,384]{1,0:T(8,128)(2,1)S(1)}, u32[]{:S(2)}, u32[]{:S(2)}) collective-permute-start(bf16[384,384]{1,0:T(8,128)(2,1)S(1)} %get-tuple-element.61.first), channel_id=1, source_target_pairs={{0,16},{16,0},{1,17},{17,1},{2,18},{18,2},{3,19},{19,3},{4,20},{20... | collective-permute-start | bytes 884744 | tf_op jit(solution)/shard_map/ppermute | solution.py:448
  77.4 1.5 %copy-start.2 = (bf16[1,768,1024]{2,1,0:T(8,128)(2,1)S(1)}, bf16[1,768,1024]{2,1,0:T(8,128)(2,1)}, u32[]{:S(2)}) copy-start(bf16[1,768,1024]{2,1,0:T(8,128)(2,1)} %param.18) | copy-start | bytes 4718596
  79.9 2.7 %collective-permute-start.21 = (bf16[128,512]{1,0:T(8,128)(2,1)S(1)}, bf16[128,512]{1,0:T(8,128)(2,1)S(1)}, u32[]{:S(2)}, u32[]{:S(2)}) collective-permute-start(bf16[128,512]{1,0:T(8,128)(2,1)S(1)} %get-tuple-element.71), channel_id=1, source_target_pairs={{0,1},{1,0},{2,3},{3,2},{4,5},{5,4},{6,7},{7,6},{8,9},{9,8},{10,11... | collective-permute-start | bytes 393224 | tf_op jit(solution)/shard_map/ppermute | solution.py:460
  80.0 2.6 %collective-permute-start.22 = (bf16[128,512]{1,0:T(8,128)(2,1)S(1)}, bf16[128,512]{1,0:T(8,128)(2,1)S(1)}, u32[]{:S(2)}, u32[]{:S(2)}) collective-permute-start(bf16[128,512]{1,0:T(8,128)(2,1)S(1)} %get-tuple-element.72), channel_id=1, source_target_pairs={{0,1},{1,0},{2,3},{3,2},{4,5},{5,4},{6,7},{7,6},{8,9},{9,8},{10,11... | collective-permute-start | bytes 393224 | tf_op jit(solution)/shard_map/ppermute | solution.py:460
  80.5 7.6 %collective-permute-start.29 = (bf16[256,384]{1,0:T(8,128)(2,1)S(1)}, bf16[256,384]{1,0:T(8,128)(2,1)S(1)}, u32[]{:S(2)}, u32[]{:S(2)}) collective-permute-start(bf16[256,384]{1,0:T(8,128)(2,1)S(1)} %get-tuple-element.68.far), channel_id=1, source_target_pairs={{0,16},{16,0},{1,17},{17,1},{2,18},{18,2},{3,19},{19,3},{4,20},{20... | collective-permute-start | bytes 589832 | tf_op jit(solution)/shard_map/ppermute | solution.py:448
  82.7 8.1 %collective-permute-start.23 = (bf16[128,1024]{1,0:T(8,128)(2,1)S(1)}, bf16[128,1024]{1,0:T(8,128)(2,1)S(1)}, u32[]{:S(2)}, u32[]{:S(2)}) collective-permute-start(bf16[128,1024]{1,0:T(8,128)(2,1)S(1)} %fold.2), channel_id=1, source_target_pairs={{0,2},{1,3},{2,0},{3,1},{4,6},{5,7},{6,4},{7,5},{8,10},{9,11},{10,... | collective-permute-start | bytes 786440 | tf_op jit(solution)/shard_map/ppermute | solution.py:460
  84.2 5.0 %collective-permute-start.24 = (bf16[128,512]{1,0:T(8,128)(2,1)S(1)}, bf16[128,512]{1,0:T(8,128)(2,1)S(1)}, u32[]{:S(2)}, u32[]{:S(2)}) collective-permute-start(bf16[128,512]{1,0:T(8,128)(2,1)S(1)} %get-tuple-element.74), channel_id=1, source_target_pairs={{0,1},{1,0},{2,3},{3,2},{4,5},{5,4},{6,7},{7,6},{8,9},{9,8},{10,11... | collective-permute-start | bytes 393224 | tf_op jit(solution)/shard_map/ppermute | solution.py:460
  84.2 11.1 %collective-permute-start.33 = (bf16[384,384]{1,0:T(8,128)(2,1)S(1)}, bf16[384,384]{1,0:T(8,128)(2,1)S(1)}, u32[]{:S(2)}, u32[]{:S(2)}) collective-permute-start(bf16[384,384]{1,0:T(8,128)(2,1)S(1)} %get-tuple-element.69.rest), channel_id=1, source_target_pairs={{0,16},{16,0},{1,17},{17,1},{2,18},{18,2},{3,19},{19,3},{4,20},{20... | collective-permute-start | bytes 884744 | tf_op jit(solution)/shard_map/ppermute | solution.py:448
  88.1 1.3 %collective-permute-start.25 = (bf16[128,512]{1,0:T(8,128)(2,1)S(1)}, bf16[128,512]{1,0:T(8,128)(2,1)S(1)}, u32[]{:S(2)}, u32[]{:S(2)}) collective-permute-start(bf16[128,512]{1,0:T(8,128)(2,1)S(1)} %get-tuple-element.75), channel_id=1, source_target_pairs={{0,1},{1,0},{2,3},{3,2},{4,5},{5,4},{6,7},{7,6},{8,9},{9,8},{10,11... | collective-permute-start | bytes 393224 | tf_op jit(solution)/shard_map/ppermute | solution.py:460
  88.7 2.2 %collective-permute-start.30 = (bf16[128,512]{1,0:T(8,128)(2,1)S(1)}, bf16[128,512]{1,0:T(8,128)(2,1)S(1)}, u32[]{:S(2)}, u32[]{:S(2)}) collective-permute-start(bf16[128,512]{1,0:T(8,128)(2,1)S(1)} %get-tuple-element.80), channel_id=1, source_target_pairs={{0,1},{1,0},{2,3},{3,2},{4,5},{5,4},{6,7},{7,6},{8,9},{9,8},{10,11... | collective-permute-start | bytes 393224 | tf_op jit(solution)/shard_map/ppermute | solution.py:460
  89.3 1.6 %collective-permute-start.31 = (bf16[128,512]{1,0:T(8,128)(2,1)S(1)}, bf16[128,512]{1,0:T(8,128)(2,1)S(1)}, u32[]{:S(2)}, u32[]{:S(2)}) collective-permute-start(bf16[128,512]{1,0:T(8,128)(2,1)S(1)} %get-tuple-element.81), channel_id=1, source_target_pairs={{0,1},{1,0},{2,3},{3,2},{4,5},{5,4},{6,7},{7,6},{8,9},{9,8},{10,11... | collective-permute-start | bytes 393224 | tf_op jit(solution)/shard_map/ppermute | solution.py:460
  91.0 9.3 %collective-permute-start.32 = (bf16[128,1024]{1,0:T(8,128)(2,1)S(1)}, bf16[128,1024]{1,0:T(8,128)(2,1)S(1)}, u32[]{:S(2)}, u32[]{:S(2)}) collective-permute-start(bf16[128,1024]{1,0:T(8,128)(2,1)S(1)} %fold.3), channel_id=1, source_target_pairs={{0,2},{1,3},{2,0},{3,1},{4,6},{5,7},{6,4},{7,5},{8,10},{9,11},{10,... | collective-permute-start | bytes 786440 | tf_op jit(solution)/shard_map/ppermute | solution.py:460
  93.0 7.0 %collective-permute-start.26 = (bf16[64,1024]{1,0:T(8,128)(2,1)S(1)}, bf16[64,1024]{1,0:T(8,128)(2,1)S(1)}, u32[]{:S(2)}, u32[]{:S(2)}) collective-permute-start(bf16[64,1024]{1,0:T(8,128)(2,1)S(1)} %get-tuple-element.76.own), channel_id=1, source_target_pairs={{1,9},{3,11},{5,13},{7,15},{9,1},{11,3},{13,5},{15,7},{17,25},{19,... | collective-permute-start | bytes 393224 | tf_op jit(solution)/shard_map/ppermute | solution.py:457
  93.7 21.6 %copy-start.7 = (f32[2048]{0:T(1024)S(1)}, f32[2048]{0:T(1024)}, u32[]{:S(2)}) copy-start(f32[2048]{0:T(1024)} %param.19) | copy-start | bytes 24580
  93.7 6.3 %collective-permute-start.27 = (bf16[64,1024]{1,0:T(8,128)(2,1)S(1)}, bf16[64,1024]{1,0:T(8,128)(2,1)S(1)}, u32[]{:S(2)}, u32[]{:S(2)}) collective-permute-start(bf16[64,1024]{1,0:T(8,128)(2,1)S(1)} %get-tuple-element.77), channel_id=1, source_target_pairs={{0,4},{1,13},{2,6},{3,15},{4,0},{5,9},{6,2},{7,11},{8,12},{9,5},{1... | collective-permute-start | bytes 393224 | tf_op jit(solution)/shard_map/ppermute | solution.py:457
  95.9 4.1 %collective-permute-start.34 = (bf16[128,512]{1,0:T(8,128)(2,1)S(1)}, bf16[128,512]{1,0:T(8,128)(2,1)S(1)}, u32[]{:S(2)}, u32[]{:S(2)}) collective-permute-start(bf16[128,512]{1,0:T(8,128)(2,1)S(1)} %get-tuple-element.84), channel_id=1, source_target_pairs={{0,1},{1,0},{2,3},{3,2},{4,5},{5,4},{6,7},{7,6},{8,9},{9,8},{10,11... | collective-permute-start | bytes 393224 | tf_op jit(solution)/shard_map/ppermute | solution.py:460
  98.9 1.3 %collective-permute-start.35 = (bf16[128,512]{1,0:T(8,128)(2,1)S(1)}, bf16[128,512]{1,0:T(8,128)(2,1)S(1)}, u32[]{:S(2)}, u32[]{:S(2)}) collective-permute-start(bf16[128,512]{1,0:T(8,128)(2,1)S(1)} %get-tuple-element.85), channel_id=1, source_target_pairs={{0,1},{1,0},{2,3},{3,2},{4,5},{5,4},{6,7},{7,6},{8,9},{9,8},{10,11... | collective-permute-start | bytes 393224 | tf_op jit(solution)/shard_map/ppermute | solution.py:460
  100.3 5.0 %collective-permute-start.36 = (bf16[64,1024]{1,0:T(8,128)(2,1)S(1)}, bf16[64,1024]{1,0:T(8,128)(2,1)S(1)}, u32[]{:S(2)}, u32[]{:S(2)}) collective-permute-start(bf16[64,1024]{1,0:T(8,128)(2,1)S(1)} %get-tuple-element.86), channel_id=1, source_target_pairs={{0,16},{1,25},{2,18},{3,27},{4,20},{5,29},{6,22},{7,31},{8,24},{9,... | collective-permute-start | bytes 393224 | tf_op jit(solution)/shard_map/ppermute | solution.py:457
  101.9 5.9 %collective-permute-start.37 = (bf16[64,1024]{1,0:T(8,128)(2,1)S(1)}, bf16[64,1024]{1,0:T(8,128)(2,1)S(1)}, u32[]{:S(2)}, u32[]{:S(2)}) collective-permute-start(bf16[64,1024]{1,0:T(8,128)(2,1)S(1)} %get-tuple-element.87), channel_id=1, source_target_pairs={{0,20},{1,29},{2,22},{3,31},{4,16},{5,25},{6,18},{7,27},{8,28},{9,... | collective-permute-start | bytes 393224 | tf_op jit(solution)/shard_map/ppermute | solution.py:457
  107.9 7.3 %collective-permute-start.38 = (bf16[64,1024]{1,0:T(8,128)(2,1)S(1)}, bf16[64,1024]{1,0:T(8,128)(2,1)S(1)}, u32[]{:S(2)}, u32[]{:S(2)}) collective-permute-start(bf16[64,1024]{1,0:T(8,128)(2,1)S(1)} %get-tuple-element.89), channel_id=1, source_target_pairs={{0,1},{1,0},{2,3},{3,2},{4,5},{5,4},{6,7},{7,6},{8,9},{9,8},{10,11... | collective-permute-start | bytes 393224 | tf_op jit(solution)/shard_map/ppermute | solution.py:460

commit v17 on v16

--- a/solution.py
+++ b/solution.py
@@ -327,11 +327,11 @@
         for i in range(2):
             for j in range(2):
                 ref, start = places[j]
-                kept = aligned(start // small + (outer ^ (2 * core + i)), small)
+                kept = aligned(start // small + (outer ^ (core if i else 3 - core)), small)
                 at = (2 * i + j) * small
                 rows[at : at + small, cols] = ref[kept, :]
                 ref, start = places[1 - j]
-                sent = aligned(start // small + (outer ^ (2 - 2 * core + i)), small)
+                sent = aligned(start // small + (outer ^ (1 - core if i else 2 + core)), small)
                 rows[count + at : count + at + small, cols] = ref[sent, :]
     for at in range(0, wd.shape[1], 256):
         value = dot(rows[...], wd[:, at : at + 256]).astype(BF16)
@@ -391,8 +391,8 @@
 def gather_kernel(own, a0, a1, b0, b1, keep_ref, send_ref):
     expert, outer, inner, dp = seat()
     small = own.shape[0] // 2
-    start = jnp.where((inner & 1) == 0, own[...].astype(F32), a0[...].astype(F32))
-    for i, total in enumerate((start + a1[...].astype(F32), b0[...].astype(F32) + b1[...].astype(F32))):
+    last = jnp.where((inner & 1) == 0, own[...].astype(F32), a1[...].astype(F32))
+    for i, total in enumerate((a0[...].astype(F32) + last, b0[...].astype(F32) + b1[...].astype(F32))):
         rows = slice(i * small, (i + 1) * small)
         keep_ref[rows, :] = total[:small]
         send_ref[rows, :] = total[small:].astype(BF16)
@@ -451,7 +451,7 @@
         pairs = []
         for at in range(2 * expert_count):
             d, e = divmod(at, expert_count)
-            step = 2 * (e % 2) + i
+            step = e % 2 if i else 3 - e % 2
             if step or cross:
                 pairs.append((at, (d ^ cross) * expert_count + (e ^ (4 * step))))
         return lax.ppermute(x, ("dp", "expert"), pairs)
@@ -612,8 +612,8 @@
     )
     far = swap_inner(fold(keep_far, swap_cores(send[:2])), 2)
     first_far = far
-    own, second = pieces(far, keep_near, send[2:])
-    mine = [send_outer(own, 0, False), send_outer(second, 1, False)]
+    first, own = pieces(far, keep_near, send[2:])
+    mine = [send_outer(first, 0, False), send_outer(own, 1, False)]
 
     keep_far, send = down(down_far_kernel, far_other, 2)
     far = swap_inner(fold(after(keep_far, own), swap_cores(send)), 2)

time: 116 us -> 117 us (level)
  waiting for transfers between devices: 47.3 us -> 50.9 us
  starting transfers between devices: 48 us -> 44.7 us
    ppermute x20, starting transfers between devices: 21.2 us -> 13.1 us  [swap_inner(): return lax.ppermute(x, 'expert', [(i, i ^ j) for i in range(expert_count)])]
    ppermute x4, starting transfers between devices: 4.77 us -> 9.53 us  [send_outer(): return lax.ppermute(x, ('dp', 'expert'), pairs)]
    ppermute x4, waiting for transfers between devices: 6.02 us -> 9.43 us  [send_outer(): return lax.ppermute(x, ('dp', 'expert'), pairs)]
  transfers between devices with their start and end apart: 39 -> 39, of which waited for: 19 -> 18; matrix products, arithmetic and copies ran while one was open for 1% -> 1% of each run, Pallas kernels for 11% -> 11%
where the time goes in v17:
time: 117 us; the launch traced here: 116 us
  waiting for transfers between devices  50.9 us (44%)
  starting transfers between devices  44.7 us (38%)
  Pallas kernels  13.9 us (12%)
  local copies, waits for them, and re-layouts  4.58 us (4%)
  between operations  1.56 us (1%)
    ppermute x8, waiting for transfers between devices, swap_outer(): lax.ppermute(x, 'expert', [(i, i ^ 4 * s) for i in range(expert_count)])  19.1 us
    pallas_call x17, Pallas kernels, call(): pl.pallas_call(kernel, out_shape=outs, in_specs=[first] + [vmem] * (len(a...  13.5 us
    ppermute x20, starting transfers between devices, swap_inner(): return lax.ppermute(x, 'expert', [(i, i ^ j) for i in range(expert_count)])  13.1 us
    ppermute x20, waiting for transfers between devices, swap_inner(): return lax.ppermute(x, 'expert', [(i, i ^ j) for i in range(expert_count)])  12 us
    ppermute x8, starting transfers between devices, swap_outer(): lax.ppermute(x, 'expert', [(i, i ^ 4 * s) for i in range(expert_count)])  11 us
    ppermute x7, starting transfers between devices, swap_dp(): return lax.ppermute(x, 'dp', [(0, 1), (1, 0)])  11 us
    ppermute x7, waiting for transfers between devices, swap_dp(): return lax.ppermute(x, 'dp', [(0, 1), (1, 0)])  10.3 us
    ppermute x4, starting transfers between devices, send_outer(): return lax.ppermute(x, ('dp', 'expert'), pairs)  9.53 us
  transfers between devices with their start and end apart: 39, of which 18 were waited for; matrix products, arithmetic and copies ran while one was open for 1% of the time, Pallas kernels for 11%

profile of v17, /device:TPU:0, one launch (start us, length us, event | category | flops | bytes accessed | tf_op | source)
XLA Modules:
  0.0 116.3 jit_solution(14030360903357018080)
XLA Ops:
  0.6 1.9 %copy-done = bf16[1,1024,1536]{2,1,0:T(8,128)(2,1)S(1)} copy-done((bf16[1,1024,1536]{2,1,0:T(8,128)(2,1)S(1)}, bf16[1,1024,1536]{2,1,0:T(8,128)(2,1)}, u32[]{:S(2)}) %copy-start) | copy-done | bytes 3145752
  2.5 0.2 weight_piece.3
  2.7 3.0 %collective-permute-start.8 = (bf16[1024,768]{1,0:T(8,128)(2,1)S(1)}, bf16[1024,768]{1,0:T(8,128)(2,1)S(1)}, u32[]{:S(2)}, u32[]{:S(2)}) collective-permute-start(bf16[1024,768]{1,0:T(8,128)(2,1)S(1)} %weight_piece.3), channel_id=1, source_target_pairs={{0,16},{16,0},{1,17},{17,1},{2,18},{18,2},{3,19},{19,3},{4,20},{20... | collective-permute-start | bytes 4718600 | tf_op jit(solution)/shard_map/ppermute | solution.py:448
  5.7 1.5 %collective-permute-start.5 = (bf16[2048,128]{1,0:T(8,128)(2,1)}, bf16[2048,128]{1,0:T(8,128)(2,1)}, u32[]{:S(2)}, u32[]{:S(2)}) collective-permute-start(bf16[2048,128]{1,0:T(8,128)(2,1)} %w0.1), channel_id=1, source_target_pairs={{0,2},{1,3},{2,0},{3,1},{4,6},{5,7},{6,4},{7,5},{8,10},{9,11},{10,... | collective-permute-start | bytes 1572872 | tf_op jit(solution)/shard_map/ppermute | solution.py:460
  7.2 0.6 cut_resid.1
  7.9 2.6 %collective-permute-start.2 = (bf16[64,512]{1,0:T(8,128)(2,1)}, bf16[64,512]{1,0:T(8,128)(2,1)S(1)}, u32[]{:S(2)}, u32[]{:S(2)}) collective-permute-start(bf16[64,512]{1,0:T(8,128)(2,1)} %get-tuple-element.47), channel_id=1, source_target_pairs={{0,8},{1,9},{2,10},{3,11},{4,12},{5,13},{6,14},{7,15},{8,0},{9,1},... | collective-permute-start | bytes 196616 | tf_op jit(solution)/shard_map/ppermute | solution.py:463
  10.5 0.3 collective-permute-start.1
  10.8 1.6 %collective-permute-start = (bf16[64,2048]{1,0:T(8,128)(2,1)S(1)}, bf16[64,2048]{1,0:T(8,128)(2,1)}, u32[]{:S(2)}, u32[]{:S(2)}) collective-permute-start(bf16[64,2048]{1,0:T(8,128)(2,1)S(1)} %bitcast.17), channel_id=1, source_target_pairs={{0,4},{1,5},{2,6},{3,7},{4,0},{5,1},{6,2},{7,3},{8,12},{9,13},{10,... | collective-permute-start | bytes 786440 | tf_op jit(solution)/shard_map/ppermute | solution.py:463
  12.4 0.2 weight_piece.2
  12.6 1.0 copy-done.8
  13.6 0.8 copy-done.10
  15.2 0.8 copy.13
  15.9 0.4 share.1
  16.4 3.1 %collective-permute-done.5.w2 = bf16[2048,128]{1,0:T(8,128)(2,1)} collective-permute-done((bf16[2048,128]{1,0:T(8,128)(2,1)}, bf16[2048,128]{1,0:T(8,128)(2,1)}, u32[]{:S(2)}, u32[]{:S(2)}) %collective-permute-start.5) | collective-permute-done | bytes 524320 | tf_op jit(solution)/shard_map/ppermute | solution.py:460
  19.5 0.5 collective-permute-start.6
  20.0 5.4 %collective-permute-done.1.a2 = bf16[64,2048]{1,0:T(8,128)(2,1)} collective-permute-done((bf16[64,2048]{1,0:T(8,128)(2,1)S(1)}, bf16[64,2048]{1,0:T(8,128)(2,1)}, u32[]{:S(2)}, u32[]{:S(2)}) %collective-permute-start.1) | collective-permute-done | bytes 262176 | tf_op jit(solution)/shard_map/ppermute | solution.py:463
  25.4 0.2 collective-permute-start.3
  25.6 0.8 pad_maximum_fusion
  26.4 1.9 %collective-permute-start.4 = (bf16[64,512]{1,0:T(8,128)(2,1)S(1)}, bf16[64,512]{1,0:T(8,128)(2,1)S(1)}, u32[]{:S(2)}, u32[]{:S(2)}) collective-permute-start(bf16[64,512]{1,0:T(8,128)(2,1)S(1)} %pad_maximum_fusion), channel_id=1, source_target_pairs={{0,4},{1,5},{2,6},{3,7},{4,0},{5,1},{6,2},{7,3},{8,12},{9,13},{10,... | collective-permute-start | bytes 196616 | tf_op jit(solution)/shard_map/ppermute | solution.py:463
  28.2 6.7 %collective-permute-done.4.r13 = bf16[64,512]{1,0:T(8,128)(2,1)S(1)} collective-permute-done((bf16[64,512]{1,0:T(8,128)(2,1)S(1)}, bf16[64,512]{1,0:T(8,128)(2,1)S(1)}, u32[]{:S(2)}, u32[]{:S(2)}) %collective-permute-start.4) | collective-permute-done | bytes 65568 | tf_op jit(solution)/shard_map/ppermute | solution.py:463
  34.9 2.8 %projection.1 = (bf16[128,512]{1,0:T(8,128)(2,1)S(1)}, bf16[128,512]{1,0:T(8,128)(2,1)S(1)}) custom-call(bf16[64,2048]{1,0:T(8,128)(2,1)S(1)} %bitcast.18, bf16[64,2048]{1,0:T(8,128)(2,1)} %collective-permute-done.a1, bf16[64,2048]{1,0:T(8,128)(2,1)} %collective-permute-done.1.a2, bf16[64,2048]{1,0:T(8,128)(2,1)S(1)} %collective-permute-done.3.a3, ...), custom_call_target="tpu_custom_call" | custom-call | flops 1 | bytes 1 | tf_op jit(solution)/shard_map/projection/pallas_call | solution.py:436
  37.8 0.6 collective-permute-start.9
  38.3 1.5 %collective-permute-start.19 = (bf16[640,768]{1,0:T(8,128)(2,1)S(1)}, bf16[640,768]{1,0:T(8,128)(2,1)S(1)}, u32[]{:S(2)}, u32[]{:S(2)}) collective-permute-start(bf16[640,768]{1,0:T(8,128)(2,1)S(1)} %copy-done.9), channel_id=1, source_target_pairs={{0,16},{16,0},{1,17},{17,1},{2,18},{18,2},{3,19},{19,3},{4,20},{20... | collective-permute-start | bytes 2949128 | tf_op jit(solution)/shard_map/ppermute | solution.py:448
  39.9 1.1 collective-permute-done.8.early
  41.0 3.3 %collective-permute-done.9.arrived = bf16[128,512]{1,0:T(8,128)(2,1)S(1)} collective-permute-done((bf16[128,512]{1,0:T(8,128)(2,1)S(1)}, bf16[128,512]{1,0:T(8,128)(2,1)S(1)}, u32[]{:S(2)}, u32[]{:S(2)}) %collective-permute-start.9) | collective-permute-done | bytes 131104 | tf_op jit(solution)/shard_map/ppermute | solution.py:448
  44.3 3.5 %collective-permute-start.12 = (bf16[144,512]{1,0:T(8,128)(2,1)S(1)}, bf16[144,512]{1,0:T(8,128)(2,1)S(1)}, u32[]{:S(2)}, u32[]{:S(2)}) collective-permute-start(bf16[144,512]{1,0:T(8,128)(2,1)S(1)} %stream.1.b0), channel_id=1, source_target_pairs={{0,12},{1,13},{2,14},{3,15},{4,8},{5,9},{6,10},{7,11},{8,4},{9,5},... | collective-permute-start | bytes 442376 | tf_op jit(solution)/shard_map/ppermute | solution.py:463
  47.9 0.9 collective-permute-start.10
  48.8 1.6 %collective-permute-start.13 = (bf16[144,512]{1,0:T(8,128)(2,1)S(1)}, bf16[144,512]{1,0:T(8,128)(2,1)S(1)}, u32[]{:S(2)}, u32[]{:S(2)}) collective-permute-start(bf16[144,512]{1,0:T(8,128)(2,1)S(1)} %stream.1.b0), channel_id=1, source_target_pairs={{0,2},{1,3},{2,0},{3,1},{4,6},{5,7},{6,4},{7,5},{8,10},{9,11},{10,... | collective-permute-start | bytes 442376 | tf_op jit(solution)/shard_map/ppermute | solution.py:460
  50.3 2.6 %collective-permute-done.12.b3 = bf16[144,512]{1,0:T(8,128)(2,1)S(1)} collective-permute-done((bf16[144,512]{1,0:T(8,128)(2,1)S(1)}, bf16[144,512]{1,0:T(8,128)(2,1)S(1)}, u32[]{:S(2)}, u32[]{:S(2)}) %collective-permute-start.12) | collective-permute-done | bytes 147488 | tf_op jit(solution)/shard_map/ppermute | solution.py:463
  53.0 1.3 %collective-permute-start.16 = (bf16[144,512]{1,0:T(8,128)(2,1)S(1)}, bf16[144,512]{1,0:T(8,128)(2,1)S(1)}, u32[]{:S(2)}, u32[]{:S(2)}) collective-permute-start(bf16[144,512]{1,0:T(8,128)(2,1)S(1)} %collective-permute-done.12.b3), channel_id=1, source_target_pairs={{0,2},{1,3},{2,0},{3,1},{4,6},{5,7},{6,4},{7,5},{8,10},{9,11},{10,... | collective-permute-start | bytes 442376 | tf_op jit(solution)/shard_map/ppermute | solution.py:460
  54.2 4.5 %collective-permute-done.11.b2 = bf16[144,512]{1,0:T(8,128)(2,1)S(1)} collective-permute-done((bf16[144,512]{1,0:T(8,128)(2,1)S(1)}, bf16[144,512]{1,0:T(8,128)(2,1)S(1)}, u32[]{:S(2)}, u32[]{:S(2)}) %collective-permute-start.11) | collective-permute-done | bytes 147488 | tf_op jit(solution)/shard_map/ppermute | solution.py:463
  58.7 1.3 %collective-permute-start.15 = (bf16[144,512]{1,0:T(8,128)(2,1)S(1)}, bf16[144,512]{1,0:T(8,128)(2,1)S(1)}, u32[]{:S(2)}, u32[]{:S(2)}) collective-permute-start(bf16[144,512]{1,0:T(8,128)(2,1)S(1)} %collective-permute-done.11.b2), channel_id=1, source_target_pairs={{0,2},{1,3},{2,0},{3,1},{4,6},{5,7},{6,4},{7,5},{8,10},{9,11},{10,... | collective-permute-start | bytes 442376 | tf_op jit(solution)/shard_map/ppermute | solution.py:460
  60.0 0.7 collective-permute-start.14
  60.8 1.3 %collective-permute-start.20 = (bf16[384,768]{1,0:T(8,128)(2,1)S(1)}, bf16[384,768]{1,0:T(8,128)(2,1)S(1)}, u32[]{:S(2)}, u32[]{:S(2)}) collective-permute-start(bf16[384,768]{1,0:T(8,128)(2,1)S(1)} %copy-done.11), channel_id=1, source_target_pairs={{0,16},{16,0},{1,17},{17,1},{2,18},{18,2},{3,19},{19,3},{4,20},{20... | collective-permute-start | bytes 1769480 | tf_op jit(solution)/shard_map/ppermute | solution.py:448
  62.1 0.3 norm.2
  62.5 2.6 %collective-permute-done.15.b2 = bf16[144,512]{1,0:T(8,128)(2,1)S(1)} collective-permute-done((bf16[144,512]{1,0:T(8,128)(2,1)S(1)}, bf16[144,512]{1,0:T(8,128)(2,1)S(1)}, u32[]{:S(2)}, u32[]{:S(2)}) %collective-permute-start.15) | collective-permute-done | bytes 147488 | tf_op jit(solution)/shard_map/ppermute | solution.py:460
  65.2 1.6 %collective-permute-done.14.b1 = bf16[144,512]{1,0:T(8,128)(2,1)S(1)} collective-permute-done((bf16[144,512]{1,0:T(8,128)(2,1)S(1)}, bf16[144,512]{1,0:T(8,128)(2,1)S(1)}, u32[]{:S(2)}, u32[]{:S(2)}) %collective-permute-start.14) | collective-permute-done | bytes 147488 | tf_op jit(solution)/shard_map/ppermute | solution.py:460
  66.7 0.9 norm.3
  67.6 2.0 %collective-permute-done.17.group_cx = bf16[128,2176]{1,0:T(8,128)(2,1)S(1)} collective-permute-done((bf16[128,2176]{1,0:T(8,128)(2,1)S(1)}, bf16[128,2176]{1,0:T(8,128)(2,1)S(1)}, u32[]{:S(2)}, u32[]{:S(2)}) %collective-permute-start.17) | collective-permute-done | bytes 557088 | tf_op jit(solution)/shard_map/ppermute | solution.py:460
  69.6 3.4 %first_gate_up.1 = (bf16[384,384]{1,0:T(8,128)(2,1)S(1)}, bf16[128,384]{1,0:T(8,128)(2,1)S(1)}, f32[512,768]{1,0:T(8,128)S(1)}, bf16[512,1024]{1,0:T(8,128)(2,1)S(1)}, f32[512,128]{1,0:T(8,128)S(1)}) custom-call(bf16[128,2176]{1,0:T(8,128)(2,1)S(1)} %get-tuple-element.59.group_x, bf16[128,2176]{1,0:T(8,128)(2,1)S(1)} %collective-permute-done.17.group_cx, ...), custom_call_target="tpu_custom_call" | custom-call | flops 1 | bytes 1 | tf_op jit(solution)/shard_map/first_gate_up/pallas_call | solution.py:436
  73.0 1.4 %collective-permute-start.28 = (bf16[384,384]{1,0:T(8,128)(2,1)S(1)}, bf16[384,384]{1,0:T(8,128)(2,1)S(1)}, u32[]{:S(2)}, u32[]{:S(2)}) collective-permute-start(bf16[384,384]{1,0:T(8,128)(2,1)S(1)} %get-tuple-element.61.first), channel_id=1, source_target_pairs={{0,16},{16,0},{1,17},{17,1},{2,18},{18,2},{3,19},{19,3},{4,20},{20... | collective-permute-start | bytes 884744 | tf_op jit(solution)/shard_map/ppermute | solution.py:448
  74.4 3.1 %collective-permute-done.20.refs_1_ = bf16[384,768]{1,0:T(8,128)(2,1)S(1)} collective-permute-done((bf16[384,768]{1,0:T(8,128)(2,1)S(1)}, bf16[384,768]{1,0:T(8,128)(2,1)S(1)}, u32[]{:S(2)}, u32[]{:S(2)}) %collective-permute-start.20) | collective-permute-done | bytes 589856 | tf_op jit(solution)/shard_map/ppermute | solution.py:448
  77.4 1.5 %last_gate_up.1 = (bf16[256,384]{1,0:T(8,128)(2,1)S(1)}, bf16[384,384]{1,0:T(8,128)(2,1)S(1)}) custom-call(bf16[128,384]{1,0:T(8,128)(2,1)S(1)} %get-tuple-element.62.second, f32[512,768]{1,0:T(8,128)S(1)} %get-tuple-element.63.part, bf16[512,1024]{1,0:T(8,128)(2,1)S(1)} %get-tuple-element.64.other, f32[512,128]{1,0:T(8,128)S(1)} %get-tuple-element.65.share, ...), custom_call_target="tpu_custom_call" | custom-call | flops 1 | bytes 1 | tf_op jit(solution)/shard_map/last_gate_up/pallas_call | solution.py:436
  78.9 1.0 down_both.1
  80.0 0.5 collective-permute-start.22
  80.5 2.1 %collective-permute-start.29 = (bf16[256,384]{1,0:T(8,128)(2,1)S(1)}, bf16[256,384]{1,0:T(8,128)(2,1)S(1)}, u32[]{:S(2)}, u32[]{:S(2)}) collective-permute-start(bf16[256,384]{1,0:T(8,128)(2,1)S(1)} %get-tuple-element.68.far), channel_id=1, source_target_pairs={{0,16},{16,0},{1,17},{17,1},{2,18},{18,2},{3,19},{19,3},{4,20},{20... | collective-permute-start | bytes 589832 | tf_op jit(solution)/shard_map/ppermute | solution.py:448
  82.7 1.6 %collective-permute-start.23 = (bf16[128,1024]{1,0:T(8,128)(2,1)S(1)}, bf16[128,1024]{1,0:T(8,128)(2,1)S(1)}, u32[]{:S(2)}, u32[]{:S(2)}) collective-permute-start(bf16[128,1024]{1,0:T(8,128)(2,1)S(1)} %fold.2), channel_id=1, source_target_pairs={{0,2},{1,3},{2,0},{3,1},{4,6},{5,7},{6,4},{7,5},{8,10},{9,11},{10,... | collective-permute-start | bytes 786440 | tf_op jit(solution)/shard_map/ppermute | solution.py:460
  84.2 1.1 collective-permute-start.33
  85.3 2.8 %collective-permute-done.29.far = bf16[256,384]{1,0:T(8,128)(2,1)S(1)} collective-permute-done((bf16[256,384]{1,0:T(8,128)(2,1)S(1)}, bf16[256,384]{1,0:T(8,128)(2,1)S(1)}, u32[]{:S(2)}, u32[]{:S(2)}) %collective-permute-start.29) | collective-permute-done | bytes 196640 | tf_op jit(solution)/shard_map/ppermute | solution.py:448
  88.1 0.6 down.2
  88.7 0.6 collective-permute-start.30
  89.4 1.3 %collective-permute-done.23.far = bf16[128,1024]{1,0:T(8,128)(2,1)S(1)} collective-permute-done((bf16[128,1024]{1,0:T(8,128)(2,1)S(1)}, bf16[128,1024]{1,0:T(8,128)(2,1)S(1)}, u32[]{:S(2)}, u32[]{:S(2)}) %collective-permute-start.23) | collective-permute-done | bytes 262176 | tf_op jit(solution)/shard_map/ppermute | solution.py:460
  90.9 2.0 %collective-permute-start.32 = (bf16[128,1024]{1,0:T(8,128)(2,1)S(1)}, bf16[128,1024]{1,0:T(8,128)(2,1)S(1)}, u32[]{:S(2)}, u32[]{:S(2)}) collective-permute-start(bf16[128,1024]{1,0:T(8,128)(2,1)S(1)} %fold.3), channel_id=1, source_target_pairs={{0,2},{1,3},{2,0},{3,1},{4,6},{5,7},{6,4},{7,5},{8,10},{9,11},{10,... | collective-permute-start | bytes 786440 | tf_op jit(solution)/shard_map/ppermute | solution.py:460
  93.0 0.7 collective-permute-start.27
  93.6 3.7 %collective-permute-start.26 = (bf16[64,1024]{1,0:T(8,128)(2,1)S(1)}, bf16[64,1024]{1,0:T(8,128)(2,1)S(1)}, u32[]{:S(2)}, u32[]{:S(2)}) collective-permute-start(bf16[64,1024]{1,0:T(8,128)(2,1)S(1)} %get-tuple-element.77), channel_id=1, source_target_pairs={{0,12},{1,9},{2,14},{3,11},{4,8},{5,13},{6,10},{7,15},{8,4},{9,1},... | collective-permute-start | bytes 393224 | tf_op jit(solution)/shard_map/ppermute | solution.py:457
  97.3 0.6 down.3
  97.9 1.2 %collective-permute-start.34 = (bf16[128,512]{1,0:T(8,128)(2,1)S(1)}, bf16[128,512]{1,0:T(8,128)(2,1)S(1)}, u32[]{:S(2)}, u32[]{:S(2)}) collective-permute-start(bf16[128,512]{1,0:T(8,128)(2,1)S(1)} %get-tuple-element.84), channel_id=1, source_target_pairs={{0,1},{1,0},{2,3},{3,2},{4,5},{5,4},{6,7},{7,6},{8,9},{9,8},{10,11... | collective-permute-start | bytes 393224 | tf_op jit(solution)/shard_map/ppermute | solution.py:460
  99.2 2.4 %collective-permute-done.26.a0 = bf16[64,1024]{1,0:T(8,128)(2,1)S(1)} collective-permute-done((bf16[64,1024]{1,0:T(8,128)(2,1)S(1)}, bf16[64,1024]{1,0:T(8,128)(2,1)S(1)}, u32[]{:S(2)}, u32[]{:S(2)}) %collective-permute-start.26) | collective-permute-done | bytes 131104 | tf_op jit(solution)/shard_map/ppermute | solution.py:457
  101.7 4.7 %collective-permute-start.36 = (bf16[64,1024]{1,0:T(8,128)(2,1)S(1)}, bf16[64,1024]{1,0:T(8,128)(2,1)S(1)}, u32[]{:S(2)}, u32[]{:S(2)}) collective-permute-start(bf16[64,1024]{1,0:T(8,128)(2,1)S(1)} %get-tuple-element.86), channel_id=1, source_target_pairs={{0,28},{1,25},{2,30},{3,27},{4,24},{5,29},{6,26},{7,31},{8,20},{9,... | collective-permute-start | bytes 393224 | tf_op jit(solution)/shard_map/ppermute | solution.py:457
  106.4 0.5 collective-permute-start.37
  106.9 3.9 %collective-permute-done.36.b0 = bf16[64,1024]{1,0:T(8,128)(2,1)S(1)} collective-permute-done((bf16[64,1024]{1,0:T(8,128)(2,1)S(1)}, bf16[64,1024]{1,0:T(8,128)(2,1)S(1)}, u32[]{:S(2)}, u32[]{:S(2)}) %collective-permute-start.36) | collective-permute-done | bytes 131104 | tf_op jit(solution)/shard_map/ppermute | solution.py:457
  110.8 3.2 %collective-permute-done.37.b1 = bf16[64,1024]{1,0:T(8,128)(2,1)S(1)} collective-permute-done((bf16[64,1024]{1,0:T(8,128)(2,1)S(1)}, bf16[64,1024]{1,0:T(8,128)(2,1)S(1)}, u32[]{:S(2)}, u32[]{:S(2)}) %collective-permute-start.37) | collective-permute-done | bytes 131104 | tf_op jit(solution)/shard_map/ppermute | solution.py:457
  114.1 1.3 %collective-permute-done.38.core = bf16[64,1024]{1,0:T(8,128)(2,1)S(1)} collective-permute-done((bf16[64,1024]{1,0:T(8,128)(2,1)S(1)}, bf16[64,1024]{1,0:T(8,128)(2,1)S(1)}, u32[]{:S(2)}, u32[]{:S(2)}) %collective-permute-start.38) | collective-permute-done | bytes 131104 | tf_op jit(solution)/shard_map/ppermute | solution.py:460
  115.5 0.8 closing.1
  (63 shorter events, 1.2 us)
Async XLA Ops:
  0.6 1.9 %copy-start = (bf16[1,1024,1536]{2,1,0:T(8,128)(2,1)S(1)}, bf16[1,1024,1536]{2,1,0:T(8,128)(2,1)}, u32[]{:S(2)}) copy-start(bf16[1,1024,1536]{2,1,0:T(8,128)(2,1)} %param.17) | copy-start | bytes 9437188
  2.5 4.7 %copy-start.4 = (bf16[1,32,2048]{2,1,0:T(8,128)(2,1)S(1)}, bf16[1,32,2048]{2,1,0:T(8,128)(2,1)}, u32[]{:S(2)}) copy-start(bf16[1,32,2048]{2,1,0:T(8,128)(2,1)} %param.11) | copy-start | bytes 393220
  2.5 7.9 %copy-start.3 = (bf16[1,64,2048]{2,1,0:T(8,128)(2,1)S(1)}, bf16[1,64,2048]{2,1,0:T(8,128)(2,1)}, u32[]{:S(2)}) copy-start(bf16[1,64,2048]{2,1,0:T(8,128)(2,1)} %param.10) | copy-start | bytes 786436
  2.7 38.3 %collective-permute-start.8 = (bf16[1024,768]{1,0:T(8,128)(2,1)S(1)}, bf16[1024,768]{1,0:T(8,128)(2,1)S(1)}, u32[]{:S(2)}, u32[]{:S(2)}) collective-permute-start(bf16[1024,768]{1,0:T(8,128)(2,1)S(1)} %weight_piece.3), channel_id=1, source_target_pairs={{0,16},{16,0},{1,17},{17,1},{2,18},{18,2},{3,19},{19,3},{4,20},{20... | collective-permute-start | bytes 4718600 | tf_op jit(solution)/shard_map/ppermute | solution.py:448
  5.7 13.7 %collective-permute-start.5 = (bf16[2048,128]{1,0:T(8,128)(2,1)}, bf16[2048,128]{1,0:T(8,128)(2,1)}, u32[]{:S(2)}, u32[]{:S(2)}) collective-permute-start(bf16[2048,128]{1,0:T(8,128)(2,1)} %w0.1), channel_id=1, source_target_pairs={{0,2},{1,3},{2,0},{3,1},{4,6},{5,7},{6,4},{7,5},{8,10},{9,11},{10,... | collective-permute-start | bytes 1572872 | tf_op jit(solution)/shard_map/ppermute | solution.py:460
  7.9 4.7 %copy-start.6 = (bf16[32,512]{1,0:T(8,128)(2,1)}, bf16[32,512]{1,0:T(8,128)(2,1)S(1)}, u32[]{:S(2)}) copy-start(bf16[32,512]{1,0:T(8,128)(2,1)S(1)} %get-tuple-element.49) | copy-start | bytes 98308
  7.9 11.6 %collective-permute-start.2 = (bf16[64,512]{1,0:T(8,128)(2,1)}, bf16[64,512]{1,0:T(8,128)(2,1)S(1)}, u32[]{:S(2)}, u32[]{:S(2)}) collective-permute-start(bf16[64,512]{1,0:T(8,128)(2,1)} %get-tuple-element.47), channel_id=1, source_target_pairs={{0,8},{1,9},{2,10},{3,11},{4,12},{5,13},{6,14},{7,15},{8,0},{9,1},... | collective-permute-start | bytes 196616 | tf_op jit(solution)/shard_map/ppermute | solution.py:463
  10.5 4.6 %copy-start.12 = (s32[1,32,8]{1,2,0:T(8,128)S(1)}, s32[1,32,8]{1,2,0:T(8,128)}, u32[]{:S(2)}) copy-start(s32[1,32,8]{1,2,0:T(8,128)} %param.14) | copy-start | bytes 3076
  10.5 14.9 %collective-permute-start.1 = (bf16[64,2048]{1,0:T(8,128)(2,1)S(1)}, bf16[64,2048]{1,0:T(8,128)(2,1)}, u32[]{:S(2)}, u32[]{:S(2)}) collective-permute-start(bf16[64,2048]{1,0:T(8,128)(2,1)S(1)} %bitcast.16), channel_id=1, source_target_pairs={{0,8},{1,9},{2,10},{3,11},{4,12},{5,13},{6,14},{7,15},{8,0},{9,1},... | collective-permute-start | bytes 786440 | tf_op jit(solution)/shard_map/ppermute | solution.py:463
  10.8 14.5 %collective-permute-start = (bf16[64,2048]{1,0:T(8,128)(2,1)S(1)}, bf16[64,2048]{1,0:T(8,128)(2,1)}, u32[]{:S(2)}, u32[]{:S(2)}) collective-permute-start(bf16[64,2048]{1,0:T(8,128)(2,1)S(1)} %bitcast.17), channel_id=1, source_target_pairs={{0,4},{1,5},{2,6},{3,7},{4,0},{5,1},{6,2},{7,3},{8,12},{9,13},{10,... | collective-permute-start | bytes 786440 | tf_op jit(solution)/shard_map/ppermute | solution.py:463
  12.6 1.0 copy-start.8
  13.6 0.8 copy-start.10
  19.4 15.4 %collective-permute-start.7 = (bf16[2048,128]{1,0:T(8,128)(2,1)}, bf16[2048,128]{1,0:T(8,128)(2,1)S(1)}, u32[]{:S(2)}, u32[]{:S(2)}) collective-permute-start(bf16[2048,128]{1,0:T(8,128)(2,1)} %collective-permute-done.5.w2), channel_id=1, source_target_pairs={{0,1},{1,0},{2,3},{3,2},{4,5},{5,4},{6,7},{7,6},{8,9},{9,8},{10,11... | collective-permute-start | bytes 1572872 | tf_op jit(solution)/shard_map/ppermute | solution.py:460
  19.5 15.4 %collective-permute-start.6 = (bf16[2048,128]{1,0:T(8,128)(2,1)}, bf16[2048,128]{1,0:T(8,128)(2,1)S(1)}, u32[]{:S(2)}, u32[]{:S(2)}) collective-permute-start(bf16[2048,128]{1,0:T(8,128)(2,1)} %w0.1), channel_id=1, source_target_pairs={{0,1},{1,0},{2,3},{3,2},{4,5},{5,4},{6,7},{7,6},{8,9},{9,8},{10,11... | collective-permute-start | bytes 1572872 | tf_op jit(solution)/shard_map/ppermute | solution.py:460
  25.4 9.5 %collective-permute-start.3 = (bf16[64,2048]{1,0:T(8,128)(2,1)}, bf16[64,2048]{1,0:T(8,128)(2,1)S(1)}, u32[]{:S(2)}, u32[]{:S(2)}) collective-permute-start(bf16[64,2048]{1,0:T(8,128)(2,1)} %collective-permute-done.1.a2), channel_id=1, source_target_pairs={{0,4},{1,5},{2,6},{3,7},{4,0},{5,1},{6,2},{7,3},{8,12},{9,13},{10,... | collective-permute-start | bytes 786440 | tf_op jit(solution)/shard_map/ppermute | solution.py:463
  26.3 12.0 %copy-start.9 = (bf16[640,768]{1,0:T(8,128)(2,1)S(1)}, bf16[640,768]{1,0:T(8,128)(2,1)}, u32[]{:S(2)}) copy-start(bf16[640,768]{1,0:T(8,128)(2,1)} %copy-done.8) | copy-start | bytes 2949124
  26.3 34.4 %copy-start.11 = (bf16[384,768]{1,0:T(8,128)(2,1)S(1)}, bf16[384,768]{1,0:T(8,128)(2,1)}, u32[]{:S(2)}) copy-start(bf16[384,768]{1,0:T(8,128)(2,1)} %copy-done.10) | copy-start | bytes 1769476
  26.4 35.7 %copy-start.5 = (f32[2048]{0:T(1024)S(1)}, f32[2048]{0:T(1024)}, u32[]{:S(2)}) copy-start(f32[2048]{0:T(1024)} %param.13) | copy-start | bytes 24580
  26.4 8.5 %collective-permute-start.4 = (bf16[64,512]{1,0:T(8,128)(2,1)S(1)}, bf16[64,512]{1,0:T(8,128)(2,1)S(1)}, u32[]{:S(2)}, u32[]{:S(2)}) collective-permute-start(bf16[64,512]{1,0:T(8,128)(2,1)S(1)} %pad_maximum_fusion), channel_id=1, source_target_pairs={{0,4},{1,5},{2,6},{3,7},{4,0},{5,1},{6,2},{7,3},{8,12},{9,13},{10,... | collective-permute-start | bytes 196616 | tf_op jit(solution)/shard_map/ppermute | solution.py:463
  34.9 34.7 %copy-start.1 = (bf16[1,1024,1536]{2,1,0:T(8,128)(2,1)S(1)}, bf16[1,1024,1536]{2,1,0:T(8,128)(2,1)}, u32[]{:S(2)}) copy-start(bf16[1,1024,1536]{2,1,0:T(8,128)(2,1)} %param.17) | copy-start | bytes 9437188
  37.8 6.5 %collective-permute-start.9 = (bf16[128,512]{1,0:T(8,128)(2,1)S(1)}, bf16[128,512]{1,0:T(8,128)(2,1)S(1)}, u32[]{:S(2)}, u32[]{:S(2)}) collective-permute-start(bf16[128,512]{1,0:T(8,128)(2,1)S(1)} %get-tuple-element.56), channel_id=1, source_target_pairs={{0,16},{16,0},{1,17},{17,1},{2,18},{18,2},{3,19},{19,3},{4,20},{20... | collective-permute-start | bytes 393224 | tf_op jit(solution)/shard_map/ppermute | solution.py:448
  38.3 39.1 %collective-permute-start.19 = (bf16[640,768]{1,0:T(8,128)(2,1)S(1)}, bf16[640,768]{1,0:T(8,128)(2,1)S(1)}, u32[]{:S(2)}, u32[]{:S(2)}) collective-permute-start(bf16[640,768]{1,0:T(8,128)(2,1)S(1)} %copy-done.9), channel_id=1, source_target_pairs={{0,16},{16,0},{1,17},{17,1},{2,18},{18,2},{3,19},{19,3},{4,20},{20... | collective-permute-start | bytes 2949128 | tf_op jit(solution)/shard_map/ppermute | solution.py:448
  44.3 8.6 %collective-permute-start.12 = (bf16[144,512]{1,0:T(8,128)(2,1)S(1)}, bf16[144,512]{1,0:T(8,128)(2,1)S(1)}, u32[]{:S(2)}, u32[]{:S(2)}) collective-permute-start(bf16[144,512]{1,0:T(8,128)(2,1)S(1)} %stream.1.b0), channel_id=1, source_target_pairs={{0,12},{1,13},{2,14},{3,15},{4,8},{5,9},{6,10},{7,11},{8,4},{9,5},... | collective-permute-start | bytes 442376 | tf_op jit(solution)/shard_map/ppermute | solution.py:463
  47.8 10.9 %collective-permute-start.11 = (bf16[144,512]{1,0:T(8,128)(2,1)S(1)}, bf16[144,512]{1,0:T(8,128)(2,1)S(1)}, u32[]{:S(2)}, u32[]{:S(2)}) collective-permute-start(bf16[144,512]{1,0:T(8,128)(2,1)S(1)} %stream.1.b0), channel_id=1, source_target_pairs={{0,8},{1,9},{2,10},{3,11},{4,12},{5,13},{6,14},{7,15},{8,0},{9,1},... | collective-permute-start | bytes 442376 | tf_op jit(solution)/shard_map/ppermute | solution.py:463
  47.9 12.2 %collective-permute-start.10 = (bf16[144,512]{1,0:T(8,128)(2,1)S(1)}, bf16[144,512]{1,0:T(8,128)(2,1)S(1)}, u32[]{:S(2)}, u32[]{:S(2)}) collective-permute-start(bf16[144,512]{1,0:T(8,128)(2,1)S(1)} %stream.1.b0), channel_id=1, source_target_pairs={{0,4},{1,5},{2,6},{3,7},{4,0},{5,1},{6,2},{7,3},{8,12},{9,13},{10,... | collective-permute-start | bytes 442376 | tf_op jit(solution)/shard_map/ppermute | solution.py:463
  48.8 12.0 %collective-permute-start.13 = (bf16[144,512]{1,0:T(8,128)(2,1)S(1)}, bf16[144,512]{1,0:T(8,128)(2,1)S(1)}, u32[]{:S(2)}, u32[]{:S(2)}) collective-permute-start(bf16[144,512]{1,0:T(8,128)(2,1)S(1)} %stream.1.b0), channel_id=1, source_target_pairs={{0,2},{1,3},{2,0},{3,1},{4,6},{5,7},{6,4},{7,5},{8,10},{9,11},{10,... | collective-permute-start | bytes 442376 | tf_op jit(solution)/shard_map/ppermute | solution.py:460
  53.0 9.5 %collective-permute-start.16 = (bf16[144,512]{1,0:T(8,128)(2,1)S(1)}, bf16[144,512]{1,0:T(8,128)(2,1)S(1)}, u32[]{:S(2)}, u32[]{:S(2)}) collective-permute-start(bf16[144,512]{1,0:T(8,128)(2,1)S(1)} %collective-permute-done.12.b3), channel_id=1, source_target_pairs={{0,2},{1,3},{2,0},{3,1},{4,6},{5,7},{6,4},{7,5},{8,10},{9,11},{10,... | collective-permute-start | bytes 442376 | tf_op jit(solution)/shard_map/ppermute | solution.py:460
  58.7 6.4 %collective-permute-start.15 = (bf16[144,512]{1,0:T(8,128)(2,1)S(1)}, bf16[144,512]{1,0:T(8,128)(2,1)S(1)}, u32[]{:S(2)}, u32[]{:S(2)}) collective-permute-start(bf16[144,512]{1,0:T(8,128)(2,1)S(1)} %collective-permute-done.11.b2), channel_id=1, source_target_pairs={{0,2},{1,3},{2,0},{3,1},{4,6},{5,7},{6,4},{7,5},{8,10},{9,11},{10,... | collective-permute-start | bytes 442376 | tf_op jit(solution)/shard_map/ppermute | solution.py:460
  60.0 6.7 %collective-permute-start.14 = (bf16[144,512]{1,0:T(8,128)(2,1)S(1)}, bf16[144,512]{1,0:T(8,128)(2,1)S(1)}, u32[]{:S(2)}, u32[]{:S(2)}) collective-permute-start(bf16[144,512]{1,0:T(8,128)(2,1)S(1)} %collective-permute-done.10.b1), channel_id=1, source_target_pairs={{0,2},{1,3},{2,0},{3,1},{4,6},{5,7},{6,4},{7,5},{8,10},{9,11},{10,... | collective-permute-start | bytes 442376 | tf_op jit(solution)/shard_map/ppermute | solution.py:460
  60.8 16.7 %collective-permute-start.20 = (bf16[384,768]{1,0:T(8,128)(2,1)S(1)}, bf16[384,768]{1,0:T(8,128)(2,1)S(1)}, u32[]{:S(2)}, u32[]{:S(2)}) collective-permute-start(bf16[384,768]{1,0:T(8,128)(2,1)S(1)} %copy-done.11), channel_id=1, source_target_pairs={{0,16},{16,0},{1,17},{17,1},{2,18},{18,2},{3,19},{19,3},{4,20},{20... | collective-permute-start | bytes 1769480 | tf_op jit(solution)/shard_map/ppermute | solution.py:448
  62.4 5.2 %collective-permute-start.18 = (bf16[128,2176]{1,0:T(8,128)(2,1)S(1)}, bf16[128,2176]{1,0:T(8,128)(2,1)S(1)}, u32[]{:S(2)}, u32[]{:S(2)}) collective-permute-start(bf16[128,2176]{1,0:T(8,128)(2,1)S(1)} %get-tuple-element.60.group), channel_id=1, source_target_pairs={{0,1},{1,0},{2,3},{3,2},{4,5},{5,4},{6,7},{7,6},{8,9},{9,8},{10,11... | collective-permute-start | bytes 1671176 | tf_op jit(solution)/shard_map/ppermute | solution.py:460
  67.6 2.0 %collective-permute-start.17 = (bf16[128,2176]{1,0:T(8,128)(2,1)S(1)}, bf16[128,2176]{1,0:T(8,128)(2,1)S(1)}, u32[]{:S(2)}, u32[]{:S(2)}) collective-permute-start(bf16[128,2176]{1,0:T(8,128)(2,1)S(1)} %get-tuple-element.59.group_x), channel_id=1, source_target_pairs={{0,1},{1,0},{2,3},{3,2},{4,5},{5,4},{6,7},{7,6},{8,9},{9,8},{10,11... | collective-permute-start | bytes 1671176 | tf_op jit(solution)/shard_map/ppermute | solution.py:460
  73.0 15.1 %collective-permute-start.28 = (bf16[384,384]{1,0:T(8,128)(2,1)S(1)}, bf16[384,384]{1,0:T(8,128)(2,1)S(1)}, u32[]{:S(2)}, u32[]{:S(2)}) collective-permute-start(bf16[384,384]{1,0:T(8,128)(2,1)S(1)} %get-tuple-element.61.first), channel_id=1, source_target_pairs={{0,16},{16,0},{1,17},{17,1},{2,18},{18,2},{3,19},{19,3},{4,20},{20... | collective-permute-start | bytes 884744 | tf_op jit(solution)/shard_map/ppermute | solution.py:448
  77.4 1.5 %copy-start.2 = (bf16[1,768,1024]{2,1,0:T(8,128)(2,1)S(1)}, bf16[1,768,1024]{2,1,0:T(8,128)(2,1)}, u32[]{:S(2)}) copy-start(bf16[1,768,1024]{2,1,0:T(8,128)(2,1)} %param.18) | copy-start | bytes 4718596
  79.9 2.7 %collective-permute-start.21 = (bf16[128,512]{1,0:T(8,128)(2,1)S(1)}, bf16[128,512]{1,0:T(8,128)(2,1)S(1)}, u32[]{:S(2)}, u32[]{:S(2)}) collective-permute-start(bf16[128,512]{1,0:T(8,128)(2,1)S(1)} %get-tuple-element.71), channel_id=1, source_target_pairs={{0,1},{1,0},{2,3},{3,2},{4,5},{5,4},{6,7},{7,6},{8,9},{9,8},{10,11... | collective-permute-start | bytes 393224 | tf_op jit(solution)/shard_map/ppermute | solution.py:460
  80.0 2.6 %collective-permute-start.22 = (bf16[128,512]{1,0:T(8,128)(2,1)S(1)}, bf16[128,512]{1,0:T(8,128)(2,1)S(1)}, u32[]{:S(2)}, u32[]{:S(2)}) collective-permute-start(bf16[128,512]{1,0:T(8,128)(2,1)S(1)} %get-tuple-element.72), channel_id=1, source_target_pairs={{0,1},{1,0},{2,3},{3,2},{4,5},{5,4},{6,7},{7,6},{8,9},{9,8},{10,11... | collective-permute-start | bytes 393224 | tf_op jit(solution)/shard_map/ppermute | solution.py:460
  80.5 7.6 %collective-permute-start.29 = (bf16[256,384]{1,0:T(8,128)(2,1)S(1)}, bf16[256,384]{1,0:T(8,128)(2,1)S(1)}, u32[]{:S(2)}, u32[]{:S(2)}) collective-permute-start(bf16[256,384]{1,0:T(8,128)(2,1)S(1)} %get-tuple-element.68.far), channel_id=1, source_target_pairs={{0,16},{16,0},{1,17},{17,1},{2,18},{18,2},{3,19},{19,3},{4,20},{20... | collective-permute-start | bytes 589832 | tf_op jit(solution)/shard_map/ppermute | solution.py:448
  82.7 8.1 %collective-permute-start.23 = (bf16[128,1024]{1,0:T(8,128)(2,1)S(1)}, bf16[128,1024]{1,0:T(8,128)(2,1)S(1)}, u32[]{:S(2)}, u32[]{:S(2)}) collective-permute-start(bf16[128,1024]{1,0:T(8,128)(2,1)S(1)} %fold.2), channel_id=1, source_target_pairs={{0,2},{1,3},{2,0},{3,1},{4,6},{5,7},{6,4},{7,5},{8,10},{9,11},{10,... | collective-permute-start | bytes 786440 | tf_op jit(solution)/shard_map/ppermute | solution.py:460
  84.2 5.0 %collective-permute-start.24 = (bf16[128,512]{1,0:T(8,128)(2,1)S(1)}, bf16[128,512]{1,0:T(8,128)(2,1)S(1)}, u32[]{:S(2)}, u32[]{:S(2)}) collective-permute-start(bf16[128,512]{1,0:T(8,128)(2,1)S(1)} %get-tuple-element.74), channel_id=1, source_target_pairs={{0,1},{1,0},{2,3},{3,2},{4,5},{5,4},{6,7},{7,6},{8,9},{9,8},{10,11... | collective-permute-start | bytes 393224 | tf_op jit(solution)/shard_map/ppermute | solution.py:460
  84.2 13.1 %collective-permute-start.33 = (bf16[384,384]{1,0:T(8,128)(2,1)S(1)}, bf16[384,384]{1,0:T(8,128)(2,1)S(1)}, u32[]{:S(2)}, u32[]{:S(2)}) collective-permute-start(bf16[384,384]{1,0:T(8,128)(2,1)S(1)} %get-tuple-element.69.rest), channel_id=1, source_target_pairs={{0,16},{16,0},{1,17},{17,1},{2,18},{18,2},{3,19},{19,3},{4,20},{20... | collective-permute-start | bytes 884744 | tf_op jit(solution)/shard_map/ppermute | solution.py:448
  88.1 1.3 %collective-permute-start.25 = (bf16[128,512]{1,0:T(8,128)(2,1)S(1)}, bf16[128,512]{1,0:T(8,128)(2,1)S(1)}, u32[]{:S(2)}, u32[]{:S(2)}) collective-permute-start(bf16[128,512]{1,0:T(8,128)(2,1)S(1)} %get-tuple-element.75), channel_id=1, source_target_pairs={{0,1},{1,0},{2,3},{3,2},{4,5},{5,4},{6,7},{7,6},{8,9},{9,8},{10,11... | collective-permute-start | bytes 393224 | tf_op jit(solution)/shard_map/ppermute | solution.py:460
  88.7 2.2 %collective-permute-start.30 = (bf16[128,512]{1,0:T(8,128)(2,1)S(1)}, bf16[128,512]{1,0:T(8,128)(2,1)S(1)}, u32[]{:S(2)}, u32[]{:S(2)}) collective-permute-start(bf16[128,512]{1,0:T(8,128)(2,1)S(1)} %get-tuple-element.80), channel_id=1, source_target_pairs={{0,1},{1,0},{2,3},{3,2},{4,5},{5,4},{6,7},{7,6},{8,9},{9,8},{10,11... | collective-permute-start | bytes 393224 | tf_op jit(solution)/shard_map/ppermute | solution.py:460
  89.2 1.6 %collective-permute-start.31 = (bf16[128,512]{1,0:T(8,128)(2,1)S(1)}, bf16[128,512]{1,0:T(8,128)(2,1)S(1)}, u32[]{:S(2)}, u32[]{:S(2)}) collective-permute-start(bf16[128,512]{1,0:T(8,128)(2,1)S(1)} %get-tuple-element.81), channel_id=1, source_target_pairs={{0,1},{1,0},{2,3},{3,2},{4,5},{5,4},{6,7},{7,6},{8,9},{9,8},{10,11... | collective-permute-start | bytes 393224 | tf_op jit(solution)/shard_map/ppermute | solution.py:460
  90.9 10.7 %collective-permute-start.32 = (bf16[128,1024]{1,0:T(8,128)(2,1)S(1)}, bf16[128,1024]{1,0:T(8,128)(2,1)S(1)}, u32[]{:S(2)}, u32[]{:S(2)}) collective-permute-start(bf16[128,1024]{1,0:T(8,128)(2,1)S(1)} %fold.3), channel_id=1, source_target_pairs={{0,2},{1,3},{2,0},{3,1},{4,6},{5,7},{6,4},{7,5},{8,10},{9,11},{10,... | collective-permute-start | bytes 786440 | tf_op jit(solution)/shard_map/ppermute | solution.py:460
  93.0 8.6 %collective-permute-start.27 = (bf16[64,1024]{1,0:T(8,128)(2,1)S(1)}, bf16[64,1024]{1,0:T(8,128)(2,1)S(1)}, u32[]{:S(2)}, u32[]{:S(2)}) collective-permute-start(bf16[64,1024]{1,0:T(8,128)(2,1)S(1)} %get-tuple-element.76.own), channel_id=1, source_target_pairs={{1,5},{3,7},{5,1},{7,3},{9,13},{11,15},{13,9},{15,11},{17,21},{19,... | collective-permute-start | bytes 393224 | tf_op jit(solution)/shard_map/ppermute | solution.py:457
  93.6 21.8 %copy-start.7 = (f32[2048]{0:T(1024)S(1)}, f32[2048]{0:T(1024)}, u32[]{:S(2)}) copy-start(f32[2048]{0:T(1024)} %param.19) | copy-start | bytes 24580
  93.6 7.9 %collective-permute-start.26 = (bf16[64,1024]{1,0:T(8,128)(2,1)S(1)}, bf16[64,1024]{1,0:T(8,128)(2,1)S(1)}, u32[]{:S(2)}, u32[]{:S(2)}) collective-permute-start(bf16[64,1024]{1,0:T(8,128)(2,1)S(1)} %get-tuple-element.77), channel_id=1, source_target_pairs={{0,12},{1,9},{2,14},{3,11},{4,8},{5,13},{6,10},{7,15},{8,4},{9,1},... | collective-permute-start | bytes 393224 | tf_op jit(solution)/shard_map/ppermute | solution.py:457
  97.9 3.7 %collective-permute-start.34 = (bf16[128,512]{1,0:T(8,128)(2,1)S(1)}, bf16[128,512]{1,0:T(8,128)(2,1)S(1)}, u32[]{:S(2)}, u32[]{:S(2)}) collective-permute-start(bf16[128,512]{1,0:T(8,128)(2,1)S(1)} %get-tuple-element.84), channel_id=1, source_target_pairs={{0,1},{1,0},{2,3},{3,2},{4,5},{5,4},{6,7},{7,6},{8,9},{9,8},{10,11... | collective-permute-start | bytes 393224 | tf_op jit(solution)/shard_map/ppermute | solution.py:460
  99.1 2.5 %collective-permute-start.35 = (bf16[128,512]{1,0:T(8,128)(2,1)S(1)}, bf16[128,512]{1,0:T(8,128)(2,1)S(1)}, u32[]{:S(2)}, u32[]{:S(2)}) collective-permute-start(bf16[128,512]{1,0:T(8,128)(2,1)S(1)} %get-tuple-element.85), channel_id=1, source_target_pairs={{0,1},{1,0},{2,3},{3,2},{4,5},{5,4},{6,7},{7,6},{8,9},{9,8},{10,11... | collective-permute-start | bytes 393224 | tf_op jit(solution)/shard_map/ppermute | solution.py:460
  101.7 9.1 %collective-permute-start.36 = (bf16[64,1024]{1,0:T(8,128)(2,1)S(1)}, bf16[64,1024]{1,0:T(8,128)(2,1)S(1)}, u32[]{:S(2)}, u32[]{:S(2)}) collective-permute-start(bf16[64,1024]{1,0:T(8,128)(2,1)S(1)} %get-tuple-element.86), channel_id=1, source_target_pairs={{0,28},{1,25},{2,30},{3,27},{4,24},{5,29},{6,26},{7,31},{8,20},{9,... | collective-permute-start | bytes 393224 | tf_op jit(solution)/shard_map/ppermute | solution.py:457
  106.4 7.6 %collective-permute-start.37 = (bf16[64,1024]{1,0:T(8,128)(2,1)S(1)}, bf16[64,1024]{1,0:T(8,128)(2,1)S(1)}, u32[]{:S(2)}, u32[]{:S(2)}) collective-permute-start(bf16[64,1024]{1,0:T(8,128)(2,1)S(1)} %get-tuple-element.87), channel_id=1, source_target_pairs={{0,16},{1,21},{2,18},{3,23},{4,20},{5,17},{6,22},{7,19},{8,24},{9,... | collective-permute-start | bytes 393224 | tf_op jit(solution)/shard_map/ppermute | solution.py:457
  114.0 1.4 %collective-permute-start.38 = (bf16[64,1024]{1,0:T(8,128)(2,1)S(1)}, bf16[64,1024]{1,0:T(8,128)(2,1)S(1)}, u32[]{:S(2)}, u32[]{:S(2)}) collective-permute-start(bf16[64,1024]{1,0:T(8,128)(2,1)S(1)} %get-tuple-element.89), channel_id=1, source_target_pairs={{0,1},{1,0},{2,3},{3,2},{4,5},{5,4},{6,7},{7,6},{8,9},{9,8},{10,11... | collective-permute-start | bytes 393224 | tf_op jit(solution)/shard_map/ppermute | solution.py:460

commit v18 on v14

--- a/solution.py
+++ b/solution.py
@@ -327,11 +327,11 @@
         for i in range(2):
             for j in range(2):
                 ref, start = places[j]
-                kept = aligned(start // small + ((outer + 2 * core + i) & 3), small)
+                kept = aligned(start // small + ((outer + 2 * core + 1 - i) & 3), small)
                 at = (2 * i + j) * small
                 rows[at : at + small, cols] = ref[kept, :]
                 ref, start = places[1 - j]
-                sent = aligned(start // small + ((outer + 2 - 2 * core + i) & 3), small)
+                sent = aligned(start // small + ((outer + 3 - 2 * core - i) & 3), small)
                 rows[count + at : count + at + small, cols] = ref[sent, :]
     for at in range(0, wd.shape[1], 256):
         value = dot(rows[...], wd[:, at : at + 256]).astype(BF16)
@@ -391,8 +391,8 @@
 def gather_kernel(own, a0, a1, b0, b1, keep_ref, send_ref):
     expert, outer, inner, dp = seat()
     small = own.shape[0] // 2
-    start = jnp.where((inner & 1) == 0, own[...].astype(F32), a0[...].astype(F32))
-    for i, total in enumerate((start + a1[...].astype(F32), b0[...].astype(F32) + b1[...].astype(F32))):
+    last = jnp.where((inner & 1) == 0, own[...].astype(F32), a1[...].astype(F32))
+    for i, total in enumerate((a0[...].astype(F32) + last, b0[...].astype(F32) + b1[...].astype(F32))):
         rows = slice(i * small, (i + 1) * small)
         keep_ref[rows, :] = total[:small]
         send_ref[rows, :] = total[small:].astype(BF16)
@@ -456,7 +456,7 @@
         pairs = []
         for at in range(2 * expert_count):
             d, e = divmod(at, expert_count)
-            step = 2 * (e % 2) + i
+            step = 2 * (e % 2) + 1 - i
             if step or cross:
                 pairs.append((at, (d ^ cross) * expert_count + (e + 4 * step) % expert_count))
         return lax.ppermute(x, ("dp", "expert"), pairs)
@@ -617,8 +617,8 @@
     )
     far = swap_inner(fold(keep_far, swap_cores(send[:2])), 2)
     first_far = far
-    own, second = pieces(far, keep_near, send[2:])
-    mine = [send_outer(own, 0, False), send_outer(second, 1, False)]
+    first, own = pieces(far, keep_near, send[2:])
+    mine = [send_outer(first, 0, False), send_outer(own, 1, False)]
 
     keep_far, send = down(down_far_kernel, far_other, 2)
     far = swap_inner(fold(after(keep_far, own), swap_cores(send)), 2)

time: 115 us -> 116 us (level)
  starting transfers between devices: 41.7 us -> 43.9 us
  waiting for transfers between devices: 52.5 us -> 51.1 us
    ppermute x20, starting transfers between devices: 15.6 us -> 18.2 us  [swap_inner(): return lax.ppermute(x, 'expert', [(i, i ^ j) for i in range(expert_count)])]
  transfers between devices with their start and end apart: 39 -> 39, of which waited for: 18 -> 17; matrix products, arithmetic and copies ran while one was open for 1% -> 1% of each run, Pallas kernels for 11% -> 11%
where the time goes in v18:
time: 116 us
  waiting for transfers between devices  51.1 us (44%)
  starting transfers between devices  43.9 us (38%)
  Pallas kernels  13.8 us (12%)
  local copies, waits for them, and re-layouts  4.58 us (4%)
  between operations  1.56 us (1%)
    ppermute x20, starting transfers between devices, swap_inner(): return lax.ppermute(x, 'expert', [(i, i ^ j) for i in range(expert_count)])  18.2 us
    pallas_call x17, Pallas kernels, call(): pl.pallas_call(kernel, out_shape=outs, in_specs=[first] + [vmem] * (len(a...  13.4 us
    ppermute x5, waiting for transfers between devices, swap_outer(): lax.ppermute(x, 'expert', [(i, i ^ 4 * s) for i in range(expert_count)])  12.1 us
    ppermute x20, waiting for transfers between devices, swap_inner(): return lax.ppermute(x, 'expert', [(i, i ^ j) for i in range(expert_count)])  11.3 us
    ppermute x7, starting transfers between devices, swap_dp(): return lax.ppermute(x, 'dp', [(0, 1), (1, 0)])  10.7 us
    ppermute x4, waiting for transfers between devices, send_outer(): return lax.ppermute(x, ('dp', 'expert'), pairs)  10.2 us
    ppermute x7, waiting for transfers between devices, swap_dp(): return lax.ppermute(x, 'dp', [(0, 1), (1, 0)])  9.83 us
    ppermute x3, waiting for transfers between devices, shift_outer(): lax.ppermute(x, 'expert', [(i, (i + 4 * s) % expert_count) for i in range...  7.64 us
  transfers between devices with their start and end apart: 39, of which 17 were waited for; matrix products, arithmetic and copies ran while one was open for 1% of the time, Pallas kernels for 11%

profile of v18, /device:TPU:0, one launch (start us, length us, event | category | flops | bytes accessed | tf_op | source)
XLA Modules:
  0.0 115.6 jit_solution(2383183027707236613)
XLA Ops:
  0.6 1.9 %copy-done = bf16[1,1024,1536]{2,1,0:T(8,128)(2,1)S(1)} copy-done((bf16[1,1024,1536]{2,1,0:T(8,128)(2,1)S(1)}, bf16[1,1024,1536]{2,1,0:T(8,128)(2,1)}, u32[]{:S(2)}) %copy-start) | copy-done | bytes 3145752
  2.5 0.2 weight_piece.3
  2.7 3.0 %collective-permute-start.8 = (bf16[1024,768]{1,0:T(8,128)(2,1)S(1)}, bf16[1024,768]{1,0:T(8,128)(2,1)S(1)}, u32[]{:S(2)}, u32[]{:S(2)}) collective-permute-start(bf16[1024,768]{1,0:T(8,128)(2,1)S(1)} %weight_piece.3), channel_id=1, source_target_pairs={{0,16},{16,0},{1,17},{17,1},{2,18},{18,2},{3,19},{19,3},{4,20},{20... | collective-permute-start | bytes 4718600 | tf_op jit(solution)/shard_map/ppermute | solution.py:448
  5.7 1.5 %collective-permute-start.5 = (bf16[2048,128]{1,0:T(8,128)(2,1)}, bf16[2048,128]{1,0:T(8,128)(2,1)}, u32[]{:S(2)}, u32[]{:S(2)}) collective-permute-start(bf16[2048,128]{1,0:T(8,128)(2,1)} %w0.1), channel_id=1, source_target_pairs={{0,2},{1,3},{2,0},{3,1},{4,6},{5,7},{6,4},{7,5},{8,10},{9,11},{10,... | collective-permute-start | bytes 1572872 | tf_op jit(solution)/shard_map/ppermute | solution.py:465
  7.2 0.6 cut_resid.1
  7.9 2.6 %collective-permute-start.2 = (bf16[64,512]{1,0:T(8,128)(2,1)}, bf16[64,512]{1,0:T(8,128)(2,1)S(1)}, u32[]{:S(2)}, u32[]{:S(2)}) collective-permute-start(bf16[64,512]{1,0:T(8,128)(2,1)} %get-tuple-element.47), channel_id=1, source_target_pairs={{0,8},{1,9},{2,10},{3,11},{4,12},{5,13},{6,14},{7,15},{8,0},{9,1},... | collective-permute-start | bytes 196616 | tf_op jit(solution)/shard_map/ppermute | solution.py:468
  10.5 0.3 collective-permute-start.1
  10.8 1.6 %collective-permute-start = (bf16[64,2048]{1,0:T(8,128)(2,1)S(1)}, bf16[64,2048]{1,0:T(8,128)(2,1)}, u32[]{:S(2)}, u32[]{:S(2)}) collective-permute-start(bf16[64,2048]{1,0:T(8,128)(2,1)S(1)} %bitcast.17), channel_id=1, source_target_pairs={{0,4},{1,5},{2,6},{3,7},{4,0},{5,1},{6,2},{7,3},{8,12},{9,13},{10,... | collective-permute-start | bytes 786440 | tf_op jit(solution)/shard_map/ppermute | solution.py:468
  12.4 0.2 weight_piece.2
  12.6 1.0 copy-done.8
  13.6 0.8 copy-done.10
  15.2 0.8 copy.13
  15.9 0.4 share.1
  16.4 3.1 %collective-permute-done.5.w2 = bf16[2048,128]{1,0:T(8,128)(2,1)} collective-permute-done((bf16[2048,128]{1,0:T(8,128)(2,1)}, bf16[2048,128]{1,0:T(8,128)(2,1)}, u32[]{:S(2)}, u32[]{:S(2)}) %collective-permute-start.5) | collective-permute-done | bytes 524320 | tf_op jit(solution)/shard_map/ppermute | solution.py:465
  19.5 0.5 collective-permute-start.6
  20.0 5.4 %collective-permute-done.1.a2 = bf16[64,2048]{1,0:T(8,128)(2,1)} collective-permute-done((bf16[64,2048]{1,0:T(8,128)(2,1)S(1)}, bf16[64,2048]{1,0:T(8,128)(2,1)}, u32[]{:S(2)}, u32[]{:S(2)}) %collective-permute-start.1) | collective-permute-done | bytes 262176 | tf_op jit(solution)/shard_map/ppermute | solution.py:468
  25.4 0.2 collective-permute-start.3
  25.6 0.8 pad_maximum_fusion
  26.4 1.9 %collective-permute-start.4 = (bf16[64,512]{1,0:T(8,128)(2,1)S(1)}, bf16[64,512]{1,0:T(8,128)(2,1)S(1)}, u32[]{:S(2)}, u32[]{:S(2)}) collective-permute-start(bf16[64,512]{1,0:T(8,128)(2,1)S(1)} %pad_maximum_fusion), channel_id=1, source_target_pairs={{0,4},{1,5},{2,6},{3,7},{4,0},{5,1},{6,2},{7,3},{8,12},{9,13},{10,... | collective-permute-start | bytes 196616 | tf_op jit(solution)/shard_map/ppermute | solution.py:468
  28.2 6.7 %collective-permute-done.4.r13 = bf16[64,512]{1,0:T(8,128)(2,1)S(1)} collective-permute-done((bf16[64,512]{1,0:T(8,128)(2,1)S(1)}, bf16[64,512]{1,0:T(8,128)(2,1)S(1)}, u32[]{:S(2)}, u32[]{:S(2)}) %collective-permute-start.4) | collective-permute-done | bytes 65568 | tf_op jit(solution)/shard_map/ppermute | solution.py:468
  34.9 2.8 %projection.1 = (bf16[128,512]{1,0:T(8,128)(2,1)S(1)}, bf16[128,512]{1,0:T(8,128)(2,1)S(1)}) custom-call(bf16[64,2048]{1,0:T(8,128)(2,1)S(1)} %bitcast.18, bf16[64,2048]{1,0:T(8,128)(2,1)} %collective-permute-done.a1, bf16[64,2048]{1,0:T(8,128)(2,1)} %collective-permute-done.1.a2, bf16[64,2048]{1,0:T(8,128)(2,1)S(1)} %collective-permute-done.3.a3, ...), custom_call_target="tpu_custom_call" | custom-call | flops 1 | bytes 1 | tf_op jit(solution)/shard_map/projection/pallas_call | solution.py:436
  37.8 0.6 collective-permute-start.9
  38.3 1.5 %collective-permute-start.19 = (bf16[640,768]{1,0:T(8,128)(2,1)S(1)}, bf16[640,768]{1,0:T(8,128)(2,1)S(1)}, u32[]{:S(2)}, u32[]{:S(2)}) collective-permute-start(bf16[640,768]{1,0:T(8,128)(2,1)S(1)} %copy-done.9), channel_id=1, source_target_pairs={{0,16},{16,0},{1,17},{17,1},{2,18},{18,2},{3,19},{19,3},{4,20},{20... | collective-permute-start | bytes 2949128 | tf_op jit(solution)/shard_map/ppermute | solution.py:448
  39.9 1.1 collective-permute-done.8.early
  41.0 3.3 %collective-permute-done.9.arrived = bf16[128,512]{1,0:T(8,128)(2,1)S(1)} collective-permute-done((bf16[128,512]{1,0:T(8,128)(2,1)S(1)}, bf16[128,512]{1,0:T(8,128)(2,1)S(1)}, u32[]{:S(2)}, u32[]{:S(2)}) %collective-permute-start.9) | collective-permute-done | bytes 131104 | tf_op jit(solution)/shard_map/ppermute | solution.py:448
  44.3 3.5 %collective-permute-start.12 = (bf16[144,512]{1,0:T(8,128)(2,1)S(1)}, bf16[144,512]{1,0:T(8,128)(2,1)S(1)}, u32[]{:S(2)}, u32[]{:S(2)}) collective-permute-start(bf16[144,512]{1,0:T(8,128)(2,1)S(1)} %stream.1.b0), channel_id=1, source_target_pairs={{0,12},{1,13},{2,14},{3,15},{4,0},{5,1},{6,2},{7,3},{8,4},{9,5},{1... | collective-permute-start | bytes 442376 | tf_op jit(solution)/shard_map/ppermute | solution.py:451
  47.8 0.8 collective-permute-start.10
  48.7 1.9 %collective-permute-start.13 = (bf16[144,512]{1,0:T(8,128)(2,1)S(1)}, bf16[144,512]{1,0:T(8,128)(2,1)S(1)}, u32[]{:S(2)}, u32[]{:S(2)}) collective-permute-start(bf16[144,512]{1,0:T(8,128)(2,1)S(1)} %stream.1.b0), channel_id=1, source_target_pairs={{0,2},{1,3},{2,0},{3,1},{4,6},{5,7},{6,4},{7,5},{8,10},{9,11},{10,... | collective-permute-start | bytes 442376 | tf_op jit(solution)/shard_map/ppermute | solution.py:465
  50.5 1.6 %collective-permute-done.12.b3 = bf16[144,512]{1,0:T(8,128)(2,1)S(1)} collective-permute-done((bf16[144,512]{1,0:T(8,128)(2,1)S(1)}, bf16[144,512]{1,0:T(8,128)(2,1)S(1)}, u32[]{:S(2)}, u32[]{:S(2)}) %collective-permute-start.12) | collective-permute-done | bytes 147488 | tf_op jit(solution)/shard_map/ppermute | solution.py:451
  52.1 1.7 %collective-permute-start.16 = (bf16[144,512]{1,0:T(8,128)(2,1)S(1)}, bf16[144,512]{1,0:T(8,128)(2,1)S(1)}, u32[]{:S(2)}, u32[]{:S(2)}) collective-permute-start(bf16[144,512]{1,0:T(8,128)(2,1)S(1)} %collective-permute-done.12.b3), channel_id=1, source_target_pairs={{0,2},{1,3},{2,0},{3,1},{4,6},{5,7},{6,4},{7,5},{8,10},{9,11},{10,... | collective-permute-start | bytes 442376 | tf_op jit(solution)/shard_map/ppermute | solution.py:465
  53.8 6.0 %collective-permute-done.11.b2 = bf16[144,512]{1,0:T(8,128)(2,1)S(1)} collective-permute-done((bf16[144,512]{1,0:T(8,128)(2,1)S(1)}, bf16[144,512]{1,0:T(8,128)(2,1)S(1)}, u32[]{:S(2)}, u32[]{:S(2)}) %collective-permute-start.11) | collective-permute-done | bytes 147488 | tf_op jit(solution)/shard_map/ppermute | solution.py:451
  59.9 1.1 collective-permute-start.15
  61.0 0.9 collective-permute-start.14
  61.9 1.2 collective-permute-start.20
  63.1 0.3 norm.2
  63.5 2.3 %collective-permute-done.15.b2 = bf16[144,512]{1,0:T(8,128)(2,1)S(1)} collective-permute-done((bf16[144,512]{1,0:T(8,128)(2,1)S(1)}, bf16[144,512]{1,0:T(8,128)(2,1)S(1)}, u32[]{:S(2)}, u32[]{:S(2)}) %collective-permute-start.15) | collective-permute-done | bytes 147488 | tf_op jit(solution)/shard_map/ppermute | solution.py:465
  65.8 1.6 %collective-permute-done.14.b1 = bf16[144,512]{1,0:T(8,128)(2,1)S(1)} collective-permute-done((bf16[144,512]{1,0:T(8,128)(2,1)S(1)}, bf16[144,512]{1,0:T(8,128)(2,1)S(1)}, u32[]{:S(2)}, u32[]{:S(2)}) %collective-permute-start.14) | collective-permute-done | bytes 147488 | tf_op jit(solution)/shard_map/ppermute | solution.py:465
  67.3 0.8 norm.3
  68.1 2.0 %collective-permute-done.17.group_cx = bf16[128,2176]{1,0:T(8,128)(2,1)S(1)} collective-permute-done((bf16[128,2176]{1,0:T(8,128)(2,1)S(1)}, bf16[128,2176]{1,0:T(8,128)(2,1)S(1)}, u32[]{:S(2)}, u32[]{:S(2)}) %collective-permute-start.17) | collective-permute-done | bytes 557088 | tf_op jit(solution)/shard_map/ppermute | solution.py:465
  70.1 3.4 %first_gate_up.1 = (bf16[384,384]{1,0:T(8,128)(2,1)S(1)}, bf16[128,384]{1,0:T(8,128)(2,1)S(1)}, f32[512,768]{1,0:T(8,128)S(1)}, bf16[512,1024]{1,0:T(8,128)(2,1)S(1)}, f32[512,128]{1,0:T(8,128)S(1)}) custom-call(bf16[128,2176]{1,0:T(8,128)(2,1)S(1)} %get-tuple-element.59.group_x, bf16[128,2176]{1,0:T(8,128)(2,1)S(1)} %collective-permute-done.17.group_cx, ...), custom_call_target="tpu_custom_call" | custom-call | flops 1 | bytes 1 | tf_op jit(solution)/shard_map/first_gate_up/pallas_call | solution.py:436
  73.5 0.9 collective-permute-start.28
  74.4 2.6 %collective-permute-done.20.refs_1_ = bf16[384,768]{1,0:T(8,128)(2,1)S(1)} collective-permute-done((bf16[384,768]{1,0:T(8,128)(2,1)S(1)}, bf16[384,768]{1,0:T(8,128)(2,1)S(1)}, u32[]{:S(2)}, u32[]{:S(2)}) %collective-permute-start.20) | collective-permute-done | bytes 589856 | tf_op jit(solution)/shard_map/ppermute | solution.py:448
  77.1 1.5 %last_gate_up.1 = (bf16[256,384]{1,0:T(8,128)(2,1)S(1)}, bf16[384,384]{1,0:T(8,128)(2,1)S(1)}) custom-call(bf16[128,384]{1,0:T(8,128)(2,1)S(1)} %get-tuple-element.62.second, f32[512,768]{1,0:T(8,128)S(1)} %get-tuple-element.63.part, bf16[512,1024]{1,0:T(8,128)(2,1)S(1)} %get-tuple-element.64.other, f32[512,128]{1,0:T(8,128)S(1)} %get-tuple-element.65.share, ...), custom_call_target="tpu_custom_call" | custom-call | flops 1 | bytes 1 | tf_op jit(solution)/shard_map/last_gate_up/pallas_call | solution.py:436
  78.5 1.0 down_both.1
  79.6 0.5 collective-permute-start.22
  80.1 2.5 %collective-permute-start.29 = (bf16[256,384]{1,0:T(8,128)(2,1)S(1)}, bf16[256,384]{1,0:T(8,128)(2,1)S(1)}, u32[]{:S(2)}, u32[]{:S(2)}) collective-permute-start(bf16[256,384]{1,0:T(8,128)(2,1)S(1)} %get-tuple-element.68.far), channel_id=1, source_target_pairs={{0,16},{16,0},{1,17},{17,1},{2,18},{18,2},{3,19},{19,3},{4,20},{20... | collective-permute-start | bytes 589832 | tf_op jit(solution)/shard_map/ppermute | solution.py:448
  82.7 1.6 %collective-permute-start.23 = (bf16[128,1024]{1,0:T(8,128)(2,1)S(1)}, bf16[128,1024]{1,0:T(8,128)(2,1)S(1)}, u32[]{:S(2)}, u32[]{:S(2)}) collective-permute-start(bf16[128,1024]{1,0:T(8,128)(2,1)S(1)} %fold.2), channel_id=1, source_target_pairs={{0,2},{1,3},{2,0},{3,1},{4,6},{5,7},{6,4},{7,5},{8,10},{9,11},{10,... | collective-permute-start | bytes 786440 | tf_op jit(solution)/shard_map/ppermute | solution.py:465
  84.2 1.1 collective-permute-start.33
  85.3 2.8 %collective-permute-done.29.far = bf16[256,384]{1,0:T(8,128)(2,1)S(1)} collective-permute-done((bf16[256,384]{1,0:T(8,128)(2,1)S(1)}, bf16[256,384]{1,0:T(8,128)(2,1)S(1)}, u32[]{:S(2)}, u32[]{:S(2)}) %collective-permute-start.29) | collective-permute-done | bytes 196640 | tf_op jit(solution)/shard_map/ppermute | solution.py:448
  88.1 0.6 down.2
  88.7 0.6 collective-permute-start.30
  89.4 1.3 %collective-permute-done.23.far = bf16[128,1024]{1,0:T(8,128)(2,1)S(1)} collective-permute-done((bf16[128,1024]{1,0:T(8,128)(2,1)S(1)}, bf16[128,1024]{1,0:T(8,128)(2,1)S(1)}, u32[]{:S(2)}, u32[]{:S(2)}) %collective-permute-start.23) | collective-permute-done | bytes 262176 | tf_op jit(solution)/shard_map/ppermute | solution.py:465
  90.9 2.0 %collective-permute-start.32 = (bf16[128,1024]{1,0:T(8,128)(2,1)S(1)}, bf16[128,1024]{1,0:T(8,128)(2,1)S(1)}, u32[]{:S(2)}, u32[]{:S(2)}) collective-permute-start(bf16[128,1024]{1,0:T(8,128)(2,1)S(1)} %fold.3), channel_id=1, source_target_pairs={{0,2},{1,3},{2,0},{3,1},{4,6},{5,7},{6,4},{7,5},{8,10},{9,11},{10,... | collective-permute-start | bytes 786440 | tf_op jit(solution)/shard_map/ppermute | solution.py:465
  93.0 0.7 collective-permute-start.27
  93.7 1.6 %collective-permute-start.26 = (bf16[64,1024]{1,0:T(8,128)(2,1)S(1)}, bf16[64,1024]{1,0:T(8,128)(2,1)S(1)}, u32[]{:S(2)}, u32[]{:S(2)}) collective-permute-start(bf16[64,1024]{1,0:T(8,128)(2,1)S(1)} %get-tuple-element.77), channel_id=1, source_target_pairs={{0,4},{1,13},{2,6},{3,15},{4,8},{5,1},{6,10},{7,3},{8,12},{9,5},{1... | collective-permute-start | bytes 393224 | tf_op jit(solution)/shard_map/ppermute | solution.py:462
  95.3 0.6 down.3
  95.9 3.0 %collective-permute-start.34 = (bf16[128,512]{1,0:T(8,128)(2,1)S(1)}, bf16[128,512]{1,0:T(8,128)(2,1)S(1)}, u32[]{:S(2)}, u32[]{:S(2)}) collective-permute-start(bf16[128,512]{1,0:T(8,128)(2,1)S(1)} %get-tuple-element.84), channel_id=1, source_target_pairs={{0,1},{1,0},{2,3},{3,2},{4,5},{5,4},{6,7},{7,6},{8,9},{9,8},{10,11... | collective-permute-start | bytes 393224 | tf_op jit(solution)/shard_map/ppermute | solution.py:465
  99.0 2.8 %collective-permute-done.26.a0 = bf16[64,1024]{1,0:T(8,128)(2,1)S(1)} collective-permute-done((bf16[64,1024]{1,0:T(8,128)(2,1)S(1)}, bf16[64,1024]{1,0:T(8,128)(2,1)S(1)}, u32[]{:S(2)}, u32[]{:S(2)}) %collective-permute-start.26) | collective-permute-done | bytes 131104 | tf_op jit(solution)/shard_map/ppermute | solution.py:462
  101.9 0.7 collective-permute-start.36
  102.6 0.9 collective-permute-start.37
  103.5 7.5 %collective-permute-done.36.b0 = bf16[64,1024]{1,0:T(8,128)(2,1)S(1)} collective-permute-done((bf16[64,1024]{1,0:T(8,128)(2,1)S(1)}, bf16[64,1024]{1,0:T(8,128)(2,1)S(1)}, u32[]{:S(2)}, u32[]{:S(2)}) %collective-permute-start.36) | collective-permute-done | bytes 131104 | tf_op jit(solution)/shard_map/ppermute | solution.py:462
  111.1 2.7 %collective-permute-start.38 = (bf16[64,1024]{1,0:T(8,128)(2,1)S(1)}, bf16[64,1024]{1,0:T(8,128)(2,1)S(1)}, u32[]{:S(2)}, u32[]{:S(2)}) collective-permute-start(bf16[64,1024]{1,0:T(8,128)(2,1)S(1)} %get-tuple-element.89), channel_id=1, source_target_pairs={{0,1},{1,0},{2,3},{3,2},{4,5},{5,4},{6,7},{7,6},{8,9},{9,8},{10,11... | collective-permute-start | bytes 393224 | tf_op jit(solution)/shard_map/ppermute | solution.py:465
  113.8 1.0 collective-permute-done.38.core
  114.8 0.8 closing.1
  (63 shorter events, 1.1 us)
Async XLA Ops:
  0.6 1.9 %copy-start = (bf16[1,1024,1536]{2,1,0:T(8,128)(2,1)S(1)}, bf16[1,1024,1536]{2,1,0:T(8,128)(2,1)}, u32[]{:S(2)}) copy-start(bf16[1,1024,1536]{2,1,0:T(8,128)(2,1)} %param.17) | copy-start | bytes 9437188
  2.5 4.7 %copy-start.4 = (bf16[1,32,2048]{2,1,0:T(8,128)(2,1)S(1)}, bf16[1,32,2048]{2,1,0:T(8,128)(2,1)}, u32[]{:S(2)}) copy-start(bf16[1,32,2048]{2,1,0:T(8,128)(2,1)} %param.11) | copy-start | bytes 393220
  2.5 7.9 %copy-start.3 = (bf16[1,64,2048]{2,1,0:T(8,128)(2,1)S(1)}, bf16[1,64,2048]{2,1,0:T(8,128)(2,1)}, u32[]{:S(2)}) copy-start(bf16[1,64,2048]{2,1,0:T(8,128)(2,1)} %param.10) | copy-start | bytes 786436
  2.7 38.3 %collective-permute-start.8 = (bf16[1024,768]{1,0:T(8,128)(2,1)S(1)}, bf16[1024,768]{1,0:T(8,128)(2,1)S(1)}, u32[]{:S(2)}, u32[]{:S(2)}) collective-permute-start(bf16[1024,768]{1,0:T(8,128)(2,1)S(1)} %weight_piece.3), channel_id=1, source_target_pairs={{0,16},{16,0},{1,17},{17,1},{2,18},{18,2},{3,19},{19,3},{4,20},{20... | collective-permute-start | bytes 4718600 | tf_op jit(solution)/shard_map/ppermute | solution.py:448
  5.7 13.7 %collective-permute-start.5 = (bf16[2048,128]{1,0:T(8,128)(2,1)}, bf16[2048,128]{1,0:T(8,128)(2,1)}, u32[]{:S(2)}, u32[]{:S(2)}) collective-permute-start(bf16[2048,128]{1,0:T(8,128)(2,1)} %w0.1), channel_id=1, source_target_pairs={{0,2},{1,3},{2,0},{3,1},{4,6},{5,7},{6,4},{7,5},{8,10},{9,11},{10,... | collective-permute-start | bytes 1572872 | tf_op jit(solution)/shard_map/ppermute | solution.py:465
  7.9 4.7 %copy-start.6 = (bf16[32,512]{1,0:T(8,128)(2,1)}, bf16[32,512]{1,0:T(8,128)(2,1)S(1)}, u32[]{:S(2)}) copy-start(bf16[32,512]{1,0:T(8,128)(2,1)S(1)} %get-tuple-element.49) | copy-start | bytes 98308
  7.9 11.6 %collective-permute-start.2 = (bf16[64,512]{1,0:T(8,128)(2,1)}, bf16[64,512]{1,0:T(8,128)(2,1)S(1)}, u32[]{:S(2)}, u32[]{:S(2)}) collective-permute-start(bf16[64,512]{1,0:T(8,128)(2,1)} %get-tuple-element.47), channel_id=1, source_target_pairs={{0,8},{1,9},{2,10},{3,11},{4,12},{5,13},{6,14},{7,15},{8,0},{9,1},... | collective-permute-start | bytes 196616 | tf_op jit(solution)/shard_map/ppermute | solution.py:468
  10.5 4.6 %copy-start.12 = (s32[1,32,8]{1,2,0:T(8,128)S(1)}, s32[1,32,8]{1,2,0:T(8,128)}, u32[]{:S(2)}) copy-start(s32[1,32,8]{1,2,0:T(8,128)} %param.14) | copy-start | bytes 3076
  10.5 14.9 %collective-permute-start.1 = (bf16[64,2048]{1,0:T(8,128)(2,1)S(1)}, bf16[64,2048]{1,0:T(8,128)(2,1)}, u32[]{:S(2)}, u32[]{:S(2)}) collective-permute-start(bf16[64,2048]{1,0:T(8,128)(2,1)S(1)} %bitcast.16), channel_id=1, source_target_pairs={{0,8},{1,9},{2,10},{3,11},{4,12},{5,13},{6,14},{7,15},{8,0},{9,1},... | collective-permute-start | bytes 786440 | tf_op jit(solution)/shard_map/ppermute | solution.py:468
  10.8 14.5 %collective-permute-start = (bf16[64,2048]{1,0:T(8,128)(2,1)S(1)}, bf16[64,2048]{1,0:T(8,128)(2,1)}, u32[]{:S(2)}, u32[]{:S(2)}) collective-permute-start(bf16[64,2048]{1,0:T(8,128)(2,1)S(1)} %bitcast.17), channel_id=1, source_target_pairs={{0,4},{1,5},{2,6},{3,7},{4,0},{5,1},{6,2},{7,3},{8,12},{9,13},{10,... | collective-permute-start | bytes 786440 | tf_op jit(solution)/shard_map/ppermute | solution.py:468
  12.6 1.0 copy-start.8
  13.6 0.8 copy-start.10
  19.4 15.4 %collective-permute-start.7 = (bf16[2048,128]{1,0:T(8,128)(2,1)}, bf16[2048,128]{1,0:T(8,128)(2,1)S(1)}, u32[]{:S(2)}, u32[]{:S(2)}) collective-permute-start(bf16[2048,128]{1,0:T(8,128)(2,1)} %collective-permute-done.5.w2), channel_id=1, source_target_pairs={{0,1},{1,0},{2,3},{3,2},{4,5},{5,4},{6,7},{7,6},{8,9},{9,8},{10,11... | collective-permute-start | bytes 1572872 | tf_op jit(solution)/shard_map/ppermute | solution.py:465
  19.5 15.4 %collective-permute-start.6 = (bf16[2048,128]{1,0:T(8,128)(2,1)}, bf16[2048,128]{1,0:T(8,128)(2,1)S(1)}, u32[]{:S(2)}, u32[]{:S(2)}) collective-permute-start(bf16[2048,128]{1,0:T(8,128)(2,1)} %w0.1), channel_id=1, source_target_pairs={{0,1},{1,0},{2,3},{3,2},{4,5},{5,4},{6,7},{7,6},{8,9},{9,8},{10,11... | collective-permute-start | bytes 1572872 | tf_op jit(solution)/shard_map/ppermute | solution.py:465
  25.4 9.5 %collective-permute-start.3 = (bf16[64,2048]{1,0:T(8,128)(2,1)}, bf16[64,2048]{1,0:T(8,128)(2,1)S(1)}, u32[]{:S(2)}, u32[]{:S(2)}) collective-permute-start(bf16[64,2048]{1,0:T(8,128)(2,1)} %collective-permute-done.1.a2), channel_id=1, source_target_pairs={{0,4},{1,5},{2,6},{3,7},{4,0},{5,1},{6,2},{7,3},{8,12},{9,13},{10,... | collective-permute-start | bytes 786440 | tf_op jit(solution)/shard_map/ppermute | solution.py:468
  26.3 12.0 %copy-start.9 = (bf16[640,768]{1,0:T(8,128)(2,1)S(1)}, bf16[640,768]{1,0:T(8,128)(2,1)}, u32[]{:S(2)}) copy-start(bf16[640,768]{1,0:T(8,128)(2,1)} %copy-done.8) | copy-start | bytes 2949124
  26.3 35.6 %copy-start.11 = (bf16[384,768]{1,0:T(8,128)(2,1)S(1)}, bf16[384,768]{1,0:T(8,128)(2,1)}, u32[]{:S(2)}) copy-start(bf16[384,768]{1,0:T(8,128)(2,1)} %copy-done.10) | copy-start | bytes 1769476
  26.4 36.7 %copy-start.5 = (f32[2048]{0:T(1024)S(1)}, f32[2048]{0:T(1024)}, u32[]{:S(2)}) copy-start(f32[2048]{0:T(1024)} %param.13) | copy-start | bytes 24580
  26.4 8.5 %collective-permute-start.4 = (bf16[64,512]{1,0:T(8,128)(2,1)S(1)}, bf16[64,512]{1,0:T(8,128)(2,1)S(1)}, u32[]{:S(2)}, u32[]{:S(2)}) collective-permute-start(bf16[64,512]{1,0:T(8,128)(2,1)S(1)} %pad_maximum_fusion), channel_id=1, source_target_pairs={{0,4},{1,5},{2,6},{3,7},{4,0},{5,1},{6,2},{7,3},{8,12},{9,13},{10,... | collective-permute-start | bytes 196616 | tf_op jit(solution)/shard_map/ppermute | solution.py:468
  34.9 35.2 %copy-start.1 = (bf16[1,1024,1536]{2,1,0:T(8,128)(2,1)S(1)}, bf16[1,1024,1536]{2,1,0:T(8,128)(2,1)}, u32[]{:S(2)}) copy-start(bf16[1,1024,1536]{2,1,0:T(8,128)(2,1)} %param.17) | copy-start | bytes 9437188
  37.8 6.5 %collective-permute-start.9 = (bf16[128,512]{1,0:T(8,128)(2,1)S(1)}, bf16[128,512]{1,0:T(8,128)(2,1)S(1)}, u32[]{:S(2)}, u32[]{:S(2)}) collective-permute-start(bf16[128,512]{1,0:T(8,128)(2,1)S(1)} %get-tuple-element.56), channel_id=1, source_target_pairs={{0,16},{16,0},{1,17},{17,1},{2,18},{18,2},{3,19},{19,3},{4,20},{20... | collective-permute-start | bytes 393224 | tf_op jit(solution)/shard_map/ppermute | solution.py:448
  38.3 38.7 %collective-permute-start.19 = (bf16[640,768]{1,0:T(8,128)(2,1)S(1)}, bf16[640,768]{1,0:T(8,128)(2,1)S(1)}, u32[]{:S(2)}, u32[]{:S(2)}) collective-permute-start(bf16[640,768]{1,0:T(8,128)(2,1)S(1)} %copy-done.9), channel_id=1, source_target_pairs={{0,16},{16,0},{1,17},{17,1},{2,18},{18,2},{3,19},{19,3},{4,20},{20... | collective-permute-start | bytes 2949128 | tf_op jit(solution)/shard_map/ppermute | solution.py:448
  44.3 7.8 %collective-permute-start.12 = (bf16[144,512]{1,0:T(8,128)(2,1)S(1)}, bf16[144,512]{1,0:T(8,128)(2,1)S(1)}, u32[]{:S(2)}, u32[]{:S(2)}) collective-permute-start(bf16[144,512]{1,0:T(8,128)(2,1)S(1)} %stream.1.b0), channel_id=1, source_target_pairs={{0,12},{1,13},{2,14},{3,15},{4,0},{5,1},{6,2},{7,3},{8,4},{9,5},{1... | collective-permute-start | bytes 442376 | tf_op jit(solution)/shard_map/ppermute | solution.py:451
  47.8 12.0 %collective-permute-start.11 = (bf16[144,512]{1,0:T(8,128)(2,1)S(1)}, bf16[144,512]{1,0:T(8,128)(2,1)S(1)}, u32[]{:S(2)}, u32[]{:S(2)}) collective-permute-start(bf16[144,512]{1,0:T(8,128)(2,1)S(1)} %stream.1.b0), channel_id=1, source_target_pairs={{0,8},{1,9},{2,10},{3,11},{4,12},{5,13},{6,14},{7,15},{8,0},{9,1},... | collective-permute-start | bytes 442376 | tf_op jit(solution)/shard_map/ppermute | solution.py:451
  47.8 13.2 %collective-permute-start.10 = (bf16[144,512]{1,0:T(8,128)(2,1)S(1)}, bf16[144,512]{1,0:T(8,128)(2,1)S(1)}, u32[]{:S(2)}, u32[]{:S(2)}) collective-permute-start(bf16[144,512]{1,0:T(8,128)(2,1)S(1)} %stream.1.b0), channel_id=1, source_target_pairs={{0,4},{1,5},{2,6},{3,7},{4,8},{5,9},{6,10},{7,11},{8,12},{9,13},{1... | collective-permute-start | bytes 442376 | tf_op jit(solution)/shard_map/ppermute | solution.py:451
  48.7 13.2 %collective-permute-start.13 = (bf16[144,512]{1,0:T(8,128)(2,1)S(1)}, bf16[144,512]{1,0:T(8,128)(2,1)S(1)}, u32[]{:S(2)}, u32[]{:S(2)}) collective-permute-start(bf16[144,512]{1,0:T(8,128)(2,1)S(1)} %stream.1.b0), channel_id=1, source_target_pairs={{0,2},{1,3},{2,0},{3,1},{4,6},{5,7},{6,4},{7,5},{8,10},{9,11},{10,... | collective-permute-start | bytes 442376 | tf_op jit(solution)/shard_map/ppermute | solution.py:465
  52.1 11.3 %collective-permute-start.16 = (bf16[144,512]{1,0:T(8,128)(2,1)S(1)}, bf16[144,512]{1,0:T(8,128)(2,1)S(1)}, u32[]{:S(2)}, u32[]{:S(2)}) collective-permute-start(bf16[144,512]{1,0:T(8,128)(2,1)S(1)} %collective-permute-done.12.b3), channel_id=1, source_target_pairs={{0,2},{1,3},{2,0},{3,1},{4,6},{5,7},{6,4},{7,5},{8,10},{9,11},{10,... | collective-permute-start | bytes 442376 | tf_op jit(solution)/shard_map/ppermute | solution.py:465
  59.9 5.9 %collective-permute-start.15 = (bf16[144,512]{1,0:T(8,128)(2,1)S(1)}, bf16[144,512]{1,0:T(8,128)(2,1)S(1)}, u32[]{:S(2)}, u32[]{:S(2)}) collective-permute-start(bf16[144,512]{1,0:T(8,128)(2,1)S(1)} %collective-permute-done.11.b2), channel_id=1, source_target_pairs={{0,2},{1,3},{2,0},{3,1},{4,6},{5,7},{6,4},{7,5},{8,10},{9,11},{10,... | collective-permute-start | bytes 442376 | tf_op jit(solution)/shard_map/ppermute | solution.py:465
  61.0 6.3 %collective-permute-start.14 = (bf16[144,512]{1,0:T(8,128)(2,1)S(1)}, bf16[144,512]{1,0:T(8,128)(2,1)S(1)}, u32[]{:S(2)}, u32[]{:S(2)}) collective-permute-start(bf16[144,512]{1,0:T(8,128)(2,1)S(1)} %collective-permute-done.10.b1), channel_id=1, source_target_pairs={{0,2},{1,3},{2,0},{3,1},{4,6},{5,7},{6,4},{7,5},{8,10},{9,11},{10,... | collective-permute-start | bytes 442376 | tf_op jit(solution)/shard_map/ppermute | solution.py:465
  61.9 15.1 %collective-permute-start.20 = (bf16[384,768]{1,0:T(8,128)(2,1)S(1)}, bf16[384,768]{1,0:T(8,128)(2,1)S(1)}, u32[]{:S(2)}, u32[]{:S(2)}) collective-permute-start(bf16[384,768]{1,0:T(8,128)(2,1)S(1)} %copy-done.11), channel_id=1, source_target_pairs={{0,16},{16,0},{1,17},{17,1},{2,18},{18,2},{3,19},{19,3},{4,20},{20... | collective-permute-start | bytes 1769480 | tf_op jit(solution)/shard_map/ppermute | solution.py:448
  63.4 4.7 %collective-permute-start.18 = (bf16[128,2176]{1,0:T(8,128)(2,1)S(1)}, bf16[128,2176]{1,0:T(8,128)(2,1)S(1)}, u32[]{:S(2)}, u32[]{:S(2)}) collective-permute-start(bf16[128,2176]{1,0:T(8,128)(2,1)S(1)} %get-tuple-element.60.group), channel_id=1, source_target_pairs={{0,1},{1,0},{2,3},{3,2},{4,5},{5,4},{6,7},{7,6},{8,9},{9,8},{10,11... | collective-permute-start | bytes 1671176 | tf_op jit(solution)/shard_map/ppermute | solution.py:465
  68.1 2.0 %collective-permute-start.17 = (bf16[128,2176]{1,0:T(8,128)(2,1)S(1)}, bf16[128,2176]{1,0:T(8,128)(2,1)S(1)}, u32[]{:S(2)}, u32[]{:S(2)}) collective-permute-start(bf16[128,2176]{1,0:T(8,128)(2,1)S(1)} %get-tuple-element.59.group_x), channel_id=1, source_target_pairs={{0,1},{1,0},{2,3},{3,2},{4,5},{5,4},{6,7},{7,6},{8,9},{9,8},{10,11... | collective-permute-start | bytes 1671176 | tf_op jit(solution)/shard_map/ppermute | solution.py:465
  73.5 14.6 %collective-permute-start.28 = (bf16[384,384]{1,0:T(8,128)(2,1)S(1)}, bf16[384,384]{1,0:T(8,128)(2,1)S(1)}, u32[]{:S(2)}, u32[]{:S(2)}) collective-permute-start(bf16[384,384]{1,0:T(8,128)(2,1)S(1)} %get-tuple-element.61.first), channel_id=1, source_target_pairs={{0,16},{16,0},{1,17},{17,1},{2,18},{18,2},{3,19},{19,3},{4,20},{20... | collective-permute-start | bytes 884744 | tf_op jit(solution)/shard_map/ppermute | solution.py:448
  77.1 1.5 %copy-start.2 = (bf16[1,768,1024]{2,1,0:T(8,128)(2,1)S(1)}, bf16[1,768,1024]{2,1,0:T(8,128)(2,1)}, u32[]{:S(2)}) copy-start(bf16[1,768,1024]{2,1,0:T(8,128)(2,1)} %param.18) | copy-start | bytes 4718596
  79.5 3.1 %collective-permute-start.21 = (bf16[128,512]{1,0:T(8,128)(2,1)S(1)}, bf16[128,512]{1,0:T(8,128)(2,1)S(1)}, u32[]{:S(2)}, u32[]{:S(2)}) collective-permute-start(bf16[128,512]{1,0:T(8,128)(2,1)S(1)} %get-tuple-element.71), channel_id=1, source_target_pairs={{0,1},{1,0},{2,3},{3,2},{4,5},{5,4},{6,7},{7,6},{8,9},{9,8},{10,11... | collective-permute-start | bytes 393224 | tf_op jit(solution)/shard_map/ppermute | solution.py:465
  79.6 3.0 %collective-permute-start.22 = (bf16[128,512]{1,0:T(8,128)(2,1)S(1)}, bf16[128,512]{1,0:T(8,128)(2,1)S(1)}, u32[]{:S(2)}, u32[]{:S(2)}) collective-permute-start(bf16[128,512]{1,0:T(8,128)(2,1)S(1)} %get-tuple-element.72), channel_id=1, source_target_pairs={{0,1},{1,0},{2,3},{3,2},{4,5},{5,4},{6,7},{7,6},{8,9},{9,8},{10,11... | collective-permute-start | bytes 393224 | tf_op jit(solution)/shard_map/ppermute | solution.py:465
  80.1 8.0 %collective-permute-start.29 = (bf16[256,384]{1,0:T(8,128)(2,1)S(1)}, bf16[256,384]{1,0:T(8,128)(2,1)S(1)}, u32[]{:S(2)}, u32[]{:S(2)}) collective-permute-start(bf16[256,384]{1,0:T(8,128)(2,1)S(1)} %get-tuple-element.68.far), channel_id=1, source_target_pairs={{0,16},{16,0},{1,17},{17,1},{2,18},{18,2},{3,19},{19,3},{4,20},{20... | collective-permute-start | bytes 589832 | tf_op jit(solution)/shard_map/ppermute | solution.py:448
  82.7 8.1 %collective-permute-start.23 = (bf16[128,1024]{1,0:T(8,128)(2,1)S(1)}, bf16[128,1024]{1,0:T(8,128)(2,1)S(1)}, u32[]{:S(2)}, u32[]{:S(2)}) collective-permute-start(bf16[128,1024]{1,0:T(8,128)(2,1)S(1)} %fold.2), channel_id=1, source_target_pairs={{0,2},{1,3},{2,0},{3,1},{4,6},{5,7},{6,4},{7,5},{8,10},{9,11},{10,... | collective-permute-start | bytes 786440 | tf_op jit(solution)/shard_map/ppermute | solution.py:465
  84.2 5.0 %collective-permute-start.24 = (bf16[128,512]{1,0:T(8,128)(2,1)S(1)}, bf16[128,512]{1,0:T(8,128)(2,1)S(1)}, u32[]{:S(2)}, u32[]{:S(2)}) collective-permute-start(bf16[128,512]{1,0:T(8,128)(2,1)S(1)} %get-tuple-element.74), channel_id=1, source_target_pairs={{0,1},{1,0},{2,3},{3,2},{4,5},{5,4},{6,7},{7,6},{8,9},{9,8},{10,11... | collective-permute-start | bytes 393224 | tf_op jit(solution)/shard_map/ppermute | solution.py:465
  84.2 11.1 %collective-permute-start.33 = (bf16[384,384]{1,0:T(8,128)(2,1)S(1)}, bf16[384,384]{1,0:T(8,128)(2,1)S(1)}, u32[]{:S(2)}, u32[]{:S(2)}) collective-permute-start(bf16[384,384]{1,0:T(8,128)(2,1)S(1)} %get-tuple-element.69.rest), channel_id=1, source_target_pairs={{0,16},{16,0},{1,17},{17,1},{2,18},{18,2},{3,19},{19,3},{4,20},{20... | collective-permute-start | bytes 884744 | tf_op jit(solution)/shard_map/ppermute | solution.py:448
  88.1 1.3 %collective-permute-start.25 = (bf16[128,512]{1,0:T(8,128)(2,1)S(1)}, bf16[128,512]{1,0:T(8,128)(2,1)S(1)}, u32[]{:S(2)}, u32[]{:S(2)}) collective-permute-start(bf16[128,512]{1,0:T(8,128)(2,1)S(1)} %get-tuple-element.75), channel_id=1, source_target_pairs={{0,1},{1,0},{2,3},{3,2},{4,5},{5,4},{6,7},{7,6},{8,9},{9,8},{10,11... | collective-permute-start | bytes 393224 | tf_op jit(solution)/shard_map/ppermute | solution.py:465
  88.7 2.2 %collective-permute-start.30 = (bf16[128,512]{1,0:T(8,128)(2,1)S(1)}, bf16[128,512]{1,0:T(8,128)(2,1)S(1)}, u32[]{:S(2)}, u32[]{:S(2)}) collective-permute-start(bf16[128,512]{1,0:T(8,128)(2,1)S(1)} %get-tuple-element.80), channel_id=1, source_target_pairs={{0,1},{1,0},{2,3},{3,2},{4,5},{5,4},{6,7},{7,6},{8,9},{9,8},{10,11... | collective-permute-start | bytes 393224 | tf_op jit(solution)/shard_map/ppermute | solution.py:465
  89.2 1.6 %collective-permute-start.31 = (bf16[128,512]{1,0:T(8,128)(2,1)S(1)}, bf16[128,512]{1,0:T(8,128)(2,1)S(1)}, u32[]{:S(2)}, u32[]{:S(2)}) collective-permute-start(bf16[128,512]{1,0:T(8,128)(2,1)S(1)} %get-tuple-element.81), channel_id=1, source_target_pairs={{0,1},{1,0},{2,3},{3,2},{4,5},{5,4},{6,7},{7,6},{8,9},{9,8},{10,11... | collective-permute-start | bytes 393224 | tf_op jit(solution)/shard_map/ppermute | solution.py:465
  90.9 10.8 %collective-permute-start.32 = (bf16[128,1024]{1,0:T(8,128)(2,1)S(1)}, bf16[128,1024]{1,0:T(8,128)(2,1)S(1)}, u32[]{:S(2)}, u32[]{:S(2)}) collective-permute-start(bf16[128,1024]{1,0:T(8,128)(2,1)S(1)} %fold.3), channel_id=1, source_target_pairs={{0,2},{1,3},{2,0},{3,1},{4,6},{5,7},{6,4},{7,5},{8,10},{9,11},{10,... | collective-permute-start | bytes 786440 | tf_op jit(solution)/shard_map/ppermute | solution.py:465
  93.0 8.8 %collective-permute-start.27 = (bf16[64,1024]{1,0:T(8,128)(2,1)S(1)}, bf16[64,1024]{1,0:T(8,128)(2,1)S(1)}, u32[]{:S(2)}, u32[]{:S(2)}) collective-permute-start(bf16[64,1024]{1,0:T(8,128)(2,1)S(1)} %get-tuple-element.76.own), channel_id=1, source_target_pairs={{1,9},{3,11},{5,13},{7,15},{9,1},{11,3},{13,5},{15,7},{17,25},{19,... | collective-permute-start | bytes 393224 | tf_op jit(solution)/shard_map/ppermute | solution.py:462
  93.6 21.1 %copy-start.7 = (f32[2048]{0:T(1024)S(1)}, f32[2048]{0:T(1024)}, u32[]{:S(2)}) copy-start(f32[2048]{0:T(1024)} %param.19) | copy-start | bytes 24580
  93.7 8.1 %collective-permute-start.26 = (bf16[64,1024]{1,0:T(8,128)(2,1)S(1)}, bf16[64,1024]{1,0:T(8,128)(2,1)S(1)}, u32[]{:S(2)}, u32[]{:S(2)}) collective-permute-start(bf16[64,1024]{1,0:T(8,128)(2,1)S(1)} %get-tuple-element.77), channel_id=1, source_target_pairs={{0,4},{1,13},{2,6},{3,15},{4,8},{5,1},{6,10},{7,3},{8,12},{9,5},{1... | collective-permute-start | bytes 393224 | tf_op jit(solution)/shard_map/ppermute | solution.py:462
  95.9 5.9 %collective-permute-start.34 = (bf16[128,512]{1,0:T(8,128)(2,1)S(1)}, bf16[128,512]{1,0:T(8,128)(2,1)S(1)}, u32[]{:S(2)}, u32[]{:S(2)}) collective-permute-start(bf16[128,512]{1,0:T(8,128)(2,1)S(1)} %get-tuple-element.84), channel_id=1, source_target_pairs={{0,1},{1,0},{2,3},{3,2},{4,5},{5,4},{6,7},{7,6},{8,9},{9,8},{10,11... | collective-permute-start | bytes 393224 | tf_op jit(solution)/shard_map/ppermute | solution.py:465
  98.9 2.9 %collective-permute-start.35 = (bf16[128,512]{1,0:T(8,128)(2,1)S(1)}, bf16[128,512]{1,0:T(8,128)(2,1)S(1)}, u32[]{:S(2)}, u32[]{:S(2)}) collective-permute-start(bf16[128,512]{1,0:T(8,128)(2,1)S(1)} %get-tuple-element.85), channel_id=1, source_target_pairs={{0,1},{1,0},{2,3},{3,2},{4,5},{5,4},{6,7},{7,6},{8,9},{9,8},{10,11... | collective-permute-start | bytes 393224 | tf_op jit(solution)/shard_map/ppermute | solution.py:465
  101.9 9.1 %collective-permute-start.36 = (bf16[64,1024]{1,0:T(8,128)(2,1)S(1)}, bf16[64,1024]{1,0:T(8,128)(2,1)S(1)}, u32[]{:S(2)}, u32[]{:S(2)}) collective-permute-start(bf16[64,1024]{1,0:T(8,128)(2,1)S(1)} %get-tuple-element.86), channel_id=1, source_target_pairs={{0,20},{1,29},{2,22},{3,31},{4,24},{5,17},{6,26},{7,19},{8,28},{9,... | collective-permute-start | bytes 393224 | tf_op jit(solution)/shard_map/ppermute | solution.py:462
  102.6 8.4 %collective-permute-start.37 = (bf16[64,1024]{1,0:T(8,128)(2,1)S(1)}, bf16[64,1024]{1,0:T(8,128)(2,1)S(1)}, u32[]{:S(2)}, u32[]{:S(2)}) collective-permute-start(bf16[64,1024]{1,0:T(8,128)(2,1)S(1)} %get-tuple-element.87), channel_id=1, source_target_pairs={{0,16},{1,25},{2,18},{3,27},{4,20},{5,29},{6,22},{7,31},{8,24},{9,... | collective-permute-start | bytes 393224 | tf_op jit(solution)/shard_map/ppermute | solution.py:462
  111.1 3.7 %collective-permute-start.38 = (bf16[64,1024]{1,0:T(8,128)(2,1)S(1)}, bf16[64,1024]{1,0:T(8,128)(2,1)S(1)}, u32[]{:S(2)}, u32[]{:S(2)}) collective-permute-start(bf16[64,1024]{1,0:T(8,128)(2,1)S(1)} %get-tuple-element.89), channel_id=1, source_target_pairs={{0,1},{1,0},{2,3},{3,2},{4,5},{5,4},{6,7},{7,6},{8,9},{9,8},{10,11... | collective-permute-start | bytes 393224 | tf_op jit(solution)/shard_map/ppermute | solution.py:465

commit v19 on v14

--- a/solution.py
+++ b/solution.py
@@ -388,11 +388,31 @@
         second[:, cols] = total[half:]
 
 
-def gather_kernel(own, a0, a1, b0, b1, keep_ref, send_ref):
-    expert, outer, inner, dp = seat()
-    small = own.shape[0] // 2
-    start = jnp.where((inner & 1) == 0, own[...].astype(F32), a0[...].astype(F32))
-    for i, total in enumerate((start + a1[...].astype(F32), b0[...].astype(F32) + b1[...].astype(F32))):
+def messages_kernel(keep_far, keep_near, *refs):
+    *cores, first, second = refs
+    half = first.shape[0] // 2
+    parts = len(cores) // 2
+    for h, (keep, core) in enumerate(((keep_far, cores[:parts]), (keep_near, cores[parts:]))):
+        for at in range(0, keep.shape[1], 256):
+            cols = slice(at, at + 256)
+            total = added(keep, core, cols).astype(BF16)
+            first[h * half : (h + 1) * half, cols] = total[:half]
+            second[h * half : (h + 1) * half, cols] = total[half:]
+
+
+def outer_sum_kernel(own, a0, a1, far_ref, near_ref):
+    expert, outer, inner, dp = seat()
+    half = far_ref.shape[0]
+    total = jnp.where((inner & 1) == 0, own[...].astype(F32), a0[...].astype(F32)) + a1[...].astype(F32)
+    far_ref[...] = total[:half].astype(BF16)
+    near_ref[...] = total[half:]
+
+
+def gather_kernel(near, far, b0, b1, keep_ref, send_ref):
+    small = near.shape[0] // 2
+    for i, total in enumerate(
+        (near[...] + far[...].astype(F32), b0[...].astype(F32) + b1[...].astype(F32))
+    ):
         rows = slice(i * small, (i + 1) * small)
         keep_ref[rows, :] = total[:small]
         send_ref[rows, :] = total[small:].astype(BF16)
@@ -615,15 +635,26 @@
     keep_far, *send, keep_near = call(
         down_both_kernel, "down_both", 16, outs, inner_first, inner_far, inner_rest, w_down[0], scratch=scratch
     )
-    far = swap_inner(fold(keep_far, swap_cores(send[:2])), 2)
-    first_far = far
-    own, second = pieces(far, keep_near, send[2:])
-    mine = [send_outer(own, 0, False), send_outer(second, 1, False)]
+    message = shape_of(4 * rows_here, half_width)
+    own, second = call(
+        messages_kernel, "messages", 4, (message, message), keep_far, keep_near, *swap_cores(send)
+    )
+    half_message = shape_of(2 * rows_here, half_width)
+    mine_far, mine_near = call(
+        outer_sum_kernel,
+        "outer_sum",
+        4,
+        (half_message, shape_of(2 * rows_here, half_width, dtype=F32)),
+        own,
+        send_outer(own, 0, False),
+        send_outer(second, 1, False),
+    )
+    mine_far = swap_inner(mine_far, 2)
 
     keep_far, send = down(down_far_kernel, far_other, 2)
-    far = swap_inner(fold(after(keep_far, own), swap_cores(send)), 2)
-    keep_near, send = down(down_near_kernel, rest_other, 2)
-    cut = pieces(far, after(keep_near, *mine), send)
+    far = swap_inner(fold(keep_far, swap_cores(send)), 2)
+    keep_near, send = down(down_near_kernel, after(rest_other, mine_near), 2)
+    cut = pieces(far, keep_near, send)
     others = [send_outer(cut[i], i, True) for i in range(2)]
 
     sums = shape_of(2 * rows_here, half_width)
@@ -632,8 +663,8 @@
         "gather",
         4,
         (shape_of(2 * rows_here, half_width, dtype=F32), sums),
-        own,
-        *mine,
+        mine_near,
+        mine_far,
         *others,
     )
     out = shape_of(rows_here, model_width)

time: 115 us -> 114 us (level)
  waiting for transfers between devices: 52.5 us -> 50.4 us
    ppermute x4, waiting for transfers between devices: 11.4 us -> 7.22 us  [send_outer(): return lax.ppermute(x, ('dp', 'expert'), pairs)]
    ppermute x20, waiting for transfers between devices: 11.6 us -> 15 us  [swap_inner(): return lax.ppermute(x, 'expert', [(i, i ^ j) for i in range(expert_count)])]
    ppermute x20, starting transfers between devices: 15.6 us -> 18 us  [swap_inner(): return lax.ppermute(x, 'expert', [(i, i ^ j) for i in range(expert_count)])]
    ppermute x7, waiting for transfers between devices: 9.83 us -> 8.48 us  [swap_dp(): return lax.ppermute(x, 'dp', [(0, 1), (1, 0)])]
  transfers between devices with their start and end apart: 39 -> 39, of which waited for: 18 -> 22; matrix products, arithmetic and copies ran while one was open for 1% -> 1% of each run, Pallas kernels for 11% -> 11%
where the time goes in v19:
time: 114 us
  waiting for transfers between devices  50.4 us (44%)
  starting transfers between devices  42.8 us (38%)
  Pallas kernels  13.8 us (12%)
  local copies, waits for them, and re-layouts  4.6 us (4%)
  between operations  1.54 us (1%)
    ppermute x20, starting transfers between devices, swap_inner(): return lax.ppermute(x, 'expert', [(i, i ^ j) for i in range(expert_count)])  18 us
    ppermute x20, waiting for transfers between devices, swap_inner(): return lax.ppermute(x, 'expert', [(i, i ^ j) for i in range(expert_count)])  15 us
    pallas_call x17, Pallas kernels, call(): pl.pallas_call(kernel, out_shape=outs, in_specs=[first] + [vmem] * (len(a...  13.4 us
    ppermute x5, waiting for transfers between devices, swap_outer(): lax.ppermute(x, 'expert', [(i, i ^ 4 * s) for i in range(expert_count)])  12.1 us
    ppermute x7, starting transfers between devices, swap_dp(): return lax.ppermute(x, 'dp', [(0, 1), (1, 0)])  9.85 us
    ppermute x7, waiting for transfers between devices, swap_dp(): return lax.ppermute(x, 'dp', [(0, 1), (1, 0)])  8.48 us
    ppermute x3, waiting for transfers between devices, shift_outer(): lax.ppermute(x, 'expert', [(i, (i + 4 * s) % expert_count) for i in range...  7.64 us
    ppermute x4, waiting for transfers between devices, send_outer(): return lax.ppermute(x, ('dp', 'expert'), pairs)  7.22 us
  transfers between devices with their start and end apart: 39, of which 22 were waited for; matrix products, arithmetic and copies ran while one was open for 1% of the time, Pallas kernels for 11%

profile of v19, /device:TPU:0, one launch (start us, length us, event | category | flops | bytes accessed | tf_op | source)
XLA Modules:
  0.0 114.0 jit_solution(11967742712010610787)
XLA Ops:
  0.6 1.9 %copy-done = bf16[1,1024,1536]{2,1,0:T(8,128)(2,1)S(1)} copy-done((bf16[1,1024,1536]{2,1,0:T(8,128)(2,1)S(1)}, bf16[1,1024,1536]{2,1,0:T(8,128)(2,1)}, u32[]{:S(2)}) %copy-start) | copy-done | bytes 3145752
  2.7 3.0 %collective-permute-start.8 = (bf16[1024,768]{1,0:T(8,128)(2,1)S(1)}, bf16[1024,768]{1,0:T(8,128)(2,1)S(1)}, u32[]{:S(2)}, u32[]{:S(2)}) collective-permute-start(bf16[1024,768]{1,0:T(8,128)(2,1)S(1)} %weight_piece.3), channel_id=1, source_target_pairs={{0,16},{16,0},{1,17},{17,1},{2,18},{18,2},{3,19},{19,3},{4,20},{20... | collective-permute-start | bytes 4718600 | tf_op jit(solution)/shard_map/ppermute | solution.py:468
  5.7 1.5 %collective-permute-start.5 = (bf16[2048,128]{1,0:T(8,128)(2,1)}, bf16[2048,128]{1,0:T(8,128)(2,1)}, u32[]{:S(2)}, u32[]{:S(2)}) collective-permute-start(bf16[2048,128]{1,0:T(8,128)(2,1)} %w0.1), channel_id=1, source_target_pairs={{0,2},{1,3},{2,0},{3,1},{4,6},{5,7},{6,4},{7,5},{8,10},{9,11},{10,... | collective-permute-start | bytes 1572872 | tf_op jit(solution)/shard_map/ppermute | solution.py:485
  7.2 0.6 cut_resid.1
  7.9 2.6 %collective-permute-start.2 = (bf16[64,512]{1,0:T(8,128)(2,1)}, bf16[64,512]{1,0:T(8,128)(2,1)S(1)}, u32[]{:S(2)}, u32[]{:S(2)}) collective-permute-start(bf16[64,512]{1,0:T(8,128)(2,1)} %get-tuple-element.48), channel_id=1, source_target_pairs={{0,8},{1,9},{2,10},{3,11},{4,12},{5,13},{6,14},{7,15},{8,0},{9,1},... | collective-permute-start | bytes 196616 | tf_op jit(solution)/shard_map/ppermute | solution.py:488
  10.5 0.3 collective-permute-start.1
  10.8 1.6 %collective-permute-start = (bf16[64,2048]{1,0:T(8,128)(2,1)S(1)}, bf16[64,2048]{1,0:T(8,128)(2,1)}, u32[]{:S(2)}, u32[]{:S(2)}) collective-permute-start(bf16[64,2048]{1,0:T(8,128)(2,1)S(1)} %bitcast.17), channel_id=1, source_target_pairs={{0,4},{1,5},{2,6},{3,7},{4,0},{5,1},{6,2},{7,3},{8,12},{9,13},{10,... | collective-permute-start | bytes 786440 | tf_op jit(solution)/shard_map/ppermute | solution.py:488
  12.6 1.0 copy-done.8
  13.6 0.8 copy-done.10
  15.2 0.8 copy.13
  15.9 0.4 share.1
  16.4 3.0 %collective-permute-done.5.w2 = bf16[2048,128]{1,0:T(8,128)(2,1)} collective-permute-done((bf16[2048,128]{1,0:T(8,128)(2,1)}, bf16[2048,128]{1,0:T(8,128)(2,1)}, u32[]{:S(2)}, u32[]{:S(2)}) %collective-permute-start.5) | collective-permute-done | bytes 524320 | tf_op jit(solution)/shard_map/ppermute | solution.py:485
  19.5 0.5 collective-permute-start.6
  20.0 5.4 %collective-permute-done.1.a2 = bf16[64,2048]{1,0:T(8,128)(2,1)} collective-permute-done((bf16[64,2048]{1,0:T(8,128)(2,1)S(1)}, bf16[64,2048]{1,0:T(8,128)(2,1)}, u32[]{:S(2)}, u32[]{:S(2)}) %collective-permute-start.1) | collective-permute-done | bytes 262176 | tf_op jit(solution)/shard_map/ppermute | solution.py:488
  25.6 0.8 pad_maximum_fusion
  26.4 1.9 %collective-permute-start.4 = (bf16[64,512]{1,0:T(8,128)(2,1)S(1)}, bf16[64,512]{1,0:T(8,128)(2,1)S(1)}, u32[]{:S(2)}, u32[]{:S(2)}) collective-permute-start(bf16[64,512]{1,0:T(8,128)(2,1)S(1)} %pad_maximum_fusion), channel_id=1, source_target_pairs={{0,4},{1,5},{2,6},{3,7},{4,0},{5,1},{6,2},{7,3},{8,12},{9,13},{10,... | collective-permute-start | bytes 196616 | tf_op jit(solution)/shard_map/ppermute | solution.py:488
  28.2 6.7 %collective-permute-done.4.r13 = bf16[64,512]{1,0:T(8,128)(2,1)S(1)} collective-permute-done((bf16[64,512]{1,0:T(8,128)(2,1)S(1)}, bf16[64,512]{1,0:T(8,128)(2,1)S(1)}, u32[]{:S(2)}, u32[]{:S(2)}) %collective-permute-start.4) | collective-permute-done | bytes 65568 | tf_op jit(solution)/shard_map/ppermute | solution.py:488
  34.9 2.8 %projection.1 = (bf16[128,512]{1,0:T(8,128)(2,1)S(1)}, bf16[128,512]{1,0:T(8,128)(2,1)S(1)}) custom-call(bf16[64,2048]{1,0:T(8,128)(2,1)S(1)} %bitcast.18, bf16[64,2048]{1,0:T(8,128)(2,1)} %collective-permute-done.a1, bf16[64,2048]{1,0:T(8,128)(2,1)} %collective-permute-done.1.a2, bf16[64,2048]{1,0:T(8,128)(2,1)S(1)} %collective-permute-done.3.a3, ...), custom_call_target="tpu_custom_call" | custom-call | flops 1 | bytes 1 | tf_op jit(solution)/shard_map/projection/pallas_call | solution.py:456
  37.8 0.6 collective-permute-start.9
  38.3 1.5 %collective-permute-start.19 = (bf16[640,768]{1,0:T(8,128)(2,1)S(1)}, bf16[640,768]{1,0:T(8,128)(2,1)S(1)}, u32[]{:S(2)}, u32[]{:S(2)}) collective-permute-start(bf16[640,768]{1,0:T(8,128)(2,1)S(1)} %copy-done.9), channel_id=1, source_target_pairs={{0,16},{16,0},{1,17},{17,1},{2,18},{18,2},{3,19},{19,3},{4,20},{20... | collective-permute-start | bytes 2949128 | tf_op jit(solution)/shard_map/ppermute | solution.py:468
  39.9 1.1 collective-permute-done.8.early
  41.0 3.3 %collective-permute-done.9.arrived = bf16[128,512]{1,0:T(8,128)(2,1)S(1)} collective-permute-done((bf16[128,512]{1,0:T(8,128)(2,1)S(1)}, bf16[128,512]{1,0:T(8,128)(2,1)S(1)}, u32[]{:S(2)}, u32[]{:S(2)}) %collective-permute-start.9) | collective-permute-done | bytes 131104 | tf_op jit(solution)/shard_map/ppermute | solution.py:468
  44.3 3.5 %collective-permute-start.12 = (bf16[144,512]{1,0:T(8,128)(2,1)S(1)}, bf16[144,512]{1,0:T(8,128)(2,1)S(1)}, u32[]{:S(2)}, u32[]{:S(2)}) collective-permute-start(bf16[144,512]{1,0:T(8,128)(2,1)S(1)} %stream.1.b0), channel_id=1, source_target_pairs={{0,12},{1,13},{2,14},{3,15},{4,0},{5,1},{6,2},{7,3},{8,4},{9,5},{1... | collective-permute-start | bytes 442376 | tf_op jit(solution)/shard_map/ppermute | solution.py:471
  47.8 0.8 collective-permute-start.10
  48.7 1.9 %collective-permute-start.13 = (bf16[144,512]{1,0:T(8,128)(2,1)S(1)}, bf16[144,512]{1,0:T(8,128)(2,1)S(1)}, u32[]{:S(2)}, u32[]{:S(2)}) collective-permute-start(bf16[144,512]{1,0:T(8,128)(2,1)S(1)} %stream.1.b0), channel_id=1, source_target_pairs={{0,2},{1,3},{2,0},{3,1},{4,6},{5,7},{6,4},{7,5},{8,10},{9,11},{10,... | collective-permute-start | bytes 442376 | tf_op jit(solution)/shard_map/ppermute | solution.py:485
  50.5 1.6 %collective-permute-done.12.b3 = bf16[144,512]{1,0:T(8,128)(2,1)S(1)} collective-permute-done((bf16[144,512]{1,0:T(8,128)(2,1)S(1)}, bf16[144,512]{1,0:T(8,128)(2,1)S(1)}, u32[]{:S(2)}, u32[]{:S(2)}) %collective-permute-start.12) | collective-permute-done | bytes 147488 | tf_op jit(solution)/shard_map/ppermute | solution.py:471
  52.1 1.7 %collective-permute-start.16 = (bf16[144,512]{1,0:T(8,128)(2,1)S(1)}, bf16[144,512]{1,0:T(8,128)(2,1)S(1)}, u32[]{:S(2)}, u32[]{:S(2)}) collective-permute-start(bf16[144,512]{1,0:T(8,128)(2,1)S(1)} %collective-permute-done.12.b3), channel_id=1, source_target_pairs={{0,2},{1,3},{2,0},{3,1},{4,6},{5,7},{6,4},{7,5},{8,10},{9,11},{10,... | collective-permute-start | bytes 442376 | tf_op jit(solution)/shard_map/ppermute | solution.py:485
  53.8 6.0 %collective-permute-done.11.b2 = bf16[144,512]{1,0:T(8,128)(2,1)S(1)} collective-permute-done((bf16[144,512]{1,0:T(8,128)(2,1)S(1)}, bf16[144,512]{1,0:T(8,128)(2,1)S(1)}, u32[]{:S(2)}, u32[]{:S(2)}) %collective-permute-start.11) | collective-permute-done | bytes 147488 | tf_op jit(solution)/shard_map/ppermute | solution.py:471
  59.9 1.1 collective-permute-start.15
  61.0 0.9 collective-permute-start.14
  61.9 1.2 %collective-permute-start.20 = (bf16[384,768]{1,0:T(8,128)(2,1)S(1)}, bf16[384,768]{1,0:T(8,128)(2,1)S(1)}, u32[]{:S(2)}, u32[]{:S(2)}) collective-permute-start(bf16[384,768]{1,0:T(8,128)(2,1)S(1)} %copy-done.11), channel_id=1, source_target_pairs={{0,16},{16,0},{1,17},{17,1},{2,18},{18,2},{3,19},{19,3},{4,20},{20... | collective-permute-start | bytes 1769480 | tf_op jit(solution)/shard_map/ppermute | solution.py:468
  63.1 0.3 norm.2
  63.5 2.3 %collective-permute-done.15.b2 = bf16[144,512]{1,0:T(8,128)(2,1)S(1)} collective-permute-done((bf16[144,512]{1,0:T(8,128)(2,1)S(1)}, bf16[144,512]{1,0:T(8,128)(2,1)S(1)}, u32[]{:S(2)}, u32[]{:S(2)}) %collective-permute-start.15) | collective-permute-done | bytes 147488 | tf_op jit(solution)/shard_map/ppermute | solution.py:485
  65.8 1.6 %collective-permute-done.14.b1 = bf16[144,512]{1,0:T(8,128)(2,1)S(1)} collective-permute-done((bf16[144,512]{1,0:T(8,128)(2,1)S(1)}, bf16[144,512]{1,0:T(8,128)(2,1)S(1)}, u32[]{:S(2)}, u32[]{:S(2)}) %collective-permute-start.14) | collective-permute-done | bytes 147488 | tf_op jit(solution)/shard_map/ppermute | solution.py:485
  67.3 0.8 norm.3
  68.1 2.0 %collective-permute-done.17.group_cx = bf16[128,2176]{1,0:T(8,128)(2,1)S(1)} collective-permute-done((bf16[128,2176]{1,0:T(8,128)(2,1)S(1)}, bf16[128,2176]{1,0:T(8,128)(2,1)S(1)}, u32[]{:S(2)}, u32[]{:S(2)}) %collective-permute-start.17) | collective-permute-done | bytes 557088 | tf_op jit(solution)/shard_map/ppermute | solution.py:485
  70.1 3.4 %first_gate_up.1 = (bf16[384,384]{1,0:T(8,128)(2,1)S(1)}, bf16[128,384]{1,0:T(8,128)(2,1)S(1)}, f32[512,768]{1,0:T(8,128)S(1)}, bf16[512,1024]{1,0:T(8,128)(2,1)S(1)}, f32[512,128]{1,0:T(8,128)S(1)}) custom-call(bf16[128,2176]{1,0:T(8,128)(2,1)S(1)} %get-tuple-element.60.group_x, bf16[128,2176]{1,0:T(8,128)(2,1)S(1)} %collective-permute-done.17.group_cx, ...), custom_call_target="tpu_custom_call" | custom-call | flops 1 | bytes 1 | tf_op jit(solution)/shard_map/first_gate_up/pallas_call | solution.py:456
  73.5 0.9 collective-permute-start.28
  74.4 2.6 %collective-permute-done.20.refs_1_ = bf16[384,768]{1,0:T(8,128)(2,1)S(1)} collective-permute-done((bf16[384,768]{1,0:T(8,128)(2,1)S(1)}, bf16[384,768]{1,0:T(8,128)(2,1)S(1)}, u32[]{:S(2)}, u32[]{:S(2)}) %collective-permute-start.20) | collective-permute-done | bytes 589856 | tf_op jit(solution)/shard_map/ppermute | solution.py:468
  77.1 1.5 %last_gate_up.1 = (bf16[256,384]{1,0:T(8,128)(2,1)S(1)}, bf16[384,384]{1,0:T(8,128)(2,1)S(1)}) custom-call(bf16[128,384]{1,0:T(8,128)(2,1)S(1)} %get-tuple-element.63.second, f32[512,768]{1,0:T(8,128)S(1)} %get-tuple-element.64.part, bf16[512,1024]{1,0:T(8,128)(2,1)S(1)} %get-tuple-element.65.other, f32[512,128]{1,0:T(8,128)S(1)} %get-tuple-element.66.share, ...), custom_call_target="tpu_custom_call" | custom-call | flops 1 | bytes 1 | tf_op jit(solution)/shard_map/last_gate_up/pallas_call | solution.py:456
  78.5 1.0 down_both.1
  79.6 2.6 %collective-permute-start.29 = (bf16[256,384]{1,0:T(8,128)(2,1)S(1)}, bf16[256,384]{1,0:T(8,128)(2,1)S(1)}, u32[]{:S(2)}, u32[]{:S(2)}) collective-permute-start(bf16[256,384]{1,0:T(8,128)(2,1)S(1)} %get-tuple-element.69.far), channel_id=1, source_target_pairs={{0,16},{16,0},{1,17},{17,1},{2,18},{18,2},{3,19},{19,3},{4,20},{20... | collective-permute-start | bytes 589832 | tf_op jit(solution)/shard_map/ppermute | solution.py:468
  82.3 0.3 collective-permute-start.23
  82.9 0.7 collective-permute-done.22.refs_1_
  83.7 0.3 collective-permute-done.24.refs_3_
  84.2 1.6 %collective-permute-start.26 = (bf16[128,1024]{1,0:T(8,128)(2,1)S(1)}, bf16[128,1024]{1,0:T(8,128)(2,1)S(1)}, u32[]{:S(2)}, u32[]{:S(2)}) collective-permute-start(bf16[128,1024]{1,0:T(8,128)(2,1)S(1)} %get-tuple-element.78), channel_id=1, source_target_pairs={{0,4},{1,13},{2,6},{3,15},{4,8},{5,1},{6,10},{7,3},{8,12},{9,5},{1... | collective-permute-start | bytes 786440 | tf_op jit(solution)/shard_map/ppermute | solution.py:482
  85.8 0.7 collective-permute-start.25
  86.5 1.4 %collective-permute-done.29.far = bf16[256,384]{1,0:T(8,128)(2,1)S(1)} collective-permute-done((bf16[256,384]{1,0:T(8,128)(2,1)S(1)}, bf16[256,384]{1,0:T(8,128)(2,1)S(1)}, u32[]{:S(2)}, u32[]{:S(2)}) %collective-permute-start.29) | collective-permute-done | bytes 196640 | tf_op jit(solution)/shard_map/ppermute | solution.py:468
  87.9 0.6 down.2
  88.5 1.8 %collective-permute-start.30 = (bf16[128,512]{1,0:T(8,128)(2,1)S(1)}, bf16[128,512]{1,0:T(8,128)(2,1)S(1)}, u32[]{:S(2)}, u32[]{:S(2)}) collective-permute-start(bf16[128,512]{1,0:T(8,128)(2,1)S(1)} %get-tuple-element.82), channel_id=1, source_target_pairs={{0,1},{1,0},{2,3},{3,2},{4,5},{5,4},{6,7},{7,6},{8,9},{9,8},{10,11... | collective-permute-start | bytes 393224 | tf_op jit(solution)/shard_map/ppermute | solution.py:485
  90.4 0.9 collective-permute-done.30.refs_0_
  91.3 0.4 collective-permute-done.31.refs_1_
  91.8 1.6 %collective-permute-start.32 = (bf16[128,1024]{1,0:T(8,128)(2,1)S(1)}, bf16[128,1024]{1,0:T(8,128)(2,1)S(1)}, u32[]{:S(2)}, u32[]{:S(2)}) collective-permute-start(bf16[128,1024]{1,0:T(8,128)(2,1)S(1)} %fold.1), channel_id=1, source_target_pairs={{0,2},{1,3},{2,0},{3,1},{4,6},{5,7},{6,4},{7,5},{8,10},{9,11},{10,... | collective-permute-start | bytes 786440 | tf_op jit(solution)/shard_map/ppermute | solution.py:485
  93.3 1.8 %collective-permute-done.26.a1 = bf16[128,1024]{1,0:T(8,128)(2,1)S(1)} collective-permute-done((bf16[128,1024]{1,0:T(8,128)(2,1)S(1)}, bf16[128,1024]{1,0:T(8,128)(2,1)S(1)}, u32[]{:S(2)}, u32[]{:S(2)}) %collective-permute-start.26) | collective-permute-done | bytes 262176 | tf_op jit(solution)/shard_map/ppermute | solution.py:482
  95.3 0.6 down.3
  95.9 4.5 %collective-permute-start.34 = (bf16[128,512]{1,0:T(8,128)(2,1)S(1)}, bf16[128,512]{1,0:T(8,128)(2,1)S(1)}, u32[]{:S(2)}, u32[]{:S(2)}) collective-permute-start(bf16[128,512]{1,0:T(8,128)(2,1)S(1)} %get-tuple-element.86), channel_id=1, source_target_pairs={{0,1},{1,0},{2,3},{3,2},{4,5},{5,4},{6,7},{7,6},{8,9},{9,8},{10,11... | collective-permute-start | bytes 393224 | tf_op jit(solution)/shard_map/ppermute | solution.py:485
  100.4 1.5 %collective-permute-start.27 = (bf16[64,1024]{1,0:T(8,128)(2,1)S(1)}, bf16[64,1024]{1,0:T(8,128)(2,1)S(1)}, u32[]{:S(2)}, u32[]{:S(2)}) collective-permute-start(bf16[64,1024]{1,0:T(8,128)(2,1)S(1)} %get-tuple-element.80), channel_id=1, source_target_pairs={{0,2},{1,3},{2,0},{3,1},{4,6},{5,7},{6,4},{7,5},{8,10},{9,11},{10,... | collective-permute-start | bytes 393224 | tf_op jit(solution)/shard_map/ppermute | solution.py:485
  102.0 1.5 %collective-permute-start.36 = (bf16[64,1024]{1,0:T(8,128)(2,1)S(1)}, bf16[64,1024]{1,0:T(8,128)(2,1)S(1)}, u32[]{:S(2)}, u32[]{:S(2)}) collective-permute-start(bf16[64,1024]{1,0:T(8,128)(2,1)S(1)} %get-tuple-element.88), channel_id=1, source_target_pairs={{0,16},{1,25},{2,18},{3,27},{4,20},{5,29},{6,22},{7,31},{8,24},{9,... | collective-permute-start | bytes 393224 | tf_op jit(solution)/shard_map/ppermute | solution.py:482
  103.5 0.3 collective-permute-start.37
  103.8 2.4 %collective-permute-done.27.far = bf16[64,1024]{1,0:T(8,128)(2,1)S(1)} collective-permute-done((bf16[64,1024]{1,0:T(8,128)(2,1)S(1)}, bf16[64,1024]{1,0:T(8,128)(2,1)S(1)}, u32[]{:S(2)}, u32[]{:S(2)}) %collective-permute-start.27) | collective-permute-done | bytes 131104 | tf_op jit(solution)/shard_map/ppermute | solution.py:485
  106.3 3.7 %collective-permute-done.36.b0 = bf16[64,1024]{1,0:T(8,128)(2,1)S(1)} collective-permute-done((bf16[64,1024]{1,0:T(8,128)(2,1)S(1)}, bf16[64,1024]{1,0:T(8,128)(2,1)S(1)}, u32[]{:S(2)}, u32[]{:S(2)}) %collective-permute-start.36) | collective-permute-done | bytes 131104 | tf_op jit(solution)/shard_map/ppermute | solution.py:482
  110.0 1.7 %collective-permute-done.37.b1 = bf16[64,1024]{1,0:T(8,128)(2,1)S(1)} collective-permute-done((bf16[64,1024]{1,0:T(8,128)(2,1)S(1)}, bf16[64,1024]{1,0:T(8,128)(2,1)S(1)}, u32[]{:S(2)}, u32[]{:S(2)}) %collective-permute-start.37) | collective-permute-done | bytes 131104 | tf_op jit(solution)/shard_map/ppermute | solution.py:482
  111.8 1.3 %collective-permute-done.38.core = bf16[64,1024]{1,0:T(8,128)(2,1)S(1)} collective-permute-done((bf16[64,1024]{1,0:T(8,128)(2,1)S(1)}, bf16[64,1024]{1,0:T(8,128)(2,1)S(1)}, u32[]{:S(2)}, u32[]{:S(2)}) %collective-permute-start.38) | collective-permute-done | bytes 131104 | tf_op jit(solution)/shard_map/ppermute | solution.py:485
  113.1 0.8 closing.1
  (63 shorter events, 2.2 us)
Async XLA Ops:
  0.6 1.9 %copy-start = (bf16[1,1024,1536]{2,1,0:T(8,128)(2,1)S(1)}, bf16[1,1024,1536]{2,1,0:T(8,128)(2,1)}, u32[]{:S(2)}) copy-start(bf16[1,1024,1536]{2,1,0:T(8,128)(2,1)} %param.17) | copy-start | bytes 9437188
  2.5 4.7 %copy-start.4 = (bf16[1,32,2048]{2,1,0:T(8,128)(2,1)S(1)}, bf16[1,32,2048]{2,1,0:T(8,128)(2,1)}, u32[]{:S(2)}) copy-start(bf16[1,32,2048]{2,1,0:T(8,128)(2,1)} %param.11) | copy-start | bytes 393220
  2.5 7.9 %copy-start.3 = (bf16[1,64,2048]{2,1,0:T(8,128)(2,1)S(1)}, bf16[1,64,2048]{2,1,0:T(8,128)(2,1)}, u32[]{:S(2)}) copy-start(bf16[1,64,2048]{2,1,0:T(8,128)(2,1)} %param.10) | copy-start | bytes 786436
  2.7 38.3 %collective-permute-start.8 = (bf16[1024,768]{1,0:T(8,128)(2,1)S(1)}, bf16[1024,768]{1,0:T(8,128)(2,1)S(1)}, u32[]{:S(2)}, u32[]{:S(2)}) collective-permute-start(bf16[1024,768]{1,0:T(8,128)(2,1)S(1)} %weight_piece.3), channel_id=1, source_target_pairs={{0,16},{16,0},{1,17},{17,1},{2,18},{18,2},{3,19},{19,3},{4,20},{20... | collective-permute-start | bytes 4718600 | tf_op jit(solution)/shard_map/ppermute | solution.py:468
  5.7 13.7 %collective-permute-start.5 = (bf16[2048,128]{1,0:T(8,128)(2,1)}, bf16[2048,128]{1,0:T(8,128)(2,1)}, u32[]{:S(2)}, u32[]{:S(2)}) collective-permute-start(bf16[2048,128]{1,0:T(8,128)(2,1)} %w0.1), channel_id=1, source_target_pairs={{0,2},{1,3},{2,0},{3,1},{4,6},{5,7},{6,4},{7,5},{8,10},{9,11},{10,... | collective-permute-start | bytes 1572872 | tf_op jit(solution)/shard_map/ppermute | solution.py:485
  7.9 4.7 %copy-start.6 = (bf16[32,512]{1,0:T(8,128)(2,1)}, bf16[32,512]{1,0:T(8,128)(2,1)S(1)}, u32[]{:S(2)}) copy-start(bf16[32,512]{1,0:T(8,128)(2,1)S(1)} %get-tuple-element.50) | copy-start | bytes 98308
  7.9 11.6 %collective-permute-start.2 = (bf16[64,512]{1,0:T(8,128)(2,1)}, bf16[64,512]{1,0:T(8,128)(2,1)S(1)}, u32[]{:S(2)}, u32[]{:S(2)}) collective-permute-start(bf16[64,512]{1,0:T(8,128)(2,1)} %get-tuple-element.48), channel_id=1, source_target_pairs={{0,8},{1,9},{2,10},{3,11},{4,12},{5,13},{6,14},{7,15},{8,0},{9,1},... | collective-permute-start | bytes 196616 | tf_op jit(solution)/shard_map/ppermute | solution.py:488
  10.5 4.6 %copy-start.12 = (s32[1,32,8]{1,2,0:T(8,128)S(1)}, s32[1,32,8]{1,2,0:T(8,128)}, u32[]{:S(2)}) copy-start(s32[1,32,8]{1,2,0:T(8,128)} %param.14) | copy-start | bytes 3076
  10.5 14.9 %collective-permute-start.1 = (bf16[64,2048]{1,0:T(8,128)(2,1)S(1)}, bf16[64,2048]{1,0:T(8,128)(2,1)}, u32[]{:S(2)}, u32[]{:S(2)}) collective-permute-start(bf16[64,2048]{1,0:T(8,128)(2,1)S(1)} %bitcast.16), channel_id=1, source_target_pairs={{0,8},{1,9},{2,10},{3,11},{4,12},{5,13},{6,14},{7,15},{8,0},{9,1},... | collective-permute-start | bytes 786440 | tf_op jit(solution)/shard_map/ppermute | solution.py:488
  10.8 14.5 %collective-permute-start = (bf16[64,2048]{1,0:T(8,128)(2,1)S(1)}, bf16[64,2048]{1,0:T(8,128)(2,1)}, u32[]{:S(2)}, u32[]{:S(2)}) collective-permute-start(bf16[64,2048]{1,0:T(8,128)(2,1)S(1)} %bitcast.17), channel_id=1, source_target_pairs={{0,4},{1,5},{2,6},{3,7},{4,0},{5,1},{6,2},{7,3},{8,12},{9,13},{10,... | collective-permute-start | bytes 786440 | tf_op jit(solution)/shard_map/ppermute | solution.py:488
  12.6 1.0 copy-start.8
  13.6 0.8 copy-start.10
  19.4 15.4 %collective-permute-start.7 = (bf16[2048,128]{1,0:T(8,128)(2,1)}, bf16[2048,128]{1,0:T(8,128)(2,1)S(1)}, u32[]{:S(2)}, u32[]{:S(2)}) collective-permute-start(bf16[2048,128]{1,0:T(8,128)(2,1)} %collective-permute-done.5.w2), channel_id=1, source_target_pairs={{0,1},{1,0},{2,3},{3,2},{4,5},{5,4},{6,7},{7,6},{8,9},{9,8},{10,11... | collective-permute-start | bytes 1572872 | tf_op jit(solution)/shard_map/ppermute | solution.py:485
  19.5 15.4 %collective-permute-start.6 = (bf16[2048,128]{1,0:T(8,128)(2,1)}, bf16[2048,128]{1,0:T(8,128)(2,1)S(1)}, u32[]{:S(2)}, u32[]{:S(2)}) collective-permute-start(bf16[2048,128]{1,0:T(8,128)(2,1)} %w0.1), channel_id=1, source_target_pairs={{0,1},{1,0},{2,3},{3,2},{4,5},{5,4},{6,7},{7,6},{8,9},{9,8},{10,11... | collective-permute-start | bytes 1572872 | tf_op jit(solution)/shard_map/ppermute | solution.py:485
  25.4 9.5 %collective-permute-start.3 = (bf16[64,2048]{1,0:T(8,128)(2,1)}, bf16[64,2048]{1,0:T(8,128)(2,1)S(1)}, u32[]{:S(2)}, u32[]{:S(2)}) collective-permute-start(bf16[64,2048]{1,0:T(8,128)(2,1)} %collective-permute-done.1.a2), channel_id=1, source_target_pairs={{0,4},{1,5},{2,6},{3,7},{4,0},{5,1},{6,2},{7,3},{8,12},{9,13},{10,... | collective-permute-start | bytes 786440 | tf_op jit(solution)/shard_map/ppermute | solution.py:488
  26.3 12.0 %copy-start.9 = (bf16[640,768]{1,0:T(8,128)(2,1)S(1)}, bf16[640,768]{1,0:T(8,128)(2,1)}, u32[]{:S(2)}) copy-start(bf16[640,768]{1,0:T(8,128)(2,1)} %copy-done.8) | copy-start | bytes 2949124
  26.3 35.6 %copy-start.11 = (bf16[384,768]{1,0:T(8,128)(2,1)S(1)}, bf16[384,768]{1,0:T(8,128)(2,1)}, u32[]{:S(2)}) copy-start(bf16[384,768]{1,0:T(8,128)(2,1)} %copy-done.10) | copy-start | bytes 1769476
  26.4 36.7 %copy-start.5 = (f32[2048]{0:T(1024)S(1)}, f32[2048]{0:T(1024)}, u32[]{:S(2)}) copy-start(f32[2048]{0:T(1024)} %param.13) | copy-start | bytes 24580
  26.4 8.5 %collective-permute-start.4 = (bf16[64,512]{1,0:T(8,128)(2,1)S(1)}, bf16[64,512]{1,0:T(8,128)(2,1)S(1)}, u32[]{:S(2)}, u32[]{:S(2)}) collective-permute-start(bf16[64,512]{1,0:T(8,128)(2,1)S(1)} %pad_maximum_fusion), channel_id=1, source_target_pairs={{0,4},{1,5},{2,6},{3,7},{4,0},{5,1},{6,2},{7,3},{8,12},{9,13},{10,... | collective-permute-start | bytes 196616 | tf_op jit(solution)/shard_map/ppermute | solution.py:488
  34.9 35.2 %copy-start.1 = (bf16[1,1024,1536]{2,1,0:T(8,128)(2,1)S(1)}, bf16[1,1024,1536]{2,1,0:T(8,128)(2,1)}, u32[]{:S(2)}) copy-start(bf16[1,1024,1536]{2,1,0:T(8,128)(2,1)} %param.17) | copy-start | bytes 9437188
  37.8 6.5 %collective-permute-start.9 = (bf16[128,512]{1,0:T(8,128)(2,1)S(1)}, bf16[128,512]{1,0:T(8,128)(2,1)S(1)}, u32[]{:S(2)}, u32[]{:S(2)}) collective-permute-start(bf16[128,512]{1,0:T(8,128)(2,1)S(1)} %get-tuple-element.57), channel_id=1, source_target_pairs={{0,16},{16,0},{1,17},{17,1},{2,18},{18,2},{3,19},{19,3},{4,20},{20... | collective-permute-start | bytes 393224 | tf_op jit(solution)/shard_map/ppermute | solution.py:468
  38.3 38.7 %collective-permute-start.19 = (bf16[640,768]{1,0:T(8,128)(2,1)S(1)}, bf16[640,768]{1,0:T(8,128)(2,1)S(1)}, u32[]{:S(2)}, u32[]{:S(2)}) collective-permute-start(bf16[640,768]{1,0:T(8,128)(2,1)S(1)} %copy-done.9), channel_id=1, source_target_pairs={{0,16},{16,0},{1,17},{17,1},{2,18},{18,2},{3,19},{19,3},{4,20},{20... | collective-permute-start | bytes 2949128 | tf_op jit(solution)/shard_map/ppermute | solution.py:468
  44.3 7.8 %collective-permute-start.12 = (bf16[144,512]{1,0:T(8,128)(2,1)S(1)}, bf16[144,512]{1,0:T(8,128)(2,1)S(1)}, u32[]{:S(2)}, u32[]{:S(2)}) collective-permute-start(bf16[144,512]{1,0:T(8,128)(2,1)S(1)} %stream.1.b0), channel_id=1, source_target_pairs={{0,12},{1,13},{2,14},{3,15},{4,0},{5,1},{6,2},{7,3},{8,4},{9,5},{1... | collective-permute-start | bytes 442376 | tf_op jit(solution)/shard_map/ppermute | solution.py:471
  47.8 12.0 %collective-permute-start.11 = (bf16[144,512]{1,0:T(8,128)(2,1)S(1)}, bf16[144,512]{1,0:T(8,128)(2,1)S(1)}, u32[]{:S(2)}, u32[]{:S(2)}) collective-permute-start(bf16[144,512]{1,0:T(8,128)(2,1)S(1)} %stream.1.b0), channel_id=1, source_target_pairs={{0,8},{1,9},{2,10},{3,11},{4,12},{5,13},{6,14},{7,15},{8,0},{9,1},... | collective-permute-start | bytes 442376 | tf_op jit(solution)/shard_map/ppermute | solution.py:471
  47.8 13.2 %collective-permute-start.10 = (bf16[144,512]{1,0:T(8,128)(2,1)S(1)}, bf16[144,512]{1,0:T(8,128)(2,1)S(1)}, u32[]{:S(2)}, u32[]{:S(2)}) collective-permute-start(bf16[144,512]{1,0:T(8,128)(2,1)S(1)} %stream.1.b0), channel_id=1, source_target_pairs={{0,4},{1,5},{2,6},{3,7},{4,8},{5,9},{6,10},{7,11},{8,12},{9,13},{1... | collective-permute-start | bytes 442376 | tf_op jit(solution)/shard_map/ppermute | solution.py:471
  48.7 13.2 %collective-permute-start.13 = (bf16[144,512]{1,0:T(8,128)(2,1)S(1)}, bf16[144,512]{1,0:T(8,128)(2,1)S(1)}, u32[]{:S(2)}, u32[]{:S(2)}) collective-permute-start(bf16[144,512]{1,0:T(8,128)(2,1)S(1)} %stream.1.b0), channel_id=1, source_target_pairs={{0,2},{1,3},{2,0},{3,1},{4,6},{5,7},{6,4},{7,5},{8,10},{9,11},{10,... | collective-permute-start | bytes 442376 | tf_op jit(solution)/shard_map/ppermute | solution.py:485
  52.1 11.3 %collective-permute-start.16 = (bf16[144,512]{1,0:T(8,128)(2,1)S(1)}, bf16[144,512]{1,0:T(8,128)(2,1)S(1)}, u32[]{:S(2)}, u32[]{:S(2)}) collective-permute-start(bf16[144,512]{1,0:T(8,128)(2,1)S(1)} %collective-permute-done.12.b3), channel_id=1, source_target_pairs={{0,2},{1,3},{2,0},{3,1},{4,6},{5,7},{6,4},{7,5},{8,10},{9,11},{10,... | collective-permute-start | bytes 442376 | tf_op jit(solution)/shard_map/ppermute | solution.py:485
  59.9 5.9 %collective-permute-start.15 = (bf16[144,512]{1,0:T(8,128)(2,1)S(1)}, bf16[144,512]{1,0:T(8,128)(2,1)S(1)}, u32[]{:S(2)}, u32[]{:S(2)}) collective-permute-start(bf16[144,512]{1,0:T(8,128)(2,1)S(1)} %collective-permute-done.11.b2), channel_id=1, source_target_pairs={{0,2},{1,3},{2,0},{3,1},{4,6},{5,7},{6,4},{7,5},{8,10},{9,11},{10,... | collective-permute-start | bytes 442376 | tf_op jit(solution)/shard_map/ppermute | solution.py:485
  61.0 6.3 %collective-permute-start.14 = (bf16[144,512]{1,0:T(8,128)(2,1)S(1)}, bf16[144,512]{1,0:T(8,128)(2,1)S(1)}, u32[]{:S(2)}, u32[]{:S(2)}) collective-permute-start(bf16[144,512]{1,0:T(8,128)(2,1)S(1)} %collective-permute-done.10.b1), channel_id=1, source_target_pairs={{0,2},{1,3},{2,0},{3,1},{4,6},{5,7},{6,4},{7,5},{8,10},{9,11},{10,... | collective-permute-start | bytes 442376 | tf_op jit(solution)/shard_map/ppermute | solution.py:485
  61.9 15.1 %collective-permute-start.20 = (bf16[384,768]{1,0:T(8,128)(2,1)S(1)}, bf16[384,768]{1,0:T(8,128)(2,1)S(1)}, u32[]{:S(2)}, u32[]{:S(2)}) collective-permute-start(bf16[384,768]{1,0:T(8,128)(2,1)S(1)} %copy-done.11), channel_id=1, source_target_pairs={{0,16},{16,0},{1,17},{17,1},{2,18},{18,2},{3,19},{19,3},{4,20},{20... | collective-permute-start | bytes 1769480 | tf_op jit(solution)/shard_map/ppermute | solution.py:468
  63.4 4.7 %collective-permute-start.18 = (bf16[128,2176]{1,0:T(8,128)(2,1)S(1)}, bf16[128,2176]{1,0:T(8,128)(2,1)S(1)}, u32[]{:S(2)}, u32[]{:S(2)}) collective-permute-start(bf16[128,2176]{1,0:T(8,128)(2,1)S(1)} %get-tuple-element.61.group), channel_id=1, source_target_pairs={{0,1},{1,0},{2,3},{3,2},{4,5},{5,4},{6,7},{7,6},{8,9},{9,8},{10,11... | collective-permute-start | bytes 1671176 | tf_op jit(solution)/shard_map/ppermute | solution.py:485
  68.1 2.0 %collective-permute-start.17 = (bf16[128,2176]{1,0:T(8,128)(2,1)S(1)}, bf16[128,2176]{1,0:T(8,128)(2,1)S(1)}, u32[]{:S(2)}, u32[]{:S(2)}) collective-permute-start(bf16[128,2176]{1,0:T(8,128)(2,1)S(1)} %get-tuple-element.60.group_x), channel_id=1, source_target_pairs={{0,1},{1,0},{2,3},{3,2},{4,5},{5,4},{6,7},{7,6},{8,9},{9,8},{10,11... | collective-permute-start | bytes 1671176 | tf_op jit(solution)/shard_map/ppermute | solution.py:485
  73.5 14.4 %collective-permute-start.28 = (bf16[384,384]{1,0:T(8,128)(2,1)S(1)}, bf16[384,384]{1,0:T(8,128)(2,1)S(1)}, u32[]{:S(2)}, u32[]{:S(2)}) collective-permute-start(bf16[384,384]{1,0:T(8,128)(2,1)S(1)} %get-tuple-element.62.first), channel_id=1, source_target_pairs={{0,16},{16,0},{1,17},{17,1},{2,18},{18,2},{3,19},{19,3},{4,20},{20... | collective-permute-start | bytes 884744 | tf_op jit(solution)/shard_map/ppermute | solution.py:468
  77.1 1.5 %copy-start.2 = (bf16[1,768,1024]{2,1,0:T(8,128)(2,1)S(1)}, bf16[1,768,1024]{2,1,0:T(8,128)(2,1)}, u32[]{:S(2)}) copy-start(bf16[1,768,1024]{2,1,0:T(8,128)(2,1)} %param.18) | copy-start | bytes 4718596
  79.5 3.2 %collective-permute-start.21 = (bf16[128,512]{1,0:T(8,128)(2,1)S(1)}, bf16[128,512]{1,0:T(8,128)(2,1)S(1)}, u32[]{:S(2)}, u32[]{:S(2)}) collective-permute-start(bf16[128,512]{1,0:T(8,128)(2,1)S(1)} %get-tuple-element.73), channel_id=1, source_target_pairs={{0,1},{1,0},{2,3},{3,2},{4,5},{5,4},{6,7},{7,6},{8,9},{9,8},{10,11... | collective-permute-start | bytes 393224 | tf_op jit(solution)/shard_map/ppermute | solution.py:485
  79.6 8.3 %collective-permute-start.29 = (bf16[256,384]{1,0:T(8,128)(2,1)S(1)}, bf16[256,384]{1,0:T(8,128)(2,1)S(1)}, u32[]{:S(2)}, u32[]{:S(2)}) collective-permute-start(bf16[256,384]{1,0:T(8,128)(2,1)S(1)} %get-tuple-element.69.far), channel_id=1, source_target_pairs={{0,16},{16,0},{1,17},{17,1},{2,18},{18,2},{3,19},{19,3},{4,20},{20... | collective-permute-start | bytes 589832 | tf_op jit(solution)/shard_map/ppermute | solution.py:468
  82.2 1.3 %collective-permute-start.22 = (bf16[128,512]{1,0:T(8,128)(2,1)S(1)}, bf16[128,512]{1,0:T(8,128)(2,1)S(1)}, u32[]{:S(2)}, u32[]{:S(2)}) collective-permute-start(bf16[128,512]{1,0:T(8,128)(2,1)S(1)} %get-tuple-element.74), channel_id=1, source_target_pairs={{0,1},{1,0},{2,3},{3,2},{4,5},{5,4},{6,7},{7,6},{8,9},{9,8},{10,11... | collective-permute-start | bytes 393224 | tf_op jit(solution)/shard_map/ppermute | solution.py:485
  82.3 1.4 %collective-permute-start.23 = (bf16[128,512]{1,0:T(8,128)(2,1)S(1)}, bf16[128,512]{1,0:T(8,128)(2,1)S(1)}, u32[]{:S(2)}, u32[]{:S(2)}) collective-permute-start(bf16[128,512]{1,0:T(8,128)(2,1)S(1)} %get-tuple-element.75), channel_id=1, source_target_pairs={{0,1},{1,0},{2,3},{3,2},{4,5},{5,4},{6,7},{7,6},{8,9},{9,8},{10,11... | collective-permute-start | bytes 393224 | tf_op jit(solution)/shard_map/ppermute | solution.py:485
  82.7 1.3 %collective-permute-start.24 = (bf16[128,512]{1,0:T(8,128)(2,1)S(1)}, bf16[128,512]{1,0:T(8,128)(2,1)S(1)}, u32[]{:S(2)}, u32[]{:S(2)}) collective-permute-start(bf16[128,512]{1,0:T(8,128)(2,1)S(1)} %get-tuple-element.76), channel_id=1, source_target_pairs={{0,1},{1,0},{2,3},{3,2},{4,5},{5,4},{6,7},{7,6},{8,9},{9,8},{10,11... | collective-permute-start | bytes 393224 | tf_op jit(solution)/shard_map/ppermute | solution.py:485
  83.5 11.7 %collective-permute-start.33 = (bf16[384,384]{1,0:T(8,128)(2,1)S(1)}, bf16[384,384]{1,0:T(8,128)(2,1)S(1)}, u32[]{:S(2)}, u32[]{:S(2)}) collective-permute-start(bf16[384,384]{1,0:T(8,128)(2,1)S(1)} %get-tuple-element.70.rest), channel_id=1, source_target_pairs={{0,16},{16,0},{1,17},{17,1},{2,18},{18,2},{3,19},{19,3},{4,20},{20... | collective-permute-start | bytes 884744 | tf_op jit(solution)/shard_map/ppermute | solution.py:468
  84.2 11.0 %collective-permute-start.26 = (bf16[128,1024]{1,0:T(8,128)(2,1)S(1)}, bf16[128,1024]{1,0:T(8,128)(2,1)S(1)}, u32[]{:S(2)}, u32[]{:S(2)}) collective-permute-start(bf16[128,1024]{1,0:T(8,128)(2,1)S(1)} %get-tuple-element.78), channel_id=1, source_target_pairs={{0,4},{1,13},{2,6},{3,15},{4,8},{5,1},{6,10},{7,3},{8,12},{9,5},{1... | collective-permute-start | bytes 786440 | tf_op jit(solution)/shard_map/ppermute | solution.py:482
  85.8 9.4 %collective-permute-start.25 = (bf16[128,1024]{1,0:T(8,128)(2,1)S(1)}, bf16[128,1024]{1,0:T(8,128)(2,1)S(1)}, u32[]{:S(2)}, u32[]{:S(2)}) collective-permute-start(bf16[128,1024]{1,0:T(8,128)(2,1)S(1)} %get-tuple-element.77.own), channel_id=1, source_target_pairs={{1,9},{3,11},{5,13},{7,15},{9,1},{11,3},{13,5},{15,7},{17,25},{19,... | collective-permute-start | bytes 786440 | tf_op jit(solution)/shard_map/ppermute | solution.py:482
  88.5 2.8 %collective-permute-start.30 = (bf16[128,512]{1,0:T(8,128)(2,1)S(1)}, bf16[128,512]{1,0:T(8,128)(2,1)S(1)}, u32[]{:S(2)}, u32[]{:S(2)}) collective-permute-start(bf16[128,512]{1,0:T(8,128)(2,1)S(1)} %get-tuple-element.82), channel_id=1, source_target_pairs={{0,1},{1,0},{2,3},{3,2},{4,5},{5,4},{6,7},{7,6},{8,9},{9,8},{10,11... | collective-permute-start | bytes 393224 | tf_op jit(solution)/shard_map/ppermute | solution.py:485
  90.3 1.3 %collective-permute-start.31 = (bf16[128,512]{1,0:T(8,128)(2,1)S(1)}, bf16[128,512]{1,0:T(8,128)(2,1)S(1)}, u32[]{:S(2)}, u32[]{:S(2)}) collective-permute-start(bf16[128,512]{1,0:T(8,128)(2,1)S(1)} %get-tuple-element.83), channel_id=1, source_target_pairs={{0,1},{1,0},{2,3},{3,2},{4,5},{5,4},{6,7},{7,6},{8,9},{9,8},{10,11... | collective-permute-start | bytes 393224 | tf_op jit(solution)/shard_map/ppermute | solution.py:485
  91.8 10.2 %collective-permute-start.32 = (bf16[128,1024]{1,0:T(8,128)(2,1)S(1)}, bf16[128,1024]{1,0:T(8,128)(2,1)S(1)}, u32[]{:S(2)}, u32[]{:S(2)}) collective-permute-start(bf16[128,1024]{1,0:T(8,128)(2,1)S(1)} %fold.1), channel_id=1, source_target_pairs={{0,2},{1,3},{2,0},{3,1},{4,6},{5,7},{6,4},{7,5},{8,10},{9,11},{10,... | collective-permute-start | bytes 786440 | tf_op jit(solution)/shard_map/ppermute | solution.py:485
  95.3 17.8 %copy-start.7 = (f32[2048]{0:T(1024)S(1)}, f32[2048]{0:T(1024)}, u32[]{:S(2)}) copy-start(f32[2048]{0:T(1024)} %param.19) | copy-start | bytes 24580
  95.9 6.0 %collective-permute-start.34 = (bf16[128,512]{1,0:T(8,128)(2,1)S(1)}, bf16[128,512]{1,0:T(8,128)(2,1)S(1)}, u32[]{:S(2)}, u32[]{:S(2)}) collective-permute-start(bf16[128,512]{1,0:T(8,128)(2,1)S(1)} %get-tuple-element.86), channel_id=1, source_target_pairs={{0,1},{1,0},{2,3},{3,2},{4,5},{5,4},{6,7},{7,6},{8,9},{9,8},{10,11... | collective-permute-start | bytes 393224 | tf_op jit(solution)/shard_map/ppermute | solution.py:485
  100.4 1.6 %collective-permute-start.35 = (bf16[128,512]{1,0:T(8,128)(2,1)S(1)}, bf16[128,512]{1,0:T(8,128)(2,1)S(1)}, u32[]{:S(2)}, u32[]{:S(2)}) collective-permute-start(bf16[128,512]{1,0:T(8,128)(2,1)S(1)} %get-tuple-element.87), channel_id=1, source_target_pairs={{0,1},{1,0},{2,3},{3,2},{4,5},{5,4},{6,7},{7,6},{8,9},{9,8},{10,11... | collective-permute-start | bytes 393224 | tf_op jit(solution)/shard_map/ppermute | solution.py:485
  100.4 5.8 %collective-permute-start.27 = (bf16[64,1024]{1,0:T(8,128)(2,1)S(1)}, bf16[64,1024]{1,0:T(8,128)(2,1)S(1)}, u32[]{:S(2)}, u32[]{:S(2)}) collective-permute-start(bf16[64,1024]{1,0:T(8,128)(2,1)S(1)} %get-tuple-element.80), channel_id=1, source_target_pairs={{0,2},{1,3},{2,0},{3,1},{4,6},{5,7},{6,4},{7,5},{8,10},{9,11},{10,... | collective-permute-start | bytes 393224 | tf_op jit(solution)/shard_map/ppermute | solution.py:485
  102.0 7.9 %collective-permute-start.36 = (bf16[64,1024]{1,0:T(8,128)(2,1)S(1)}, bf16[64,1024]{1,0:T(8,128)(2,1)S(1)}, u32[]{:S(2)}, u32[]{:S(2)}) collective-permute-start(bf16[64,1024]{1,0:T(8,128)(2,1)S(1)} %get-tuple-element.88), channel_id=1, source_target_pairs={{0,16},{1,25},{2,18},{3,27},{4,20},{5,29},{6,22},{7,31},{8,24},{9,... | collective-permute-start | bytes 393224 | tf_op jit(solution)/shard_map/ppermute | solution.py:482
  103.5 8.1 %collective-permute-start.37 = (bf16[64,1024]{1,0:T(8,128)(2,1)S(1)}, bf16[64,1024]{1,0:T(8,128)(2,1)S(1)}, u32[]{:S(2)}, u32[]{:S(2)}) collective-permute-start(bf16[64,1024]{1,0:T(8,128)(2,1)S(1)} %get-tuple-element.89), channel_id=1, source_target_pairs={{0,20},{1,29},{2,22},{3,31},{4,24},{5,17},{6,26},{7,19},{8,28},{9,... | collective-permute-start | bytes 393224 | tf_op jit(solution)/shard_map/ppermute | solution.py:482
  111.7 1.4 %collective-permute-start.38 = (bf16[64,1024]{1,0:T(8,128)(2,1)S(1)}, bf16[64,1024]{1,0:T(8,128)(2,1)S(1)}, u32[]{:S(2)}, u32[]{:S(2)}) collective-permute-start(bf16[64,1024]{1,0:T(8,128)(2,1)S(1)} %get-tuple-element.91), channel_id=1, source_target_pairs={{0,1},{1,0},{2,3},{3,2},{4,5},{5,4},{6,7},{7,6},{8,9},{9,8},{10,11... | collective-permute-start | bytes 393224 | tf_op jit(solution)/shard_map/ppermute | solution.py:485

commit v20 on v19

--- a/solution.py
+++ b/solution.py
@@ -653,8 +653,8 @@
 
     keep_far, send = down(down_far_kernel, far_other, 2)
     far = swap_inner(fold(keep_far, swap_cores(send)), 2)
-    keep_near, send = down(down_near_kernel, after(rest_other, mine_near), 2)
-    cut = pieces(far, keep_near, send)
+    keep_near, send = down(down_near_kernel, rest_other, 2)
+    cut = pieces(far, keep_near, [send[0], after(send[1], mine_near)])
     others = [send_outer(cut[i], i, True) for i in range(2)]
 
     sums = shape_of(2 * rows_here, half_width)

time: 114 us -> 113 us (level)
    ppermute x4, waiting for transfers between devices: 7.22 us -> 5.85 us  [send_outer(): return lax.ppermute(x, ('dp', 'expert'), pairs)]
  transfers between devices with their start and end apart: 39 -> 39, of which waited for: 22 -> 23; matrix products, arithmetic and copies ran while one was open for 1% -> 1% of each run, Pallas kernels for 11% -> 11%
where the time goes in v20:
time: 113 us
  waiting for transfers between devices  49.4 us (44%)
  starting transfers between devices  42.8 us (38%)
  Pallas kernels  13.8 us (12%)
  local copies, waits for them, and re-layouts  4.6 us (4%)
  between operations  1.54 us (1%)
    ppermute x20, starting transfers between devices, swap_inner(): return lax.ppermute(x, 'expert', [(i, i ^ j) for i in range(expert_count)])  17.9 us
    ppermute x20, waiting for transfers between devices, swap_inner(): return lax.ppermute(x, 'expert', [(i, i ^ j) for i in range(expert_count)])  14.6 us
    pallas_call x17, Pallas kernels, call(): pl.pallas_call(kernel, out_shape=outs, in_specs=[first] + [vmem] * (len(a...  13.4 us
    ppermute x5, waiting for transfers between devices, swap_outer(): lax.ppermute(x, 'expert', [(i, i ^ 4 * s) for i in range(expert_count)])  12.1 us
    ppermute x7, starting transfers between devices, swap_dp(): return lax.ppermute(x, 'dp', [(0, 1), (1, 0)])  9.85 us
    ppermute x7, waiting for transfers between devices, swap_dp(): return lax.ppermute(x, 'dp', [(0, 1), (1, 0)])  9.22 us
    ppermute x3, waiting for transfers between devices, shift_outer(): lax.ppermute(x, 'expert', [(i, (i + 4 * s) % expert_count) for i in range...  7.64 us
    ppermute x5, starting transfers between devices, swap_outer(): lax.ppermute(x, 'expert', [(i, i ^ 4 * s) for i in range(expert_count)])  6.59 us
  transfers between devices with their start and end apart: 39, of which 23 were waited for; matrix products, arithmetic and copies ran while one was open for 1% of the time, Pallas kernels for 11%

profile of v20, /device:TPU:0, one launch (start us, length us, event | category | flops | bytes accessed | tf_op | source)
XLA Modules:
  0.0 112.9 jit_solution(1288296547747388722)
XLA Ops:
  0.6 1.9 %copy-done = bf16[1,1024,1536]{2,1,0:T(8,128)(2,1)S(1)} copy-done((bf16[1,1024,1536]{2,1,0:T(8,128)(2,1)S(1)}, bf16[1,1024,1536]{2,1,0:T(8,128)(2,1)}, u32[]{:S(2)}) %copy-start) | copy-done | bytes 3145752
  2.7 3.0 %collective-permute-start.8 = (bf16[1024,768]{1,0:T(8,128)(2,1)S(1)}, bf16[1024,768]{1,0:T(8,128)(2,1)S(1)}, u32[]{:S(2)}, u32[]{:S(2)}) collective-permute-start(bf16[1024,768]{1,0:T(8,128)(2,1)S(1)} %weight_piece.3), channel_id=1, source_target_pairs={{0,16},{16,0},{1,17},{17,1},{2,18},{18,2},{3,19},{19,3},{4,20},{20... | collective-permute-start | bytes 4718600 | tf_op jit(solution)/shard_map/ppermute | solution.py:468
  5.7 1.5 %collective-permute-start.5 = (bf16[2048,128]{1,0:T(8,128)(2,1)}, bf16[2048,128]{1,0:T(8,128)(2,1)}, u32[]{:S(2)}, u32[]{:S(2)}) collective-permute-start(bf16[2048,128]{1,0:T(8,128)(2,1)} %w0.1), channel_id=1, source_target_pairs={{0,2},{1,3},{2,0},{3,1},{4,6},{5,7},{6,4},{7,5},{8,10},{9,11},{10,... | collective-permute-start | bytes 1572872 | tf_op jit(solution)/shard_map/ppermute | solution.py:485
  7.2 0.6 cut_resid.1
  7.9 2.6 %collective-permute-start.2 = (bf16[64,512]{1,0:T(8,128)(2,1)}, bf16[64,512]{1,0:T(8,128)(2,1)S(1)}, u32[]{:S(2)}, u32[]{:S(2)}) collective-permute-start(bf16[64,512]{1,0:T(8,128)(2,1)} %get-tuple-element.48), channel_id=1, source_target_pairs={{0,8},{1,9},{2,10},{3,11},{4,12},{5,13},{6,14},{7,15},{8,0},{9,1},... | collective-permute-start | bytes 196616 | tf_op jit(solution)/shard_map/ppermute | solution.py:488
  10.5 0.3 collective-permute-start.1
  10.8 1.6 %collective-permute-start = (bf16[64,2048]{1,0:T(8,128)(2,1)S(1)}, bf16[64,2048]{1,0:T(8,128)(2,1)}, u32[]{:S(2)}, u32[]{:S(2)}) collective-permute-start(bf16[64,2048]{1,0:T(8,128)(2,1)S(1)} %bitcast.17), channel_id=1, source_target_pairs={{0,4},{1,5},{2,6},{3,7},{4,0},{5,1},{6,2},{7,3},{8,12},{9,13},{10,... | collective-permute-start | bytes 786440 | tf_op jit(solution)/shard_map/ppermute | solution.py:488
  12.6 1.0 copy-done.8
  13.6 0.8 copy-done.10
  15.2 0.8 copy.13
  15.9 0.4 share.1
  16.4 3.0 %collective-permute-done.5.w2 = bf16[2048,128]{1,0:T(8,128)(2,1)} collective-permute-done((bf16[2048,128]{1,0:T(8,128)(2,1)}, bf16[2048,128]{1,0:T(8,128)(2,1)}, u32[]{:S(2)}, u32[]{:S(2)}) %collective-permute-start.5) | collective-permute-done | bytes 524320 | tf_op jit(solution)/shard_map/ppermute | solution.py:485
  19.5 0.5 collective-permute-start.6
  20.0 5.4 %collective-permute-done.1.a2 = bf16[64,2048]{1,0:T(8,128)(2,1)} collective-permute-done((bf16[64,2048]{1,0:T(8,128)(2,1)S(1)}, bf16[64,2048]{1,0:T(8,128)(2,1)}, u32[]{:S(2)}, u32[]{:S(2)}) %collective-permute-start.1) | collective-permute-done | bytes 262176 | tf_op jit(solution)/shard_map/ppermute | solution.py:488
  25.6 0.8 pad_maximum_fusion
  26.4 1.9 %collective-permute-start.4 = (bf16[64,512]{1,0:T(8,128)(2,1)S(1)}, bf16[64,512]{1,0:T(8,128)(2,1)S(1)}, u32[]{:S(2)}, u32[]{:S(2)}) collective-permute-start(bf16[64,512]{1,0:T(8,128)(2,1)S(1)} %pad_maximum_fusion), channel_id=1, source_target_pairs={{0,4},{1,5},{2,6},{3,7},{4,0},{5,1},{6,2},{7,3},{8,12},{9,13},{10,... | collective-permute-start | bytes 196616 | tf_op jit(solution)/shard_map/ppermute | solution.py:488
  28.2 6.7 %collective-permute-done.4.r13 = bf16[64,512]{1,0:T(8,128)(2,1)S(1)} collective-permute-done((bf16[64,512]{1,0:T(8,128)(2,1)S(1)}, bf16[64,512]{1,0:T(8,128)(2,1)S(1)}, u32[]{:S(2)}, u32[]{:S(2)}) %collective-permute-start.4) | collective-permute-done | bytes 65568 | tf_op jit(solution)/shard_map/ppermute | solution.py:488
  34.9 2.8 %projection.1 = (bf16[128,512]{1,0:T(8,128)(2,1)S(1)}, bf16[128,512]{1,0:T(8,128)(2,1)S(1)}) custom-call(bf16[64,2048]{1,0:T(8,128)(2,1)S(1)} %bitcast.18, bf16[64,2048]{1,0:T(8,128)(2,1)} %collective-permute-done.a1, bf16[64,2048]{1,0:T(8,128)(2,1)} %collective-permute-done.1.a2, bf16[64,2048]{1,0:T(8,128)(2,1)S(1)} %collective-permute-done.3.a3, ...), custom_call_target="tpu_custom_call" | custom-call | flops 1 | bytes 1 | tf_op jit(solution)/shard_map/projection/pallas_call | solution.py:456
  37.8 0.6 collective-permute-start.9
  38.3 1.5 %collective-permute-start.19 = (bf16[640,768]{1,0:T(8,128)(2,1)S(1)}, bf16[640,768]{1,0:T(8,128)(2,1)S(1)}, u32[]{:S(2)}, u32[]{:S(2)}) collective-permute-start(bf16[640,768]{1,0:T(8,128)(2,1)S(1)} %copy-done.9), channel_id=1, source_target_pairs={{0,16},{16,0},{1,17},{17,1},{2,18},{18,2},{3,19},{19,3},{4,20},{20... | collective-permute-start | bytes 2949128 | tf_op jit(solution)/shard_map/ppermute | solution.py:468
  39.9 1.1 collective-permute-done.8.early
  41.0 3.3 %collective-permute-done.9.arrived = bf16[128,512]{1,0:T(8,128)(2,1)S(1)} collective-permute-done((bf16[128,512]{1,0:T(8,128)(2,1)S(1)}, bf16[128,512]{1,0:T(8,128)(2,1)S(1)}, u32[]{:S(2)}, u32[]{:S(2)}) %collective-permute-start.9) | collective-permute-done | bytes 131104 | tf_op jit(solution)/shard_map/ppermute | solution.py:468
  44.3 3.5 %collective-permute-start.12 = (bf16[144,512]{1,0:T(8,128)(2,1)S(1)}, bf16[144,512]{1,0:T(8,128)(2,1)S(1)}, u32[]{:S(2)}, u32[]{:S(2)}) collective-permute-start(bf16[144,512]{1,0:T(8,128)(2,1)S(1)} %stream.1.b0), channel_id=1, source_target_pairs={{0,12},{1,13},{2,14},{3,15},{4,0},{5,1},{6,2},{7,3},{8,4},{9,5},{1... | collective-permute-start | bytes 442376 | tf_op jit(solution)/shard_map/ppermute | solution.py:471
  47.8 0.8 collective-permute-start.10
  48.7 1.9 %collective-permute-start.13 = (bf16[144,512]{1,0:T(8,128)(2,1)S(1)}, bf16[144,512]{1,0:T(8,128)(2,1)S(1)}, u32[]{:S(2)}, u32[]{:S(2)}) collective-permute-start(bf16[144,512]{1,0:T(8,128)(2,1)S(1)} %stream.1.b0), channel_id=1, source_target_pairs={{0,2},{1,3},{2,0},{3,1},{4,6},{5,7},{6,4},{7,5},{8,10},{9,11},{10,... | collective-permute-start | bytes 442376 | tf_op jit(solution)/shard_map/ppermute | solution.py:485
  50.5 1.6 %collective-permute-done.12.b3 = bf16[144,512]{1,0:T(8,128)(2,1)S(1)} collective-permute-done((bf16[144,512]{1,0:T(8,128)(2,1)S(1)}, bf16[144,512]{1,0:T(8,128)(2,1)S(1)}, u32[]{:S(2)}, u32[]{:S(2)}) %collective-permute-start.12) | collective-permute-done | bytes 147488 | tf_op jit(solution)/shard_map/ppermute | solution.py:471
  52.1 1.7 %collective-permute-start.16 = (bf16[144,512]{1,0:T(8,128)(2,1)S(1)}, bf16[144,512]{1,0:T(8,128)(2,1)S(1)}, u32[]{:S(2)}, u32[]{:S(2)}) collective-permute-start(bf16[144,512]{1,0:T(8,128)(2,1)S(1)} %collective-permute-done.12.b3), channel_id=1, source_target_pairs={{0,2},{1,3},{2,0},{3,1},{4,6},{5,7},{6,4},{7,5},{8,10},{9,11},{10,... | collective-permute-start | bytes 442376 | tf_op jit(solution)/shard_map/ppermute | solution.py:485
  53.8 6.0 %collective-permute-done.11.b2 = bf16[144,512]{1,0:T(8,128)(2,1)S(1)} collective-permute-done((bf16[144,512]{1,0:T(8,128)(2,1)S(1)}, bf16[144,512]{1,0:T(8,128)(2,1)S(1)}, u32[]{:S(2)}, u32[]{:S(2)}) %collective-permute-start.11) | collective-permute-done | bytes 147488 | tf_op jit(solution)/shard_map/ppermute | solution.py:471
  59.9 1.1 collective-permute-start.15
  61.0 0.9 collective-permute-start.14
  61.9 1.2 %collective-permute-start.20 = (bf16[384,768]{1,0:T(8,128)(2,1)S(1)}, bf16[384,768]{1,0:T(8,128)(2,1)S(1)}, u32[]{:S(2)}, u32[]{:S(2)}) collective-permute-start(bf16[384,768]{1,0:T(8,128)(2,1)S(1)} %copy-done.11), channel_id=1, source_target_pairs={{0,16},{16,0},{1,17},{17,1},{2,18},{18,2},{3,19},{19,3},{4,20},{20... | collective-permute-start | bytes 1769480 | tf_op jit(solution)/shard_map/ppermute | solution.py:468
  63.5 2.3 %collective-permute-done.15.b2 = bf16[144,512]{1,0:T(8,128)(2,1)S(1)} collective-permute-done((bf16[144,512]{1,0:T(8,128)(2,1)S(1)}, bf16[144,512]{1,0:T(8,128)(2,1)S(1)}, u32[]{:S(2)}, u32[]{:S(2)}) %collective-permute-start.15) | collective-permute-done | bytes 147488 | tf_op jit(solution)/shard_map/ppermute | solution.py:485
  65.8 1.6 %collective-permute-done.14.b1 = bf16[144,512]{1,0:T(8,128)(2,1)S(1)} collective-permute-done((bf16[144,512]{1,0:T(8,128)(2,1)S(1)}, bf16[144,512]{1,0:T(8,128)(2,1)S(1)}, u32[]{:S(2)}, u32[]{:S(2)}) %collective-permute-start.14) | collective-permute-done | bytes 147488 | tf_op jit(solution)/shard_map/ppermute | solution.py:485
  67.3 0.8 norm.3
  68.1 2.0 %collective-permute-done.17.group_cx = bf16[128,2176]{1,0:T(8,128)(2,1)S(1)} collective-permute-done((bf16[128,2176]{1,0:T(8,128)(2,1)S(1)}, bf16[128,2176]{1,0:T(8,128)(2,1)S(1)}, u32[]{:S(2)}, u32[]{:S(2)}) %collective-permute-start.17) | collective-permute-done | bytes 557088 | tf_op jit(solution)/shard_map/ppermute | solution.py:485
  70.1 3.4 %first_gate_up.1 = (bf16[384,384]{1,0:T(8,128)(2,1)S(1)}, bf16[128,384]{1,0:T(8,128)(2,1)S(1)}, f32[512,768]{1,0:T(8,128)S(1)}, bf16[512,1024]{1,0:T(8,128)(2,1)S(1)}, f32[512,128]{1,0:T(8,128)S(1)}) custom-call(bf16[128,2176]{1,0:T(8,128)(2,1)S(1)} %get-tuple-element.60.group_x, bf16[128,2176]{1,0:T(8,128)(2,1)S(1)} %collective-permute-done.17.group_cx, ...), custom_call_target="tpu_custom_call" | custom-call | flops 1 | bytes 1 | tf_op jit(solution)/shard_map/first_gate_up/pallas_call | solution.py:456
  73.5 0.9 collective-permute-start.28
  74.4 2.6 %collective-permute-done.20.refs_1_ = bf16[384,768]{1,0:T(8,128)(2,1)S(1)} collective-permute-done((bf16[384,768]{1,0:T(8,128)(2,1)S(1)}, bf16[384,768]{1,0:T(8,128)(2,1)S(1)}, u32[]{:S(2)}, u32[]{:S(2)}) %collective-permute-start.20) | collective-permute-done | bytes 589856 | tf_op jit(solution)/shard_map/ppermute | solution.py:468
  77.1 1.5 %last_gate_up.1 = (bf16[256,384]{1,0:T(8,128)(2,1)S(1)}, bf16[384,384]{1,0:T(8,128)(2,1)S(1)}) custom-call(bf16[128,384]{1,0:T(8,128)(2,1)S(1)} %get-tuple-element.63.second, f32[512,768]{1,0:T(8,128)S(1)} %get-tuple-element.64.part, bf16[512,1024]{1,0:T(8,128)(2,1)S(1)} %get-tuple-element.65.other, f32[512,128]{1,0:T(8,128)S(1)} %get-tuple-element.66.share, ...), custom_call_target="tpu_custom_call" | custom-call | flops 1 | bytes 1 | tf_op jit(solution)/shard_map/last_gate_up/pallas_call | solution.py:456
  78.5 1.0 down_both.1
  79.6 2.6 %collective-permute-start.29 = (bf16[256,384]{1,0:T(8,128)(2,1)S(1)}, bf16[256,384]{1,0:T(8,128)(2,1)S(1)}, u32[]{:S(2)}, u32[]{:S(2)}) collective-permute-start(bf16[256,384]{1,0:T(8,128)(2,1)S(1)} %get-tuple-element.69.far), channel_id=1, source_target_pairs={{0,16},{16,0},{1,17},{17,1},{2,18},{18,2},{3,19},{19,3},{4,20},{20... | collective-permute-start | bytes 589832 | tf_op jit(solution)/shard_map/ppermute | solution.py:468
  82.3 0.3 collective-permute-start.23
  82.9 0.7 collective-permute-done.22.refs_1_
  83.7 0.3 collective-permute-done.24.refs_3_
  84.2 1.6 %collective-permute-start.26 = (bf16[128,1024]{1,0:T(8,128)(2,1)S(1)}, bf16[128,1024]{1,0:T(8,128)(2,1)S(1)}, u32[]{:S(2)}, u32[]{:S(2)}) collective-permute-start(bf16[128,1024]{1,0:T(8,128)(2,1)S(1)} %get-tuple-element.78), channel_id=1, source_target_pairs={{0,4},{1,13},{2,6},{3,15},{4,8},{5,1},{6,10},{7,3},{8,12},{9,5},{1... | collective-permute-start | bytes 786440 | tf_op jit(solution)/shard_map/ppermute | solution.py:482
  85.8 0.7 collective-permute-start.25
  86.5 1.5 %collective-permute-done.29.far = bf16[256,384]{1,0:T(8,128)(2,1)S(1)} collective-permute-done((bf16[256,384]{1,0:T(8,128)(2,1)S(1)}, bf16[256,384]{1,0:T(8,128)(2,1)S(1)}, u32[]{:S(2)}, u32[]{:S(2)}) %collective-permute-start.29) | collective-permute-done | bytes 196640 | tf_op jit(solution)/shard_map/ppermute | solution.py:468
  87.9 0.6 down.2
  88.5 1.8 %collective-permute-start.30 = (bf16[128,512]{1,0:T(8,128)(2,1)S(1)}, bf16[128,512]{1,0:T(8,128)(2,1)S(1)}, u32[]{:S(2)}, u32[]{:S(2)}) collective-permute-start(bf16[128,512]{1,0:T(8,128)(2,1)S(1)} %get-tuple-element.82), channel_id=1, source_target_pairs={{0,1},{1,0},{2,3},{3,2},{4,5},{5,4},{6,7},{7,6},{8,9},{9,8},{10,11... | collective-permute-start | bytes 393224 | tf_op jit(solution)/shard_map/ppermute | solution.py:485
  90.4 0.9 collective-permute-done.30.refs_0_
  91.3 0.4 collective-permute-done.31.refs_1_
  91.7 1.6 %collective-permute-start.32 = (bf16[128,1024]{1,0:T(8,128)(2,1)S(1)}, bf16[128,1024]{1,0:T(8,128)(2,1)S(1)}, u32[]{:S(2)}, u32[]{:S(2)}) collective-permute-start(bf16[128,1024]{1,0:T(8,128)(2,1)S(1)} %fold.1), channel_id=1, source_target_pairs={{0,2},{1,3},{2,0},{3,1},{4,6},{5,7},{6,4},{7,5},{8,10},{9,11},{10,... | collective-permute-start | bytes 786440 | tf_op jit(solution)/shard_map/ppermute | solution.py:485
  93.3 0.7 collective-permute-done.33.rest
  94.0 0.6 down.3
  94.7 0.5 collective-permute-done.26.a1
  95.2 4.5 %collective-permute-start.35 = (bf16[128,512]{1,0:T(8,128)(2,1)S(1)}, bf16[128,512]{1,0:T(8,128)(2,1)S(1)}, u32[]{:S(2)}, u32[]{:S(2)}) collective-permute-start(bf16[128,512]{1,0:T(8,128)(2,1)S(1)} %get-tuple-element.87), channel_id=1, source_target_pairs={{0,1},{1,0},{2,3},{3,2},{4,5},{5,4},{6,7},{7,6},{8,9},{9,8},{10,11... | collective-permute-start | bytes 393224 | tf_op jit(solution)/shard_map/ppermute | solution.py:485
  99.7 1.5 %collective-permute-start.27 = (bf16[64,1024]{1,0:T(8,128)(2,1)S(1)}, bf16[64,1024]{1,0:T(8,128)(2,1)S(1)}, u32[]{:S(2)}, u32[]{:S(2)}) collective-permute-start(bf16[64,1024]{1,0:T(8,128)(2,1)S(1)} %get-tuple-element.80), channel_id=1, source_target_pairs={{0,2},{1,3},{2,0},{3,1},{4,6},{5,7},{6,4},{7,5},{8,10},{9,11},{10,... | collective-permute-start | bytes 393224 | tf_op jit(solution)/shard_map/ppermute | solution.py:485
  101.3 1.5 %collective-permute-start.36 = (bf16[64,1024]{1,0:T(8,128)(2,1)S(1)}, bf16[64,1024]{1,0:T(8,128)(2,1)S(1)}, u32[]{:S(2)}, u32[]{:S(2)}) collective-permute-start(bf16[64,1024]{1,0:T(8,128)(2,1)S(1)} %get-tuple-element.88), channel_id=1, source_target_pairs={{0,16},{1,25},{2,18},{3,27},{4,20},{5,29},{6,22},{7,31},{8,24},{9,... | collective-permute-start | bytes 393224 | tf_op jit(solution)/shard_map/ppermute | solution.py:482
  102.8 0.3 collective-permute-start.37
  103.1 2.1 %collective-permute-done.27.far = bf16[64,1024]{1,0:T(8,128)(2,1)S(1)} collective-permute-done((bf16[64,1024]{1,0:T(8,128)(2,1)S(1)}, bf16[64,1024]{1,0:T(8,128)(2,1)S(1)}, u32[]{:S(2)}, u32[]{:S(2)}) %collective-permute-start.27) | collective-permute-done | bytes 131104 | tf_op jit(solution)/shard_map/ppermute | solution.py:485
  105.2 4.0 %collective-permute-done.36.b0 = bf16[64,1024]{1,0:T(8,128)(2,1)S(1)} collective-permute-done((bf16[64,1024]{1,0:T(8,128)(2,1)S(1)}, bf16[64,1024]{1,0:T(8,128)(2,1)S(1)}, u32[]{:S(2)}, u32[]{:S(2)}) %collective-permute-start.36) | collective-permute-done | bytes 131104 | tf_op jit(solution)/shard_map/ppermute | solution.py:482
  109.2 1.3 %collective-permute-done.37.b1 = bf16[64,1024]{1,0:T(8,128)(2,1)S(1)} collective-permute-done((bf16[64,1024]{1,0:T(8,128)(2,1)S(1)}, bf16[64,1024]{1,0:T(8,128)(2,1)S(1)}, u32[]{:S(2)}, u32[]{:S(2)}) %collective-permute-start.37) | collective-permute-done | bytes 131104 | tf_op jit(solution)/shard_map/ppermute | solution.py:482
  110.7 1.3 %collective-permute-done.38.core = bf16[64,1024]{1,0:T(8,128)(2,1)S(1)} collective-permute-done((bf16[64,1024]{1,0:T(8,128)(2,1)S(1)}, bf16[64,1024]{1,0:T(8,128)(2,1)S(1)}, u32[]{:S(2)}, u32[]{:S(2)}) %collective-permute-start.38) | collective-permute-done | bytes 131104 | tf_op jit(solution)/shard_map/ppermute | solution.py:485
  112.0 0.8 closing.1
  (63 shorter events, 2.5 us)
Async XLA Ops:
  0.6 1.9 %copy-start = (bf16[1,1024,1536]{2,1,0:T(8,128)(2,1)S(1)}, bf16[1,1024,1536]{2,1,0:T(8,128)(2,1)}, u32[]{:S(2)}) copy-start(bf16[1,1024,1536]{2,1,0:T(8,128)(2,1)} %param.17) | copy-start | bytes 9437188
  2.5 4.7 %copy-start.4 = (bf16[1,32,2048]{2,1,0:T(8,128)(2,1)S(1)}, bf16[1,32,2048]{2,1,0:T(8,128)(2,1)}, u32[]{:S(2)}) copy-start(bf16[1,32,2048]{2,1,0:T(8,128)(2,1)} %param.11) | copy-start | bytes 393220
  2.5 7.9 %copy-start.3 = (bf16[1,64,2048]{2,1,0:T(8,128)(2,1)S(1)}, bf16[1,64,2048]{2,1,0:T(8,128)(2,1)}, u32[]{:S(2)}) copy-start(bf16[1,64,2048]{2,1,0:T(8,128)(2,1)} %param.10) | copy-start | bytes 786436
  2.7 38.3 %collective-permute-start.8 = (bf16[1024,768]{1,0:T(8,128)(2,1)S(1)}, bf16[1024,768]{1,0:T(8,128)(2,1)S(1)}, u32[]{:S(2)}, u32[]{:S(2)}) collective-permute-start(bf16[1024,768]{1,0:T(8,128)(2,1)S(1)} %weight_piece.3), channel_id=1, source_target_pairs={{0,16},{16,0},{1,17},{17,1},{2,18},{18,2},{3,19},{19,3},{4,20},{20... | collective-permute-start | bytes 4718600 | tf_op jit(solution)/shard_map/ppermute | solution.py:468
  5.7 13.7 %collective-permute-start.5 = (bf16[2048,128]{1,0:T(8,128)(2,1)}, bf16[2048,128]{1,0:T(8,128)(2,1)}, u32[]{:S(2)}, u32[]{:S(2)}) collective-permute-start(bf16[2048,128]{1,0:T(8,128)(2,1)} %w0.1), channel_id=1, source_target_pairs={{0,2},{1,3},{2,0},{3,1},{4,6},{5,7},{6,4},{7,5},{8,10},{9,11},{10,... | collective-permute-start | bytes 1572872 | tf_op jit(solution)/shard_map/ppermute | solution.py:485
  7.9 4.7 %copy-start.6 = (bf16[32,512]{1,0:T(8,128)(2,1)}, bf16[32,512]{1,0:T(8,128)(2,1)S(1)}, u32[]{:S(2)}) copy-start(bf16[32,512]{1,0:T(8,128)(2,1)S(1)} %get-tuple-element.50) | copy-start | bytes 98308
  7.9 11.6 %collective-permute-start.2 = (bf16[64,512]{1,0:T(8,128)(2,1)}, bf16[64,512]{1,0:T(8,128)(2,1)S(1)}, u32[]{:S(2)}, u32[]{:S(2)}) collective-permute-start(bf16[64,512]{1,0:T(8,128)(2,1)} %get-tuple-element.48), channel_id=1, source_target_pairs={{0,8},{1,9},{2,10},{3,11},{4,12},{5,13},{6,14},{7,15},{8,0},{9,1},... | collective-permute-start | bytes 196616 | tf_op jit(solution)/shard_map/ppermute | solution.py:488
  10.5 4.6 %copy-start.12 = (s32[1,32,8]{1,2,0:T(8,128)S(1)}, s32[1,32,8]{1,2,0:T(8,128)}, u32[]{:S(2)}) copy-start(s32[1,32,8]{1,2,0:T(8,128)} %param.14) | copy-start | bytes 3076
  10.5 14.9 %collective-permute-start.1 = (bf16[64,2048]{1,0:T(8,128)(2,1)S(1)}, bf16[64,2048]{1,0:T(8,128)(2,1)}, u32[]{:S(2)}, u32[]{:S(2)}) collective-permute-start(bf16[64,2048]{1,0:T(8,128)(2,1)S(1)} %bitcast.16), channel_id=1, source_target_pairs={{0,8},{1,9},{2,10},{3,11},{4,12},{5,13},{6,14},{7,15},{8,0},{9,1},... | collective-permute-start | bytes 786440 | tf_op jit(solution)/shard_map/ppermute | solution.py:488
  10.8 14.5 %collective-permute-start = (bf16[64,2048]{1,0:T(8,128)(2,1)S(1)}, bf16[64,2048]{1,0:T(8,128)(2,1)}, u32[]{:S(2)}, u32[]{:S(2)}) collective-permute-start(bf16[64,2048]{1,0:T(8,128)(2,1)S(1)} %bitcast.17), channel_id=1, source_target_pairs={{0,4},{1,5},{2,6},{3,7},{4,0},{5,1},{6,2},{7,3},{8,12},{9,13},{10,... | collective-permute-start | bytes 786440 | tf_op jit(solution)/shard_map/ppermute | solution.py:488
  12.6 1.0 copy-start.8
  13.6 0.8 copy-start.10
  19.4 15.4 %collective-permute-start.7 = (bf16[2048,128]{1,0:T(8,128)(2,1)}, bf16[2048,128]{1,0:T(8,128)(2,1)S(1)}, u32[]{:S(2)}, u32[]{:S(2)}) collective-permute-start(bf16[2048,128]{1,0:T(8,128)(2,1)} %collective-permute-done.5.w2), channel_id=1, source_target_pairs={{0,1},{1,0},{2,3},{3,2},{4,5},{5,4},{6,7},{7,6},{8,9},{9,8},{10,11... | collective-permute-start | bytes 1572872 | tf_op jit(solution)/shard_map/ppermute | solution.py:485
  19.5 15.4 %collective-permute-start.6 = (bf16[2048,128]{1,0:T(8,128)(2,1)}, bf16[2048,128]{1,0:T(8,128)(2,1)S(1)}, u32[]{:S(2)}, u32[]{:S(2)}) collective-permute-start(bf16[2048,128]{1,0:T(8,128)(2,1)} %w0.1), channel_id=1, source_target_pairs={{0,1},{1,0},{2,3},{3,2},{4,5},{5,4},{6,7},{7,6},{8,9},{9,8},{10,11... | collective-permute-start | bytes 1572872 | tf_op jit(solution)/shard_map/ppermute | solution.py:485
  25.4 9.5 %collective-permute-start.3 = (bf16[64,2048]{1,0:T(8,128)(2,1)}, bf16[64,2048]{1,0:T(8,128)(2,1)S(1)}, u32[]{:S(2)}, u32[]{:S(2)}) collective-permute-start(bf16[64,2048]{1,0:T(8,128)(2,1)} %collective-permute-done.1.a2), channel_id=1, source_target_pairs={{0,4},{1,5},{2,6},{3,7},{4,0},{5,1},{6,2},{7,3},{8,12},{9,13},{10,... | collective-permute-start | bytes 786440 | tf_op jit(solution)/shard_map/ppermute | solution.py:488
  26.3 12.0 %copy-start.9 = (bf16[640,768]{1,0:T(8,128)(2,1)S(1)}, bf16[640,768]{1,0:T(8,128)(2,1)}, u32[]{:S(2)}) copy-start(bf16[640,768]{1,0:T(8,128)(2,1)} %copy-done.8) | copy-start | bytes 2949124
  26.3 35.6 %copy-start.11 = (bf16[384,768]{1,0:T(8,128)(2,1)S(1)}, bf16[384,768]{1,0:T(8,128)(2,1)}, u32[]{:S(2)}) copy-start(bf16[384,768]{1,0:T(8,128)(2,1)} %copy-done.10) | copy-start | bytes 1769476
  26.4 36.7 %copy-start.5 = (f32[2048]{0:T(1024)S(1)}, f32[2048]{0:T(1024)}, u32[]{:S(2)}) copy-start(f32[2048]{0:T(1024)} %param.13) | copy-start | bytes 24580
  26.4 8.5 %collective-permute-start.4 = (bf16[64,512]{1,0:T(8,128)(2,1)S(1)}, bf16[64,512]{1,0:T(8,128)(2,1)S(1)}, u32[]{:S(2)}, u32[]{:S(2)}) collective-permute-start(bf16[64,512]{1,0:T(8,128)(2,1)S(1)} %pad_maximum_fusion), channel_id=1, source_target_pairs={{0,4},{1,5},{2,6},{3,7},{4,0},{5,1},{6,2},{7,3},{8,12},{9,13},{10,... | collective-permute-start | bytes 196616 | tf_op jit(solution)/shard_map/ppermute | solution.py:488
  34.9 35.2 %copy-start.1 = (bf16[1,1024,1536]{2,1,0:T(8,128)(2,1)S(1)}, bf16[1,1024,1536]{2,1,0:T(8,128)(2,1)}, u32[]{:S(2)}) copy-start(bf16[1,1024,1536]{2,1,0:T(8,128)(2,1)} %param.17) | copy-start | bytes 9437188
  37.8 6.5 %collective-permute-start.9 = (bf16[128,512]{1,0:T(8,128)(2,1)S(1)}, bf16[128,512]{1,0:T(8,128)(2,1)S(1)}, u32[]{:S(2)}, u32[]{:S(2)}) collective-permute-start(bf16[128,512]{1,0:T(8,128)(2,1)S(1)} %get-tuple-element.57), channel_id=1, source_target_pairs={{0,16},{16,0},{1,17},{17,1},{2,18},{18,2},{3,19},{19,3},{4,20},{20... | collective-permute-start | bytes 393224 | tf_op jit(solution)/shard_map/ppermute | solution.py:468
  38.3 38.7 %collective-permute-start.19 = (bf16[640,768]{1,0:T(8,128)(2,1)S(1)}, bf16[640,768]{1,0:T(8,128)(2,1)S(1)}, u32[]{:S(2)}, u32[]{:S(2)}) collective-permute-start(bf16[640,768]{1,0:T(8,128)(2,1)S(1)} %copy-done.9), channel_id=1, source_target_pairs={{0,16},{16,0},{1,17},{17,1},{2,18},{18,2},{3,19},{19,3},{4,20},{20... | collective-permute-start | bytes 2949128 | tf_op jit(solution)/shard_map/ppermute | solution.py:468
  44.3 7.8 %collective-permute-start.12 = (bf16[144,512]{1,0:T(8,128)(2,1)S(1)}, bf16[144,512]{1,0:T(8,128)(2,1)S(1)}, u32[]{:S(2)}, u32[]{:S(2)}) collective-permute-start(bf16[144,512]{1,0:T(8,128)(2,1)S(1)} %stream.1.b0), channel_id=1, source_target_pairs={{0,12},{1,13},{2,14},{3,15},{4,0},{5,1},{6,2},{7,3},{8,4},{9,5},{1... | collective-permute-start | bytes 442376 | tf_op jit(solution)/shard_map/ppermute | solution.py:471
  47.8 12.0 %collective-permute-start.11 = (bf16[144,512]{1,0:T(8,128)(2,1)S(1)}, bf16[144,512]{1,0:T(8,128)(2,1)S(1)}, u32[]{:S(2)}, u32[]{:S(2)}) collective-permute-start(bf16[144,512]{1,0:T(8,128)(2,1)S(1)} %stream.1.b0), channel_id=1, source_target_pairs={{0,8},{1,9},{2,10},{3,11},{4,12},{5,13},{6,14},{7,15},{8,0},{9,1},... | collective-permute-start | bytes 442376 | tf_op jit(solution)/shard_map/ppermute | solution.py:471
  47.8 13.2 %collective-permute-start.10 = (bf16[144,512]{1,0:T(8,128)(2,1)S(1)}, bf16[144,512]{1,0:T(8,128)(2,1)S(1)}, u32[]{:S(2)}, u32[]{:S(2)}) collective-permute-start(bf16[144,512]{1,0:T(8,128)(2,1)S(1)} %stream.1.b0), channel_id=1, source_target_pairs={{0,4},{1,5},{2,6},{3,7},{4,8},{5,9},{6,10},{7,11},{8,12},{9,13},{1... | collective-permute-start | bytes 442376 | tf_op jit(solution)/shard_map/ppermute | solution.py:471
  48.7 13.2 %collective-permute-start.13 = (bf16[144,512]{1,0:T(8,128)(2,1)S(1)}, bf16[144,512]{1,0:T(8,128)(2,1)S(1)}, u32[]{:S(2)}, u32[]{:S(2)}) collective-permute-start(bf16[144,512]{1,0:T(8,128)(2,1)S(1)} %stream.1.b0), channel_id=1, source_target_pairs={{0,2},{1,3},{2,0},{3,1},{4,6},{5,7},{6,4},{7,5},{8,10},{9,11},{10,... | collective-permute-start | bytes 442376 | tf_op jit(solution)/shard_map/ppermute | solution.py:485
  52.1 11.3 %collective-permute-start.16 = (bf16[144,512]{1,0:T(8,128)(2,1)S(1)}, bf16[144,512]{1,0:T(8,128)(2,1)S(1)}, u32[]{:S(2)}, u32[]{:S(2)}) collective-permute-start(bf16[144,512]{1,0:T(8,128)(2,1)S(1)} %collective-permute-done.12.b3), channel_id=1, source_target_pairs={{0,2},{1,3},{2,0},{3,1},{4,6},{5,7},{6,4},{7,5},{8,10},{9,11},{10,... | collective-permute-start | bytes 442376 | tf_op jit(solution)/shard_map/ppermute | solution.py:485
  59.9 5.9 %collective-permute-start.15 = (bf16[144,512]{1,0:T(8,128)(2,1)S(1)}, bf16[144,512]{1,0:T(8,128)(2,1)S(1)}, u32[]{:S(2)}, u32[]{:S(2)}) collective-permute-start(bf16[144,512]{1,0:T(8,128)(2,1)S(1)} %collective-permute-done.11.b2), channel_id=1, source_target_pairs={{0,2},{1,3},{2,0},{3,1},{4,6},{5,7},{6,4},{7,5},{8,10},{9,11},{10,... | collective-permute-start | bytes 442376 | tf_op jit(solution)/shard_map/ppermute | solution.py:485
  61.0 6.3 %collective-permute-start.14 = (bf16[144,512]{1,0:T(8,128)(2,1)S(1)}, bf16[144,512]{1,0:T(8,128)(2,1)S(1)}, u32[]{:S(2)}, u32[]{:S(2)}) collective-permute-start(bf16[144,512]{1,0:T(8,128)(2,1)S(1)} %collective-permute-done.10.b1), channel_id=1, source_target_pairs={{0,2},{1,3},{2,0},{3,1},{4,6},{5,7},{6,4},{7,5},{8,10},{9,11},{10,... | collective-permute-start | bytes 442376 | tf_op jit(solution)/shard_map/ppermute | solution.py:485
  61.9 15.1 %collective-permute-start.20 = (bf16[384,768]{1,0:T(8,128)(2,1)S(1)}, bf16[384,768]{1,0:T(8,128)(2,1)S(1)}, u32[]{:S(2)}, u32[]{:S(2)}) collective-permute-start(bf16[384,768]{1,0:T(8,128)(2,1)S(1)} %copy-done.11), channel_id=1, source_target_pairs={{0,16},{16,0},{1,17},{17,1},{2,18},{18,2},{3,19},{19,3},{4,20},{20... | collective-permute-start | bytes 1769480 | tf_op jit(solution)/shard_map/ppermute | solution.py:468
  63.4 4.7 %collective-permute-start.18 = (bf16[128,2176]{1,0:T(8,128)(2,1)S(1)}, bf16[128,2176]{1,0:T(8,128)(2,1)S(1)}, u32[]{:S(2)}, u32[]{:S(2)}) collective-permute-start(bf16[128,2176]{1,0:T(8,128)(2,1)S(1)} %get-tuple-element.61.group), channel_id=1, source_target_pairs={{0,1},{1,0},{2,3},{3,2},{4,5},{5,4},{6,7},{7,6},{8,9},{9,8},{10,11... | collective-permute-start | bytes 1671176 | tf_op jit(solution)/shard_map/ppermute | solution.py:485
  68.1 2.0 %collective-permute-start.17 = (bf16[128,2176]{1,0:T(8,128)(2,1)S(1)}, bf16[128,2176]{1,0:T(8,128)(2,1)S(1)}, u32[]{:S(2)}, u32[]{:S(2)}) collective-permute-start(bf16[128,2176]{1,0:T(8,128)(2,1)S(1)} %get-tuple-element.60.group_x), channel_id=1, source_target_pairs={{0,1},{1,0},{2,3},{3,2},{4,5},{5,4},{6,7},{7,6},{8,9},{9,8},{10,11... | collective-permute-start | bytes 1671176 | tf_op jit(solution)/shard_map/ppermute | solution.py:485
  73.5 14.4 %collective-permute-start.28 = (bf16[384,384]{1,0:T(8,128)(2,1)S(1)}, bf16[384,384]{1,0:T(8,128)(2,1)S(1)}, u32[]{:S(2)}, u32[]{:S(2)}) collective-permute-start(bf16[384,384]{1,0:T(8,128)(2,1)S(1)} %get-tuple-element.62.first), channel_id=1, source_target_pairs={{0,16},{16,0},{1,17},{17,1},{2,18},{18,2},{3,19},{19,3},{4,20},{20... | collective-permute-start | bytes 884744 | tf_op jit(solution)/shard_map/ppermute | solution.py:468
  77.1 1.5 %copy-start.2 = (bf16[1,768,1024]{2,1,0:T(8,128)(2,1)S(1)}, bf16[1,768,1024]{2,1,0:T(8,128)(2,1)}, u32[]{:S(2)}) copy-start(bf16[1,768,1024]{2,1,0:T(8,128)(2,1)} %param.18) | copy-start | bytes 4718596
  79.5 3.2 %collective-permute-start.21 = (bf16[128,512]{1,0:T(8,128)(2,1)S(1)}, bf16[128,512]{1,0:T(8,128)(2,1)S(1)}, u32[]{:S(2)}, u32[]{:S(2)}) collective-permute-start(bf16[128,512]{1,0:T(8,128)(2,1)S(1)} %get-tuple-element.73), channel_id=1, source_target_pairs={{0,1},{1,0},{2,3},{3,2},{4,5},{5,4},{6,7},{7,6},{8,9},{9,8},{10,11... | collective-permute-start | bytes 393224 | tf_op jit(solution)/shard_map/ppermute | solution.py:485
  79.6 8.3 %collective-permute-start.29 = (bf16[256,384]{1,0:T(8,128)(2,1)S(1)}, bf16[256,384]{1,0:T(8,128)(2,1)S(1)}, u32[]{:S(2)}, u32[]{:S(2)}) collective-permute-start(bf16[256,384]{1,0:T(8,128)(2,1)S(1)} %get-tuple-element.69.far), channel_id=1, source_target_pairs={{0,16},{16,0},{1,17},{17,1},{2,18},{18,2},{3,19},{19,3},{4,20},{20... | collective-permute-start | bytes 589832 | tf_op jit(solution)/shard_map/ppermute | solution.py:468
  82.2 1.3 %collective-permute-start.22 = (bf16[128,512]{1,0:T(8,128)(2,1)S(1)}, bf16[128,512]{1,0:T(8,128)(2,1)S(1)}, u32[]{:S(2)}, u32[]{:S(2)}) collective-permute-start(bf16[128,512]{1,0:T(8,128)(2,1)S(1)} %get-tuple-element.74), channel_id=1, source_target_pairs={{0,1},{1,0},{2,3},{3,2},{4,5},{5,4},{6,7},{7,6},{8,9},{9,8},{10,11... | collective-permute-start | bytes 393224 | tf_op jit(solution)/shard_map/ppermute | solution.py:485
  82.3 1.4 %collective-permute-start.23 = (bf16[128,512]{1,0:T(8,128)(2,1)S(1)}, bf16[128,512]{1,0:T(8,128)(2,1)S(1)}, u32[]{:S(2)}, u32[]{:S(2)}) collective-permute-start(bf16[128,512]{1,0:T(8,128)(2,1)S(1)} %get-tuple-element.75), channel_id=1, source_target_pairs={{0,1},{1,0},{2,3},{3,2},{4,5},{5,4},{6,7},{7,6},{8,9},{9,8},{10,11... | collective-permute-start | bytes 393224 | tf_op jit(solution)/shard_map/ppermute | solution.py:485
  82.7 1.3 %collective-permute-start.24 = (bf16[128,512]{1,0:T(8,128)(2,1)S(1)}, bf16[128,512]{1,0:T(8,128)(2,1)S(1)}, u32[]{:S(2)}, u32[]{:S(2)}) collective-permute-start(bf16[128,512]{1,0:T(8,128)(2,1)S(1)} %get-tuple-element.76), channel_id=1, source_target_pairs={{0,1},{1,0},{2,3},{3,2},{4,5},{5,4},{6,7},{7,6},{8,9},{9,8},{10,11... | collective-permute-start | bytes 393224 | tf_op jit(solution)/shard_map/ppermute | solution.py:485
  83.5 10.5 %collective-permute-start.33 = (bf16[384,384]{1,0:T(8,128)(2,1)S(1)}, bf16[384,384]{1,0:T(8,128)(2,1)S(1)}, u32[]{:S(2)}, u32[]{:S(2)}) collective-permute-start(bf16[384,384]{1,0:T(8,128)(2,1)S(1)} %get-tuple-element.70.rest), channel_id=1, source_target_pairs={{0,16},{16,0},{1,17},{17,1},{2,18},{18,2},{3,19},{19,3},{4,20},{20... | collective-permute-start | bytes 884744 | tf_op jit(solution)/shard_map/ppermute | solution.py:468
  84.2 11.0 %collective-permute-start.26 = (bf16[128,1024]{1,0:T(8,128)(2,1)S(1)}, bf16[128,1024]{1,0:T(8,128)(2,1)S(1)}, u32[]{:S(2)}, u32[]{:S(2)}) collective-permute-start(bf16[128,1024]{1,0:T(8,128)(2,1)S(1)} %get-tuple-element.78), channel_id=1, source_target_pairs={{0,4},{1,13},{2,6},{3,15},{4,8},{5,1},{6,10},{7,3},{8,12},{9,5},{1... | collective-permute-start | bytes 786440 | tf_op jit(solution)/shard_map/ppermute | solution.py:482
  85.8 9.4 %collective-permute-start.25 = (bf16[128,1024]{1,0:T(8,128)(2,1)S(1)}, bf16[128,1024]{1,0:T(8,128)(2,1)S(1)}, u32[]{:S(2)}, u32[]{:S(2)}) collective-permute-start(bf16[128,1024]{1,0:T(8,128)(2,1)S(1)} %get-tuple-element.77.own), channel_id=1, source_target_pairs={{1,9},{3,11},{5,13},{7,15},{9,1},{11,3},{13,5},{15,7},{17,25},{19,... | collective-permute-start | bytes 786440 | tf_op jit(solution)/shard_map/ppermute | solution.py:482
  88.5 2.8 %collective-permute-start.30 = (bf16[128,512]{1,0:T(8,128)(2,1)S(1)}, bf16[128,512]{1,0:T(8,128)(2,1)S(1)}, u32[]{:S(2)}, u32[]{:S(2)}) collective-permute-start(bf16[128,512]{1,0:T(8,128)(2,1)S(1)} %get-tuple-element.82), channel_id=1, source_target_pairs={{0,1},{1,0},{2,3},{3,2},{4,5},{5,4},{6,7},{7,6},{8,9},{9,8},{10,11... | collective-permute-start | bytes 393224 | tf_op jit(solution)/shard_map/ppermute | solution.py:485
  90.3 1.3 %collective-permute-start.31 = (bf16[128,512]{1,0:T(8,128)(2,1)S(1)}, bf16[128,512]{1,0:T(8,128)(2,1)S(1)}, u32[]{:S(2)}, u32[]{:S(2)}) collective-permute-start(bf16[128,512]{1,0:T(8,128)(2,1)S(1)} %get-tuple-element.83), channel_id=1, source_target_pairs={{0,1},{1,0},{2,3},{3,2},{4,5},{5,4},{6,7},{7,6},{8,9},{9,8},{10,11... | collective-permute-start | bytes 393224 | tf_op jit(solution)/shard_map/ppermute | solution.py:485
  91.7 9.5 %collective-permute-start.32 = (bf16[128,1024]{1,0:T(8,128)(2,1)S(1)}, bf16[128,1024]{1,0:T(8,128)(2,1)S(1)}, u32[]{:S(2)}, u32[]{:S(2)}) collective-permute-start(bf16[128,1024]{1,0:T(8,128)(2,1)S(1)} %fold.1), channel_id=1, source_target_pairs={{0,2},{1,3},{2,0},{3,1},{4,6},{5,7},{6,4},{7,5},{8,10},{9,11},{10,... | collective-permute-start | bytes 786440 | tf_op jit(solution)/shard_map/ppermute | solution.py:485
  94.6 17.5 %copy-start.7 = (f32[2048]{0:T(1024)S(1)}, f32[2048]{0:T(1024)}, u32[]{:S(2)}) copy-start(f32[2048]{0:T(1024)} %param.19) | copy-start | bytes 24580
  94.6 6.6 %collective-permute-start.34 = (bf16[128,512]{1,0:T(8,128)(2,1)S(1)}, bf16[128,512]{1,0:T(8,128)(2,1)S(1)}, u32[]{:S(2)}, u32[]{:S(2)}) collective-permute-start(bf16[128,512]{1,0:T(8,128)(2,1)S(1)} %get-tuple-element.85), channel_id=1, source_target_pairs={{0,1},{1,0},{2,3},{3,2},{4,5},{5,4},{6,7},{7,6},{8,9},{9,8},{10,11... | collective-permute-start | bytes 393224 | tf_op jit(solution)/shard_map/ppermute | solution.py:485
  95.2 6.0 %collective-permute-start.35 = (bf16[128,512]{1,0:T(8,128)(2,1)S(1)}, bf16[128,512]{1,0:T(8,128)(2,1)S(1)}, u32[]{:S(2)}, u32[]{:S(2)}) collective-permute-start(bf16[128,512]{1,0:T(8,128)(2,1)S(1)} %get-tuple-element.87), channel_id=1, source_target_pairs={{0,1},{1,0},{2,3},{3,2},{4,5},{5,4},{6,7},{7,6},{8,9},{9,8},{10,11... | collective-permute-start | bytes 393224 | tf_op jit(solution)/shard_map/ppermute | solution.py:485
  99.7 5.5 %collective-permute-start.27 = (bf16[64,1024]{1,0:T(8,128)(2,1)S(1)}, bf16[64,1024]{1,0:T(8,128)(2,1)S(1)}, u32[]{:S(2)}, u32[]{:S(2)}) collective-permute-start(bf16[64,1024]{1,0:T(8,128)(2,1)S(1)} %get-tuple-element.80), channel_id=1, source_target_pairs={{0,2},{1,3},{2,0},{3,1},{4,6},{5,7},{6,4},{7,5},{8,10},{9,11},{10,... | collective-permute-start | bytes 393224 | tf_op jit(solution)/shard_map/ppermute | solution.py:485
  101.3 7.9 %collective-permute-start.36 = (bf16[64,1024]{1,0:T(8,128)(2,1)S(1)}, bf16[64,1024]{1,0:T(8,128)(2,1)S(1)}, u32[]{:S(2)}, u32[]{:S(2)}) collective-permute-start(bf16[64,1024]{1,0:T(8,128)(2,1)S(1)} %get-tuple-element.88), channel_id=1, source_target_pairs={{0,16},{1,25},{2,18},{3,27},{4,20},{5,29},{6,22},{7,31},{8,24},{9,... | collective-permute-start | bytes 393224 | tf_op jit(solution)/shard_map/ppermute | solution.py:482
  102.8 7.8 %collective-permute-start.37 = (bf16[64,1024]{1,0:T(8,128)(2,1)S(1)}, bf16[64,1024]{1,0:T(8,128)(2,1)S(1)}, u32[]{:S(2)}, u32[]{:S(2)}) collective-permute-start(bf16[64,1024]{1,0:T(8,128)(2,1)S(1)} %get-tuple-element.89), channel_id=1, source_target_pairs={{0,20},{1,29},{2,22},{3,31},{4,24},{5,17},{6,26},{7,19},{8,28},{9,... | collective-permute-start | bytes 393224 | tf_op jit(solution)/shard_map/ppermute | solution.py:482
  110.6 1.4 %collective-permute-start.38 = (bf16[64,1024]{1,0:T(8,128)(2,1)S(1)}, bf16[64,1024]{1,0:T(8,128)(2,1)S(1)}, u32[]{:S(2)}, u32[]{:S(2)}) collective-permute-start(bf16[64,1024]{1,0:T(8,128)(2,1)S(1)} %get-tuple-element.91), channel_id=1, source_target_pairs={{0,1},{1,0},{2,3},{3,2},{4,5},{5,4},{6,7},{7,6},{8,9},{9,8},{10,11... | collective-permute-start | bytes 393224 | tf_op jit(solution)/shard_map/ppermute | solution.py:485

commit v21 on v20

--- a/solution.py
+++ b/solution.py
@@ -400,18 +400,19 @@
             second[h * half : (h + 1) * half, cols] = total[half:]
 
 
-def outer_sum_kernel(own, a0, a1, far_ref, near_ref):
-    expert, outer, inner, dp = seat()
-    half = far_ref.shape[0]
+def outer_sum_kernel(own, a0, a1, far_a, far_b, near_ref):
+    expert, outer, inner, dp = seat()
+    half, side = far_a.shape
     total = jnp.where((inner & 1) == 0, own[...].astype(F32), a0[...].astype(F32)) + a1[...].astype(F32)
-    far_ref[...] = total[:half].astype(BF16)
+    far_a[...] = total[:half, :side].astype(BF16)
+    far_b[...] = total[:half, side:].astype(BF16)
     near_ref[...] = total[half:]
 
 
-def gather_kernel(near, far, b0, b1, keep_ref, send_ref):
+def gather_kernel(near, far_a, far_b, b0, b1, keep_ref, send_ref):
     small = near.shape[0] // 2
     for i, total in enumerate(
-        (near[...] + far[...].astype(F32), b0[...].astype(F32) + b1[...].astype(F32))
+        (near[...] + jnp.concatenate([far_a[...], far_b[...]], axis=1).astype(F32), b0[...].astype(F32) + b1[...].astype(F32))
     ):
         rows = slice(i * small, (i + 1) * small)
         keep_ref[rows, :] = total[:small]
@@ -639,17 +640,17 @@
     own, second = call(
         messages_kernel, "messages", 4, (message, message), keep_far, keep_near, *swap_cores(send)
     )
-    half_message = shape_of(2 * rows_here, half_width)
-    mine_far, mine_near = call(
+    half_message = shape_of(2 * rows_here, half_width // 2)
+    *mine_far, mine_near = call(
         outer_sum_kernel,
         "outer_sum",
         4,
-        (half_message, shape_of(2 * rows_here, half_width, dtype=F32)),
+        (half_message, half_message, shape_of(2 * rows_here, half_width, dtype=F32)),
         own,
         send_outer(own, 0, False),
         send_outer(second, 1, False),
     )
-    mine_far = swap_inner(mine_far, 2)
+    mine_far = [swap_inner(half, 2) for half in mine_far]
 
     keep_far, send = down(down_far_kernel, far_other, 2)
     far = swap_inner(fold(keep_far, swap_cores(send)), 2)
@@ -664,7 +665,7 @@
         4,
         (shape_of(2 * rows_here, half_width, dtype=F32), sums),
         mine_near,
-        mine_far,
+        *mine_far,
         *others,
     )
     out = shape_of(rows_here, model_width)

time: 113 us -> 113 us (level)
    ppermute x4, waiting for transfers between devices: 5.85 us -> 1.98 us  [send_outer(): return lax.ppermute(x, ('dp', 'expert'), pairs)]
    ppermute x20 -> x21, waiting for transfers between devices: 14.6 us -> 17.9 us  [swap_inner(): return lax.ppermute(x, 'expert', [(i, i ^ j) for i in range(expert_count)])]
    ppermute x20 -> x21, starting transfers between devices: 17.9 us -> 18.5 us  [swap_inner(): return lax.ppermute(x, 'expert', [(i, i ^ j) for i in range(expert_count)])]
  transfers between devices with their start and end apart: 39 -> 40, of which waited for: 23 -> 24; matrix products, arithmetic and copies ran while one was open for 1% -> 1% of each run, Pallas kernels for 11% -> 11%
where the time goes in v21:
time: 113 us
  waiting for transfers between devices  48.8 us (43%)
  starting transfers between devices  43.3 us (38%)
  Pallas kernels  13.8 us (12%)
  local copies, waits for them, and re-layouts  4.59 us (4%)
  between operations  1.54 us (1%)
    ppermute x21, starting transfers between devices, swap_inner(): return lax.ppermute(x, 'expert', [(i, i ^ j) for i in range(expert_count)])  18.5 us
    ppermute x21, waiting for transfers between devices, swap_inner(): return lax.ppermute(x, 'expert', [(i, i ^ j) for i in range(expert_count)])  17.9 us
    pallas_call x17, Pallas kernels, call(): pl.pallas_call(kernel, out_shape=outs, in_specs=[first] + [vmem] * (len(a...  13.4 us
    ppermute x5, waiting for transfers between devices, swap_outer(): lax.ppermute(x, 'expert', [(i, i ^ 4 * s) for i in range(expert_count)])  12.1 us
    ppermute x7, starting transfers between devices, swap_dp(): return lax.ppermute(x, 'dp', [(0, 1), (1, 0)])  9.85 us
    ppermute x7, waiting for transfers between devices, swap_dp(): return lax.ppermute(x, 'dp', [(0, 1), (1, 0)])  9.22 us
    ppermute x3, waiting for transfers between devices, shift_outer(): lax.ppermute(x, 'expert', [(i, (i + 4 * s) % expert_count) for i in range...  7.64 us
    ppermute x5, starting transfers between devices, swap_outer(): lax.ppermute(x, 'expert', [(i, i ^ 4 * s) for i in range(expert_count)])  6.59 us
  transfers between devices with their start and end apart: 40, of which 24 were waited for; matrix products, arithmetic and copies ran while one was open for 1% of the time, Pallas kernels for 11%

profile of v21, /device:TPU:0, one launch (start us, length us, event | category | flops | bytes accessed | tf_op | source)
XLA Modules:
  0.0 112.7 jit_solution(3152242592308481993)
XLA Ops:
  0.6 1.9 %copy-done = bf16[1,1024,1536]{2,1,0:T(8,128)(2,1)S(1)} copy-done((bf16[1,1024,1536]{2,1,0:T(8,128)(2,1)S(1)}, bf16[1,1024,1536]{2,1,0:T(8,128)(2,1)}, u32[]{:S(2)}) %copy-start) | copy-done | bytes 3145752
  2.7 3.0 %collective-permute-start.8 = (bf16[1024,768]{1,0:T(8,128)(2,1)S(1)}, bf16[1024,768]{1,0:T(8,128)(2,1)S(1)}, u32[]{:S(2)}, u32[]{:S(2)}) collective-permute-start(bf16[1024,768]{1,0:T(8,128)(2,1)S(1)} %weight_piece.3), channel_id=1, source_target_pairs={{0,16},{16,0},{1,17},{17,1},{2,18},{18,2},{3,19},{19,3},{4,20},{20... | collective-permute-start | bytes 4718600 | tf_op jit(solution)/shard_map/ppermute | solution.py:469
  5.7 1.5 %collective-permute-start.5 = (bf16[2048,128]{1,0:T(8,128)(2,1)}, bf16[2048,128]{1,0:T(8,128)(2,1)}, u32[]{:S(2)}, u32[]{:S(2)}) collective-permute-start(bf16[2048,128]{1,0:T(8,128)(2,1)} %w0.1), channel_id=1, source_target_pairs={{0,2},{1,3},{2,0},{3,1},{4,6},{5,7},{6,4},{7,5},{8,10},{9,11},{10,... | collective-permute-start | bytes 1572872 | tf_op jit(solution)/shard_map/ppermute | solution.py:486
  7.2 0.6 cut_resid.1
  7.9 2.6 %collective-permute-start.2 = (bf16[64,512]{1,0:T(8,128)(2,1)}, bf16[64,512]{1,0:T(8,128)(2,1)S(1)}, u32[]{:S(2)}, u32[]{:S(2)}) collective-permute-start(bf16[64,512]{1,0:T(8,128)(2,1)} %get-tuple-element.49), channel_id=1, source_target_pairs={{0,8},{1,9},{2,10},{3,11},{4,12},{5,13},{6,14},{7,15},{8,0},{9,1},... | collective-permute-start | bytes 196616 | tf_op jit(solution)/shard_map/ppermute | solution.py:489
  10.5 0.3 collective-permute-start.1
  10.8 1.6 %collective-permute-start = (bf16[64,2048]{1,0:T(8,128)(2,1)S(1)}, bf16[64,2048]{1,0:T(8,128)(2,1)}, u32[]{:S(2)}, u32[]{:S(2)}) collective-permute-start(bf16[64,2048]{1,0:T(8,128)(2,1)S(1)} %bitcast.17), channel_id=1, source_target_pairs={{0,4},{1,5},{2,6},{3,7},{4,0},{5,1},{6,2},{7,3},{8,12},{9,13},{10,... | collective-permute-start | bytes 786440 | tf_op jit(solution)/shard_map/ppermute | solution.py:489
  12.6 1.0 copy-done.8
  13.6 0.8 copy-done.10
  15.2 0.8 copy.13
  15.9 0.4 share.1
  16.4 3.0 %collective-permute-done.5.w2 = bf16[2048,128]{1,0:T(8,128)(2,1)} collective-permute-done((bf16[2048,128]{1,0:T(8,128)(2,1)}, bf16[2048,128]{1,0:T(8,128)(2,1)}, u32[]{:S(2)}, u32[]{:S(2)}) %collective-permute-start.5) | collective-permute-done | bytes 524320 | tf_op jit(solution)/shard_map/ppermute | solution.py:486
  19.5 0.5 collective-permute-start.6
  20.0 5.4 %collective-permute-done.1.a2 = bf16[64,2048]{1,0:T(8,128)(2,1)} collective-permute-done((bf16[64,2048]{1,0:T(8,128)(2,1)S(1)}, bf16[64,2048]{1,0:T(8,128)(2,1)}, u32[]{:S(2)}, u32[]{:S(2)}) %collective-permute-start.1) | collective-permute-done | bytes 262176 | tf_op jit(solution)/shard_map/ppermute | solution.py:489
  25.6 0.8 pad_maximum_fusion
  26.4 1.9 %collective-permute-start.4 = (bf16[64,512]{1,0:T(8,128)(2,1)S(1)}, bf16[64,512]{1,0:T(8,128)(2,1)S(1)}, u32[]{:S(2)}, u32[]{:S(2)}) collective-permute-start(bf16[64,512]{1,0:T(8,128)(2,1)S(1)} %pad_maximum_fusion), channel_id=1, source_target_pairs={{0,4},{1,5},{2,6},{3,7},{4,0},{5,1},{6,2},{7,3},{8,12},{9,13},{10,... | collective-permute-start | bytes 196616 | tf_op jit(solution)/shard_map/ppermute | solution.py:489
  28.2 6.7 %collective-permute-done.4.r13 = bf16[64,512]{1,0:T(8,128)(2,1)S(1)} collective-permute-done((bf16[64,512]{1,0:T(8,128)(2,1)S(1)}, bf16[64,512]{1,0:T(8,128)(2,1)S(1)}, u32[]{:S(2)}, u32[]{:S(2)}) %collective-permute-start.4) | collective-permute-done | bytes 65568 | tf_op jit(solution)/shard_map/ppermute | solution.py:489
  34.9 2.8 %projection.1 = (bf16[128,512]{1,0:T(8,128)(2,1)S(1)}, bf16[128,512]{1,0:T(8,128)(2,1)S(1)}) custom-call(bf16[64,2048]{1,0:T(8,128)(2,1)S(1)} %bitcast.18, bf16[64,2048]{1,0:T(8,128)(2,1)} %collective-permute-done.a1, bf16[64,2048]{1,0:T(8,128)(2,1)} %collective-permute-done.1.a2, bf16[64,2048]{1,0:T(8,128)(2,1)S(1)} %collective-permute-done.3.a3, ...), custom_call_target="tpu_custom_call" | custom-call | flops 1 | bytes 1 | tf_op jit(solution)/shard_map/projection/pallas_call | solution.py:457
  37.8 0.6 collective-permute-start.9
  38.3 1.5 %collective-permute-start.19 = (bf16[640,768]{1,0:T(8,128)(2,1)S(1)}, bf16[640,768]{1,0:T(8,128)(2,1)S(1)}, u32[]{:S(2)}, u32[]{:S(2)}) collective-permute-start(bf16[640,768]{1,0:T(8,128)(2,1)S(1)} %copy-done.9), channel_id=1, source_target_pairs={{0,16},{16,0},{1,17},{17,1},{2,18},{18,2},{3,19},{19,3},{4,20},{20... | collective-permute-start | bytes 2949128 | tf_op jit(solution)/shard_map/ppermute | solution.py:469
  39.9 1.1 collective-permute-done.8.early
  41.0 3.3 %collective-permute-done.9.arrived = bf16[128,512]{1,0:T(8,128)(2,1)S(1)} collective-permute-done((bf16[128,512]{1,0:T(8,128)(2,1)S(1)}, bf16[128,512]{1,0:T(8,128)(2,1)S(1)}, u32[]{:S(2)}, u32[]{:S(2)}) %collective-permute-start.9) | collective-permute-done | bytes 131104 | tf_op jit(solution)/shard_map/ppermute | solution.py:469
  44.3 3.5 %collective-permute-start.12 = (bf16[144,512]{1,0:T(8,128)(2,1)S(1)}, bf16[144,512]{1,0:T(8,128)(2,1)S(1)}, u32[]{:S(2)}, u32[]{:S(2)}) collective-permute-start(bf16[144,512]{1,0:T(8,128)(2,1)S(1)} %stream.1.b0), channel_id=1, source_target_pairs={{0,12},{1,13},{2,14},{3,15},{4,0},{5,1},{6,2},{7,3},{8,4},{9,5},{1... | collective-permute-start | bytes 442376 | tf_op jit(solution)/shard_map/ppermute | solution.py:472
  47.8 0.8 collective-permute-start.10
  48.7 1.9 %collective-permute-start.13 = (bf16[144,512]{1,0:T(8,128)(2,1)S(1)}, bf16[144,512]{1,0:T(8,128)(2,1)S(1)}, u32[]{:S(2)}, u32[]{:S(2)}) collective-permute-start(bf16[144,512]{1,0:T(8,128)(2,1)S(1)} %stream.1.b0), channel_id=1, source_target_pairs={{0,2},{1,3},{2,0},{3,1},{4,6},{5,7},{6,4},{7,5},{8,10},{9,11},{10,... | collective-permute-start | bytes 442376 | tf_op jit(solution)/shard_map/ppermute | solution.py:486
  50.5 1.6 %collective-permute-done.12.b3 = bf16[144,512]{1,0:T(8,128)(2,1)S(1)} collective-permute-done((bf16[144,512]{1,0:T(8,128)(2,1)S(1)}, bf16[144,512]{1,0:T(8,128)(2,1)S(1)}, u32[]{:S(2)}, u32[]{:S(2)}) %collective-permute-start.12) | collective-permute-done | bytes 147488 | tf_op jit(solution)/shard_map/ppermute | solution.py:472
  52.1 1.7 %collective-permute-start.16 = (bf16[144,512]{1,0:T(8,128)(2,1)S(1)}, bf16[144,512]{1,0:T(8,128)(2,1)S(1)}, u32[]{:S(2)}, u32[]{:S(2)}) collective-permute-start(bf16[144,512]{1,0:T(8,128)(2,1)S(1)} %collective-permute-done.12.b3), channel_id=1, source_target_pairs={{0,2},{1,3},{2,0},{3,1},{4,6},{5,7},{6,4},{7,5},{8,10},{9,11},{10,... | collective-permute-start | bytes 442376 | tf_op jit(solution)/shard_map/ppermute | solution.py:486
  53.8 6.0 %collective-permute-done.11.b2 = bf16[144,512]{1,0:T(8,128)(2,1)S(1)} collective-permute-done((bf16[144,512]{1,0:T(8,128)(2,1)S(1)}, bf16[144,512]{1,0:T(8,128)(2,1)S(1)}, u32[]{:S(2)}, u32[]{:S(2)}) %collective-permute-start.11) | collective-permute-done | bytes 147488 | tf_op jit(solution)/shard_map/ppermute | solution.py:472
  59.9 1.1 collective-permute-start.15
  61.0 0.9 collective-permute-start.14
  61.9 1.2 %collective-permute-start.20 = (bf16[384,768]{1,0:T(8,128)(2,1)S(1)}, bf16[384,768]{1,0:T(8,128)(2,1)S(1)}, u32[]{:S(2)}, u32[]{:S(2)}) collective-permute-start(bf16[384,768]{1,0:T(8,128)(2,1)S(1)} %copy-done.11), channel_id=1, source_target_pairs={{0,16},{16,0},{1,17},{17,1},{2,18},{18,2},{3,19},{19,3},{4,20},{20... | collective-permute-start | bytes 1769480 | tf_op jit(solution)/shard_map/ppermute | solution.py:469
  63.5 2.3 %collective-permute-done.15.b2 = bf16[144,512]{1,0:T(8,128)(2,1)S(1)} collective-permute-done((bf16[144,512]{1,0:T(8,128)(2,1)S(1)}, bf16[144,512]{1,0:T(8,128)(2,1)S(1)}, u32[]{:S(2)}, u32[]{:S(2)}) %collective-permute-start.15) | collective-permute-done | bytes 147488 | tf_op jit(solution)/shard_map/ppermute | solution.py:486
  65.8 1.6 %collective-permute-done.14.b1 = bf16[144,512]{1,0:T(8,128)(2,1)S(1)} collective-permute-done((bf16[144,512]{1,0:T(8,128)(2,1)S(1)}, bf16[144,512]{1,0:T(8,128)(2,1)S(1)}, u32[]{:S(2)}, u32[]{:S(2)}) %collective-permute-start.14) | collective-permute-done | bytes 147488 | tf_op jit(solution)/shard_map/ppermute | solution.py:486
  67.3 0.8 norm.3
  68.1 2.0 %collective-permute-done.17.group_cx = bf16[128,2176]{1,0:T(8,128)(2,1)S(1)} collective-permute-done((bf16[128,2176]{1,0:T(8,128)(2,1)S(1)}, bf16[128,2176]{1,0:T(8,128)(2,1)S(1)}, u32[]{:S(2)}, u32[]{:S(2)}) %collective-permute-start.17) | collective-permute-done | bytes 557088 | tf_op jit(solution)/shard_map/ppermute | solution.py:486
  70.1 3.4 %first_gate_up.1 = (bf16[384,384]{1,0:T(8,128)(2,1)S(1)}, bf16[128,384]{1,0:T(8,128)(2,1)S(1)}, f32[512,768]{1,0:T(8,128)S(1)}, bf16[512,1024]{1,0:T(8,128)(2,1)S(1)}, f32[512,128]{1,0:T(8,128)S(1)}) custom-call(bf16[128,2176]{1,0:T(8,128)(2,1)S(1)} %get-tuple-element.61.group_x, bf16[128,2176]{1,0:T(8,128)(2,1)S(1)} %collective-permute-done.17.group_cx, ...), custom_call_target="tpu_custom_call" | custom-call | flops 1 | bytes 1 | tf_op jit(solution)/shard_map/first_gate_up/pallas_call | solution.py:457
  73.5 0.9 collective-permute-start.29
  74.4 2.6 %collective-permute-done.20.refs_1_ = bf16[384,768]{1,0:T(8,128)(2,1)S(1)} collective-permute-done((bf16[384,768]{1,0:T(8,128)(2,1)S(1)}, bf16[384,768]{1,0:T(8,128)(2,1)S(1)}, u32[]{:S(2)}, u32[]{:S(2)}) %collective-permute-start.20) | collective-permute-done | bytes 589856 | tf_op jit(solution)/shard_map/ppermute | solution.py:469
  77.1 1.5 %last_gate_up.1 = (bf16[256,384]{1,0:T(8,128)(2,1)S(1)}, bf16[384,384]{1,0:T(8,128)(2,1)S(1)}) custom-call(bf16[128,384]{1,0:T(8,128)(2,1)S(1)} %get-tuple-element.64.second, f32[512,768]{1,0:T(8,128)S(1)} %get-tuple-element.65.part, bf16[512,1024]{1,0:T(8,128)(2,1)S(1)} %get-tuple-element.66.other, f32[512,128]{1,0:T(8,128)S(1)} %get-tuple-element.67.share, ...), custom_call_target="tpu_custom_call" | custom-call | flops 1 | bytes 1 | tf_op jit(solution)/shard_map/last_gate_up/pallas_call | solution.py:457
  78.5 1.0 down_both.1
  79.6 2.6 %collective-permute-start.30 = (bf16[256,384]{1,0:T(8,128)(2,1)S(1)}, bf16[256,384]{1,0:T(8,128)(2,1)S(1)}, u32[]{:S(2)}, u32[]{:S(2)}) collective-permute-start(bf16[256,384]{1,0:T(8,128)(2,1)S(1)} %get-tuple-element.70.far), channel_id=1, source_target_pairs={{0,16},{16,0},{1,17},{17,1},{2,18},{18,2},{3,19},{19,3},{4,20},{20... | collective-permute-start | bytes 589832 | tf_op jit(solution)/shard_map/ppermute | solution.py:469
  82.3 0.3 collective-permute-start.23
  82.9 0.7 collective-permute-done.22.refs_1_
  84.2 1.6 %collective-permute-start.26 = (bf16[128,1024]{1,0:T(8,128)(2,1)S(1)}, bf16[128,1024]{1,0:T(8,128)(2,1)S(1)}, u32[]{:S(2)}, u32[]{:S(2)}) collective-permute-start(bf16[128,1024]{1,0:T(8,128)(2,1)S(1)} %get-tuple-element.79), channel_id=1, source_target_pairs={{0,4},{1,13},{2,6},{3,15},{4,8},{5,1},{6,10},{7,3},{8,12},{9,5},{1... | collective-permute-start | bytes 786440 | tf_op jit(solution)/shard_map/ppermute | solution.py:483
  85.8 0.7 collective-permute-start.25
  86.5 1.5 %collective-permute-done.30.far = bf16[256,384]{1,0:T(8,128)(2,1)S(1)} collective-permute-done((bf16[256,384]{1,0:T(8,128)(2,1)S(1)}, bf16[256,384]{1,0:T(8,128)(2,1)S(1)}, u32[]{:S(2)}, u32[]{:S(2)}) %collective-permute-start.30) | collective-permute-done | bytes 196640 | tf_op jit(solution)/shard_map/ppermute | solution.py:469
  87.9 0.6 down.2
  88.5 1.8 %collective-permute-start.31 = (bf16[128,512]{1,0:T(8,128)(2,1)S(1)}, bf16[128,512]{1,0:T(8,128)(2,1)S(1)}, u32[]{:S(2)}, u32[]{:S(2)}) collective-permute-start(bf16[128,512]{1,0:T(8,128)(2,1)S(1)} %get-tuple-element.84), channel_id=1, source_target_pairs={{0,1},{1,0},{2,3},{3,2},{4,5},{5,4},{6,7},{7,6},{8,9},{9,8},{10,11... | collective-permute-start | bytes 393224 | tf_op jit(solution)/shard_map/ppermute | solution.py:486
  90.4 0.9 collective-permute-done.31.refs_0_
  91.3 0.4 collective-permute-done.32.refs_1_
  91.7 1.6 %collective-permute-start.33 = (bf16[128,1024]{1,0:T(8,128)(2,1)S(1)}, bf16[128,1024]{1,0:T(8,128)(2,1)S(1)}, u32[]{:S(2)}, u32[]{:S(2)}) collective-permute-start(bf16[128,1024]{1,0:T(8,128)(2,1)S(1)} %fold.1), channel_id=1, source_target_pairs={{0,2},{1,3},{2,0},{3,1},{4,6},{5,7},{6,4},{7,5},{8,10},{9,11},{10,... | collective-permute-start | bytes 786440 | tf_op jit(solution)/shard_map/ppermute | solution.py:486
  93.3 0.7 collective-permute-done.34.rest
  94.0 0.6 down.3
  94.7 0.5 collective-permute-done.26.a1
  95.2 4.5 %collective-permute-start.36 = (bf16[128,512]{1,0:T(8,128)(2,1)S(1)}, bf16[128,512]{1,0:T(8,128)(2,1)S(1)}, u32[]{:S(2)}, u32[]{:S(2)}) collective-permute-start(bf16[128,512]{1,0:T(8,128)(2,1)S(1)} %get-tuple-element.89), channel_id=1, source_target_pairs={{0,1},{1,0},{2,3},{3,2},{4,5},{5,4},{6,7},{7,6},{8,9},{9,8},{10,11... | collective-permute-start | bytes 393224 | tf_op jit(solution)/shard_map/ppermute | solution.py:486
  99.7 1.0 collective-permute-done.36.refs_1_
  100.8 1.5 %collective-permute-start.37 = (bf16[64,1024]{1,0:T(8,128)(2,1)S(1)}, bf16[64,1024]{1,0:T(8,128)(2,1)S(1)}, u32[]{:S(2)}, u32[]{:S(2)}) collective-permute-start(bf16[64,1024]{1,0:T(8,128)(2,1)S(1)} %get-tuple-element.90), channel_id=1, source_target_pairs={{0,16},{1,25},{2,18},{3,27},{4,20},{5,29},{6,22},{7,31},{8,24},{9,... | collective-permute-start | bytes 393224 | tf_op jit(solution)/shard_map/ppermute | solution.py:483
  102.6 1.5 %collective-permute-start.27 = (bf16[64,512]{1,0:T(8,128)(2,1)S(1)}, bf16[64,512]{1,0:T(8,128)(2,1)S(1)}, u32[]{:S(2)}, u32[]{:S(2)}) collective-permute-start(bf16[64,512]{1,0:T(8,128)(2,1)S(1)} %get-tuple-element.81), channel_id=1, source_target_pairs={{0,2},{1,3},{2,0},{3,1},{4,6},{5,7},{6,4},{7,5},{8,10},{9,11},{10,... | collective-permute-start | bytes 196616 | tf_op jit(solution)/shard_map/ppermute | solution.py:486
  104.1 0.5 collective-permute-start.28
  104.6 2.2 %collective-permute-done.27.far_a = bf16[64,512]{1,0:T(8,128)(2,1)S(1)} collective-permute-done((bf16[64,512]{1,0:T(8,128)(2,1)S(1)}, bf16[64,512]{1,0:T(8,128)(2,1)S(1)}, u32[]{:S(2)}, u32[]{:S(2)}) %collective-permute-start.27) | collective-permute-done | bytes 65568 | tf_op jit(solution)/shard_map/ppermute | solution.py:486
  106.8 2.1 %collective-permute-done.28.far_b = bf16[64,512]{1,0:T(8,128)(2,1)S(1)} collective-permute-done((bf16[64,512]{1,0:T(8,128)(2,1)S(1)}, bf16[64,512]{1,0:T(8,128)(2,1)S(1)}, u32[]{:S(2)}, u32[]{:S(2)}) %collective-permute-start.28) | collective-permute-done | bytes 65568 | tf_op jit(solution)/shard_map/ppermute | solution.py:486
  108.9 1.5 %collective-permute-done.38.b1 = bf16[64,1024]{1,0:T(8,128)(2,1)S(1)} collective-permute-done((bf16[64,1024]{1,0:T(8,128)(2,1)S(1)}, bf16[64,1024]{1,0:T(8,128)(2,1)S(1)}, u32[]{:S(2)}, u32[]{:S(2)}) %collective-permute-start.38) | collective-permute-done | bytes 131104 | tf_op jit(solution)/shard_map/ppermute | solution.py:483
  110.6 1.3 %collective-permute-done.39.core = bf16[64,1024]{1,0:T(8,128)(2,1)S(1)} collective-permute-done((bf16[64,1024]{1,0:T(8,128)(2,1)S(1)}, bf16[64,1024]{1,0:T(8,128)(2,1)S(1)}, u32[]{:S(2)}, u32[]{:S(2)}) %collective-permute-start.39) | collective-permute-done | bytes 131104 | tf_op jit(solution)/shard_map/ppermute | solution.py:486
  111.9 0.8 closing.1
  (65 shorter events, 3.1 us)
Async XLA Ops:
  0.6 1.9 %copy-start = (bf16[1,1024,1536]{2,1,0:T(8,128)(2,1)S(1)}, bf16[1,1024,1536]{2,1,0:T(8,128)(2,1)}, u32[]{:S(2)}) copy-start(bf16[1,1024,1536]{2,1,0:T(8,128)(2,1)} %param.17) | copy-start | bytes 9437188
  2.5 4.7 %copy-start.4 = (bf16[1,32,2048]{2,1,0:T(8,128)(2,1)S(1)}, bf16[1,32,2048]{2,1,0:T(8,128)(2,1)}, u32[]{:S(2)}) copy-start(bf16[1,32,2048]{2,1,0:T(8,128)(2,1)} %param.11) | copy-start | bytes 393220
  2.5 7.9 %copy-start.3 = (bf16[1,64,2048]{2,1,0:T(8,128)(2,1)S(1)}, bf16[1,64,2048]{2,1,0:T(8,128)(2,1)}, u32[]{:S(2)}) copy-start(bf16[1,64,2048]{2,1,0:T(8,128)(2,1)} %param.10) | copy-start | bytes 786436
  2.7 38.3 %collective-permute-start.8 = (bf16[1024,768]{1,0:T(8,128)(2,1)S(1)}, bf16[1024,768]{1,0:T(8,128)(2,1)S(1)}, u32[]{:S(2)}, u32[]{:S(2)}) collective-permute-start(bf16[1024,768]{1,0:T(8,128)(2,1)S(1)} %weight_piece.3), channel_id=1, source_target_pairs={{0,16},{16,0},{1,17},{17,1},{2,18},{18,2},{3,19},{19,3},{4,20},{20... | collective-permute-start | bytes 4718600 | tf_op jit(solution)/shard_map/ppermute | solution.py:469
  5.7 13.7 %collective-permute-start.5 = (bf16[2048,128]{1,0:T(8,128)(2,1)}, bf16[2048,128]{1,0:T(8,128)(2,1)}, u32[]{:S(2)}, u32[]{:S(2)}) collective-permute-start(bf16[2048,128]{1,0:T(8,128)(2,1)} %w0.1), channel_id=1, source_target_pairs={{0,2},{1,3},{2,0},{3,1},{4,6},{5,7},{6,4},{7,5},{8,10},{9,11},{10,... | collective-permute-start | bytes 1572872 | tf_op jit(solution)/shard_map/ppermute | solution.py:486
  7.9 4.7 %copy-start.6 = (bf16[32,512]{1,0:T(8,128)(2,1)}, bf16[32,512]{1,0:T(8,128)(2,1)S(1)}, u32[]{:S(2)}) copy-start(bf16[32,512]{1,0:T(8,128)(2,1)S(1)} %get-tuple-element.51) | copy-start | bytes 98308
  7.9 11.6 %collective-permute-start.2 = (bf16[64,512]{1,0:T(8,128)(2,1)}, bf16[64,512]{1,0:T(8,128)(2,1)S(1)}, u32[]{:S(2)}, u32[]{:S(2)}) collective-permute-start(bf16[64,512]{1,0:T(8,128)(2,1)} %get-tuple-element.49), channel_id=1, source_target_pairs={{0,8},{1,9},{2,10},{3,11},{4,12},{5,13},{6,14},{7,15},{8,0},{9,1},... | collective-permute-start | bytes 196616 | tf_op jit(solution)/shard_map/ppermute | solution.py:489
  10.5 4.6 %copy-start.12 = (s32[1,32,8]{1,2,0:T(8,128)S(1)}, s32[1,32,8]{1,2,0:T(8,128)}, u32[]{:S(2)}) copy-start(s32[1,32,8]{1,2,0:T(8,128)} %param.14) | copy-start | bytes 3076
  10.5 14.9 %collective-permute-start.1 = (bf16[64,2048]{1,0:T(8,128)(2,1)S(1)}, bf16[64,2048]{1,0:T(8,128)(2,1)}, u32[]{:S(2)}, u32[]{:S(2)}) collective-permute-start(bf16[64,2048]{1,0:T(8,128)(2,1)S(1)} %bitcast.16), channel_id=1, source_target_pairs={{0,8},{1,9},{2,10},{3,11},{4,12},{5,13},{6,14},{7,15},{8,0},{9,1},... | collective-permute-start | bytes 786440 | tf_op jit(solution)/shard_map/ppermute | solution.py:489
  10.8 14.5 %collective-permute-start = (bf16[64,2048]{1,0:T(8,128)(2,1)S(1)}, bf16[64,2048]{1,0:T(8,128)(2,1)}, u32[]{:S(2)}, u32[]{:S(2)}) collective-permute-start(bf16[64,2048]{1,0:T(8,128)(2,1)S(1)} %bitcast.17), channel_id=1, source_target_pairs={{0,4},{1,5},{2,6},{3,7},{4,0},{5,1},{6,2},{7,3},{8,12},{9,13},{10,... | collective-permute-start | bytes 786440 | tf_op jit(solution)/shard_map/ppermute | solution.py:489
  12.6 1.0 copy-start.8
  13.6 0.8 copy-start.10
  19.4 15.4 %collective-permute-start.7 = (bf16[2048,128]{1,0:T(8,128)(2,1)}, bf16[2048,128]{1,0:T(8,128)(2,1)S(1)}, u32[]{:S(2)}, u32[]{:S(2)}) collective-permute-start(bf16[2048,128]{1,0:T(8,128)(2,1)} %collective-permute-done.5.w2), channel_id=1, source_target_pairs={{0,1},{1,0},{2,3},{3,2},{4,5},{5,4},{6,7},{7,6},{8,9},{9,8},{10,11... | collective-permute-start | bytes 1572872 | tf_op jit(solution)/shard_map/ppermute | solution.py:486
  19.5 15.4 %collective-permute-start.6 = (bf16[2048,128]{1,0:T(8,128)(2,1)}, bf16[2048,128]{1,0:T(8,128)(2,1)S(1)}, u32[]{:S(2)}, u32[]{:S(2)}) collective-permute-start(bf16[2048,128]{1,0:T(8,128)(2,1)} %w0.1), channel_id=1, source_target_pairs={{0,1},{1,0},{2,3},{3,2},{4,5},{5,4},{6,7},{7,6},{8,9},{9,8},{10,11... | collective-permute-start | bytes 1572872 | tf_op jit(solution)/shard_map/ppermute | solution.py:486
  25.4 9.5 %collective-permute-start.3 = (bf16[64,2048]{1,0:T(8,128)(2,1)}, bf16[64,2048]{1,0:T(8,128)(2,1)S(1)}, u32[]{:S(2)}, u32[]{:S(2)}) collective-permute-start(bf16[64,2048]{1,0:T(8,128)(2,1)} %collective-permute-done.1.a2), channel_id=1, source_target_pairs={{0,4},{1,5},{2,6},{3,7},{4,0},{5,1},{6,2},{7,3},{8,12},{9,13},{10,... | collective-permute-start | bytes 786440 | tf_op jit(solution)/shard_map/ppermute | solution.py:489
  26.3 12.0 %copy-start.9 = (bf16[640,768]{1,0:T(8,128)(2,1)S(1)}, bf16[640,768]{1,0:T(8,128)(2,1)}, u32[]{:S(2)}) copy-start(bf16[640,768]{1,0:T(8,128)(2,1)} %copy-done.8) | copy-start | bytes 2949124
  26.3 35.6 %copy-start.11 = (bf16[384,768]{1,0:T(8,128)(2,1)S(1)}, bf16[384,768]{1,0:T(8,128)(2,1)}, u32[]{:S(2)}) copy-start(bf16[384,768]{1,0:T(8,128)(2,1)} %copy-done.10) | copy-start | bytes 1769476
  26.4 36.7 %copy-start.5 = (f32[2048]{0:T(1024)S(1)}, f32[2048]{0:T(1024)}, u32[]{:S(2)}) copy-start(f32[2048]{0:T(1024)} %param.13) | copy-start | bytes 24580
  26.4 8.5 %collective-permute-start.4 = (bf16[64,512]{1,0:T(8,128)(2,1)S(1)}, bf16[64,512]{1,0:T(8,128)(2,1)S(1)}, u32[]{:S(2)}, u32[]{:S(2)}) collective-permute-start(bf16[64,512]{1,0:T(8,128)(2,1)S(1)} %pad_maximum_fusion), channel_id=1, source_target_pairs={{0,4},{1,5},{2,6},{3,7},{4,0},{5,1},{6,2},{7,3},{8,12},{9,13},{10,... | collective-permute-start | bytes 196616 | tf_op jit(solution)/shard_map/ppermute | solution.py:489
  34.9 35.2 %copy-start.1 = (bf16[1,1024,1536]{2,1,0:T(8,128)(2,1)S(1)}, bf16[1,1024,1536]{2,1,0:T(8,128)(2,1)}, u32[]{:S(2)}) copy-start(bf16[1,1024,1536]{2,1,0:T(8,128)(2,1)} %param.17) | copy-start | bytes 9437188
  37.8 6.5 %collective-permute-start.9 = (bf16[128,512]{1,0:T(8,128)(2,1)S(1)}, bf16[128,512]{1,0:T(8,128)(2,1)S(1)}, u32[]{:S(2)}, u32[]{:S(2)}) collective-permute-start(bf16[128,512]{1,0:T(8,128)(2,1)S(1)} %get-tuple-element.58), channel_id=1, source_target_pairs={{0,16},{16,0},{1,17},{17,1},{2,18},{18,2},{3,19},{19,3},{4,20},{20... | collective-permute-start | bytes 393224 | tf_op jit(solution)/shard_map/ppermute | solution.py:469
  38.3 38.7 %collective-permute-start.19 = (bf16[640,768]{1,0:T(8,128)(2,1)S(1)}, bf16[640,768]{1,0:T(8,128)(2,1)S(1)}, u32[]{:S(2)}, u32[]{:S(2)}) collective-permute-start(bf16[640,768]{1,0:T(8,128)(2,1)S(1)} %copy-done.9), channel_id=1, source_target_pairs={{0,16},{16,0},{1,17},{17,1},{2,18},{18,2},{3,19},{19,3},{4,20},{20... | collective-permute-start | bytes 2949128 | tf_op jit(solution)/shard_map/ppermute | solution.py:469
  44.3 7.8 %collective-permute-start.12 = (bf16[144,512]{1,0:T(8,128)(2,1)S(1)}, bf16[144,512]{1,0:T(8,128)(2,1)S(1)}, u32[]{:S(2)}, u32[]{:S(2)}) collective-permute-start(bf16[144,512]{1,0:T(8,128)(2,1)S(1)} %stream.1.b0), channel_id=1, source_target_pairs={{0,12},{1,13},{2,14},{3,15},{4,0},{5,1},{6,2},{7,3},{8,4},{9,5},{1... | collective-permute-start | bytes 442376 | tf_op jit(solution)/shard_map/ppermute | solution.py:472
  47.8 12.0 %collective-permute-start.11 = (bf16[144,512]{1,0:T(8,128)(2,1)S(1)}, bf16[144,512]{1,0:T(8,128)(2,1)S(1)}, u32[]{:S(2)}, u32[]{:S(2)}) collective-permute-start(bf16[144,512]{1,0:T(8,128)(2,1)S(1)} %stream.1.b0), channel_id=1, source_target_pairs={{0,8},{1,9},{2,10},{3,11},{4,12},{5,13},{6,14},{7,15},{8,0},{9,1},... | collective-permute-start | bytes 442376 | tf_op jit(solution)/shard_map/ppermute | solution.py:472
  47.8 13.2 %collective-permute-start.10 = (bf16[144,512]{1,0:T(8,128)(2,1)S(1)}, bf16[144,512]{1,0:T(8,128)(2,1)S(1)}, u32[]{:S(2)}, u32[]{:S(2)}) collective-permute-start(bf16[144,512]{1,0:T(8,128)(2,1)S(1)} %stream.1.b0), channel_id=1, source_target_pairs={{0,4},{1,5},{2,6},{3,7},{4,8},{5,9},{6,10},{7,11},{8,12},{9,13},{1... | collective-permute-start | bytes 442376 | tf_op jit(solution)/shard_map/ppermute | solution.py:472
  48.7 13.2 %collective-permute-start.13 = (bf16[144,512]{1,0:T(8,128)(2,1)S(1)}, bf16[144,512]{1,0:T(8,128)(2,1)S(1)}, u32[]{:S(2)}, u32[]{:S(2)}) collective-permute-start(bf16[144,512]{1,0:T(8,128)(2,1)S(1)} %stream.1.b0), channel_id=1, source_target_pairs={{0,2},{1,3},{2,0},{3,1},{4,6},{5,7},{6,4},{7,5},{8,10},{9,11},{10,... | collective-permute-start | bytes 442376 | tf_op jit(solution)/shard_map/ppermute | solution.py:486
  52.1 11.3 %collective-permute-start.16 = (bf16[144,512]{1,0:T(8,128)(2,1)S(1)}, bf16[144,512]{1,0:T(8,128)(2,1)S(1)}, u32[]{:S(2)}, u32[]{:S(2)}) collective-permute-start(bf16[144,512]{1,0:T(8,128)(2,1)S(1)} %collective-permute-done.12.b3), channel_id=1, source_target_pairs={{0,2},{1,3},{2,0},{3,1},{4,6},{5,7},{6,4},{7,5},{8,10},{9,11},{10,... | collective-permute-start | bytes 442376 | tf_op jit(solution)/shard_map/ppermute | solution.py:486
  59.9 5.9 %collective-permute-start.15 = (bf16[144,512]{1,0:T(8,128)(2,1)S(1)}, bf16[144,512]{1,0:T(8,128)(2,1)S(1)}, u32[]{:S(2)}, u32[]{:S(2)}) collective-permute-start(bf16[144,512]{1,0:T(8,128)(2,1)S(1)} %collective-permute-done.11.b2), channel_id=1, source_target_pairs={{0,2},{1,3},{2,0},{3,1},{4,6},{5,7},{6,4},{7,5},{8,10},{9,11},{10,... | collective-permute-start | bytes 442376 | tf_op jit(solution)/shard_map/ppermute | solution.py:486
  61.0 6.3 %collective-permute-start.14 = (bf16[144,512]{1,0:T(8,128)(2,1)S(1)}, bf16[144,512]{1,0:T(8,128)(2,1)S(1)}, u32[]{:S(2)}, u32[]{:S(2)}) collective-permute-start(bf16[144,512]{1,0:T(8,128)(2,1)S(1)} %collective-permute-done.10.b1), channel_id=1, source_target_pairs={{0,2},{1,3},{2,0},{3,1},{4,6},{5,7},{6,4},{7,5},{8,10},{9,11},{10,... | collective-permute-start | bytes 442376 | tf_op jit(solution)/shard_map/ppermute | solution.py:486
  61.9 15.1 %collective-permute-start.20 = (bf16[384,768]{1,0:T(8,128)(2,1)S(1)}, bf16[384,768]{1,0:T(8,128)(2,1)S(1)}, u32[]{:S(2)}, u32[]{:S(2)}) collective-permute-start(bf16[384,768]{1,0:T(8,128)(2,1)S(1)} %copy-done.11), channel_id=1, source_target_pairs={{0,16},{16,0},{1,17},{17,1},{2,18},{18,2},{3,19},{19,3},{4,20},{20... | collective-permute-start | bytes 1769480 | tf_op jit(solution)/shard_map/ppermute | solution.py:469
  63.4 4.7 %collective-permute-start.18 = (bf16[128,2176]{1,0:T(8,128)(2,1)S(1)}, bf16[128,2176]{1,0:T(8,128)(2,1)S(1)}, u32[]{:S(2)}, u32[]{:S(2)}) collective-permute-start(bf16[128,2176]{1,0:T(8,128)(2,1)S(1)} %get-tuple-element.62.group), channel_id=1, source_target_pairs={{0,1},{1,0},{2,3},{3,2},{4,5},{5,4},{6,7},{7,6},{8,9},{9,8},{10,11... | collective-permute-start | bytes 1671176 | tf_op jit(solution)/shard_map/ppermute | solution.py:486
  68.1 2.0 %collective-permute-start.17 = (bf16[128,2176]{1,0:T(8,128)(2,1)S(1)}, bf16[128,2176]{1,0:T(8,128)(2,1)S(1)}, u32[]{:S(2)}, u32[]{:S(2)}) collective-permute-start(bf16[128,2176]{1,0:T(8,128)(2,1)S(1)} %get-tuple-element.61.group_x), channel_id=1, source_target_pairs={{0,1},{1,0},{2,3},{3,2},{4,5},{5,4},{6,7},{7,6},{8,9},{9,8},{10,11... | collective-permute-start | bytes 1671176 | tf_op jit(solution)/shard_map/ppermute | solution.py:486
  73.5 14.4 %collective-permute-start.29 = (bf16[384,384]{1,0:T(8,128)(2,1)S(1)}, bf16[384,384]{1,0:T(8,128)(2,1)S(1)}, u32[]{:S(2)}, u32[]{:S(2)}) collective-permute-start(bf16[384,384]{1,0:T(8,128)(2,1)S(1)} %get-tuple-element.63.first), channel_id=1, source_target_pairs={{0,16},{16,0},{1,17},{17,1},{2,18},{18,2},{3,19},{19,3},{4,20},{20... | collective-permute-start | bytes 884744 | tf_op jit(solution)/shard_map/ppermute | solution.py:469
  77.1 1.5 %copy-start.2 = (bf16[1,768,1024]{2,1,0:T(8,128)(2,1)S(1)}, bf16[1,768,1024]{2,1,0:T(8,128)(2,1)}, u32[]{:S(2)}) copy-start(bf16[1,768,1024]{2,1,0:T(8,128)(2,1)} %param.18) | copy-start | bytes 4718596
  79.5 3.2 %collective-permute-start.21 = (bf16[128,512]{1,0:T(8,128)(2,1)S(1)}, bf16[128,512]{1,0:T(8,128)(2,1)S(1)}, u32[]{:S(2)}, u32[]{:S(2)}) collective-permute-start(bf16[128,512]{1,0:T(8,128)(2,1)S(1)} %get-tuple-element.74), channel_id=1, source_target_pairs={{0,1},{1,0},{2,3},{3,2},{4,5},{5,4},{6,7},{7,6},{8,9},{9,8},{10,11... | collective-permute-start | bytes 393224 | tf_op jit(solution)/shard_map/ppermute | solution.py:486
  79.6 8.3 %collective-permute-start.30 = (bf16[256,384]{1,0:T(8,128)(2,1)S(1)}, bf16[256,384]{1,0:T(8,128)(2,1)S(1)}, u32[]{:S(2)}, u32[]{:S(2)}) collective-permute-start(bf16[256,384]{1,0:T(8,128)(2,1)S(1)} %get-tuple-element.70.far), channel_id=1, source_target_pairs={{0,16},{16,0},{1,17},{17,1},{2,18},{18,2},{3,19},{19,3},{4,20},{20... | collective-permute-start | bytes 589832 | tf_op jit(solution)/shard_map/ppermute | solution.py:469
  82.2 1.3 %collective-permute-start.22 = (bf16[128,512]{1,0:T(8,128)(2,1)S(1)}, bf16[128,512]{1,0:T(8,128)(2,1)S(1)}, u32[]{:S(2)}, u32[]{:S(2)}) collective-permute-start(bf16[128,512]{1,0:T(8,128)(2,1)S(1)} %get-tuple-element.75), channel_id=1, source_target_pairs={{0,1},{1,0},{2,3},{3,2},{4,5},{5,4},{6,7},{7,6},{8,9},{9,8},{10,11... | collective-permute-start | bytes 393224 | tf_op jit(solution)/shard_map/ppermute | solution.py:486
  82.3 1.4 %collective-permute-start.23 = (bf16[128,512]{1,0:T(8,128)(2,1)S(1)}, bf16[128,512]{1,0:T(8,128)(2,1)S(1)}, u32[]{:S(2)}, u32[]{:S(2)}) collective-permute-start(bf16[128,512]{1,0:T(8,128)(2,1)S(1)} %get-tuple-element.76), channel_id=1, source_target_pairs={{0,1},{1,0},{2,3},{3,2},{4,5},{5,4},{6,7},{7,6},{8,9},{9,8},{10,11... | collective-permute-start | bytes 393224 | tf_op jit(solution)/shard_map/ppermute | solution.py:486
  82.7 1.3 %collective-permute-start.24 = (bf16[128,512]{1,0:T(8,128)(2,1)S(1)}, bf16[128,512]{1,0:T(8,128)(2,1)S(1)}, u32[]{:S(2)}, u32[]{:S(2)}) collective-permute-start(bf16[128,512]{1,0:T(8,128)(2,1)S(1)} %get-tuple-element.77), channel_id=1, source_target_pairs={{0,1},{1,0},{2,3},{3,2},{4,5},{5,4},{6,7},{7,6},{8,9},{9,8},{10,11... | collective-permute-start | bytes 393224 | tf_op jit(solution)/shard_map/ppermute | solution.py:486
  83.5 10.5 %collective-permute-start.34 = (bf16[384,384]{1,0:T(8,128)(2,1)S(1)}, bf16[384,384]{1,0:T(8,128)(2,1)S(1)}, u32[]{:S(2)}, u32[]{:S(2)}) collective-permute-start(bf16[384,384]{1,0:T(8,128)(2,1)S(1)} %get-tuple-element.71.rest), channel_id=1, source_target_pairs={{0,16},{16,0},{1,17},{17,1},{2,18},{18,2},{3,19},{19,3},{4,20},{20... | collective-permute-start | bytes 884744 | tf_op jit(solution)/shard_map/ppermute | solution.py:469
  84.2 11.0 %collective-permute-start.26 = (bf16[128,1024]{1,0:T(8,128)(2,1)S(1)}, bf16[128,1024]{1,0:T(8,128)(2,1)S(1)}, u32[]{:S(2)}, u32[]{:S(2)}) collective-permute-start(bf16[128,1024]{1,0:T(8,128)(2,1)S(1)} %get-tuple-element.79), channel_id=1, source_target_pairs={{0,4},{1,13},{2,6},{3,15},{4,8},{5,1},{6,10},{7,3},{8,12},{9,5},{1... | collective-permute-start | bytes 786440 | tf_op jit(solution)/shard_map/ppermute | solution.py:483
  85.8 9.4 %collective-permute-start.25 = (bf16[128,1024]{1,0:T(8,128)(2,1)S(1)}, bf16[128,1024]{1,0:T(8,128)(2,1)S(1)}, u32[]{:S(2)}, u32[]{:S(2)}) collective-permute-start(bf16[128,1024]{1,0:T(8,128)(2,1)S(1)} %get-tuple-element.78.own), channel_id=1, source_target_pairs={{1,9},{3,11},{5,13},{7,15},{9,1},{11,3},{13,5},{15,7},{17,25},{19,... | collective-permute-start | bytes 786440 | tf_op jit(solution)/shard_map/ppermute | solution.py:483
  88.5 2.8 %collective-permute-start.31 = (bf16[128,512]{1,0:T(8,128)(2,1)S(1)}, bf16[128,512]{1,0:T(8,128)(2,1)S(1)}, u32[]{:S(2)}, u32[]{:S(2)}) collective-permute-start(bf16[128,512]{1,0:T(8,128)(2,1)S(1)} %get-tuple-element.84), channel_id=1, source_target_pairs={{0,1},{1,0},{2,3},{3,2},{4,5},{5,4},{6,7},{7,6},{8,9},{9,8},{10,11... | collective-permute-start | bytes 393224 | tf_op jit(solution)/shard_map/ppermute | solution.py:486
  90.3 1.3 %collective-permute-start.32 = (bf16[128,512]{1,0:T(8,128)(2,1)S(1)}, bf16[128,512]{1,0:T(8,128)(2,1)S(1)}, u32[]{:S(2)}, u32[]{:S(2)}) collective-permute-start(bf16[128,512]{1,0:T(8,128)(2,1)S(1)} %get-tuple-element.85), channel_id=1, source_target_pairs={{0,1},{1,0},{2,3},{3,2},{4,5},{5,4},{6,7},{7,6},{8,9},{9,8},{10,11... | collective-permute-start | bytes 393224 | tf_op jit(solution)/shard_map/ppermute | solution.py:486
  91.7 9.0 %collective-permute-start.33 = (bf16[128,1024]{1,0:T(8,128)(2,1)S(1)}, bf16[128,1024]{1,0:T(8,128)(2,1)S(1)}, u32[]{:S(2)}, u32[]{:S(2)}) collective-permute-start(bf16[128,1024]{1,0:T(8,128)(2,1)S(1)} %fold.1), channel_id=1, source_target_pairs={{0,2},{1,3},{2,0},{3,1},{4,6},{5,7},{6,4},{7,5},{8,10},{9,11},{10,... | collective-permute-start | bytes 786440 | tf_op jit(solution)/shard_map/ppermute | solution.py:486
  94.6 17.3 %copy-start.7 = (f32[2048]{0:T(1024)S(1)}, f32[2048]{0:T(1024)}, u32[]{:S(2)}) copy-start(f32[2048]{0:T(1024)} %param.19) | copy-start | bytes 24580
  94.6 5.1 %collective-permute-start.35 = (bf16[128,512]{1,0:T(8,128)(2,1)S(1)}, bf16[128,512]{1,0:T(8,128)(2,1)S(1)}, u32[]{:S(2)}, u32[]{:S(2)}) collective-permute-start(bf16[128,512]{1,0:T(8,128)(2,1)S(1)} %get-tuple-element.87), channel_id=1, source_target_pairs={{0,1},{1,0},{2,3},{3,2},{4,5},{5,4},{6,7},{7,6},{8,9},{9,8},{10,11... | collective-permute-start | bytes 393224 | tf_op jit(solution)/shard_map/ppermute | solution.py:486
  95.2 5.5 %collective-permute-start.36 = (bf16[128,512]{1,0:T(8,128)(2,1)S(1)}, bf16[128,512]{1,0:T(8,128)(2,1)S(1)}, u32[]{:S(2)}, u32[]{:S(2)}) collective-permute-start(bf16[128,512]{1,0:T(8,128)(2,1)S(1)} %get-tuple-element.89), channel_id=1, source_target_pairs={{0,1},{1,0},{2,3},{3,2},{4,5},{5,4},{6,7},{7,6},{8,9},{9,8},{10,11... | collective-permute-start | bytes 393224 | tf_op jit(solution)/shard_map/ppermute | solution.py:486
  100.8 8.1 %collective-permute-start.37 = (bf16[64,1024]{1,0:T(8,128)(2,1)S(1)}, bf16[64,1024]{1,0:T(8,128)(2,1)S(1)}, u32[]{:S(2)}, u32[]{:S(2)}) collective-permute-start(bf16[64,1024]{1,0:T(8,128)(2,1)S(1)} %get-tuple-element.90), channel_id=1, source_target_pairs={{0,16},{1,25},{2,18},{3,27},{4,20},{5,29},{6,22},{7,31},{8,24},{9,... | collective-permute-start | bytes 393224 | tf_op jit(solution)/shard_map/ppermute | solution.py:483
  102.3 8.2 %collective-permute-start.38 = (bf16[64,1024]{1,0:T(8,128)(2,1)S(1)}, bf16[64,1024]{1,0:T(8,128)(2,1)S(1)}, u32[]{:S(2)}, u32[]{:S(2)}) collective-permute-start(bf16[64,1024]{1,0:T(8,128)(2,1)S(1)} %get-tuple-element.91), channel_id=1, source_target_pairs={{0,20},{1,29},{2,22},{3,31},{4,24},{5,17},{6,26},{7,19},{8,28},{9,... | collective-permute-start | bytes 393224 | tf_op jit(solution)/shard_map/ppermute | solution.py:483
  102.6 4.3 %collective-permute-start.27 = (bf16[64,512]{1,0:T(8,128)(2,1)S(1)}, bf16[64,512]{1,0:T(8,128)(2,1)S(1)}, u32[]{:S(2)}, u32[]{:S(2)}) collective-permute-start(bf16[64,512]{1,0:T(8,128)(2,1)S(1)} %get-tuple-element.81), channel_id=1, source_target_pairs={{0,2},{1,3},{2,0},{3,1},{4,6},{5,7},{6,4},{7,5},{8,10},{9,11},{10,... | collective-permute-start | bytes 196616 | tf_op jit(solution)/shard_map/ppermute | solution.py:486
  104.1 4.9 %collective-permute-start.28 = (bf16[64,512]{1,0:T(8,128)(2,1)S(1)}, bf16[64,512]{1,0:T(8,128)(2,1)S(1)}, u32[]{:S(2)}, u32[]{:S(2)}) collective-permute-start(bf16[64,512]{1,0:T(8,128)(2,1)S(1)} %get-tuple-element.82), channel_id=1, source_target_pairs={{0,2},{1,3},{2,0},{3,1},{4,6},{5,7},{6,4},{7,5},{8,10},{9,11},{10,... | collective-permute-start | bytes 196616 | tf_op jit(solution)/shard_map/ppermute | solution.py:486
  110.5 1.4 %collective-permute-start.39 = (bf16[64,1024]{1,0:T(8,128)(2,1)S(1)}, bf16[64,1024]{1,0:T(8,128)(2,1)S(1)}, u32[]{:S(2)}, u32[]{:S(2)}) collective-permute-start(bf16[64,1024]{1,0:T(8,128)(2,1)S(1)} %get-tuple-element.93), channel_id=1, source_target_pairs={{0,1},{1,0},{2,3},{3,2},{4,5},{5,4},{6,7},{7,6},{8,9},{9,8},{10,11... | collective-permute-start | bytes 393224 | tf_op jit(solution)/shard_map/ppermute | solution.py:486

commit v22 on v20

--- a/solution.py
+++ b/solution.py
@@ -631,7 +631,7 @@
         outs = (shape_of(2 * rows_here, half_width),) * 2
         return call(pieces_kernel, "pieces", 4, outs, far, keep, *swap_cores(send))
 
-    outs = (quarter_out, *parts_of(2), *parts_of(2), quarter_out)
+    outs = (quarter_out, *parts_of(1), *parts_of(1), quarter_out)
     keep_far, *send, keep_near = call(
         down_both_kernel, "down_both", 16, outs, inner_first, inner_far, inner_rest, w_down[0], scratch=scratch
     )

time: 113 us -> 112 us (level)
    ppermute x20 -> x18, waiting for transfers between devices: 14.6 us -> 12.1 us  [swap_inner(): return lax.ppermute(x, 'expert', [(i, i ^ j) for i in range(expert_count)])]
    ppermute x7, waiting for transfers between devices: 9.22 us -> 11.2 us  [swap_dp(): return lax.ppermute(x, 'dp', [(0, 1), (1, 0)])]
    ppermute x20 -> x18, starting transfers between devices: 17.9 us -> 16.2 us  [swap_inner(): return lax.ppermute(x, 'expert', [(i, i ^ j) for i in range(expert_count)])]
    ppermute x4, starting transfers between devices: 4.07 us -> 5.52 us  [send_outer(): return lax.ppermute(x, ('dp', 'expert'), pairs)]
  transfers between devices with their start and end apart: 39 -> 37, of which waited for: 23 -> 19; matrix products, arithmetic and copies ran while one was open for 1% -> 1% of each run, Pallas kernels for 11% -> 11%
where the time goes in v22:
time: 112 us
  waiting for transfers between devices  49 us (44%)
  starting transfers between devices  42.3 us (38%)
  Pallas kernels  13.8 us (12%)
  local copies, waits for them, and re-layouts  4.58 us (4%)
  between operations  1.57 us (1%)
    ppermute x18, starting transfers between devices, swap_inner(): return lax.ppermute(x, 'expert', [(i, i ^ j) for i in range(expert_count)])  16.2 us
    pallas_call x17, Pallas kernels, call(): pl.pallas_call(kernel, out_shape=outs, in_specs=[first] + [vmem] * (len(a...  13.4 us
    ppermute x18, waiting for transfers between devices, swap_inner(): return lax.ppermute(x, 'expert', [(i, i ^ j) for i in range(expert_count)])  12.1 us
    ppermute x5, waiting for transfers between devices, swap_outer(): lax.ppermute(x, 'expert', [(i, i ^ 4 * s) for i in range(expert_count)])  12.1 us
    ppermute x7, waiting for transfers between devices, swap_dp(): return lax.ppermute(x, 'dp', [(0, 1), (1, 0)])  11.2 us
    ppermute x7, starting transfers between devices, swap_dp(): return lax.ppermute(x, 'dp', [(0, 1), (1, 0)])  9.72 us
    ppermute x3, waiting for transfers between devices, shift_outer(): lax.ppermute(x, 'expert', [(i, (i + 4 * s) % expert_count) for i in range...  7.64 us
    ppermute x5, starting transfers between devices, swap_outer(): lax.ppermute(x, 'expert', [(i, i ^ 4 * s) for i in range(expert_count)])  6.59 us
  transfers between devices with their start and end apart: 37, of which 19 were waited for; matrix products, arithmetic and copies ran while one was open for 1% of the time, Pallas kernels for 11%

profile of v22, /device:TPU:0, one launch (start us, length us, event | category | flops | bytes accessed | tf_op | source)
XLA Modules:
  0.0 112.1 jit_solution(5638736101206797416)
XLA Ops:
  0.6 1.9 %copy-done = bf16[1,1024,1536]{2,1,0:T(8,128)(2,1)S(1)} copy-done((bf16[1,1024,1536]{2,1,0:T(8,128)(2,1)S(1)}, bf16[1,1024,1536]{2,1,0:T(8,128)(2,1)}, u32[]{:S(2)}) %copy-start) | copy-done | bytes 3145752
  2.7 3.0 %collective-permute-start.8 = (bf16[1024,768]{1,0:T(8,128)(2,1)S(1)}, bf16[1024,768]{1,0:T(8,128)(2,1)S(1)}, u32[]{:S(2)}, u32[]{:S(2)}) collective-permute-start(bf16[1024,768]{1,0:T(8,128)(2,1)S(1)} %weight_piece.3), channel_id=1, source_target_pairs={{0,16},{16,0},{1,17},{17,1},{2,18},{18,2},{3,19},{19,3},{4,20},{20... | collective-permute-start | bytes 4718600 | tf_op jit(solution)/shard_map/ppermute | solution.py:468
  5.7 1.5 %collective-permute-start.5 = (bf16[2048,128]{1,0:T(8,128)(2,1)}, bf16[2048,128]{1,0:T(8,128)(2,1)}, u32[]{:S(2)}, u32[]{:S(2)}) collective-permute-start(bf16[2048,128]{1,0:T(8,128)(2,1)} %w0.1), channel_id=1, source_target_pairs={{0,2},{1,3},{2,0},{3,1},{4,6},{5,7},{6,4},{7,5},{8,10},{9,11},{10,... | collective-permute-start | bytes 1572872 | tf_op jit(solution)/shard_map/ppermute | solution.py:485
  7.2 0.6 cut_resid.1
  7.9 2.6 %collective-permute-start.2 = (bf16[64,512]{1,0:T(8,128)(2,1)}, bf16[64,512]{1,0:T(8,128)(2,1)S(1)}, u32[]{:S(2)}, u32[]{:S(2)}) collective-permute-start(bf16[64,512]{1,0:T(8,128)(2,1)} %get-tuple-element.46), channel_id=1, source_target_pairs={{0,8},{1,9},{2,10},{3,11},{4,12},{5,13},{6,14},{7,15},{8,0},{9,1},... | collective-permute-start | bytes 196616 | tf_op jit(solution)/shard_map/ppermute | solution.py:488
  10.5 0.3 collective-permute-start.1
  10.8 1.6 %collective-permute-start = (bf16[64,2048]{1,0:T(8,128)(2,1)S(1)}, bf16[64,2048]{1,0:T(8,128)(2,1)}, u32[]{:S(2)}, u32[]{:S(2)}) collective-permute-start(bf16[64,2048]{1,0:T(8,128)(2,1)S(1)} %bitcast.17), channel_id=1, source_target_pairs={{0,4},{1,5},{2,6},{3,7},{4,0},{5,1},{6,2},{7,3},{8,12},{9,13},{10,... | collective-permute-start | bytes 786440 | tf_op jit(solution)/shard_map/ppermute | solution.py:488
  12.4 0.2 weight_piece.2
  12.6 1.0 copy-done.8
  13.6 0.8 copy-done.10
  15.2 0.8 copy.13
  15.9 0.4 share.1
  16.4 3.1 %collective-permute-done.5.w2 = bf16[2048,128]{1,0:T(8,128)(2,1)} collective-permute-done((bf16[2048,128]{1,0:T(8,128)(2,1)}, bf16[2048,128]{1,0:T(8,128)(2,1)}, u32[]{:S(2)}, u32[]{:S(2)}) %collective-permute-start.5) | collective-permute-done | bytes 524320 | tf_op jit(solution)/shard_map/ppermute | solution.py:485
  19.5 0.5 collective-permute-start.6
  20.0 5.4 %collective-permute-done.1.a2 = bf16[64,2048]{1,0:T(8,128)(2,1)} collective-permute-done((bf16[64,2048]{1,0:T(8,128)(2,1)S(1)}, bf16[64,2048]{1,0:T(8,128)(2,1)}, u32[]{:S(2)}, u32[]{:S(2)}) %collective-permute-start.1) | collective-permute-done | bytes 262176 | tf_op jit(solution)/shard_map/ppermute | solution.py:488
  25.4 0.2 collective-permute-start.3
  25.6 0.8 pad_maximum_fusion
  26.4 1.9 %collective-permute-start.4 = (bf16[64,512]{1,0:T(8,128)(2,1)S(1)}, bf16[64,512]{1,0:T(8,128)(2,1)S(1)}, u32[]{:S(2)}, u32[]{:S(2)}) collective-permute-start(bf16[64,512]{1,0:T(8,128)(2,1)S(1)} %pad_maximum_fusion), channel_id=1, source_target_pairs={{0,4},{1,5},{2,6},{3,7},{4,0},{5,1},{6,2},{7,3},{8,12},{9,13},{10,... | collective-permute-start | bytes 196616 | tf_op jit(solution)/shard_map/ppermute | solution.py:488
  28.2 6.7 %collective-permute-done.4.r13 = bf16[64,512]{1,0:T(8,128)(2,1)S(1)} collective-permute-done((bf16[64,512]{1,0:T(8,128)(2,1)S(1)}, bf16[64,512]{1,0:T(8,128)(2,1)S(1)}, u32[]{:S(2)}, u32[]{:S(2)}) %collective-permute-start.4) | collective-permute-done | bytes 65568 | tf_op jit(solution)/shard_map/ppermute | solution.py:488
  34.9 2.8 %projection.1 = (bf16[128,512]{1,0:T(8,128)(2,1)S(1)}, bf16[128,512]{1,0:T(8,128)(2,1)S(1)}) custom-call(bf16[64,2048]{1,0:T(8,128)(2,1)S(1)} %bitcast.18, bf16[64,2048]{1,0:T(8,128)(2,1)} %collective-permute-done.a1, bf16[64,2048]{1,0:T(8,128)(2,1)} %collective-permute-done.1.a2, bf16[64,2048]{1,0:T(8,128)(2,1)S(1)} %collective-permute-done.3.a3, ...), custom_call_target="tpu_custom_call" | custom-call | flops 1 | bytes 1 | tf_op jit(solution)/shard_map/projection/pallas_call | solution.py:456
  37.8 0.6 collective-permute-start.9
  38.3 1.5 %collective-permute-start.19 = (bf16[640,768]{1,0:T(8,128)(2,1)S(1)}, bf16[640,768]{1,0:T(8,128)(2,1)S(1)}, u32[]{:S(2)}, u32[]{:S(2)}) collective-permute-start(bf16[640,768]{1,0:T(8,128)(2,1)S(1)} %copy-done.9), channel_id=1, source_target_pairs={{0,16},{16,0},{1,17},{17,1},{2,18},{18,2},{3,19},{19,3},{4,20},{20... | collective-permute-start | bytes 2949128 | tf_op jit(solution)/shard_map/ppermute | solution.py:468
  39.9 1.1 collective-permute-done.8.early
  41.0 3.3 %collective-permute-done.9.arrived = bf16[128,512]{1,0:T(8,128)(2,1)S(1)} collective-permute-done((bf16[128,512]{1,0:T(8,128)(2,1)S(1)}, bf16[128,512]{1,0:T(8,128)(2,1)S(1)}, u32[]{:S(2)}, u32[]{:S(2)}) %collective-permute-start.9) | collective-permute-done | bytes 131104 | tf_op jit(solution)/shard_map/ppermute | solution.py:468
  44.3 3.5 %collective-permute-start.12 = (bf16[144,512]{1,0:T(8,128)(2,1)S(1)}, bf16[144,512]{1,0:T(8,128)(2,1)S(1)}, u32[]{:S(2)}, u32[]{:S(2)}) collective-permute-start(bf16[144,512]{1,0:T(8,128)(2,1)S(1)} %stream.1.b0), channel_id=1, source_target_pairs={{0,12},{1,13},{2,14},{3,15},{4,0},{5,1},{6,2},{7,3},{8,4},{9,5},{1... | collective-permute-start | bytes 442376 | tf_op jit(solution)/shard_map/ppermute | solution.py:471
  47.8 0.8 collective-permute-start.10
  48.7 1.9 %collective-permute-start.13 = (bf16[144,512]{1,0:T(8,128)(2,1)S(1)}, bf16[144,512]{1,0:T(8,128)(2,1)S(1)}, u32[]{:S(2)}, u32[]{:S(2)}) collective-permute-start(bf16[144,512]{1,0:T(8,128)(2,1)S(1)} %stream.1.b0), channel_id=1, source_target_pairs={{0,2},{1,3},{2,0},{3,1},{4,6},{5,7},{6,4},{7,5},{8,10},{9,11},{10,... | collective-permute-start | bytes 442376 | tf_op jit(solution)/shard_map/ppermute | solution.py:485
  50.5 1.6 %collective-permute-done.12.b3 = bf16[144,512]{1,0:T(8,128)(2,1)S(1)} collective-permute-done((bf16[144,512]{1,0:T(8,128)(2,1)S(1)}, bf16[144,512]{1,0:T(8,128)(2,1)S(1)}, u32[]{:S(2)}, u32[]{:S(2)}) %collective-permute-start.12) | collective-permute-done | bytes 147488 | tf_op jit(solution)/shard_map/ppermute | solution.py:471
  52.1 1.7 %collective-permute-start.16 = (bf16[144,512]{1,0:T(8,128)(2,1)S(1)}, bf16[144,512]{1,0:T(8,128)(2,1)S(1)}, u32[]{:S(2)}, u32[]{:S(2)}) collective-permute-start(bf16[144,512]{1,0:T(8,128)(2,1)S(1)} %collective-permute-done.12.b3), channel_id=1, source_target_pairs={{0,2},{1,3},{2,0},{3,1},{4,6},{5,7},{6,4},{7,5},{8,10},{9,11},{10,... | collective-permute-start | bytes 442376 | tf_op jit(solution)/shard_map/ppermute | solution.py:485
  53.8 6.0 %collective-permute-done.11.b2 = bf16[144,512]{1,0:T(8,128)(2,1)S(1)} collective-permute-done((bf16[144,512]{1,0:T(8,128)(2,1)S(1)}, bf16[144,512]{1,0:T(8,128)(2,1)S(1)}, u32[]{:S(2)}, u32[]{:S(2)}) %collective-permute-start.11) | collective-permute-done | bytes 147488 | tf_op jit(solution)/shard_map/ppermute | solution.py:471
  59.9 1.1 %collective-permute-start.15 = (bf16[144,512]{1,0:T(8,128)(2,1)S(1)}, bf16[144,512]{1,0:T(8,128)(2,1)S(1)}, u32[]{:S(2)}, u32[]{:S(2)}) collective-permute-start(bf16[144,512]{1,0:T(8,128)(2,1)S(1)} %collective-permute-done.11.b2), channel_id=1, source_target_pairs={{0,2},{1,3},{2,0},{3,1},{4,6},{5,7},{6,4},{7,5},{8,10},{9,11},{10,... | collective-permute-start | bytes 442376 | tf_op jit(solution)/shard_map/ppermute | solution.py:485
  61.0 0.9 collective-permute-start.14
  61.9 1.2 %collective-permute-start.20 = (bf16[384,768]{1,0:T(8,128)(2,1)S(1)}, bf16[384,768]{1,0:T(8,128)(2,1)S(1)}, u32[]{:S(2)}, u32[]{:S(2)}) collective-permute-start(bf16[384,768]{1,0:T(8,128)(2,1)S(1)} %copy-done.11), channel_id=1, source_target_pairs={{0,16},{16,0},{1,17},{17,1},{2,18},{18,2},{3,19},{19,3},{4,20},{20... | collective-permute-start | bytes 1769480 | tf_op jit(solution)/shard_map/ppermute | solution.py:468
  63.1 0.3 norm.2
  63.5 2.3 %collective-permute-done.15.b2 = bf16[144,512]{1,0:T(8,128)(2,1)S(1)} collective-permute-done((bf16[144,512]{1,0:T(8,128)(2,1)S(1)}, bf16[144,512]{1,0:T(8,128)(2,1)S(1)}, u32[]{:S(2)}, u32[]{:S(2)}) %collective-permute-start.15) | collective-permute-done | bytes 147488 | tf_op jit(solution)/shard_map/ppermute | solution.py:485
  65.8 1.6 %collective-permute-done.14.b1 = bf16[144,512]{1,0:T(8,128)(2,1)S(1)} collective-permute-done((bf16[144,512]{1,0:T(8,128)(2,1)S(1)}, bf16[144,512]{1,0:T(8,128)(2,1)S(1)}, u32[]{:S(2)}, u32[]{:S(2)}) %collective-permute-start.14) | collective-permute-done | bytes 147488 | tf_op jit(solution)/shard_map/ppermute | solution.py:485
  67.3 0.8 norm.3
  68.1 2.0 %collective-permute-done.17.group_cx = bf16[128,2176]{1,0:T(8,128)(2,1)S(1)} collective-permute-done((bf16[128,2176]{1,0:T(8,128)(2,1)S(1)}, bf16[128,2176]{1,0:T(8,128)(2,1)S(1)}, u32[]{:S(2)}, u32[]{:S(2)}) %collective-permute-start.17) | collective-permute-done | bytes 557088 | tf_op jit(solution)/shard_map/ppermute | solution.py:485
  70.1 3.4 %first_gate_up.1 = (bf16[384,384]{1,0:T(8,128)(2,1)S(1)}, bf16[128,384]{1,0:T(8,128)(2,1)S(1)}, f32[512,768]{1,0:T(8,128)S(1)}, bf16[512,1024]{1,0:T(8,128)(2,1)S(1)}, f32[512,128]{1,0:T(8,128)S(1)}) custom-call(bf16[128,2176]{1,0:T(8,128)(2,1)S(1)} %get-tuple-element.58.group_x, bf16[128,2176]{1,0:T(8,128)(2,1)S(1)} %collective-permute-done.17.group_cx, ...), custom_call_target="tpu_custom_call" | custom-call | flops 1 | bytes 1 | tf_op jit(solution)/shard_map/first_gate_up/pallas_call | solution.py:456
  73.5 0.9 collective-permute-start.26
  74.4 2.6 %collective-permute-done.20.refs_1_ = bf16[384,768]{1,0:T(8,128)(2,1)S(1)} collective-permute-done((bf16[384,768]{1,0:T(8,128)(2,1)S(1)}, bf16[384,768]{1,0:T(8,128)(2,1)S(1)}, u32[]{:S(2)}, u32[]{:S(2)}) %collective-permute-start.20) | collective-permute-done | bytes 589856 | tf_op jit(solution)/shard_map/ppermute | solution.py:468
  77.1 1.5 %last_gate_up.1 = (bf16[256,384]{1,0:T(8,128)(2,1)S(1)}, bf16[384,384]{1,0:T(8,128)(2,1)S(1)}) custom-call(bf16[128,384]{1,0:T(8,128)(2,1)S(1)} %get-tuple-element.61.second, f32[512,768]{1,0:T(8,128)S(1)} %get-tuple-element.62.part, bf16[512,1024]{1,0:T(8,128)(2,1)S(1)} %get-tuple-element.63.other, f32[512,128]{1,0:T(8,128)S(1)} %get-tuple-element.64.share, ...), custom_call_target="tpu_custom_call" | custom-call | flops 1 | bytes 1 | tf_op jit(solution)/shard_map/last_gate_up/pallas_call | solution.py:456
  78.5 1.0 down_both.1
  79.6 0.5 collective-permute-start.22
  80.1 2.5 %collective-permute-start.27 = (bf16[256,384]{1,0:T(8,128)(2,1)S(1)}, bf16[256,384]{1,0:T(8,128)(2,1)S(1)}, u32[]{:S(2)}, u32[]{:S(2)}) collective-permute-start(bf16[256,384]{1,0:T(8,128)(2,1)S(1)} %get-tuple-element.67.far), channel_id=1, source_target_pairs={{0,16},{16,0},{1,17},{17,1},{2,18},{18,2},{3,19},{19,3},{4,20},{20... | collective-permute-start | bytes 589832 | tf_op jit(solution)/shard_map/ppermute | solution.py:468
  82.8 2.1 %collective-permute-start.24 = (bf16[128,1024]{1,0:T(8,128)(2,1)S(1)}, bf16[128,1024]{1,0:T(8,128)(2,1)S(1)}, u32[]{:S(2)}, u32[]{:S(2)}) collective-permute-start(bf16[128,1024]{1,0:T(8,128)(2,1)S(1)} %get-tuple-element.74), channel_id=1, source_target_pairs={{0,4},{1,13},{2,6},{3,15},{4,8},{5,1},{6,10},{7,3},{8,12},{9,5},{1... | collective-permute-start | bytes 786440 | tf_op jit(solution)/shard_map/ppermute | solution.py:482
  84.9 0.7 collective-permute-start.23
  85.5 2.8 %collective-permute-done.27.far = bf16[256,384]{1,0:T(8,128)(2,1)S(1)} collective-permute-done((bf16[256,384]{1,0:T(8,128)(2,1)S(1)}, bf16[256,384]{1,0:T(8,128)(2,1)S(1)}, u32[]{:S(2)}, u32[]{:S(2)}) %collective-permute-start.27) | collective-permute-done | bytes 196640 | tf_op jit(solution)/shard_map/ppermute | solution.py:468
  88.3 0.6 down.2
  89.0 0.5 collective-permute-start.29
  89.5 0.8 collective-permute-done.28.refs_0_
  90.3 0.2 collective-permute-done.29.refs_1_
  90.6 2.1 %collective-permute-start.30 = (bf16[128,1024]{1,0:T(8,128)(2,1)S(1)}, bf16[128,1024]{1,0:T(8,128)(2,1)S(1)}, u32[]{:S(2)}, u32[]{:S(2)}) collective-permute-start(bf16[128,1024]{1,0:T(8,128)(2,1)S(1)} %fold.1), channel_id=1, source_target_pairs={{0,2},{1,3},{2,0},{3,1},{4,6},{5,7},{6,4},{7,5},{8,10},{9,11},{10,... | collective-permute-start | bytes 786440 | tf_op jit(solution)/shard_map/ppermute | solution.py:485
  92.7 1.4 %collective-permute-done.31.rest = bf16[384,384]{1,0:T(8,128)(2,1)S(1)} collective-permute-done((bf16[384,384]{1,0:T(8,128)(2,1)S(1)}, bf16[384,384]{1,0:T(8,128)(2,1)S(1)}, u32[]{:S(2)}, u32[]{:S(2)}) %collective-permute-start.31) | collective-permute-done | bytes 294944 | tf_op jit(solution)/shard_map/ppermute | solution.py:468
  94.1 0.6 down.3
  94.9 3.3 %collective-permute-start.33 = (bf16[128,512]{1,0:T(8,128)(2,1)S(1)}, bf16[128,512]{1,0:T(8,128)(2,1)S(1)}, u32[]{:S(2)}, u32[]{:S(2)}) collective-permute-start(bf16[128,512]{1,0:T(8,128)(2,1)S(1)} %get-tuple-element.83), channel_id=1, source_target_pairs={{0,1},{1,0},{2,3},{3,2},{4,5},{5,4},{6,7},{7,6},{8,9},{9,8},{10,11... | collective-permute-start | bytes 393224 | tf_op jit(solution)/shard_map/ppermute | solution.py:485
  98.2 1.8 %collective-permute-start.25 = (bf16[64,1024]{1,0:T(8,128)(2,1)S(1)}, bf16[64,1024]{1,0:T(8,128)(2,1)S(1)}, u32[]{:S(2)}, u32[]{:S(2)}) collective-permute-start(bf16[64,1024]{1,0:T(8,128)(2,1)S(1)} %get-tuple-element.76), channel_id=1, source_target_pairs={{0,2},{1,3},{2,0},{3,1},{4,6},{5,7},{6,4},{7,5},{8,10},{9,11},{10,... | collective-permute-start | bytes 393224 | tf_op jit(solution)/shard_map/ppermute | solution.py:485
  100.1 1.6 %collective-permute-start.34 = (bf16[64,1024]{1,0:T(8,128)(2,1)S(1)}, bf16[64,1024]{1,0:T(8,128)(2,1)S(1)}, u32[]{:S(2)}, u32[]{:S(2)}) collective-permute-start(bf16[64,1024]{1,0:T(8,128)(2,1)S(1)} %get-tuple-element.84), channel_id=1, source_target_pairs={{0,16},{1,25},{2,18},{3,27},{4,20},{5,29},{6,22},{7,31},{8,24},{9,... | collective-permute-start | bytes 393224 | tf_op jit(solution)/shard_map/ppermute | solution.py:482
  101.7 1.2 %collective-permute-start.35 = (bf16[64,1024]{1,0:T(8,128)(2,1)S(1)}, bf16[64,1024]{1,0:T(8,128)(2,1)S(1)}, u32[]{:S(2)}, u32[]{:S(2)}) collective-permute-start(bf16[64,1024]{1,0:T(8,128)(2,1)S(1)} %get-tuple-element.85), channel_id=1, source_target_pairs={{0,20},{1,29},{2,22},{3,31},{4,24},{5,17},{6,26},{7,19},{8,28},{9,... | collective-permute-start | bytes 393224 | tf_op jit(solution)/shard_map/ppermute | solution.py:482
  102.9 0.9 collective-permute-done.25.far
  103.7 4.7 %collective-permute-done.34.b0 = bf16[64,1024]{1,0:T(8,128)(2,1)S(1)} collective-permute-done((bf16[64,1024]{1,0:T(8,128)(2,1)S(1)}, bf16[64,1024]{1,0:T(8,128)(2,1)S(1)}, u32[]{:S(2)}, u32[]{:S(2)}) %collective-permute-start.34) | collective-permute-done | bytes 131104 | tf_op jit(solution)/shard_map/ppermute | solution.py:482
  108.4 1.3 %collective-permute-done.35.b1 = bf16[64,1024]{1,0:T(8,128)(2,1)S(1)} collective-permute-done((bf16[64,1024]{1,0:T(8,128)(2,1)S(1)}, bf16[64,1024]{1,0:T(8,128)(2,1)S(1)}, u32[]{:S(2)}, u32[]{:S(2)}) %collective-permute-start.35) | collective-permute-done | bytes 131104 | tf_op jit(solution)/shard_map/ppermute | solution.py:482
  109.9 1.3 %collective-permute-done.36.core = bf16[64,1024]{1,0:T(8,128)(2,1)S(1)} collective-permute-done((bf16[64,1024]{1,0:T(8,128)(2,1)S(1)}, bf16[64,1024]{1,0:T(8,128)(2,1)S(1)}, u32[]{:S(2)}, u32[]{:S(2)}) %collective-permute-start.36) | collective-permute-done | bytes 131104 | tf_op jit(solution)/shard_map/ppermute | solution.py:485
  111.2 0.8 closing.1
  (59 shorter events, 1.3 us)
Async XLA Ops:
  0.6 1.9 %copy-start = (bf16[1,1024,1536]{2,1,0:T(8,128)(2,1)S(1)}, bf16[1,1024,1536]{2,1,0:T(8,128)(2,1)}, u32[]{:S(2)}) copy-start(bf16[1,1024,1536]{2,1,0:T(8,128)(2,1)} %param.17) | copy-start | bytes 9437188
  2.5 4.7 %copy-start.4 = (bf16[1,32,2048]{2,1,0:T(8,128)(2,1)S(1)}, bf16[1,32,2048]{2,1,0:T(8,128)(2,1)}, u32[]{:S(2)}) copy-start(bf16[1,32,2048]{2,1,0:T(8,128)(2,1)} %param.11) | copy-start | bytes 393220
  2.5 7.9 %copy-start.3 = (bf16[1,64,2048]{2,1,0:T(8,128)(2,1)S(1)}, bf16[1,64,2048]{2,1,0:T(8,128)(2,1)}, u32[]{:S(2)}) copy-start(bf16[1,64,2048]{2,1,0:T(8,128)(2,1)} %param.10) | copy-start | bytes 786436
  2.7 38.3 %collective-permute-start.8 = (bf16[1024,768]{1,0:T(8,128)(2,1)S(1)}, bf16[1024,768]{1,0:T(8,128)(2,1)S(1)}, u32[]{:S(2)}, u32[]{:S(2)}) collective-permute-start(bf16[1024,768]{1,0:T(8,128)(2,1)S(1)} %weight_piece.3), channel_id=1, source_target_pairs={{0,16},{16,0},{1,17},{17,1},{2,18},{18,2},{3,19},{19,3},{4,20},{20... | collective-permute-start | bytes 4718600 | tf_op jit(solution)/shard_map/ppermute | solution.py:468
  5.7 13.7 %collective-permute-start.5 = (bf16[2048,128]{1,0:T(8,128)(2,1)}, bf16[2048,128]{1,0:T(8,128)(2,1)}, u32[]{:S(2)}, u32[]{:S(2)}) collective-permute-start(bf16[2048,128]{1,0:T(8,128)(2,1)} %w0.1), channel_id=1, source_target_pairs={{0,2},{1,3},{2,0},{3,1},{4,6},{5,7},{6,4},{7,5},{8,10},{9,11},{10,... | collective-permute-start | bytes 1572872 | tf_op jit(solution)/shard_map/ppermute | solution.py:485
  7.9 4.7 %copy-start.6 = (bf16[32,512]{1,0:T(8,128)(2,1)}, bf16[32,512]{1,0:T(8,128)(2,1)S(1)}, u32[]{:S(2)}) copy-start(bf16[32,512]{1,0:T(8,128)(2,1)S(1)} %get-tuple-element.48) | copy-start | bytes 98308
  7.9 11.6 %collective-permute-start.2 = (bf16[64,512]{1,0:T(8,128)(2,1)}, bf16[64,512]{1,0:T(8,128)(2,1)S(1)}, u32[]{:S(2)}, u32[]{:S(2)}) collective-permute-start(bf16[64,512]{1,0:T(8,128)(2,1)} %get-tuple-element.46), channel_id=1, source_target_pairs={{0,8},{1,9},{2,10},{3,11},{4,12},{5,13},{6,14},{7,15},{8,0},{9,1},... | collective-permute-start | bytes 196616 | tf_op jit(solution)/shard_map/ppermute | solution.py:488
  10.5 4.6 %copy-start.12 = (s32[1,32,8]{1,2,0:T(8,128)S(1)}, s32[1,32,8]{1,2,0:T(8,128)}, u32[]{:S(2)}) copy-start(s32[1,32,8]{1,2,0:T(8,128)} %param.14) | copy-start | bytes 3076
  10.5 14.9 %collective-permute-start.1 = (bf16[64,2048]{1,0:T(8,128)(2,1)S(1)}, bf16[64,2048]{1,0:T(8,128)(2,1)}, u32[]{:S(2)}, u32[]{:S(2)}) collective-permute-start(bf16[64,2048]{1,0:T(8,128)(2,1)S(1)} %bitcast.16), channel_id=1, source_target_pairs={{0,8},{1,9},{2,10},{3,11},{4,12},{5,13},{6,14},{7,15},{8,0},{9,1},... | collective-permute-start | bytes 786440 | tf_op jit(solution)/shard_map/ppermute | solution.py:488
  10.8 14.5 %collective-permute-start = (bf16[64,2048]{1,0:T(8,128)(2,1)S(1)}, bf16[64,2048]{1,0:T(8,128)(2,1)}, u32[]{:S(2)}, u32[]{:S(2)}) collective-permute-start(bf16[64,2048]{1,0:T(8,128)(2,1)S(1)} %bitcast.17), channel_id=1, source_target_pairs={{0,4},{1,5},{2,6},{3,7},{4,0},{5,1},{6,2},{7,3},{8,12},{9,13},{10,... | collective-permute-start | bytes 786440 | tf_op jit(solution)/shard_map/ppermute | solution.py:488
  12.6 1.0 copy-start.8
  13.6 0.8 copy-start.10
  19.4 15.4 %collective-permute-start.7 = (bf16[2048,128]{1,0:T(8,128)(2,1)}, bf16[2048,128]{1,0:T(8,128)(2,1)S(1)}, u32[]{:S(2)}, u32[]{:S(2)}) collective-permute-start(bf16[2048,128]{1,0:T(8,128)(2,1)} %collective-permute-done.5.w2), channel_id=1, source_target_pairs={{0,1},{1,0},{2,3},{3,2},{4,5},{5,4},{6,7},{7,6},{8,9},{9,8},{10,11... | collective-permute-start | bytes 1572872 | tf_op jit(solution)/shard_map/ppermute | solution.py:485
  19.5 15.4 %collective-permute-start.6 = (bf16[2048,128]{1,0:T(8,128)(2,1)}, bf16[2048,128]{1,0:T(8,128)(2,1)S(1)}, u32[]{:S(2)}, u32[]{:S(2)}) collective-permute-start(bf16[2048,128]{1,0:T(8,128)(2,1)} %w0.1), channel_id=1, source_target_pairs={{0,1},{1,0},{2,3},{3,2},{4,5},{5,4},{6,7},{7,6},{8,9},{9,8},{10,11... | collective-permute-start | bytes 1572872 | tf_op jit(solution)/shard_map/ppermute | solution.py:485
  25.4 9.5 %collective-permute-start.3 = (bf16[64,2048]{1,0:T(8,128)(2,1)}, bf16[64,2048]{1,0:T(8,128)(2,1)S(1)}, u32[]{:S(2)}, u32[]{:S(2)}) collective-permute-start(bf16[64,2048]{1,0:T(8,128)(2,1)} %collective-permute-done.1.a2), channel_id=1, source_target_pairs={{0,4},{1,5},{2,6},{3,7},{4,0},{5,1},{6,2},{7,3},{8,12},{9,13},{10,... | collective-permute-start | bytes 786440 | tf_op jit(solution)/shard_map/ppermute | solution.py:488
  26.3 12.0 %copy-start.9 = (bf16[640,768]{1,0:T(8,128)(2,1)S(1)}, bf16[640,768]{1,0:T(8,128)(2,1)}, u32[]{:S(2)}) copy-start(bf16[640,768]{1,0:T(8,128)(2,1)} %copy-done.8) | copy-start | bytes 2949124
  26.3 35.6 %copy-start.11 = (bf16[384,768]{1,0:T(8,128)(2,1)S(1)}, bf16[384,768]{1,0:T(8,128)(2,1)}, u32[]{:S(2)}) copy-start(bf16[384,768]{1,0:T(8,128)(2,1)} %copy-done.10) | copy-start | bytes 1769476
  26.4 36.7 %copy-start.5 = (f32[2048]{0:T(1024)S(1)}, f32[2048]{0:T(1024)}, u32[]{:S(2)}) copy-start(f32[2048]{0:T(1024)} %param.13) | copy-start | bytes 24580
  26.4 8.5 %collective-permute-start.4 = (bf16[64,512]{1,0:T(8,128)(2,1)S(1)}, bf16[64,512]{1,0:T(8,128)(2,1)S(1)}, u32[]{:S(2)}, u32[]{:S(2)}) collective-permute-start(bf16[64,512]{1,0:T(8,128)(2,1)S(1)} %pad_maximum_fusion), channel_id=1, source_target_pairs={{0,4},{1,5},{2,6},{3,7},{4,0},{5,1},{6,2},{7,3},{8,12},{9,13},{10,... | collective-permute-start | bytes 196616 | tf_op jit(solution)/shard_map/ppermute | solution.py:488
  34.9 35.2 %copy-start.1 = (bf16[1,1024,1536]{2,1,0:T(8,128)(2,1)S(1)}, bf16[1,1024,1536]{2,1,0:T(8,128)(2,1)}, u32[]{:S(2)}) copy-start(bf16[1,1024,1536]{2,1,0:T(8,128)(2,1)} %param.17) | copy-start | bytes 9437188
  37.8 6.5 %collective-permute-start.9 = (bf16[128,512]{1,0:T(8,128)(2,1)S(1)}, bf16[128,512]{1,0:T(8,128)(2,1)S(1)}, u32[]{:S(2)}, u32[]{:S(2)}) collective-permute-start(bf16[128,512]{1,0:T(8,128)(2,1)S(1)} %get-tuple-element.55), channel_id=1, source_target_pairs={{0,16},{16,0},{1,17},{17,1},{2,18},{18,2},{3,19},{19,3},{4,20},{20... | collective-permute-start | bytes 393224 | tf_op jit(solution)/shard_map/ppermute | solution.py:468
  38.3 38.7 %collective-permute-start.19 = (bf16[640,768]{1,0:T(8,128)(2,1)S(1)}, bf16[640,768]{1,0:T(8,128)(2,1)S(1)}, u32[]{:S(2)}, u32[]{:S(2)}) collective-permute-start(bf16[640,768]{1,0:T(8,128)(2,1)S(1)} %copy-done.9), channel_id=1, source_target_pairs={{0,16},{16,0},{1,17},{17,1},{2,18},{18,2},{3,19},{19,3},{4,20},{20... | collective-permute-start | bytes 2949128 | tf_op jit(solution)/shard_map/ppermute | solution.py:468
  44.3 7.8 %collective-permute-start.12 = (bf16[144,512]{1,0:T(8,128)(2,1)S(1)}, bf16[144,512]{1,0:T(8,128)(2,1)S(1)}, u32[]{:S(2)}, u32[]{:S(2)}) collective-permute-start(bf16[144,512]{1,0:T(8,128)(2,1)S(1)} %stream.1.b0), channel_id=1, source_target_pairs={{0,12},{1,13},{2,14},{3,15},{4,0},{5,1},{6,2},{7,3},{8,4},{9,5},{1... | collective-permute-start | bytes 442376 | tf_op jit(solution)/shard_map/ppermute | solution.py:471
  47.8 12.0 %collective-permute-start.11 = (bf16[144,512]{1,0:T(8,128)(2,1)S(1)}, bf16[144,512]{1,0:T(8,128)(2,1)S(1)}, u32[]{:S(2)}, u32[]{:S(2)}) collective-permute-start(bf16[144,512]{1,0:T(8,128)(2,1)S(1)} %stream.1.b0), channel_id=1, source_target_pairs={{0,8},{1,9},{2,10},{3,11},{4,12},{5,13},{6,14},{7,15},{8,0},{9,1},... | collective-permute-start | bytes 442376 | tf_op jit(solution)/shard_map/ppermute | solution.py:471
  47.8 13.2 %collective-permute-start.10 = (bf16[144,512]{1,0:T(8,128)(2,1)S(1)}, bf16[144,512]{1,0:T(8,128)(2,1)S(1)}, u32[]{:S(2)}, u32[]{:S(2)}) collective-permute-start(bf16[144,512]{1,0:T(8,128)(2,1)S(1)} %stream.1.b0), channel_id=1, source_target_pairs={{0,4},{1,5},{2,6},{3,7},{4,8},{5,9},{6,10},{7,11},{8,12},{9,13},{1... | collective-permute-start | bytes 442376 | tf_op jit(solution)/shard_map/ppermute | solution.py:471
  48.7 13.2 %collective-permute-start.13 = (bf16[144,512]{1,0:T(8,128)(2,1)S(1)}, bf16[144,512]{1,0:T(8,128)(2,1)S(1)}, u32[]{:S(2)}, u32[]{:S(2)}) collective-permute-start(bf16[144,512]{1,0:T(8,128)(2,1)S(1)} %stream.1.b0), channel_id=1, source_target_pairs={{0,2},{1,3},{2,0},{3,1},{4,6},{5,7},{6,4},{7,5},{8,10},{9,11},{10,... | collective-permute-start | bytes 442376 | tf_op jit(solution)/shard_map/ppermute | solution.py:485
  52.1 11.3 %collective-permute-start.16 = (bf16[144,512]{1,0:T(8,128)(2,1)S(1)}, bf16[144,512]{1,0:T(8,128)(2,1)S(1)}, u32[]{:S(2)}, u32[]{:S(2)}) collective-permute-start(bf16[144,512]{1,0:T(8,128)(2,1)S(1)} %collective-permute-done.12.b3), channel_id=1, source_target_pairs={{0,2},{1,3},{2,0},{3,1},{4,6},{5,7},{6,4},{7,5},{8,10},{9,11},{10,... | collective-permute-start | bytes 442376 | tf_op jit(solution)/shard_map/ppermute | solution.py:485
  59.9 5.9 %collective-permute-start.15 = (bf16[144,512]{1,0:T(8,128)(2,1)S(1)}, bf16[144,512]{1,0:T(8,128)(2,1)S(1)}, u32[]{:S(2)}, u32[]{:S(2)}) collective-permute-start(bf16[144,512]{1,0:T(8,128)(2,1)S(1)} %collective-permute-done.11.b2), channel_id=1, source_target_pairs={{0,2},{1,3},{2,0},{3,1},{4,6},{5,7},{6,4},{7,5},{8,10},{9,11},{10,... | collective-permute-start | bytes 442376 | tf_op jit(solution)/shard_map/ppermute | solution.py:485
  61.0 6.3 %collective-permute-start.14 = (bf16[144,512]{1,0:T(8,128)(2,1)S(1)}, bf16[144,512]{1,0:T(8,128)(2,1)S(1)}, u32[]{:S(2)}, u32[]{:S(2)}) collective-permute-start(bf16[144,512]{1,0:T(8,128)(2,1)S(1)} %collective-permute-done.10.b1), channel_id=1, source_target_pairs={{0,2},{1,3},{2,0},{3,1},{4,6},{5,7},{6,4},{7,5},{8,10},{9,11},{10,... | collective-permute-start | bytes 442376 | tf_op jit(solution)/shard_map/ppermute | solution.py:485
  61.9 15.1 %collective-permute-start.20 = (bf16[384,768]{1,0:T(8,128)(2,1)S(1)}, bf16[384,768]{1,0:T(8,128)(2,1)S(1)}, u32[]{:S(2)}, u32[]{:S(2)}) collective-permute-start(bf16[384,768]{1,0:T(8,128)(2,1)S(1)} %copy-done.11), channel_id=1, source_target_pairs={{0,16},{16,0},{1,17},{17,1},{2,18},{18,2},{3,19},{19,3},{4,20},{20... | collective-permute-start | bytes 1769480 | tf_op jit(solution)/shard_map/ppermute | solution.py:468
  63.4 4.7 %collective-permute-start.18 = (bf16[128,2176]{1,0:T(8,128)(2,1)S(1)}, bf16[128,2176]{1,0:T(8,128)(2,1)S(1)}, u32[]{:S(2)}, u32[]{:S(2)}) collective-permute-start(bf16[128,2176]{1,0:T(8,128)(2,1)S(1)} %get-tuple-element.59.group), channel_id=1, source_target_pairs={{0,1},{1,0},{2,3},{3,2},{4,5},{5,4},{6,7},{7,6},{8,9},{9,8},{10,11... | collective-permute-start | bytes 1671176 | tf_op jit(solution)/shard_map/ppermute | solution.py:485
  68.1 2.0 %collective-permute-start.17 = (bf16[128,2176]{1,0:T(8,128)(2,1)S(1)}, bf16[128,2176]{1,0:T(8,128)(2,1)S(1)}, u32[]{:S(2)}, u32[]{:S(2)}) collective-permute-start(bf16[128,2176]{1,0:T(8,128)(2,1)S(1)} %get-tuple-element.58.group_x), channel_id=1, source_target_pairs={{0,1},{1,0},{2,3},{3,2},{4,5},{5,4},{6,7},{7,6},{8,9},{9,8},{10,11... | collective-permute-start | bytes 1671176 | tf_op jit(solution)/shard_map/ppermute | solution.py:485
  73.5 14.8 %collective-permute-start.26 = (bf16[384,384]{1,0:T(8,128)(2,1)S(1)}, bf16[384,384]{1,0:T(8,128)(2,1)S(1)}, u32[]{:S(2)}, u32[]{:S(2)}) collective-permute-start(bf16[384,384]{1,0:T(8,128)(2,1)S(1)} %get-tuple-element.60.first), channel_id=1, source_target_pairs={{0,16},{16,0},{1,17},{17,1},{2,18},{18,2},{3,19},{19,3},{4,20},{20... | collective-permute-start | bytes 884744 | tf_op jit(solution)/shard_map/ppermute | solution.py:468
  77.1 1.5 %copy-start.2 = (bf16[1,768,1024]{2,1,0:T(8,128)(2,1)S(1)}, bf16[1,768,1024]{2,1,0:T(8,128)(2,1)}, u32[]{:S(2)}) copy-start(bf16[1,768,1024]{2,1,0:T(8,128)(2,1)} %param.18) | copy-start | bytes 4718596
  79.5 3.1 %collective-permute-start.21 = (bf16[128,1024]{1,0:T(8,128)(2,1)S(1)}, bf16[128,1024]{1,0:T(8,128)(2,1)S(1)}, u32[]{:S(2)}, u32[]{:S(2)}) collective-permute-start(bf16[128,1024]{1,0:T(8,128)(2,1)S(1)} %get-tuple-element.71), channel_id=1, source_target_pairs={{0,1},{1,0},{2,3},{3,2},{4,5},{5,4},{6,7},{7,6},{8,9},{9,8},{10,11... | collective-permute-start | bytes 786440 | tf_op jit(solution)/shard_map/ppermute | solution.py:485
  79.6 3.0 %collective-permute-start.22 = (bf16[128,1024]{1,0:T(8,128)(2,1)S(1)}, bf16[128,1024]{1,0:T(8,128)(2,1)S(1)}, u32[]{:S(2)}, u32[]{:S(2)}) collective-permute-start(bf16[128,1024]{1,0:T(8,128)(2,1)S(1)} %get-tuple-element.72), channel_id=1, source_target_pairs={{0,1},{1,0},{2,3},{3,2},{4,5},{5,4},{6,7},{7,6},{8,9},{9,8},{10,11... | collective-permute-start | bytes 786440 | tf_op jit(solution)/shard_map/ppermute | solution.py:485
  80.1 8.2 %collective-permute-start.27 = (bf16[256,384]{1,0:T(8,128)(2,1)S(1)}, bf16[256,384]{1,0:T(8,128)(2,1)S(1)}, u32[]{:S(2)}, u32[]{:S(2)}) collective-permute-start(bf16[256,384]{1,0:T(8,128)(2,1)S(1)} %get-tuple-element.67.far), channel_id=1, source_target_pairs={{0,16},{16,0},{1,17},{17,1},{2,18},{18,2},{3,19},{19,3},{4,20},{20... | collective-permute-start | bytes 589832 | tf_op jit(solution)/shard_map/ppermute | solution.py:468
  82.6 11.5 %collective-permute-start.31 = (bf16[384,384]{1,0:T(8,128)(2,1)S(1)}, bf16[384,384]{1,0:T(8,128)(2,1)S(1)}, u32[]{:S(2)}, u32[]{:S(2)}) collective-permute-start(bf16[384,384]{1,0:T(8,128)(2,1)S(1)} %get-tuple-element.68.rest), channel_id=1, source_target_pairs={{0,16},{16,0},{1,17},{17,1},{2,18},{18,2},{3,19},{19,3},{4,20},{20... | collective-permute-start | bytes 884744 | tf_op jit(solution)/shard_map/ppermute | solution.py:468
  82.8 12.0 %collective-permute-start.24 = (bf16[128,1024]{1,0:T(8,128)(2,1)S(1)}, bf16[128,1024]{1,0:T(8,128)(2,1)S(1)}, u32[]{:S(2)}, u32[]{:S(2)}) collective-permute-start(bf16[128,1024]{1,0:T(8,128)(2,1)S(1)} %get-tuple-element.74), channel_id=1, source_target_pairs={{0,4},{1,13},{2,6},{3,15},{4,8},{5,1},{6,10},{7,3},{8,12},{9,5},{1... | collective-permute-start | bytes 786440 | tf_op jit(solution)/shard_map/ppermute | solution.py:482
  84.9 9.9 %collective-permute-start.23 = (bf16[128,1024]{1,0:T(8,128)(2,1)S(1)}, bf16[128,1024]{1,0:T(8,128)(2,1)S(1)}, u32[]{:S(2)}, u32[]{:S(2)}) collective-permute-start(bf16[128,1024]{1,0:T(8,128)(2,1)S(1)} %get-tuple-element.73.own), channel_id=1, source_target_pairs={{1,9},{3,11},{5,13},{7,15},{9,1},{11,3},{13,5},{15,7},{17,25},{19,... | collective-permute-start | bytes 786440 | tf_op jit(solution)/shard_map/ppermute | solution.py:482
  88.9 1.4 %collective-permute-start.28 = (bf16[128,512]{1,0:T(8,128)(2,1)S(1)}, bf16[128,512]{1,0:T(8,128)(2,1)S(1)}, u32[]{:S(2)}, u32[]{:S(2)}) collective-permute-start(bf16[128,512]{1,0:T(8,128)(2,1)S(1)} %get-tuple-element.78), channel_id=1, source_target_pairs={{0,1},{1,0},{2,3},{3,2},{4,5},{5,4},{6,7},{7,6},{8,9},{9,8},{10,11... | collective-permute-start | bytes 393224 | tf_op jit(solution)/shard_map/ppermute | solution.py:485
  89.0 1.5 %collective-permute-start.29 = (bf16[128,512]{1,0:T(8,128)(2,1)S(1)}, bf16[128,512]{1,0:T(8,128)(2,1)S(1)}, u32[]{:S(2)}, u32[]{:S(2)}) collective-permute-start(bf16[128,512]{1,0:T(8,128)(2,1)S(1)} %get-tuple-element.79), channel_id=1, source_target_pairs={{0,1},{1,0},{2,3},{3,2},{4,5},{5,4},{6,7},{7,6},{8,9},{9,8},{10,11... | collective-permute-start | bytes 393224 | tf_op jit(solution)/shard_map/ppermute | solution.py:485
  90.6 9.4 %collective-permute-start.30 = (bf16[128,1024]{1,0:T(8,128)(2,1)S(1)}, bf16[128,1024]{1,0:T(8,128)(2,1)S(1)}, u32[]{:S(2)}, u32[]{:S(2)}) collective-permute-start(bf16[128,1024]{1,0:T(8,128)(2,1)S(1)} %fold.1), channel_id=1, source_target_pairs={{0,2},{1,3},{2,0},{3,1},{4,6},{5,7},{6,4},{7,5},{8,10},{9,11},{10,... | collective-permute-start | bytes 786440 | tf_op jit(solution)/shard_map/ppermute | solution.py:485
  94.7 16.6 %copy-start.7 = (f32[2048]{0:T(1024)S(1)}, f32[2048]{0:T(1024)}, u32[]{:S(2)}) copy-start(f32[2048]{0:T(1024)} %param.19) | copy-start | bytes 24580
  94.7 5.3 %collective-permute-start.32 = (bf16[128,512]{1,0:T(8,128)(2,1)S(1)}, bf16[128,512]{1,0:T(8,128)(2,1)S(1)}, u32[]{:S(2)}, u32[]{:S(2)}) collective-permute-start(bf16[128,512]{1,0:T(8,128)(2,1)S(1)} %get-tuple-element.81), channel_id=1, source_target_pairs={{0,1},{1,0},{2,3},{3,2},{4,5},{5,4},{6,7},{7,6},{8,9},{9,8},{10,11... | collective-permute-start | bytes 393224 | tf_op jit(solution)/shard_map/ppermute | solution.py:485
  94.9 5.1 %collective-permute-start.33 = (bf16[128,512]{1,0:T(8,128)(2,1)S(1)}, bf16[128,512]{1,0:T(8,128)(2,1)S(1)}, u32[]{:S(2)}, u32[]{:S(2)}) collective-permute-start(bf16[128,512]{1,0:T(8,128)(2,1)S(1)} %get-tuple-element.83), channel_id=1, source_target_pairs={{0,1},{1,0},{2,3},{3,2},{4,5},{5,4},{6,7},{7,6},{8,9},{9,8},{10,11... | collective-permute-start | bytes 393224 | tf_op jit(solution)/shard_map/ppermute | solution.py:485
  98.2 5.6 %collective-permute-start.25 = (bf16[64,1024]{1,0:T(8,128)(2,1)S(1)}, bf16[64,1024]{1,0:T(8,128)(2,1)S(1)}, u32[]{:S(2)}, u32[]{:S(2)}) collective-permute-start(bf16[64,1024]{1,0:T(8,128)(2,1)S(1)} %get-tuple-element.76), channel_id=1, source_target_pairs={{0,2},{1,3},{2,0},{3,1},{4,6},{5,7},{6,4},{7,5},{8,10},{9,11},{10,... | collective-permute-start | bytes 393224 | tf_op jit(solution)/shard_map/ppermute | solution.py:485
  100.1 8.3 %collective-permute-start.34 = (bf16[64,1024]{1,0:T(8,128)(2,1)S(1)}, bf16[64,1024]{1,0:T(8,128)(2,1)S(1)}, u32[]{:S(2)}, u32[]{:S(2)}) collective-permute-start(bf16[64,1024]{1,0:T(8,128)(2,1)S(1)} %get-tuple-element.84), channel_id=1, source_target_pairs={{0,16},{1,25},{2,18},{3,27},{4,20},{5,29},{6,22},{7,31},{8,24},{9,... | collective-permute-start | bytes 393224 | tf_op jit(solution)/shard_map/ppermute | solution.py:482
  101.7 8.0 %collective-permute-start.35 = (bf16[64,1024]{1,0:T(8,128)(2,1)S(1)}, bf16[64,1024]{1,0:T(8,128)(2,1)S(1)}, u32[]{:S(2)}, u32[]{:S(2)}) collective-permute-start(bf16[64,1024]{1,0:T(8,128)(2,1)S(1)} %get-tuple-element.85), channel_id=1, source_target_pairs={{0,20},{1,29},{2,22},{3,31},{4,24},{5,17},{6,26},{7,19},{8,28},{9,... | collective-permute-start | bytes 393224 | tf_op jit(solution)/shard_map/ppermute | solution.py:482
  109.8 1.4 %collective-permute-start.36 = (bf16[64,1024]{1,0:T(8,128)(2,1)S(1)}, bf16[64,1024]{1,0:T(8,128)(2,1)S(1)}, u32[]{:S(2)}, u32[]{:S(2)}) collective-permute-start(bf16[64,1024]{1,0:T(8,128)(2,1)S(1)} %get-tuple-element.87), channel_id=1, source_target_pairs={{0,1},{1,0},{2,3},{3,2},{4,5},{5,4},{6,7},{7,6},{8,9},{9,8},{10,11... | collective-permute-start | bytes 393224 | tf_op jit(solution)/shard_map/ppermute | solution.py:485
